TPU v7x, 32 devices: a whole 2x2x4 slice. The times are simulated.
32 devices in a mesh: rows: 16 (over z, x, core), cols: 2 (over y).
Axes of the slice: x: 2, y: 2, z: 4, core: 2. Of those that a mesh axis runs over, the one named last changes fastest.
Arguments:
- fact_cells: bfloat16 [768, 8, 512], P('rows', 'cols'), may hold values from -6 to 6
- gain_col: float32 [512], replicated, may hold values from 0.1 to 1.9
- w_qkv: bfloat16 [512, 1536], replicated, may hold values from -0.25 to 0.25
- w_col_out: bfloat16 [512, 512], replicated, may hold values from -0.25 to 0.25
- gain_tile: float32 [512], replicated, may hold values from 0.1 to 1.9
- w_query: bfloat16 [512, 512], replicated, may hold values from -0.25 to 0.25
- w_tile_out: bfloat16 [512, 512], replicated, may hold values from -0.25 to 0.25
- tile_kv: bfloat16 [64, 128, 8, 128], P('rows', None, 'cols'), may hold values from -70 to 70
- tile_ids: int32 [16, 12], P('rows'), may hold values from -1 to 63, as said below
- key_mask: int32 [768, 12], P('rows'), may hold values from 0 to 1, as said below
Outputs:
- layer_out: bfloat16 [768, 8, 512], P('rows', 'cols')
Inputs may be any that keep to these rules, and one draw needn't show every extreme that they name: `tile_ids`: tile t is held by index t // 4 of rows. In every block the first slots, 9 of them or more, hold distinct tile ids and the rest hold -1; some block fills all 12 slots. The listed tiles of one block are held by distinct indices of rows. `key_mask`: 0 wherever the row's block holds -1 in that slot; 1 in slot 0 of every row.
All inputs are finite; a program needn't handle non-finite values.
Results may differ from a plain program's by a relative error of at most 0.023.
The roundings to bfloat16 on the way count: a program that leaves them out, or rounds other values in their place, can miss the bound.
Values may be sent and summed in bfloat16 or wider, within the bound.
No kernel may reach another device: no remote copies, remote signals or barrier semaphores. Data moves between devices by JAX's collectives and lax.ppermute only.
A program may use at most 64 MiB of HBM per device.

v0:
```python
import jax
import jax.numpy as jnp
from jax import lax
from jax.sharding import PartitionSpec as P


def rms_scale(values, gain_vec):
    mean_sq = jnp.mean(values * values, axis=-1, keepdims=True)
    return values * lax.rsqrt(mean_sq + 1e-05) * gain_vec


def soft_weights(scores, axes):
    row_top = jnp.max(scores, axis=axes, keepdims=True)
    expo_vals = jnp.exp(scores - row_top)
    return (expo_vals / jnp.sum(expo_vals, axis=axes, keepdims=True)).astype(jnp.bfloat16)


def column_attend(queries, keyvals, head_size):
    key_part = keyvals[..., :head_size]
    val_part = keyvals[..., head_size:]
    scores = jnp.einsum(
        "rchd,rkhd->rhck", queries, key_part, preferred_element_type=jnp.float32
    ) * head_size ** (-0.5)
    col_weights = soft_weights(scores, (3,))
    return jnp.einsum(
        "rhck,rkhd->rchd", col_weights, val_part, preferred_element_type=jnp.float32
    ).astype(jnp.bfloat16)


def tile_attend(queries, fetched, key_mask, head_size):
    key_part = fetched[..., :head_size]
    val_part = fetched[..., head_size:]
    row_count, col_count, head_count = queries.shape[:3]
    q_blocks = queries.reshape(row_count // 4, 4, col_count, head_count, head_size)
    m_blocks = key_mask.reshape(row_count // 4, 4, key_mask.shape[1])

    def one_block(block_pair):
        block_q, block_m = block_pair
        scores = jnp.einsum(
            "rchd,tkhd->rchtk", block_q, key_part, preferred_element_type=jnp.float32
        ) * head_size ** (-0.5)
        live_keys = (block_m > 0)[:, None, None, :, None]
        scores = jnp.where(live_keys, scores, -1e30)
        tile_weights = soft_weights(scores, (3, 4))
        return jnp.einsum(
            "rchtk,tkhd->rchd", tile_weights, val_part, preferred_element_type=jnp.float32
        ).astype(jnp.bfloat16)

    answer = lax.map(one_block, (q_blocks, m_blocks))
    return answer.reshape(row_count, col_count, head_count, head_size)


def fetch_all(tile_kv, tile_ids):
    gathered = lax.all_gather(tile_kv, "rows", axis=0, tiled=True)
    return jnp.take(gathered, jnp.maximum(tile_ids[0], 0), axis=0)


def project(normed, weight):
    return jnp.dot(normed.reshape(-1, weight.shape[0]), weight, preferred_element_type=jnp.float32)


def shards(
    fact_cells,
    gain_col,
    w_qkv,
    w_col_out,
    gain_tile,
    w_query,
    w_tile_out,
    tile_kv,
    tile_ids,
    key_mask,
):
    model_width = fact_cells.shape[2]
    head_size = tile_kv.shape[3] // 2
    heads_all = model_width // head_size
    fetched = fetch_all(tile_kv, tile_ids)
    row_count, col_local = (fact_cells.shape[0], fact_cells.shape[1])
    residual = fact_cells.astype(jnp.float32)
    normed = rms_scale(residual, gain_col).astype(jnp.bfloat16)
    packed = (
        project(normed, w_qkv)
        .astype(jnp.bfloat16)
        .reshape(row_count, col_local, 3, heads_all, head_size)
    )
    queries = packed[:, :, 0]
    keyvals = jnp.concatenate([packed[:, :, 1], packed[:, :, 2]], axis=-1)
    queries_h, keyvals_h = (
        lax.all_to_all(queries, "cols", split_axis=2, concat_axis=1, tiled=True),
        lax.all_to_all(keyvals, "cols", split_axis=2, concat_axis=1, tiled=True),
    )
    mixed_col = column_attend(queries_h, keyvals_h, head_size)
    mixed_back = lax.all_to_all(mixed_col, "cols", split_axis=1, concat_axis=2, tiled=True)
    residual = residual + project(mixed_back, w_col_out).reshape(residual.shape)
    normed2 = rms_scale(residual, gain_tile).astype(jnp.bfloat16)
    asked_q = (
        project(normed2, w_query)
        .astype(jnp.bfloat16)
        .reshape(row_count, col_local, heads_all, head_size)
    )
    asked_h = lax.all_to_all(asked_q, "cols", split_axis=2, concat_axis=1, tiled=True)
    answer = tile_attend(asked_h, fetched, key_mask, head_size)
    answer_back = lax.all_to_all(answer, "cols", split_axis=1, concat_axis=2, tiled=True)
    final_out = residual + project(answer_back, w_tile_out).reshape(residual.shape)
    return final_out.astype(jnp.bfloat16)


def solution(mesh):
    placed = (
        P("rows", "cols", None),
        P(),
        P(),
        P(),
        P(),
        P(),
        P(),
        P("rows", None, "cols", None),
        P("rows", None),
        P("rows", None),
    )
    return jax.shard_map(
        shards, mesh=mesh, in_specs=placed, out_specs=P("rows", "cols", None), check_vma=False
    )
```

profile of v0, /device:TPU:0, one launch (start us, length us, event | category | flops | bytes accessed | tf_op | source)
XLA Modules:
  0.0 145.7 jit_solution(3236836319116097506)
XLA Ops:
  6.5 2.1 %copy.70 = bf16[4,128,4,128]{3,1,2,0:T(8,128)(2,1)} copy(bf16[4,128,4,128]{3,2,1,0:T(4,128)(2,1)} %param.19) | data formatting | bytes 1048576 | tf_op args[7]
  11.7 4.2 %all-to-all-start.1 = ((bf16[2,2,24576]{2,1,0:T(2,128)(2,1)}), bf16[2,2,24576]{2,1,0:T(2,128)(2,1)S(1)}, u32[]{:S(2)}, u32[]{:S(2)}) async-start(bf16[2,2,24576]{2,1,0:T(2,128)(2,1)} %reshape.105), calls=%async_computation.1 | async-start | bytes 393216 | tf_op jit(solution)/shard_map/all_to_all | solution.py:89
  16.3 1.3 pad_maximum_fusion
  17.7 3.4 %all-to-all-done.1 = bf16[2,2,24576]{2,1,0:T(2,128)(2,1)S(1)} async-done(((bf16[2,2,24576]{2,1,0:T(2,128)(2,1)}), bf16[2,2,24576]{2,1,0:T(2,128)(2,1)S(1)}, u32[]{:S(2)}, u32[]{:S(2)}) %all-to-all-start.1) | async-done | bytes 196640 | tf_op jit(solution)/shard_map/all_to_all | solution.py:89
  21.1 3.5 %all-to-all-start = ((bf16[48,4,8,128]{3,1,0,2:T(4,128)(2,1)}), bf16[48,4,8,128]{3,1,0,2:T(4,128)(2,1)S(1)}, u32[]{:S(2)}, u32[]{:S(2)}) async-start(bf16[48,4,8,128]{3,1,0,2:T(4,128)(2,1)} %pad_maximum_fusion), calls=%async_computation | async-start | bytes 786432 | tf_op jit(solution)/shard_map/all_to_all | solution.py:90
  25.0 5.8 %all-to-all-done = bf16[48,4,8,128]{3,1,0,2:T(4,128)(2,1)S(1)} async-done(((bf16[48,4,8,128]{3,1,0,2:T(4,128)(2,1)}), bf16[48,4,8,128]{3,1,0,2:T(4,128)(2,1)S(1)}, u32[]{:S(2)}, u32[]{:S(2)}) %all-to-all-start) | async-done | bytes 393248 | tf_op jit(solution)/shard_map/all_to_all | solution.py:90
  33.9 3.4 %all-to-all-start.2 = ((bf16[2,2,24576]{2,1,0:T(2,128)(2,1)}), bf16[2,2,24576]{2,1,0:T(2,128)(2,1)S(1)}, u32[]{:S(2)}, u32[]{:S(2)}) async-start(bf16[2,2,24576]{2,1,0:T(2,128)(2,1)} %reshape.107), calls=%async_computation.2 | async-start | bytes 393216 | tf_op jit(solution)/shard_map/all_to_all | solution.py:93
  38.1 4.1 %all-to-all-done.2 = bf16[2,2,24576]{2,1,0:T(2,128)(2,1)S(1)} async-done(((bf16[2,2,24576]{2,1,0:T(2,128)(2,1)}), bf16[2,2,24576]{2,1,0:T(2,128)(2,1)S(1)}, u32[]{:S(2)}, u32[]{:S(2)}) %all-to-all-start.2) | async-done | bytes 196640 | tf_op jit(solution)/shard_map/all_to_all | solution.py:93
  43.6 1.3 convolution_convert_fusion.2
  46.3 3.4 %all-to-all-start.3 = ((bf16[2,2,24576]{2,1,0:T(2,128)(2,1)}), bf16[2,2,24576]{2,1,0:T(2,128)(2,1)S(1)}, u32[]{:S(2)}, u32[]{:S(2)}) async-start(bf16[2,2,24576]{2,1,0:T(2,128)(2,1)} %reshape.109), calls=%async_computation.3 | async-start | bytes 393216 | tf_op jit(solution)/shard_map/all_to_all | solution.py:101
  49.8 4.8 %all-to-all-done.3 = bf16[2,2,24576]{2,1,0:T(2,128)(2,1)S(1)} async-done(((bf16[2,2,24576]{2,1,0:T(2,128)(2,1)}), bf16[2,2,24576]{2,1,0:T(2,128)(2,1)S(1)}, u32[]{:S(2)}, u32[]{:S(2)}) %all-to-all-start.3) | async-done | bytes 196640 | tf_op jit(solution)/shard_map/all_to_all | solution.py:101
  55.8 31.4 %all-gather.2.cloned.1.call-done = bf16[64,128,4,128]{3,1,2,0:T(8,128)(2,1)} async-done(((bf16[4,128,4,128]{3,1,2,0:T(8,128)(2,1)}), bf16[64,128,4,128]{3,1,2,0:T(8,128)(2,1)}) %all-gather.2.cloned.1.call-update) | async-done | bytes 8388624 | tf_op jit(solution)/shard_map/all_gather | solution.py:54
  87.2 4.2 %gather_fusion = bf16[12,128,4,128]{3,1,2,0:T(8,128)(2,1)S(1)} fusion(bf16[64,128,4,128]{3,1,2,0:T(8,128)(2,1)} %all-gather.2.cloned.1.call-done, s32[1024]{0:T(1024)S(1)} %pad_clamp_fusion), kind=kCustom, calls=%fused_computation | custom fusion | bytes 3145776 | tf_op jit(solution)/shard_map/jit(_take)/gather | solution.py:55
  91.6 2.3 %fusion.27 = (bf16[12,128,4,64]{3,1,2,0:T(8,128)(2,1)}, bf16[12,128,4,64]{3,1,2,0:T(8,128)(2,1)}) fusion(bf16[12,128,4,128]{3,1,2,0:T(8,128)(2,1)S(1)} %broadcast_select_fusion), kind=kLoop, calls=%fused_computation.56 | loop fusion | bytes 3145728 | tf_op jit(solution)/shard_map/slice | solution.py:32
  93.9 1.8 %copy.72 = bf16[12,128,4,64]{1,3,0,2:T(8,128)(2,1)S(1)} copy(bf16[12,128,4,64]{3,1,2,0:T(8,128)(2,1)} %get-tuple-element.71) | data formatting | bytes 1572864 | tf_op jit(solution)/shard_map/while | solution.py:49
  95.7 2.5 %copy.73 = bf16[12,128,4,64]{1,3,0,2:T(8,128)(2,1)} copy(bf16[12,128,4,64]{3,1,2,0:T(8,128)(2,1)} %get-tuple-element.70) | data formatting | bytes 1572864 | tf_op jit(solution)/shard_map/while | solution.py:49
  98.2 30.6 %while.10 = (s32[]{:T(128)}, bf16[12,4,8,4,64]{4,2,3,1,0:T(8,128)(2,1)S(1)}, s32[12,4,12]{2,1,0:T(4,128)}, bf16[12,4,8,4,64]{4,2,3,1,0:T(8,128)(2,1)}, bf16[12,1...) while((s32[]{:T(128)}, bf16[12,4,8,4,64]{4,2,3,1,0:T(8,128)(2,1)S(1)}, ...), condition=%wide.region_7.8_spmd, body=%wide.region_4.0_spmd.sunk | while | flops 51912496 | bytes 7196049 | solution.py:49
  99.0 1.1 fusion.49
  101.5 1.1 fusion.49
  104.1 1.1 fusion.49
  109.2 1.1 fusion.49
  114.3 1.1 fusion.49
  116.8 1.1 fusion.49
  129.3 7.7 %all_to_all.81 = bf16[2,2,24576]{2,1,0:T(2,128)(2,1)S(1)} all-to-all(bf16[2,2,24576]{2,1,0:T(2,128)(2,1)S(1)} %reshape.111), channel_id=1, replica_groups=mesh['rows'=16,'cols'=2] {'cols'}, dimensions={0} | all-to-all | bytes 393216 | tf_op jit(solution)/shard_map/all_to_all | solution.py:103
  (146 shorter events, 37.7 us)
Async XLA Ops:
  6.5 2.6 %copy-start = (bf16[512,1536]{1,0:T(8,128)(2,1)S(1)}, bf16[512,1536]{1,0:T(8,128)(2,1)}, u32[]{:S(2)}) copy-start(bf16[512,1536]{1,0:T(8,128)(2,1)} %param.14) | copy-start | bytes 4718596
  6.5 2.1 %copy-start.1 = (bf16[48,4,512]{2,1,0:T(4,128)(2,1)S(1)}, bf16[48,4,512]{2,1,0:T(4,128)(2,1)}, u32[]{:S(2)}) copy-start(bf16[48,4,512]{2,1,0:T(4,128)(2,1)} %param.12) | copy-start | bytes 589828
  6.5 2.3 %copy-start.8 = (f32[512]{0:T(512)S(1)}, f32[512]{0:T(512)}, u32[]{:S(2)}) copy-start(f32[512]{0:T(512)} %param.13) | copy-start | bytes 6148
  6.5 80.6 %all-gather.2.cloned.1.call-start = ((), (), s32[]{:S(2)}) async-start(), calls=%async_computation.5 | async-start | bytes 8912896 | tf_op jit(solution)/shard_map/all_gather | solution.py:54
  11.7 9.4 %all-to-all-start.1 = ((bf16[2,2,24576]{2,1,0:T(2,128)(2,1)}), bf16[2,2,24576]{2,1,0:T(2,128)(2,1)S(1)}, u32[]{:S(2)}, u32[]{:S(2)}) async-start(bf16[2,2,24576]{2,1,0:T(2,128)(2,1)} %reshape.105), calls=%async_computation.1 | async-start | bytes 393216 | tf_op jit(solution)/shard_map/all_to_all | solution.py:89
  16.0 8.6 %copy-start.10 = (s32[1,12]{1,0:T(1,128)S(1)}, s32[1,12]{1,0:T(1,128)}, u32[]{:S(2)}) copy-start(s32[1,12]{1,0:T(1,128)} %param.20) | copy-start | bytes 148
  21.1 9.7 %all-to-all-start = ((bf16[48,4,8,128]{3,1,0,2:T(4,128)(2,1)}), bf16[48,4,8,128]{3,1,0,2:T(4,128)(2,1)S(1)}, u32[]{:S(2)}, u32[]{:S(2)}) async-start(bf16[48,4,8,128]{3,1,0,2:T(4,128)(2,1)} %pad_maximum_fusion), calls=%async_computation | async-start | bytes 786432 | tf_op jit(solution)/shard_map/all_to_all | solution.py:90
  32.7 4.7 %copy-start.7 = (s32[48,12]{0,1:T(8,128)S(1)}, s32[48,12]{0,1:T(8,128)}, u32[]{:S(2)}) copy-start(s32[48,12]{0,1:T(8,128)} %param.21) | copy-start | bytes 6916
  32.9 10.0 %copy-start.2 = (bf16[48,4,512]{2,1,0:T(4,128)(2,1)S(1)}, bf16[48,4,512]{2,1,0:T(4,128)(2,1)}, u32[]{:S(2)}) copy-start(bf16[48,4,512]{2,1,0:T(4,128)(2,1)} %param.12) | copy-start | bytes 589828
  32.9 10.0 %copy-start.4 = (bf16[512,512]{1,0:T(8,128)(2,1)S(1)}, bf16[512,512]{1,0:T(8,128)(2,1)}, u32[]{:S(2)}) copy-start(bf16[512,512]{1,0:T(8,128)(2,1)} %param.15) | copy-start | bytes 1572868
  33.9 8.2 %all-to-all-start.2 = ((bf16[2,2,24576]{2,1,0:T(2,128)(2,1)}), bf16[2,2,24576]{2,1,0:T(2,128)(2,1)S(1)}, u32[]{:S(2)}, u32[]{:S(2)}) async-start(bf16[2,2,24576]{2,1,0:T(2,128)(2,1)} %reshape.107), calls=%async_computation.2 | async-start | bytes 393216 | tf_op jit(solution)/shard_map/all_to_all | solution.py:93
  38.1 5.2 %copy-start.9 = (f32[512]{0:T(512)S(1)}, f32[512]{0:T(512)}, u32[]{:S(2)}) copy-start(f32[512]{0:T(512)} %param.16) | copy-start | bytes 6148
  46.3 8.2 %all-to-all-start.3 = ((bf16[2,2,24576]{2,1,0:T(2,128)(2,1)}), bf16[2,2,24576]{2,1,0:T(2,128)(2,1)S(1)}, u32[]{:S(2)}, u32[]{:S(2)}) async-start(bf16[2,2,24576]{2,1,0:T(2,128)(2,1)} %reshape.109), calls=%async_computation.3 | async-start | bytes 393216 | tf_op jit(solution)/shard_map/all_to_all | solution.py:101
  95.7 2.5 %copy-start.6 = (bf16[12,4,8,4,64]{4,2,3,1,0:T(8,128)(2,1)S(1)}, bf16[12,4,8,4,64]{4,2,3,1,0:T(8,128)(2,1)}, u32[]{:S(2)}) copy-start(bf16[12,4,8,4,64]{4,2,3,1,0:T(8,128)(2,1)} %custom-call.2) | copy-start | bytes 589828
  100.7 2.1 %copy-start.3 = (bf16[12,128,4,64]{1,3,0,2:T(8,128)(2,1)S(1)}, bf16[12,128,4,64]{1,3,0,2:T(8,128)(2,1)}, u32[]{:S(2)}) copy-start(bf16[12,128,4,64]{1,3,0,2:T(8,128)(2,1)} %get-tuple-element.139) | copy-start | bytes 2359300 | tf_op jit(solution)/shard_map/while
  105.9 2.1 %copy-start.3 = (bf16[12,128,4,64]{1,3,0,2:T(8,128)(2,1)S(1)}, bf16[12,128,4,64]{1,3,0,2:T(8,128)(2,1)}, u32[]{:S(2)}) copy-start(bf16[12,128,4,64]{1,3,0,2:T(8,128)(2,1)} %get-tuple-element.139) | copy-start | bytes 2359300 | tf_op jit(solution)/shard_map/while
  108.4 2.1 %copy-start.3 = (bf16[12,128,4,64]{1,3,0,2:T(8,128)(2,1)S(1)}, bf16[12,128,4,64]{1,3,0,2:T(8,128)(2,1)}, u32[]{:S(2)}) copy-start(bf16[12,128,4,64]{1,3,0,2:T(8,128)(2,1)} %get-tuple-element.139) | copy-start | bytes 2359300 | tf_op jit(solution)/shard_map/while
  111.0 2.1 %copy-start.3 = (bf16[12,128,4,64]{1,3,0,2:T(8,128)(2,1)S(1)}, bf16[12,128,4,64]{1,3,0,2:T(8,128)(2,1)}, u32[]{:S(2)}) copy-start(bf16[12,128,4,64]{1,3,0,2:T(8,128)(2,1)} %get-tuple-element.139) | copy-start | bytes 2359300 | tf_op jit(solution)/shard_map/while
  113.5 2.1 %copy-start.3 = (bf16[12,128,4,64]{1,3,0,2:T(8,128)(2,1)S(1)}, bf16[12,128,4,64]{1,3,0,2:T(8,128)(2,1)}, u32[]{:S(2)}) copy-start(bf16[12,128,4,64]{1,3,0,2:T(8,128)(2,1)} %get-tuple-element.139) | copy-start | bytes 2359300 | tf_op jit(solution)/shard_map/while
  116.1 2.1 %copy-start.3 = (bf16[12,128,4,64]{1,3,0,2:T(8,128)(2,1)S(1)}, bf16[12,128,4,64]{1,3,0,2:T(8,128)(2,1)}, u32[]{:S(2)}) copy-start(bf16[12,128,4,64]{1,3,0,2:T(8,128)(2,1)} %get-tuple-element.139) | copy-start | bytes 2359300 | tf_op jit(solution)/shard_map/while
  121.1 2.1 %copy-start.3 = (bf16[12,128,4,64]{1,3,0,2:T(8,128)(2,1)S(1)}, bf16[12,128,4,64]{1,3,0,2:T(8,128)(2,1)}, u32[]{:S(2)}) copy-start(bf16[12,128,4,64]{1,3,0,2:T(8,128)(2,1)} %get-tuple-element.139) | copy-start | bytes 2359300 | tf_op jit(solution)/shard_map/while
  123.7 2.1 %copy-start.3 = (bf16[12,128,4,64]{1,3,0,2:T(8,128)(2,1)S(1)}, bf16[12,128,4,64]{1,3,0,2:T(8,128)(2,1)}, u32[]{:S(2)}) copy-start(bf16[12,128,4,64]{1,3,0,2:T(8,128)(2,1)} %get-tuple-element.139) | copy-start | bytes 2359300 | tf_op jit(solution)/shard_map/while
  126.3 2.1 %copy-start.3 = (bf16[12,128,4,64]{1,3,0,2:T(8,128)(2,1)S(1)}, bf16[12,128,4,64]{1,3,0,2:T(8,128)(2,1)}, u32[]{:S(2)}) copy-start(bf16[12,128,4,64]{1,3,0,2:T(8,128)(2,1)} %get-tuple-element.139) | copy-start | bytes 2359300 | tf_op jit(solution)/shard_map/while
  129.3 8.5 %copy-start.5 = (bf16[512,512]{1,0:T(8,128)(2,1)S(1)}, bf16[512,512]{1,0:T(8,128)(2,1)}, u32[]{:S(2)}) copy-start(bf16[512,512]{1,0:T(8,128)(2,1)} %param.18) | copy-start | bytes 1572868
  (3 other events, 6.3 us)
Sparse Core Ops, SparseCore 0:
  9.5 77.5 all-gather.1
where the time goes:
time: 147 us; the launch traced here: 146 us
  waiting for transfers between devices  49.5 us (34%)
  local copies, waits for them, and re-layouts  23.8 us (16%)
  matrix products  21.9 us (15%)
  starting transfers between devices  14.6 us (10%)
  other arithmetic  14.2 us (10%)
  between operations  13.8 us (9%)
  blocking collectives  7.68 us (5%)
    all_gather x1, waiting for transfers between devices, fetch_all(): gathered = lax.all_gather(tile_kv, 'rows', axis=0, tiled=True)  31.4 us
    dot_general x12, matrix products, one_block(): jnp.einsum('rchd,tkhd->rchtk', block_q, key_part, preferred_element_type=...  13.1 us
    gt x12, other arithmetic, one_block(): live_keys = (block_m > 0)[:, None, None, :, None]  8.98 us
    all_to_all x1, blocking collectives, shards(): lax.all_to_all(answer, 'cols', split_axis=1, concat_axis=2, tiled=True)  7.68 us
    unnamed x31, local copies, waits for them, and re-layouts  7.48 us
    all_to_all x1, waiting for transfers between devices, shards(): lax.all_to_all(keyvals, 'cols', split_axis=2, concat_axis=1, tiled=True)  5.81 us
    all_to_all x1, waiting for transfers between devices, shards(): lax.all_to_all(asked_q, 'cols', split_axis=2, concat_axis=1, tiled=True)  4.79 us
    dot_general x12, matrix products, one_block(): jnp.einsum('rchtk,tkhd->rchd', tile_weights, val_part, preferred_element_...  4.66 us
  transfers between devices with their start and end apart: 5, of which 5 were waited for; matrix products, arithmetic and copies ran while one was open for 10% of the time, Pallas kernels for 0%

commit v1 on v0

v1 whole, which is shorter than its diff:
```python
import jax
import jax.numpy as jnp
from jax import lax
from jax.sharding import PartitionSpec as P


def rms_scale(values, gain_vec):
    mean_sq = jnp.mean(values * values, axis=-1, keepdims=True)
    return values * lax.rsqrt(mean_sq + 1e-05) * gain_vec


def soft_weights(scores, axes):
    row_top = jnp.max(scores, axis=axes, keepdims=True)
    expo_vals = jnp.exp(scores - row_top)
    return (expo_vals / jnp.sum(expo_vals, axis=axes, keepdims=True)).astype(jnp.bfloat16)


def project(values, weight):
    return jnp.dot(values, weight, preferred_element_type=jnp.float32)


def turn(size, step):
    return [(src, (src + step) % size) for src in range(size)]


def from_ahead(value, axis, size, step):
    return lax.ppermute(value, axis, turn(size, -step))


def fetch_tiles(tile_kv, tile_ids, row_size):
    tiles_here = tile_kv.shape[0]
    me = lax.axis_index("rows")
    all_ids = lax.all_gather(tile_ids[0], "rows", axis=0)
    mine = (all_ids >= 0) & (all_ids // tiles_here == me)
    wanted = jnp.sum(jnp.where(mine, all_ids % tiles_here, 0), axis=1)
    heads_first = jnp.transpose(tile_kv, (0, 2, 1, 3))
    outgoing = jnp.take(heads_first, wanted, axis=0)
    return lax.all_to_all(outgoing, "rows", split_axis=0, concat_axis=0, tiled=True)


def shards(row_size, col_size, fact_cells, gain_col, w_qkv, w_col_out, gain_tile, w_query, w_tile_out,
           tile_kv, tile_ids, key_mask):
    width = fact_cells.shape[2]
    head_size = tile_kv.shape[3] // 2
    heads_here = tile_kv.shape[2]
    heads_all = width // head_size
    rows, cols = fact_cells.shape[:2]
    tiles_here = tile_kv.shape[0]
    scale = head_size ** (-0.5)
    col_me = lax.axis_index("cols")

    others = [from_ahead(fact_cells, "cols", col_size, step) for step in range(1, col_size)]
    fetched = fetch_tiles(tile_kv, tile_ids, row_size)

    cells = jnp.concatenate([fact_cells] + others, axis=1)
    cols_all = cells.shape[1]
    residual = cells.astype(jnp.float32).reshape(-1, width)
    normed = rms_scale(residual, gain_col).astype(jnp.bfloat16)
    packed = project(normed, w_qkv).astype(jnp.bfloat16).reshape(rows, cols_all, 3, heads_all, head_size)
    scores = jnp.einsum("rchd,rkhd->rhck", packed[:, :, 0], packed[:, :, 1], preferred_element_type=jnp.float32) * scale
    mixed_col = jnp.einsum("rhck,rkhd->rchd", soft_weights(scores, (3,)), packed[:, :, 2],
                           preferred_element_type=jnp.float32).astype(jnp.bfloat16)
    residual = residual + project(mixed_col.reshape(-1, width), w_col_out)
    normed2 = rms_scale(residual, gain_tile).astype(jnp.bfloat16)
    group = heads_here * head_size
    query_here = lax.dynamic_slice_in_dim(w_query, col_me * group, group, 1)
    asked = project(normed2, query_here).astype(jnp.bfloat16).reshape(rows, cols_all, heads_here, head_size)

    holder = jnp.where(tile_ids[0] >= 0, tile_ids[0] // tiles_here, -1)
    slot_of = (holder[:, None] == jnp.arange(row_size)[None, :]) & (key_mask[:, :, None] > 0)
    live = jnp.any(slot_of, axis=1)

    key_part = fetched[..., :head_size]
    val_part = fetched[..., head_size:]
    scores = jnp.einsum("rchd,thkd->hrctk", asked, key_part, preferred_element_type=jnp.float32) * scale
    scores = jnp.where(live[None, :, None, :, None], scores, -1e30)
    weights = soft_weights(scores, (3, 4))
    answer = jnp.einsum("hrctk,thkd->rchd", weights, val_part, preferred_element_type=jnp.float32)
    answer = answer.astype(jnp.bfloat16).reshape(rows, cols_all, group)

    final = residual.reshape(rows, cols_all, width)[:, :cols].reshape(-1, width)
    for step in range(col_size):
        part = answer[:, step * cols:(step + 1) * cols].reshape(-1, group)
        if step:
            part = lax.ppermute(part, "cols", turn(col_size, step))
        start = (col_me - step) % col_size * group
        final = final + project(part, lax.dynamic_slice_in_dim(w_tile_out, start, group, 0))
    return final.astype(jnp.bfloat16).reshape(rows, cols, width)


def solution(mesh):
    row_size, col_size = mesh.shape["rows"], mesh.shape["cols"]
    placed = (P("rows", "cols", None), P(), P(), P(), P(), P(), P(), P("rows", None, "cols", None),
              P("rows", None), P("rows", None))

    def body(*arrays):
        return shards(row_size, col_size, *arrays)

    return jax.shard_map(body, mesh=mesh, in_specs=placed, out_specs=P("rows", "cols", None), check_vma=False)
```

time: 147 us -> 109 us (0.74)
  the two profiles are of different devices: /device:TPU:0 before, /device:TPU:10 now
where the time goes in v1:
time: 109 us; the launch traced here: 108 us
  waiting for transfers between devices  31.4 us (29%)
  local copies, waits for them, and re-layouts  17.6 us (16%)
  matrix products  17.2 us (16%)
  blocking collectives  15.3 us (14%)
  starting transfers between devices  14.4 us (13%)
  other arithmetic  12.3 us (11%)
    all_to_all x1, waiting for transfers between devices, fetch_tiles(): lax.all_to_all(outgoing, 'rows', split_axis=0, concat_axis=0, tiled=True)  23 us
    all_gather x1, blocking collectives, fetch_tiles(): all_ids = lax.all_gather(tile_ids[0], 'rows', axis=0)  15.3 us
    all_to_all x1, starting transfers between devices, fetch_tiles(): lax.all_to_all(outgoing, 'rows', split_axis=0, concat_axis=0, tiled=True)  11.2 us
    ppermute x1, waiting for transfers between devices, from_ahead(): return lax.ppermute(value, axis, turn(size, -step))  5.11 us
    convert_element_type x1, other arithmetic, soft_weights(): (expo_vals / jnp.sum(expo_vals, axis=axes, keepdims=True)).astype(jnp.bfl...  4.41 us
    sub x1, matrix products, soft_weights(): expo_vals = jnp.exp(scores - row_top)  4.16 us
    dot_general x5, matrix products, project(): return jnp.dot(values, weight, preferred_element_type=jnp.float32)  4.14 us
    dot_general x1, matrix products, shards(): jnp.einsum('hrctk,thkd->rchd', weights, val_part, preferred_element_type=...  4.02 us
  transfers between devices with their start and end apart: 3, of which 3 were waited for; matrix products, arithmetic and copies ran while one was open for 16% of the time, Pallas kernels for 0%

profile of v1, /device:TPU:10, one launch (start us, length us, event | category | flops | bytes accessed | tf_op | source)
XLA Modules:
  0.0 108.4 jit_solution(6663205254077864323)
XLA Ops:
  0.0 15.3 %all-gather = s32[16,1,12]{2,1,0:T(1,128)S(1)} all-gather(s32[1,1,12]{2,1,0:T(1,128)} %bitcast.85), channel_id=1, replica_groups=mesh['rows'=16,'cols'=2] {'rows'}, dimensions={0}, use_global_device_ids=true | all-gather | bytes 816 | tf_op jit(solution)/shard_map/all_gather | solution.py:33
  15.4 1.1 %copy.104 = bf16[4,128,4,128]{3,1,2,0:T(8,128)(2,1)S(1)} copy(bf16[4,128,4,128]{3,2,1,0:T(4,128)(2,1)} %param.17) | data formatting | bytes 1048576 | tf_op args[7]
  16.6 2.2 %gather_fusion = bf16[16,4,128,128]{3,2,1,0:T(8,128)(2,1)} fusion(bf16[4,4,128,128]{3,2,1,0:T(8,128)(2,1)S(1)} %bitcast.81, s32[1024]{0:T(1024)S(1)} %pad_clamp_fusion), kind=kCustom, calls=%fused_computation | custom fusion | bytes 4194368 | tf_op jit(solution)/shard_map/jit(_take)/gather | solution.py:37
  18.8 3.2 %broadcast_select_fusion = bf16[16,4,128,128]{3,2,1,0:T(8,128)(2,1)} fusion(bf16[16,4,128,128]{3,2,1,0:T(8,128)(2,1)} %gather_fusion, pred[16]{0:T(512)(128)(4,1)S(1)} %compare_and_fusion), kind=kLoop, calls=%fused_computation.10 | loop fusion | flops 1048576 | bytes 4194320 | tf_op jit(solution)/shard_map/jit(_take)/select_n | solution.py:37
  22.0 3.9 %copy.48 = bf16[16,4,128,128]{2,3,1,0:T(8,128)(2,1)} copy(bf16[16,4,128,128]{3,2,1,0:T(8,128)(2,1)} %broadcast_select_fusion) | data formatting | bytes 4194304 | tf_op jit(solution)/shard_map/jit(_take)/select_n | solution.py:37
  25.9 11.2 %all-to-all-start = ((bf16[16,4,128,128]{2,3,1,0:T(8,128)(2,1)}), bf16[16,4,128,128]{2,3,1,0:T(8,128)(2,1)}, u32[]{:S(2)}, u32[]{:S(2)}) async-start(bf16[16,4,128,128]{2,3,1,0:T(8,128)(2,1)} %copy.48), calls=%async_computation | async-start | bytes 4194304 | tf_op jit(solution)/shard_map/all_to_all | solution.py:38
  37.2 1.6 %collective-permute-start = (bf16[48,4,512]{2,1,0:T(4,128)(2,1)S(1)}, bf16[48,4,512]{2,1,0:T(4,128)(2,1)S(1)}, u32[]{:S(2)}, u32[]{:S(2)}) collective-permute-start(bf16[48,4,512]{2,1,0:T(4,128)(2,1)S(1)} %copy-done.2), channel_id=1, source_target_pairs={{0,1},{1,0},{2,3},{3,2},{4,5},{5,4},{6,7},{7,6},{8,9},{9,8},{10,11... | collective-permute-start | bytes 589832 | tf_op jit(solution)/shard_map/ppermute | solution.py:27
  39.1 5.1 %collective-permute-done = bf16[48,4,512]{2,1,0:T(4,128)(2,1)S(1)} collective-permute-done((bf16[48,4,512]{2,1,0:T(4,128)(2,1)S(1)}, bf16[48,4,512]{2,1,0:T(4,128)(2,1)S(1)}, u32[]{:S(2)}, u32[]{:S(2)}) %collective-permute-start) | collective-permute-done | bytes 196640 | tf_op jit(solution)/shard_map/ppermute | solution.py:27
  44.6 0.9 convolution_convert_fusion
  45.5 2.7 %reshape.135 = bf16[48,8,3,8,64]{4,3,2,1,0:T(8,128)(2,1)} reshape(bf16[384,1536]{1,0:T(8,128)(2,1)S(1)} %convolution_convert_fusion) | data formatting | bytes 2359296 | tf_op jit(solution)/shard_map/reshape | solution.py:59
  48.2 3.1 %fusion.44 = (bf16[48,8,1,8,64]{4,3,2,1,0:T(8,128)(2,1)S(1)}, bf16[48,8,1,8,64]{4,3,2,1,0:T(8,128)(2,1)S(1)}, bf16[48,8,1,8,64]{4,3,2,1,0:T(8,128)(2,1)}) fusion(bf16[48,8,3,8,64]{4,3,2,1,0:T(8,128)(2,1)} %reshape.135), kind=kLoop, calls=%fused_computation.82 | loop fusion | bytes 2359296 | tf_op jit(solution)/shard_map/slice | solution.py:61
  51.4 4.2 %fusion.47 = (f32[48,8,8]{2,1,0:T(8,128)}, f32[48,8,8,8]{2,3,1,0:T(8,128)}) fusion(bf16[48,8,1,8,64]{4,3,2,1,0:T(8,128)(2,1)} %get-tuple-element.7, bf16[48,8,1,8,64]{4,3,2,1,0:T(8,128)(2,1)S(1)} %get-tuple-element.6), kind=kOutput, calls=%fused_computation.85 | convolution fusion | flops 3219463 | bytes 897024 | tf_op jit(solution)/shard_map/sub | solution.py:14
  55.5 2.1 %fusion.7 = bf16[48,8,8,64]{3,1,2,0:T(8,128)(2,1)S(1)} fusion(f32[48,8,8,8]{2,3,1,0:T(8,128)} %get-tuple-element.13, bf16[48,8,1,8,64]{4,3,2,1,0:T(8,128)(2,1)S(1)} %get-tuple-element.5, f32[48,8,8]{2,1,0:T(8,128)} %get-tuple-element.12), kind=kOutput, calls=%fused_computation.16 | convolution fusion | flops 3391488 | bytes 897024 | tf_op jit(solution)/shard_map/rhck,rkhd->rchd/dot_general | solution.py:61
  58.3 1.6 %multiply_reduce_fusion = (f32[384]{0:T(512)S(1)}, f32[384,512]{1,0:T(8,128)S(1)}) fusion(bf16[384,512]{1,0:T(8,128)(2,1)S(1)} %reshape.136, bf16[512,512]{1,0:T(8,128)(2,1)} %param.13, bf16[48,4,512]{2,1,0:T(4,128)(2,1)S(1)} %collective-permute-done, bf16[48,4,512]{2,1,0:T(4,128)(2,1)S(1)} %copy-done.2), kind=kOutput, calls=%fused_computation.38 | convolution fusion | flops 202702464 | bytes 2098688 | tf_op jit(solution)/shard_map/dot_general | solution.py:19
  60.1 1.3 %convolution_convert_fusion.2 = bf16[384,256]{1,0:T(8,128)(2,1)S(1)} fusion(f32[384,512]{1,0:T(8,128)S(1)} %get-tuple-element.15, f32[512]{0:T(512)S(1)} %copy-done.4, f32[384]{0:T(512)S(1)} %add_rsqrt_fusion.1, bf16[512,512]{1,0:T(8,128)(2,1)} %param.15, s32[]{:T(128)S(6)} %select_n.84), kind=kOutput, calls=%fused_computation.24 | convolution fusion | flops 101351424 | bytes 1248772 | tf_op jit(solution)/shard_map/dot_general | solution.py:19
  61.6 23.0 %all-to-all-done = bf16[16,4,128,128]{2,3,1,0:T(8,128)(2,1)} async-done(((bf16[16,4,128,128]{2,3,1,0:T(8,128)(2,1)}), bf16[16,4,128,128]{2,3,1,0:T(8,128)(2,1)}, u32[]{:S(2)}, u32[]{:S(2)}) %all-to-all-start) | async-done | bytes 2097184 | tf_op jit(solution)/shard_map/all_to_all | solution.py:38
  84.6 1.8 %fusion.45 = (bf16[16,4,128,64]{2,3,1,0:T(8,128)(2,1)S(1)}, bf16[16,4,128,64]{2,3,1,0:T(8,128)(2,1)S(1)}) fusion(bf16[16,4,128,128]{2,3,1,0:T(8,128)(2,1)} %all-to-all-done), kind=kLoop, calls=%fused_computation.83 | loop fusion | bytes 4194304 | tf_op jit(solution)/shard_map/slice | solution.py:74
  86.4 2.8 %fusion.1 = (f32[4,48,8]{2,1,0:T(8,128)S(1)}, f32[4,48,8,16,128]{4,2,3,1,0:T(8,128)S(1)}) fusion(pred[48,16]{1,0:T(8,128)(4,1)S(1)} %copy.50, bf16[16,4,128,64]{2,3,1,0:T(8,128)(2,1)S(1)} %get-tuple-element.9, bf16[48,8,4,64,1]{3,2,1,0,4:T(4,128)(2,1)S(1)} %bitcast.83), kind=kOutput, calls=%fused_computation.5 | convolution fusion | flops 412088832 | bytes 13835008 | tf_op jit(solution)/shard_map/rchd,thkd->hrctk/dot_general | solution.py:75
  89.2 4.0 %fusion.2 = f32[4,48,8]{2,1,0:T(8,128)S(1)} fusion(f32[4,48,8,16,128]{4,2,3,1,0:T(8,128)S(1)} %get-tuple-element.17, f32[4,48,8]{2,1,0:T(8,128)S(1)} %get-tuple-element.16, pred[48,16]{1,0:T(8,128)(4,1)S(1)} %copy.50), kind=kLoop, calls=%fused_computation.6 | loop fusion | flops 12581376 | bytes 12595968 | tf_op jit(solution)/shard_map/reduce_sum | solution.py:15
  93.2 4.4 %divide_convert_fusion = bf16[4,48,8,16,128]{4,2,3,1,0:T(8,128)(2,1)S(1)} fusion(f32[4,48,8,16,128]{4,2,3,1,0:T(8,128)S(1)} %get-tuple-element.17, f32[4,48,8]{2,1,0:T(8,128)S(1)} %fusion.2, f32[4,48,8]{2,1,0:T(8,128)S(1)} %get-tuple-element.16, pred[48,16]{1,0:T(8,128)(4,1)S(1)} %copy.50), kind=kLoop, calls=%fused_computation.2 | loop fusion | flops 15728640 | bytes 18887424 | tf_op jit(solution)/shard_map/convert_element_type | solution.py:15
  97.6 4.0 %fusion.14 = bf16[48,8,4,64]{3,0,1,2:T(8,128)(2,1)S(1)} fusion(bf16[4,48,8,16,128]{4,2,3,1,0:T(8,128)(2,1)S(1)} %divide_convert_fusion, bf16[16,4,128,64]{2,3,1,0:T(8,128)(2,1)S(1)} %get-tuple-element.8), kind=kOutput, calls=%fused_computation.20 | convolution fusion | flops 402751488 | bytes 7536640 | tf_op jit(solution)/shard_map/hrctk,thkd->rchd/dot_general | solution.py:78
  102.4 1.6 %collective-permute-start.1 = (bf16[192,256]{1,0:T(8,128)(2,1)S(1)}, bf16[192,256]{1,0:T(8,128)(2,1)S(1)}, u32[]{:S(2)}, u32[]{:S(2)}) collective-permute-start(bf16[192,256]{1,0:T(8,128)(2,1)S(1)} %reshape.142), channel_id=1, source_target_pairs={{0,1},{1,0},{2,3},{3,2},{4,5},{5,4},{6,7},{7,6},{8,9},{9,8},{10,11... | collective-permute-start | bytes 294920 | tf_op jit(solution)/shard_map/ppermute | solution.py:85
  104.2 3.3 %collective-permute-done.1 = bf16[192,256]{1,0:T(8,128)(2,1)S(1)} collective-permute-done((bf16[192,256]{1,0:T(8,128)(2,1)S(1)}, bf16[192,256]{1,0:T(8,128)(2,1)S(1)}, u32[]{:S(2)}, u32[]{:S(2)}) %collective-permute-start.1) | collective-permute-done | bytes 98336 | tf_op jit(solution)/shard_map/ppermute | solution.py:85
  107.6 0.7 reshape.143
  (39 shorter events, 3.0 us)
Async XLA Ops:
  0.0 44.6 %copy-start = (bf16[512,1536]{1,0:T(8,128)(2,1)S(1)}, bf16[512,1536]{1,0:T(8,128)(2,1)}, u32[]{:S(2)}) copy-start(bf16[512,1536]{1,0:T(8,128)(2,1)} %param.12) | copy-start | bytes 4718596
  22.0 15.2 %copy-start.2 = (bf16[48,4,512]{2,1,0:T(4,128)(2,1)S(1)}, bf16[48,4,512]{2,1,0:T(4,128)(2,1)}, u32[]{:S(2)}) copy-start(bf16[48,4,512]{2,1,0:T(4,128)(2,1)} %param.10) | copy-start | bytes 589828
  22.0 16.8 %copy-start.5 = (s32[1,12]{1,0:T(1,128)S(1)}, s32[1,12]{1,0:T(1,128)}, u32[]{:S(2)}) copy-start(s32[1,12]{1,0:T(1,128)} %param.18) | copy-start | bytes 148
  25.9 12.9 %copy-start.3 = (s32[48,12]{0,1:T(8,128)S(1)}, s32[48,12]{0,1:T(8,128)}, u32[]{:S(2)}) copy-start(s32[48,12]{0,1:T(8,128)} %param.19) | copy-start | bytes 6916
  25.9 18.7 %copy-start.6 = (f32[512]{0:T(512)S(1)}, f32[512]{0:T(512)}, u32[]{:S(2)}) copy-start(f32[512]{0:T(512)} %param.11) | copy-start | bytes 6148
  25.9 58.6 %all-to-all-start = ((bf16[16,4,128,128]{2,3,1,0:T(8,128)(2,1)}), bf16[16,4,128,128]{2,3,1,0:T(8,128)(2,1)}, u32[]{:S(2)}, u32[]{:S(2)}) async-start(bf16[16,4,128,128]{2,3,1,0:T(8,128)(2,1)} %copy.48), calls=%async_computation | async-start | bytes 4194304 | tf_op jit(solution)/shard_map/all_to_all | solution.py:38
  37.2 7.0 %collective-permute-start = (bf16[48,4,512]{2,1,0:T(4,128)(2,1)S(1)}, bf16[48,4,512]{2,1,0:T(4,128)(2,1)S(1)}, u32[]{:S(2)}, u32[]{:S(2)}) collective-permute-start(bf16[48,4,512]{2,1,0:T(4,128)(2,1)S(1)} %copy-done.2), channel_id=1, source_target_pairs={{0,1},{1,0},{2,3},{3,2},{4,5},{5,4},{6,7},{7,6},{8,9},{9,8},{10,11... | collective-permute-start | bytes 589832 | tf_op jit(solution)/shard_map/ppermute | solution.py:27
  57.6 2.5 %copy-start.4 = (f32[512]{0:T(512)S(1)}, f32[512]{0:T(512)}, u32[]{:S(2)}) copy-start(f32[512]{0:T(512)} %param.14) | copy-start | bytes 6148
  97.6 6.4 %copy-start.1 = (bf16[512,512]{1,0:T(8,128)(2,1)S(1)}, bf16[512,512]{1,0:T(8,128)(2,1)}, u32[]{:S(2)}) copy-start(bf16[512,512]{1,0:T(8,128)(2,1)} %param.16) | copy-start | bytes 1572868
  102.4 5.1 %collective-permute-start.1 = (bf16[192,256]{1,0:T(8,128)(2,1)S(1)}, bf16[192,256]{1,0:T(8,128)(2,1)S(1)}, u32[]{:S(2)}, u32[]{:S(2)}) collective-permute-start(bf16[192,256]{1,0:T(8,128)(2,1)S(1)} %reshape.142), channel_id=1, source_target_pairs={{0,1},{1,0},{2,3},{3,2},{4,5},{5,4},{6,7},{7,6},{8,9},{9,8},{10,11... | collective-permute-start | bytes 294920 | tf_op jit(solution)/shard_map/ppermute | solution.py:85

commit v2 on v1

v2 whole, which is shorter than its diff:
```python
import functools

import jax
import jax.numpy as jnp
from jax import lax
from jax.experimental import pallas as pl
from jax.experimental.pallas import tpu as pltpu
from jax.sharding import PartitionSpec as P

ROW_GROUP = 16
BIG = -1e30
VMEM_BYTES = 48 * 1024 * 1024


def params():
    return pltpu.CompilerParams(vmem_limit_bytes=VMEM_BYTES)


def dot_rows(left, right):
    return lax.dot_general(left, right, (((1,), (0,)), ((), ())), preferred_element_type=jnp.float32)


def dot_lanes(left, right):
    return lax.dot_general(left, right, (((1,), (1,)), ((), ())), preferred_element_type=jnp.float32)


def rms_scale(values, gain_vec):
    mean_sq = jnp.mean(values * values, axis=-1, keepdims=True)
    return values * lax.rsqrt(mean_sq + 1e-05) * gain_vec


def pick_kernel(count, wanted_ref, tiles_ref, out_ref):
    for peer in range(count):
        out_ref[peer] = tiles_ref[wanted_ref[peer]]


def pick(tiles, wanted):
    count = wanted.shape[0]
    return pl.pallas_call(
        functools.partial(pick_kernel, count),
        out_shape=jax.ShapeDtypeStruct((count,) + tiles.shape[1:], tiles.dtype),
        in_specs=[pl.BlockSpec(memory_space=pltpu.SMEM), pl.BlockSpec(memory_space=pltpu.VMEM)],
        out_specs=pl.BlockSpec(memory_space=pltpu.VMEM),
        compiler_params=params(),
        cost_estimate=pl.CostEstimate(flops=0, bytes_accessed=tiles.size * 2 + count * tiles[0].size * 2, transcendentals=0),
        name="pick",
    )(wanted, tiles)


def front_kernel(groups, heads, head_size, chunk, cols, *refs):
    cell_refs, refs = refs[:groups], refs[groups:]
    (gain_col_ref, w_qkv_ref, w_out_ref, gain_tile_ref, w_query_ref,
     resid_ref, asked_ref, normed_ref, packed_ref) = refs
    own_rows, width = cell_refs[0].shape
    steps = own_rows // chunk
    span = groups * chunk
    for step in range(steps):
        for group in range(groups):
            cells = cell_refs[group][pl.ds(step * chunk, chunk), :].astype(jnp.float32)
            normed_ref[pl.ds(step * span + group * chunk, chunk), :] = rms_scale(cells, gain_col_ref[...]).astype(jnp.bfloat16)
    for part in range(3):
        packed_ref[part] = dot_rows(normed_ref[...], w_qkv_ref[:, pl.ds(part * width, width)]).astype(jnp.bfloat16)
    row_of = lax.broadcasted_iota(jnp.int32, (span, span), 0) % chunk // cols
    col_of = lax.broadcasted_iota(jnp.int32, (span, span), 1) % chunk // cols
    same_row = row_of == col_of
    lane_low = lax.broadcasted_iota(jnp.int32, (span, 2 * head_size), 1) < head_size
    scale = head_size ** (-0.5)
    for step in range(steps):
        rows = pl.ds(step * span, span)
        for pair in range(heads // 2):
            lanes = pl.ds(pair * 2 * head_size, 2 * head_size)
            query, keys, vals = packed_ref[0, rows, lanes], packed_ref[1, rows, lanes], packed_ref[2, rows, lanes]
            mixed = []
            for low in (True, False):
                query_one = jnp.where(lane_low == low, query, jnp.zeros_like(query))
                scores = jnp.where(same_row, dot_lanes(query_one, keys) * scale, BIG)
                expo = jnp.exp(scores - jnp.max(scores, axis=1, keepdims=True))
                weights = (expo / jnp.sum(expo, axis=1, keepdims=True)).astype(jnp.bfloat16)
                mixed.append(dot_rows(weights, vals))
            normed_ref[rows, lanes] = jnp.where(lane_low, mixed[0], mixed[1]).astype(jnp.bfloat16)
    delta = dot_rows(normed_ref[...], w_out_ref[...])
    for step in range(steps):
        for group in range(groups):
            start = step * span + group * chunk
            resid = cell_refs[group][pl.ds(step * chunk, chunk), :].astype(jnp.float32) + delta[start:start + chunk]
            if group == 0:
                resid_ref[pl.ds(step * chunk, chunk), :] = resid
            normed_ref[pl.ds(start, chunk), :] = rms_scale(resid, gain_tile_ref[...]).astype(jnp.bfloat16)
    asked = dot_rows(normed_ref[...], w_query_ref[...]).astype(jnp.bfloat16)
    asked_ref[...] = asked * jnp.bfloat16(scale)


def front(cells, gain_col, w_qkv, w_out, gain_tile, w_query, heads, head_size, cols):
    groups = len(cells)
    own_rows, width = cells[0].shape
    total = groups * own_rows
    asked_width = w_query.shape[1]
    vmem = pl.BlockSpec(memory_space=pltpu.VMEM)
    return pl.pallas_call(
        functools.partial(front_kernel, groups, heads, head_size, ROW_GROUP * cols, cols),
        out_shape=(jax.ShapeDtypeStruct((own_rows, width), jnp.float32),
                   jax.ShapeDtypeStruct((total, asked_width), jnp.bfloat16)),
        in_specs=[vmem] * (groups + 5),
        out_specs=(vmem, vmem),
        scratch_shapes=[pltpu.VMEM((total, width), jnp.bfloat16), pltpu.VMEM((3, total, width), jnp.bfloat16)],
        compiler_params=params(),
        cost_estimate=pl.CostEstimate(flops=2 * total * width * (4 * width + asked_width), bytes_accessed=4 * 1024 * 1024,
                                      transcendentals=total * heads * 128),
        name="front",
    )(*cells, gain_col.reshape(1, width), w_qkv, w_out, gain_tile.reshape(1, width), w_query)


def weigh(query, bias, tiles):
    slots, keys, lanes = tiles.shape
    scores = dot_lanes(query, tiles.reshape(slots * keys, lanes))
    parts = [scores[:, s * keys:(s + 1) * keys] + bias[:, s:s + 1] for s in range(slots)]
    top = parts[0]
    for part in parts[1:]:
        top = jnp.maximum(top, part)
    top = jnp.max(top, axis=1, keepdims=True)
    expo = [jnp.exp(part - top) for part in parts]
    total = expo[0]
    for part in expo[1:]:
        total = total + part
    total = jnp.sum(total, axis=1, keepdims=True)
    probs = jnp.concatenate([part.astype(jnp.bfloat16) for part in expo], axis=1)
    return top, total, dot_rows(probs, tiles.reshape(slots * keys, lanes))


def first_kernel(heads, chunk, asked_ref, bias_ref, tiles_ref, state_ref):
    rows_all, lanes = asked_ref.shape[0], tiles_ref.shape[3]
    lane = lax.broadcasted_iota(jnp.int32, (chunk, lanes), 1)
    for step in range(rows_all // chunk):
        rows = pl.ds(step * chunk, chunk)
        for head in range(heads):
            top, total, summed = weigh(asked_ref[rows, pl.ds(head * lanes, lanes)], bias_ref[rows, :], tiles_ref[:, head])
            state_ref[head, rows, :] = jnp.where(lane < lanes // 4, top, jnp.where(lane < lanes // 2, total, summed))


def first_tiles(asked, bias, tiles):
    slots, heads, keys, lanes = tiles.shape
    rows = asked.shape[0]
    vmem = pl.BlockSpec(memory_space=pltpu.VMEM)
    return pl.pallas_call(
        functools.partial(first_kernel, heads, 128),
        out_shape=jax.ShapeDtypeStruct((heads, rows, lanes), jnp.float32),
        in_specs=[vmem] * 3,
        out_specs=vmem,
        compiler_params=params(),
        cost_estimate=pl.CostEstimate(flops=4 * rows * heads * slots * keys * lanes, bytes_accessed=4 * 1024 * 1024,
                                      transcendentals=rows * heads * slots * keys),
        name="first_tiles",
    )(asked, bias, tiles)


def last_kernel(groups, first_head, heads, chunk, asked_ref, bias_ref, tiles_ref, state_ref, *out_refs):
    rows_all, lanes = asked_ref.shape[0], tiles_ref.shape[3]
    half = lanes // 2
    span = groups * chunk
    lane_low = lax.broadcasted_iota(jnp.int32, (span, lanes), 1) < half
    for step in range(rows_all // span):
        rows = pl.ds(step * span, span)
        answers = []
        for head in range(heads):
            query = asked_ref[rows, pl.ds((first_head + head) * lanes, lanes)]
            top, total, summed = weigh(query, bias_ref[rows, :], tiles_ref[:, head])
            state = state_ref[first_head + head, rows, :]
            old_top, old_total = state[:, 0:1], state[:, lanes // 4:lanes // 4 + 1]
            new_top = jnp.maximum(top, old_top)
            keep, add = jnp.exp(old_top - new_top), jnp.exp(top - new_top)
            whole = old_total * keep + total * add
            answers.append((state * keep + summed * add) / whole)
        if heads % 2 == 0:
            for pair in range(heads // 2):
                low = pltpu.roll(answers[2 * pair], half, 1)
                both = jnp.where(lane_low, low, answers[2 * pair + 1]).astype(jnp.bfloat16)
                for group in range(groups):
                    out_refs[group][pl.ds(step * chunk, chunk), pl.ds(pair * lanes, lanes)] = both[group * chunk:(group + 1) * chunk]
        else:
            for head in range(heads):
                one = answers[head][:, half:].astype(jnp.bfloat16)
                for group in range(groups):
                    out_refs[group][pl.ds(step * chunk, chunk), pl.ds(head * half, half)] = one[group * chunk:(group + 1) * chunk]


def last_tiles(asked, bias, tiles, state, first_head, groups, cols):
    slots, heads, keys, lanes = tiles.shape
    rows = asked.shape[0]
    vmem = pl.BlockSpec(memory_space=pltpu.VMEM)
    out = jax.ShapeDtypeStruct((rows // groups, heads * lanes // 2), jnp.bfloat16)
    return pl.pallas_call(
        functools.partial(last_kernel, groups, first_head, heads, ROW_GROUP * cols),
        out_shape=(out,) * groups,
        in_specs=[vmem] * 4,
        out_specs=(vmem,) * groups,
        compiler_params=params(),
        cost_estimate=pl.CostEstimate(flops=4 * rows * heads * slots * keys * lanes, bytes_accessed=4 * 1024 * 1024,
                                      transcendentals=rows * heads * slots * keys),
        name="last_tiles",
    )(asked, bias, tiles, state)


def turn(size, step):
    return [(src, (src + step) % size) for src in range(size)]


def shards(row_size, col_size, fact_cells, gain_col, w_qkv, w_col_out, gain_tile, w_query, w_tile_out,
           tile_kv, tile_ids, key_mask):
    rows, cols, width = fact_cells.shape
    tiles_here, keys, heads_here, lanes = tile_kv.shape
    head_size = lanes // 2
    heads_all = width // head_size
    group_width = heads_here * head_size
    half = row_size // 2
    parts = 2 if heads_here % 2 == 0 else 1
    part_heads = heads_here // parts
    col_me = lax.axis_index("cols")
    my_half = lax.axis_index("rows") // half
    halves = [list(range(half)), list(range(half, row_size))]

    def swap(value):
        return lax.all_to_all(value, "rows", split_axis=0, concat_axis=0, tiled=True, axis_index_groups=halves)

    listed = tile_ids[0] >= 0
    holder = jnp.where(listed, tile_ids[0] // tiles_here, -1)
    match = holder[:, None] == jnp.arange(row_size)[None, :]
    wanted = jnp.sum(jnp.where(match, (tile_ids[0] % tiles_here)[:, None], 0), axis=0).astype(jnp.int32)
    wanted = jnp.roll(wanted, -my_half * half).reshape(2, half)
    asked_of = jnp.broadcast_to(wanted.T[:, :, None], (half, 2, 128))
    asked_by = swap(asked_of)[:, :, 0]

    cells = [fact_cells.reshape(rows * cols, width)]
    for step in range(1, col_size):
        cells.append(lax.ppermute(cells[0], "cols", turn(col_size, -step)))

    heads_first = jnp.transpose(tile_kv, (0, 2, 1, 3))
    mirrored = [lax.ppermute(heads_first[:, part * part_heads:(part + 1) * part_heads], "rows", turn(row_size, half))
                for part in range(parts)]
    near = swap(pick(heads_first, asked_by[:, 0]))

    query_here = lax.dynamic_slice_in_dim(w_query, col_me * group_width, group_width, 1)
    query_here = jnp.pad(query_here.reshape(width, heads_here, head_size), ((0, 0), (0, 0), (0, head_size)))
    residual, asked = front(cells, gain_col, w_qkv, w_col_out, gain_tile, query_here.reshape(width, heads_here * lanes),
                            heads_all, head_size, cols)

    live = jnp.any(match[None, :, :] & (key_mask[:, :, None] > 0), axis=1)
    bias = jnp.where(live, 0.0, BIG).astype(jnp.float32)
    bias = jnp.roll(bias, -my_half * half, axis=1)
    bias = jnp.broadcast_to(bias.reshape(rows // ROW_GROUP, 1, ROW_GROUP, 1, row_size),
                            (rows // ROW_GROUP, col_size, ROW_GROUP, cols, row_size)).reshape(-1, row_size)
    state = first_tiles(asked, bias[:, :half], near)

    final = residual
    for part in range(parts):
        far = swap(pick(mirrored[part], asked_by[:, 1]))
        answers = last_tiles(asked, bias[:, half:], far, state, part * part_heads, col_size, cols)
        for step in range(col_size):
            answer = lax.ppermute(answers[step], "cols", turn(col_size, step)) if step else answers[0]
            start = (col_me - step) % col_size * group_width + part * part_heads * head_size
            weight = lax.dynamic_slice_in_dim(w_tile_out, start, part_heads * head_size, 0)
            final = final + dot_rows(answer, weight)
    return final.astype(jnp.bfloat16).reshape(rows, cols, width)


def solution(mesh):
    row_size, col_size = mesh.shape["rows"], mesh.shape["cols"]
    placed = (P("rows", "cols", None), P(), P(), P(), P(), P(), P(), P("rows", None, "cols", None),
              P("rows", None), P("rows", None))

    def body(*arrays):
        return shards(row_size, col_size, *arrays)

    return jax.shard_map(body, mesh=mesh, in_specs=placed, out_specs=P("rows", "cols", None), check_vma=False)
```

time: 109 us -> 94.9 us (0.87)
  the two profiles are of different devices: /device:TPU:10 before, /device:TPU:0 now
where the time goes in v2:
time: 94.9 us; the launch traced here: 94.3 us
  waiting for transfers between devices  27.1 us (29%)
  Pallas kernels  25.7 us (27%)
  starting transfers between devices  24.1 us (25%)
  blocking collectives  8.46 us (9%)
  local copies, waits for them, and re-layouts  7.58 us (8%)
    ppermute x2, waiting for transfers between devices, shards(): lax.ppermute(heads_first[:, part * part_heads:(part + 1) * part_heads], '...  16.2 us
    all_to_all x3, starting transfers between devices, swap(): lax.all_to_all(value, 'rows', split_axis=0, concat_axis=0, tiled=True, ax...  13.5 us
    pallas_call x1, Pallas kernels, front(): pl.pallas_call(functools.partial(front_kernel, groups, heads, head_size,...  8.89 us
    all_to_all x1, blocking collectives, swap(): lax.all_to_all(value, 'rows', split_axis=0, concat_axis=0, tiled=True, ax...  8.46 us
    all_to_all x3, waiting for transfers between devices, swap(): lax.all_to_all(value, 'rows', split_axis=0, concat_axis=0, tiled=True, ax...  7.86 us
    pallas_call x2, Pallas kernels, last_tiles(): pl.pallas_call(functools.partial(last_kernel, groups, first_head, heads,...  7.78 us
    ppermute x2, starting transfers between devices, shards(): lax.ppermute(heads_first[:, part * part_heads:(part + 1) * part_heads], '...  6.9 us
    unnamed x22, local copies, waits for them, and re-layouts  4.91 us
  transfers between devices with their start and end apart: 8, of which 5 were waited for; matrix products, arithmetic and copies ran while one was open for 3% of the time, Pallas kernels for 26%

profile of v2, /device:TPU:0, one launch (start us, length us, event | category | flops | bytes accessed | tf_op | source)
XLA Modules:
  0.0 94.3 jit_solution(4676420007640116401)
XLA Ops:
  0.0 1.2 %copy.38 = bf16[4,128,4,128]{3,1,2,0:T(8,128)(2,1)S(1)} copy(bf16[4,128,4,128]{3,2,1,0:T(4,128)(2,1)} %param.17) | data formatting | bytes 1048576 | tf_op args[7]
  1.3 4.1 %collective-permute-start.1 = (bf16[4,2,128,128]{3,2,1,0:T(8,128)(2,1)S(1)}, bf16[4,2,128,128]{3,2,1,0:T(8,128)(2,1)S(1)}, u32[]{:S(2)}, u32[]{:S(2)}) collective-permute-start(bf16[4,2,128,128]{3,2,1,0:T(8,128)(2,1)S(1)} %get-tuple-element.17), channel_id=1, source_target_pairs={{0,16},{2,18},{4,20},{6,22},{8,24},{10,26},{12,28},{14,30},{16,0},... | collective-permute-start | bytes 786440 | tf_op jit(solution)/shard_map/ppermute | solution.py:237
  5.9 8.5 %all_to_all.20 = s32[8,2,128]{2,1,0:T(2,128)S(1)} all-to-all(s32[8,2,128]{2,1,0:T(2,128)S(1)} %broadcast_in_dim.46), channel_id=1, replica_groups={{0,2,4,6,8,10,12,14},{16,18,20,22,24,26,28,30},{1,3,5,7,9,11,13,15},{17..., dimensions={0} | all-to-all | bytes 16384 | tf_op jit(solution)/shard_map/all_to_all | solution.py:222
  14.4 2.9 %collective-permute-done.1.tiles_ref = bf16[4,2,128,128]{3,2,1,0:T(8,128)(2,1)S(1)} collective-permute-done((bf16[4,2,128,128]{3,2,1,0:T(8,128)(2,1)S(1)}, bf16[4,2,128,128]{3,2,1,0:T(8,128)(2,1)S(1)}, u32[]{:S(2)}, u32[]{:S(2)}) %collective-permute-start.1) | collective-permute-done | bytes 262176 | tf_op jit(solution)/shard_map/ppermute | solution.py:237
  17.3 1.4 %pick.3 = bf16[8,2,128,128]{3,2,1,0:T(8,128)(2,1)} custom-call(s32[8]{0:T(128)S(1)} %get-tuple-element.22.wanted_ref, bf16[4,2,128,128]{3,2,1,0:T(8,128)(2,1)S(1)} %collective-permute-done.1.tiles_ref), custom_call_target="tpu_custom_call" | custom-call | bytes 786432 | tf_op jit(solution)/shard_map/pick/pallas_call | solution.py:39
  18.7 3.5 %all-to-all-start.1 = ((bf16[8,2,128,128]{3,2,1,0:T(8,128)(2,1)}), bf16[8,2,128,128]{3,2,1,0:T(8,128)(2,1)S(1)}, u32[]{:S(2)}, u32[]{:S(2)}) async-start(bf16[8,2,128,128]{3,2,1,0:T(8,128)(2,1)} %pick.3), calls=%async_computation.1 | async-start | bytes 1048576 | tf_op jit(solution)/shard_map/all_to_all | solution.py:222
  22.2 1.6 %pick.4 = bf16[8,4,128,128]{3,2,1,0:T(8,128)(2,1)} custom-call(s32[8]{0:T(128)S(1)} %get-tuple-element.21.wanted_ref, bf16[4,4,128,128]{3,2,1,0:T(8,128)(2,1)S(1)} %bitcast.36), custom_call_target="tpu_custom_call" | custom-call | bytes 1572864 | tf_op jit(solution)/shard_map/pick/pallas_call | solution.py:39
  23.8 7.1 %all-to-all-done.1.tiles_ref = bf16[8,2,128,128]{3,2,1,0:T(8,128)(2,1)S(1)} async-done(((bf16[8,2,128,128]{3,2,1,0:T(8,128)(2,1)}), bf16[8,2,128,128]{3,2,1,0:T(8,128)(2,1)S(1)}, u32[]{:S(2)}, u32[]{:S(2)}) %all-to-all-start.1) | async-done | bytes 524320 | tf_op jit(solution)/shard_map/all_to_all | solution.py:222
  31.0 3.6 %all-to-all-start.2 = ((bf16[8,4,128,128]{3,2,1,0:T(8,128)(2,1)}), bf16[8,4,128,128]{3,2,1,0:T(8,128)(2,1)S(1)}, u32[]{:S(2)}, u32[]{:S(2)}) async-start(bf16[8,4,128,128]{3,2,1,0:T(8,128)(2,1)} %pick.4), calls=%async_computation.2 | async-start | bytes 2097152 | tf_op jit(solution)/shard_map/all_to_all | solution.py:222
  34.6 1.6 %collective-permute-start = (bf16[192,512]{1,0:T(8,128)(2,1)S(1)}, bf16[192,512]{1,0:T(8,128)(2,1)S(1)}, u32[]{:S(2)}, u32[]{:S(2)}) collective-permute-start(bf16[192,512]{1,0:T(8,128)(2,1)S(1)} %reshape.102.refs_0_), channel_id=1, source_target_pairs={{0,1},{1,0},{2,3},{3,2},{4,5},{5,4},{6,7},{7,6},{8,9},{9,8},{10,11... | collective-permute-start | bytes 589832 | tf_op jit(solution)/shard_map/ppermute | solution.py:234
  36.2 2.8 %collective-permute-start.3 = (bf16[4,2,128,128]{3,2,1,0:T(8,128)(2,1)S(1)}, bf16[4,2,128,128]{3,2,1,0:T(8,128)(2,1)S(1)}, u32[]{:S(2)}, u32[]{:S(2)}) collective-permute-start(bf16[4,2,128,128]{3,2,1,0:T(8,128)(2,1)S(1)} %get-tuple-element.18), channel_id=1, source_target_pairs={{0,16},{2,18},{4,20},{6,22},{8,24},{10,26},{12,28},{14,30},{16,0},... | collective-permute-start | bytes 786440 | tf_op jit(solution)/shard_map/ppermute | solution.py:237
  39.1 13.3 %collective-permute-done.3.tiles_ref = bf16[4,2,128,128]{3,2,1,0:T(8,128)(2,1)S(1)} collective-permute-done((bf16[4,2,128,128]{3,2,1,0:T(8,128)(2,1)S(1)}, bf16[4,2,128,128]{3,2,1,0:T(8,128)(2,1)S(1)}, u32[]{:S(2)}, u32[]{:S(2)}) %collective-permute-start.3) | collective-permute-done | bytes 262176 | tf_op jit(solution)/shard_map/ppermute | solution.py:237
  52.4 1.4 %pick.5 = bf16[8,2,128,128]{3,2,1,0:T(8,128)(2,1)} custom-call(s32[8]{0:T(128)S(1)} %get-tuple-element.22.wanted_ref, bf16[4,2,128,128]{3,2,1,0:T(8,128)(2,1)S(1)} %collective-permute-done.3.tiles_ref), custom_call_target="tpu_custom_call" | custom-call | bytes 786432 | tf_op jit(solution)/shard_map/pick/pallas_call | solution.py:39
  54.5 1.0 %copy-done.1 = bf16[8,4,128,128]{3,2,1,0:T(8,128)(2,1)} copy-done((bf16[8,4,128,128]{3,2,1,0:T(8,128)(2,1)}, bf16[8,4,128,128]{3,2,1,0:T(8,128)(2,1)S(1)}, u32[]{:S(2)}) %copy-start.1) | copy-done | bytes 1048600
  55.5 6.4 %all-to-all-start.3 = ((bf16[8,2,128,128]{3,2,1,0:T(8,128)(2,1)}), bf16[8,2,128,128]{3,2,1,0:T(8,128)(2,1)S(1)}, u32[]{:S(2)}, u32[]{:S(2)}) async-start(bf16[8,2,128,128]{3,2,1,0:T(8,128)(2,1)} %pick.5), calls=%async_computation.3 | async-start | bytes 1048576 | tf_op jit(solution)/shard_map/all_to_all | solution.py:222
  62.2 1.0 %constant_dynamic-slice_fusion = bf16[512,256]{1,0:T(8,128)(2,1)S(1)} fusion(bf16[512,512]{1,0:T(8,128)(2,1)} %param.15, s32[]{:T(128)S(6)} %select_n.87), kind=kLoop, calls=%fused_computation.25 | loop fusion | bytes 524292 | tf_op jit(solution)/shard_map/dynamic_slice | solution.py:241
  63.9 1.4 %copy-done.3 = bf16[512,1536]{1,0:T(8,128)(2,1)S(1)} copy-done((bf16[512,1536]{1,0:T(8,128)(2,1)S(1)}, bf16[512,1536]{1,0:T(8,128)(2,1)}, u32[]{:S(2)}) %copy-start.3) | copy-done | bytes 1572888
  65.3 1.0 %copy-done.4 = bf16[512,512]{1,0:T(8,128)(2,1)S(1)} copy-done((bf16[512,512]{1,0:T(8,128)(2,1)S(1)}, bf16[512,512]{1,0:T(8,128)(2,1)}, u32[]{:S(2)}) %copy-start.4) | copy-done | bytes 524312
  66.3 8.9 %front.1 = (f32[192,512]{1,0:T(8,128)S(1)}, bf16[384,512]{1,0:T(8,128)(2,1)S(1)}) custom-call(bf16[192,512]{1,0:T(8,128)(2,1)S(1)} %reshape.102.refs_0_, bf16[192,512]{1,0:T(8,128)(2,1)S(1)} %collective-permute-done.refs_1_, f32[1,512]{1,0:T(1,128)S(1)} %bitcast.37, bf16[512,1536]{1,0:T(8,128)(2,1)S(1)} %copy-done.3, bf16[512,512]{1,0:T(8,128)(2,1)S(1)} %copy-done.4, ...), custom_call_target="tpu_custom_call" | custom-call | flops 1006632960 | bytes 4194304 | tf_op jit(solution)/shard_map/front/pallas_call | solution.py:99
  75.2 4.7 %first_tiles.1.state_ref = f32[4,384,128]{2,1,0:T(8,128)S(1)} custom-call(bf16[384,512]{1,0:T(8,128)(2,1)S(1)} %get-tuple-element.12.asked_ref, f32[384,8]{1,0:T(8,128)S(1)} %get-tuple-element.19.bias_ref, bf16[8,4,128,128]{3,2,1,0:T(8,128)(2,1)S(1)} %copy-done.2), custom_call_target="tpu_custom_call" | custom-call | flops 805306368 | bytes 4194304 | tf_op jit(solution)/shard_map/first_tiles/pallas_call | solution.py:144
  79.9 3.8 %last_tiles.2 = (bf16[192,128]{1,0:T(8,128)(2,1)S(1)}, bf16[192,128]{1,0:T(8,128)(2,1)S(1)}) custom-call(bf16[384,512]{1,0:T(8,128)(2,1)S(1)} %get-tuple-element.12.asked_ref, f32[384,8]{1,0:T(8,128)S(1)} %get-tuple-element.20.bias_ref, bf16[8,2,128,128]{3,2,1,0:T(8,128)(2,1)S(1)} %all-to-all-done.1.tiles_ref, f32[4,384,128]{2,1,0:T(8,128)S(1)} %first_tiles.1.state_ref), custom_call_target="tpu_custom_call" | custom-call | flops 402653184 | bytes 4194304 | tf_op jit(solution)/shard_map/last_tiles/pallas_call | solution.py:191
  83.7 1.6 %collective-permute-start.2 = (bf16[192,128]{1,0:T(8,128)(2,1)S(1)}, bf16[192,128]{1,0:T(8,128)(2,1)S(1)}, u32[]{:S(2)}, u32[]{:S(2)}) collective-permute-start(bf16[192,128]{1,0:T(8,128)(2,1)S(1)} %get-tuple-element.14), channel_id=1, source_target_pairs={{0,1},{1,0},{2,3},{3,2},{4,5},{5,4},{6,7},{7,6},{8,9},{9,8},{10,11... | collective-permute-start | bytes 147464 | tf_op jit(solution)/shard_map/ppermute | solution.py:258
  85.3 4.0 %last_tiles.3 = (bf16[192,128]{1,0:T(8,128)(2,1)S(1)}, bf16[192,128]{1,0:T(8,128)(2,1)S(1)}) custom-call(bf16[384,512]{1,0:T(8,128)(2,1)S(1)} %get-tuple-element.12.asked_ref, f32[384,8]{1,0:T(8,128)S(1)} %get-tuple-element.20.bias_ref, bf16[8,2,128,128]{3,2,1,0:T(8,128)(2,1)S(1)} %all-to-all-done.3.tiles_ref, f32[4,384,128]{2,1,0:T(8,128)S(1)} %first_tiles.1.state_ref), custom_call_target="tpu_custom_call" | custom-call | flops 402653184 | bytes 4194304 | tf_op jit(solution)/shard_map/last_tiles/pallas_call | solution.py:191
  90.4 3.0 %collective-permute-done.4 = bf16[192,128]{1,0:T(8,128)(2,1)S(1)} collective-permute-done((bf16[192,128]{1,0:T(8,128)(2,1)S(1)}, bf16[192,128]{1,0:T(8,128)(2,1)S(1)}, u32[]{:S(2)}, u32[]{:S(2)}) %collective-permute-start.4) | collective-permute-done | bytes 49184 | tf_op jit(solution)/shard_map/ppermute | solution.py:258
  (49 shorter events, 4.4 us)
Async XLA Ops:
  0.0 89.8 %copy-start = (bf16[512,512]{1,0:T(8,128)(2,1)S(1)}, bf16[512,512]{1,0:T(8,128)(2,1)}, u32[]{:S(2)}) copy-start(bf16[512,512]{1,0:T(8,128)(2,1)} %param.16) | copy-start | bytes 1572868
  0.0 5.4 %copy-start.9 = (s32[1,12]{1,0:T(1,128)S(1)}, s32[1,12]{1,0:T(1,128)}, u32[]{:S(2)}) copy-start(s32[1,12]{1,0:T(1,128)} %param.18) | copy-start | bytes 148
  1.3 16.1 %collective-permute-start.1 = (bf16[4,2,128,128]{3,2,1,0:T(8,128)(2,1)S(1)}, bf16[4,2,128,128]{3,2,1,0:T(8,128)(2,1)S(1)}, u32[]{:S(2)}, u32[]{:S(2)}) collective-permute-start(bf16[4,2,128,128]{3,2,1,0:T(8,128)(2,1)S(1)} %get-tuple-element.17), channel_id=1, source_target_pairs={{0,16},{2,18},{4,20},{6,22},{8,24},{10,26},{12,28},{14,30},{16,0},... | collective-permute-start | bytes 786440 | tf_op jit(solution)/shard_map/ppermute | solution.py:237
  18.7 12.3 %all-to-all-start.1 = ((bf16[8,2,128,128]{3,2,1,0:T(8,128)(2,1)}), bf16[8,2,128,128]{3,2,1,0:T(8,128)(2,1)S(1)}, u32[]{:S(2)}, u32[]{:S(2)}) async-start(bf16[8,2,128,128]{3,2,1,0:T(8,128)(2,1)} %pick.3), calls=%async_computation.1 | async-start | bytes 1048576 | tf_op jit(solution)/shard_map/all_to_all | solution.py:222
  22.2 12.3 %copy-start.7 = (bf16[48,4,512]{2,1,0:T(4,128)(2,1)S(1)}, bf16[48,4,512]{2,1,0:T(4,128)(2,1)}, u32[]{:S(2)}) copy-start(bf16[48,4,512]{2,1,0:T(4,128)(2,1)} %param.10) | copy-start | bytes 589828
  23.8 15.3 %copy-start.8 = (s32[48,12]{0,1:T(8,128)S(1)}, s32[48,12]{0,1:T(8,128)}, u32[]{:S(2)}) copy-start(s32[48,12]{0,1:T(8,128)} %param.19) | copy-start | bytes 6916
  31.0 23.6 %all-to-all-start.2 = ((bf16[8,4,128,128]{3,2,1,0:T(8,128)(2,1)}), bf16[8,4,128,128]{3,2,1,0:T(8,128)(2,1)S(1)}, u32[]{:S(2)}, u32[]{:S(2)}) async-start(bf16[8,4,128,128]{3,2,1,0:T(8,128)(2,1)} %pick.4), calls=%async_computation.2 | async-start | bytes 2097152 | tf_op jit(solution)/shard_map/all_to_all | solution.py:222
  34.6 29.2 %collective-permute-start = (bf16[192,512]{1,0:T(8,128)(2,1)S(1)}, bf16[192,512]{1,0:T(8,128)(2,1)S(1)}, u32[]{:S(2)}, u32[]{:S(2)}) collective-permute-start(bf16[192,512]{1,0:T(8,128)(2,1)S(1)} %reshape.102.refs_0_), channel_id=1, source_target_pairs={{0,1},{1,0},{2,3},{3,2},{4,5},{5,4},{6,7},{7,6},{8,9},{9,8},{10,11... | collective-permute-start | bytes 589832 | tf_op jit(solution)/shard_map/ppermute | solution.py:234
  36.2 16.2 %collective-permute-start.3 = (bf16[4,2,128,128]{3,2,1,0:T(8,128)(2,1)S(1)}, bf16[4,2,128,128]{3,2,1,0:T(8,128)(2,1)S(1)}, u32[]{:S(2)}, u32[]{:S(2)}) collective-permute-start(bf16[4,2,128,128]{3,2,1,0:T(8,128)(2,1)S(1)} %get-tuple-element.18), channel_id=1, source_target_pairs={{0,16},{2,18},{4,20},{6,22},{8,24},{10,26},{12,28},{14,30},{16,0},... | collective-permute-start | bytes 786440 | tf_op jit(solution)/shard_map/ppermute | solution.py:237
  54.5 1.0 %copy-start.1 = (bf16[8,4,128,128]{3,2,1,0:T(8,128)(2,1)}, bf16[8,4,128,128]{3,2,1,0:T(8,128)(2,1)S(1)}, u32[]{:S(2)}) copy-start(bf16[8,4,128,128]{3,2,1,0:T(8,128)(2,1)S(1)} %all-to-all-done.2.tiles_ref) | copy-start | bytes 3145732
  55.5 29.7 %all-to-all-start.3 = ((bf16[8,2,128,128]{3,2,1,0:T(8,128)(2,1)}), bf16[8,2,128,128]{3,2,1,0:T(8,128)(2,1)S(1)}, u32[]{:S(2)}, u32[]{:S(2)}) async-start(bf16[8,2,128,128]{3,2,1,0:T(8,128)(2,1)} %pick.5), calls=%async_computation.3 | async-start | bytes 1048576 | tf_op jit(solution)/shard_map/all_to_all | solution.py:222
  63.2 0.7 copy-start.5
  63.2 0.7 copy-start.6
  63.9 1.4 %copy-start.3 = (bf16[512,1536]{1,0:T(8,128)(2,1)S(1)}, bf16[512,1536]{1,0:T(8,128)(2,1)}, u32[]{:S(2)}) copy-start(bf16[512,1536]{1,0:T(8,128)(2,1)} %refs_3_.1) | copy-start | bytes 4718596
  65.3 1.0 %copy-start.4 = (bf16[512,512]{1,0:T(8,128)(2,1)S(1)}, bf16[512,512]{1,0:T(8,128)(2,1)}, u32[]{:S(2)}) copy-start(bf16[512,512]{1,0:T(8,128)(2,1)} %refs_4_.1) | copy-start | bytes 1572868
  66.3 8.9 %copy-start.2 = (bf16[8,4,128,128]{3,2,1,0:T(8,128)(2,1)S(1)}, bf16[8,4,128,128]{3,2,1,0:T(8,128)(2,1)}, u32[]{:S(2)}) copy-start(bf16[8,4,128,128]{3,2,1,0:T(8,128)(2,1)} %copy-done.1) | copy-start | bytes 3145732
  83.7 6.5 %collective-permute-start.2 = (bf16[192,128]{1,0:T(8,128)(2,1)S(1)}, bf16[192,128]{1,0:T(8,128)(2,1)S(1)}, u32[]{:S(2)}, u32[]{:S(2)}) collective-permute-start(bf16[192,128]{1,0:T(8,128)(2,1)S(1)} %get-tuple-element.14), channel_id=1, source_target_pairs={{0,1},{1,0},{2,3},{3,2},{4,5},{5,4},{6,7},{7,6},{8,9},{9,8},{10,11... | collective-permute-start | bytes 147464 | tf_op jit(solution)/shard_map/ppermute | solution.py:258
  89.2 4.1 %collective-permute-start.4 = (bf16[192,128]{1,0:T(8,128)(2,1)S(1)}, bf16[192,128]{1,0:T(8,128)(2,1)S(1)}, u32[]{:S(2)}, u32[]{:S(2)}) collective-permute-start(bf16[192,128]{1,0:T(8,128)(2,1)S(1)} %get-tuple-element.16), channel_id=1, source_target_pairs={{0,1},{1,0},{2,3},{3,2},{4,5},{5,4},{6,7},{7,6},{8,9},{9,8},{10,11... | collective-permute-start | bytes 147464 | tf_op jit(solution)/shard_map/ppermute | solution.py:258

commit v3 on v2

--- a/solution.py
+++ b/solution.py
@@ -60,24 +60,28 @@
             normed_ref[pl.ds(step * span + group * chunk, chunk), :] = rms_scale(cells, gain_col_ref[...]).astype(jnp.bfloat16)
     for part in range(3):
         packed_ref[part] = dot_rows(normed_ref[...], w_qkv_ref[:, pl.ds(part * width, width)]).astype(jnp.bfloat16)
-    row_of = lax.broadcasted_iota(jnp.int32, (span, span), 0) % chunk // cols
-    col_of = lax.broadcasted_iota(jnp.int32, (span, span), 1) % chunk // cols
+    stacked = heads * span
+    row_of = lax.broadcasted_iota(jnp.int32, (stacked, span), 0) % chunk // cols
+    col_of = lax.broadcasted_iota(jnp.int32, (stacked, span), 1) % chunk // cols
     same_row = row_of == col_of
     lane_low = lax.broadcasted_iota(jnp.int32, (span, 2 * head_size), 1) < head_size
     scale = head_size ** (-0.5)
     for step in range(steps):
         rows = pl.ds(step * span, span)
+        scores = []
+        for head in range(heads):
+            lanes = pl.ds(head // 2 * 2 * head_size, 2 * head_size)
+            query = packed_ref[0, rows, lanes]
+            query = jnp.where(lane_low == (head % 2 == 0), query, jnp.zeros_like(query))
+            scores.append(dot_lanes(query, packed_ref[1, rows, lanes]))
+        scores = jnp.where(same_row, jnp.concatenate(scores, axis=0) * scale, BIG)
+        expo = jnp.exp(scores - jnp.max(scores, axis=1, keepdims=True))
+        weights = (expo / jnp.sum(expo, axis=1, keepdims=True)).astype(jnp.bfloat16)
         for pair in range(heads // 2):
             lanes = pl.ds(pair * 2 * head_size, 2 * head_size)
-            query, keys, vals = packed_ref[0, rows, lanes], packed_ref[1, rows, lanes], packed_ref[2, rows, lanes]
-            mixed = []
-            for low in (True, False):
-                query_one = jnp.where(lane_low == low, query, jnp.zeros_like(query))
-                scores = jnp.where(same_row, dot_lanes(query_one, keys) * scale, BIG)
-                expo = jnp.exp(scores - jnp.max(scores, axis=1, keepdims=True))
-                weights = (expo / jnp.sum(expo, axis=1, keepdims=True)).astype(jnp.bfloat16)
-                mixed.append(dot_rows(weights, vals))
-            normed_ref[rows, lanes] = jnp.where(lane_low, mixed[0], mixed[1]).astype(jnp.bfloat16)
+            start = 2 * pair * span
+            mixed = dot_rows(weights[start:start + 2 * span], packed_ref[2, rows, lanes])
+            normed_ref[rows, lanes] = jnp.where(lane_low, mixed[:span], mixed[span:]).astype(jnp.bfloat16)
     delta = dot_rows(normed_ref[...], w_out_ref[...])
     for step in range(steps):
         for group in range(groups):
@@ -142,7 +146,7 @@
     rows = asked.shape[0]
     vmem = pl.BlockSpec(memory_space=pltpu.VMEM)
     return pl.pallas_call(
-        functools.partial(first_kernel, heads, 128),
+        functools.partial(first_kernel, heads, rows if rows <= 512 else 128),
         out_shape=jax.ShapeDtypeStruct((heads, rows, lanes), jnp.float32),
         in_specs=[vmem] * 3,
         out_specs=vmem,
@@ -157,9 +161,18 @@
     rows_all, lanes = asked_ref.shape[0], tiles_ref.shape[3]
     half = lanes // 2
     span = groups * chunk
-    lane_low = lax.broadcasted_iota(jnp.int32, (span, lanes), 1) < half
-    for step in range(rows_all // span):
-        rows = pl.ds(step * span, span)
+    block = rows_all if rows_all <= 512 else span
+    lane_low = lax.broadcasted_iota(jnp.int32, (block, lanes), 1) < half
+
+    def put(step, values, lane, lane_count):
+        for part in range(block // span):
+            for group in range(groups):
+                start = part * span + group * chunk
+                place = pl.ds(step * (block // groups) + part * chunk, chunk)
+                out_refs[group][place, pl.ds(lane, lane_count)] = values[start:start + chunk]
+
+    for step in range(rows_all // block):
+        rows = pl.ds(step * block, block)
         answers = []
         for head in range(heads):
             query = asked_ref[rows, pl.ds((first_head + head) * lanes, lanes)]
@@ -168,19 +181,15 @@
             old_top, old_total = state[:, 0:1], state[:, lanes // 4:lanes // 4 + 1]
             new_top = jnp.maximum(top, old_top)
             keep, add = jnp.exp(old_top - new_top), jnp.exp(top - new_top)
-            whole = old_total * keep + total * add
-            answers.append((state * keep + summed * add) / whole)
+            inverse = 1.0 / (old_total * keep + total * add)
+            answers.append(state * (keep * inverse) + summed * (add * inverse))
         if heads % 2 == 0:
             for pair in range(heads // 2):
                 low = pltpu.roll(answers[2 * pair], half, 1)
-                both = jnp.where(lane_low, low, answers[2 * pair + 1]).astype(jnp.bfloat16)
-                for group in range(groups):
-                    out_refs[group][pl.ds(step * chunk, chunk), pl.ds(pair * lanes, lanes)] = both[group * chunk:(group + 1) * chunk]
+                put(step, jnp.where(lane_low, low, answers[2 * pair + 1]).astype(jnp.bfloat16), pair * lanes, lanes)
         else:
             for head in range(heads):
-                one = answers[head][:, half:].astype(jnp.bfloat16)
-                for group in range(groups):
-                    out_refs[group][pl.ds(step * chunk, chunk), pl.ds(head * half, half)] = one[group * chunk:(group + 1) * chunk]
+                put(step, answers[head][:, half:].astype(jnp.bfloat16), head * half, half)
 
 
 def last_tiles(asked, bias, tiles, state, first_head, groups, cols):
@@ -212,8 +221,6 @@
     heads_all = width // head_size
     group_width = heads_here * head_size
     half = row_size // 2
-    parts = 2 if heads_here % 2 == 0 else 1
-    part_heads = heads_here // parts
     col_me = lax.axis_index("cols")
     my_half = lax.axis_index("rows") // half
     halves = [list(range(half)), list(range(half, row_size))]
@@ -234,8 +241,7 @@
         cells.append(lax.ppermute(cells[0], "cols", turn(col_size, -step)))
 
     heads_first = jnp.transpose(tile_kv, (0, 2, 1, 3))
-    mirrored = [lax.ppermute(heads_first[:, part * part_heads:(part + 1) * part_heads], "rows", turn(row_size, half))
-                for part in range(parts)]
+    mirrored = lax.ppermute(heads_first, "rows", turn(row_size, half))
     near = swap(pick(heads_first, asked_by[:, 0]))
 
     query_here = lax.dynamic_slice_in_dim(w_query, col_me * group_width, group_width, 1)
@@ -248,17 +254,19 @@
     bias = jnp.roll(bias, -my_half * half, axis=1)
     bias = jnp.broadcast_to(bias.reshape(rows // ROW_GROUP, 1, ROW_GROUP, 1, row_size),
                             (rows // ROW_GROUP, col_size, ROW_GROUP, cols, row_size)).reshape(-1, row_size)
-    state = first_tiles(asked, bias[:, :half], near)
+    near_bias, far_bias = bias[:, :half], bias[:, half:]
+
+    asked, residual, near, far_by, near_bias, far_bias = lax.optimization_barrier(
+        (asked, residual, near, asked_by[:, 1], near_bias, far_bias))
+    far = swap(pick(mirrored, far_by))
+    state = first_tiles(asked, near_bias, near)
+    answers = last_tiles(asked, far_bias, far, state, 0, col_size, cols)
 
     final = residual
-    for part in range(parts):
-        far = swap(pick(mirrored[part], asked_by[:, 1]))
-        answers = last_tiles(asked, bias[:, half:], far, state, part * part_heads, col_size, cols)
-        for step in range(col_size):
-            answer = lax.ppermute(answers[step], "cols", turn(col_size, step)) if step else answers[0]
-            start = (col_me - step) % col_size * group_width + part * part_heads * head_size
-            weight = lax.dynamic_slice_in_dim(w_tile_out, start, part_heads * head_size, 0)
-            final = final + dot_rows(answer, weight)
+    for step in range(col_size):
+        answer = lax.ppermute(answers[step], "cols", turn(col_size, step)) if step else answers[0]
+        start = (col_me - step) % col_size * group_width
+        final = final + dot_rows(answer, lax.dynamic_slice_in_dim(w_tile_out, start, group_width, 0))
     return final.astype(jnp.bfloat16).reshape(rows, cols, width)
 
 

time: 94.9 us -> 77.2 us (0.81)
  local copies, waits for them, and re-layouts: 7.58 us -> 18.2 us
  Pallas kernels: 25.7 us -> 16.3 us
  blocking collectives: 8.46 us -> 0 us
  waiting for transfers between devices: 27.1 us -> 20.7 us
  starting transfers between devices: 24.1 us -> 19.5 us
    ppermute x2 -> x1, waiting for transfers between devices: 16.2 us -> 0.01 us  [shards(): mirrored = lax.ppermute(heads_first, 'rows', turn(row_size, half))]
    all_to_all x3, waiting for transfers between devices: 7.86 us -> 17.8 us  [swap(): lax.all_to_all(value, 'rows', split_axis=0, concat_axis=0, tiled=True, ax...]
    all_to_all x1 -> x0, blocking collectives: 8.46 us -> none  [swap(): lax.all_to_all(value, 'rows', split_axis=0, concat_axis=0, tiled=True, ax...]
    unnamed x22 -> x38, local copies, waits for them, and re-layouts: 4.91 us -> 11.1 us
    pallas_call x1, Pallas kernels: 8.89 us -> 2.93 us  [front(): pl.pallas_call(functools.partial(front_kernel, groups, heads, head_size,...]
    ppermute x2 -> x1, starting transfers between devices: 6.9 us -> 2.65 us  [shards(): mirrored = lax.ppermute(heads_first, 'rows', turn(row_size, half))]
    pallas_call x2 -> x1, Pallas kernels: 7.78 us -> 5.05 us  [last_tiles(): pl.pallas_call(functools.partial(last_kernel, groups, first_head, heads,...]
    broadcast_in_dim x2, local copies, waits for them, and re-layouts: 0.11 us -> 1.46 us  [shards(): jnp.broadcast_to(bias.reshape(rows // ROW_GROUP, 1, ROW_GROUP, 1, row_siz...]
  transfers between devices with their start and end apart: 8 -> 6, of which waited for: 5 -> 4; matrix products, arithmetic and copies ran while one was open for 3% -> 9% of each run, Pallas kernels for 26% -> 10%
where the time goes in v3:
time: 77.2 us; the launch traced here: 76.5 us
  waiting for transfers between devices  20.7 us (27%)
  starting transfers between devices  19.5 us (25%)
  local copies, waits for them, and re-layouts  18.2 us (24%)
  Pallas kernels  16.3 us (21%)
  other arithmetic  1.09 us (1%)
    all_to_all x3, waiting for transfers between devices, swap(): lax.all_to_all(value, 'rows', split_axis=0, concat_axis=0, tiled=True, ax...  17.8 us
    all_to_all x3, starting transfers between devices, swap(): lax.all_to_all(value, 'rows', split_axis=0, concat_axis=0, tiled=True, ax...  13.7 us
    unnamed x38, local copies, waits for them, and re-layouts  11.1 us
    pallas_call x1, Pallas kernels, first_tiles(): pl.pallas_call(functools.partial(first_kernel, heads, rows if rows <= 512...  5.07 us
    pallas_call x1, Pallas kernels, last_tiles(): pl.pallas_call(functools.partial(last_kernel, groups, first_head, heads,...  5.05 us
    pallas_call x2, Pallas kernels, pick(): pl.pallas_call(functools.partial(pick_kernel, count), out_shape=jax.Shape...  3.26 us
    pallas_call x1, Pallas kernels, front(): pl.pallas_call(functools.partial(front_kernel, groups, heads, head_size,...  2.93 us
    ppermute x1, waiting for transfers between devices, shards(): lax.ppermute(answers[step], 'cols', turn(col_size, step))  2.89 us
  transfers between devices with their start and end apart: 6, of which 4 were waited for; matrix products, arithmetic and copies ran while one was open for 9% of the time, Pallas kernels for 10%

profile of v3, /device:TPU:0, one launch (start us, length us, event | category | flops | bytes accessed | tf_op | source)
XLA Modules:
  0.0 76.5 jit_solution(3646073583307519769)
XLA Ops:
  1.8 5.2 %all-to-all-start = ((s32[8,2,128]{2,1,0:T(2,128)}), s32[8,2,128]{2,1,0:T(2,128)S(1)}, u32[]{:S(2)}, u32[]{:S(2)}) async-start(s32[8,2,128]{2,1,0:T(2,128)} %broadcast_in_dim.42), calls=%async_computation | async-start | bytes 16384 | tf_op jit(solution)/shard_map/all_to_all | solution.py:229
  7.0 1.1 %copy.38 = bf16[4,128,4,128]{3,1,2,0:T(8,128)(2,1)S(1)} copy(bf16[4,128,4,128]{3,2,1,0:T(4,128)(2,1)} %param.17) | data formatting | bytes 1048576 | tf_op args[7]
  8.2 3.5 %all-to-all-done = s32[8,2,128]{2,1,0:T(2,128)S(1)} async-done(((s32[8,2,128]{2,1,0:T(2,128)}), s32[8,2,128]{2,1,0:T(2,128)S(1)}, u32[]{:S(2)}, u32[]{:S(2)}) %all-to-all-start) | async-done | bytes 8224 | tf_op jit(solution)/shard_map/all_to_all | solution.py:229
  11.8 1.6 %pick.2 = bf16[8,4,128,128]{3,2,1,0:T(8,128)(2,1)} custom-call(s32[8]{0:T(128)S(1)} %get-tuple-element.28.wanted_ref, bf16[4,4,128,128]{3,2,1,0:T(8,128)(2,1)S(1)} %bitcast.33), custom_call_target="tpu_custom_call" | custom-call | bytes 1572864 | tf_op jit(solution)/shard_map/pick/pallas_call | solution.py:39
  13.5 3.7 %all-to-all-start.1 = ((bf16[8,4,128,128]{3,2,1,0:T(8,128)(2,1)}), bf16[8,4,128,128]{3,2,1,0:T(8,128)(2,1)S(1)}, u32[]{:S(2)}, u32[]{:S(2)}) async-start(bf16[8,4,128,128]{3,2,1,0:T(8,128)(2,1)} %pick.2), calls=%async_computation.1 | async-start | bytes 2097152 | tf_op jit(solution)/shard_map/all_to_all | solution.py:229
  17.2 2.7 %collective-permute-start.1 = (bf16[4,4,128,128]{3,2,1,0:T(8,128)(2,1)S(1)}, bf16[4,4,128,128]{3,2,1,0:T(8,128)(2,1)S(1)}, u32[]{:S(2)}, u32[]{:S(2)}) collective-permute-start(bf16[4,4,128,128]{3,2,1,0:T(8,128)(2,1)S(1)} %bitcast.34), channel_id=1, source_target_pairs={{0,16},{2,18},{4,20},{6,22},{8,24},{10,26},{12,28},{14,30},{16,0},... | collective-permute-start | bytes 1572872 | tf_op jit(solution)/shard_map/ppermute | solution.py:244
  19.9 1.6 %collective-permute-start = (bf16[192,512]{1,0:T(8,128)(2,1)S(1)}, bf16[192,512]{1,0:T(8,128)(2,1)S(1)}, u32[]{:S(2)}, u32[]{:S(2)}) collective-permute-start(bf16[192,512]{1,0:T(8,128)(2,1)S(1)} %reshape.102.refs_0_), channel_id=1, source_target_pairs={{0,1},{1,0},{2,3},{3,2},{4,5},{5,4},{6,7},{7,6},{8,9},{9,8},{10,11... | collective-permute-start | bytes 589832 | tf_op jit(solution)/shard_map/ppermute | solution.py:241
  22.4 1.0 %constant_dynamic-slice_fusion = bf16[512,256]{1,0:T(8,128)(2,1)S(1)} fusion(bf16[512,512]{1,0:T(8,128)(2,1)} %param.15, s32[]{:T(128)S(6)} %select_n.77), kind=kLoop, calls=%fused_computation.19 | loop fusion | bytes 524292 | tf_op jit(solution)/shard_map/dynamic_slice | solution.py:247
  24.4 1.3 %copy.34.refs_6_ = bf16[512,512]{1,0:T(8,128)(2,1)S(1)} copy(bf16[512,512]{0,1:T(8,128)(2,1)} %bitcast.37) | data formatting | bytes 1048576 | tf_op jit(solution)/shard_map/reshape | solution.py:249
  27.9 0.9 %copy-done.2 = bf16[192,512]{1,0:T(8,128)(2,1)S(1)} copy-done((bf16[192,512]{1,0:T(8,128)(2,1)S(1)}, bf16[192,512]{1,0:T(8,128)(2,1)}, u32[]{:S(2)}) %copy-start.2) | copy-done | bytes 196632
  28.9 1.4 %copy-done.5 = bf16[512,1536]{1,0:T(8,128)(2,1)S(1)} copy-done((bf16[512,1536]{1,0:T(8,128)(2,1)S(1)}, bf16[512,1536]{1,0:T(8,128)(2,1)}, u32[]{:S(2)}) %copy-start.5) | copy-done | bytes 1572888
  30.3 1.0 %copy-done.6 = bf16[512,512]{1,0:T(8,128)(2,1)S(1)} copy-done((bf16[512,512]{1,0:T(8,128)(2,1)S(1)}, bf16[512,512]{1,0:T(8,128)(2,1)}, u32[]{:S(2)}) %copy-start.6) | copy-done | bytes 524312
  32.2 2.9 %front.1 = (f32[192,512]{1,0:T(8,128)S(1)}, bf16[384,512]{1,0:T(8,128)(2,1)S(1)}) custom-call(bf16[192,512]{1,0:T(8,128)(2,1)S(1)} %copy-done.2, bf16[192,512]{1,0:T(8,128)(2,1)S(1)} %copy-done.8, f32[1,512]{1,0:T(1,128)S(1)} %bitcast.35, bf16[512,1536]{1,0:T(8,128)(2,1)S(1)} %copy-done.5, bf16[512,512]{1,0:T(8,128)(2,1)S(1)} %copy-done.6, ...), custom_call_target="tpu_custom_call" | custom-call | flops 1006632960 | bytes 4194304 | tf_op jit(solution)/shard_map/front/pallas_call | solution.py:103
  35.9 6.9 %all-to-all-done.1.tiles_ref = bf16[8,4,128,128]{3,2,1,0:T(8,128)(2,1)S(1)} async-done(((bf16[8,4,128,128]{3,2,1,0:T(8,128)(2,1)}), bf16[8,4,128,128]{3,2,1,0:T(8,128)(2,1)S(1)}, u32[]{:S(2)}, u32[]{:S(2)}) %all-to-all-start.1) | async-done | bytes 1048608 | tf_op jit(solution)/shard_map/all_to_all | solution.py:229
  42.8 1.6 %pick.3 = bf16[8,4,128,128]{3,2,1,0:T(8,128)(2,1)} custom-call(s32[8]{0:T(128)S(1)} %get-tuple-element.20.wanted_ref, bf16[4,4,128,128]{3,2,1,0:T(8,128)(2,1)S(1)} %collective-permute-done.1.tiles_ref), custom_call_target="tpu_custom_call" | custom-call | bytes 1572864 | tf_op jit(solution)/shard_map/pick/pallas_call | solution.py:39
  44.4 4.8 %all-to-all-start.2 = ((bf16[8,4,128,128]{3,2,1,0:T(8,128)(2,1)}), bf16[8,4,128,128]{3,2,1,0:T(8,128)(2,1)S(1)}, u32[]{:S(2)}, u32[]{:S(2)}) async-start(bf16[8,4,128,128]{3,2,1,0:T(8,128)(2,1)} %pick.3), calls=%async_computation.2 | async-start | bytes 2097152 | tf_op jit(solution)/shard_map/all_to_all | solution.py:229
  49.2 1.0 %copy-done.14 = bf16[384,512]{1,0:T(8,128)(2,1)S(1)} copy-done((bf16[384,512]{1,0:T(8,128)(2,1)S(1)}, bf16[384,512]{1,0:T(8,128)(2,1)}, u32[]{:S(2)}) %copy-start.14) | copy-done | bytes 393240
  50.3 5.1 %first_tiles.1.state_ref = f32[4,384,128]{2,1,0:T(8,128)S(1)} custom-call(bf16[384,512]{1,0:T(8,128)(2,1)S(1)} %copy-done.14, f32[384,8]{1,0:T(8,128)S(1)} %copy-done.4, bf16[8,4,128,128]{3,2,1,0:T(8,128)(2,1)S(1)} %all-to-all-done.1.tiles_ref), custom_call_target="tpu_custom_call" | custom-call | flops 805306368 | bytes 4194304 | tf_op jit(solution)/shard_map/first_tiles/pallas_call | solution.py:148
  56.3 7.4 %all-to-all-done.2.tiles_ref = bf16[8,4,128,128]{3,2,1,0:T(8,128)(2,1)S(1)} async-done(((bf16[8,4,128,128]{3,2,1,0:T(8,128)(2,1)}), bf16[8,4,128,128]{3,2,1,0:T(8,128)(2,1)S(1)}, u32[]{:S(2)}, u32[]{:S(2)}) %all-to-all-start.2) | async-done | bytes 1048608 | tf_op jit(solution)/shard_map/all_to_all | solution.py:229
  63.7 1.1 %copy-done.12 = f32[4,384,128]{2,1,0:T(8,128)S(1)} copy-done((f32[4,384,128]{2,1,0:T(8,128)S(1)}, f32[4,384,128]{2,1,0:T(8,128)}, u32[]{:S(2)}) %copy-start.12) | copy-done | bytes 786456
  64.8 1.0 %copy-done.15 = bf16[384,512]{1,0:T(8,128)(2,1)S(1)} copy-done((bf16[384,512]{1,0:T(8,128)(2,1)S(1)}, bf16[384,512]{1,0:T(8,128)(2,1)}, u32[]{:S(2)}) %copy-start.15) | copy-done | bytes 393240
  65.8 5.1 %last_tiles.1 = (bf16[192,256]{1,0:T(8,128)(2,1)S(1)}, bf16[192,256]{1,0:T(8,128)(2,1)S(1)}) custom-call(bf16[384,512]{1,0:T(8,128)(2,1)S(1)} %copy-done.15, f32[384,8]{1,0:T(8,128)S(1)} %copy-done.3, bf16[8,4,128,128]{3,2,1,0:T(8,128)(2,1)S(1)} %all-to-all-done.2.tiles_ref, f32[4,384,128]{2,1,0:T(8,128)S(1)} %copy-done.12), custom_call_target="tpu_custom_call" | custom-call | flops 805306368 | bytes 4194304 | tf_op jit(solution)/shard_map/last_tiles/pallas_call | solution.py:200
  70.8 1.6 %collective-permute-start.2 = (bf16[192,256]{1,0:T(8,128)(2,1)S(1)}, bf16[192,256]{1,0:T(8,128)(2,1)S(1)}, u32[]{:S(2)}, u32[]{:S(2)}) collective-permute-start(bf16[192,256]{1,0:T(8,128)(2,1)S(1)} %get-tuple-element.24), channel_id=1, source_target_pairs={{0,1},{1,0},{2,3},{3,2},{4,5},{5,4},{6,7},{7,6},{8,9},{9,8},{10,11... | collective-permute-start | bytes 294920 | tf_op jit(solution)/shard_map/ppermute | solution.py:267
  72.6 2.9 %collective-permute-done.2 = bf16[192,256]{1,0:T(8,128)(2,1)S(1)} collective-permute-done((bf16[192,256]{1,0:T(8,128)(2,1)S(1)}, bf16[192,256]{1,0:T(8,128)(2,1)S(1)}, u32[]{:S(2)}, u32[]{:S(2)}) %collective-permute-start.2) | collective-permute-done | bytes 98336 | tf_op jit(solution)/shard_map/ppermute | solution.py:267
  (55 shorter events, 9.9 us)
Async XLA Ops:
  0.0 72.4 %copy-start = (bf16[512,512]{1,0:T(8,128)(2,1)S(1)}, bf16[512,512]{1,0:T(8,128)(2,1)}, u32[]{:S(2)}) copy-start(bf16[512,512]{1,0:T(8,128)(2,1)} %param.16) | copy-start | bytes 1572868
  1.8 9.9 %all-to-all-start = ((s32[8,2,128]{2,1,0:T(2,128)}), s32[8,2,128]{2,1,0:T(2,128)S(1)}, u32[]{:S(2)}, u32[]{:S(2)}) async-start(s32[8,2,128]{2,1,0:T(2,128)} %broadcast_in_dim.42), calls=%async_computation | async-start | bytes 16384 | tf_op jit(solution)/shard_map/all_to_all | solution.py:229
  11.8 8.0 %copy-start.16 = (bf16[48,4,512]{2,1,0:T(4,128)(2,1)S(1)}, bf16[48,4,512]{2,1,0:T(4,128)(2,1)}, u32[]{:S(2)}) copy-start(bf16[48,4,512]{2,1,0:T(4,128)(2,1)} %param.10) | copy-start | bytes 589828
  13.5 8.1 %copy-start.17 = (s32[48,12]{0,1:T(8,128)S(1)}, s32[48,12]{0,1:T(8,128)}, u32[]{:S(2)}) copy-start(s32[48,12]{0,1:T(8,128)} %param.19) | copy-start | bytes 6916
  13.5 29.3 %all-to-all-start.1 = ((bf16[8,4,128,128]{3,2,1,0:T(8,128)(2,1)}), bf16[8,4,128,128]{3,2,1,0:T(8,128)(2,1)S(1)}, u32[]{:S(2)}, u32[]{:S(2)}) async-start(bf16[8,4,128,128]{3,2,1,0:T(8,128)(2,1)} %pick.2), calls=%async_computation.1 | async-start | bytes 2097152 | tf_op jit(solution)/shard_map/all_to_all | solution.py:229
  17.2 25.6 %collective-permute-start.1 = (bf16[4,4,128,128]{3,2,1,0:T(8,128)(2,1)S(1)}, bf16[4,4,128,128]{3,2,1,0:T(8,128)(2,1)S(1)}, u32[]{:S(2)}, u32[]{:S(2)}) collective-permute-start(bf16[4,4,128,128]{3,2,1,0:T(8,128)(2,1)S(1)} %bitcast.34), channel_id=1, source_target_pairs={{0,16},{2,18},{4,20},{6,22},{8,24},{10,26},{12,28},{14,30},{16,0},... | collective-permute-start | bytes 1572872 | tf_op jit(solution)/shard_map/ppermute | solution.py:244
  19.9 6.5 %copy-start.1 = (bf16[192,512]{1,0:T(8,128)(2,1)}, bf16[192,512]{1,0:T(8,128)(2,1)S(1)}, u32[]{:S(2)}) copy-start(bf16[192,512]{1,0:T(8,128)(2,1)S(1)} %reshape.102.refs_0_) | copy-start | bytes 589828
  19.9 7.4 %collective-permute-start = (bf16[192,512]{1,0:T(8,128)(2,1)S(1)}, bf16[192,512]{1,0:T(8,128)(2,1)S(1)}, u32[]{:S(2)}, u32[]{:S(2)}) collective-permute-start(bf16[192,512]{1,0:T(8,128)(2,1)S(1)} %reshape.102.refs_0_), channel_id=1, source_target_pairs={{0,1},{1,0},{2,3},{3,2},{4,5},{5,4},{6,7},{7,6},{8,9},{9,8},{10,11... | collective-permute-start | bytes 589832 | tf_op jit(solution)/shard_map/ppermute | solution.py:241
  23.4 4.6 %copy-start.9 = (f32[512]{0:T(512)S(1)}, f32[512]{0:T(512)}, u32[]{:S(2)}) copy-start(f32[512]{0:T(512)} %param.11) | copy-start | bytes 6148
  23.4 4.6 %copy-start.10 = (f32[512]{0:T(512)S(1)}, f32[512]{0:T(512)}, u32[]{:S(2)}) copy-start(f32[512]{0:T(512)} %param.14) | copy-start | bytes 6148
  27.2 0.7 copy-start.7
  27.9 0.9 %copy-start.2 = (bf16[192,512]{1,0:T(8,128)(2,1)S(1)}, bf16[192,512]{1,0:T(8,128)(2,1)}, u32[]{:S(2)}) copy-start(bf16[192,512]{1,0:T(8,128)(2,1)} %copy-done.1) | copy-start | bytes 589828
  28.9 1.4 %copy-start.5 = (bf16[512,1536]{1,0:T(8,128)(2,1)S(1)}, bf16[512,1536]{1,0:T(8,128)(2,1)}, u32[]{:S(2)}) copy-start(bf16[512,1536]{1,0:T(8,128)(2,1)} %refs_3_.1) | copy-start | bytes 4718596
  30.3 1.0 %copy-start.6 = (bf16[512,512]{1,0:T(8,128)(2,1)S(1)}, bf16[512,512]{1,0:T(8,128)(2,1)}, u32[]{:S(2)}) copy-start(bf16[512,512]{1,0:T(8,128)(2,1)} %refs_4_.1) | copy-start | bytes 1572868
  31.3 0.9 %copy-start.8 = (bf16[192,512]{1,0:T(8,128)(2,1)S(1)}, bf16[192,512]{1,0:T(8,128)(2,1)}, u32[]{:S(2)}) copy-start(bf16[192,512]{1,0:T(8,128)(2,1)} %copy-done.7) | copy-start | bytes 589828
  35.2 0.8 copy-start.13
  42.8 6.4 %copy-start.4 = (f32[384,8]{1,0:T(8,128)S(1)}, f32[384,8]{1,0:T(8,128)}, u32[]{:S(2)}) copy-start(f32[384,8]{1,0:T(8,128)} %get-tuple-element.21.bias_ref) | copy-start | bytes 36868
  44.4 19.2 %all-to-all-start.2 = ((bf16[8,4,128,128]{3,2,1,0:T(8,128)(2,1)}), bf16[8,4,128,128]{3,2,1,0:T(8,128)(2,1)S(1)}, u32[]{:S(2)}, u32[]{:S(2)}) async-start(bf16[8,4,128,128]{3,2,1,0:T(8,128)(2,1)} %pick.3), calls=%async_computation.2 | async-start | bytes 2097152 | tf_op jit(solution)/shard_map/all_to_all | solution.py:229
  49.2 14.5 %copy-start.3 = (f32[384,8]{1,0:T(8,128)S(1)}, f32[384,8]{1,0:T(8,128)}, u32[]{:S(2)}) copy-start(f32[384,8]{1,0:T(8,128)} %get-tuple-element.19.bias_ref) | copy-start | bytes 36868
  49.2 1.0 %copy-start.14 = (bf16[384,512]{1,0:T(8,128)(2,1)S(1)}, bf16[384,512]{1,0:T(8,128)(2,1)}, u32[]{:S(2)}) copy-start(bf16[384,512]{1,0:T(8,128)(2,1)} %copy-done.13) | copy-start | bytes 1179652
  55.4 0.9 %copy-start.11 = (f32[4,384,128]{2,1,0:T(8,128)}, f32[4,384,128]{2,1,0:T(8,128)S(1)}, u32[]{:S(2)}) copy-start(f32[4,384,128]{2,1,0:T(8,128)S(1)} %first_tiles.1.state_ref) | copy-start | bytes 2359300
  63.7 1.1 %copy-start.12 = (f32[4,384,128]{2,1,0:T(8,128)S(1)}, f32[4,384,128]{2,1,0:T(8,128)}, u32[]{:S(2)}) copy-start(f32[4,384,128]{2,1,0:T(8,128)} %copy-done.11) | copy-start | bytes 2359300
  64.8 1.0 %copy-start.15 = (bf16[384,512]{1,0:T(8,128)(2,1)S(1)}, bf16[384,512]{1,0:T(8,128)(2,1)}, u32[]{:S(2)}) copy-start(bf16[384,512]{1,0:T(8,128)(2,1)} %copy-done.13) | copy-start | bytes 1179652
  70.8 4.7 %collective-permute-start.2 = (bf16[192,256]{1,0:T(8,128)(2,1)S(1)}, bf16[192,256]{1,0:T(8,128)(2,1)S(1)}, u32[]{:S(2)}, u32[]{:S(2)}) collective-permute-start(bf16[192,256]{1,0:T(8,128)(2,1)S(1)} %get-tuple-element.24), channel_id=1, source_target_pairs={{0,1},{1,0},{2,3},{3,2},{4,5},{5,4},{6,7},{7,6},{8,9},{9,8},{10,11... | collective-permute-start | bytes 294920 | tf_op jit(solution)/shard_map/ppermute | solution.py:267

commit v4 on v3

v4 whole, which is shorter than its diff:
```python
import functools

import jax
import jax.numpy as jnp
from jax import lax
from jax.experimental import pallas as pl
from jax.experimental.pallas import tpu as pltpu
from jax.sharding import PartitionSpec as P

ROW_GROUP = 16
BIG = -1e30
MIB = 1024 * 1024
VMEM = pl.BlockSpec(memory_space=pltpu.VMEM)


def params(rows):
    return pltpu.CompilerParams(vmem_limit_bytes=(14 if rows <= 512 else 48) * MIB)


def dot_rows(left, right):
    return lax.dot_general(left, right, (((1,), (0,)), ((), ())), preferred_element_type=jnp.float32)


def dot_lanes(left, right):
    return lax.dot_general(left, right, (((1,), (1,)), ((), ())), preferred_element_type=jnp.float32)


def rms_scale(values, gain_vec):
    mean_sq = jnp.mean(values * values, axis=-1, keepdims=True)
    return values * lax.rsqrt(mean_sq + 1e-05) * gain_vec


def iota(shape, dim):
    return lax.broadcasted_iota(jnp.int32, shape, dim)


def pick_kernel(count, wanted_ref, tiles_ref, out_ref):
    for peer in range(count):
        out_ref[peer] = tiles_ref[wanted_ref[peer]]


def pick(tiles, wanted):
    count = wanted.shape[0]
    return pl.pallas_call(
        functools.partial(pick_kernel, count),
        out_shape=jax.ShapeDtypeStruct((count,) + tiles.shape[1:], tiles.dtype),
        in_specs=[pl.BlockSpec(memory_space=pltpu.SMEM), VMEM],
        out_specs=VMEM,
        compiler_params=params(0),
        cost_estimate=pl.CostEstimate(flops=0, bytes_accessed=2 * MIB, transcendentals=0),
        name="pick",
    )(wanted, tiles)


def front_kernel(groups, heads, head_size, chunk, cols, row_size, *refs):
    cell_refs, refs = refs[:groups], refs[groups:]
    (holder_ref, mask_ref, gain_col_ref, w_qkv_ref, w_out_ref, gain_tile_ref, w_query_ref,
     resid_ref, asked_ref, normed_ref, packed_ref) = refs
    own_rows, width = cell_refs[0].shape
    steps = own_rows // chunk
    span = groups * chunk
    lanes_two = 2 * head_size
    for step in range(steps):
        for group in range(groups):
            cells = cell_refs[group][pl.ds(step * chunk, chunk), :].astype(jnp.float32)
            normed_ref[pl.ds(step * span + group * chunk, chunk), :] = rms_scale(cells, gain_col_ref[...]).astype(jnp.bfloat16)
    for part in range(3):
        packed_ref[part] = dot_rows(normed_ref[...], w_qkv_ref[:, pl.ds(part * width, width)]).astype(jnp.bfloat16)
    stacked = heads * span
    same_row = iota((stacked, span), 0) % chunk // cols == iota((stacked, span), 1) % chunk // cols
    lane_low = iota((span, lanes_two), 1) < head_size
    scale = head_size ** (-0.5)
    for step in range(steps):
        rows = pl.ds(step * span, span)
        scores = []
        for head in range(heads):
            lanes = pl.ds(head // 2 * lanes_two, lanes_two)
            query = packed_ref[0, rows, lanes]
            query = jnp.where(lane_low == (head % 2 == 0), query, jnp.zeros_like(query))
            scores.append(dot_lanes(query, packed_ref[1, rows, lanes]))
        scores = jnp.where(same_row, jnp.concatenate(scores, axis=0) * scale, BIG)
        expo = jnp.exp(scores - jnp.max(scores, axis=1, keepdims=True))
        weights = (expo / jnp.sum(expo, axis=1, keepdims=True)).astype(jnp.bfloat16)
        for pair in range(heads // 2):
            lanes = pl.ds(pair * lanes_two, lanes_two)
            start = 2 * pair * span
            mixed = dot_rows(weights[start:start + 2 * span], packed_ref[2, rows, lanes])
            normed_ref[rows, lanes] = jnp.where(lane_low, mixed[:span], mixed[span:]).astype(jnp.bfloat16)
    delta = dot_rows(normed_ref[...], w_out_ref[...])
    for step in range(steps):
        for group in range(groups):
            start = step * span + group * chunk
            resid = cell_refs[group][pl.ds(step * chunk, chunk), :].astype(jnp.float32) + delta[start:start + chunk]
            if group == 0:
                resid_ref[pl.ds(step * chunk, chunk), :] = resid
            normed_ref[pl.ds(start, chunk), :] = rms_scale(resid, gain_tile_ref[...]).astype(jnp.bfloat16)
    slots = mask_ref.shape[1]
    place = (holder_ref[...] + head_size == iota((slots, lanes_two), 1)).astype(jnp.bfloat16)
    live = dot_rows((mask_ref[...] > 0).astype(jnp.bfloat16), place)
    lane = iota(live.shape, 1)
    shut = jnp.where((lane >= head_size) & (lane < head_size + row_size) & (live < 0.5), 1.0, 0.0).astype(jnp.bfloat16)
    total = steps * span
    cell = iota((total, shut.shape[0]), 0)
    row_of = cell // span * (chunk // cols) + cell % chunk // cols
    spread = (row_of == iota((total, shut.shape[0]), 1)).astype(jnp.bfloat16)
    bias = dot_rows(spread, shut) * BIG
    asked = dot_rows(normed_ref[...], w_query_ref[...]).astype(jnp.bfloat16).astype(jnp.float32) * scale
    heads_here = asked.shape[1] // head_size
    low = iota((total, lanes_two), 1) < head_size
    for head in range(heads_here):
        if heads_here % 2 == 0:
            two = asked[:, head // 2 * lanes_two:(head // 2 + 1) * lanes_two]
            one = two if head % 2 == 0 else pltpu.roll(two, head_size, 1)
            query = jnp.where(low, one, bias)
        else:
            one = asked[:, head * head_size:(head + 1) * head_size]
            query = jnp.concatenate([one, bias[:, head_size:]], axis=1)
        asked_ref[:, pl.ds(head * lanes_two, lanes_two)] = query.astype(jnp.bfloat16)


def front(cells, holder, key_mask, gain_col, w_qkv, w_out, gain_tile, w_query, heads, head_size, cols, row_size):
    groups = len(cells)
    own_rows, width = cells[0].shape
    total = groups * own_rows
    asked_width = 2 * w_query.shape[1]
    return pl.pallas_call(
        functools.partial(front_kernel, groups, heads, head_size, ROW_GROUP * cols, cols, row_size),
        out_shape=(jax.ShapeDtypeStruct((own_rows, width), jnp.float32),
                   jax.ShapeDtypeStruct((total, asked_width), jnp.bfloat16)),
        in_specs=[VMEM] * (groups + 7),
        out_specs=(VMEM, VMEM),
        scratch_shapes=[pltpu.VMEM((total, width), jnp.bfloat16), pltpu.VMEM((3, total, width), jnp.bfloat16)],
        compiler_params=params(total),
        cost_estimate=pl.CostEstimate(flops=2 * total * width * (4 * width + asked_width), bytes_accessed=4 * MIB,
                                      transcendentals=total * heads * 128),
        name="front",
    )(*cells, holder, key_mask, gain_col.reshape(1, width), w_qkv, w_out, gain_tile.reshape(1, width), w_query)


def weigh(query, tiles, first_holder):
    slots, keys, lanes = tiles.shape
    half = lanes // 2
    lane = iota(tiles.shape, 2)
    slot = iota(tiles.shape, 0)
    marks = (lane == slot + (half + first_holder)).astype(tiles.dtype)
    key_part = jnp.where(lane < half, tiles, marks).reshape(slots * keys, lanes)
    val_part = jnp.where(lane < half, jnp.ones_like(tiles), tiles).reshape(slots * keys, lanes)
    scores = dot_lanes(query, key_part)
    top = jnp.max(scores, axis=1, keepdims=True)
    return top, dot_rows(jnp.exp(scores - top).astype(jnp.bfloat16), val_part)


def first_kernel(heads, block, asked_ref, tiles_ref, sums_ref, tops_ref):
    rows_all, lanes = asked_ref.shape[0], tiles_ref.shape[3]
    lane = iota((block, lanes), 1)
    for step in range(rows_all // block):
        rows = pl.ds(step * block, block)
        tops = jnp.zeros((block, lanes), jnp.float32)
        for head in range(heads):
            top, sums_ref[head, rows, :] = weigh(asked_ref[rows, pl.ds(head * lanes, lanes)], tiles_ref[:, head], 0)
            tops = jnp.where(lane == head, top, tops)
        tops_ref[rows, :] = tops


def first_tiles(asked, tiles):
    slots, heads, keys, lanes = tiles.shape
    rows = asked.shape[0]
    return pl.pallas_call(
        functools.partial(first_kernel, heads, rows if rows <= 512 else 128),
        out_shape=(jax.ShapeDtypeStruct((heads, rows, lanes), jnp.float32), jax.ShapeDtypeStruct((rows, lanes), jnp.float32)),
        in_specs=[VMEM] * 2,
        out_specs=(VMEM, VMEM),
        compiler_params=params(rows),
        cost_estimate=pl.CostEstimate(flops=4 * rows * heads * slots * keys * lanes, bytes_accessed=4 * MIB,
                                      transcendentals=rows * heads * slots * keys),
        name="first_tiles",
    )(asked, tiles)


def last_kernel(groups, first_holder, first_head, heads, chunk, asked_ref, tiles_ref, sums_ref, tops_ref, *out_refs):
    rows_all, lanes = asked_ref.shape[0], tiles_ref.shape[3]
    half = lanes // 2
    span = groups * chunk
    block = rows_all if rows_all <= 512 else span
    lane_low = iota((block, lanes), 1) < half

    def put(step, values, lane, lane_count):
        for part in range(block // span):
            for group in range(groups):
                start = part * span + group * chunk
                place = pl.ds(step * (block // groups) + part * chunk, chunk)
                out_refs[group][place, pl.ds(lane, lane_count)] = values[start:start + chunk]

    for step in range(rows_all // block):
        rows = pl.ds(step * block, block)
        low = None
        for head in range(heads):
            here = first_head + head
            top, sums = weigh(asked_ref[rows, pl.ds(here * lanes, lanes)], tiles_ref[:, head], first_holder)
            old_top = tops_ref[rows, here:here + 1]
            new_top = jnp.maximum(top, old_top)
            sums = sums_ref[here, rows, :] * jnp.exp(old_top - new_top) + sums * jnp.exp(top - new_top)
            turned = pltpu.roll(sums, half, 1)
            if heads % 2:
                put(step, (sums / turned)[:, half:].astype(jnp.bfloat16), head * half, half)
            elif head % 2 == 0:
                low = turned / sums
            else:
                put(step, jnp.where(lane_low, low, sums / turned).astype(jnp.bfloat16), head // 2 * lanes, lanes)


def last_tiles(asked, tiles, sums, tops, first_holder, first_head, groups, cols):
    slots, heads, keys, lanes = tiles.shape
    rows = asked.shape[0]
    out = jax.ShapeDtypeStruct((rows // groups, heads * lanes // 2), jnp.bfloat16)
    return pl.pallas_call(
        functools.partial(last_kernel, groups, first_holder, first_head, heads, ROW_GROUP * cols),
        out_shape=(out,) * groups,
        in_specs=[VMEM] * 4,
        out_specs=(VMEM,) * groups,
        compiler_params=params(rows),
        cost_estimate=pl.CostEstimate(flops=4 * rows * heads * slots * keys * lanes, bytes_accessed=4 * MIB,
                                      transcendentals=rows * heads * slots * keys),
        name="last_tiles",
    )(asked, tiles, sums, tops)


def turn(size, step):
    return [(src, (src + step) % size) for src in range(size)]


def shards(row_size, col_size, fact_cells, gain_col, w_qkv, w_col_out, gain_tile, w_query, w_tile_out,
           tile_kv, tile_ids, key_mask):
    rows, cols, width = fact_cells.shape
    tiles_here, keys, heads_here, lanes = tile_kv.shape
    head_size = lanes // 2
    heads_all = width // head_size
    group_width = heads_here * head_size
    half = row_size // 2
    col_me = lax.axis_index("cols")
    my_half = lax.axis_index("rows") // half
    halves = [list(range(half)), list(range(half, row_size))]
    assert row_size <= head_size and row_size % 2 == 0

    def swap(value):
        return lax.all_to_all(value, "rows", split_axis=0, concat_axis=0, tiled=True, axis_index_groups=halves)

    heads_first = jnp.transpose(tile_kv, (0, 2, 1, 3))
    mirrored = lax.ppermute(heads_first, "rows", turn(row_size, half))

    listed = tile_ids[0] >= 0
    holder = jnp.where(listed, (tile_ids[0] // tiles_here + my_half * half) % row_size, -1)
    wanted = jnp.sum(jnp.where(holder[:, None] == jnp.arange(row_size)[None, :], (tile_ids[0] % tiles_here)[:, None], 0), axis=0)
    asked_of = jnp.broadcast_to(wanted.astype(jnp.int32).reshape(2, half).T[:, :, None], (half, 2, 128))
    asked_by = swap(asked_of)[:, :, 0]

    cells = [fact_cells.reshape(rows * cols, width)]
    for step in range(1, col_size):
        cells.append(lax.ppermute(cells[0], "cols", turn(col_size, -step)))

    near = swap(pick(heads_first, asked_by[:, 0]))
    mirrored, near = lax.optimization_barrier((mirrored, near))
    far_sent = pick(mirrored, asked_by[:, 1])

    cells, far_sent = lax.optimization_barrier((cells, far_sent))
    far = swap(far_sent)
    query_here = lax.dynamic_slice_in_dim(w_query, col_me * group_width, group_width, 1)
    residual, asked = front(cells, holder[:, None], key_mask, gain_col, w_qkv, w_col_out, gain_tile, query_here,
                            heads_all, head_size, cols, row_size)
    sums, tops = first_tiles(asked, near)
    answers = last_tiles(asked, far, sums, tops, half, 0, col_size, cols)

    final = residual
    for step in range(col_size):
        answer = lax.ppermute(answers[step], "cols", turn(col_size, step)) if step else answers[0]
        start = (col_me - step) % col_size * group_width
        final = final + dot_rows(answer, lax.dynamic_slice_in_dim(w_tile_out, start, group_width, 0))
    return final.astype(jnp.bfloat16).reshape(rows, cols, width)


def solution(mesh):
    row_size, col_size = mesh.shape["rows"], mesh.shape["cols"]
    placed = (P("rows", "cols", None), P(), P(), P(), P(), P(), P(), P("rows", None, "cols", None),
              P("rows", None), P("rows", None))

    def body(*arrays):
        return shards(row_size, col_size, *arrays)

    return jax.shard_map(body, mesh=mesh, in_specs=placed, out_specs=P("rows", "cols", None), check_vma=False)
```

time: 77.2 us -> 74.3 us (0.962)
  waiting for transfers between devices: 20.7 us -> 31.4 us
  local copies, waits for them, and re-layouts: 18.2 us -> 10.3 us
  Pallas kernels: 16.3 us -> 11.2 us
    ppermute x1, waiting for transfers between devices: 0.01 us -> 19.3 us  [shards(): mirrored = lax.ppermute(heads_first, 'rows', turn(row_size, half))]
    all_to_all x3, waiting for transfers between devices: 17.8 us -> 9.21 us  [swap(): lax.all_to_all(value, 'rows', split_axis=0, concat_axis=0, tiled=True, ax...]
    unnamed x38 -> x26, local copies, waits for them, and re-layouts: 11.1 us -> 7.47 us
    pallas_call x1, Pallas kernels: 5.07 us -> 2.38 us  [first_tiles(): pl.pallas_call(functools.partial(first_kernel, heads, rows if rows <= 512...]
    pallas_call x1, Pallas kernels: 5.05 us -> 2.51 us  [last_tiles(): pl.pallas_call(functools.partial(last_kernel, groups, first_holder, first...]
    broadcast_in_dim x3 -> x1, local copies, waits for them, and re-layouts: 2.14 us -> 0.68 us  [shards(): jnp.broadcast_to(wanted.astype(jnp.int32).reshape(2, half).T[:, :, None],...]
    reshape x2 -> x1, local copies, waits for them, and re-layouts: 1.34 us -> 0.08 us  [shards(): wanted.astype(jnp.int32).reshape(2, half).T[:, :, None]]
    pad x1 -> x0, local copies, waits for them, and re-layouts: 0.86 us -> none  [shards(): jnp.pad(query_here.reshape(width, heads_here, head_size), ((0, 0), (0, 0)...]
  transfers between devices with their start and end apart: 6 -> 6, of which waited for: 4 -> 5; matrix products, arithmetic and copies ran while one was open for 9% -> 3% of each run, Pallas kernels for 10% -> 10%
where the time goes in v4:
time: 74.3 us; the launch traced here: 73.8 us
  waiting for transfers between devices  31.4 us (42%)
  starting transfers between devices  19.5 us (26%)
  Pallas kernels  11.2 us (15%)
  local copies, waits for them, and re-layouts  10.3 us (14%)
  other arithmetic  0.84 us (1%)
    ppermute x1, waiting for transfers between devices, shards(): mirrored = lax.ppermute(heads_first, 'rows', turn(row_size, half))  19.3 us
    all_to_all x3, starting transfers between devices, swap(): lax.all_to_all(value, 'rows', split_axis=0, concat_axis=0, tiled=True, ax...  13.7 us
    all_to_all x3, waiting for transfers between devices, swap(): lax.all_to_all(value, 'rows', split_axis=0, concat_axis=0, tiled=True, ax...  9.21 us
    unnamed x26, local copies, waits for them, and re-layouts  7.47 us
    pallas_call x2, Pallas kernels, pick(): pl.pallas_call(functools.partial(pick_kernel, count), out_shape=jax.Shape...  3.22 us
    pallas_call x1, Pallas kernels, front(): pl.pallas_call(functools.partial(front_kernel, groups, heads, head_size,...  3.11 us
    ppermute x1, waiting for transfers between devices, shards(): lax.ppermute(answers[step], 'cols', turn(col_size, step))  2.89 us
    ppermute x1, starting transfers between devices, shards(): mirrored = lax.ppermute(heads_first, 'rows', turn(row_size, half))  2.65 us
  transfers between devices with their start and end apart: 6, of which 5 were waited for; matrix products, arithmetic and copies ran while one was open for 3% of the time, Pallas kernels for 10%

profile of v4, /device:TPU:0, one launch (start us, length us, event | category | flops | bytes accessed | tf_op | source)
XLA Modules:
  0.0 73.8 jit_solution(7800850580297702202)
XLA Ops:
  1.7 5.2 %all-to-all-start = ((s32[8,2,128]{2,1,0:T(2,128)}), s32[8,2,128]{2,1,0:T(2,128)S(1)}, u32[]{:S(2)}, u32[]{:S(2)}) async-start(s32[8,2,128]{2,1,0:T(2,128)} %broadcast_in_dim.26), calls=%async_computation | async-start | bytes 16384 | tf_op jit(solution)/shard_map/all_to_all | solution.py:246
  6.9 1.1 %copy.37 = bf16[4,128,4,128]{3,1,2,0:T(8,128)(2,1)S(1)} copy(bf16[4,128,4,128]{3,2,1,0:T(4,128)(2,1)} %param.17) | data formatting | bytes 1048576 | tf_op args[7]
  8.0 3.5 %all-to-all-done = s32[8,2,128]{2,1,0:T(2,128)S(1)} async-done(((s32[8,2,128]{2,1,0:T(2,128)}), s32[8,2,128]{2,1,0:T(2,128)S(1)}, u32[]{:S(2)}, u32[]{:S(2)}) %all-to-all-start) | async-done | bytes 8224 | tf_op jit(solution)/shard_map/all_to_all | solution.py:246
  11.7 1.6 %pick.2 = bf16[8,4,128,128]{3,2,1,0:T(8,128)(2,1)} custom-call(s32[8]{0:T(128)S(1)} %get-tuple-element.27.wanted_ref, bf16[4,4,128,128]{3,2,1,0:T(8,128)(2,1)S(1)} %bitcast.33), custom_call_target="tpu_custom_call" | custom-call | bytes 2097152 | tf_op jit(solution)/shard_map/pick/pallas_call | solution.py:44
  13.3 3.6 %all-to-all-start.1 = ((bf16[8,4,128,128]{3,2,1,0:T(8,128)(2,1)}), bf16[8,4,128,128]{3,2,1,0:T(8,128)(2,1)S(1)}, u32[]{:S(2)}, u32[]{:S(2)}) async-start(bf16[8,4,128,128]{3,2,1,0:T(8,128)(2,1)} %pick.2), calls=%async_computation.1 | async-start | bytes 2097152 | tf_op jit(solution)/shard_map/all_to_all | solution.py:246
  16.9 2.7 %collective-permute-start.1 = (bf16[4,4,128,128]{3,2,1,0:T(8,128)(2,1)S(1)}, bf16[4,4,128,128]{3,2,1,0:T(8,128)(2,1)S(1)}, u32[]{:S(2)}, u32[]{:S(2)}) collective-permute-start(bf16[4,4,128,128]{3,2,1,0:T(8,128)(2,1)S(1)} %bitcast.34), channel_id=1, source_target_pairs={{0,16},{2,18},{4,20},{6,22},{8,24},{10,26},{12,28},{14,30},{16,0},... | collective-permute-start | bytes 1572872 | tf_op jit(solution)/shard_map/ppermute | solution.py:249
  19.6 1.6 %collective-permute-start = (bf16[192,512]{1,0:T(8,128)(2,1)S(1)}, bf16[192,512]{1,0:T(8,128)(2,1)S(1)}, u32[]{:S(2)}, u32[]{:S(2)}) collective-permute-start(bf16[192,512]{1,0:T(8,128)(2,1)S(1)} %reshape.160.refs_0_), channel_id=1, source_target_pairs={{0,1},{1,0},{2,3},{3,2},{4,5},{5,4},{6,7},{7,6},{8,9},{9,8},{10,11... | collective-permute-start | bytes 589832 | tf_op jit(solution)/shard_map/ppermute | solution.py:259
  21.2 19.3 %collective-permute-done.1.tiles_ref = bf16[4,4,128,128]{3,2,1,0:T(8,128)(2,1)S(1)} collective-permute-done((bf16[4,4,128,128]{3,2,1,0:T(8,128)(2,1)S(1)}, bf16[4,4,128,128]{3,2,1,0:T(8,128)(2,1)S(1)}, u32[]{:S(2)}, u32[]{:S(2)}) %collective-permute-start.1) | collective-permute-done | bytes 524320 | tf_op jit(solution)/shard_map/ppermute | solution.py:249
  40.4 2.0 %all-to-all-done.1.tiles_ref = bf16[8,4,128,128]{3,2,1,0:T(8,128)(2,1)S(1)} async-done(((bf16[8,4,128,128]{3,2,1,0:T(8,128)(2,1)}), bf16[8,4,128,128]{3,2,1,0:T(8,128)(2,1)S(1)}, u32[]{:S(2)}, u32[]{:S(2)}) %all-to-all-start.1) | async-done | bytes 1048608 | tf_op jit(solution)/shard_map/all_to_all | solution.py:246
  42.5 1.6 %pick.3 = bf16[8,4,128,128]{3,2,1,0:T(8,128)(2,1)} custom-call(s32[8]{0:T(128)S(1)} %get-tuple-element.28.wanted_ref, bf16[4,4,128,128]{3,2,1,0:T(8,128)(2,1)S(1)} %collective-permute-done.1.tiles_ref), custom_call_target="tpu_custom_call" | custom-call | bytes 2097152 | tf_op jit(solution)/shard_map/pick/pallas_call | solution.py:44
  44.1 4.9 %all-to-all-start.2 = ((bf16[8,4,128,128]{3,2,1,0:T(8,128)(2,1)}), bf16[8,4,128,128]{3,2,1,0:T(8,128)(2,1)S(1)}, u32[]{:S(2)}, u32[]{:S(2)}) async-start(bf16[8,4,128,128]{3,2,1,0:T(8,128)(2,1)} %pick.3), calls=%async_computation.2 | async-start | bytes 2097152 | tf_op jit(solution)/shard_map/all_to_all | solution.py:246
  49.2 1.0 %constant_dynamic-slice_fusion.refs_8_ = bf16[512,256]{1,0:T(8,128)(2,1)S(1)} fusion(bf16[512,512]{1,0:T(8,128)(2,1)} %param.15, s32[]{:T(128)S(6)} %select_n.90), kind=kLoop, calls=%fused_computation.31 | loop fusion | bytes 524292 | tf_op jit(solution)/shard_map/dynamic_slice | solution.py:267
  50.2 1.4 %copy-done.1 = bf16[512,1536]{1,0:T(8,128)(2,1)S(1)} copy-done((bf16[512,1536]{1,0:T(8,128)(2,1)S(1)}, bf16[512,1536]{1,0:T(8,128)(2,1)}, u32[]{:S(2)}) %copy-start.1) | copy-done | bytes 1572888
  51.6 1.0 %copy-done.2 = bf16[512,512]{1,0:T(8,128)(2,1)S(1)} copy-done((bf16[512,512]{1,0:T(8,128)(2,1)S(1)}, bf16[512,512]{1,0:T(8,128)(2,1)}, u32[]{:S(2)}) %copy-start.2) | copy-done | bytes 524312
  52.7 3.1 %front.1 = (f32[192,512]{1,0:T(8,128)S(1)}, bf16[384,512]{1,0:T(8,128)(2,1)S(1)}) custom-call(bf16[192,512]{1,0:T(8,128)(2,1)S(1)} %reshape.160.refs_0_, bf16[192,512]{1,0:T(8,128)(2,1)S(1)} %collective-permute-done.refs_1_, s32[12,1]{1,0:T(8,128)S(1)} %fusion.7.refs_2_, s32[48,12]{1,0:T(8,128)S(1)} %copy.35.refs_3_, f32[1,512]{1,0:T(1,128)S(1)} %bitcast.35, ...), custom_call_target="tpu_custom_call" | custom-call | flops 1006632960 | bytes 4194304 | tf_op jit(solution)/shard_map/front/pallas_call | solution.py:126
  55.8 2.4 %first_tiles.1 = (f32[4,384,128]{2,1,0:T(8,128)S(1)}, f32[384,128]{1,0:T(8,128)S(1)}) custom-call(bf16[384,512]{1,0:T(8,128)(2,1)S(1)} %get-tuple-element.20.asked_ref, bf16[8,4,128,128]{3,2,1,0:T(8,128)(2,1)S(1)} %all-to-all-done.1.tiles_ref), custom_call_target="tpu_custom_call" | custom-call | flops 805306368 | bytes 4194304 | tf_op jit(solution)/shard_map/first_tiles/pallas_call | solution.py:168
  58.2 0.9 %copy-done.5 = f32[4,384,128]{2,1,0:T(8,128)} copy-done((f32[4,384,128]{2,1,0:T(8,128)}, f32[4,384,128]{2,1,0:T(8,128)S(1)}, u32[]{:S(2)}) %copy-start.5) | copy-done | bytes 786456
  59.1 0.7 %copy-done.7 = bf16[384,512]{1,0:T(8,128)(2,1)} copy-done((bf16[384,512]{1,0:T(8,128)(2,1)}, bf16[384,512]{1,0:T(8,128)(2,1)S(1)}, u32[]{:S(2)}) %copy-start.7) | copy-done | bytes 393240
  59.8 3.6 %all-to-all-done.2.tiles_ref = bf16[8,4,128,128]{3,2,1,0:T(8,128)(2,1)S(1)} async-done(((bf16[8,4,128,128]{3,2,1,0:T(8,128)(2,1)}), bf16[8,4,128,128]{3,2,1,0:T(8,128)(2,1)S(1)}, u32[]{:S(2)}, u32[]{:S(2)}) %all-to-all-start.2) | async-done | bytes 1048608 | tf_op jit(solution)/shard_map/all_to_all | solution.py:246
  63.5 1.1 %copy-done.6 = f32[4,384,128]{2,1,0:T(8,128)S(1)} copy-done((f32[4,384,128]{2,1,0:T(8,128)S(1)}, f32[4,384,128]{2,1,0:T(8,128)}, u32[]{:S(2)}) %copy-start.6) | copy-done | bytes 786456
  64.6 1.0 %copy-done.8 = bf16[384,512]{1,0:T(8,128)(2,1)S(1)} copy-done((bf16[384,512]{1,0:T(8,128)(2,1)S(1)}, bf16[384,512]{1,0:T(8,128)(2,1)}, u32[]{:S(2)}) %copy-start.8) | copy-done | bytes 393240
  65.6 2.5 %last_tiles.1 = (bf16[192,256]{1,0:T(8,128)(2,1)S(1)}, bf16[192,256]{1,0:T(8,128)(2,1)S(1)}) custom-call(bf16[384,512]{1,0:T(8,128)(2,1)S(1)} %copy-done.8, bf16[8,4,128,128]{3,2,1,0:T(8,128)(2,1)S(1)} %all-to-all-done.2.tiles_ref, f32[4,384,128]{2,1,0:T(8,128)S(1)} %copy-done.6, f32[384,128]{1,0:T(8,128)S(1)} %get-tuple-element.24.tops_ref), custom_call_target="tpu_custom_call" | custom-call | flops 805306368 | bytes 4194304 | tf_op jit(solution)/shard_map/last_tiles/pallas_call | solution.py:216
  68.1 1.6 %collective-permute-start.2 = (bf16[192,256]{1,0:T(8,128)(2,1)S(1)}, bf16[192,256]{1,0:T(8,128)(2,1)S(1)}, u32[]{:S(2)}, u32[]{:S(2)}) collective-permute-start(bf16[192,256]{1,0:T(8,128)(2,1)S(1)} %get-tuple-element.26), channel_id=1, source_target_pairs={{0,1},{1,0},{2,3},{3,2},{4,5},{5,4},{6,7},{7,6},{8,9},{9,8},{10,11... | collective-permute-start | bytes 294920 | tf_op jit(solution)/shard_map/ppermute | solution.py:275
  69.9 2.9 %collective-permute-done.2 = bf16[192,256]{1,0:T(8,128)(2,1)S(1)} collective-permute-done((bf16[192,256]{1,0:T(8,128)(2,1)S(1)}, bf16[192,256]{1,0:T(8,128)(2,1)S(1)}, u32[]{:S(2)}, u32[]{:S(2)}) %collective-permute-start.2) | collective-permute-done | bytes 98336 | tf_op jit(solution)/shard_map/ppermute | solution.py:275
  (33 shorter events, 3.2 us)
Async XLA Ops:
  0.0 69.7 %copy-start = (bf16[512,512]{1,0:T(8,128)(2,1)S(1)}, bf16[512,512]{1,0:T(8,128)(2,1)}, u32[]{:S(2)}) copy-start(bf16[512,512]{1,0:T(8,128)(2,1)} %param.16) | copy-start | bytes 1572868
  1.7 9.9 %all-to-all-start = ((s32[8,2,128]{2,1,0:T(2,128)}), s32[8,2,128]{2,1,0:T(2,128)S(1)}, u32[]{:S(2)}, u32[]{:S(2)}) async-start(s32[8,2,128]{2,1,0:T(2,128)} %broadcast_in_dim.26), calls=%async_computation | async-start | bytes 16384 | tf_op jit(solution)/shard_map/all_to_all | solution.py:246
  11.7 7.8 %copy-start.9 = (bf16[48,4,512]{2,1,0:T(4,128)(2,1)S(1)}, bf16[48,4,512]{2,1,0:T(4,128)(2,1)}, u32[]{:S(2)}) copy-start(bf16[48,4,512]{2,1,0:T(4,128)(2,1)} %param.10) | copy-start | bytes 589828
  13.3 29.2 %all-to-all-start.1 = ((bf16[8,4,128,128]{3,2,1,0:T(8,128)(2,1)}), bf16[8,4,128,128]{3,2,1,0:T(8,128)(2,1)S(1)}, u32[]{:S(2)}, u32[]{:S(2)}) async-start(bf16[8,4,128,128]{3,2,1,0:T(8,128)(2,1)} %pick.2), calls=%async_computation.1 | async-start | bytes 2097152 | tf_op jit(solution)/shard_map/all_to_all | solution.py:246
  16.9 23.6 %collective-permute-start.1 = (bf16[4,4,128,128]{3,2,1,0:T(8,128)(2,1)S(1)}, bf16[4,4,128,128]{3,2,1,0:T(8,128)(2,1)S(1)}, u32[]{:S(2)}, u32[]{:S(2)}) collective-permute-start(bf16[4,4,128,128]{3,2,1,0:T(8,128)(2,1)S(1)} %bitcast.34), channel_id=1, source_target_pairs={{0,16},{2,18},{4,20},{6,22},{8,24},{10,26},{12,28},{14,30},{16,0},... | collective-permute-start | bytes 1572872 | tf_op jit(solution)/shard_map/ppermute | solution.py:249
  19.6 24.5 %collective-permute-start = (bf16[192,512]{1,0:T(8,128)(2,1)S(1)}, bf16[192,512]{1,0:T(8,128)(2,1)S(1)}, u32[]{:S(2)}, u32[]{:S(2)}) collective-permute-start(bf16[192,512]{1,0:T(8,128)(2,1)S(1)} %reshape.160.refs_0_), channel_id=1, source_target_pairs={{0,1},{1,0},{2,3},{3,2},{4,5},{5,4},{6,7},{7,6},{8,9},{9,8},{10,11... | collective-permute-start | bytes 589832 | tf_op jit(solution)/shard_map/ppermute | solution.py:259
  42.5 6.5 %copy-start.11 = (s32[1,12]{1,0:T(1,128)S(1)}, s32[1,12]{1,0:T(1,128)}, u32[]{:S(2)}) copy-start(s32[1,12]{1,0:T(1,128)} %param.18) | copy-start | bytes 148
  42.5 6.6 %copy-start.10 = (s32[48,12]{0,1:T(8,128)S(1)}, s32[48,12]{0,1:T(8,128)}, u32[]{:S(2)}) copy-start(s32[48,12]{0,1:T(8,128)} %param.19) | copy-start | bytes 6916
  44.1 6.1 %copy-start.3 = (f32[512]{0:T(512)S(1)}, f32[512]{0:T(512)}, u32[]{:S(2)}) copy-start(f32[512]{0:T(512)} %param.11) | copy-start | bytes 6148
  44.1 6.1 %copy-start.4 = (f32[512]{0:T(512)S(1)}, f32[512]{0:T(512)}, u32[]{:S(2)}) copy-start(f32[512]{0:T(512)} %param.14) | copy-start | bytes 6148
  44.1 19.4 %all-to-all-start.2 = ((bf16[8,4,128,128]{3,2,1,0:T(8,128)(2,1)}), bf16[8,4,128,128]{3,2,1,0:T(8,128)(2,1)S(1)}, u32[]{:S(2)}, u32[]{:S(2)}) async-start(bf16[8,4,128,128]{3,2,1,0:T(8,128)(2,1)} %pick.3), calls=%async_computation.2 | async-start | bytes 2097152 | tf_op jit(solution)/shard_map/all_to_all | solution.py:246
  50.2 1.4 %copy-start.1 = (bf16[512,1536]{1,0:T(8,128)(2,1)S(1)}, bf16[512,1536]{1,0:T(8,128)(2,1)}, u32[]{:S(2)}) copy-start(bf16[512,1536]{1,0:T(8,128)(2,1)} %refs_5_.1) | copy-start | bytes 4718596
  51.6 1.0 %copy-start.2 = (bf16[512,512]{1,0:T(8,128)(2,1)S(1)}, bf16[512,512]{1,0:T(8,128)(2,1)}, u32[]{:S(2)}) copy-start(bf16[512,512]{1,0:T(8,128)(2,1)} %refs_6_.1) | copy-start | bytes 1572868
  58.2 0.9 %copy-start.5 = (f32[4,384,128]{2,1,0:T(8,128)}, f32[4,384,128]{2,1,0:T(8,128)S(1)}, u32[]{:S(2)}) copy-start(f32[4,384,128]{2,1,0:T(8,128)S(1)} %get-tuple-element.23.sums_ref) | copy-start | bytes 2359300
  59.1 0.7 %copy-start.7 = (bf16[384,512]{1,0:T(8,128)(2,1)}, bf16[384,512]{1,0:T(8,128)(2,1)S(1)}, u32[]{:S(2)}) copy-start(bf16[384,512]{1,0:T(8,128)(2,1)S(1)} %get-tuple-element.20.asked_ref) | copy-start | bytes 1179652
  63.5 1.1 %copy-start.6 = (f32[4,384,128]{2,1,0:T(8,128)S(1)}, f32[4,384,128]{2,1,0:T(8,128)}, u32[]{:S(2)}) copy-start(f32[4,384,128]{2,1,0:T(8,128)} %copy-done.5) | copy-start | bytes 2359300
  64.6 1.0 %copy-start.8 = (bf16[384,512]{1,0:T(8,128)(2,1)S(1)}, bf16[384,512]{1,0:T(8,128)(2,1)}, u32[]{:S(2)}) copy-start(bf16[384,512]{1,0:T(8,128)(2,1)} %copy-done.7) | copy-start | bytes 1179652
  68.1 4.7 %collective-permute-start.2 = (bf16[192,256]{1,0:T(8,128)(2,1)S(1)}, bf16[192,256]{1,0:T(8,128)(2,1)S(1)}, u32[]{:S(2)}, u32[]{:S(2)}) collective-permute-start(bf16[192,256]{1,0:T(8,128)(2,1)S(1)} %get-tuple-element.26), channel_id=1, source_target_pairs={{0,1},{1,0},{2,3},{3,2},{4,5},{5,4},{6,7},{7,6},{8,9},{9,8},{10,11... | collective-permute-start | bytes 294920 | tf_op jit(solution)/shard_map/ppermute | solution.py:275

commit v5 on v4

--- a/solution.py
+++ b/solution.py
@@ -11,6 +11,8 @@
 BIG = -1e30
 MIB = 1024 * 1024
 VMEM = pl.BlockSpec(memory_space=pltpu.VMEM)
+HBM = pl.BlockSpec(memory_space=pltpu.HBM)
+ANY = pl.BlockSpec(memory_space=pl.ANY)
 
 
 def params(rows):
@@ -34,28 +36,28 @@
     return lax.broadcasted_iota(jnp.int32, shape, dim)
 
 
-def pick_kernel(count, wanted_ref, tiles_ref, out_ref):
+def pick_kernel(count, wanted_ref, tiles_ref, after_ref, out_ref):
     for peer in range(count):
         out_ref[peer] = tiles_ref[wanted_ref[peer]]
 
 
-def pick(tiles, wanted):
+def pick(tiles, wanted, after):
     count = wanted.shape[0]
     return pl.pallas_call(
         functools.partial(pick_kernel, count),
         out_shape=jax.ShapeDtypeStruct((count,) + tiles.shape[1:], tiles.dtype),
-        in_specs=[pl.BlockSpec(memory_space=pltpu.SMEM), VMEM],
+        in_specs=[pl.BlockSpec(memory_space=pltpu.SMEM), VMEM, ANY],
         out_specs=VMEM,
         compiler_params=params(0),
         cost_estimate=pl.CostEstimate(flops=0, bytes_accessed=2 * MIB, transcendentals=0),
         name="pick",
-    )(wanted, tiles)
+    )(wanted, tiles, after)
 
 
 def front_kernel(groups, heads, head_size, chunk, cols, row_size, *refs):
     cell_refs, refs = refs[:groups], refs[groups:]
     (holder_ref, mask_ref, gain_col_ref, w_qkv_ref, w_out_ref, gain_tile_ref, w_query_ref,
-     resid_ref, asked_ref, normed_ref, packed_ref) = refs
+     after_ref, resid_ref, asked_hbm, normed_ref, packed_ref, asked_ref, sem) = refs
     own_rows, width = cell_refs[0].shape
     steps = own_rows // chunk
     span = groups * chunk
@@ -115,26 +117,30 @@
         else:
             one = asked[:, head * head_size:(head + 1) * head_size]
             query = jnp.concatenate([one, bias[:, head_size:]], axis=1)
-        asked_ref[:, pl.ds(head * lanes_two, lanes_two)] = query.astype(jnp.bfloat16)
-
-
-def front(cells, holder, key_mask, gain_col, w_qkv, w_out, gain_tile, w_query, heads, head_size, cols, row_size):
+        asked_ref[head] = query.astype(jnp.bfloat16)
+    copy = pltpu.make_async_copy(asked_ref, asked_hbm, sem)
+    copy.start()
+    copy.wait()
+
+
+def front(cells, holder, key_mask, gain_col, w_qkv, w_out, gain_tile, w_query, heads, head_size, cols, row_size, after):
     groups = len(cells)
     own_rows, width = cells[0].shape
     total = groups * own_rows
-    asked_width = 2 * w_query.shape[1]
+    asked_shape = (w_query.shape[1] // head_size, total, 2 * head_size)
     return pl.pallas_call(
         functools.partial(front_kernel, groups, heads, head_size, ROW_GROUP * cols, cols, row_size),
         out_shape=(jax.ShapeDtypeStruct((own_rows, width), jnp.float32),
-                   jax.ShapeDtypeStruct((total, asked_width), jnp.bfloat16)),
-        in_specs=[VMEM] * (groups + 7),
-        out_specs=(VMEM, VMEM),
-        scratch_shapes=[pltpu.VMEM((total, width), jnp.bfloat16), pltpu.VMEM((3, total, width), jnp.bfloat16)],
+                   jax.ShapeDtypeStruct(asked_shape, jnp.bfloat16)),
+        in_specs=[VMEM] * (groups + 7) + [ANY],
+        out_specs=(VMEM, HBM),
+        scratch_shapes=[pltpu.VMEM((total, width), jnp.bfloat16), pltpu.VMEM((3, total, width), jnp.bfloat16),
+                        pltpu.VMEM(asked_shape, jnp.bfloat16), pltpu.SemaphoreType.DMA],
         compiler_params=params(total),
-        cost_estimate=pl.CostEstimate(flops=2 * total * width * (4 * width + asked_width), bytes_accessed=4 * MIB,
+        cost_estimate=pl.CostEstimate(flops=2 * total * width * 5 * width, bytes_accessed=4 * MIB,
                                       transcendentals=total * heads * 128),
         name="front",
-    )(*cells, holder, key_mask, gain_col.reshape(1, width), w_qkv, w_out, gain_tile.reshape(1, width), w_query)
+    )(*cells, holder, key_mask, gain_col.reshape(1, width), w_qkv, w_out, gain_tile.reshape(1, width), w_query, after)
 
 
 def weigh(query, tiles, first_holder):
@@ -150,26 +156,37 @@
     return top, dot_rows(jnp.exp(scores - top).astype(jnp.bfloat16), val_part)
 
 
-def first_kernel(heads, block, asked_ref, tiles_ref, sums_ref, tops_ref):
-    rows_all, lanes = asked_ref.shape[0], tiles_ref.shape[3]
+def first_kernel(block, asked_hbm, tiles_ref, state_hbm, asked_ref, state_ref, sems):
+    heads, rows_all, lanes = asked_hbm.shape
     lane = iota((block, lanes), 1)
+    copies = [pltpu.make_async_copy(asked_hbm.at[head], asked_ref.at[head], sems.at[head]) for head in range(heads)]
+    for copy in copies:
+        copy.start()
     for step in range(rows_all // block):
         rows = pl.ds(step * block, block)
         tops = jnp.zeros((block, lanes), jnp.float32)
         for head in range(heads):
-            top, sums_ref[head, rows, :] = weigh(asked_ref[rows, pl.ds(head * lanes, lanes)], tiles_ref[:, head], 0)
+            if step == 0:
+                copies[head].wait()
+            top, state_ref[head, rows, :] = weigh(asked_ref[head, rows, :], tiles_ref[:, head], 0)
             tops = jnp.where(lane == head, top, tops)
-        tops_ref[rows, :] = tops
+        state_ref[heads, rows, :] = tops
+    copy = pltpu.make_async_copy(state_ref, state_hbm, sems.at[heads])
+    copy.start()
+    copy.wait()
 
 
 def first_tiles(asked, tiles):
     slots, heads, keys, lanes = tiles.shape
-    rows = asked.shape[0]
+    rows = asked.shape[1]
+    state_shape = (heads + 1, rows, lanes)
     return pl.pallas_call(
-        functools.partial(first_kernel, heads, rows if rows <= 512 else 128),
-        out_shape=(jax.ShapeDtypeStruct((heads, rows, lanes), jnp.float32), jax.ShapeDtypeStruct((rows, lanes), jnp.float32)),
-        in_specs=[VMEM] * 2,
-        out_specs=(VMEM, VMEM),
+        functools.partial(first_kernel, rows if rows <= 512 else 128),
+        out_shape=jax.ShapeDtypeStruct(state_shape, jnp.float32),
+        in_specs=[HBM, VMEM],
+        out_specs=HBM,
+        scratch_shapes=[pltpu.VMEM(asked.shape, jnp.bfloat16), pltpu.VMEM(state_shape, jnp.float32),
+                        pltpu.SemaphoreType.DMA((heads + 1,))],
         compiler_params=params(rows),
         cost_estimate=pl.CostEstimate(flops=4 * rows * heads * slots * keys * lanes, bytes_accessed=4 * MIB,
                                       transcendentals=rows * heads * slots * keys),
@@ -177,8 +194,9 @@
     )(asked, tiles)
 
 
-def last_kernel(groups, first_holder, first_head, heads, chunk, asked_ref, tiles_ref, sums_ref, tops_ref, *out_refs):
-    rows_all, lanes = asked_ref.shape[0], tiles_ref.shape[3]
+def last_kernel(groups, first_holder, first_head, heads, chunk, asked_hbm, tiles_ref, state_hbm, *refs):
+    out_refs, (asked_ref, state_ref, tops_ref, sems) = refs[:groups], refs[groups:]
+    heads_here, rows_all, lanes = asked_hbm.shape
     half = lanes // 2
     span = groups * chunk
     block = rows_all if rows_all <= 512 else span
@@ -191,38 +209,49 @@
                 place = pl.ds(step * (block // groups) + part * chunk, chunk)
                 out_refs[group][place, pl.ds(lane, lane_count)] = values[start:start + chunk]
 
+    copies = [pltpu.make_async_copy(asked_hbm.at[first_head + head], asked_ref.at[head], sems.at[head]) for head in range(heads)]
+    copies.append(pltpu.make_async_copy(state_hbm.at[pl.ds(first_head, heads)], state_ref, sems.at[heads]))
+    copies.append(pltpu.make_async_copy(state_hbm.at[heads_here], tops_ref, sems.at[heads + 1]))
+    for copy in copies:
+        copy.start()
     for step in range(rows_all // block):
         rows = pl.ds(step * block, block)
         low = None
         for head in range(heads):
-            here = first_head + head
-            top, sums = weigh(asked_ref[rows, pl.ds(here * lanes, lanes)], tiles_ref[:, head], first_holder)
-            old_top = tops_ref[rows, here:here + 1]
+            if step == 0:
+                copies[head].wait()
+            top, sums = weigh(asked_ref[head, rows, :], tiles_ref[:, head], first_holder)
+            if step == 0 and head == 0:
+                copies[heads].wait()
+                copies[heads + 1].wait()
+            old_top = tops_ref[rows, first_head + head:first_head + head + 1]
             new_top = jnp.maximum(top, old_top)
-            sums = sums_ref[here, rows, :] * jnp.exp(old_top - new_top) + sums * jnp.exp(top - new_top)
+            sums = state_ref[head, rows, :] * jnp.exp(old_top - new_top) + sums * jnp.exp(top - new_top)
             turned = pltpu.roll(sums, half, 1)
-            if heads % 2:
-                put(step, (sums / turned)[:, half:].astype(jnp.bfloat16), head * half, half)
-            elif head % 2 == 0:
+            if head % 2:
+                put(step, jnp.where(lane_low, low, sums / turned).astype(jnp.bfloat16), head // 2 * lanes, lanes)
+            elif head + 1 < heads:
                 low = turned / sums
             else:
-                put(step, jnp.where(lane_low, low, sums / turned).astype(jnp.bfloat16), head // 2 * lanes, lanes)
-
-
-def last_tiles(asked, tiles, sums, tops, first_holder, first_head, groups, cols):
+                put(step, (turned / sums)[:, :half].astype(jnp.bfloat16), head * half, half)
+
+
+def last_tiles(asked, tiles, state, first_holder, first_head, groups, cols):
     slots, heads, keys, lanes = tiles.shape
-    rows = asked.shape[0]
+    rows = asked.shape[1]
     out = jax.ShapeDtypeStruct((rows // groups, heads * lanes // 2), jnp.bfloat16)
     return pl.pallas_call(
         functools.partial(last_kernel, groups, first_holder, first_head, heads, ROW_GROUP * cols),
         out_shape=(out,) * groups,
-        in_specs=[VMEM] * 4,
+        in_specs=[HBM, VMEM, HBM],
         out_specs=(VMEM,) * groups,
+        scratch_shapes=[pltpu.VMEM((heads, rows, lanes), jnp.bfloat16), pltpu.VMEM((heads, rows, lanes), jnp.float32),
+                        pltpu.VMEM((rows, lanes), jnp.float32), pltpu.SemaphoreType.DMA((heads + 2,))],
         compiler_params=params(rows),
         cost_estimate=pl.CostEstimate(flops=4 * rows * heads * slots * keys * lanes, bytes_accessed=4 * MIB,
                                       transcendentals=rows * heads * slots * keys),
         name="last_tiles",
-    )(asked, tiles, sums, tops)
+    )(asked, tiles, state)
 
 
 def turn(size, step):
@@ -245,8 +274,9 @@
     def swap(value):
         return lax.all_to_all(value, "rows", split_axis=0, concat_axis=0, tiled=True, axis_index_groups=halves)
 
+    parts = [(0, heads_here - 1), (heads_here - 1, heads_here)] if heads_here > 1 else [(0, 1)]
     heads_first = jnp.transpose(tile_kv, (0, 2, 1, 3))
-    mirrored = lax.ppermute(heads_first, "rows", turn(row_size, half))
+    mirrored = [lax.ppermute(heads_first[:, low:high], "rows", turn(row_size, half)) for low, high in parts]
 
     listed = tile_ids[0] >= 0
     holder = jnp.where(listed, (tile_ids[0] // tiles_here + my_half * half) % row_size, -1)
@@ -258,23 +288,26 @@
     for step in range(1, col_size):
         cells.append(lax.ppermute(cells[0], "cols", turn(col_size, -step)))
 
-    near = swap(pick(heads_first, asked_by[:, 0]))
-    mirrored, near = lax.optimization_barrier((mirrored, near))
-    far_sent = pick(mirrored, asked_by[:, 1])
-
-    cells, far_sent = lax.optimization_barrier((cells, far_sent))
-    far = swap(far_sent)
+    near_by, far_by = asked_by[:, 0], asked_by[:, 1]
+    sent = pick(heads_first, near_by, mirrored[0])
+    near = swap(sent)
+    far = []
+    for arrived in mirrored:
+        sent = pick(arrived, far_by, sent)
+        far.append(swap(sent))
     query_here = lax.dynamic_slice_in_dim(w_query, col_me * group_width, group_width, 1)
     residual, asked = front(cells, holder[:, None], key_mask, gain_col, w_qkv, w_col_out, gain_tile, query_here,
-                            heads_all, head_size, cols, row_size)
-    sums, tops = first_tiles(asked, near)
-    answers = last_tiles(asked, far, sums, tops, half, 0, col_size, cols)
+                            heads_all, head_size, cols, row_size, sent)
+    state = first_tiles(asked, near)
 
     final = residual
-    for step in range(col_size):
-        answer = lax.ppermute(answers[step], "cols", turn(col_size, step)) if step else answers[0]
-        start = (col_me - step) % col_size * group_width
-        final = final + dot_rows(answer, lax.dynamic_slice_in_dim(w_tile_out, start, group_width, 0))
+    for (low, high), tiles in zip(parts, far):
+        answers = last_tiles(asked, tiles, state, half, low, col_size, cols)
+        for step in range(col_size):
+            answer = lax.ppermute(answers[step], "cols", turn(col_size, step)) if step else answers[0]
+            start = (col_me - step) % col_size * group_width + low * head_size
+            weight = lax.dynamic_slice_in_dim(w_tile_out, start, (high - low) * head_size, 0)
+            final = final + dot_rows(answer, weight)
     return final.astype(jnp.bfloat16).reshape(rows, cols, width)
 
 

time: 74.3 us -> 94.3 us (1.27)
  blocking collectives: 0 us -> 23.2 us
  waiting for transfers between devices: 31.4 us -> 22.9 us
  Pallas kernels: 11.2 us -> 18.4 us
  local copies, waits for them, and re-layouts: 10.3 us -> 7 us
  starting transfers between devices: 19.5 us -> 21.1 us
    all_to_all x0 -> x2, blocking collectives: none -> 23.2 us  [swap(): lax.all_to_all(value, 'rows', split_axis=0, concat_axis=0, tiled=True, ax...]
    all_to_all x3 -> x2, waiting for transfers between devices: 9.21 us -> 0.88 us  [swap(): lax.all_to_all(value, 'rows', split_axis=0, concat_axis=0, tiled=True, ax...]
    ppermute x1 -> x2, starting transfers between devices: 2.65 us -> 7.29 us  [shards(): lax.ppermute(heads_first[:, low:high], 'rows', turn(row_size, half))]
    pallas_call x1 -> x2, Pallas kernels: 2.51 us -> 6.45 us  [last_tiles(): pl.pallas_call(functools.partial(last_kernel, groups, first_holder, first...]
    all_to_all x3 -> x2, starting transfers between devices: 13.7 us -> 10.1 us  [swap(): lax.all_to_all(value, 'rows', split_axis=0, concat_axis=0, tiled=True, ax...]
    pallas_call x1, Pallas kernels: 2.38 us -> 5.16 us  [first_tiles(): pl.pallas_call(functools.partial(first_kernel, rows if rows <= 512 else 1...]
    unnamed x26 -> x24, local copies, waits for them, and re-layouts: 7.47 us -> 4.78 us
    ppermute x1 -> x2, starting transfers between devices: 1.58 us -> 2.16 us  [shards(): lax.ppermute(answers[step], 'cols', turn(col_size, step))]
  transfers between devices with their start and end apart: 6 -> 7, of which waited for: 5 -> 4; matrix products, arithmetic and copies ran while one was open for 3% -> 2% of each run, Pallas kernels for 10% -> 17%
where the time goes in v5:
time: 94.3 us; the launch traced here: 93.8 us
  blocking collectives  23.2 us (25%)
  waiting for transfers between devices  22.9 us (24%)
  starting transfers between devices  21.1 us (22%)
  Pallas kernels  18.4 us (20%)
  local copies, waits for them, and re-layouts  7 us (7%)
    all_to_all x2, blocking collectives, swap(): lax.all_to_all(value, 'rows', split_axis=0, concat_axis=0, tiled=True, ax...  23.2 us
    ppermute x2, waiting for transfers between devices, shards(): lax.ppermute(heads_first[:, low:high], 'rows', turn(row_size, half))  19 us
    all_to_all x2, starting transfers between devices, swap(): lax.all_to_all(value, 'rows', split_axis=0, concat_axis=0, tiled=True, ax...  10.1 us
    ppermute x2, starting transfers between devices, shards(): lax.ppermute(heads_first[:, low:high], 'rows', turn(row_size, half))  7.29 us
    pallas_call x2, Pallas kernels, last_tiles(): pl.pallas_call(functools.partial(last_kernel, groups, first_holder, first...  6.45 us
    pallas_call x1, Pallas kernels, first_tiles(): pl.pallas_call(functools.partial(first_kernel, rows if rows <= 512 else 1...  5.16 us
    unnamed x24, local copies, waits for them, and re-layouts  4.78 us
    pallas_call x3, Pallas kernels, pick(): pl.pallas_call(functools.partial(pick_kernel, count), out_shape=jax.Shape...  3.47 us
  transfers between devices with their start and end apart: 7, of which 4 were waited for; matrix products, arithmetic and copies ran while one was open for 2% of the time, Pallas kernels for 17%

profile of v5, /device:TPU:0, one launch (start us, length us, event | category | flops | bytes accessed | tf_op | source)
XLA Modules:
  0.0 93.8 jit_solution(14089182157524083746)
XLA Ops:
  0.0 1.2 %copy.37 = bf16[4,128,4,128]{3,1,2,0:T(8,128)(2,1)S(1)} copy(bf16[4,128,4,128]{3,2,1,0:T(4,128)(2,1)} %param.17) | data formatting | bytes 1048576 | tf_op args[7]
  1.3 4.1 %collective-permute-start.2 = (bf16[4,3,128,128]{3,2,1,0:T(8,128)(2,1)S(1)}, bf16[4,3,128,128]{3,2,1,0:T(8,128)(2,1)S(1)}, u32[]{:S(2)}, u32[]{:S(2)}) collective-permute-start(bf16[4,3,128,128]{3,2,1,0:T(8,128)(2,1)S(1)} %slice.22), channel_id=1, source_target_pairs={{0,16},{2,18},{4,20},{6,22},{8,24},{10,26},{12,28},{14,30},{16,0},... | collective-permute-start | bytes 1179656 | tf_op jit(solution)/shard_map/ppermute | solution.py:279
  5.7 8.3 %all_to_all.20 = s32[8,2,128]{2,1,0:T(2,128)S(1)} all-to-all(s32[8,2,128]{2,1,0:T(2,128)S(1)} %broadcast_in_dim.26), channel_id=1, replica_groups={{0,2,4,6,8,10,12,14},{16,18,20,22,24,26,28,30},{1,3,5,7,9,11,13,15},{17..., dimensions={0} | all-to-all | bytes 16384 | tf_op jit(solution)/shard_map/all_to_all | solution.py:275
  14.1 8.8 %collective-permute-done.2.after_ref.tiles_ref = bf16[4,3,128,128]{3,2,1,0:T(8,128)(2,1)S(1)} collective-permute-done((bf16[4,3,128,128]{3,2,1,0:T(8,128)(2,1)S(1)}, bf16[4,3,128,128]{3,2,1,0:T(8,128)(2,1)S(1)}, u32[]{:S(2)}, u32[]{:S(2)}) %collective-permute-start.2) | collective-permute-done | bytes 393248 | tf_op jit(solution)/shard_map/ppermute | solution.py:279
  22.9 1.6 %pick.3.after_ref = bf16[8,4,128,128]{3,2,1,0:T(8,128)(2,1)} custom-call(s32[8]{0:T(128)S(1)} %get-tuple-element.17.wanted_ref, bf16[4,4,128,128]{3,2,1,0:T(8,128)(2,1)S(1)} %bitcast.36, bf16[4,3,128,128]{3,2,1,0:T(8,128)(2,1)S(1)} %collective-permute-done.2.after_ref.tiles_ref), custom_call_target="tpu_custom_call" | custom-call | bytes 2097152 | tf_op jit(solution)/shard_map/pick/pallas_call | solution.py:46
  25.1 15.0 %all_to_all.21.tiles_ref = bf16[8,3,128,128]{3,2,1,0:T(8,128)(2,1)} all-to-all(bf16[8,3,128,128]{3,2,1,0:T(8,128)(2,1)S(1)} %pick.4.after_ref), channel_id=1, replica_groups={{0,2,4,6,8,10,12,14},{16,18,20,22,24,26,28,30},{1,3,5,7,9,11,13,15},{17..., dimensions={0} | all-to-all | bytes 1572864 | tf_op jit(solution)/shard_map/all_to_all | solution.py:275
  40.1 3.6 %all-to-all-start.2 = ((bf16[8,4,128,128]{3,2,1,0:T(8,128)(2,1)}), bf16[8,4,128,128]{3,2,1,0:T(8,128)(2,1)S(1)}, u32[]{:S(2)}, u32[]{:S(2)}) async-start(bf16[8,4,128,128]{3,2,1,0:T(8,128)(2,1)} %pick.3.after_ref), calls=%async_computation.2 | async-start | bytes 2097152 | tf_op jit(solution)/shard_map/all_to_all | solution.py:275
  43.7 3.2 %collective-permute-start.1 = (bf16[4,1,128,128]{3,2,1,0:T(8,128)(2,1)S(1)}, bf16[4,1,128,128]{3,2,1,0:T(8,128)(2,1)S(1)}, u32[]{:S(2)}, u32[]{:S(2)}) collective-permute-start(bf16[4,1,128,128]{3,2,1,0:T(8,128)(2,1)S(1)} %slice.21), channel_id=1, source_target_pairs={{0,16},{2,18},{4,20},{6,22},{8,24},{10,26},{12,28},{14,30},{16,0},... | collective-permute-start | bytes 393224 | tf_op jit(solution)/shard_map/ppermute | solution.py:279
  47.0 1.6 %collective-permute-start = (bf16[192,512]{1,0:T(8,128)(2,1)S(1)}, bf16[192,512]{1,0:T(8,128)(2,1)S(1)}, u32[]{:S(2)}, u32[]{:S(2)}) collective-permute-start(bf16[192,512]{1,0:T(8,128)(2,1)S(1)} %reshape.160.refs_0_), channel_id=1, source_target_pairs={{0,1},{1,0},{2,3},{3,2},{4,5},{5,4},{6,7},{7,6},{8,9},{9,8},{10,11... | collective-permute-start | bytes 589832 | tf_op jit(solution)/shard_map/ppermute | solution.py:289
  48.6 10.2 %collective-permute-done.1.tiles_ref = bf16[4,1,128,128]{3,2,1,0:T(8,128)(2,1)S(1)} collective-permute-done((bf16[4,1,128,128]{3,2,1,0:T(8,128)(2,1)S(1)}, bf16[4,1,128,128]{3,2,1,0:T(8,128)(2,1)S(1)}, u32[]{:S(2)}, u32[]{:S(2)}) %collective-permute-start.1) | collective-permute-done | bytes 131104 | tf_op jit(solution)/shard_map/ppermute | solution.py:279
  58.8 1.3 %pick.5.refs_9_ = bf16[8,1,128,128]{3,2,1,0:T(8,128)(2,1)} custom-call(s32[8]{0:T(128)S(1)} %get-tuple-element.18.wanted_ref, bf16[4,1,128,128]{3,2,1,0:T(8,128)(2,1)S(1)} %collective-permute-done.1.tiles_ref, bf16[8,3,128,128]{3,2,1,0:T(8,128)(2,1)S(1)} %pick.4.after_ref), custom_call_target="tpu_custom_call" | custom-call | bytes 2097152 | tf_op jit(solution)/shard_map/pick/pallas_call | solution.py:46
  60.0 0.9 all-to-all-done.2.tiles_ref
  60.9 6.5 %all-to-all-start.3 = ((bf16[8,1,128,128]{3,2,1,0:T(8,128)(2,1)}), bf16[8,1,128,128]{3,2,1,0:T(8,128)(2,1)S(1)}, u32[]{:S(2)}, u32[]{:S(2)}) async-start(bf16[8,1,128,128]{3,2,1,0:T(8,128)(2,1)} %pick.5.refs_9_), calls=%async_computation.3 | async-start | bytes 524288 | tf_op jit(solution)/shard_map/all_to_all | solution.py:275
  67.4 1.0 %constant_dynamic-slice_fusion.refs_8_ = bf16[512,256]{1,0:T(8,128)(2,1)S(1)} fusion(bf16[512,512]{1,0:T(8,128)(2,1)} %param.15, s32[]{:T(128)S(6)} %select_n.95), kind=kLoop, calls=%fused_computation.35 | loop fusion | bytes 524292 | tf_op jit(solution)/shard_map/dynamic_slice | solution.py:298
  68.7 1.4 %copy-done.4 = bf16[512,1536]{1,0:T(8,128)(2,1)S(1)} copy-done((bf16[512,1536]{1,0:T(8,128)(2,1)S(1)}, bf16[512,1536]{1,0:T(8,128)(2,1)}, u32[]{:S(2)}) %copy-start.4) | copy-done | bytes 1572888
  70.1 1.0 %copy-done.5 = bf16[512,512]{1,0:T(8,128)(2,1)S(1)} copy-done((bf16[512,512]{1,0:T(8,128)(2,1)S(1)}, bf16[512,512]{1,0:T(8,128)(2,1)}, u32[]{:S(2)}) %copy-start.5) | copy-done | bytes 524312
  71.1 3.3 %front.1 = (f32[192,512]{1,0:T(8,128)S(1)}, bf16[4,384,128]{2,1,0:T(8,128)(2,1)S(1)}) custom-call(bf16[192,512]{1,0:T(8,128)(2,1)S(1)} %reshape.160.refs_0_, bf16[192,512]{1,0:T(8,128)(2,1)S(1)} %collective-permute-done.refs_1_, s32[12,1]{1,0:T(8,128)S(1)} %fusion.13.refs_2_, s32[48,12]{1,0:T(8,128)S(1)} %copy.35.refs_3_, f32[1,512]{1,0:T(1,128)S(1)} %bitcast.38, ...), custom_call_target="tpu_custom_call" | custom-call | flops 1006632960 | bytes 4194304 | tf_op jit(solution)/shard_map/front/pallas_call | solution.py:131
  74.5 5.2 %first_tiles.1.state_hbm = f32[5,384,128]{2,1,0:T(8,128)S(1)} custom-call(bf16[4,384,128]{2,1,0:T(8,128)(2,1)S(1)} %get-tuple-element.12.asked_hbm, bf16[8,4,128,128]{3,2,1,0:T(8,128)(2,1)S(1)} %all-to-all-done.2.tiles_ref), custom_call_target="tpu_custom_call" | custom-call | flops 805306368 | bytes 4194304 | tf_op jit(solution)/shard_map/first_tiles/pallas_call | solution.py:183
  79.7 4.5 %last_tiles.2 = (bf16[192,192]{1,0:T(8,128)(2,1)S(1)}, bf16[192,192]{1,0:T(8,128)(2,1)S(1)}) custom-call(bf16[4,384,128]{2,1,0:T(8,128)(2,1)S(1)} %get-tuple-element.12.asked_hbm, bf16[8,3,128,128]{3,2,1,0:T(8,128)(2,1)S(1)} %copy-done.1, f32[5,384,128]{2,1,0:T(8,128)S(1)} %first_tiles.1.state_hbm), custom_call_target="tpu_custom_call" | custom-call | flops 603979776 | bytes 4194304 | tf_op jit(solution)/shard_map/last_tiles/pallas_call | solution.py:243
  84.2 1.6 %collective-permute-start.3 = (bf16[192,192]{1,0:T(8,128)(2,1)S(1)}, bf16[192,192]{1,0:T(8,128)(2,1)S(1)}, u32[]{:S(2)}, u32[]{:S(2)}) collective-permute-start(bf16[192,192]{1,0:T(8,128)(2,1)S(1)} %get-tuple-element.14), channel_id=1, source_target_pairs={{0,1},{1,0},{2,3},{3,2},{4,5},{5,4},{6,7},{7,6},{8,9},{9,8},{10,11... | collective-permute-start | bytes 221192 | tf_op jit(solution)/shard_map/ppermute | solution.py:307
  85.8 1.0 %copy-done.3 = bf16[4,384,128]{2,1,0:T(8,128)(2,1)S(1)} copy-done((bf16[4,384,128]{2,1,0:T(8,128)(2,1)S(1)}, bf16[4,384,128]{2,1,0:T(8,128)(2,1)}, u32[]{:S(2)}) %copy-start.3) | copy-done | bytes 393240
  86.8 2.0 %last_tiles.3 = (bf16[192,64]{1,0:T(8,128)(2,1)S(1)}, bf16[192,64]{1,0:T(8,128)(2,1)S(1)}) custom-call(bf16[4,384,128]{2,1,0:T(8,128)(2,1)S(1)} %copy-done.3, bf16[8,1,128,128]{3,2,1,0:T(8,128)(2,1)S(1)} %all-to-all-done.3.tiles_ref, f32[5,384,128]{2,1,0:T(8,128)S(1)} %first_tiles.1.state_hbm), custom_call_target="tpu_custom_call" | custom-call | flops 201326592 | bytes 4194304 | tf_op jit(solution)/shard_map/last_tiles/pallas_call | solution.py:243
  89.9 3.0 %collective-permute-done.4 = bf16[192,64]{1,0:T(8,128)(2,1)S(1)} collective-permute-done((bf16[192,64]{1,0:T(8,128)(2,1)S(1)}, bf16[192,64]{1,0:T(8,128)(2,1)S(1)}, u32[]{:S(2)}, u32[]{:S(2)}) %collective-permute-start.4) | collective-permute-done | bytes 24608 | tf_op jit(solution)/shard_map/ppermute | solution.py:307
  93.1 0.7 reshape.164
  (41 shorter events, 2.7 us)
Async XLA Ops:
  0.0 89.3 %copy-start = (bf16[512,512]{1,0:T(8,128)(2,1)S(1)}, bf16[512,512]{1,0:T(8,128)(2,1)}, u32[]{:S(2)}) copy-start(bf16[512,512]{1,0:T(8,128)(2,1)} %param.16) | copy-start | bytes 1572868
  0.0 5.4 %copy-start.10 = (s32[1,12]{1,0:T(1,128)S(1)}, s32[1,12]{1,0:T(1,128)}, u32[]{:S(2)}) copy-start(s32[1,12]{1,0:T(1,128)} %param.18) | copy-start | bytes 148
  1.3 21.6 %collective-permute-start.2 = (bf16[4,3,128,128]{3,2,1,0:T(8,128)(2,1)S(1)}, bf16[4,3,128,128]{3,2,1,0:T(8,128)(2,1)S(1)}, u32[]{:S(2)}, u32[]{:S(2)}) collective-permute-start(bf16[4,3,128,128]{3,2,1,0:T(8,128)(2,1)S(1)} %slice.22), channel_id=1, source_target_pairs={{0,16},{2,18},{4,20},{6,22},{8,24},{10,26},{12,28},{14,30},{16,0},... | collective-permute-start | bytes 1179656 | tf_op jit(solution)/shard_map/ppermute | solution.py:279
  25.1 21.8 %copy-start.8 = (bf16[48,4,512]{2,1,0:T(4,128)(2,1)S(1)}, bf16[48,4,512]{2,1,0:T(4,128)(2,1)}, u32[]{:S(2)}) copy-start(bf16[48,4,512]{2,1,0:T(4,128)(2,1)} %param.10) | copy-start | bytes 589828
  40.1 20.8 %all-to-all-start.2 = ((bf16[8,4,128,128]{3,2,1,0:T(8,128)(2,1)}), bf16[8,4,128,128]{3,2,1,0:T(8,128)(2,1)S(1)}, u32[]{:S(2)}, u32[]{:S(2)}) async-start(bf16[8,4,128,128]{3,2,1,0:T(8,128)(2,1)} %pick.3.after_ref), calls=%async_computation.2 | async-start | bytes 2097152 | tf_op jit(solution)/shard_map/all_to_all | solution.py:275
  43.7 24.9 %copy-start.9 = (s32[48,12]{0,1:T(8,128)S(1)}, s32[48,12]{0,1:T(8,128)}, u32[]{:S(2)}) copy-start(s32[48,12]{0,1:T(8,128)} %param.19) | copy-start | bytes 6916
  43.7 25.0 %copy-start.6 = (f32[512]{0:T(512)S(1)}, f32[512]{0:T(512)}, u32[]{:S(2)}) copy-start(f32[512]{0:T(512)} %param.11) | copy-start | bytes 6148
  43.7 25.0 %copy-start.7 = (f32[512]{0:T(512)S(1)}, f32[512]{0:T(512)}, u32[]{:S(2)}) copy-start(f32[512]{0:T(512)} %param.14) | copy-start | bytes 6148
  43.7 15.0 %collective-permute-start.1 = (bf16[4,1,128,128]{3,2,1,0:T(8,128)(2,1)S(1)}, bf16[4,1,128,128]{3,2,1,0:T(8,128)(2,1)S(1)}, u32[]{:S(2)}, u32[]{:S(2)}) collective-permute-start(bf16[4,1,128,128]{3,2,1,0:T(8,128)(2,1)S(1)} %slice.21), channel_id=1, source_target_pairs={{0,16},{2,18},{4,20},{6,22},{8,24},{10,26},{12,28},{14,30},{16,0},... | collective-permute-start | bytes 393224 | tf_op jit(solution)/shard_map/ppermute | solution.py:279
  47.0 21.7 %collective-permute-start = (bf16[192,512]{1,0:T(8,128)(2,1)S(1)}, bf16[192,512]{1,0:T(8,128)(2,1)S(1)}, u32[]{:S(2)}, u32[]{:S(2)}) collective-permute-start(bf16[192,512]{1,0:T(8,128)(2,1)S(1)} %reshape.160.refs_0_), channel_id=1, source_target_pairs={{0,1},{1,0},{2,3},{3,2},{4,5},{5,4},{6,7},{7,6},{8,9},{9,8},{10,11... | collective-permute-start | bytes 589832 | tf_op jit(solution)/shard_map/ppermute | solution.py:289
  60.9 24.9 %all-to-all-start.3 = ((bf16[8,1,128,128]{3,2,1,0:T(8,128)(2,1)}), bf16[8,1,128,128]{3,2,1,0:T(8,128)(2,1)S(1)}, u32[]{:S(2)}, u32[]{:S(2)}) async-start(bf16[8,1,128,128]{3,2,1,0:T(8,128)(2,1)} %pick.5.refs_9_), calls=%async_computation.3 | async-start | bytes 524288 | tf_op jit(solution)/shard_map/all_to_all | solution.py:275
  68.7 1.4 %copy-start.4 = (bf16[512,1536]{1,0:T(8,128)(2,1)S(1)}, bf16[512,1536]{1,0:T(8,128)(2,1)}, u32[]{:S(2)}) copy-start(bf16[512,1536]{1,0:T(8,128)(2,1)} %refs_5_.1) | copy-start | bytes 4718596
  70.1 1.0 %copy-start.5 = (bf16[512,512]{1,0:T(8,128)(2,1)S(1)}, bf16[512,512]{1,0:T(8,128)(2,1)}, u32[]{:S(2)}) copy-start(bf16[512,512]{1,0:T(8,128)(2,1)} %refs_6_.1) | copy-start | bytes 1572868
  74.5 9.7 %copy-start.2 = (bf16[4,384,128]{2,1,0:T(8,128)(2,1)}, bf16[4,384,128]{2,1,0:T(8,128)(2,1)S(1)}, u32[]{:S(2)}) copy-start(bf16[4,384,128]{2,1,0:T(8,128)(2,1)S(1)} %get-tuple-element.12.asked_hbm) | copy-start | bytes 1179652
  74.5 5.2 %copy-start.1 = (bf16[8,3,128,128]{3,2,1,0:T(8,128)(2,1)S(1)}, bf16[8,3,128,128]{3,2,1,0:T(8,128)(2,1)}, u32[]{:S(2)}) copy-start(bf16[8,3,128,128]{3,2,1,0:T(8,128)(2,1)} %all_to_all.21.tiles_ref) | copy-start | bytes 2359300
  84.2 5.5 %collective-permute-start.3 = (bf16[192,192]{1,0:T(8,128)(2,1)S(1)}, bf16[192,192]{1,0:T(8,128)(2,1)S(1)}, u32[]{:S(2)}, u32[]{:S(2)}) collective-permute-start(bf16[192,192]{1,0:T(8,128)(2,1)S(1)} %get-tuple-element.14), channel_id=1, source_target_pairs={{0,1},{1,0},{2,3},{3,2},{4,5},{5,4},{6,7},{7,6},{8,9},{9,8},{10,11... | collective-permute-start | bytes 221192 | tf_op jit(solution)/shard_map/ppermute | solution.py:307
  85.8 1.0 %copy-start.3 = (bf16[4,384,128]{2,1,0:T(8,128)(2,1)S(1)}, bf16[4,384,128]{2,1,0:T(8,128)(2,1)}, u32[]{:S(2)}) copy-start(bf16[4,384,128]{2,1,0:T(8,128)(2,1)} %copy-done.2) | copy-start | bytes 1179652
  88.7 4.2 %collective-permute-start.4 = (bf16[192,64]{1,0:T(8,128)(2,1)S(1)}, bf16[192,64]{1,0:T(8,128)(2,1)S(1)}, u32[]{:S(2)}, u32[]{:S(2)}) collective-permute-start(bf16[192,64]{1,0:T(8,128)(2,1)S(1)} %get-tuple-element.16), channel_id=1, source_target_pairs={{0,1},{1,0},{2,3},{3,2},{4,5},{5,4},{6,7},{7,6},{8,9},{9,8},{10,11... | collective-permute-start | bytes 73736 | tf_op jit(solution)/shard_map/ppermute | solution.py:307

commit v6 on v4

--- a/solution.py
+++ b/solution.py
@@ -11,10 +11,11 @@
 BIG = -1e30
 MIB = 1024 * 1024
 VMEM = pl.BlockSpec(memory_space=pltpu.VMEM)
+ANY = pl.BlockSpec(memory_space=pl.ANY)
 
 
 def params(rows):
-    return pltpu.CompilerParams(vmem_limit_bytes=(14 if rows <= 512 else 48) * MIB)
+    return pltpu.CompilerParams(vmem_limit_bytes=(20 if rows <= 512 else 48) * MIB)
 
 
 def dot_rows(left, right):
@@ -34,28 +35,54 @@
     return lax.broadcasted_iota(jnp.int32, shape, dim)
 
 
-def pick_kernel(count, wanted_ref, tiles_ref, out_ref):
-    for peer in range(count):
-        out_ref[peer] = tiles_ref[wanted_ref[peer]]
-
-
-def pick(tiles, wanted):
+def pick_kernel(parts, wanted_ref, *refs):
+    tile_refs, out_ref = refs[:parts], refs[-1]
+    for peer in range(out_ref.shape[0]):
+        low = 0
+        for tiles_ref in tile_refs:
+            high = low + tiles_ref.shape[1]
+            out_ref[peer, low:high] = tiles_ref[wanted_ref[peer]]
+            low = high
+
+
+def pick(tiles, wanted, after):
     count = wanted.shape[0]
-    return pl.pallas_call(
-        functools.partial(pick_kernel, count),
-        out_shape=jax.ShapeDtypeStruct((count,) + tiles.shape[1:], tiles.dtype),
-        in_specs=[pl.BlockSpec(memory_space=pltpu.SMEM), VMEM],
+    heads = sum(part.shape[1] for part in tiles)
+    return pl.pallas_call(
+        functools.partial(pick_kernel, len(tiles)),
+        out_shape=jax.ShapeDtypeStruct((count, heads) + tiles[0].shape[2:], tiles[0].dtype),
+        in_specs=[pl.BlockSpec(memory_space=pltpu.SMEM)] + [VMEM] * len(tiles) + [ANY] * len(after),
         out_specs=VMEM,
         compiler_params=params(0),
         cost_estimate=pl.CostEstimate(flops=0, bytes_accessed=2 * MIB, transcendentals=0),
         name="pick",
-    )(wanted, tiles)
+    )(wanted, *tiles, *after)
+
+
+def pick_each_kernel(wanted_ref, me_ref, tiles_ref, *refs):
+    out_refs = refs[-wanted_ref.shape[0]:]
+    for step, out_ref in enumerate(out_refs):
+        out_ref[...] = tiles_ref[wanted_ref[me_ref[0] ^ step]]
+
+
+def pick_each(tiles, wanted, me, after):
+    count = wanted.shape[0]
+    smem = pl.BlockSpec(memory_space=pltpu.SMEM)
+    return pl.pallas_call(
+        pick_each_kernel,
+        out_shape=(jax.ShapeDtypeStruct(tiles.shape[1:], tiles.dtype),) * count,
+        in_specs=[smem, smem, VMEM] + [ANY] * len(after),
+        out_specs=(VMEM,) * count,
+        compiler_params=params(0),
+        cost_estimate=pl.CostEstimate(flops=0, bytes_accessed=2 * MIB, transcendentals=0),
+        name="pick_each",
+    )(wanted, me, tiles, *after)
 
 
 def front_kernel(groups, heads, head_size, chunk, cols, row_size, *refs):
     cell_refs, refs = refs[:groups], refs[groups:]
     (holder_ref, mask_ref, gain_col_ref, w_qkv_ref, w_out_ref, gain_tile_ref, w_query_ref,
-     resid_ref, asked_ref, normed_ref, packed_ref) = refs
+     after_ref, resid_ref, asked_ref, normed_ref, packed_ref) = refs
     own_rows, width = cell_refs[0].shape
     steps = own_rows // chunk
     span = groups * chunk
@@ -115,70 +142,43 @@
         else:
             one = asked[:, head * head_size:(head + 1) * head_size]
             query = jnp.concatenate([one, bias[:, head_size:]], axis=1)
-        asked_ref[:, pl.ds(head * lanes_two, lanes_two)] = query.astype(jnp.bfloat16)
-
-
-def front(cells, holder, key_mask, gain_col, w_qkv, w_out, gain_tile, w_query, heads, head_size, cols, row_size):
+        asked_ref[head] = query.astype(jnp.bfloat16)
+
+
+def front(cells, holder, key_mask, gain_col, w_qkv, w_out, gain_tile, w_query, heads, head_size, cols, row_size, after):
     groups = len(cells)
     own_rows, width = cells[0].shape
     total = groups * own_rows
-    asked_width = 2 * w_query.shape[1]
+    asked_shape = (w_query.shape[1] // head_size, total, 2 * head_size)
     return pl.pallas_call(
         functools.partial(front_kernel, groups, heads, head_size, ROW_GROUP * cols, cols, row_size),
         out_shape=(jax.ShapeDtypeStruct((own_rows, width), jnp.float32),
-                   jax.ShapeDtypeStruct((total, asked_width), jnp.bfloat16)),
-        in_specs=[VMEM] * (groups + 7),
+                   jax.ShapeDtypeStruct(asked_shape, jnp.bfloat16)),
+        in_specs=[VMEM] * (groups + 7) + [ANY],
         out_specs=(VMEM, VMEM),
         scratch_shapes=[pltpu.VMEM((total, width), jnp.bfloat16), pltpu.VMEM((3, total, width), jnp.bfloat16)],
         compiler_params=params(total),
-        cost_estimate=pl.CostEstimate(flops=2 * total * width * (4 * width + asked_width), bytes_accessed=4 * MIB,
+        cost_estimate=pl.CostEstimate(flops=2 * total * width * 5 * width, bytes_accessed=4 * MIB,
                                       transcendentals=total * heads * 128),
         name="front",
-    )(*cells, holder, key_mask, gain_col.reshape(1, width), w_qkv, w_out, gain_tile.reshape(1, width), w_query)
-
-
-def weigh(query, tiles, first_holder):
+    )(*cells, holder, key_mask, gain_col.reshape(1, width), w_qkv, w_out, gain_tile.reshape(1, width), w_query, after)
+
+
+def weigh(query, tiles):
     slots, keys, lanes = tiles.shape
     half = lanes // 2
     lane = iota(tiles.shape, 2)
-    slot = iota(tiles.shape, 0)
-    marks = (lane == slot + (half + first_holder)).astype(tiles.dtype)
+    marks = (lane == iota(tiles.shape, 0) + half).astype(tiles.dtype)
     key_part = jnp.where(lane < half, tiles, marks).reshape(slots * keys, lanes)
     val_part = jnp.where(lane < half, jnp.ones_like(tiles), tiles).reshape(slots * keys, lanes)
     scores = dot_lanes(query, key_part)
     top = jnp.max(scores, axis=1, keepdims=True)
-    return top, dot_rows(jnp.exp(scores - top).astype(jnp.bfloat16), val_part)
-
-
-def first_kernel(heads, block, asked_ref, tiles_ref, sums_ref, tops_ref):
-    rows_all, lanes = asked_ref.shape[0], tiles_ref.shape[3]
-    lane = iota((block, lanes), 1)
-    for step in range(rows_all // block):
-        rows = pl.ds(step * block, block)
-        tops = jnp.zeros((block, lanes), jnp.float32)
-        for head in range(heads):
-            top, sums_ref[head, rows, :] = weigh(asked_ref[rows, pl.ds(head * lanes, lanes)], tiles_ref[:, head], 0)
-            tops = jnp.where(lane == head, top, tops)
-        tops_ref[rows, :] = tops
-
-
-def first_tiles(asked, tiles):
-    slots, heads, keys, lanes = tiles.shape
-    rows = asked.shape[0]
-    return pl.pallas_call(
-        functools.partial(first_kernel, heads, rows if rows <= 512 else 128),
-        out_shape=(jax.ShapeDtypeStruct((heads, rows, lanes), jnp.float32), jax.ShapeDtypeStruct((rows, lanes), jnp.float32)),
-        in_specs=[VMEM] * 2,
-        out_specs=(VMEM, VMEM),
-        compiler_params=params(rows),
-        cost_estimate=pl.CostEstimate(flops=4 * rows * heads * slots * keys * lanes, bytes_accessed=4 * MIB,
-                                      transcendentals=rows * heads * slots * keys),
-        name="first_tiles",
-    )(asked, tiles)
-
-
-def last_kernel(groups, first_holder, first_head, heads, chunk, asked_ref, tiles_ref, sums_ref, tops_ref, *out_refs):
-    rows_all, lanes = asked_ref.shape[0], tiles_ref.shape[3]
+    return dot_rows(jnp.exp(scores - top).astype(jnp.bfloat16), val_part)
+
+
+def attend_kernel(groups, tile_count, chunk, asked_ref, *refs):
+    tile_refs, out_refs = refs[:tile_count], refs[tile_count:]
+    heads, rows_all, lanes = asked_ref.shape
     half = lanes // 2
     span = groups * chunk
     block = rows_all if rows_all <= 512 else span
@@ -192,37 +192,33 @@
                 out_refs[group][place, pl.ds(lane, lane_count)] = values[start:start + chunk]
 
     for step in range(rows_all // block):
-        rows = pl.ds(step * block, block)
         low = None
         for head in range(heads):
-            here = first_head + head
-            top, sums = weigh(asked_ref[rows, pl.ds(here * lanes, lanes)], tiles_ref[:, head], first_holder)
-            old_top = tops_ref[rows, here:here + 1]
-            new_top = jnp.maximum(top, old_top)
-            sums = sums_ref[here, rows, :] * jnp.exp(old_top - new_top) + sums * jnp.exp(top - new_top)
+            tiles = jnp.concatenate([ref[:, head] for ref in tile_refs], axis=0)
+            sums = weigh(asked_ref[head, pl.ds(step * block, block), :], tiles)
             turned = pltpu.roll(sums, half, 1)
-            if heads % 2:
-                put(step, (sums / turned)[:, half:].astype(jnp.bfloat16), head * half, half)
-            elif head % 2 == 0:
+            if head % 2:
+                put(step, jnp.where(lane_low, low, sums / turned).astype(jnp.bfloat16), head // 2 * lanes, lanes)
+            elif head + 1 < heads:
                 low = turned / sums
             else:
-                put(step, jnp.where(lane_low, low, sums / turned).astype(jnp.bfloat16), head // 2 * lanes, lanes)
-
-
-def last_tiles(asked, tiles, sums, tops, first_holder, first_head, groups, cols):
-    slots, heads, keys, lanes = tiles.shape
-    rows = asked.shape[0]
+                put(step, (turned / sums)[:, :half].astype(jnp.bfloat16), head * half, half)
+
+
+def attend(asked, tiles, groups, cols):
+    heads, rows, lanes = asked.shape
+    keys = sum(part.shape[0] * part.shape[2] for part in tiles)
     out = jax.ShapeDtypeStruct((rows // groups, heads * lanes // 2), jnp.bfloat16)
     return pl.pallas_call(
-        functools.partial(last_kernel, groups, first_holder, first_head, heads, ROW_GROUP * cols),
+        functools.partial(attend_kernel, groups, len(tiles), ROW_GROUP * cols),
         out_shape=(out,) * groups,
-        in_specs=[VMEM] * 4,
+        in_specs=[VMEM] * (1 + len(tiles)),
         out_specs=(VMEM,) * groups,
         compiler_params=params(rows),
-        cost_estimate=pl.CostEstimate(flops=4 * rows * heads * slots * keys * lanes, bytes_accessed=4 * MIB,
-                                      transcendentals=rows * heads * slots * keys),
-        name="last_tiles",
-    )(asked, tiles, sums, tops)
+        cost_estimate=pl.CostEstimate(flops=4 * rows * heads * keys * lanes, bytes_accessed=4 * MIB,
+                                      transcendentals=rows * heads * keys),
+        name="attend",
+    )(asked, *tiles)
 
 
 def turn(size, step):
@@ -238,15 +234,18 @@
     group_width = heads_here * head_size
     half = row_size // 2
     col_me = lax.axis_index("cols")
-    my_half = lax.axis_index("rows") // half
+    row_me = lax.axis_index("rows")
+    my_half, my_place = row_me // half, row_me % half
     halves = [list(range(half)), list(range(half, row_size))]
     assert row_size <= head_size and row_size % 2 == 0
 
     def swap(value):
         return lax.all_to_all(value, "rows", split_axis=0, concat_axis=0, tiled=True, axis_index_groups=halves)
 
+    middle = max(heads_here // 2, 1)
     heads_first = jnp.transpose(tile_kv, (0, 2, 1, 3))
-    mirrored = lax.ppermute(heads_first, "rows", turn(row_size, half))
+    mirrored = [lax.ppermute(heads_first[:, low:low + middle], "rows", turn(row_size, half))
+                for low in range(0, heads_here, middle)]
 
     listed = tile_ids[0] >= 0
     holder = jnp.where(listed, (tile_ids[0] // tiles_here + my_half * half) % row_size, -1)
@@ -258,17 +257,22 @@
     for step in range(1, col_size):
         cells.append(lax.ppermute(cells[0], "cols", turn(col_size, -step)))
 
-    near = swap(pick(heads_first, asked_by[:, 0]))
-    mirrored, near = lax.optimization_barrier((mirrored, near))
-    far_sent = pick(mirrored, asked_by[:, 1])
-
-    cells, far_sent = lax.optimization_barrier((cells, far_sent))
-    far = swap(far_sent)
+    near_by, far_by = asked_by[:, 0], asked_by[:, 1]
+    if half <= 8 and half & (half - 1) == 0:
+        sent = pick_each(heads_first, near_by, my_place.reshape(1), mirrored[:1])
+        near = [sent[0][None]]
+        for step in range(1, half):
+            pairs = [(row, row // half * half + (row % half ^ step)) for row in range(row_size)]
+            near.append(lax.ppermute(sent[step][None], "rows", pairs))
+        holder = jnp.where((holder >= 0) & (holder < half), holder ^ my_place, holder)
+    else:
+        near = [swap(pick([heads_first], near_by, mirrored[:1]))]
+    sent = pick(mirrored, far_by, near)
+    far = swap(sent)
     query_here = lax.dynamic_slice_in_dim(w_query, col_me * group_width, group_width, 1)
     residual, asked = front(cells, holder[:, None], key_mask, gain_col, w_qkv, w_col_out, gain_tile, query_here,
-                            heads_all, head_size, cols, row_size)
-    sums, tops = first_tiles(asked, near)
-    answers = last_tiles(asked, far, sums, tops, half, 0, col_size, cols)
+                            heads_all, head_size, cols, row_size, sent)
+    answers = attend(asked, near + [far], col_size, cols)
 
     final = residual
     for step in range(col_size):

time: 74.3 us -> 85.3 us (1.15)
  local copies, waits for them, and re-layouts: 10.3 us -> 22.8 us
  Pallas kernels: 11.2 us -> 9.99 us
    unnamed x26 -> x58, local copies, waits for them, and re-layouts: 7.47 us -> 19.3 us
    ppermute x1 -> x9, starting transfers between devices: 2.65 us -> 8.91 us  [the longest x7 4.47 us: shards(): near.append(lax.ppermute(sent[step][None], 'rows', pairs))]
    all_to_all x3 -> x2, starting transfers between devices: 13.7 us -> 7.48 us  [swap(): lax.all_to_all(value, 'rows', split_axis=0, concat_axis=0, tiled=True, ax...]
    all_to_all x3 -> x2, waiting for transfers between devices: 9.21 us -> 5.09 us  [swap(): lax.all_to_all(value, 'rows', split_axis=0, concat_axis=0, tiled=True, ax...]
    ppermute x1, waiting for transfers between devices: 0.01 us -> 2.59 us  [shards(): cells.append(lax.ppermute(cells[0], 'cols', turn(col_size, -step)))]
    ppermute x1 -> x9, waiting for transfers between devices: 19.3 us -> 21.1 us  [the longest x2 10.8 us: shards(): lax.ppermute(heads_first[:, low:low + middle], 'rows', turn(row_size, half))]
    pallas_call x4 -> x3, Pallas kernels: 8.11 us -> 6.88 us  [the longest x1 4.64 us: attend(): pl.pallas_call(functools.partial(attend_kernel, groups, len(tiles), ROW_G...]
  transfers between devices with their start and end apart: 6 -> 13, of which waited for: 5 -> 11; matrix products, arithmetic and copies ran while one was open for 3% -> 5% of each run, Pallas kernels for 10% -> 4%
where the time goes in v6:
time: 85.3 us; the launch traced here: 84.7 us
  waiting for transfers between devices  31.6 us (37%)
  local copies, waits for them, and re-layouts  22.8 us (27%)
  starting transfers between devices  19.6 us (23%)
  Pallas kernels  9.99 us (12%)
    unnamed x58, local copies, waits for them, and re-layouts  19.3 us
    ppermute x2, waiting for transfers between devices, shards(): lax.ppermute(heads_first[:, low:low + middle], 'rows', turn(row_size, half))  10.8 us
    ppermute x7, waiting for transfers between devices, shards(): near.append(lax.ppermute(sent[step][None], 'rows', pairs))  10.2 us
    all_to_all x2, starting transfers between devices, swap(): lax.all_to_all(value, 'rows', split_axis=0, concat_axis=0, tiled=True, ax...  7.48 us
    all_to_all x2, waiting for transfers between devices, swap(): lax.all_to_all(value, 'rows', split_axis=0, concat_axis=0, tiled=True, ax...  5.09 us
    pallas_call x1, Pallas kernels, attend(): pl.pallas_call(functools.partial(attend_kernel, groups, len(tiles), ROW_G...  4.64 us
    ppermute x7, starting transfers between devices, shards(): near.append(lax.ppermute(sent[step][None], 'rows', pairs))  4.47 us
    ppermute x2, starting transfers between devices, shards(): lax.ppermute(heads_first[:, low:low + middle], 'rows', turn(row_size, half))  4.44 us
  transfers between devices with their start and end apart: 13, of which 11 were waited for; matrix products, arithmetic and copies ran while one was open for 5% of the time, Pallas kernels for 4%

profile of v6, /device:TPU:0, one launch (start us, length us, event | category | flops | bytes accessed | tf_op | source)
XLA Modules:
  0.0 84.7 jit_solution(9390852092327733520)
XLA Ops:
  0.0 1.2 %copy.37 = bf16[4,128,4,128]{3,1,2,0:T(8,128)(2,1)S(1)} copy(bf16[4,128,4,128]{3,2,1,0:T(4,128)(2,1)} %param.17) | data formatting | bytes 1048576 | tf_op args[7]
  1.3 4.1 %collective-permute-start.1 = (bf16[4,2,128,128]{3,2,1,0:T(8,128)(2,1)S(1)}, bf16[4,2,128,128]{3,2,1,0:T(8,128)(2,1)S(1)}, u32[]{:S(2)}, u32[]{:S(2)}) collective-permute-start(bf16[4,2,128,128]{3,2,1,0:T(8,128)(2,1)S(1)} %get-tuple-element.30), channel_id=1, source_target_pairs={{0,16},{2,18},{4,20},{6,22},{8,24},{10,26},{12,28},{14,30},{16,0},... | collective-permute-start | bytes 786440 | tf_op jit(solution)/shard_map/ppermute | solution.py:247
  6.3 3.8 %all-to-all-start = ((s32[8,2,128]{2,1,0:T(2,128)}), s32[8,2,128]{2,1,0:T(2,128)S(1)}, u32[]{:S(2)}, u32[]{:S(2)}) async-start(s32[8,2,128]{2,1,0:T(2,128)} %broadcast_in_dim.50), calls=%async_computation | async-start | bytes 16384 | tf_op jit(solution)/shard_map/all_to_all | solution.py:243
  10.5 4.5 %all-to-all-done = s32[8,2,128]{2,1,0:T(2,128)S(1)} async-done(((s32[8,2,128]{2,1,0:T(2,128)}), s32[8,2,128]{2,1,0:T(2,128)S(1)}, u32[]{:S(2)}, u32[]{:S(2)}) %all-to-all-start) | async-done | bytes 8224 | tf_op jit(solution)/shard_map/all_to_all | solution.py:243
  15.0 8.7 %collective-permute-done.1.refs_0_ = bf16[4,2,128,128]{3,2,1,0:T(8,128)(2,1)S(1)} collective-permute-done((bf16[4,2,128,128]{3,2,1,0:T(8,128)(2,1)S(1)}, bf16[4,2,128,128]{3,2,1,0:T(8,128)(2,1)S(1)}, u32[]{:S(2)}, u32[]{:S(2)}) %collective-permute-start.1) | collective-permute-done | bytes 262176 | tf_op jit(solution)/shard_map/ppermute | solution.py:247
  24.5 1.9 %collective-permute-start.4 = (bf16[1,4,128,128]{3,2,1,0:T(8,128)(2,1)S(1)}, bf16[1,4,128,128]{3,2,1,0:T(8,128)(2,1)S(1)}, u32[]{:S(2)}, u32[]{:S(2)}) collective-permute-start(bf16[1,4,128,128]{3,2,1,0:T(8,128)(2,1)S(1)} %bitcast.53), channel_id=1, source_target_pairs={{0,4},{2,6},{4,0},{6,2},{8,12},{10,14},{12,8},{14,10},{16,20},{18,... | collective-permute-start | bytes 393224 | tf_op jit(solution)/shard_map/ppermute | solution.py:266
  26.5 2.1 %collective-permute-done.2.refs_1_ = bf16[4,2,128,128]{3,2,1,0:T(8,128)(2,1)S(1)} collective-permute-done((bf16[4,2,128,128]{3,2,1,0:T(8,128)(2,1)S(1)}, bf16[4,2,128,128]{3,2,1,0:T(8,128)(2,1)S(1)}, u32[]{:S(2)}, u32[]{:S(2)}) %collective-permute-start.2) | collective-permute-done | bytes 262176 | tf_op jit(solution)/shard_map/ppermute | solution.py:247
  28.9 1.3 %collective-permute-start.8 = (bf16[1,4,128,128]{3,2,1,0:T(8,128)(2,1)S(1)}, bf16[1,4,128,128]{3,2,1,0:T(8,128)(2,1)S(1)}, u32[]{:S(2)}, u32[]{:S(2)}) collective-permute-start(bf16[1,4,128,128]{3,2,1,0:T(8,128)(2,1)S(1)} %bitcast.49), channel_id=1, source_target_pairs={{0,12},{2,14},{4,8},{6,10},{8,4},{10,6},{12,0},{14,2},{16,28},{18,... | collective-permute-start | bytes 393224 | tf_op jit(solution)/shard_map/ppermute | solution.py:266
  31.6 1.3 %collective-permute-done.5.refs_5_.refs_3_ = bf16[1,4,128,128]{3,2,1,0:T(8,128)(2,1)S(1)} collective-permute-done((bf16[1,4,128,128]{3,2,1,0:T(8,128)(2,1)S(1)}, bf16[1,4,128,128]{3,2,1,0:T(8,128)(2,1)S(1)}, u32[]{:S(2)}, u32[]{:S(2)}) %collective-permute-start.5) | collective-permute-done | bytes 131104 | tf_op jit(solution)/shard_map/ppermute | solution.py:266
  32.9 1.5 %collective-permute-done.7.refs_7_.refs_5_ = bf16[1,4,128,128]{3,2,1,0:T(8,128)(2,1)S(1)} collective-permute-done((bf16[1,4,128,128]{3,2,1,0:T(8,128)(2,1)S(1)}, bf16[1,4,128,128]{3,2,1,0:T(8,128)(2,1)S(1)}, u32[]{:S(2)}, u32[]{:S(2)}) %collective-permute-start.7) | collective-permute-done | bytes 131104 | tf_op jit(solution)/shard_map/ppermute | solution.py:266
  34.4 5.1 %collective-permute-done.8.refs_8_.refs_6_ = bf16[1,4,128,128]{3,2,1,0:T(8,128)(2,1)S(1)} collective-permute-done((bf16[1,4,128,128]{3,2,1,0:T(8,128)(2,1)S(1)}, bf16[1,4,128,128]{3,2,1,0:T(8,128)(2,1)S(1)}, u32[]{:S(2)}, u32[]{:S(2)}) %collective-permute-start.8) | collective-permute-done | bytes 131104 | tf_op jit(solution)/shard_map/ppermute | solution.py:266
  39.5 1.7 %collective-permute-done.9.refs_9_.refs_7_ = bf16[1,4,128,128]{3,2,1,0:T(8,128)(2,1)S(1)} collective-permute-done((bf16[1,4,128,128]{3,2,1,0:T(8,128)(2,1)S(1)}, bf16[1,4,128,128]{3,2,1,0:T(8,128)(2,1)S(1)}, u32[]{:S(2)}, u32[]{:S(2)}) %collective-permute-start.9) | collective-permute-done | bytes 131104 | tf_op jit(solution)/shard_map/ppermute | solution.py:266
  41.2 1.6 %pick.1.refs_9_ = bf16[8,4,128,128]{3,2,1,0:T(8,128)(2,1)} custom-call(s32[8]{0:T(128)S(1)} %get-tuple-element.32.wanted_ref, bf16[4,2,128,128]{3,2,1,0:T(8,128)(2,1)S(1)} %collective-permute-done.1.refs_0_, bf16[4,2,128,128]{3,2,1,0:T(8,128)(2,1)S(1)} %collective-permute-done.2.refs_1_, bf16[1,4,128,128]{3,2,1,0:T(8,128)(2,1)S(1)} %bitcast.44, ...), custom_call_target="tpu_custom_call" | custom-call | bytes 2097152 | tf_op jit(solution)/shard_map/pick/pallas_call | solution.py:51
  48.1 3.7 %all-to-all-start.1 = ((bf16[8,4,128,128]{3,2,1,0:T(8,128)(2,1)}), bf16[8,4,128,128]{3,2,1,0:T(8,128)(2,1)S(1)}, u32[]{:S(2)}, u32[]{:S(2)}) async-start(bf16[8,4,128,128]{3,2,1,0:T(8,128)(2,1)} %pick.1.refs_9_), calls=%async_computation.1 | async-start | bytes 2097152 | tf_op jit(solution)/shard_map/all_to_all | solution.py:243
  51.9 1.6 %collective-permute-start = (bf16[192,512]{1,0:T(8,128)(2,1)S(1)}, bf16[192,512]{1,0:T(8,128)(2,1)S(1)}, u32[]{:S(2)}, u32[]{:S(2)}) collective-permute-start(bf16[192,512]{1,0:T(8,128)(2,1)S(1)} %reshape.184.refs_0_), channel_id=1, source_target_pairs={{0,1},{1,0},{2,3},{3,2},{4,5},{5,4},{6,7},{7,6},{8,9},{9,8},{10,11... | collective-permute-start | bytes 589832 | tf_op jit(solution)/shard_map/ppermute | solution.py:258
  54.2 1.4 %copy.35.refs_3_ = s32[48,12]{1,0:T(8,128)} copy(s32[48,12]{0,1:T(8,128)} %param.19) | data formatting | bytes 4608 | tf_op args[9]
  55.6 1.0 %constant_dynamic-slice_fusion.refs_8_ = bf16[512,256]{1,0:T(8,128)(2,1)S(1)} fusion(bf16[512,512]{1,0:T(8,128)(2,1)} %param.15, s32[]{:T(128)S(6)} %select_n.107), kind=kLoop, calls=%fused_computation.33 | loop fusion | bytes 524292 | tf_op jit(solution)/shard_map/dynamic_slice | solution.py:272
  56.6 2.6 %collective-permute-done.refs_1_ = bf16[192,512]{1,0:T(8,128)(2,1)S(1)} collective-permute-done((bf16[192,512]{1,0:T(8,128)(2,1)S(1)}, bf16[192,512]{1,0:T(8,128)(2,1)S(1)}, u32[]{:S(2)}, u32[]{:S(2)}) %collective-permute-start) | collective-permute-done | bytes 196640 | tf_op jit(solution)/shard_map/ppermute | solution.py:258
  59.2 1.0 %copy-done.2 = bf16[512,512]{1,0:T(8,128)(2,1)S(1)} copy-done((bf16[512,512]{1,0:T(8,128)(2,1)S(1)}, bf16[512,512]{1,0:T(8,128)(2,1)}, u32[]{:S(2)}) %copy-start.2) | copy-done | bytes 524312
  61.0 3.1 %front.1 = (f32[192,512]{1,0:T(8,128)S(1)}, bf16[4,384,128]{2,1,0:T(8,128)(2,1)S(1)}) custom-call(bf16[192,512]{1,0:T(8,128)(2,1)S(1)} %reshape.184.refs_0_, bf16[192,512]{1,0:T(8,128)(2,1)S(1)} %collective-permute-done.refs_1_, s32[12,1]{1,0:T(8,128)S(1)} %xor_select_fusion.refs_2_, s32[48,12]{1,0:T(8,128)S(1)} %copy-done.21, f32[1,512]{1,0:T(1,128)S(1)} %bitcast.46, ...), custom_call_target="tpu_custom_call" | custom-call | flops 1006632960 | bytes 4194304 | tf_op jit(solution)/shard_map/front/pallas_call | solution.py:153
  73.4 1.0 %copy-done.25 = bf16[4,384,128]{2,1,0:T(8,128)(2,1)S(1)} copy-done((bf16[4,384,128]{2,1,0:T(8,128)(2,1)S(1)}, bf16[4,384,128]{2,1,0:T(8,128)(2,1)}, u32[]{:S(2)}) %copy-start.25) | copy-done | bytes 393240
  74.4 4.6 %attend.1 = (bf16[192,256]{1,0:T(8,128)(2,1)S(1)}, bf16[192,256]{1,0:T(8,128)(2,1)S(1)}) custom-call(bf16[4,384,128]{2,1,0:T(8,128)(2,1)S(1)} %copy-done.25, bf16[1,4,128,128]{3,2,1,0:T(8,128)(2,1)S(1)} %bitcast.45, bf16[1,4,128,128]{3,2,1,0:T(8,128)(2,1)S(1)} %copy-done.8, bf16[1,4,128,128]{3,2,1,0:T(8,128)(2,1)S(1)} %copy-done.10, ...), custom_call_target="tpu_custom_call" | custom-call | flops 1610612736 | bytes 4194304 | tf_op jit(solution)/shard_map/attend/pallas_call | solution.py:212
  79.1 1.6 %collective-permute-start.10 = (bf16[192,256]{1,0:T(8,128)(2,1)S(1)}, bf16[192,256]{1,0:T(8,128)(2,1)S(1)}, u32[]{:S(2)}, u32[]{:S(2)}) collective-permute-start(bf16[192,256]{1,0:T(8,128)(2,1)S(1)} %get-tuple-element.28), channel_id=1, source_target_pairs={{0,1},{1,0},{2,3},{3,2},{4,5},{5,4},{6,7},{7,6},{8,9},{9,8},{10,11... | collective-permute-start | bytes 294920 | tf_op jit(solution)/shard_map/ppermute | solution.py:279
  80.8 2.9 %collective-permute-done.10 = bf16[192,256]{1,0:T(8,128)(2,1)S(1)} collective-permute-done((bf16[192,256]{1,0:T(8,128)(2,1)S(1)}, bf16[192,256]{1,0:T(8,128)(2,1)S(1)}, u32[]{:S(2)}, u32[]{:S(2)}) %collective-permute-start.10) | collective-permute-done | bytes 98336 | tf_op jit(solution)/shard_map/ppermute | solution.py:279
  (79 shorter events, 21.2 us)
Async XLA Ops:
  0.0 80.6 %copy-start = (bf16[512,512]{1,0:T(8,128)(2,1)S(1)}, bf16[512,512]{1,0:T(8,128)(2,1)}, u32[]{:S(2)}) copy-start(bf16[512,512]{1,0:T(8,128)(2,1)} %param.16) | copy-start | bytes 1572868
  0.0 5.4 %copy-start.27 = (s32[1,12]{1,0:T(1,128)S(1)}, s32[1,12]{1,0:T(1,128)}, u32[]{:S(2)}) copy-start(s32[1,12]{1,0:T(1,128)} %param.18) | copy-start | bytes 148
  1.3 22.5 %collective-permute-start.1 = (bf16[4,2,128,128]{3,2,1,0:T(8,128)(2,1)S(1)}, bf16[4,2,128,128]{3,2,1,0:T(8,128)(2,1)S(1)}, u32[]{:S(2)}, u32[]{:S(2)}) collective-permute-start(bf16[4,2,128,128]{3,2,1,0:T(8,128)(2,1)S(1)} %get-tuple-element.30), channel_id=1, source_target_pairs={{0,16},{2,18},{4,20},{6,22},{8,24},{10,26},{12,28},{14,30},{16,0},... | collective-permute-start | bytes 786440 | tf_op jit(solution)/shard_map/ppermute | solution.py:247
  6.3 8.6 %all-to-all-start = ((s32[8,2,128]{2,1,0:T(2,128)}), s32[8,2,128]{2,1,0:T(2,128)S(1)}, u32[]{:S(2)}, u32[]{:S(2)}) async-start(s32[8,2,128]{2,1,0:T(2,128)} %broadcast_in_dim.50), calls=%async_computation | async-start | bytes 16384 | tf_op jit(solution)/shard_map/all_to_all | solution.py:243
  10.1 18.5 %collective-permute-start.2 = (bf16[4,2,128,128]{3,2,1,0:T(8,128)(2,1)S(1)}, bf16[4,2,128,128]{3,2,1,0:T(8,128)(2,1)S(1)}, u32[]{:S(2)}, u32[]{:S(2)}) collective-permute-start(bf16[4,2,128,128]{3,2,1,0:T(8,128)(2,1)S(1)} %get-tuple-element.29), channel_id=1, source_target_pairs={{0,16},{2,18},{4,20},{6,22},{8,24},{10,26},{12,28},{14,30},{16,0},... | collective-permute-start | bytes 786440 | tf_op jit(solution)/shard_map/ppermute | solution.py:247
  24.4 4.5 %collective-permute-start.3 = (bf16[1,4,128,128]{3,2,1,0:T(8,128)(2,1)S(1)}, bf16[1,4,128,128]{3,2,1,0:T(8,128)(2,1)S(1)}, u32[]{:S(2)}, u32[]{:S(2)}) collective-permute-start(bf16[1,4,128,128]{3,2,1,0:T(8,128)(2,1)S(1)} %bitcast.54), channel_id=1, source_target_pairs={{0,2},{2,0},{4,6},{6,4},{8,10},{10,8},{12,14},{14,12},{16,18},{18,... | collective-permute-start | bytes 393224 | tf_op jit(solution)/shard_map/ppermute | solution.py:266
  24.5 6.3 %collective-permute-start.4 = (bf16[1,4,128,128]{3,2,1,0:T(8,128)(2,1)S(1)}, bf16[1,4,128,128]{3,2,1,0:T(8,128)(2,1)S(1)}, u32[]{:S(2)}, u32[]{:S(2)}) collective-permute-start(bf16[1,4,128,128]{3,2,1,0:T(8,128)(2,1)S(1)} %bitcast.53), channel_id=1, source_target_pairs={{0,4},{2,6},{4,0},{6,2},{8,12},{10,14},{12,8},{14,10},{16,20},{18,... | collective-permute-start | bytes 393224 | tf_op jit(solution)/shard_map/ppermute | solution.py:266
  26.4 6.5 %collective-permute-start.5 = (bf16[1,4,128,128]{3,2,1,0:T(8,128)(2,1)S(1)}, bf16[1,4,128,128]{3,2,1,0:T(8,128)(2,1)S(1)}, u32[]{:S(2)}, u32[]{:S(2)}) collective-permute-start(bf16[1,4,128,128]{3,2,1,0:T(8,128)(2,1)S(1)} %bitcast.52), channel_id=1, source_target_pairs={{0,6},{2,4},{4,2},{6,0},{8,14},{10,12},{12,10},{14,8},{16,22},{18,... | collective-permute-start | bytes 393224 | tf_op jit(solution)/shard_map/ppermute | solution.py:266
  26.4 6.5 %collective-permute-start.6 = (bf16[1,4,128,128]{3,2,1,0:T(8,128)(2,1)S(1)}, bf16[1,4,128,128]{3,2,1,0:T(8,128)(2,1)S(1)}, u32[]{:S(2)}, u32[]{:S(2)}) collective-permute-start(bf16[1,4,128,128]{3,2,1,0:T(8,128)(2,1)S(1)} %bitcast.51), channel_id=1, source_target_pairs={{0,8},{2,10},{4,12},{6,14},{8,0},{10,2},{12,4},{14,6},{16,24},{18,... | collective-permute-start | bytes 393224 | tf_op jit(solution)/shard_map/ppermute | solution.py:266
  28.6 5.9 %collective-permute-start.7 = (bf16[1,4,128,128]{3,2,1,0:T(8,128)(2,1)S(1)}, bf16[1,4,128,128]{3,2,1,0:T(8,128)(2,1)S(1)}, u32[]{:S(2)}, u32[]{:S(2)}) collective-permute-start(bf16[1,4,128,128]{3,2,1,0:T(8,128)(2,1)S(1)} %bitcast.50), channel_id=1, source_target_pairs={{0,10},{2,8},{4,14},{6,12},{8,2},{10,0},{12,6},{14,4},{16,26},{18,... | collective-permute-start | bytes 393224 | tf_op jit(solution)/shard_map/ppermute | solution.py:266
  28.9 10.7 %collective-permute-start.8 = (bf16[1,4,128,128]{3,2,1,0:T(8,128)(2,1)S(1)}, bf16[1,4,128,128]{3,2,1,0:T(8,128)(2,1)S(1)}, u32[]{:S(2)}, u32[]{:S(2)}) collective-permute-start(bf16[1,4,128,128]{3,2,1,0:T(8,128)(2,1)S(1)} %bitcast.49), channel_id=1, source_target_pairs={{0,12},{2,14},{4,8},{6,10},{8,4},{10,6},{12,0},{14,2},{16,28},{18,... | collective-permute-start | bytes 393224 | tf_op jit(solution)/shard_map/ppermute | solution.py:266
  30.8 10.4 %collective-permute-start.9 = (bf16[1,4,128,128]{3,2,1,0:T(8,128)(2,1)S(1)}, bf16[1,4,128,128]{3,2,1,0:T(8,128)(2,1)S(1)}, u32[]{:S(2)}, u32[]{:S(2)}) collective-permute-start(bf16[1,4,128,128]{3,2,1,0:T(8,128)(2,1)S(1)} %bitcast.48), channel_id=1, source_target_pairs={{0,14},{2,12},{4,10},{6,8},{8,6},{10,4},{12,2},{14,0},{16,30},{18,... | collective-permute-start | bytes 393224 | tf_op jit(solution)/shard_map/ppermute | solution.py:266
  48.1 3.7 %copy-start.26 = (bf16[48,4,512]{2,1,0:T(4,128)(2,1)S(1)}, bf16[48,4,512]{2,1,0:T(4,128)(2,1)}, u32[]{:S(2)}) copy-start(bf16[48,4,512]{2,1,0:T(4,128)(2,1)} %param.10) | copy-start | bytes 589828
  48.1 11.1 %copy-start.1 = (bf16[512,1536]{1,0:T(8,128)(2,1)S(1)}, bf16[512,1536]{1,0:T(8,128)(2,1)}, u32[]{:S(2)}) copy-start(bf16[512,1536]{1,0:T(8,128)(2,1)} %refs_5_.1) | copy-start | bytes 4718596
  48.1 11.1 %copy-start.22 = (f32[512]{0:T(512)S(1)}, f32[512]{0:T(512)}, u32[]{:S(2)}) copy-start(f32[512]{0:T(512)} %param.11) | copy-start | bytes 6148
  48.1 11.1 %copy-start.23 = (f32[512]{0:T(512)S(1)}, f32[512]{0:T(512)}, u32[]{:S(2)}) copy-start(f32[512]{0:T(512)} %param.14) | copy-start | bytes 6148
  48.1 18.1 %all-to-all-start.1 = ((bf16[8,4,128,128]{3,2,1,0:T(8,128)(2,1)}), bf16[8,4,128,128]{3,2,1,0:T(8,128)(2,1)S(1)}, u32[]{:S(2)}, u32[]{:S(2)}) async-start(bf16[8,4,128,128]{3,2,1,0:T(8,128)(2,1)} %pick.1.refs_9_), calls=%async_computation.1 | async-start | bytes 2097152 | tf_op jit(solution)/shard_map/all_to_all | solution.py:243
  51.9 7.3 %collective-permute-start = (bf16[192,512]{1,0:T(8,128)(2,1)S(1)}, bf16[192,512]{1,0:T(8,128)(2,1)S(1)}, u32[]{:S(2)}, u32[]{:S(2)}) collective-permute-start(bf16[192,512]{1,0:T(8,128)(2,1)S(1)} %reshape.184.refs_0_), channel_id=1, source_target_pairs={{0,1},{1,0},{2,3},{3,2},{4,5},{5,4},{6,7},{7,6},{8,9},{9,8},{10,11... | collective-permute-start | bytes 589832 | tf_op jit(solution)/shard_map/ppermute | solution.py:258
  59.2 1.0 %copy-start.2 = (bf16[512,512]{1,0:T(8,128)(2,1)S(1)}, bf16[512,512]{1,0:T(8,128)(2,1)}, u32[]{:S(2)}) copy-start(bf16[512,512]{1,0:T(8,128)(2,1)} %refs_6_.1) | copy-start | bytes 1572868
  66.2 0.9 %copy-start.6 = (bf16[4,128,128]{2,1,0:T(8,128)(2,1)S(1)}, bf16[4,128,128]{2,1,0:T(8,128)(2,1)}, u32[]{:S(2)}) copy-start(bf16[4,128,128]{2,1,0:T(8,128)(2,1)} %copy-done.5) | copy-start | bytes 393220
  67.1 0.9 %copy-start.8 = (bf16[1,4,128,128]{3,2,1,0:T(8,128)(2,1)S(1)}, bf16[1,4,128,128]{3,2,1,0:T(8,128)(2,1)}, u32[]{:S(2)}) copy-start(bf16[1,4,128,128]{3,2,1,0:T(8,128)(2,1)} %copy-done.7) | copy-start | bytes 393220
  73.4 1.0 %copy-start.25 = (bf16[4,384,128]{2,1,0:T(8,128)(2,1)S(1)}, bf16[4,384,128]{2,1,0:T(8,128)(2,1)}, u32[]{:S(2)}) copy-start(bf16[4,384,128]{2,1,0:T(8,128)(2,1)} %copy-done.24) | copy-start | bytes 1179652
  74.4 9.3 %copy-start.4 = (f32[192,512]{1,0:T(8,128)S(1)}, f32[192,512]{1,0:T(8,128)}, u32[]{:S(2)}) copy-start(f32[192,512]{1,0:T(8,128)} %copy-done.3) | copy-start | bytes 1179652
  79.1 4.7 %collective-permute-start.10 = (bf16[192,256]{1,0:T(8,128)(2,1)S(1)}, bf16[192,256]{1,0:T(8,128)(2,1)S(1)}, u32[]{:S(2)}, u32[]{:S(2)}) collective-permute-start(bf16[192,256]{1,0:T(8,128)(2,1)S(1)} %get-tuple-element.28), channel_id=1, source_target_pairs={{0,1},{1,0},{2,3},{3,2},{4,5},{5,4},{6,7},{7,6},{8,9},{9,8},{10,11... | collective-permute-start | bytes 294920 | tf_op jit(solution)/shard_map/ppermute | solution.py:279
  (17 other events, 12.9 us)

commit v7 on v6

--- a/solution.py
+++ b/solution.py
@@ -59,24 +59,30 @@
     )(wanted, *tiles, *after)
 
 
-def pick_each_kernel(wanted_ref, me_ref, tiles_ref, *refs):
-    out_refs = refs[-wanted_ref.shape[0]:]
+def pick_each_kernel(parts, wanted_ref, me_ref, *refs):
+    tile_refs, out_refs = refs[:parts], refs[-wanted_ref.shape[0]:]
     for step, out_ref in enumerate(out_refs):
-        out_ref[...] = tiles_ref[wanted_ref[me_ref[0] ^ step]]
+        tile = wanted_ref[me_ref[0] ^ step]
+        low = 0
+        for tiles_ref in tile_refs:
+            high = low + tiles_ref.shape[1]
+            out_ref[0, low:high] = tiles_ref[tile]
+            low = high
 
 
 def pick_each(tiles, wanted, me, after):
     count = wanted.shape[0]
+    heads = sum(part.shape[1] for part in tiles)
     smem = pl.BlockSpec(memory_space=pltpu.SMEM)
     return pl.pallas_call(
-        pick_each_kernel,
-        out_shape=(jax.ShapeDtypeStruct(tiles.shape[1:], tiles.dtype),) * count,
-        in_specs=[smem, smem, VMEM] + [ANY] * len(after),
+        functools.partial(pick_each_kernel, len(tiles)),
+        out_shape=(jax.ShapeDtypeStruct((1, heads) + tiles[0].shape[2:], tiles[0].dtype),) * count,
+        in_specs=[smem, smem] + [VMEM] * len(tiles) + [ANY] * len(after),
         out_specs=(VMEM,) * count,
         compiler_params=params(0),
         cost_estimate=pl.CostEstimate(flops=0, bytes_accessed=2 * MIB, transcendentals=0),
         name="pick_each",
-    )(wanted, me, tiles, *after)
+    )(wanted, me, *tiles, *after)
 
 
 def front_kernel(groups, heads, head_size, chunk, cols, row_size, *refs):
@@ -242,10 +248,9 @@
     def swap(value):
         return lax.all_to_all(value, "rows", split_axis=0, concat_axis=0, tiled=True, axis_index_groups=halves)
 
-    middle = max(heads_here // 2, 1)
     heads_first = jnp.transpose(tile_kv, (0, 2, 1, 3))
-    mirrored = [lax.ppermute(heads_first[:, low:low + middle], "rows", turn(row_size, half))
-                for low in range(0, heads_here, middle)]
+    parts = [(0, 1), (1, heads_here)] if heads_here > 1 else [(0, 1)]
+    mirrored = [lax.ppermute(heads_first[:, low:high], "rows", turn(row_size, half)) for low, high in parts]
 
     listed = tile_ids[0] >= 0
     holder = jnp.where(listed, (tile_ids[0] // tiles_here + my_half * half) % row_size, -1)
@@ -259,20 +264,26 @@
 
     near_by, far_by = asked_by[:, 0], asked_by[:, 1]
     if half <= 8 and half & (half - 1) == 0:
-        sent = pick_each(heads_first, near_by, my_place.reshape(1), mirrored[:1])
-        near = [sent[0][None]]
-        for step in range(1, half):
-            pairs = [(row, row // half * half + (row % half ^ step)) for row in range(row_size)]
-            near.append(lax.ppermute(sent[step][None], "rows", pairs))
-        holder = jnp.where((holder >= 0) & (holder < half), holder ^ my_place, holder)
+        holder = jnp.where(holder < 0, holder, holder ^ my_place)
+
+        def spread(tiles, wanted, after):
+            picked = pick_each(tiles, wanted, my_place.reshape(1), after)
+            arrived = [picked[0]]
+            for step in range(1, half):
+                pairs = [(row, row // half * half + (row % half ^ step)) for row in range(row_size)]
+                arrived.append(lax.ppermute(picked[step], "rows", pairs))
+            return picked[0], arrived
     else:
-        near = [swap(pick([heads_first], near_by, mirrored[:1]))]
-    sent = pick(mirrored, far_by, near)
-    far = swap(sent)
+        def spread(tiles, wanted, after):
+            picked = pick(tiles, wanted, after)
+            return picked, [swap(picked)]
+
+    picked, near = spread([heads_first], near_by, mirrored[:1])
+    picked, far = spread(mirrored, far_by, near)
     query_here = lax.dynamic_slice_in_dim(w_query, col_me * group_width, group_width, 1)
     residual, asked = front(cells, holder[:, None], key_mask, gain_col, w_qkv, w_col_out, gain_tile, query_here,
-                            heads_all, head_size, cols, row_size, sent)
-    answers = attend(asked, near + [far], col_size, cols)
+                            heads_all, head_size, cols, row_size, picked)
+    answers = attend(asked, near + far, col_size, cols)
 
     final = residual
     for step in range(col_size):

time: 85.3 us -> 76.3 us (0.89)
  local copies, waits for them, and re-layouts: 22.8 us -> 5.29 us
  waiting for transfers between devices: 31.6 us -> 36.3 us
  Pallas kernels: 9.99 us -> 11.7 us
  starting transfers between devices: 19.6 us -> 21.3 us
    unnamed x58 -> x20, local copies, waits for them, and re-layouts: 19.3 us -> 2.66 us
    ppermute x9 -> x16, waiting for transfers between devices: 21.1 us -> 32.9 us  [the longest x14 18.3 us: spread(): arrived.append(lax.ppermute(picked[step], 'rows', pairs))]
    all_to_all x2 -> x1, waiting for transfers between devices: 5.09 us -> 0.01 us  [swap(): lax.all_to_all(value, 'rows', split_axis=0, concat_axis=0, tiled=True, ax...]
    ppermute x9 -> x16, starting transfers between devices: 8.91 us -> 12.9 us  [the longest x14 9.9 us: spread(): arrived.append(lax.ppermute(picked[step], 'rows', pairs))]
    ppermute x1, waiting for transfers between devices: 2.59 us -> 0.01 us  [shards(): cells.append(lax.ppermute(cells[0], 'cols', turn(col_size, -step)))]
    all_to_all x2 -> x1, starting transfers between devices: 7.48 us -> 5.25 us  [swap(): lax.all_to_all(value, 'rows', split_axis=0, concat_axis=0, tiled=True, ax...]
    pallas_call x1, Pallas kernels: 4.64 us -> 5.86 us  [attend(): pl.pallas_call(functools.partial(attend_kernel, groups, len(tiles), ROW_G...]
    dynamic_slice x1, local copies, waits for them, and re-layouts: 0.97 us -> 0.02 us  [shards(): lax.dynamic_slice_in_dim(w_query, col_me * group_width, group_width, 1)]
  transfers between devices with their start and end apart: 13 -> 19, of which waited for: 11 -> 10; matrix products, arithmetic and copies ran while one was open for 5% -> 3% of each run, Pallas kernels for 4% -> 8%
where the time goes in v7:
time: 76.3 us; the launch traced here: 76.1 us
  waiting for transfers between devices  36.3 us (48%)
  starting transfers between devices  21.3 us (28%)
  Pallas kernels  11.7 us (15%)
  local copies, waits for them, and re-layouts  5.29 us (7%)
  other arithmetic  0.85 us (1%)
    ppermute x14, waiting for transfers between devices, spread(): arrived.append(lax.ppermute(picked[step], 'rows', pairs))  18.3 us
    ppermute x2, waiting for transfers between devices, shards(): lax.ppermute(heads_first[:, low:high], 'rows', turn(row_size, half))  14.6 us
    ppermute x14, starting transfers between devices, spread(): arrived.append(lax.ppermute(picked[step], 'rows', pairs))  9.9 us
    pallas_call x1, Pallas kernels, attend(): pl.pallas_call(functools.partial(attend_kernel, groups, len(tiles), ROW_G...  5.86 us
    all_to_all x1, starting transfers between devices, swap(): lax.all_to_all(value, 'rows', split_axis=0, concat_axis=0, tiled=True, ax...  5.25 us
    ppermute x1, waiting for transfers between devices, shards(): lax.ppermute(answers[step], 'cols', turn(col_size, step))  3.4 us
    pallas_call x1, Pallas kernels, front(): pl.pallas_call(functools.partial(front_kernel, groups, heads, head_size,...  3.11 us
    ppermute x2, starting transfers between devices, shards(): lax.ppermute(heads_first[:, low:high], 'rows', turn(row_size, half))  2.99 us
  transfers between devices with their start and end apart: 19, of which 10 were waited for; matrix products, arithmetic and copies ran while one was open for 3% of the time, Pallas kernels for 8%

profile of v7, /device:TPU:0, one launch (start us, length us, event | category | flops | bytes accessed | tf_op | source)
XLA Modules:
  0.0 76.1 jit_solution(173842933934001504)
XLA Ops:
  1.7 5.2 %all-to-all-start = ((s32[8,2,128]{2,1,0:T(2,128)}), s32[8,2,128]{2,1,0:T(2,128)S(1)}, u32[]{:S(2)}, u32[]{:S(2)}) async-start(s32[8,2,128]{2,1,0:T(2,128)} %broadcast_in_dim.26), calls=%async_computation | async-start | bytes 16384 | tf_op jit(solution)/shard_map/all_to_all | solution.py:249
  6.9 1.1 %copy.37 = bf16[4,128,4,128]{3,1,2,0:T(8,128)(2,1)S(1)} copy(bf16[4,128,4,128]{3,2,1,0:T(4,128)(2,1)} %param.17) | data formatting | bytes 1048576 | tf_op args[7]
  8.1 2.7 %collective-permute-start.1 = (bf16[4,1,128,128]{3,2,1,0:T(8,128)(2,1)S(1)}, bf16[4,1,128,128]{3,2,1,0:T(8,128)(2,1)S(1)}, u32[]{:S(2)}, u32[]{:S(2)}) collective-permute-start(bf16[4,1,128,128]{3,2,1,0:T(8,128)(2,1)S(1)} %slice.21), channel_id=1, source_target_pairs={{0,16},{2,18},{4,20},{6,22},{8,24},{10,26},{12,28},{14,30},{16,0},... | collective-permute-start | bytes 393224 | tf_op jit(solution)/shard_map/ppermute | solution.py:253
  12.0 14.6 %collective-permute-done.1.refs_1_.refs_0_ = bf16[4,1,128,128]{3,2,1,0:T(8,128)(2,1)S(1)} collective-permute-done((bf16[4,1,128,128]{3,2,1,0:T(8,128)(2,1)S(1)}, bf16[4,1,128,128]{3,2,1,0:T(8,128)(2,1)S(1)}, u32[]{:S(2)}, u32[]{:S(2)}) %collective-permute-start.1) | collective-permute-done | bytes 131104 | tf_op jit(solution)/shard_map/ppermute | solution.py:253
  26.6 1.3 %pick_each.2 = (bf16[1,4,128,128]{3,2,1,0:T(8,128)(2,1)S(1)}, bf16[1,4,128,128]{3,2,1,0:T(8,128)(2,1)S(1)}, bf16[1,4,128,128]{3,2,1,0:T(8,128)(2,1)S(1)}, bf16[1...) custom-call(s32[8]{0:T(128)S(1)} %get-tuple-element.45.wanted_ref, ...), custom_call_target="tpu_custom_call" | custom-call | bytes 2097152 | tf_op jit(solution)/shard_map/pick_each/pallas_call | solution.py:77
  27.9 2.1 %collective-permute-start.4 = (bf16[1,4,128,128]{3,2,1,0:T(8,128)(2,1)S(1)}, bf16[1,4,128,128]{3,2,1,0:T(8,128)(2,1)S(1)}, u32[]{:S(2)}, u32[]{:S(2)}) collective-permute-start(bf16[1,4,128,128]{3,2,1,0:T(8,128)(2,1)S(1)} %get-tuple-element.27), channel_id=1, source_target_pairs={{0,4},{2,6},{4,0},{6,2},{8,12},{10,14},{12,8},{14,10},{16,20},{18,... | collective-permute-start | bytes 393224 | tf_op jit(solution)/shard_map/ppermute | solution.py:274
  30.1 1.4 %collective-permute-start.7 = (bf16[1,4,128,128]{3,2,1,0:T(8,128)(2,1)}, bf16[1,4,128,128]{3,2,1,0:T(8,128)(2,1)S(1)}, u32[]{:S(2)}, u32[]{:S(2)}) collective-permute-start(bf16[1,4,128,128]{3,2,1,0:T(8,128)(2,1)} %get-tuple-element.30), channel_id=1, source_target_pairs={{0,10},{2,8},{4,14},{6,12},{8,2},{10,0},{12,6},{14,4},{16,26},{18,... | collective-permute-start | bytes 393224 | tf_op jit(solution)/shard_map/ppermute | solution.py:274
  31.6 2.8 %collective-permute-done.4.refs_4_.refs_2_ = bf16[1,4,128,128]{3,2,1,0:T(8,128)(2,1)S(1)} collective-permute-done((bf16[1,4,128,128]{3,2,1,0:T(8,128)(2,1)S(1)}, bf16[1,4,128,128]{3,2,1,0:T(8,128)(2,1)S(1)}, u32[]{:S(2)}, u32[]{:S(2)}) %collective-permute-start.4) | collective-permute-done | bytes 131104 | tf_op jit(solution)/shard_map/ppermute | solution.py:274
  34.3 1.3 %collective-permute-start.8 = (bf16[1,4,128,128]{3,2,1,0:T(8,128)(2,1)}, bf16[1,4,128,128]{3,2,1,0:T(8,128)(2,1)S(1)}, u32[]{:S(2)}, u32[]{:S(2)}) collective-permute-start(bf16[1,4,128,128]{3,2,1,0:T(8,128)(2,1)} %get-tuple-element.31), channel_id=1, source_target_pairs={{0,12},{2,14},{4,8},{6,10},{8,4},{10,6},{12,0},{14,2},{16,28},{18,... | collective-permute-start | bytes 393224 | tf_op jit(solution)/shard_map/ppermute | solution.py:274
  35.7 1.1 %collective-permute-done.5.refs_5_.refs_3_ = bf16[1,4,128,128]{3,2,1,0:T(8,128)(2,1)S(1)} collective-permute-done((bf16[1,4,128,128]{3,2,1,0:T(8,128)(2,1)S(1)}, bf16[1,4,128,128]{3,2,1,0:T(8,128)(2,1)S(1)}, u32[]{:S(2)}, u32[]{:S(2)}) %collective-permute-start.5) | collective-permute-done | bytes 131104 | tf_op jit(solution)/shard_map/ppermute | solution.py:274
  38.0 1.6 %collective-permute-start = (bf16[192,512]{1,0:T(8,128)(2,1)S(1)}, bf16[192,512]{1,0:T(8,128)(2,1)S(1)}, u32[]{:S(2)}, u32[]{:S(2)}) collective-permute-start(bf16[192,512]{1,0:T(8,128)(2,1)S(1)} %reshape.179.refs_0_), channel_id=1, source_target_pairs={{0,1},{1,0},{2,3},{3,2},{4,5},{5,4},{6,7},{7,6},{8,9},{9,8},{10,11... | collective-permute-start | bytes 589832 | tf_op jit(solution)/shard_map/ppermute | solution.py:263
  40.2 4.1 %collective-permute-done.8.refs_8_.refs_6_ = bf16[1,4,128,128]{3,2,1,0:T(8,128)(2,1)S(1)} collective-permute-done((bf16[1,4,128,128]{3,2,1,0:T(8,128)(2,1)}, bf16[1,4,128,128]{3,2,1,0:T(8,128)(2,1)S(1)}, u32[]{:S(2)}, u32[]{:S(2)}) %collective-permute-start.8) | collective-permute-done | bytes 131104 | tf_op jit(solution)/shard_map/ppermute | solution.py:274
  44.2 2.7 %collective-permute-done.9.refs_9_.refs_7_ = bf16[1,4,128,128]{3,2,1,0:T(8,128)(2,1)S(1)} collective-permute-done((bf16[1,4,128,128]{3,2,1,0:T(8,128)(2,1)S(1)}, bf16[1,4,128,128]{3,2,1,0:T(8,128)(2,1)S(1)}, u32[]{:S(2)}, u32[]{:S(2)}) %collective-permute-start.9) | collective-permute-done | bytes 131104 | tf_op jit(solution)/shard_map/ppermute | solution.py:274
  46.9 1.4 %pick_each.3 = (bf16[1,4,128,128]{3,2,1,0:T(8,128)(2,1)S(1)}, bf16[1,4,128,128]{3,2,1,0:T(8,128)(2,1)S(1)}, bf16[1,4,128,128]{3,2,1,0:T(8,128)(2,1)S(1)}, bf16[1...) custom-call(s32[8]{0:T(128)S(1)} %get-tuple-element.46.wanted_ref, ...), custom_call_target="tpu_custom_call" | custom-call | bytes 2097152 | tf_op jit(solution)/shard_map/pick_each/pallas_call | solution.py:77
  48.8 1.4 %collective-permute-start.12 = (bf16[1,4,128,128]{3,2,1,0:T(8,128)(2,1)}, bf16[1,4,128,128]{3,2,1,0:T(8,128)(2,1)S(1)}, u32[]{:S(2)}, u32[]{:S(2)}) collective-permute-start(bf16[1,4,128,128]{3,2,1,0:T(8,128)(2,1)} %get-tuple-element.38), channel_id=1, source_target_pairs={{0,6},{2,4},{4,2},{6,0},{8,14},{10,12},{12,10},{14,8},{16,22},{18,... | collective-permute-start | bytes 393224 | tf_op jit(solution)/shard_map/ppermute | solution.py:274
  50.3 1.8 %collective-permute-start.14 = (bf16[1,4,128,128]{3,2,1,0:T(8,128)(2,1)}, bf16[1,4,128,128]{3,2,1,0:T(8,128)(2,1)}, u32[]{:S(2)}, u32[]{:S(2)}) collective-permute-start(bf16[1,4,128,128]{3,2,1,0:T(8,128)(2,1)} %get-tuple-element.40), channel_id=1, source_target_pairs={{0,10},{2,8},{4,14},{6,12},{8,2},{10,0},{12,6},{14,4},{16,26},{18,... | collective-permute-start | bytes 393224 | tf_op jit(solution)/shard_map/ppermute | solution.py:274
  52.2 2.5 %collective-permute-done.11.refs_10_ = bf16[1,4,128,128]{3,2,1,0:T(8,128)(2,1)S(1)} collective-permute-done((bf16[1,4,128,128]{3,2,1,0:T(8,128)(2,1)S(1)}, bf16[1,4,128,128]{3,2,1,0:T(8,128)(2,1)S(1)}, u32[]{:S(2)}, u32[]{:S(2)}) %collective-permute-start.11) | collective-permute-done | bytes 131104 | tf_op jit(solution)/shard_map/ppermute | solution.py:274
  55.0 1.4 %copy-done.1 = bf16[512,1536]{1,0:T(8,128)(2,1)S(1)} copy-done((bf16[512,1536]{1,0:T(8,128)(2,1)S(1)}, bf16[512,1536]{1,0:T(8,128)(2,1)}, u32[]{:S(2)}) %copy-start.1) | copy-done | bytes 1572888
  56.4 3.1 %front.1 = (f32[192,512]{1,0:T(8,128)S(1)}, bf16[4,384,128]{2,1,0:T(8,128)(2,1)S(1)}) custom-call(bf16[192,512]{1,0:T(8,128)(2,1)S(1)} %reshape.179.refs_0_, bf16[192,512]{1,0:T(8,128)(2,1)S(1)} %collective-permute-done.refs_1_, s32[12,1]{1,0:T(8,128)S(1)} %compare_select_fusion.refs_2_, s32[48,12]{1,0:T(8,128)S(1)} %copy.35.refs_3_, f32[1,512]{1,0:T(1,128)S(1)} %bitcast.37, ...), custom_call_target="tpu_custom_call" | custom-call | flops 1006632960 | bytes 4194304 | tf_op jit(solution)/shard_map/front/pallas_call | solution.py:159
  59.5 2.9 %collective-permute-done.15.refs_14_ = bf16[1,4,128,128]{3,2,1,0:T(8,128)(2,1)} collective-permute-done((bf16[1,4,128,128]{3,2,1,0:T(8,128)(2,1)}, bf16[1,4,128,128]{3,2,1,0:T(8,128)(2,1)}, u32[]{:S(2)}, u32[]{:S(2)}) %collective-permute-start.15) | collective-permute-done | bytes 131104 | tf_op jit(solution)/shard_map/ppermute | solution.py:274
  62.4 1.7 %collective-permute-done.16.refs_15_ = bf16[1,4,128,128]{3,2,1,0:T(8,128)(2,1)} collective-permute-done((bf16[1,4,128,128]{3,2,1,0:T(8,128)(2,1)}, bf16[1,4,128,128]{3,2,1,0:T(8,128)(2,1)}, u32[]{:S(2)}, u32[]{:S(2)}) %collective-permute-start.16) | collective-permute-done | bytes 131104 | tf_op jit(solution)/shard_map/ppermute | solution.py:274
  64.0 5.9 %attend.1 = (bf16[192,256]{1,0:T(8,128)(2,1)S(1)}, bf16[192,256]{1,0:T(8,128)(2,1)S(1)}) custom-call(bf16[4,384,128]{2,1,0:T(8,128)(2,1)S(1)} %get-tuple-element.35.asked_ref, bf16[1,4,128,128]{3,2,1,0:T(8,128)(2,1)S(1)} %get-tuple-element.25.refs_2_.refs_0_, bf16[1,4,128,128]{3,2,1,0:T(8,128)(2,1)S(1)} %collective-permute-done.3.refs_3_.refs_1_, ...), custom_call_target="tpu_custom_call" | custom-call | flops 1610612736 | bytes 4194304 | tf_op jit(solution)/shard_map/attend/pallas_call | solution.py:218
  69.9 1.6 %collective-permute-start.17 = (bf16[192,256]{1,0:T(8,128)(2,1)S(1)}, bf16[192,256]{1,0:T(8,128)(2,1)S(1)}, u32[]{:S(2)}, u32[]{:S(2)}) collective-permute-start(bf16[192,256]{1,0:T(8,128)(2,1)S(1)} %get-tuple-element.44), channel_id=1, source_target_pairs={{0,1},{1,0},{2,3},{3,2},{4,5},{5,4},{6,7},{7,6},{8,9},{9,8},{10,11... | collective-permute-start | bytes 294920 | tf_op jit(solution)/shard_map/ppermute | solution.py:290
  71.7 3.4 %collective-permute-done.17 = bf16[192,256]{1,0:T(8,128)(2,1)S(1)} collective-permute-done((bf16[192,256]{1,0:T(8,128)(2,1)S(1)}, bf16[192,256]{1,0:T(8,128)(2,1)S(1)}, u32[]{:S(2)}, u32[]{:S(2)}) %collective-permute-start.17) | collective-permute-done | bytes 98336 | tf_op jit(solution)/shard_map/ppermute | solution.py:290
  (54 shorter events, 6.8 us)
Async XLA Ops:
  0.0 71.5 %copy-start = (bf16[512,512]{1,0:T(8,128)(2,1)S(1)}, bf16[512,512]{1,0:T(8,128)(2,1)}, u32[]{:S(2)}) copy-start(bf16[512,512]{1,0:T(8,128)(2,1)} %param.16) | copy-start | bytes 1572868
  0.0 37.8 %copy-start.8 = (s32[1,12]{1,0:T(1,128)S(1)}, s32[1,12]{1,0:T(1,128)}, u32[]{:S(2)}) copy-start(s32[1,12]{1,0:T(1,128)} %param.18) | copy-start | bytes 148
  0.0 37.9 %copy-start.5 = (bf16[48,4,512]{2,1,0:T(4,128)(2,1)S(1)}, bf16[48,4,512]{2,1,0:T(4,128)(2,1)}, u32[]{:S(2)}) copy-start(bf16[48,4,512]{2,1,0:T(4,128)(2,1)} %param.10) | copy-start | bytes 589828
  1.7 10.2 %all-to-all-start = ((s32[8,2,128]{2,1,0:T(2,128)}), s32[8,2,128]{2,1,0:T(2,128)S(1)}, u32[]{:S(2)}, u32[]{:S(2)}) async-start(s32[8,2,128]{2,1,0:T(2,128)} %broadcast_in_dim.26), calls=%async_computation | async-start | bytes 16384 | tf_op jit(solution)/shard_map/all_to_all | solution.py:249
  8.1 18.5 %collective-permute-start.1 = (bf16[4,1,128,128]{3,2,1,0:T(8,128)(2,1)S(1)}, bf16[4,1,128,128]{3,2,1,0:T(8,128)(2,1)S(1)}, u32[]{:S(2)}, u32[]{:S(2)}) collective-permute-start(bf16[4,1,128,128]{3,2,1,0:T(8,128)(2,1)S(1)} %slice.21), channel_id=1, source_target_pairs={{0,16},{2,18},{4,20},{6,22},{8,24},{10,26},{12,28},{14,30},{16,0},... | collective-permute-start | bytes 393224 | tf_op jit(solution)/shard_map/ppermute | solution.py:253
  11.5 35.4 %collective-permute-start.2 = (bf16[4,3,128,128]{3,2,1,0:T(8,128)(2,1)}, bf16[4,3,128,128]{3,2,1,0:T(8,128)(2,1)S(1)}, u32[]{:S(2)}, u32[]{:S(2)}) collective-permute-start(bf16[4,3,128,128]{3,2,1,0:T(8,128)(2,1)} %slice.22), channel_id=1, source_target_pairs={{0,16},{2,18},{4,20},{6,22},{8,24},{10,26},{12,28},{14,30},{16,0},... | collective-permute-start | bytes 1179656 | tf_op jit(solution)/shard_map/ppermute | solution.py:253
  26.6 28.4 %copy-start.3 = (f32[512]{0:T(512)S(1)}, f32[512]{0:T(512)}, u32[]{:S(2)}) copy-start(f32[512]{0:T(512)} %param.11) | copy-start | bytes 6148
  26.6 28.4 %copy-start.4 = (f32[512]{0:T(512)S(1)}, f32[512]{0:T(512)}, u32[]{:S(2)}) copy-start(f32[512]{0:T(512)} %param.14) | copy-start | bytes 6148
  27.9 2.2 %collective-permute-start.3 = (bf16[1,4,128,128]{3,2,1,0:T(8,128)(2,1)S(1)}, bf16[1,4,128,128]{3,2,1,0:T(8,128)(2,1)S(1)}, u32[]{:S(2)}, u32[]{:S(2)}) collective-permute-start(bf16[1,4,128,128]{3,2,1,0:T(8,128)(2,1)S(1)} %get-tuple-element.26), channel_id=1, source_target_pairs={{0,2},{2,0},{4,6},{6,4},{8,10},{10,8},{12,14},{14,12},{16,18},{18,... | collective-permute-start | bytes 393224 | tf_op jit(solution)/shard_map/ppermute | solution.py:274
  27.9 6.4 %collective-permute-start.4 = (bf16[1,4,128,128]{3,2,1,0:T(8,128)(2,1)S(1)}, bf16[1,4,128,128]{3,2,1,0:T(8,128)(2,1)S(1)}, u32[]{:S(2)}, u32[]{:S(2)}) collective-permute-start(bf16[1,4,128,128]{3,2,1,0:T(8,128)(2,1)S(1)} %get-tuple-element.27), channel_id=1, source_target_pairs={{0,4},{2,6},{4,0},{6,2},{8,12},{10,14},{12,8},{14,10},{16,20},{18,... | collective-permute-start | bytes 393224 | tf_op jit(solution)/shard_map/ppermute | solution.py:274
  30.0 6.8 %collective-permute-start.5 = (bf16[1,4,128,128]{3,2,1,0:T(8,128)(2,1)S(1)}, bf16[1,4,128,128]{3,2,1,0:T(8,128)(2,1)S(1)}, u32[]{:S(2)}, u32[]{:S(2)}) collective-permute-start(bf16[1,4,128,128]{3,2,1,0:T(8,128)(2,1)S(1)} %get-tuple-element.28), channel_id=1, source_target_pairs={{0,6},{2,4},{4,2},{6,0},{8,14},{10,12},{12,10},{14,8},{16,22},{18,... | collective-permute-start | bytes 393224 | tf_op jit(solution)/shard_map/ppermute | solution.py:274
  30.1 7.8 %collective-permute-start.6 = (bf16[1,4,128,128]{3,2,1,0:T(8,128)(2,1)S(1)}, bf16[1,4,128,128]{3,2,1,0:T(8,128)(2,1)S(1)}, u32[]{:S(2)}, u32[]{:S(2)}) collective-permute-start(bf16[1,4,128,128]{3,2,1,0:T(8,128)(2,1)S(1)} %get-tuple-element.29), channel_id=1, source_target_pairs={{0,8},{2,10},{4,12},{6,14},{8,0},{10,2},{12,4},{14,6},{16,24},{18,... | collective-permute-start | bytes 393224 | tf_op jit(solution)/shard_map/ppermute | solution.py:274
  30.1 10.0 %collective-permute-start.7 = (bf16[1,4,128,128]{3,2,1,0:T(8,128)(2,1)}, bf16[1,4,128,128]{3,2,1,0:T(8,128)(2,1)S(1)}, u32[]{:S(2)}, u32[]{:S(2)}) collective-permute-start(bf16[1,4,128,128]{3,2,1,0:T(8,128)(2,1)} %get-tuple-element.30), channel_id=1, source_target_pairs={{0,10},{2,8},{4,14},{6,12},{8,2},{10,0},{12,6},{14,4},{16,26},{18,... | collective-permute-start | bytes 393224 | tf_op jit(solution)/shard_map/ppermute | solution.py:274
  34.3 9.9 %collective-permute-start.8 = (bf16[1,4,128,128]{3,2,1,0:T(8,128)(2,1)}, bf16[1,4,128,128]{3,2,1,0:T(8,128)(2,1)S(1)}, u32[]{:S(2)}, u32[]{:S(2)}) collective-permute-start(bf16[1,4,128,128]{3,2,1,0:T(8,128)(2,1)} %get-tuple-element.31), channel_id=1, source_target_pairs={{0,12},{2,14},{4,8},{6,10},{8,4},{10,6},{12,0},{14,2},{16,28},{18,... | collective-permute-start | bytes 393224 | tf_op jit(solution)/shard_map/ppermute | solution.py:274
  36.8 10.1 %collective-permute-start.9 = (bf16[1,4,128,128]{3,2,1,0:T(8,128)(2,1)S(1)}, bf16[1,4,128,128]{3,2,1,0:T(8,128)(2,1)S(1)}, u32[]{:S(2)}, u32[]{:S(2)}) collective-permute-start(bf16[1,4,128,128]{3,2,1,0:T(8,128)(2,1)S(1)} %get-tuple-element.32), channel_id=1, source_target_pairs={{0,14},{2,12},{4,10},{6,8},{8,6},{10,4},{12,2},{14,0},{16,30},{18,... | collective-permute-start | bytes 393224 | tf_op jit(solution)/shard_map/ppermute | solution.py:274
  38.0 12.3 %collective-permute-start = (bf16[192,512]{1,0:T(8,128)(2,1)S(1)}, bf16[192,512]{1,0:T(8,128)(2,1)S(1)}, u32[]{:S(2)}, u32[]{:S(2)}) collective-permute-start(bf16[192,512]{1,0:T(8,128)(2,1)S(1)} %reshape.179.refs_0_), channel_id=1, source_target_pairs={{0,1},{1,0},{2,3},{3,2},{4,5},{5,4},{6,7},{7,6},{8,9},{9,8},{10,11... | collective-permute-start | bytes 589832 | tf_op jit(solution)/shard_map/ppermute | solution.py:263
  48.3 3.8 %collective-permute-start.10 = (bf16[1,4,128,128]{3,2,1,0:T(8,128)(2,1)S(1)}, bf16[1,4,128,128]{3,2,1,0:T(8,128)(2,1)S(1)}, u32[]{:S(2)}, u32[]{:S(2)}) collective-permute-start(bf16[1,4,128,128]{3,2,1,0:T(8,128)(2,1)S(1)} %get-tuple-element.36), channel_id=1, source_target_pairs={{0,2},{2,0},{4,6},{6,4},{8,10},{10,8},{12,14},{14,12},{16,18},{18,... | collective-permute-start | bytes 393224 | tf_op jit(solution)/shard_map/ppermute | solution.py:274
  48.4 6.3 %collective-permute-start.11 = (bf16[1,4,128,128]{3,2,1,0:T(8,128)(2,1)S(1)}, bf16[1,4,128,128]{3,2,1,0:T(8,128)(2,1)S(1)}, u32[]{:S(2)}, u32[]{:S(2)}) collective-permute-start(bf16[1,4,128,128]{3,2,1,0:T(8,128)(2,1)S(1)} %get-tuple-element.37), channel_id=1, source_target_pairs={{0,4},{2,6},{4,0},{6,2},{8,12},{10,14},{12,8},{14,10},{16,20},{18,... | collective-permute-start | bytes 393224 | tf_op jit(solution)/shard_map/ppermute | solution.py:274
  48.8 10.7 %collective-permute-start.12 = (bf16[1,4,128,128]{3,2,1,0:T(8,128)(2,1)}, bf16[1,4,128,128]{3,2,1,0:T(8,128)(2,1)S(1)}, u32[]{:S(2)}, u32[]{:S(2)}) collective-permute-start(bf16[1,4,128,128]{3,2,1,0:T(8,128)(2,1)} %get-tuple-element.38), channel_id=1, source_target_pairs={{0,6},{2,4},{4,2},{6,0},{8,14},{10,12},{12,10},{14,8},{16,22},{18,... | collective-permute-start | bytes 393224 | tf_op jit(solution)/shard_map/ppermute | solution.py:274
  50.3 9.2 %collective-permute-start.13 = (bf16[1,4,128,128]{3,2,1,0:T(8,128)(2,1)}, bf16[1,4,128,128]{3,2,1,0:T(8,128)(2,1)S(1)}, u32[]{:S(2)}, u32[]{:S(2)}) collective-permute-start(bf16[1,4,128,128]{3,2,1,0:T(8,128)(2,1)} %get-tuple-element.39), channel_id=1, source_target_pairs={{0,8},{2,10},{4,12},{6,14},{8,0},{10,2},{12,4},{14,6},{16,24},{18,... | collective-permute-start | bytes 393224 | tf_op jit(solution)/shard_map/ppermute | solution.py:274
  50.3 9.2 %collective-permute-start.14 = (bf16[1,4,128,128]{3,2,1,0:T(8,128)(2,1)}, bf16[1,4,128,128]{3,2,1,0:T(8,128)(2,1)}, u32[]{:S(2)}, u32[]{:S(2)}) collective-permute-start(bf16[1,4,128,128]{3,2,1,0:T(8,128)(2,1)} %get-tuple-element.40), channel_id=1, source_target_pairs={{0,10},{2,8},{4,14},{6,12},{8,2},{10,0},{12,6},{14,4},{16,26},{18,... | collective-permute-start | bytes 393224 | tf_op jit(solution)/shard_map/ppermute | solution.py:274
  52.1 10.3 %collective-permute-start.15 = (bf16[1,4,128,128]{3,2,1,0:T(8,128)(2,1)}, bf16[1,4,128,128]{3,2,1,0:T(8,128)(2,1)}, u32[]{:S(2)}, u32[]{:S(2)}) collective-permute-start(bf16[1,4,128,128]{3,2,1,0:T(8,128)(2,1)} %get-tuple-element.41), channel_id=1, source_target_pairs={{0,12},{2,14},{4,8},{6,10},{8,4},{10,6},{12,0},{14,2},{16,28},{18,... | collective-permute-start | bytes 393224 | tf_op jit(solution)/shard_map/ppermute | solution.py:274
  54.8 9.3 %collective-permute-start.16 = (bf16[1,4,128,128]{3,2,1,0:T(8,128)(2,1)}, bf16[1,4,128,128]{3,2,1,0:T(8,128)(2,1)}, u32[]{:S(2)}, u32[]{:S(2)}) collective-permute-start(bf16[1,4,128,128]{3,2,1,0:T(8,128)(2,1)} %get-tuple-element.42), channel_id=1, source_target_pairs={{0,14},{2,12},{4,10},{6,8},{8,6},{10,4},{12,2},{14,0},{16,30},{18,... | collective-permute-start | bytes 393224 | tf_op jit(solution)/shard_map/ppermute | solution.py:274
  69.9 5.2 %collective-permute-start.17 = (bf16[192,256]{1,0:T(8,128)(2,1)S(1)}, bf16[192,256]{1,0:T(8,128)(2,1)S(1)}, u32[]{:S(2)}, u32[]{:S(2)}) collective-permute-start(bf16[192,256]{1,0:T(8,128)(2,1)S(1)} %get-tuple-element.44), channel_id=1, source_target_pairs={{0,1},{1,0},{2,3},{3,2},{4,5},{5,4},{6,7},{7,6},{8,9},{9,8},{10,11... | collective-permute-start | bytes 294920 | tf_op jit(solution)/shard_map/ppermute | solution.py:290
  (4 other events, 74.9 us)

commit v8 on v7

--- a/solution.py
+++ b/solution.py
@@ -35,54 +35,41 @@
     return lax.broadcasted_iota(jnp.int32, shape, dim)
 
 
-def pick_kernel(parts, wanted_ref, *refs):
-    tile_refs, out_ref = refs[:parts], refs[-1]
+def pick_kernel(wanted_ref, tiles_ref, *refs):
+    out_ref = refs[-1]
     for peer in range(out_ref.shape[0]):
-        low = 0
-        for tiles_ref in tile_refs:
-            high = low + tiles_ref.shape[1]
-            out_ref[peer, low:high] = tiles_ref[wanted_ref[peer]]
-            low = high
+        out_ref[peer] = tiles_ref[wanted_ref[peer]]
 
 
 def pick(tiles, wanted, after):
-    count = wanted.shape[0]
-    heads = sum(part.shape[1] for part in tiles)
-    return pl.pallas_call(
-        functools.partial(pick_kernel, len(tiles)),
-        out_shape=jax.ShapeDtypeStruct((count, heads) + tiles[0].shape[2:], tiles[0].dtype),
-        in_specs=[pl.BlockSpec(memory_space=pltpu.SMEM)] + [VMEM] * len(tiles) + [ANY] * len(after),
+    return pl.pallas_call(
+        pick_kernel,
+        out_shape=jax.ShapeDtypeStruct(wanted.shape + tiles.shape[1:], tiles.dtype),
+        in_specs=[pl.BlockSpec(memory_space=pltpu.SMEM), VMEM] + [ANY] * len(after),
         out_specs=VMEM,
         compiler_params=params(0),
         cost_estimate=pl.CostEstimate(flops=0, bytes_accessed=2 * MIB, transcendentals=0),
         name="pick",
-    )(wanted, *tiles, *after)
-
-
-def pick_each_kernel(parts, wanted_ref, me_ref, *refs):
-    tile_refs, out_refs = refs[:parts], refs[-wanted_ref.shape[0]:]
-    for step, out_ref in enumerate(out_refs):
-        tile = wanted_ref[me_ref[0] ^ step]
-        low = 0
-        for tiles_ref in tile_refs:
-            high = low + tiles_ref.shape[1]
-            out_ref[0, low:high] = tiles_ref[tile]
-            low = high
+    )(wanted, tiles, *after)
+
+
+def pick_each_kernel(wanted_ref, me_ref, tiles_ref, *refs):
+    for step, out_ref in enumerate(refs[-wanted_ref.shape[0]:]):
+        out_ref[0] = tiles_ref[wanted_ref[me_ref[0] ^ step]]
 
 
 def pick_each(tiles, wanted, me, after):
     count = wanted.shape[0]
-    heads = sum(part.shape[1] for part in tiles)
     smem = pl.BlockSpec(memory_space=pltpu.SMEM)
     return pl.pallas_call(
-        functools.partial(pick_each_kernel, len(tiles)),
-        out_shape=(jax.ShapeDtypeStruct((1, heads) + tiles[0].shape[2:], tiles[0].dtype),) * count,
-        in_specs=[smem, smem] + [VMEM] * len(tiles) + [ANY] * len(after),
+        pick_each_kernel,
+        out_shape=(jax.ShapeDtypeStruct((1,) + tiles.shape[1:], tiles.dtype),) * count,
+        in_specs=[smem, smem, VMEM] + [ANY] * len(after),
         out_specs=(VMEM,) * count,
         compiler_params=params(0),
         cost_estimate=pl.CostEstimate(flops=0, bytes_accessed=2 * MIB, transcendentals=0),
         name="pick_each",
-    )(wanted, me, *tiles, *after)
+    )(wanted, me, tiles, *after)
 
 
 def front_kernel(groups, heads, head_size, chunk, cols, row_size, *refs):
@@ -170,20 +157,53 @@
     )(*cells, holder, key_mask, gain_col.reshape(1, width), w_qkv, w_out, gain_tile.reshape(1, width), w_query, after)
 
 
-def weigh(query, tiles):
+def weigh(query, tile_refs, head, first_slot):
+    tiles = jnp.concatenate([ref[:, head] for ref in tile_refs], axis=0)
     slots, keys, lanes = tiles.shape
     half = lanes // 2
     lane = iota(tiles.shape, 2)
-    marks = (lane == iota(tiles.shape, 0) + half).astype(tiles.dtype)
+    marks = (lane == iota(tiles.shape, 0) + (half + first_slot)).astype(tiles.dtype)
     key_part = jnp.where(lane < half, tiles, marks).reshape(slots * keys, lanes)
     val_part = jnp.where(lane < half, jnp.ones_like(tiles), tiles).reshape(slots * keys, lanes)
     scores = dot_lanes(query, key_part)
     top = jnp.max(scores, axis=1, keepdims=True)
-    return dot_rows(jnp.exp(scores - top).astype(jnp.bfloat16), val_part)
-
-
-def attend_kernel(groups, tile_count, chunk, asked_ref, *refs):
-    tile_refs, out_refs = refs[:tile_count], refs[tile_count:]
+    return top, dot_rows(jnp.exp(scores - top).astype(jnp.bfloat16), val_part)
+
+
+def attention_cost(asked, tiles):
+    heads, rows, lanes = asked.shape
+    keys = sum(part.shape[0] * part.shape[2] for part in tiles)
+    return pl.CostEstimate(flops=4 * rows * heads * keys * lanes, bytes_accessed=4 * MIB, transcendentals=rows * heads * keys)
+
+
+def first_kernel(count, block, asked_ref, *refs):
+    tile_refs, (sums_ref, tops_ref) = refs[:count], refs[count:]
+    heads, rows_all, lanes = asked_ref.shape
+    lane = iota((block, lanes), 1)
+    for step in range(rows_all // block):
+        rows = pl.ds(step * block, block)
+        tops = jnp.zeros((block, lanes), jnp.float32)
+        for head in range(heads):
+            top, sums_ref[head, rows, :] = weigh(asked_ref[head, rows, :], tile_refs, head, 0)
+            tops = jnp.where(lane == head, top, tops)
+        tops_ref[rows, :] = tops
+
+
+def first_tiles(asked, tiles):
+    heads, rows, lanes = asked.shape
+    return pl.pallas_call(
+        functools.partial(first_kernel, len(tiles), rows if rows <= 512 else 128),
+        out_shape=(jax.ShapeDtypeStruct((heads, rows, lanes), jnp.float32), jax.ShapeDtypeStruct((rows, lanes), jnp.float32)),
+        in_specs=[VMEM] * (1 + len(tiles)),
+        out_specs=(VMEM, VMEM),
+        compiler_params=params(rows),
+        cost_estimate=attention_cost(asked, tiles),
+        name="first_tiles",
+    )(asked, *tiles)
+
+
+def last_kernel(groups, count, first_slot, chunk, asked_ref, sums_ref, tops_ref, *refs):
+    tile_refs, out_refs = refs[:count], refs[count:]
     heads, rows_all, lanes = asked_ref.shape
     half = lanes // 2
     span = groups * chunk
@@ -198,10 +218,13 @@
                 out_refs[group][place, pl.ds(lane, lane_count)] = values[start:start + chunk]
 
     for step in range(rows_all // block):
+        rows = pl.ds(step * block, block)
         low = None
         for head in range(heads):
-            tiles = jnp.concatenate([ref[:, head] for ref in tile_refs], axis=0)
-            sums = weigh(asked_ref[head, pl.ds(step * block, block), :], tiles)
+            top, sums = weigh(asked_ref[head, rows, :], tile_refs, head, first_slot)
+            old_top = tops_ref[rows, head:head + 1]
+            new_top = jnp.maximum(top, old_top)
+            sums = sums_ref[head, rows, :] * jnp.exp(old_top - new_top) + sums * jnp.exp(top - new_top)
             turned = pltpu.roll(sums, half, 1)
             if head % 2:
                 put(step, jnp.where(lane_low, low, sums / turned).astype(jnp.bfloat16), head // 2 * lanes, lanes)
@@ -211,20 +234,18 @@
                 put(step, (turned / sums)[:, :half].astype(jnp.bfloat16), head * half, half)
 
 
-def attend(asked, tiles, groups, cols):
+def last_tiles(asked, sums, tops, tiles, first_slot, groups, cols):
     heads, rows, lanes = asked.shape
-    keys = sum(part.shape[0] * part.shape[2] for part in tiles)
     out = jax.ShapeDtypeStruct((rows // groups, heads * lanes // 2), jnp.bfloat16)
     return pl.pallas_call(
-        functools.partial(attend_kernel, groups, len(tiles), ROW_GROUP * cols),
+        functools.partial(last_kernel, groups, len(tiles), first_slot, ROW_GROUP * cols),
         out_shape=(out,) * groups,
-        in_specs=[VMEM] * (1 + len(tiles)),
+        in_specs=[VMEM] * (3 + len(tiles)),
         out_specs=(VMEM,) * groups,
         compiler_params=params(rows),
-        cost_estimate=pl.CostEstimate(flops=4 * rows * heads * keys * lanes, bytes_accessed=4 * MIB,
-                                      transcendentals=rows * heads * keys),
-        name="attend",
-    )(asked, *tiles)
+        cost_estimate=attention_cost(asked, tiles),
+        name="last_tiles",
+    )(asked, sums, tops, *tiles)
 
 
 def turn(size, step):
@@ -249,8 +270,7 @@
         return lax.all_to_all(value, "rows", split_axis=0, concat_axis=0, tiled=True, axis_index_groups=halves)
 
     heads_first = jnp.transpose(tile_kv, (0, 2, 1, 3))
-    parts = [(0, 1), (1, heads_here)] if heads_here > 1 else [(0, 1)]
-    mirrored = [lax.ppermute(heads_first[:, low:high], "rows", turn(row_size, half)) for low, high in parts]
+    mirrored = lax.ppermute(heads_first, "rows", turn(row_size, half))
 
     listed = tile_ids[0] >= 0
     holder = jnp.where(listed, (tile_ids[0] // tiles_here + my_half * half) % row_size, -1)
@@ -278,12 +298,13 @@
             picked = pick(tiles, wanted, after)
             return picked, [swap(picked)]
 
-    picked, near = spread([heads_first], near_by, mirrored[:1])
+    picked, near = spread(heads_first, near_by, [])
     picked, far = spread(mirrored, far_by, near)
     query_here = lax.dynamic_slice_in_dim(w_query, col_me * group_width, group_width, 1)
     residual, asked = front(cells, holder[:, None], key_mask, gain_col, w_qkv, w_col_out, gain_tile, query_here,
                             heads_all, head_size, cols, row_size, picked)
-    answers = attend(asked, near + far, col_size, cols)
+    sums, tops = first_tiles(asked, near)
+    answers = last_tiles(asked, sums, tops, far, half, col_size, cols)
 
     final = residual
     for step in range(col_size):

time: 76.3 us -> 71.2 us (0.933)
  waiting for transfers between devices: 36.3 us -> 21 us
  starting transfers between devices: 21.3 us -> 27.4 us
  local copies, waits for them, and re-layouts: 5.29 us -> 10.3 us
  Pallas kernels: 11.7 us -> 10.8 us
    ppermute x2 -> x1, waiting for transfers between devices: 14.6 us -> 0.01 us  [shards(): mirrored = lax.ppermute(heads_first, 'rows', turn(row_size, half))]
    ppermute x14, starting transfers between devices: 9.9 us -> 16.4 us  [spread(): arrived.append(lax.ppermute(picked[step], 'rows', pairs))]
    ppermute x14, waiting for transfers between devices: 18.3 us -> 11.9 us  [spread(): arrived.append(lax.ppermute(picked[step], 'rows', pairs))]
    all_to_all x1, waiting for transfers between devices: 0.01 us -> 5.94 us  [swap(): lax.all_to_all(value, 'rows', split_axis=0, concat_axis=0, tiled=True, ax...]
    unnamed x20 -> x24, local copies, waits for them, and re-layouts: 2.66 us -> 6.01 us
    all_to_all x1, starting transfers between devices: 5.25 us -> 3.78 us  [swap(): lax.all_to_all(value, 'rows', split_axis=0, concat_axis=0, tiled=True, ax...]
    ppermute x2 -> x1, starting transfers between devices: 2.99 us -> 4.1 us  [shards(): mirrored = lax.ppermute(heads_first, 'rows', turn(row_size, half))]
    dynamic_slice x1, local copies, waits for them, and re-layouts: 0.02 us -> 0.97 us  [shards(): lax.dynamic_slice_in_dim(w_query, col_me * group_width, group_width, 1)]
  transfers between devices with their start and end apart: 19 -> 18, of which waited for: 10 -> 9; matrix products, arithmetic and copies ran while one was open for 3% -> 8% of each run, Pallas kernels for 8% -> 12%
where the time goes in v8:
time: 71.2 us; the launch traced here: 70.9 us
  starting transfers between devices  27.4 us (38%)
  waiting for transfers between devices  21 us (29%)
  Pallas kernels  10.8 us (15%)
  local copies, waits for them, and re-layouts  10.3 us (14%)
  other arithmetic  0.78 us (1%)
    ppermute x14, starting transfers between devices, spread(): arrived.append(lax.ppermute(picked[step], 'rows', pairs))  16.4 us
    ppermute x14, waiting for transfers between devices, spread(): arrived.append(lax.ppermute(picked[step], 'rows', pairs))  11.9 us
    unnamed x24, local copies, waits for them, and re-layouts  6.01 us
    all_to_all x1, waiting for transfers between devices, swap(): lax.all_to_all(value, 'rows', split_axis=0, concat_axis=0, tiled=True, ax...  5.94 us
    ppermute x1, starting transfers between devices, shards(): mirrored = lax.ppermute(heads_first, 'rows', turn(row_size, half))  4.1 us
    all_to_all x1, starting transfers between devices, swap(): lax.all_to_all(value, 'rows', split_axis=0, concat_axis=0, tiled=True, ax...  3.78 us
    ppermute x1, waiting for transfers between devices, shards(): lax.ppermute(answers[step], 'cols', turn(col_size, step))  3.2 us
    pallas_call x1, Pallas kernels, front(): pl.pallas_call(functools.partial(front_kernel, groups, heads, head_size,...  3.11 us
  transfers between devices with their start and end apart: 18, of which 9 were waited for; matrix products, arithmetic and copies ran while one was open for 8% of the time, Pallas kernels for 12%

profile of v8, /device:TPU:0, one launch (start us, length us, event | category | flops | bytes accessed | tf_op | source)
XLA Modules:
  0.0 70.9 jit_solution(17935678534966201775)
XLA Ops:
  0.0 1.2 %copy.37 = bf16[4,128,4,128]{3,1,2,0:T(8,128)(2,1)S(1)} copy(bf16[4,128,4,128]{3,2,1,0:T(4,128)(2,1)} %param.17) | data formatting | bytes 1048576 | tf_op args[7]
  1.2 4.1 %collective-permute-start.1 = (bf16[4,4,128,128]{3,2,1,0:T(8,128)(2,1)S(1)}, bf16[4,4,128,128]{3,2,1,0:T(8,128)(2,1)S(1)}, u32[]{:S(2)}, u32[]{:S(2)}) collective-permute-start(bf16[4,4,128,128]{3,2,1,0:T(8,128)(2,1)S(1)} %bitcast.34), channel_id=1, source_target_pairs={{0,16},{2,18},{4,20},{6,22},{8,24},{10,26},{12,28},{14,30},{16,0},... | collective-permute-start | bytes 1572872 | tf_op jit(solution)/shard_map/ppermute | solution.py:273
  6.9 3.8 %all-to-all-start = ((s32[8,2,128]{2,1,0:T(2,128)}), s32[8,2,128]{2,1,0:T(2,128)S(1)}, u32[]{:S(2)}, u32[]{:S(2)}) async-start(s32[8,2,128]{2,1,0:T(2,128)} %broadcast_in_dim.26), calls=%async_computation | async-start | bytes 16384 | tf_op jit(solution)/shard_map/all_to_all | solution.py:270
  10.7 5.9 %all-to-all-done = s32[8,2,128]{2,1,0:T(2,128)S(1)} async-done(((s32[8,2,128]{2,1,0:T(2,128)}), s32[8,2,128]{2,1,0:T(2,128)S(1)}, u32[]{:S(2)}, u32[]{:S(2)}) %all-to-all-start) | async-done | bytes 8224 | tf_op jit(solution)/shard_map/all_to_all | solution.py:270
  16.8 1.3 %pick_each.2 = (bf16[1,4,128,128]{3,2,1,0:T(8,128)(2,1)S(1)}, bf16[1,4,128,128]{3,2,1,0:T(8,128)(2,1)S(1)}, bf16[1,4,128,128]{3,2,1,0:T(8,128)(2,1)S(1)}, bf16[1...) custom-call(s32[8]{0:T(128)S(1)} %get-tuple-element.49.wanted_ref, ...), custom_call_target="tpu_custom_call" | custom-call | bytes 2097152 | tf_op jit(solution)/shard_map/pick_each/pallas_call | solution.py:64
  18.1 1.5 %collective-permute-start.3 = (bf16[1,4,128,128]{3,2,1,0:T(8,128)(2,1)S(1)}, bf16[1,4,128,128]{3,2,1,0:T(8,128)(2,1)S(1)}, u32[]{:S(2)}, u32[]{:S(2)}) collective-permute-start(bf16[1,4,128,128]{3,2,1,0:T(8,128)(2,1)S(1)} %get-tuple-element.29), channel_id=1, source_target_pairs={{0,4},{2,6},{4,0},{6,2},{8,12},{10,14},{12,8},{14,10},{16,20},{18,... | collective-permute-start | bytes 393224 | tf_op jit(solution)/shard_map/ppermute | solution.py:294
  19.9 3.4 %collective-permute-start.5 = (bf16[1,4,128,128]{3,2,1,0:T(8,128)(2,1)S(1)}, bf16[1,4,128,128]{3,2,1,0:T(8,128)(2,1)S(1)}, u32[]{:S(2)}, u32[]{:S(2)}) collective-permute-start(bf16[1,4,128,128]{3,2,1,0:T(8,128)(2,1)S(1)} %get-tuple-element.31), channel_id=1, source_target_pairs={{0,8},{2,10},{4,12},{6,14},{8,0},{10,2},{12,4},{14,6},{16,24},{18,... | collective-permute-start | bytes 393224 | tf_op jit(solution)/shard_map/ppermute | solution.py:294
  23.3 1.1 %collective-permute-done.3.refs_2_ = bf16[1,4,128,128]{3,2,1,0:T(8,128)(2,1)S(1)} collective-permute-done((bf16[1,4,128,128]{3,2,1,0:T(8,128)(2,1)S(1)}, bf16[1,4,128,128]{3,2,1,0:T(8,128)(2,1)S(1)}, u32[]{:S(2)}, u32[]{:S(2)}) %collective-permute-start.3) | collective-permute-done | bytes 131104 | tf_op jit(solution)/shard_map/ppermute | solution.py:294
  24.4 3.5 %collective-permute-start.7 = (bf16[1,4,128,128]{3,2,1,0:T(8,128)(2,1)}, bf16[1,4,128,128]{3,2,1,0:T(8,128)(2,1)S(1)}, u32[]{:S(2)}, u32[]{:S(2)}) collective-permute-start(bf16[1,4,128,128]{3,2,1,0:T(8,128)(2,1)} %get-tuple-element.33), channel_id=1, source_target_pairs={{0,12},{2,14},{4,8},{6,10},{8,4},{10,6},{12,0},{14,2},{16,28},{18,... | collective-permute-start | bytes 393224 | tf_op jit(solution)/shard_map/ppermute | solution.py:294
  27.8 2.1 %collective-permute-start.8 = (bf16[1,4,128,128]{3,2,1,0:T(8,128)(2,1)}, bf16[1,4,128,128]{3,2,1,0:T(8,128)(2,1)S(1)}, u32[]{:S(2)}, u32[]{:S(2)}) collective-permute-start(bf16[1,4,128,128]{3,2,1,0:T(8,128)(2,1)} %get-tuple-element.34), channel_id=1, source_target_pairs={{0,14},{2,12},{4,10},{6,8},{8,6},{10,4},{12,2},{14,0},{16,30},{18,... | collective-permute-start | bytes 393224 | tf_op jit(solution)/shard_map/ppermute | solution.py:294
  31.6 1.5 %collective-permute-start = (bf16[192,512]{1,0:T(8,128)(2,1)S(1)}, bf16[192,512]{1,0:T(8,128)(2,1)S(1)}, u32[]{:S(2)}, u32[]{:S(2)}) collective-permute-start(bf16[192,512]{1,0:T(8,128)(2,1)S(1)} %reshape.179.refs_0_), channel_id=1, source_target_pairs={{0,1},{1,0},{2,3},{3,2},{4,5},{5,4},{6,7},{7,6},{8,9},{9,8},{10,11... | collective-permute-start | bytes 589832 | tf_op jit(solution)/shard_map/ppermute | solution.py:283
  34.1 3.9 %collective-permute-done.7.refs_6_ = bf16[1,4,128,128]{3,2,1,0:T(8,128)(2,1)S(1)} collective-permute-done((bf16[1,4,128,128]{3,2,1,0:T(8,128)(2,1)}, bf16[1,4,128,128]{3,2,1,0:T(8,128)(2,1)S(1)}, u32[]{:S(2)}, u32[]{:S(2)}) %collective-permute-start.7) | collective-permute-done | bytes 131104 | tf_op jit(solution)/shard_map/ppermute | solution.py:294
  37.9 2.7 %collective-permute-done.8.refs_7_ = bf16[1,4,128,128]{3,2,1,0:T(8,128)(2,1)S(1)} collective-permute-done((bf16[1,4,128,128]{3,2,1,0:T(8,128)(2,1)}, bf16[1,4,128,128]{3,2,1,0:T(8,128)(2,1)S(1)}, u32[]{:S(2)}, u32[]{:S(2)}) %collective-permute-start.8) | collective-permute-done | bytes 131104 | tf_op jit(solution)/shard_map/ppermute | solution.py:294
  40.7 1.3 %pick_each.3 = (bf16[1,4,128,128]{3,2,1,0:T(8,128)(2,1)S(1)}, bf16[1,4,128,128]{3,2,1,0:T(8,128)(2,1)}, bf16[1,4,128,128]{3,2,1,0:T(8,128)(2,1)}, bf16[1,4,128,1...) custom-call(s32[8]{0:T(128)S(1)} %get-tuple-element.50.wanted_ref, ...), custom_call_target="tpu_custom_call" | custom-call | bytes 2097152 | tf_op jit(solution)/shard_map/pick_each/pallas_call | solution.py:64
  47.0 1.3 %collective-permute-start.11 = (bf16[1,4,128,128]{3,2,1,0:T(8,128)(2,1)}, bf16[1,4,128,128]{3,2,1,0:T(8,128)(2,1)S(1)}, u32[]{:S(2)}, u32[]{:S(2)}) collective-permute-start(bf16[1,4,128,128]{3,2,1,0:T(8,128)(2,1)} %copy-done.6), channel_id=1, source_target_pairs={{0,6},{2,4},{4,2},{6,0},{8,14},{10,12},{12,10},{14,8},{16,22},{18,... | collective-permute-start | bytes 393224 | tf_op jit(solution)/shard_map/ppermute | solution.py:294
  48.3 1.8 %collective-permute-start.13 = (bf16[1,4,128,128]{3,2,1,0:T(8,128)(2,1)}, bf16[1,4,128,128]{3,2,1,0:T(8,128)(2,1)S(1)}, u32[]{:S(2)}, u32[]{:S(2)}) collective-permute-start(bf16[1,4,128,128]{3,2,1,0:T(8,128)(2,1)} %copy-done.4), channel_id=1, source_target_pairs={{0,10},{2,8},{4,14},{6,12},{8,2},{10,0},{12,6},{14,4},{16,26},{18,... | collective-permute-start | bytes 393224 | tf_op jit(solution)/shard_map/ppermute | solution.py:294
  51.0 1.7 %collective-permute-start.15 = (bf16[1,4,128,128]{3,2,1,0:T(8,128)(2,1)S(1)}, bf16[1,4,128,128]{3,2,1,0:T(8,128)(2,1)S(1)}, u32[]{:S(2)}, u32[]{:S(2)}) collective-permute-start(bf16[1,4,128,128]{3,2,1,0:T(8,128)(2,1)S(1)} %get-tuple-element.46), channel_id=1, source_target_pairs={{0,14},{2,12},{4,10},{6,8},{8,6},{10,4},{12,2},{14,0},{16,30},{18,... | collective-permute-start | bytes 393224 | tf_op jit(solution)/shard_map/ppermute | solution.py:294
  52.7 1.4 %copy-done.1 = bf16[512,1536]{1,0:T(8,128)(2,1)S(1)} copy-done((bf16[512,1536]{1,0:T(8,128)(2,1)S(1)}, bf16[512,1536]{1,0:T(8,128)(2,1)}, u32[]{:S(2)}) %copy-start.1) | copy-done | bytes 1572888
  54.1 3.1 %front.1 = (f32[192,512]{1,0:T(8,128)S(1)}, bf16[4,384,128]{2,1,0:T(8,128)(2,1)S(1)}) custom-call(bf16[192,512]{1,0:T(8,128)(2,1)S(1)} %reshape.179.refs_0_, bf16[192,512]{1,0:T(8,128)(2,1)S(1)} %collective-permute-done.refs_1_, s32[12,1]{1,0:T(8,128)S(1)} %compare_select_fusion.refs_2_, s32[48,12]{1,0:T(8,128)S(1)} %copy.35.refs_3_, f32[1,512]{1,0:T(1,128)S(1)} %bitcast.36, ...), custom_call_target="tpu_custom_call" | custom-call | flops 1006632960 | bytes 4194304 | tf_op jit(solution)/shard_map/front/pallas_call | solution.py:146
  57.3 2.5 %first_tiles.1 = (f32[4,384,128]{2,1,0:T(8,128)S(1)}, f32[384,128]{1,0:T(8,128)S(1)}) custom-call(bf16[4,384,128]{2,1,0:T(8,128)(2,1)S(1)} %get-tuple-element.37.asked_ref, bf16[1,4,128,128]{3,2,1,0:T(8,128)(2,1)S(1)} %get-tuple-element.27.refs_0_, bf16[1,4,128,128]{3,2,1,0:T(8,128)(2,1)S(1)} %collective-permute-done.2.refs_1_, ...), custom_call_target="tpu_custom_call" | custom-call | flops 805306368 | bytes 4194304 | tf_op jit(solution)/shard_map/first_tiles/pallas_call | solution.py:194
  60.4 1.9 %collective-permute-done.15.refs_7_ = bf16[1,4,128,128]{3,2,1,0:T(8,128)(2,1)S(1)} collective-permute-done((bf16[1,4,128,128]{3,2,1,0:T(8,128)(2,1)S(1)}, bf16[1,4,128,128]{3,2,1,0:T(8,128)(2,1)S(1)}, u32[]{:S(2)}, u32[]{:S(2)}) %collective-permute-start.15) | collective-permute-done | bytes 131104 | tf_op jit(solution)/shard_map/ppermute | solution.py:294
  62.3 2.7 %last_tiles.1 = (bf16[192,256]{1,0:T(8,128)(2,1)S(1)}, bf16[192,256]{1,0:T(8,128)(2,1)S(1)}) custom-call(bf16[4,384,128]{2,1,0:T(8,128)(2,1)S(1)} %get-tuple-element.37.asked_ref, f32[4,384,128]{2,1,0:T(8,128)S(1)} %get-tuple-element.38.sums_ref, f32[384,128]{1,0:T(8,128)S(1)} %get-tuple-element.39.tops_ref, ...), custom_call_target="tpu_custom_call" | custom-call | flops 805306368 | bytes 4194304 | tf_op jit(solution)/shard_map/last_tiles/pallas_call | solution.py:240
  64.9 1.6 %collective-permute-start.16 = (bf16[192,256]{1,0:T(8,128)(2,1)S(1)}, bf16[192,256]{1,0:T(8,128)(2,1)S(1)}, u32[]{:S(2)}, u32[]{:S(2)}) collective-permute-start(bf16[192,256]{1,0:T(8,128)(2,1)S(1)} %get-tuple-element.48), channel_id=1, source_target_pairs={{0,1},{1,0},{2,3},{3,2},{4,5},{5,4},{6,7},{7,6},{8,9},{9,8},{10,11... | collective-permute-start | bytes 294920 | tf_op jit(solution)/shard_map/ppermute | solution.py:311
  66.8 3.2 %collective-permute-done.16 = bf16[192,256]{1,0:T(8,128)(2,1)S(1)} collective-permute-done((bf16[192,256]{1,0:T(8,128)(2,1)S(1)}, bf16[192,256]{1,0:T(8,128)(2,1)S(1)}, u32[]{:S(2)}, u32[]{:S(2)}) %collective-permute-start.16) | collective-permute-done | bytes 98336 | tf_op jit(solution)/shard_map/ppermute | solution.py:311
  (55 shorter events, 12.4 us)
Async XLA Ops:
  0.0 66.6 %copy-start = (bf16[512,512]{1,0:T(8,128)(2,1)S(1)}, bf16[512,512]{1,0:T(8,128)(2,1)}, u32[]{:S(2)}) copy-start(bf16[512,512]{1,0:T(8,128)(2,1)} %param.16) | copy-start | bytes 1572868
  0.0 30.9 %copy-start.10 = (s32[1,12]{1,0:T(1,128)S(1)}, s32[1,12]{1,0:T(1,128)}, u32[]{:S(2)}) copy-start(s32[1,12]{1,0:T(1,128)} %param.18) | copy-start | bytes 148
  1.2 39.4 %collective-permute-start.1 = (bf16[4,4,128,128]{3,2,1,0:T(8,128)(2,1)S(1)}, bf16[4,4,128,128]{3,2,1,0:T(8,128)(2,1)S(1)}, u32[]{:S(2)}, u32[]{:S(2)}) collective-permute-start(bf16[4,4,128,128]{3,2,1,0:T(8,128)(2,1)S(1)} %bitcast.34), channel_id=1, source_target_pairs={{0,16},{2,18},{4,20},{6,22},{8,24},{10,26},{12,28},{14,30},{16,0},... | collective-permute-start | bytes 1572872 | tf_op jit(solution)/shard_map/ppermute | solution.py:273
  6.9 9.7 %all-to-all-start = ((s32[8,2,128]{2,1,0:T(2,128)}), s32[8,2,128]{2,1,0:T(2,128)S(1)}, u32[]{:S(2)}, u32[]{:S(2)}) async-start(s32[8,2,128]{2,1,0:T(2,128)} %broadcast_in_dim.26), calls=%async_computation | async-start | bytes 16384 | tf_op jit(solution)/shard_map/all_to_all | solution.py:270
  16.8 36.0 %copy-start.2 = (bf16[512,512]{1,0:T(8,128)(2,1)S(1)}, bf16[512,512]{1,0:T(8,128)(2,1)}, u32[]{:S(2)}) copy-start(bf16[512,512]{1,0:T(8,128)(2,1)} %refs_6_.1) | copy-start | bytes 1572868
  16.8 36.0 %copy-start.7 = (f32[512]{0:T(512)S(1)}, f32[512]{0:T(512)}, u32[]{:S(2)}) copy-start(f32[512]{0:T(512)} %param.11) | copy-start | bytes 6148
  16.8 36.0 %copy-start.8 = (f32[512]{0:T(512)S(1)}, f32[512]{0:T(512)}, u32[]{:S(2)}) copy-start(f32[512]{0:T(512)} %param.14) | copy-start | bytes 6148
  18.1 5.2 %collective-permute-start.2 = (bf16[1,4,128,128]{3,2,1,0:T(8,128)(2,1)S(1)}, bf16[1,4,128,128]{3,2,1,0:T(8,128)(2,1)S(1)}, u32[]{:S(2)}, u32[]{:S(2)}) collective-permute-start(bf16[1,4,128,128]{3,2,1,0:T(8,128)(2,1)S(1)} %get-tuple-element.28), channel_id=1, source_target_pairs={{0,2},{2,0},{4,6},{6,4},{8,10},{10,8},{12,14},{14,12},{16,18},{18,... | collective-permute-start | bytes 393224 | tf_op jit(solution)/shard_map/ppermute | solution.py:294
  18.1 6.3 %collective-permute-start.3 = (bf16[1,4,128,128]{3,2,1,0:T(8,128)(2,1)S(1)}, bf16[1,4,128,128]{3,2,1,0:T(8,128)(2,1)S(1)}, u32[]{:S(2)}, u32[]{:S(2)}) collective-permute-start(bf16[1,4,128,128]{3,2,1,0:T(8,128)(2,1)S(1)} %get-tuple-element.29), channel_id=1, source_target_pairs={{0,4},{2,6},{4,0},{6,2},{8,12},{10,14},{12,8},{14,10},{16,20},{18,... | collective-permute-start | bytes 393224 | tf_op jit(solution)/shard_map/ppermute | solution.py:294
  19.6 8.3 %collective-permute-start.4 = (bf16[1,4,128,128]{3,2,1,0:T(8,128)(2,1)S(1)}, bf16[1,4,128,128]{3,2,1,0:T(8,128)(2,1)S(1)}, u32[]{:S(2)}, u32[]{:S(2)}) collective-permute-start(bf16[1,4,128,128]{3,2,1,0:T(8,128)(2,1)S(1)} %get-tuple-element.30), channel_id=1, source_target_pairs={{0,6},{2,4},{4,2},{6,0},{8,14},{10,12},{12,10},{14,8},{16,22},{18,... | collective-permute-start | bytes 393224 | tf_op jit(solution)/shard_map/ppermute | solution.py:294
  19.9 11.6 %collective-permute-start.5 = (bf16[1,4,128,128]{3,2,1,0:T(8,128)(2,1)S(1)}, bf16[1,4,128,128]{3,2,1,0:T(8,128)(2,1)S(1)}, u32[]{:S(2)}, u32[]{:S(2)}) collective-permute-start(bf16[1,4,128,128]{3,2,1,0:T(8,128)(2,1)S(1)} %get-tuple-element.31), channel_id=1, source_target_pairs={{0,8},{2,10},{4,12},{6,14},{8,0},{10,2},{12,4},{14,6},{16,24},{18,... | collective-permute-start | bytes 393224 | tf_op jit(solution)/shard_map/ppermute | solution.py:294
  23.3 10.8 %collective-permute-start.6 = (bf16[1,4,128,128]{3,2,1,0:T(8,128)(2,1)}, bf16[1,4,128,128]{3,2,1,0:T(8,128)(2,1)S(1)}, u32[]{:S(2)}, u32[]{:S(2)}) collective-permute-start(bf16[1,4,128,128]{3,2,1,0:T(8,128)(2,1)} %get-tuple-element.32), channel_id=1, source_target_pairs={{0,10},{2,8},{4,14},{6,12},{8,2},{10,0},{12,6},{14,4},{16,26},{18,... | collective-permute-start | bytes 393224 | tf_op jit(solution)/shard_map/ppermute | solution.py:294
  24.4 13.5 %collective-permute-start.7 = (bf16[1,4,128,128]{3,2,1,0:T(8,128)(2,1)}, bf16[1,4,128,128]{3,2,1,0:T(8,128)(2,1)S(1)}, u32[]{:S(2)}, u32[]{:S(2)}) collective-permute-start(bf16[1,4,128,128]{3,2,1,0:T(8,128)(2,1)} %get-tuple-element.33), channel_id=1, source_target_pairs={{0,12},{2,14},{4,8},{6,10},{8,4},{10,6},{12,0},{14,2},{16,28},{18,... | collective-permute-start | bytes 393224 | tf_op jit(solution)/shard_map/ppermute | solution.py:294
  27.8 12.8 %collective-permute-start.8 = (bf16[1,4,128,128]{3,2,1,0:T(8,128)(2,1)}, bf16[1,4,128,128]{3,2,1,0:T(8,128)(2,1)S(1)}, u32[]{:S(2)}, u32[]{:S(2)}) collective-permute-start(bf16[1,4,128,128]{3,2,1,0:T(8,128)(2,1)} %get-tuple-element.34), channel_id=1, source_target_pairs={{0,14},{2,12},{4,10},{6,8},{8,6},{10,4},{12,2},{14,0},{16,30},{18,... | collective-permute-start | bytes 393224 | tf_op jit(solution)/shard_map/ppermute | solution.py:294
  31.6 13.6 %copy-start.9 = (s32[12,1]{1,0:T(8,128)S(1)}, s32[12,1]{1,0:T(8,128)}, u32[]{:S(2)}) copy-start(s32[12,1]{1,0:T(8,128)} %copy.27) | copy-start | bytes 148
  31.6 16.7 %collective-permute-start = (bf16[192,512]{1,0:T(8,128)(2,1)S(1)}, bf16[192,512]{1,0:T(8,128)(2,1)S(1)}, u32[]{:S(2)}, u32[]{:S(2)}) collective-permute-start(bf16[192,512]{1,0:T(8,128)(2,1)S(1)} %reshape.179.refs_0_), channel_id=1, source_target_pairs={{0,1},{1,0},{2,3},{3,2},{4,5},{5,4},{6,7},{7,6},{8,9},{9,8},{10,11... | collective-permute-start | bytes 589832 | tf_op jit(solution)/shard_map/ppermute | solution.py:283
  44.6 5.5 %collective-permute-start.9 = (bf16[1,4,128,128]{3,2,1,0:T(8,128)(2,1)}, bf16[1,4,128,128]{3,2,1,0:T(8,128)(2,1)S(1)}, u32[]{:S(2)}, u32[]{:S(2)}) collective-permute-start(bf16[1,4,128,128]{3,2,1,0:T(8,128)(2,1)} %get-tuple-element.40), channel_id=1, source_target_pairs={{0,2},{2,0},{4,6},{6,4},{8,10},{10,8},{12,14},{14,12},{16,18},{18,... | collective-permute-start | bytes 393224 | tf_op jit(solution)/shard_map/ppermute | solution.py:294
  44.7 6.4 %collective-permute-start.10 = (bf16[1,4,128,128]{3,2,1,0:T(8,128)(2,1)}, bf16[1,4,128,128]{3,2,1,0:T(8,128)(2,1)S(1)}, u32[]{:S(2)}, u32[]{:S(2)}) collective-permute-start(bf16[1,4,128,128]{3,2,1,0:T(8,128)(2,1)} %get-tuple-element.41), channel_id=1, source_target_pairs={{0,4},{2,6},{4,0},{6,2},{8,12},{10,14},{12,8},{14,10},{16,20},{18,... | collective-permute-start | bytes 393224 | tf_op jit(solution)/shard_map/ppermute | solution.py:294
  47.0 12.7 %collective-permute-start.11 = (bf16[1,4,128,128]{3,2,1,0:T(8,128)(2,1)}, bf16[1,4,128,128]{3,2,1,0:T(8,128)(2,1)S(1)}, u32[]{:S(2)}, u32[]{:S(2)}) collective-permute-start(bf16[1,4,128,128]{3,2,1,0:T(8,128)(2,1)} %copy-done.6), channel_id=1, source_target_pairs={{0,6},{2,4},{4,2},{6,0},{8,14},{10,12},{12,10},{14,8},{16,22},{18,... | collective-permute-start | bytes 393224 | tf_op jit(solution)/shard_map/ppermute | solution.py:294
  48.3 11.4 %collective-permute-start.12 = (bf16[1,4,128,128]{3,2,1,0:T(8,128)(2,1)}, bf16[1,4,128,128]{3,2,1,0:T(8,128)(2,1)S(1)}, u32[]{:S(2)}, u32[]{:S(2)}) collective-permute-start(bf16[1,4,128,128]{3,2,1,0:T(8,128)(2,1)} %copy-done.5), channel_id=1, source_target_pairs={{0,8},{2,10},{4,12},{6,14},{8,0},{10,2},{12,4},{14,6},{16,24},{18,... | collective-permute-start | bytes 393224 | tf_op jit(solution)/shard_map/ppermute | solution.py:294
  48.3 11.4 %collective-permute-start.13 = (bf16[1,4,128,128]{3,2,1,0:T(8,128)(2,1)}, bf16[1,4,128,128]{3,2,1,0:T(8,128)(2,1)S(1)}, u32[]{:S(2)}, u32[]{:S(2)}) collective-permute-start(bf16[1,4,128,128]{3,2,1,0:T(8,128)(2,1)} %copy-done.4), channel_id=1, source_target_pairs={{0,10},{2,8},{4,14},{6,12},{8,2},{10,0},{12,6},{14,4},{16,26},{18,... | collective-permute-start | bytes 393224 | tf_op jit(solution)/shard_map/ppermute | solution.py:294
  50.1 10.2 %collective-permute-start.14 = (bf16[1,4,128,128]{3,2,1,0:T(8,128)(2,1)}, bf16[1,4,128,128]{3,2,1,0:T(8,128)(2,1)S(1)}, u32[]{:S(2)}, u32[]{:S(2)}) collective-permute-start(bf16[1,4,128,128]{3,2,1,0:T(8,128)(2,1)} %copy-done.3), channel_id=1, source_target_pairs={{0,12},{2,14},{4,8},{6,10},{8,4},{10,6},{12,0},{14,2},{16,28},{18,... | collective-permute-start | bytes 393224 | tf_op jit(solution)/shard_map/ppermute | solution.py:294
  51.0 11.2 %collective-permute-start.15 = (bf16[1,4,128,128]{3,2,1,0:T(8,128)(2,1)S(1)}, bf16[1,4,128,128]{3,2,1,0:T(8,128)(2,1)S(1)}, u32[]{:S(2)}, u32[]{:S(2)}) collective-permute-start(bf16[1,4,128,128]{3,2,1,0:T(8,128)(2,1)S(1)} %get-tuple-element.46), channel_id=1, source_target_pairs={{0,14},{2,12},{4,10},{6,8},{8,6},{10,4},{12,2},{14,0},{16,30},{18,... | collective-permute-start | bytes 393224 | tf_op jit(solution)/shard_map/ppermute | solution.py:294
  64.9 5.0 %collective-permute-start.16 = (bf16[192,256]{1,0:T(8,128)(2,1)S(1)}, bf16[192,256]{1,0:T(8,128)(2,1)S(1)}, u32[]{:S(2)}, u32[]{:S(2)}) collective-permute-start(bf16[192,256]{1,0:T(8,128)(2,1)S(1)} %get-tuple-element.48), channel_id=1, source_target_pairs={{0,1},{1,0},{2,3},{3,2},{4,5},{5,4},{6,7},{7,6},{8,9},{9,8},{10,11... | collective-permute-start | bytes 294920 | tf_op jit(solution)/shard_map/ppermute | solution.py:311
  (5 other events, 4.0 us)

commit v9 on v8

--- a/solution.py
+++ b/solution.py
@@ -11,6 +11,7 @@
 BIG = -1e30
 MIB = 1024 * 1024
 VMEM = pl.BlockSpec(memory_space=pltpu.VMEM)
+SMEM = pl.BlockSpec(memory_space=pltpu.SMEM)
 ANY = pl.BlockSpec(memory_space=pl.ANY)
 
 
@@ -35,17 +36,47 @@
     return lax.broadcasted_iota(jnp.int32, shape, dim)
 
 
-def pick_kernel(wanted_ref, tiles_ref, *refs):
+def slot_of(owner, row_me, row_size, paired):
+    half = row_size // 2
+    return owner ^ row_me if paired else lax.rem(owner + lax.div(row_me, half) * half, row_size)
+
+
+def request_kernel(tiles_here, row_size, ids_ref, me_ref, out_ref):
+    half = row_size // 2
+    peer, which = iota(out_ref.shape, 0), iota(out_ref.shape, 1)
+    wanted = jnp.zeros(out_ref.shape, jnp.int32)
+    for slot in range(ids_ref.shape[1]):
+        tile = ids_ref[0, slot]
+        owner = lax.div(tile, tiles_here)
+        far = jnp.where(lax.div(owner, half) == lax.div(me_ref[0], half), 0, 1)
+        here = (peer == jnp.where(tile < 0, -1, lax.rem(owner, half))) & (which == far)
+        wanted = jnp.where(here, lax.rem(tile, tiles_here), wanted)
+    out_ref[...] = wanted
+
+
+def request(ids, me, tiles_here, row_size):
+    return pl.pallas_call(
+        functools.partial(request_kernel, tiles_here, row_size),
+        out_shape=jax.ShapeDtypeStruct((row_size // 2, 2, 128), jnp.int32),
+        in_specs=[SMEM, SMEM],
+        out_specs=VMEM,
+        compiler_params=params(0),
+        cost_estimate=pl.CostEstimate(flops=0, bytes_accessed=MIB // 4, transcendentals=0),
+        name="request",
+    )(ids, me)
+
+
+def pick_kernel(which, wanted_ref, tiles_ref, *refs):
     out_ref = refs[-1]
     for peer in range(out_ref.shape[0]):
-        out_ref[peer] = tiles_ref[wanted_ref[peer]]
-
-
-def pick(tiles, wanted, after):
-    return pl.pallas_call(
-        pick_kernel,
-        out_shape=jax.ShapeDtypeStruct(wanted.shape + tiles.shape[1:], tiles.dtype),
-        in_specs=[pl.BlockSpec(memory_space=pltpu.SMEM), VMEM] + [ANY] * len(after),
+        out_ref[peer] = tiles_ref[wanted_ref[peer, which, 0]]
+
+
+def pick(tiles, wanted, which, after):
+    return pl.pallas_call(
+        functools.partial(pick_kernel, which),
+        out_shape=jax.ShapeDtypeStruct(wanted.shape[:1] + tiles.shape[1:], tiles.dtype),
+        in_specs=[SMEM, VMEM] + [ANY] * len(after),
         out_specs=VMEM,
         compiler_params=params(0),
         cost_estimate=pl.CostEstimate(flops=0, bytes_accessed=2 * MIB, transcendentals=0),
@@ -53,18 +84,19 @@
     )(wanted, tiles, *after)
 
 
-def pick_each_kernel(wanted_ref, me_ref, tiles_ref, *refs):
-    for step, out_ref in enumerate(refs[-wanted_ref.shape[0]:]):
-        out_ref[0] = tiles_ref[wanted_ref[me_ref[0] ^ step]]
-
-
-def pick_each(tiles, wanted, me, after):
+def pick_each_kernel(which, wanted_ref, me_ref, tiles_ref, *refs):
+    half = wanted_ref.shape[0]
+    place = lax.rem(me_ref[0], half)
+    for step, out_ref in enumerate(refs[-half:]):
+        out_ref[0] = tiles_ref[wanted_ref[place ^ step, which, 0]]
+
+
+def pick_each(tiles, wanted, which, me, after):
     count = wanted.shape[0]
-    smem = pl.BlockSpec(memory_space=pltpu.SMEM)
-    return pl.pallas_call(
-        pick_each_kernel,
+    return pl.pallas_call(
+        functools.partial(pick_each_kernel, which),
         out_shape=(jax.ShapeDtypeStruct((1,) + tiles.shape[1:], tiles.dtype),) * count,
-        in_specs=[smem, smem, VMEM] + [ANY] * len(after),
+        in_specs=[SMEM, SMEM, VMEM] + [ANY] * len(after),
         out_specs=(VMEM,) * count,
         compiler_params=params(0),
         cost_estimate=pl.CostEstimate(flops=0, bytes_accessed=2 * MIB, transcendentals=0),
@@ -72,10 +104,10 @@
     )(wanted, me, tiles, *after)
 
 
-def front_kernel(groups, heads, head_size, chunk, cols, row_size, *refs):
+def front_kernel(groups, heads, head_size, chunk, cols, heads_here, tiles_here, row_size, paired, *refs):
     cell_refs, refs = refs[:groups], refs[groups:]
-    (holder_ref, mask_ref, gain_col_ref, w_qkv_ref, w_out_ref, gain_tile_ref, w_query_ref,
-     after_ref, resid_ref, asked_ref, normed_ref, packed_ref) = refs
+    (ids_ref, me_ref, mask_ref, gain_col_ref, w_qkv_ref, w_out_ref, gain_tile_ref, w_query_ref,
+     resid_ref, asked_ref, normed_ref, packed_ref) = refs
     own_rows, width = cell_refs[0].shape
     steps = own_rows // chunk
     span = groups * chunk
@@ -114,9 +146,15 @@
             if group == 0:
                 resid_ref[pl.ds(step * chunk, chunk), :] = resid
             normed_ref[pl.ds(start, chunk), :] = rms_scale(resid, gain_tile_ref[...]).astype(jnp.bfloat16)
-    slots = mask_ref.shape[1]
-    place = (holder_ref[...] + head_size == iota((slots, lanes_two), 1)).astype(jnp.bfloat16)
-    live = dot_rows((mask_ref[...] > 0).astype(jnp.bfloat16), place)
+    slots = mask_ref.shape[0]
+    slot, lane = iota((slots, lanes_two), 0), iota((slots, lanes_two), 1)
+    place = jnp.zeros((slots, lanes_two), jnp.float32)
+    for index in range(slots):
+        tile = ids_ref[0, index]
+        spot = jnp.where(tile < 0, -1, head_size + slot_of(lax.div(tile, tiles_here), me_ref[0], row_size, paired))
+        place = jnp.where((slot == index) & (lane == spot), 1.0, place)
+    live = lax.dot_general((mask_ref[...] > 0).astype(jnp.float32).astype(jnp.bfloat16), place.astype(jnp.bfloat16),
+                           (((0,), (0,)), ((), ())), preferred_element_type=jnp.float32)
     lane = iota(live.shape, 1)
     shut = jnp.where((lane >= head_size) & (lane < head_size + row_size) & (live < 0.5), 1.0, 0.0).astype(jnp.bfloat16)
     total = steps * span
@@ -124,8 +162,12 @@
     row_of = cell // span * (chunk // cols) + cell % chunk // cols
     spread = (row_of == iota((total, shut.shape[0]), 1)).astype(jnp.bfloat16)
     bias = dot_rows(spread, shut) * BIG
-    asked = dot_rows(normed_ref[...], w_query_ref[...]).astype(jnp.bfloat16).astype(jnp.float32) * scale
-    heads_here = asked.shape[1] // head_size
+    group_width = heads_here * head_size
+    if w_query_ref.shape[1] == group_width:
+        w_query = w_query_ref[...]
+    else:
+        w_query = w_query_ref[:, pl.ds(pl.multiple_of(me_ref[1] * group_width, group_width), group_width)]
+    asked = dot_rows(normed_ref[...], w_query).astype(jnp.bfloat16).astype(jnp.float32) * scale
     low = iota((total, lanes_two), 1) < head_size
     for head in range(heads_here):
         if heads_here % 2 == 0:
@@ -138,23 +180,23 @@
         asked_ref[head] = query.astype(jnp.bfloat16)
 
 
-def front(cells, holder, key_mask, gain_col, w_qkv, w_out, gain_tile, w_query, heads, head_size, cols, row_size, after):
+def front(cells, ids, me, key_mask, gain_col, w_qkv, w_out, gain_tile, w_query, heads, head_size, cols,
+          heads_here, tiles_here, row_size, paired):
     groups = len(cells)
     own_rows, width = cells[0].shape
     total = groups * own_rows
-    asked_shape = (w_query.shape[1] // head_size, total, 2 * head_size)
-    return pl.pallas_call(
-        functools.partial(front_kernel, groups, heads, head_size, ROW_GROUP * cols, cols, row_size),
+    return pl.pallas_call(
+        functools.partial(front_kernel, groups, heads, head_size, ROW_GROUP * cols, cols, heads_here, tiles_here, row_size, paired),
         out_shape=(jax.ShapeDtypeStruct((own_rows, width), jnp.float32),
-                   jax.ShapeDtypeStruct(asked_shape, jnp.bfloat16)),
-        in_specs=[VMEM] * (groups + 7) + [ANY],
+                   jax.ShapeDtypeStruct((heads_here, total, 2 * head_size), jnp.bfloat16)),
+        in_specs=[VMEM] * groups + [SMEM, SMEM] + [VMEM] * 6,
         out_specs=(VMEM, VMEM),
         scratch_shapes=[pltpu.VMEM((total, width), jnp.bfloat16), pltpu.VMEM((3, total, width), jnp.bfloat16)],
         compiler_params=params(total),
         cost_estimate=pl.CostEstimate(flops=2 * total * width * 5 * width, bytes_accessed=4 * MIB,
                                       transcendentals=total * heads * 128),
         name="front",
-    )(*cells, holder, key_mask, gain_col.reshape(1, width), w_qkv, w_out, gain_tile.reshape(1, width), w_query, after)
+    )(*cells, ids, me, key_mask.T, gain_col.reshape(1, width), w_qkv, w_out, gain_tile.reshape(1, width), w_query)
 
 
 def weigh(query, tile_refs, head, first_slot):
@@ -260,10 +302,10 @@
     heads_all = width // head_size
     group_width = heads_here * head_size
     half = row_size // 2
-    col_me = lax.axis_index("cols")
-    row_me = lax.axis_index("rows")
-    my_half, my_place = row_me // half, row_me % half
+    row_me, col_me = lax.axis_index("rows"), lax.axis_index("cols")
+    me = jnp.stack([row_me, col_me]).astype(jnp.int32)
     halves = [list(range(half)), list(range(half, row_size))]
+    paired = half <= 8 and half & (half - 1) == 0
     assert row_size <= head_size and row_size % 2 == 0
 
     def swap(value):
@@ -271,38 +313,28 @@
 
     heads_first = jnp.transpose(tile_kv, (0, 2, 1, 3))
     mirrored = lax.ppermute(heads_first, "rows", turn(row_size, half))
-
-    listed = tile_ids[0] >= 0
-    holder = jnp.where(listed, (tile_ids[0] // tiles_here + my_half * half) % row_size, -1)
-    wanted = jnp.sum(jnp.where(holder[:, None] == jnp.arange(row_size)[None, :], (tile_ids[0] % tiles_here)[:, None], 0), axis=0)
-    asked_of = jnp.broadcast_to(wanted.astype(jnp.int32).reshape(2, half).T[:, :, None], (half, 2, 128))
-    asked_by = swap(asked_of)[:, :, 0]
+    asked_by = swap(request(tile_ids, me, tiles_here, row_size))
 
     cells = [fact_cells.reshape(rows * cols, width)]
     for step in range(1, col_size):
         cells.append(lax.ppermute(cells[0], "cols", turn(col_size, -step)))
 
-    near_by, far_by = asked_by[:, 0], asked_by[:, 1]
-    if half <= 8 and half & (half - 1) == 0:
-        holder = jnp.where(holder < 0, holder, holder ^ my_place)
-
-        def spread(tiles, wanted, after):
-            picked = pick_each(tiles, wanted, my_place.reshape(1), after)
-            arrived = [picked[0]]
-            for step in range(1, half):
-                pairs = [(row, row // half * half + (row % half ^ step)) for row in range(row_size)]
-                arrived.append(lax.ppermute(picked[step], "rows", pairs))
-            return picked[0], arrived
-    else:
-        def spread(tiles, wanted, after):
-            picked = pick(tiles, wanted, after)
-            return picked, [swap(picked)]
-
-    picked, near = spread(heads_first, near_by, [])
-    picked, far = spread(mirrored, far_by, near)
-    query_here = lax.dynamic_slice_in_dim(w_query, col_me * group_width, group_width, 1)
-    residual, asked = front(cells, holder[:, None], key_mask, gain_col, w_qkv, w_col_out, gain_tile, query_here,
-                            heads_all, head_size, cols, row_size, picked)
+    def spread(tiles, which, after):
+        if not paired:
+            return [swap(pick(tiles, asked_by, which, after))]
+        picked = pick_each(tiles, asked_by, which, me, after)
+        arrived = list(picked[:1]) + [None] * (half - 1)
+        for step in sorted(range(1, half), key=lambda step: (-(step & half // 2), step & 1, -step)):
+            pairs = [(row, row ^ step) for row in range(row_size)]
+            arrived[step] = lax.ppermute(picked[step], "rows", pairs)
+        return arrived
+
+    near = spread(heads_first, 0, cells[:1])
+    if group_width % 128:
+        w_query = lax.dynamic_slice_in_dim(w_query, col_me * group_width, group_width, 1)
+    residual, asked = front(cells, tile_ids, me, key_mask, gain_col, w_qkv, w_col_out, gain_tile, w_query,
+                            heads_all, head_size, cols, heads_here, tiles_here, row_size, paired)
+    far = spread(mirrored, 1, near + [asked])
     sums, tops = first_tiles(asked, near)
     answers = last_tiles(asked, sums, tops, far, half, col_size, cols)
 

time: 71.2 us -> 67.6 us (0.949)
  blocking collectives: 0 us -> 8.26 us
  starting transfers between devices: 27.4 us -> 20.7 us
  waiting for transfers between devices: 21 us -> 15.8 us
  Pallas kernels: 10.8 us -> 12.4 us
  local copies, waits for them, and re-layouts: 10.3 us -> 9.57 us
    all_to_all x0 -> x1, blocking collectives: none -> 8.26 us  [swap(): lax.all_to_all(value, 'rows', split_axis=0, concat_axis=0, tiled=True, ax...]
    all_to_all x1 -> x0, waiting for transfers between devices: 5.94 us -> none  [swap(): lax.all_to_all(value, 'rows', split_axis=0, concat_axis=0, tiled=True, ax...]
    all_to_all x1 -> x0, starting transfers between devices: 3.78 us -> none  [swap(): lax.all_to_all(value, 'rows', split_axis=0, concat_axis=0, tiled=True, ax...]
    ppermute x14, starting transfers between devices: 16.4 us -> 13.4 us  [spread(): arrived[step] = lax.ppermute(picked[step], 'rows', pairs)]
    unnamed x24 -> x25, local copies, waits for them, and re-layouts: 6.01 us -> 7.86 us
    dynamic_slice x1 -> x0, local copies, waits for them, and re-layouts: 0.97 us -> none  [shards(): lax.dynamic_slice_in_dim(w_query, col_me * group_width, group_width, 1)]
    ppermute x14, waiting for transfers between devices: 11.9 us -> 12.7 us  [spread(): arrived[step] = lax.ppermute(picked[step], 'rows', pairs)]
    pallas_call x1, Pallas kernels: 2.65 us -> 3.41 us  [last_tiles(): pl.pallas_call(functools.partial(last_kernel, groups, len(tiles), first_s...]
  transfers between devices with their start and end apart: 18 -> 17, of which waited for: 9 -> 8; matrix products, arithmetic and copies ran while one was open for 8% -> 2% of each run, Pallas kernels for 12% -> 11%
where the time goes in v9:
time: 67.6 us; the launch traced here: 67.3 us
  starting transfers between devices  20.7 us (31%)
  waiting for transfers between devices  15.8 us (23%)
  Pallas kernels  12.4 us (18%)
  local copies, waits for them, and re-layouts  9.57 us (14%)
  blocking collectives  8.26 us (12%)
    ppermute x14, starting transfers between devices, spread(): arrived[step] = lax.ppermute(picked[step], 'rows', pairs)  13.4 us
    ppermute x14, waiting for transfers between devices, spread(): arrived[step] = lax.ppermute(picked[step], 'rows', pairs)  12.7 us
    all_to_all x1, blocking collectives, swap(): lax.all_to_all(value, 'rows', split_axis=0, concat_axis=0, tiled=True, ax...  8.26 us
    unnamed x25, local copies, waits for them, and re-layouts  7.86 us
    ppermute x1, starting transfers between devices, shards(): mirrored = lax.ppermute(heads_first, 'rows', turn(row_size, half))  4.11 us
    pallas_call x1, Pallas kernels, front(): pl.pallas_call(functools.partial(front_kernel, groups, heads, head_size,...  3.69 us
    pallas_call x1, Pallas kernels, last_tiles(): pl.pallas_call(functools.partial(last_kernel, groups, len(tiles), first_s...  3.41 us
    ppermute x1, waiting for transfers between devices, shards(): lax.ppermute(answers[step], 'cols', turn(col_size, step))  3.09 us
  transfers between devices with their start and end apart: 17, of which 8 were waited for; matrix products, arithmetic and copies ran while one was open for 2% of the time, Pallas kernels for 11%

profile of v9, /device:TPU:0, one launch (start us, length us, event | category | flops | bytes accessed | tf_op | source)
XLA Modules:
  0.0 67.3 jit_solution(6415243176266436702)
XLA Ops:
  0.0 1.2 %copy.13 = bf16[4,128,4,128]{3,1,2,0:T(8,128)(2,1)S(1)} copy(bf16[4,128,4,128]{3,2,1,0:T(4,128)(2,1)} %param.17) | data formatting | bytes 1048576 | tf_op args[7]
  1.2 4.1 %collective-permute-start.8 = (bf16[4,4,128,128]{3,2,1,0:T(8,128)(2,1)S(1)}, bf16[4,4,128,128]{3,2,1,0:T(8,128)(2,1)S(1)}, u32[]{:S(2)}, u32[]{:S(2)}) collective-permute-start(bf16[4,4,128,128]{3,2,1,0:T(8,128)(2,1)S(1)} %bitcast.10), channel_id=1, source_target_pairs={{0,16},{2,18},{4,20},{6,22},{8,24},{10,26},{12,28},{14,30},{16,0},... | collective-permute-start | bytes 1572872 | tf_op jit(solution)/shard_map/ppermute | solution.py:315
  6.3 1.6 %collective-permute-start = (bf16[192,512]{1,0:T(8,128)(2,1)S(1)}, bf16[192,512]{1,0:T(8,128)(2,1)S(1)}, u32[]{:S(2)}, u32[]{:S(2)}) collective-permute-start(bf16[192,512]{1,0:T(8,128)(2,1)S(1)} %reshape.12.refs_0_), channel_id=1, source_target_pairs={{0,1},{1,0},{2,3},{3,2},{4,5},{5,4},{6,7},{7,6},{8,9},{9,8},{10,11... | collective-permute-start | bytes 589832 | tf_op jit(solution)/shard_map/ppermute | solution.py:320
  9.3 8.3 %all_to_all.5.wanted_ref = s32[8,2,128]{2,1,0:T(2,128)S(1)} all-to-all(s32[8,2,128]{2,1,0:T(2,128)S(1)} %request.1), channel_id=1, replica_groups={{0,2,4,6,8,10,12,14},{16,18,20,22,24,26,28,30},{1,3,5,7,9,11,13,15},{17..., dimensions={0} | all-to-all | bytes 16384 | tf_op jit(solution)/shard_map/all_to_all | solution.py:312
  19.0 1.2 %collective-permute-start.3 = (bf16[1,4,128,128]{3,2,1,0:T(8,128)(2,1)S(1)}, bf16[1,4,128,128]{3,2,1,0:T(8,128)(2,1)S(1)}, u32[]{:S(2)}, u32[]{:S(2)}) collective-permute-start(bf16[1,4,128,128]{3,2,1,0:T(8,128)(2,1)S(1)} %get-tuple-element.32), channel_id=1, source_target_pairs={{0,6},{2,4},{4,2},{6,0},{8,14},{10,12},{12,10},{14,8},{16,22},{18,... | collective-permute-start | bytes 393224 | tf_op jit(solution)/shard_map/ppermute | solution.py:329
  20.2 2.5 %collective-permute-start.4 = (bf16[1,4,128,128]{3,2,1,0:T(8,128)(2,1)S(1)}, bf16[1,4,128,128]{3,2,1,0:T(8,128)(2,1)S(1)}, u32[]{:S(2)}, u32[]{:S(2)}) collective-permute-start(bf16[1,4,128,128]{3,2,1,0:T(8,128)(2,1)S(1)} %get-tuple-element.33), channel_id=1, source_target_pairs={{0,8},{2,10},{4,12},{6,14},{8,0},{10,2},{12,4},{14,6},{16,24},{18,... | collective-permute-start | bytes 393224 | tf_op jit(solution)/shard_map/ppermute | solution.py:329
  22.7 2.0 %collective-permute-done.2.refs_2_ = bf16[1,4,128,128]{3,2,1,0:T(8,128)(2,1)S(1)} collective-permute-done((bf16[1,4,128,128]{3,2,1,0:T(8,128)(2,1)S(1)}, bf16[1,4,128,128]{3,2,1,0:T(8,128)(2,1)S(1)}, u32[]{:S(2)}, u32[]{:S(2)}) %collective-permute-start.2) | collective-permute-done | bytes 131104 | tf_op jit(solution)/shard_map/ppermute | solution.py:329
  24.7 1.3 %collective-permute-start.5 = (bf16[1,4,128,128]{3,2,1,0:T(8,128)(2,1)S(1)}, bf16[1,4,128,128]{3,2,1,0:T(8,128)(2,1)S(1)}, u32[]{:S(2)}, u32[]{:S(2)}) collective-permute-start(bf16[1,4,128,128]{3,2,1,0:T(8,128)(2,1)S(1)} %get-tuple-element.34), channel_id=1, source_target_pairs={{0,10},{2,8},{4,14},{6,12},{8,2},{10,0},{12,6},{14,4},{16,26},{18,... | collective-permute-start | bytes 393224 | tf_op jit(solution)/shard_map/ppermute | solution.py:329
  26.6 2.5 %collective-permute-start.6 = (bf16[1,4,128,128]{3,2,1,0:T(8,128)(2,1)S(1)}, bf16[1,4,128,128]{3,2,1,0:T(8,128)(2,1)S(1)}, u32[]{:S(2)}, u32[]{:S(2)}) collective-permute-start(bf16[1,4,128,128]{3,2,1,0:T(8,128)(2,1)S(1)} %get-tuple-element.35), channel_id=1, source_target_pairs={{0,12},{2,14},{4,8},{6,10},{8,4},{10,6},{12,0},{14,2},{16,28},{18,... | collective-permute-start | bytes 393224 | tf_op jit(solution)/shard_map/ppermute | solution.py:329
  30.3 1.4 %copy-done.4 = bf16[512,1536]{1,0:T(8,128)(2,1)S(1)} copy-done((bf16[512,1536]{1,0:T(8,128)(2,1)S(1)}, bf16[512,1536]{1,0:T(8,128)(2,1)}, u32[]{:S(2)}) %copy-start.4) | copy-done | bytes 1572888
  31.7 1.0 %copy-done.5 = bf16[512,512]{1,0:T(8,128)(2,1)S(1)} copy-done((bf16[512,512]{1,0:T(8,128)(2,1)S(1)}, bf16[512,512]{1,0:T(8,128)(2,1)}, u32[]{:S(2)}) %copy-start.5) | copy-done | bytes 524312
  32.7 1.0 %copy-done.6 = bf16[512,512]{1,0:T(8,128)(2,1)S(1)} copy-done((bf16[512,512]{1,0:T(8,128)(2,1)S(1)}, bf16[512,512]{1,0:T(8,128)(2,1)}, u32[]{:S(2)}) %copy-start.6) | copy-done | bytes 524312
  34.7 3.7 %front.1 = (f32[192,512]{1,0:T(8,128)S(1)}, bf16[4,384,128]{2,1,0:T(8,128)(2,1)S(1)}) custom-call(bf16[192,512]{1,0:T(8,128)(2,1)S(1)} %reshape.12.refs_0_, bf16[192,512]{1,0:T(8,128)(2,1)S(1)} %copy-done.8, s32[1,12]{1,0:T(1,128)S(1)} %copy-done.3, s32[2]{0:T(128)S(1)} %pad_add_fusion.refs_3_.me_ref, s32[12,48]{1,0:T(8,128)S(1)} %bitcast.12, ...), custom_call_target="tpu_custom_call" | custom-call | flops 1006632960 | bytes 4194304 | tf_op jit(solution)/shard_map/front/pallas_call | solution.py:188
  38.4 2.2 %collective-permute-done.7.refs_7_ = bf16[1,4,128,128]{3,2,1,0:T(8,128)(2,1)S(1)} collective-permute-done((bf16[1,4,128,128]{3,2,1,0:T(8,128)(2,1)S(1)}, bf16[1,4,128,128]{3,2,1,0:T(8,128)(2,1)S(1)}, u32[]{:S(2)}, u32[]{:S(2)}) %collective-permute-start.7) | collective-permute-done | bytes 131104 | tf_op jit(solution)/shard_map/ppermute | solution.py:329
  40.7 1.5 %pick_each.3 = (bf16[1,4,128,128]{3,2,1,0:T(8,128)(2,1)S(1)}, bf16[1,4,128,128]{3,2,1,0:T(8,128)(2,1)S(1)}, bf16[1,4,128,128]{3,2,1,0:T(8,128)(2,1)S(1)}, bf16[1...) custom-call(s32[8,2,128]{2,1,0:T(2,128)S(1)} %all_to_all.5.wanted_re, ...), custom_call_target="tpu_custom_call" | custom-call | bytes 2097152 | tf_op jit(solution)/shard_map/pick_each/pallas_call | solution.py:96
  43.9 1.8 %collective-permute-start.13 = (bf16[1,4,128,128]{3,2,1,0:T(8,128)(2,1)}, bf16[1,4,128,128]{3,2,1,0:T(8,128)(2,1)S(1)}, u32[]{:S(2)}, u32[]{:S(2)}) collective-permute-start(bf16[1,4,128,128]{3,2,1,0:T(8,128)(2,1)} %get-tuple-element.44), channel_id=1, source_target_pairs={{0,10},{2,8},{4,14},{6,12},{8,2},{10,0},{12,6},{14,4},{16,26},{18,... | collective-permute-start | bytes 393224 | tf_op jit(solution)/shard_map/ppermute | solution.py:329
  45.9 2.6 %collective-permute-done.10.refs_2_ = bf16[1,4,128,128]{3,2,1,0:T(8,128)(2,1)S(1)} collective-permute-done((bf16[1,4,128,128]{3,2,1,0:T(8,128)(2,1)S(1)}, bf16[1,4,128,128]{3,2,1,0:T(8,128)(2,1)S(1)}, u32[]{:S(2)}, u32[]{:S(2)}) %collective-permute-start.10) | collective-permute-done | bytes 131104 | tf_op jit(solution)/shard_map/ppermute | solution.py:329
  48.5 1.1 %collective-permute-done.11.refs_3_ = bf16[1,4,128,128]{3,2,1,0:T(8,128)(2,1)S(1)} collective-permute-done((bf16[1,4,128,128]{3,2,1,0:T(8,128)(2,1)S(1)}, bf16[1,4,128,128]{3,2,1,0:T(8,128)(2,1)S(1)}, u32[]{:S(2)}, u32[]{:S(2)}) %collective-permute-start.11) | collective-permute-done | bytes 131104 | tf_op jit(solution)/shard_map/ppermute | solution.py:329
  51.5 2.4 %first_tiles.1 = (f32[4,384,128]{2,1,0:T(8,128)S(1)}, f32[384,128]{1,0:T(8,128)S(1)}) custom-call(bf16[4,384,128]{2,1,0:T(8,128)(2,1)S(1)} %get-tuple-element.28.asked_ref.refs_8_, bf16[1,4,128,128]{3,2,1,0:T(8,128)(2,1)S(1)} %get-tuple-element.29.refs_0_, bf16[1,4,128,128]{3,2,1,0:T(8,128)(2,1)S(1)} %collective-permute-done.1.refs_1_, ...), custom_call_target="tpu_custom_call" | custom-call | flops 805306368 | bytes 4194304 | tf_op jit(solution)/shard_map/first_tiles/pallas_call | solution.py:236
  53.9 1.8 %collective-permute-done.14.refs_6_ = bf16[1,4,128,128]{3,2,1,0:T(8,128)(2,1)S(1)} collective-permute-done((bf16[1,4,128,128]{3,2,1,0:T(8,128)(2,1)}, bf16[1,4,128,128]{3,2,1,0:T(8,128)(2,1)S(1)}, u32[]{:S(2)}, u32[]{:S(2)}) %collective-permute-start.14) | collective-permute-done | bytes 131104 | tf_op jit(solution)/shard_map/ppermute | solution.py:329
  55.8 2.2 %collective-permute-done.15.refs_7_ = bf16[1,4,128,128]{3,2,1,0:T(8,128)(2,1)S(1)} collective-permute-done((bf16[1,4,128,128]{3,2,1,0:T(8,128)(2,1)}, bf16[1,4,128,128]{3,2,1,0:T(8,128)(2,1)S(1)}, u32[]{:S(2)}, u32[]{:S(2)}) %collective-permute-start.15) | collective-permute-done | bytes 131104 | tf_op jit(solution)/shard_map/ppermute | solution.py:329
  58.0 3.4 %last_tiles.1 = (bf16[192,256]{1,0:T(8,128)(2,1)S(1)}, bf16[192,256]{1,0:T(8,128)(2,1)S(1)}) custom-call(bf16[4,384,128]{2,1,0:T(8,128)(2,1)S(1)} %get-tuple-element.28.asked_ref.refs_8_, f32[4,384,128]{2,1,0:T(8,128)S(1)} %get-tuple-element.37.sums_ref, f32[384,128]{1,0:T(8,128)S(1)} %get-tuple-element.38.tops_ref, ...), custom_call_target="tpu_custom_call" | custom-call | flops 805306368 | bytes 4194304 | tf_op jit(solution)/shard_map/last_tiles/pallas_call | solution.py:282
  61.4 1.6 %collective-permute-start.16 = (bf16[192,256]{1,0:T(8,128)(2,1)S(1)}, bf16[192,256]{1,0:T(8,128)(2,1)S(1)}, u32[]{:S(2)}, u32[]{:S(2)}) collective-permute-start(bf16[192,256]{1,0:T(8,128)(2,1)S(1)} %get-tuple-element.48), channel_id=1, source_target_pairs={{0,1},{1,0},{2,3},{3,2},{4,5},{5,4},{6,7},{7,6},{8,9},{9,8},{10,11... | collective-permute-start | bytes 294920 | tf_op jit(solution)/shard_map/ppermute | solution.py:343
  63.2 3.1 %collective-permute-done.16 = bf16[192,256]{1,0:T(8,128)(2,1)S(1)} collective-permute-done((bf16[192,256]{1,0:T(8,128)(2,1)S(1)}, bf16[192,256]{1,0:T(8,128)(2,1)S(1)}, u32[]{:S(2)}, u32[]{:S(2)}) %collective-permute-start.16) | collective-permute-done | bytes 98336 | tf_op jit(solution)/shard_map/ppermute | solution.py:343
  (47 shorter events, 11.4 us)
Async XLA Ops:
  0.0 63.0 %copy-start = (bf16[512,512]{1,0:T(8,128)(2,1)S(1)}, bf16[512,512]{1,0:T(8,128)(2,1)}, u32[]{:S(2)}) copy-start(bf16[512,512]{1,0:T(8,128)(2,1)} %param.16) | copy-start | bytes 1572868
  0.0 30.3 %copy-start.9 = (s32[48,12]{0,1:T(8,128)S(1)}, s32[48,12]{0,1:T(8,128)}, u32[]{:S(2)}) copy-start(s32[48,12]{0,1:T(8,128)} %param.19) | copy-start | bytes 6916
  0.0 30.3 %copy-start.10 = (f32[512]{0:T(512)S(1)}, f32[512]{0:T(512)}, u32[]{:S(2)}) copy-start(f32[512]{0:T(512)} %param.11) | copy-start | bytes 6148
  0.0 30.3 %copy-start.11 = (f32[512]{0:T(512)S(1)}, f32[512]{0:T(512)}, u32[]{:S(2)}) copy-start(f32[512]{0:T(512)} %param.14) | copy-start | bytes 6148
  1.2 39.5 %collective-permute-start.8 = (bf16[4,4,128,128]{3,2,1,0:T(8,128)(2,1)S(1)}, bf16[4,4,128,128]{3,2,1,0:T(8,128)(2,1)S(1)}, u32[]{:S(2)}, u32[]{:S(2)}) collective-permute-start(bf16[4,4,128,128]{3,2,1,0:T(8,128)(2,1)S(1)} %bitcast.10), channel_id=1, source_target_pairs={{0,16},{2,18},{4,20},{6,22},{8,24},{10,26},{12,28},{14,30},{16,0},... | collective-permute-start | bytes 1572872 | tf_op jit(solution)/shard_map/ppermute | solution.py:315
  6.3 22.8 %collective-permute-start = (bf16[192,512]{1,0:T(8,128)(2,1)S(1)}, bf16[192,512]{1,0:T(8,128)(2,1)S(1)}, u32[]{:S(2)}, u32[]{:S(2)}) collective-permute-start(bf16[192,512]{1,0:T(8,128)(2,1)S(1)} %reshape.12.refs_0_), channel_id=1, source_target_pairs={{0,1},{1,0},{2,3},{3,2},{4,5},{5,4},{6,7},{7,6},{8,9},{9,8},{10,11... | collective-permute-start | bytes 589832 | tf_op jit(solution)/shard_map/ppermute | solution.py:320
  18.3 2.0 %collective-permute-start.1 = (bf16[1,4,128,128]{3,2,1,0:T(8,128)(2,1)S(1)}, bf16[1,4,128,128]{3,2,1,0:T(8,128)(2,1)S(1)}, u32[]{:S(2)}, u32[]{:S(2)}) collective-permute-start(bf16[1,4,128,128]{3,2,1,0:T(8,128)(2,1)S(1)} %get-tuple-element.30), channel_id=1, source_target_pairs={{0,2},{2,0},{4,6},{6,4},{8,10},{10,8},{12,14},{14,12},{16,18},{18,... | collective-permute-start | bytes 393224 | tf_op jit(solution)/shard_map/ppermute | solution.py:329
  18.4 6.3 %collective-permute-start.2 = (bf16[1,4,128,128]{3,2,1,0:T(8,128)(2,1)S(1)}, bf16[1,4,128,128]{3,2,1,0:T(8,128)(2,1)S(1)}, u32[]{:S(2)}, u32[]{:S(2)}) collective-permute-start(bf16[1,4,128,128]{3,2,1,0:T(8,128)(2,1)S(1)} %get-tuple-element.31), channel_id=1, source_target_pairs={{0,4},{2,6},{4,0},{6,2},{8,12},{10,14},{12,8},{14,10},{16,20},{18,... | collective-permute-start | bytes 393224 | tf_op jit(solution)/shard_map/ppermute | solution.py:329
  19.0 7.6 %collective-permute-start.3 = (bf16[1,4,128,128]{3,2,1,0:T(8,128)(2,1)S(1)}, bf16[1,4,128,128]{3,2,1,0:T(8,128)(2,1)S(1)}, u32[]{:S(2)}, u32[]{:S(2)}) collective-permute-start(bf16[1,4,128,128]{3,2,1,0:T(8,128)(2,1)S(1)} %get-tuple-element.32), channel_id=1, source_target_pairs={{0,6},{2,4},{4,2},{6,0},{8,14},{10,12},{12,10},{14,8},{16,22},{18,... | collective-permute-start | bytes 393224 | tf_op jit(solution)/shard_map/ppermute | solution.py:329
  20.2 18.2 %collective-permute-start.4 = (bf16[1,4,128,128]{3,2,1,0:T(8,128)(2,1)S(1)}, bf16[1,4,128,128]{3,2,1,0:T(8,128)(2,1)S(1)}, u32[]{:S(2)}, u32[]{:S(2)}) collective-permute-start(bf16[1,4,128,128]{3,2,1,0:T(8,128)(2,1)S(1)} %get-tuple-element.33), channel_id=1, source_target_pairs={{0,8},{2,10},{4,12},{6,14},{8,0},{10,2},{12,4},{14,6},{16,24},{18,... | collective-permute-start | bytes 393224 | tf_op jit(solution)/shard_map/ppermute | solution.py:329
  24.7 13.7 %collective-permute-start.5 = (bf16[1,4,128,128]{3,2,1,0:T(8,128)(2,1)S(1)}, bf16[1,4,128,128]{3,2,1,0:T(8,128)(2,1)S(1)}, u32[]{:S(2)}, u32[]{:S(2)}) collective-permute-start(bf16[1,4,128,128]{3,2,1,0:T(8,128)(2,1)S(1)} %get-tuple-element.34), channel_id=1, source_target_pairs={{0,10},{2,8},{4,14},{6,12},{8,2},{10,0},{12,6},{14,4},{16,26},{18,... | collective-permute-start | bytes 393224 | tf_op jit(solution)/shard_map/ppermute | solution.py:329
  26.6 11.8 %collective-permute-start.6 = (bf16[1,4,128,128]{3,2,1,0:T(8,128)(2,1)S(1)}, bf16[1,4,128,128]{3,2,1,0:T(8,128)(2,1)S(1)}, u32[]{:S(2)}, u32[]{:S(2)}) collective-permute-start(bf16[1,4,128,128]{3,2,1,0:T(8,128)(2,1)S(1)} %get-tuple-element.35), channel_id=1, source_target_pairs={{0,12},{2,14},{4,8},{6,10},{8,4},{10,6},{12,0},{14,2},{16,28},{18,... | collective-permute-start | bytes 393224 | tf_op jit(solution)/shard_map/ppermute | solution.py:329
  29.8 10.8 %collective-permute-start.7 = (bf16[1,4,128,128]{3,2,1,0:T(8,128)(2,1)S(1)}, bf16[1,4,128,128]{3,2,1,0:T(8,128)(2,1)S(1)}, u32[]{:S(2)}, u32[]{:S(2)}) collective-permute-start(bf16[1,4,128,128]{3,2,1,0:T(8,128)(2,1)S(1)} %get-tuple-element.36), channel_id=1, source_target_pairs={{0,14},{2,12},{4,10},{6,8},{8,6},{10,4},{12,2},{14,0},{16,30},{18,... | collective-permute-start | bytes 393224 | tf_op jit(solution)/shard_map/ppermute | solution.py:329
  30.3 1.4 %copy-start.4 = (bf16[512,1536]{1,0:T(8,128)(2,1)S(1)}, bf16[512,1536]{1,0:T(8,128)(2,1)}, u32[]{:S(2)}) copy-start(bf16[512,1536]{1,0:T(8,128)(2,1)} %refs_6_.1) | copy-start | bytes 4718596
  31.7 1.0 %copy-start.5 = (bf16[512,512]{1,0:T(8,128)(2,1)S(1)}, bf16[512,512]{1,0:T(8,128)(2,1)}, u32[]{:S(2)}) copy-start(bf16[512,512]{1,0:T(8,128)(2,1)} %refs_7_.1) | copy-start | bytes 1572868
  40.7 1.5 %copy-start.1 = (bf16[1,4,128,128]{3,2,1,0:T(8,128)(2,1)}, bf16[1,4,128,128]{3,2,1,0:T(8,128)(2,1)S(1)}, u32[]{:S(2)}) copy-start(bf16[1,4,128,128]{3,2,1,0:T(8,128)(2,1)S(1)} %collective-permute-done.7.refs_7_) | copy-start | bytes 393220
  42.2 6.3 %collective-permute-start.10 = (bf16[1,4,128,128]{3,2,1,0:T(8,128)(2,1)S(1)}, bf16[1,4,128,128]{3,2,1,0:T(8,128)(2,1)S(1)}, u32[]{:S(2)}, u32[]{:S(2)}) collective-permute-start(bf16[1,4,128,128]{3,2,1,0:T(8,128)(2,1)S(1)} %get-tuple-element.41), channel_id=1, source_target_pairs={{0,4},{2,6},{4,0},{6,2},{8,12},{10,14},{12,8},{14,10},{16,20},{18,... | collective-permute-start | bytes 393224 | tf_op jit(solution)/shard_map/ppermute | solution.py:329
  42.7 7.0 %collective-permute-start.11 = (bf16[1,4,128,128]{3,2,1,0:T(8,128)(2,1)S(1)}, bf16[1,4,128,128]{3,2,1,0:T(8,128)(2,1)S(1)}, u32[]{:S(2)}, u32[]{:S(2)}) collective-permute-start(bf16[1,4,128,128]{3,2,1,0:T(8,128)(2,1)S(1)} %get-tuple-element.42), channel_id=1, source_target_pairs={{0,6},{2,4},{4,2},{6,0},{8,14},{10,12},{12,10},{14,8},{16,22},{18,... | collective-permute-start | bytes 393224 | tf_op jit(solution)/shard_map/ppermute | solution.py:329
  43.7 10.3 %collective-permute-start.12 = (bf16[1,4,128,128]{3,2,1,0:T(8,128)(2,1)}, bf16[1,4,128,128]{3,2,1,0:T(8,128)(2,1)S(1)}, u32[]{:S(2)}, u32[]{:S(2)}) collective-permute-start(bf16[1,4,128,128]{3,2,1,0:T(8,128)(2,1)} %get-tuple-element.43), channel_id=1, source_target_pairs={{0,8},{2,10},{4,12},{6,14},{8,0},{10,2},{12,4},{14,6},{16,24},{18,... | collective-permute-start | bytes 393224 | tf_op jit(solution)/shard_map/ppermute | solution.py:329
  43.9 10.0 %collective-permute-start.13 = (bf16[1,4,128,128]{3,2,1,0:T(8,128)(2,1)}, bf16[1,4,128,128]{3,2,1,0:T(8,128)(2,1)S(1)}, u32[]{:S(2)}, u32[]{:S(2)}) collective-permute-start(bf16[1,4,128,128]{3,2,1,0:T(8,128)(2,1)} %get-tuple-element.44), channel_id=1, source_target_pairs={{0,10},{2,8},{4,14},{6,12},{8,2},{10,0},{12,6},{14,4},{16,26},{18,... | collective-permute-start | bytes 393224 | tf_op jit(solution)/shard_map/ppermute | solution.py:329
  45.7 10.0 %collective-permute-start.14 = (bf16[1,4,128,128]{3,2,1,0:T(8,128)(2,1)}, bf16[1,4,128,128]{3,2,1,0:T(8,128)(2,1)S(1)}, u32[]{:S(2)}, u32[]{:S(2)}) collective-permute-start(bf16[1,4,128,128]{3,2,1,0:T(8,128)(2,1)} %get-tuple-element.45), channel_id=1, source_target_pairs={{0,12},{2,14},{4,8},{6,10},{8,4},{10,6},{12,0},{14,2},{16,28},{18,... | collective-permute-start | bytes 393224 | tf_op jit(solution)/shard_map/ppermute | solution.py:329
  48.5 9.5 %collective-permute-start.15 = (bf16[1,4,128,128]{3,2,1,0:T(8,128)(2,1)}, bf16[1,4,128,128]{3,2,1,0:T(8,128)(2,1)S(1)}, u32[]{:S(2)}, u32[]{:S(2)}) collective-permute-start(bf16[1,4,128,128]{3,2,1,0:T(8,128)(2,1)} %get-tuple-element.46), channel_id=1, source_target_pairs={{0,14},{2,12},{4,10},{6,8},{8,6},{10,4},{12,2},{14,0},{16,30},{18,... | collective-permute-start | bytes 393224 | tf_op jit(solution)/shard_map/ppermute | solution.py:329
  49.7 8.3 %collective-permute-start.9 = (bf16[1,4,128,128]{3,2,1,0:T(8,128)(2,1)S(1)}, bf16[1,4,128,128]{3,2,1,0:T(8,128)(2,1)}, u32[]{:S(2)}, u32[]{:S(2)}) collective-permute-start(bf16[1,4,128,128]{3,2,1,0:T(8,128)(2,1)S(1)} %get-tuple-element.40), channel_id=1, source_target_pairs={{0,2},{2,0},{4,6},{6,4},{8,10},{10,8},{12,14},{14,12},{16,18},{18,... | collective-permute-start | bytes 393224 | tf_op jit(solution)/shard_map/ppermute | solution.py:329
  61.4 4.9 %collective-permute-start.16 = (bf16[192,256]{1,0:T(8,128)(2,1)S(1)}, bf16[192,256]{1,0:T(8,128)(2,1)S(1)}, u32[]{:S(2)}, u32[]{:S(2)}) collective-permute-start(bf16[192,256]{1,0:T(8,128)(2,1)S(1)} %get-tuple-element.48), channel_id=1, source_target_pairs={{0,1},{1,0},{2,3},{3,2},{4,5},{5,4},{6,7},{7,6},{8,9},{9,8},{10,11... | collective-permute-start | bytes 294920 | tf_op jit(solution)/shard_map/ppermute | solution.py:343
  (5 other events, 4.2 us)

commit v10 on v9

--- a/solution.py
+++ b/solution.py
@@ -12,6 +12,7 @@
 MIB = 1024 * 1024
 VMEM = pl.BlockSpec(memory_space=pltpu.VMEM)
 SMEM = pl.BlockSpec(memory_space=pltpu.SMEM)
+HBM = pl.BlockSpec(memory_space=pltpu.HBM)
 ANY = pl.BlockSpec(memory_space=pl.ANY)
 
 
@@ -84,17 +85,16 @@
     )(wanted, tiles, *after)
 
 
-def pick_each_kernel(which, wanted_ref, me_ref, tiles_ref, *refs):
-    half = wanted_ref.shape[0]
-    place = lax.rem(me_ref[0], half)
-    for step, out_ref in enumerate(refs[-half:]):
+def pick_each_kernel(which, order, wanted_ref, me_ref, tiles_ref, *refs):
+    place = lax.rem(me_ref[0], wanted_ref.shape[0])
+    for step, out_ref in zip(order, refs[-len(order):]):
         out_ref[0] = tiles_ref[wanted_ref[place ^ step, which, 0]]
 
 
-def pick_each(tiles, wanted, which, me, after):
-    count = wanted.shape[0]
-    return pl.pallas_call(
-        functools.partial(pick_each_kernel, which),
+def pick_each(tiles, wanted, which, me, order, after):
+    count = len(order)
+    return pl.pallas_call(
+        functools.partial(pick_each_kernel, which, order),
         out_shape=(jax.ShapeDtypeStruct((1,) + tiles.shape[1:], tiles.dtype),) * count,
         in_specs=[SMEM, SMEM, VMEM] + [ANY] * len(after),
         out_specs=(VMEM,) * count,
@@ -106,18 +106,33 @@
 
 def front_kernel(groups, heads, head_size, chunk, cols, heads_here, tiles_here, row_size, paired, *refs):
     cell_refs, refs = refs[:groups], refs[groups:]
-    (ids_ref, me_ref, mask_ref, gain_col_ref, w_qkv_ref, w_out_ref, gain_tile_ref, w_query_ref,
-     resid_ref, asked_ref, normed_ref, packed_ref) = refs
-    own_rows, width = cell_refs[0].shape
+    (ids_ref, me_ref, mask_ref, gain_col_ref, gain_tile_ref, w_qkv_hbm, w_out_hbm, w_query_hbm,
+     resid_ref, asked_ref, normed_ref, packed_ref, w_qkv_ref, w_out_ref, w_query_ref, sems) = refs
+    own_rows, width = resid_ref.shape
     steps = own_rows // chunk
     span = groups * chunk
     lanes_two = 2 * head_size
+    group_width = heads_here * head_size
+    if w_query_hbm.shape[1] != group_width:
+        w_query_hbm = w_query_hbm.at[:, pl.ds(pl.multiple_of(me_ref[1] * group_width, group_width), group_width)]
+    copies = [pltpu.make_async_copy(w_qkv_hbm.at[:, pl.ds(part * width, width)], w_qkv_ref.at[part], sems.at[part])
+              for part in range(3)]
+    copies.append(pltpu.make_async_copy(w_out_hbm, w_out_ref, sems.at[3]))
+    copies.append(pltpu.make_async_copy(w_query_hbm, w_query_ref, sems.at[4]))
+    for copy in copies:
+        copy.start()
+
+    def cells_of(group, step):
+        cells = cell_refs[group][pl.ds(step * (chunk // cols), chunk // cols)].astype(jnp.float32)
+        return cells.reshape(chunk, width)
+
     for step in range(steps):
         for group in range(groups):
-            cells = cell_refs[group][pl.ds(step * chunk, chunk), :].astype(jnp.float32)
+            cells = cells_of(group, step)
             normed_ref[pl.ds(step * span + group * chunk, chunk), :] = rms_scale(cells, gain_col_ref[...]).astype(jnp.bfloat16)
     for part in range(3):
-        packed_ref[part] = dot_rows(normed_ref[...], w_qkv_ref[:, pl.ds(part * width, width)]).astype(jnp.bfloat16)
+        copies[part].wait()
+        packed_ref[part] = dot_rows(normed_ref[...], w_qkv_ref[part]).astype(jnp.bfloat16)
     stacked = heads * span
     same_row = iota((stacked, span), 0) % chunk // cols == iota((stacked, span), 1) % chunk // cols
     lane_low = iota((span, lanes_two), 1) < head_size
@@ -138,11 +153,12 @@
             start = 2 * pair * span
             mixed = dot_rows(weights[start:start + 2 * span], packed_ref[2, rows, lanes])
             normed_ref[rows, lanes] = jnp.where(lane_low, mixed[:span], mixed[span:]).astype(jnp.bfloat16)
+    copies[3].wait()
     delta = dot_rows(normed_ref[...], w_out_ref[...])
     for step in range(steps):
         for group in range(groups):
             start = step * span + group * chunk
-            resid = cell_refs[group][pl.ds(step * chunk, chunk), :].astype(jnp.float32) + delta[start:start + chunk]
+            resid = cells_of(group, step) + delta[start:start + chunk]
             if group == 0:
                 resid_ref[pl.ds(step * chunk, chunk), :] = resid
             normed_ref[pl.ds(start, chunk), :] = rms_scale(resid, gain_tile_ref[...]).astype(jnp.bfloat16)
@@ -162,12 +178,8 @@
     row_of = cell // span * (chunk // cols) + cell % chunk // cols
     spread = (row_of == iota((total, shut.shape[0]), 1)).astype(jnp.bfloat16)
     bias = dot_rows(spread, shut) * BIG
-    group_width = heads_here * head_size
-    if w_query_ref.shape[1] == group_width:
-        w_query = w_query_ref[...]
-    else:
-        w_query = w_query_ref[:, pl.ds(pl.multiple_of(me_ref[1] * group_width, group_width), group_width)]
-    asked = dot_rows(normed_ref[...], w_query).astype(jnp.bfloat16).astype(jnp.float32) * scale
+    copies[4].wait()
+    asked = dot_rows(normed_ref[...], w_query_ref[...]).astype(jnp.bfloat16).astype(jnp.float32) * scale
     low = iota((total, lanes_two), 1) < head_size
     for head in range(heads_here):
         if heads_here % 2 == 0:
@@ -177,39 +189,47 @@
         else:
             one = asked[:, head * head_size:(head + 1) * head_size]
             query = jnp.concatenate([one, bias[:, head_size:]], axis=1)
-        asked_ref[head] = query.astype(jnp.bfloat16)
+        query = query.astype(jnp.bfloat16)
+        for step in range(steps):
+            for group in range(groups):
+                start = step * span + group * chunk
+                asked_ref[head, pl.ds(group * own_rows + step * chunk, chunk), :] = query[start:start + chunk]
 
 
 def front(cells, ids, me, key_mask, gain_col, w_qkv, w_out, gain_tile, w_query, heads, head_size, cols,
           heads_here, tiles_here, row_size, paired):
     groups = len(cells)
-    own_rows, width = cells[0].shape
+    width = cells[0].shape[2]
+    own_rows = cells[0].shape[0] * cols
     total = groups * own_rows
+    weights = [(3, width, width), (width, width), (width, heads_here * head_size)]
     return pl.pallas_call(
         functools.partial(front_kernel, groups, heads, head_size, ROW_GROUP * cols, cols, heads_here, tiles_here, row_size, paired),
         out_shape=(jax.ShapeDtypeStruct((own_rows, width), jnp.float32),
                    jax.ShapeDtypeStruct((heads_here, total, 2 * head_size), jnp.bfloat16)),
-        in_specs=[VMEM] * groups + [SMEM, SMEM] + [VMEM] * 6,
+        in_specs=[VMEM] * groups + [SMEM, SMEM] + [VMEM] * 3 + [HBM] * 3,
         out_specs=(VMEM, VMEM),
-        scratch_shapes=[pltpu.VMEM((total, width), jnp.bfloat16), pltpu.VMEM((3, total, width), jnp.bfloat16)],
+        scratch_shapes=[pltpu.VMEM((total, width), jnp.bfloat16), pltpu.VMEM((3, total, width), jnp.bfloat16)]
+        + [pltpu.VMEM(shape, jnp.bfloat16) for shape in weights] + [pltpu.SemaphoreType.DMA((5,))],
         compiler_params=params(total),
         cost_estimate=pl.CostEstimate(flops=2 * total * width * 5 * width, bytes_accessed=4 * MIB,
                                       transcendentals=total * heads * 128),
         name="front",
-    )(*cells, ids, me, key_mask.T, gain_col.reshape(1, width), w_qkv, w_out, gain_tile.reshape(1, width), w_query)
-
-
-def weigh(query, tile_refs, head, first_slot):
-    tiles = jnp.concatenate([ref[:, head] for ref in tile_refs], axis=0)
-    slots, keys, lanes = tiles.shape
-    half = lanes // 2
-    lane = iota(tiles.shape, 2)
-    marks = (lane == iota(tiles.shape, 0) + (half + first_slot)).astype(tiles.dtype)
-    key_part = jnp.where(lane < half, tiles, marks).reshape(slots * keys, lanes)
-    val_part = jnp.where(lane < half, jnp.ones_like(tiles), tiles).reshape(slots * keys, lanes)
-    scores = dot_lanes(query, key_part)
+    )(*cells, ids, me, key_mask.T, gain_col.reshape(1, width), gain_tile.reshape(1, width), w_qkv, w_out, w_query)
+
+
+def weigh(query, tile_refs, head, slots):
+    key_parts, val_parts = [], []
+    for ref, slot in zip(tile_refs, slots):
+        tiles = ref[:, head]
+        count, keys, lanes = tiles.shape
+        lane = iota(tiles.shape, 2)
+        marks = (lane == iota(tiles.shape, 0) + (lanes // 2 + slot)).astype(tiles.dtype)
+        key_parts.append(jnp.where(lane < lanes // 2, tiles, marks).reshape(count * keys, lanes))
+        val_parts.append(jnp.where(lane < lanes // 2, jnp.ones_like(tiles), tiles).reshape(count * keys, lanes))
+    scores = dot_lanes(query, jnp.concatenate(key_parts, axis=0))
     top = jnp.max(scores, axis=1, keepdims=True)
-    return top, dot_rows(jnp.exp(scores - top).astype(jnp.bfloat16), val_part)
+    return top, dot_rows(jnp.exp(scores - top).astype(jnp.bfloat16), jnp.concatenate(val_parts, axis=0))
 
 
 def attention_cost(asked, tiles):
@@ -218,23 +238,23 @@
     return pl.CostEstimate(flops=4 * rows * heads * keys * lanes, bytes_accessed=4 * MIB, transcendentals=rows * heads * keys)
 
 
-def first_kernel(count, block, asked_ref, *refs):
-    tile_refs, (sums_ref, tops_ref) = refs[:count], refs[count:]
+def first_kernel(slots, block, asked_ref, *refs):
+    tile_refs, (sums_ref, tops_ref) = refs[:len(slots)], refs[len(slots):]
     heads, rows_all, lanes = asked_ref.shape
     lane = iota((block, lanes), 1)
     for step in range(rows_all // block):
         rows = pl.ds(step * block, block)
         tops = jnp.zeros((block, lanes), jnp.float32)
         for head in range(heads):
-            top, sums_ref[head, rows, :] = weigh(asked_ref[head, rows, :], tile_refs, head, 0)
+            top, sums_ref[head, rows, :] = weigh(asked_ref[head, rows, :], tile_refs, head, slots)
             tops = jnp.where(lane == head, top, tops)
         tops_ref[rows, :] = tops
 
 
-def first_tiles(asked, tiles):
+def first_tiles(asked, tiles, slots, own_rows):
     heads, rows, lanes = asked.shape
     return pl.pallas_call(
-        functools.partial(first_kernel, len(tiles), rows if rows <= 512 else 128),
+        functools.partial(first_kernel, slots, rows if rows <= 512 else own_rows),
         out_shape=(jax.ShapeDtypeStruct((heads, rows, lanes), jnp.float32), jax.ShapeDtypeStruct((rows, lanes), jnp.float32)),
         in_specs=[VMEM] * (1 + len(tiles)),
         out_specs=(VMEM, VMEM),
@@ -244,50 +264,64 @@
     )(asked, *tiles)
 
 
-def last_kernel(groups, count, first_slot, chunk, asked_ref, sums_ref, tops_ref, *refs):
-    tile_refs, out_refs = refs[:count], refs[count:]
-    heads, rows_all, lanes = asked_ref.shape
+def last_kernel(slots, groups, asked_ref, sums_ref, tops_ref, *refs):
+    tile_refs, out_refs = refs[:len(slots)], refs[-len(groups):]
+    heads, lanes = asked_ref.shape[0], asked_ref.shape[2]
+    block = out_refs[0].shape[0]
     half = lanes // 2
-    span = groups * chunk
-    block = rows_all if rows_all <= 512 else span
     lane_low = iota((block, lanes), 1) < half
-
-    def put(step, values, lane, lane_count):
-        for part in range(block // span):
-            for group in range(groups):
-                start = part * span + group * chunk
-                place = pl.ds(step * (block // groups) + part * chunk, chunk)
-                out_refs[group][place, pl.ds(lane, lane_count)] = values[start:start + chunk]
-
-    for step in range(rows_all // block):
-        rows = pl.ds(step * block, block)
+    for group, out_ref in zip(groups, out_refs):
+        rows = pl.ds(group * block, block)
         low = None
         for head in range(heads):
-            top, sums = weigh(asked_ref[head, rows, :], tile_refs, head, first_slot)
+            top, sums = weigh(asked_ref[head, rows, :], tile_refs, head, slots)
             old_top = tops_ref[rows, head:head + 1]
             new_top = jnp.maximum(top, old_top)
             sums = sums_ref[head, rows, :] * jnp.exp(old_top - new_top) + sums * jnp.exp(top - new_top)
             turned = pltpu.roll(sums, half, 1)
             if head % 2:
-                put(step, jnp.where(lane_low, low, sums / turned).astype(jnp.bfloat16), head // 2 * lanes, lanes)
+                out_ref[:, pl.ds(head // 2 * lanes, lanes)] = jnp.where(lane_low, low, sums / turned).astype(jnp.bfloat16)
             elif head + 1 < heads:
                 low = turned / sums
             else:
-                put(step, (turned / sums)[:, :half].astype(jnp.bfloat16), head * half, half)
-
-
-def last_tiles(asked, sums, tops, tiles, first_slot, groups, cols):
+                out_ref[:, pl.ds(head * half, half)] = (turned / sums)[:, :half].astype(jnp.bfloat16)
+
+
+def last_tiles(asked, sums, tops, tiles, slots, groups, own_rows, after):
     heads, rows, lanes = asked.shape
-    out = jax.ShapeDtypeStruct((rows // groups, heads * lanes // 2), jnp.bfloat16)
-    return pl.pallas_call(
-        functools.partial(last_kernel, groups, len(tiles), first_slot, ROW_GROUP * cols),
-        out_shape=(out,) * groups,
-        in_specs=[VMEM] * (3 + len(tiles)),
-        out_specs=(VMEM,) * groups,
+    out = jax.ShapeDtypeStruct((own_rows, heads * lanes // 2), jnp.bfloat16)
+    return pl.pallas_call(
+        functools.partial(last_kernel, slots, groups),
+        out_shape=(out,) * len(groups),
+        in_specs=[VMEM] * (3 + len(tiles)) + [ANY] * len(after),
+        out_specs=(VMEM,) * len(groups),
         compiler_params=params(rows),
-        cost_estimate=attention_cost(asked, tiles),
+        cost_estimate=attention_cost(asked[:, :own_rows * len(groups)], tiles),
         name="last_tiles",
-    )(asked, sums, tops, *tiles)
+    )(asked, sums, tops, *tiles, *after)
+
+
+def finish_kernel(me_ref, weight_ref, resid_ref, *refs):
+    answer_refs, out_ref = refs[:-1], refs[-1]
+    group_width = answer_refs[0].shape[1]
+    final = resid_ref[...]
+    for step, answer_ref in enumerate(answer_refs):
+        group = lax.rem(me_ref[1] - step + len(answer_refs), len(answer_refs))
+        rows = pl.ds(pl.multiple_of(group * group_width, group_width), group_width)
+        final = final + dot_rows(answer_ref[...], weight_ref[rows, :])
+    out_ref[...] = final.reshape(out_ref.shape).astype(out_ref.dtype)
+
+
+def finish(me, weight, residual, answers, shape):
+    return pl.pallas_call(
+        finish_kernel,
+        out_shape=jax.ShapeDtypeStruct(shape, jnp.bfloat16),
+        in_specs=[SMEM, VMEM, VMEM] + [VMEM] * len(answers),
+        out_specs=VMEM,
+        compiler_params=params(0),
+        cost_estimate=pl.CostEstimate(flops=2 * residual.size * weight.shape[0], bytes_accessed=MIB, transcendentals=0),
+        name="finish",
+    )(me, weight, residual, *answers)
 
 
 def turn(size, step):
@@ -315,35 +349,33 @@
     mirrored = lax.ppermute(heads_first, "rows", turn(row_size, half))
     asked_by = swap(request(tile_ids, me, tiles_here, row_size))
 
-    cells = [fact_cells.reshape(rows * cols, width)]
+    cells = [fact_cells]
     for step in range(1, col_size):
-        cells.append(lax.ppermute(cells[0], "cols", turn(col_size, -step)))
+        cells.append(lax.ppermute(fact_cells, "cols", turn(col_size, -step)))
+
+    order = [0] + sorted(range(1, half), key=lambda step: (-(step & half // 2), step & 1, -step))
+    slots = order if paired else [0]
 
     def spread(tiles, which, after):
         if not paired:
             return [swap(pick(tiles, asked_by, which, after))]
-        picked = pick_each(tiles, asked_by, which, me, after)
-        arrived = list(picked[:1]) + [None] * (half - 1)
-        for step in sorted(range(1, half), key=lambda step: (-(step & half // 2), step & 1, -step)):
-            pairs = [(row, row ^ step) for row in range(row_size)]
-            arrived[step] = lax.ppermute(picked[step], "rows", pairs)
-        return arrived
-
-    near = spread(heads_first, 0, cells[:1])
+        picked = pick_each(tiles, asked_by, which, me, order, after)
+        return [tile if step == 0 else lax.ppermute(tile, "rows", [(row, row ^ step) for row in range(row_size)])
+                for step, tile in zip(order, picked)]
+
+    near = spread(heads_first, 0, cells[1:])
     if group_width % 128:
         w_query = lax.dynamic_slice_in_dim(w_query, col_me * group_width, group_width, 1)
+    w_qkv, w_col_out, w_query = [pltpu.with_memory_space_constraint(weight, pltpu.HBM) for weight in (w_qkv, w_col_out, w_query)]
     residual, asked = front(cells, tile_ids, me, key_mask, gain_col, w_qkv, w_col_out, gain_tile, w_query,
                             heads_all, head_size, cols, heads_here, tiles_here, row_size, paired)
     far = spread(mirrored, 1, near + [asked])
-    sums, tops = first_tiles(asked, near)
-    answers = last_tiles(asked, sums, tops, far, half, col_size, cols)
-
-    final = residual
-    for step in range(col_size):
-        answer = lax.ppermute(answers[step], "cols", turn(col_size, step)) if step else answers[0]
-        start = (col_me - step) % col_size * group_width
-        final = final + dot_rows(answer, lax.dynamic_slice_in_dim(w_tile_out, start, group_width, 0))
-    return final.astype(jnp.bfloat16).reshape(rows, cols, width)
+    sums, tops = first_tiles(asked, near, slots, rows * cols)
+    far_slots = [half + slot for slot in slots]
+    others = last_tiles(asked, sums, tops, far, far_slots, list(range(1, col_size)), rows * cols, [])
+    own = last_tiles(asked, sums, tops, far, far_slots, [0], rows * cols, others[:1])
+    answers = list(own) + [lax.ppermute(other, "cols", turn(col_size, step + 1)) for step, other in enumerate(others)]
+    return finish(me, w_tile_out, residual, answers, fact_cells.shape)
 
 
 def solution(mesh):

time: 67.6 us -> 68 us (level)
  local copies, waits for them, and re-layouts: 9.57 us -> 1.86 us
  waiting for transfers between devices: 15.8 us -> 21.9 us
  Pallas kernels: 12.4 us -> 15.2 us
    ppermute x16, waiting for transfers between devices: 15.8 us -> 21.9 us  [the longest x14 20.5 us: spread(): lax.ppermute(tile, 'rows', [(row, row ^ step) for row in range(row_size)])]
    unnamed x25 -> x15, local copies, waits for them, and re-layouts: 7.86 us -> 1.86 us
    reshape x2 -> x0, local copies, waits for them, and re-layouts: 1.71 us -> none  [the longest x1 0.98 us: shards(): cells = [fact_cells.reshape(rows * cols, width)]]
    pallas_call x1, Pallas kernels: 3.69 us -> 5.29 us  [front(): pl.pallas_call(functools.partial(front_kernel, groups, heads, head_size,...]
    pallas_call x4 -> x6, Pallas kernels: 8.05 us -> 9.27 us  [the longest x2 3.74 us: last_tiles(): pl.pallas_call(functools.partial(last_kernel, slots, groups), out_shape=(...]
  transfers between devices with their start and end apart: 17 -> 17, of which waited for: 8 -> 9; matrix products, arithmetic and copies ran while one was open for 2% -> 0% of each run, Pallas kernels for 11% -> 16%
where the time goes in v10:
time: 68 us; the launch traced here: 67.8 us
  waiting for transfers between devices  21.9 us (32%)
  starting transfers between devices  20.2 us (30%)
  Pallas kernels  15.2 us (22%)
  blocking collectives  8.45 us (12%)
  local copies, waits for them, and re-layouts  1.86 us (3%)
    ppermute x14, waiting for transfers between devices, spread(): lax.ppermute(tile, 'rows', [(row, row ^ step) for row in range(row_size)])  20.5 us
    ppermute x14, starting transfers between devices, spread(): lax.ppermute(tile, 'rows', [(row, row ^ step) for row in range(row_size)])  13 us
    all_to_all x1, blocking collectives, swap(): lax.all_to_all(value, 'rows', split_axis=0, concat_axis=0, tiled=True, ax...  8.45 us
    pallas_call x1, Pallas kernels, front(): pl.pallas_call(functools.partial(front_kernel, groups, heads, head_size,...  5.29 us
    ppermute x1, starting transfers between devices, shards(): mirrored = lax.ppermute(heads_first, 'rows', turn(row_size, half))  4.12 us
    pallas_call x2, Pallas kernels, last_tiles(): pl.pallas_call(functools.partial(last_kernel, slots, groups), out_shape=(...  3.74 us
    pallas_call x1, Pallas kernels, first_tiles(): pl.pallas_call(functools.partial(first_kernel, slots, rows if rows <= 512...  2.5 us
    unnamed x15, local copies, waits for them, and re-layouts  1.86 us
  transfers between devices with their start and end apart: 17, of which 9 were waited for; matrix products, arithmetic and copies ran while one was open for 0% of the time, Pallas kernels for 16%

profile of v10, /device:TPU:0, one launch (start us, length us, event | category | flops | bytes accessed | tf_op | source)
XLA Modules:
  0.0 67.8 jit_solution(9171423634047234017)
XLA Ops:
  0.0 1.2 %copy.13 = bf16[4,128,4,128]{3,1,2,0:T(8,128)(2,1)S(1)} copy(bf16[4,128,4,128]{3,2,1,0:T(4,128)(2,1)} %param.17) | data formatting | bytes 1048576 | tf_op args[7]
  1.2 4.1 %collective-permute-start.8 = (bf16[4,4,128,128]{3,2,1,0:T(8,128)(2,1)S(1)}, bf16[4,4,128,128]{3,2,1,0:T(8,128)(2,1)S(1)}, u32[]{:S(2)}, u32[]{:S(2)}) collective-permute-start(bf16[4,4,128,128]{3,2,1,0:T(8,128)(2,1)S(1)} %bitcast.8), channel_id=1, source_target_pairs={{0,16},{2,18},{4,20},{6,22},{8,24},{10,26},{12,28},{14,30},{16,0},... | collective-permute-start | bytes 1572872 | tf_op jit(solution)/shard_map/ppermute | solution.py:349
  5.3 1.5 %collective-permute-start = (bf16[48,4,512]{2,1,0:T(4,128)(2,1)}, bf16[48,4,512]{2,1,0:T(4,128)(2,1)S(1)}, u32[]{:S(2)}, u32[]{:S(2)}) collective-permute-start(bf16[48,4,512]{2,1,0:T(4,128)(2,1)} %refs_0_.1), channel_id=1, source_target_pairs={{0,1},{1,0},{2,3},{3,2},{4,5},{5,4},{6,7},{7,6},{8,9},{9,8},{10,11... | collective-permute-start | bytes 589832 | tf_op jit(solution)/shard_map/ppermute | solution.py:354
  8.2 8.4 %all_to_all.5.wanted_ref = s32[8,2,128]{2,1,0:T(2,128)S(1)} all-to-all(s32[8,2,128]{2,1,0:T(2,128)S(1)} %request.1), channel_id=1, replica_groups={{0,2,4,6,8,10,12,14},{16,18,20,22,24,26,28,30},{1,3,5,7,9,11,13,15},{17..., dimensions={0} | all-to-all | bytes 16384 | tf_op jit(solution)/shard_map/all_to_all | solution.py:346
  17.4 3.5 %collective-permute-start.1 = (bf16[1,4,128,128]{3,2,1,0:T(8,128)(2,1)S(1)}, bf16[1,4,128,128]{3,2,1,0:T(8,128)(2,1)S(1)}, u32[]{:S(2)}, u32[]{:S(2)}) collective-permute-start(bf16[1,4,128,128]{3,2,1,0:T(8,128)(2,1)S(1)} %get-tuple-element.28), channel_id=1, source_target_pairs={{0,12},{2,14},{4,8},{6,10},{8,4},{10,6},{12,0},{14,2},{16,28},{18,... | collective-permute-start | bytes 393224 | tf_op jit(solution)/shard_map/ppermute | solution.py:363
  20.9 1.7 %collective-permute-start.3 = (bf16[1,4,128,128]{3,2,1,0:T(8,128)(2,1)S(1)}, bf16[1,4,128,128]{3,2,1,0:T(8,128)(2,1)S(1)}, u32[]{:S(2)}, u32[]{:S(2)}) collective-permute-start(bf16[1,4,128,128]{3,2,1,0:T(8,128)(2,1)S(1)} %get-tuple-element.30), channel_id=1, source_target_pairs={{0,14},{2,12},{4,10},{6,8},{8,6},{10,4},{12,2},{14,0},{16,30},{18,... | collective-permute-start | bytes 393224 | tf_op jit(solution)/shard_map/ppermute | solution.py:363
  22.6 0.9 %collective-permute-start.4 = (bf16[1,4,128,128]{3,2,1,0:T(8,128)(2,1)S(1)}, bf16[1,4,128,128]{3,2,1,0:T(8,128)(2,1)S(1)}, u32[]{:S(2)}, u32[]{:S(2)}) collective-permute-start(bf16[1,4,128,128]{3,2,1,0:T(8,128)(2,1)S(1)} %get-tuple-element.31), channel_id=1, source_target_pairs={{0,10},{2,8},{4,14},{6,12},{8,2},{10,0},{12,6},{14,4},{16,26},{18,... | collective-permute-start | bytes 393224 | tf_op jit(solution)/shard_map/ppermute | solution.py:363
  23.5 8.8 %collective-permute-done.1.refs_1_ = bf16[1,4,128,128]{3,2,1,0:T(8,128)(2,1)S(1)} collective-permute-done((bf16[1,4,128,128]{3,2,1,0:T(8,128)(2,1)S(1)}, bf16[1,4,128,128]{3,2,1,0:T(8,128)(2,1)S(1)}, u32[]{:S(2)}, u32[]{:S(2)}) %collective-permute-start.1) | collective-permute-done | bytes 131104 | tf_op jit(solution)/shard_map/ppermute | solution.py:363
  32.8 1.3 %collective-permute-done.2.refs_2_ = bf16[1,4,128,128]{3,2,1,0:T(8,128)(2,1)S(1)} collective-permute-done((bf16[1,4,128,128]{3,2,1,0:T(8,128)(2,1)S(1)}, bf16[1,4,128,128]{3,2,1,0:T(8,128)(2,1)S(1)}, u32[]{:S(2)}, u32[]{:S(2)}) %collective-permute-start.2) | collective-permute-done | bytes 131104 | tf_op jit(solution)/shard_map/ppermute | solution.py:363
  34.2 1.1 %collective-permute-start.6 = (bf16[1,4,128,128]{3,2,1,0:T(8,128)(2,1)S(1)}, bf16[1,4,128,128]{3,2,1,0:T(8,128)(2,1)S(1)}, u32[]{:S(2)}, u32[]{:S(2)}) collective-permute-start(bf16[1,4,128,128]{3,2,1,0:T(8,128)(2,1)S(1)} %get-tuple-element.33), channel_id=1, source_target_pairs={{0,6},{2,4},{4,2},{6,0},{8,14},{10,12},{12,10},{14,8},{16,22},{18,... | collective-permute-start | bytes 393224 | tf_op jit(solution)/shard_map/ppermute | solution.py:363
  35.3 2.6 %collective-permute-done.3.refs_3_ = bf16[1,4,128,128]{3,2,1,0:T(8,128)(2,1)S(1)} collective-permute-done((bf16[1,4,128,128]{3,2,1,0:T(8,128)(2,1)S(1)}, bf16[1,4,128,128]{3,2,1,0:T(8,128)(2,1)S(1)}, u32[]{:S(2)}, u32[]{:S(2)}) %collective-permute-start.3) | collective-permute-done | bytes 131104 | tf_op jit(solution)/shard_map/ppermute | solution.py:363
  38.0 5.3 %front.1 = (f32[192,512]{1,0:T(8,128)S(1)}, bf16[4,384,128]{2,1,0:T(8,128)(2,1)S(1)}) custom-call(bf16[48,4,512]{2,1,0:T(4,128)(2,1)S(1)} %copy-done.3, bf16[48,4,512]{2,1,0:T(4,128)(2,1)S(1)} %collective-permute-done.refs_1_.refs_0_, s32[1,12]{1,0:T(1,128)S(1)} %copy-done.2, s32[2]{0:T(128)S(1)} %pad_add_fusion.refs_3_.me_ref, s32[12,48]{1,0:T(8,128)S(1)} %bitcast.10, ...), custom_call_target="tpu_custom_call" | custom-call | flops 1006632960 | bytes 4194304 | tf_op jit(solution)/shard_map/front/pallas_call | solution.py:206
  44.2 1.9 %collective-permute-start.10 = (bf16[1,4,128,128]{3,2,1,0:T(8,128)(2,1)S(1)}, bf16[1,4,128,128]{3,2,1,0:T(8,128)(2,1)S(1)}, u32[]{:S(2)}, u32[]{:S(2)}) collective-permute-start(bf16[1,4,128,128]{3,2,1,0:T(8,128)(2,1)S(1)} %get-tuple-element.39), channel_id=1, source_target_pairs={{0,8},{2,10},{4,12},{6,14},{8,0},{10,2},{12,4},{14,6},{16,24},{18,... | collective-permute-start | bytes 393224 | tf_op jit(solution)/shard_map/ppermute | solution.py:363
  46.9 2.0 %collective-permute-start.12 = (bf16[1,4,128,128]{3,2,1,0:T(8,128)(2,1)S(1)}, bf16[1,4,128,128]{3,2,1,0:T(8,128)(2,1)S(1)}, u32[]{:S(2)}, u32[]{:S(2)}) collective-permute-start(bf16[1,4,128,128]{3,2,1,0:T(8,128)(2,1)S(1)} %get-tuple-element.41), channel_id=1, source_target_pairs={{0,10},{2,8},{4,14},{6,12},{8,2},{10,0},{12,6},{14,4},{16,26},{18,... | collective-permute-start | bytes 393224 | tf_op jit(solution)/shard_map/ppermute | solution.py:363
  49.3 2.1 %collective-permute-done.9.refs_1_ = bf16[1,4,128,128]{3,2,1,0:T(8,128)(2,1)S(1)} collective-permute-done((bf16[1,4,128,128]{3,2,1,0:T(8,128)(2,1)S(1)}, bf16[1,4,128,128]{3,2,1,0:T(8,128)(2,1)S(1)}, u32[]{:S(2)}, u32[]{:S(2)}) %collective-permute-start.9) | collective-permute-done | bytes 131104 | tf_op jit(solution)/shard_map/ppermute | solution.py:363
  51.4 1.8 %collective-permute-done.10.refs_2_ = bf16[1,4,128,128]{3,2,1,0:T(8,128)(2,1)S(1)} collective-permute-done((bf16[1,4,128,128]{3,2,1,0:T(8,128)(2,1)S(1)}, bf16[1,4,128,128]{3,2,1,0:T(8,128)(2,1)S(1)}, u32[]{:S(2)}, u32[]{:S(2)}) %collective-permute-start.10) | collective-permute-done | bytes 131104 | tf_op jit(solution)/shard_map/ppermute | solution.py:363
  53.2 2.5 %first_tiles.1 = (f32[4,384,128]{2,1,0:T(8,128)S(1)}, f32[384,128]{1,0:T(8,128)S(1)}) custom-call(bf16[4,384,128]{2,1,0:T(8,128)(2,1)S(1)} %get-tuple-element.26.asked_ref.refs_8_, bf16[1,4,128,128]{3,2,1,0:T(8,128)(2,1)S(1)} %get-tuple-element.27.refs_0_, bf16[1,4,128,128]{3,2,1,0:T(8,128)(2,1)S(1)} %collective-permute-done.1.refs_1_, ...), custom_call_target="tpu_custom_call" | custom-call | flops 805306368 | bytes 4194304 | tf_op jit(solution)/shard_map/first_tiles/pallas_call | solution.py:256
  56.2 1.8 %collective-permute-done.12.refs_4_ = bf16[1,4,128,128]{3,2,1,0:T(8,128)(2,1)S(1)} collective-permute-done((bf16[1,4,128,128]{3,2,1,0:T(8,128)(2,1)S(1)}, bf16[1,4,128,128]{3,2,1,0:T(8,128)(2,1)S(1)}, u32[]{:S(2)}, u32[]{:S(2)}) %collective-permute-start.12) | collective-permute-done | bytes 131104 | tf_op jit(solution)/shard_map/ppermute | solution.py:363
  58.0 1.6 %collective-permute-done.14.refs_6_ = bf16[1,4,128,128]{3,2,1,0:T(8,128)(2,1)S(1)} collective-permute-done((bf16[1,4,128,128]{3,2,1,0:T(8,128)(2,1)S(1)}, bf16[1,4,128,128]{3,2,1,0:T(8,128)(2,1)S(1)}, u32[]{:S(2)}, u32[]{:S(2)}) %collective-permute-start.14) | collective-permute-done | bytes 131104 | tf_op jit(solution)/shard_map/ppermute | solution.py:363
  59.5 1.9 %last_tiles.2.refs_8_ = bf16[192,256]{1,0:T(8,128)(2,1)S(1)} custom-call(bf16[4,384,128]{2,1,0:T(8,128)(2,1)S(1)} %get-tuple-element.26.asked_ref.refs_8_, f32[4,384,128]{2,1,0:T(8,128)S(1)} %get-tuple-element.35.sums_ref, f32[384,128]{1,0:T(8,128)S(1)} %get-tuple-element.36.tops_ref, bf16[1,4,128,128]{3,2,1,0:T(8,128)(2,1)S(1)} %get-tuple-element.37.refs_0_, ...), custom_call_target="tpu_custom_call" | custom-call | flops 402653184 | bytes 4194304 | tf_op jit(solution)/shard_map/last_tiles/pallas_call | solution.py:293
  61.4 1.6 %collective-permute-start.16 = (bf16[192,256]{1,0:T(8,128)(2,1)S(1)}, bf16[192,256]{1,0:T(8,128)(2,1)S(1)}, u32[]{:S(2)}, u32[]{:S(2)}) collective-permute-start(bf16[192,256]{1,0:T(8,128)(2,1)S(1)} %last_tiles.2.refs_8_), channel_id=1, source_target_pairs={{0,1},{1,0},{2,3},{3,2},{4,5},{5,4},{6,7},{7,6},{8,9},{9,8},{10,11... | collective-permute-start | bytes 294920 | tf_op jit(solution)/shard_map/ppermute | solution.py:377
  63.0 1.9 %last_tiles.3.refs_0_ = bf16[192,256]{1,0:T(8,128)(2,1)S(1)} custom-call(bf16[4,384,128]{2,1,0:T(8,128)(2,1)S(1)} %get-tuple-element.26.asked_ref.refs_8_, f32[4,384,128]{2,1,0:T(8,128)S(1)} %get-tuple-element.35.sums_ref, f32[384,128]{1,0:T(8,128)S(1)} %get-tuple-element.36.tops_ref, bf16[1,4,128,128]{3,2,1,0:T(8,128)(2,1)S(1)} %get-tuple-element.37.refs_0_, ...), custom_call_target="tpu_custom_call" | custom-call | flops 402653184 | bytes 4194304 | tf_op jit(solution)/shard_map/last_tiles/pallas_call | solution.py:293
  64.9 1.4 %collective-permute-done.16.refs_1_ = bf16[192,256]{1,0:T(8,128)(2,1)S(1)} collective-permute-done((bf16[192,256]{1,0:T(8,128)(2,1)S(1)}, bf16[192,256]{1,0:T(8,128)(2,1)S(1)}, u32[]{:S(2)}, u32[]{:S(2)}) %collective-permute-start.16) | collective-permute-done | bytes 98336 | tf_op jit(solution)/shard_map/ppermute | solution.py:377
  66.3 1.5 %finish.1 = bf16[48,4,512]{2,1,0:T(4,128)(2,1)} custom-call(s32[2]{0:T(128)S(1)} %pad_add_fusion.refs_3_.me_ref, bf16[512,512]{1,0:T(8,128)(2,1)S(1)} %copy-done, f32[192,512]{1,0:T(8,128)S(1)} %get-tuple-element.25.resid_ref, bf16[192,256]{1,0:T(8,128)(2,1)S(1)} %last_tiles.3.refs_0_, bf16[192,256]{1,0:T(8,128)(2,1)S(1)} %collective-permute-done.16.refs_1_), custom_call_target="tpu_custom_call" | custom-call | flops 100663296 | bytes 1048576 | tf_op jit(solution)/shard_map/finish/pallas_call | solution.py:316
  (35 shorter events, 5.4 us)
Async XLA Ops:
  0.0 38.0 %copy-start.3 = (bf16[48,4,512]{2,1,0:T(4,128)(2,1)S(1)}, bf16[48,4,512]{2,1,0:T(4,128)(2,1)}, u32[]{:S(2)}) copy-start(bf16[48,4,512]{2,1,0:T(4,128)(2,1)} %refs_0_.1) | copy-start | bytes 589828
  0.0 38.0 %copy-start.2 = (s32[1,12]{1,0:T(1,128)S(1)}, s32[1,12]{1,0:T(1,128)}, u32[]{:S(2)}) copy-start(s32[1,12]{1,0:T(1,128)} %ids_ref.1) | copy-start | bytes 148
  0.0 38.0 %copy-start.4 = (s32[48,12]{0,1:T(8,128)S(1)}, s32[48,12]{0,1:T(8,128)}, u32[]{:S(2)}) copy-start(s32[48,12]{0,1:T(8,128)} %param.19) | copy-start | bytes 6916
  0.0 38.0 %copy-start.6 = (f32[512]{0:T(512)S(1)}, f32[512]{0:T(512)}, u32[]{:S(2)}) copy-start(f32[512]{0:T(512)} %param.14) | copy-start | bytes 6148
  0.0 38.0 %copy-start.5 = (f32[512]{0:T(512)S(1)}, f32[512]{0:T(512)}, u32[]{:S(2)}) copy-start(f32[512]{0:T(512)} %param.11) | copy-start | bytes 6148
  1.2 42.1 %collective-permute-start.8 = (bf16[4,4,128,128]{3,2,1,0:T(8,128)(2,1)S(1)}, bf16[4,4,128,128]{3,2,1,0:T(8,128)(2,1)S(1)}, u32[]{:S(2)}, u32[]{:S(2)}) collective-permute-start(bf16[4,4,128,128]{3,2,1,0:T(8,128)(2,1)S(1)} %bitcast.8), channel_id=1, source_target_pairs={{0,16},{2,18},{4,20},{6,22},{8,24},{10,26},{12,28},{14,30},{16,0},... | collective-permute-start | bytes 1572872 | tf_op jit(solution)/shard_map/ppermute | solution.py:349
  5.3 11.3 %collective-permute-start = (bf16[48,4,512]{2,1,0:T(4,128)(2,1)}, bf16[48,4,512]{2,1,0:T(4,128)(2,1)S(1)}, u32[]{:S(2)}, u32[]{:S(2)}) collective-permute-start(bf16[48,4,512]{2,1,0:T(4,128)(2,1)} %refs_0_.1), channel_id=1, source_target_pairs={{0,1},{1,0},{2,3},{3,2},{4,5},{5,4},{6,7},{7,6},{8,9},{9,8},{10,11... | collective-permute-start | bytes 589832 | tf_op jit(solution)/shard_map/ppermute | solution.py:354
  6.9 0.7 copy-start.1
  17.4 14.9 %collective-permute-start.1 = (bf16[1,4,128,128]{3,2,1,0:T(8,128)(2,1)S(1)}, bf16[1,4,128,128]{3,2,1,0:T(8,128)(2,1)S(1)}, u32[]{:S(2)}, u32[]{:S(2)}) collective-permute-start(bf16[1,4,128,128]{3,2,1,0:T(8,128)(2,1)S(1)} %get-tuple-element.28), channel_id=1, source_target_pairs={{0,12},{2,14},{4,8},{6,10},{8,4},{10,6},{12,0},{14,2},{16,28},{18,... | collective-permute-start | bytes 393224 | tf_op jit(solution)/shard_map/ppermute | solution.py:363
  20.9 13.3 %collective-permute-start.2 = (bf16[1,4,128,128]{3,2,1,0:T(8,128)(2,1)S(1)}, bf16[1,4,128,128]{3,2,1,0:T(8,128)(2,1)S(1)}, u32[]{:S(2)}, u32[]{:S(2)}) collective-permute-start(bf16[1,4,128,128]{3,2,1,0:T(8,128)(2,1)S(1)} %get-tuple-element.29), channel_id=1, source_target_pairs={{0,8},{2,10},{4,12},{6,14},{8,0},{10,2},{12,4},{14,6},{16,24},{18,... | collective-permute-start | bytes 393224 | tf_op jit(solution)/shard_map/ppermute | solution.py:363
  20.9 17.0 %collective-permute-start.3 = (bf16[1,4,128,128]{3,2,1,0:T(8,128)(2,1)S(1)}, bf16[1,4,128,128]{3,2,1,0:T(8,128)(2,1)S(1)}, u32[]{:S(2)}, u32[]{:S(2)}) collective-permute-start(bf16[1,4,128,128]{3,2,1,0:T(8,128)(2,1)S(1)} %get-tuple-element.30), channel_id=1, source_target_pairs={{0,14},{2,12},{4,10},{6,8},{8,6},{10,4},{12,2},{14,0},{16,30},{18,... | collective-permute-start | bytes 393224 | tf_op jit(solution)/shard_map/ppermute | solution.py:363
  22.6 20.7 %collective-permute-start.4 = (bf16[1,4,128,128]{3,2,1,0:T(8,128)(2,1)S(1)}, bf16[1,4,128,128]{3,2,1,0:T(8,128)(2,1)S(1)}, u32[]{:S(2)}, u32[]{:S(2)}) collective-permute-start(bf16[1,4,128,128]{3,2,1,0:T(8,128)(2,1)S(1)} %get-tuple-element.31), channel_id=1, source_target_pairs={{0,10},{2,8},{4,14},{6,12},{8,2},{10,0},{12,6},{14,4},{16,26},{18,... | collective-permute-start | bytes 393224 | tf_op jit(solution)/shard_map/ppermute | solution.py:363
  32.3 11.0 %collective-permute-start.5 = (bf16[1,4,128,128]{3,2,1,0:T(8,128)(2,1)S(1)}, bf16[1,4,128,128]{3,2,1,0:T(8,128)(2,1)S(1)}, u32[]{:S(2)}, u32[]{:S(2)}) collective-permute-start(bf16[1,4,128,128]{3,2,1,0:T(8,128)(2,1)S(1)} %get-tuple-element.32), channel_id=1, source_target_pairs={{0,4},{2,6},{4,0},{6,2},{8,12},{10,14},{12,8},{14,10},{16,20},{18,... | collective-permute-start | bytes 393224 | tf_op jit(solution)/shard_map/ppermute | solution.py:363
  34.2 9.2 %collective-permute-start.6 = (bf16[1,4,128,128]{3,2,1,0:T(8,128)(2,1)S(1)}, bf16[1,4,128,128]{3,2,1,0:T(8,128)(2,1)S(1)}, u32[]{:S(2)}, u32[]{:S(2)}) collective-permute-start(bf16[1,4,128,128]{3,2,1,0:T(8,128)(2,1)S(1)} %get-tuple-element.33), channel_id=1, source_target_pairs={{0,6},{2,4},{4,2},{6,0},{8,14},{10,12},{12,10},{14,8},{16,22},{18,... | collective-permute-start | bytes 393224 | tf_op jit(solution)/shard_map/ppermute | solution.py:363
  37.9 5.4 %collective-permute-start.7 = (bf16[1,4,128,128]{3,2,1,0:T(8,128)(2,1)S(1)}, bf16[1,4,128,128]{3,2,1,0:T(8,128)(2,1)S(1)}, u32[]{:S(2)}, u32[]{:S(2)}) collective-permute-start(bf16[1,4,128,128]{3,2,1,0:T(8,128)(2,1)S(1)} %get-tuple-element.34), channel_id=1, source_target_pairs={{0,2},{2,0},{4,6},{6,4},{8,10},{10,8},{12,14},{14,12},{16,18},{18,... | collective-permute-start | bytes 393224 | tf_op jit(solution)/shard_map/ppermute | solution.py:363
  44.1 7.3 %collective-permute-start.9 = (bf16[1,4,128,128]{3,2,1,0:T(8,128)(2,1)S(1)}, bf16[1,4,128,128]{3,2,1,0:T(8,128)(2,1)S(1)}, u32[]{:S(2)}, u32[]{:S(2)}) collective-permute-start(bf16[1,4,128,128]{3,2,1,0:T(8,128)(2,1)S(1)} %get-tuple-element.38), channel_id=1, source_target_pairs={{0,12},{2,14},{4,8},{6,10},{8,4},{10,6},{12,0},{14,2},{16,28},{18,... | collective-permute-start | bytes 393224 | tf_op jit(solution)/shard_map/ppermute | solution.py:363
  44.2 9.0 %collective-permute-start.10 = (bf16[1,4,128,128]{3,2,1,0:T(8,128)(2,1)S(1)}, bf16[1,4,128,128]{3,2,1,0:T(8,128)(2,1)S(1)}, u32[]{:S(2)}, u32[]{:S(2)}) collective-permute-start(bf16[1,4,128,128]{3,2,1,0:T(8,128)(2,1)S(1)} %get-tuple-element.39), channel_id=1, source_target_pairs={{0,8},{2,10},{4,12},{6,14},{8,0},{10,2},{12,4},{14,6},{16,24},{18,... | collective-permute-start | bytes 393224 | tf_op jit(solution)/shard_map/ppermute | solution.py:363
  46.1 10.1 %collective-permute-start.11 = (bf16[1,4,128,128]{3,2,1,0:T(8,128)(2,1)S(1)}, bf16[1,4,128,128]{3,2,1,0:T(8,128)(2,1)S(1)}, u32[]{:S(2)}, u32[]{:S(2)}) collective-permute-start(bf16[1,4,128,128]{3,2,1,0:T(8,128)(2,1)S(1)} %get-tuple-element.40), channel_id=1, source_target_pairs={{0,14},{2,12},{4,10},{6,8},{8,6},{10,4},{12,2},{14,0},{16,30},{18,... | collective-permute-start | bytes 393224 | tf_op jit(solution)/shard_map/ppermute | solution.py:363
  46.9 11.1 %collective-permute-start.12 = (bf16[1,4,128,128]{3,2,1,0:T(8,128)(2,1)S(1)}, bf16[1,4,128,128]{3,2,1,0:T(8,128)(2,1)S(1)}, u32[]{:S(2)}, u32[]{:S(2)}) collective-permute-start(bf16[1,4,128,128]{3,2,1,0:T(8,128)(2,1)S(1)} %get-tuple-element.41), channel_id=1, source_target_pairs={{0,10},{2,8},{4,14},{6,12},{8,2},{10,0},{12,6},{14,4},{16,26},{18,... | collective-permute-start | bytes 393224 | tf_op jit(solution)/shard_map/ppermute | solution.py:363
  48.9 9.1 %collective-permute-start.13 = (bf16[1,4,128,128]{3,2,1,0:T(8,128)(2,1)S(1)}, bf16[1,4,128,128]{3,2,1,0:T(8,128)(2,1)S(1)}, u32[]{:S(2)}, u32[]{:S(2)}) collective-permute-start(bf16[1,4,128,128]{3,2,1,0:T(8,128)(2,1)S(1)} %get-tuple-element.42), channel_id=1, source_target_pairs={{0,4},{2,6},{4,0},{6,2},{8,12},{10,14},{12,8},{14,10},{16,20},{18,... | collective-permute-start | bytes 393224 | tf_op jit(solution)/shard_map/ppermute | solution.py:363
  51.4 8.1 %collective-permute-start.14 = (bf16[1,4,128,128]{3,2,1,0:T(8,128)(2,1)S(1)}, bf16[1,4,128,128]{3,2,1,0:T(8,128)(2,1)S(1)}, u32[]{:S(2)}, u32[]{:S(2)}) collective-permute-start(bf16[1,4,128,128]{3,2,1,0:T(8,128)(2,1)S(1)} %get-tuple-element.43), channel_id=1, source_target_pairs={{0,6},{2,4},{4,2},{6,0},{8,14},{10,12},{12,10},{14,8},{16,22},{18,... | collective-permute-start | bytes 393224 | tf_op jit(solution)/shard_map/ppermute | solution.py:363
  53.2 6.3 %collective-permute-start.15 = (bf16[1,4,128,128]{3,2,1,0:T(8,128)(2,1)S(1)}, bf16[1,4,128,128]{3,2,1,0:T(8,128)(2,1)S(1)}, u32[]{:S(2)}, u32[]{:S(2)}) collective-permute-start(bf16[1,4,128,128]{3,2,1,0:T(8,128)(2,1)S(1)} %get-tuple-element.44), channel_id=1, source_target_pairs={{0,2},{2,0},{4,6},{6,4},{8,10},{10,8},{12,14},{14,12},{16,18},{18,... | collective-permute-start | bytes 393224 | tf_op jit(solution)/shard_map/ppermute | solution.py:363
  61.4 4.9 %copy-start = (bf16[512,512]{1,0:T(8,128)(2,1)S(1)}, bf16[512,512]{1,0:T(8,128)(2,1)}, u32[]{:S(2)}) copy-start(bf16[512,512]{1,0:T(8,128)(2,1)} %weight_ref.1) | copy-start | bytes 1572868
  61.4 4.9 %collective-permute-start.16 = (bf16[192,256]{1,0:T(8,128)(2,1)S(1)}, bf16[192,256]{1,0:T(8,128)(2,1)S(1)}, u32[]{:S(2)}, u32[]{:S(2)}) collective-permute-start(bf16[192,256]{1,0:T(8,128)(2,1)S(1)} %last_tiles.2.refs_8_), channel_id=1, source_target_pairs={{0,1},{1,0},{2,3},{3,2},{4,5},{5,4},{6,7},{7,6},{8,9},{9,8},{10,11... | collective-permute-start | bytes 294920 | tf_op jit(solution)/shard_map/ppermute | solution.py:377

commit v11 on v10

--- a/solution.py
+++ b/solution.py
@@ -353,25 +353,25 @@
     for step in range(1, col_size):
         cells.append(lax.ppermute(fact_cells, "cols", turn(col_size, -step)))
 
-    order = [0] + sorted(range(1, half), key=lambda step: (-(step & half // 2), step & 1, -step))
-    slots = order if paired else [0]
-
-    def spread(tiles, which, after):
+    near_order = [0] + sorted(range(1, half), key=lambda step: (step & half // 2, step & 1, step))
+    far_order = [0, 1] + sorted(range(2, half), key=lambda step: (step != 2, not step & half // 2, step & 1, step))
+    near_slots, far_slots = (near_order, [half + step for step in far_order]) if paired else ([0], [half])
+
+    def spread(tiles, which, order, after):
         if not paired:
             return [swap(pick(tiles, asked_by, which, after))]
         picked = pick_each(tiles, asked_by, which, me, order, after)
         return [tile if step == 0 else lax.ppermute(tile, "rows", [(row, row ^ step) for row in range(row_size)])
                 for step, tile in zip(order, picked)]
 
-    near = spread(heads_first, 0, cells[1:])
     if group_width % 128:
         w_query = lax.dynamic_slice_in_dim(w_query, col_me * group_width, group_width, 1)
     w_qkv, w_col_out, w_query = [pltpu.with_memory_space_constraint(weight, pltpu.HBM) for weight in (w_qkv, w_col_out, w_query)]
     residual, asked = front(cells, tile_ids, me, key_mask, gain_col, w_qkv, w_col_out, gain_tile, w_query,
                             heads_all, head_size, cols, heads_here, tiles_here, row_size, paired)
-    far = spread(mirrored, 1, near + [asked])
-    sums, tops = first_tiles(asked, near, slots, rows * cols)
-    far_slots = [half + slot for slot in slots]
+    near = spread(heads_first, 0, near_order, [asked])
+    far = spread(mirrored, 1, far_order, near)
+    sums, tops = first_tiles(asked, near, near_slots, rows * cols)
     others = last_tiles(asked, sums, tops, far, far_slots, list(range(1, col_size)), rows * cols, [])
     own = last_tiles(asked, sums, tops, far, far_slots, [0], rows * cols, others[:1])
     answers = list(own) + [lax.ppermute(other, "cols", turn(col_size, step + 1)) for step, other in enumerate(others)]

time: 68 us -> 66.5 us (0.978)
  blocking collectives: 8.45 us -> 0 us
  starting transfers between devices: 20.2 us -> 24.2 us
  local copies, waits for them, and re-layouts: 1.86 us -> 5.43 us
  waiting for transfers between devices: 21.9 us -> 20.7 us
    all_to_all x1 -> x0, blocking collectives: 8.45 us -> none  [swap(): lax.all_to_all(value, 'rows', split_axis=0, concat_axis=0, tiled=True, ax...]
    all_to_all x0 -> x1, starting transfers between devices: none -> 3.78 us  [swap(): lax.all_to_all(value, 'rows', split_axis=0, concat_axis=0, tiled=True, ax...]
    unnamed x15, local copies, waits for them, and re-layouts: 1.86 us -> 5.43 us
    ppermute x14, waiting for transfers between devices: 20.5 us -> 17.7 us  [spread(): lax.ppermute(tile, 'rows', [(row, row ^ step) for row in range(row_size)])]
    ppermute x1, waiting for transfers between devices: 1.42 us -> 3.02 us  [shards(): lax.ppermute(other, 'cols', turn(col_size, step + 1))]
    ppermute x1, starting transfers between devices: 4.12 us -> 2.65 us  [shards(): mirrored = lax.ppermute(heads_first, 'rows', turn(row_size, half))]
    ppermute x1, starting transfers between devices: 1.52 us -> 2.97 us  [shards(): cells.append(lax.ppermute(fact_cells, 'cols', turn(col_size, -step)))]
    ppermute x14, starting transfers between devices: 13 us -> 14.2 us  [spread(): lax.ppermute(tile, 'rows', [(row, row ^ step) for row in range(row_size)])]
  transfers between devices with their start and end apart: 17 -> 18, of which waited for: 9 -> 8; matrix products, arithmetic and copies ran while one was open for 0% -> 2% of each run, Pallas kernels for 16% -> 17%
where the time goes in v11:
time: 66.5 us; the launch traced here: 66.1 us
  starting transfers between devices  24.2 us (36%)
  waiting for transfers between devices  20.7 us (31%)
  Pallas kernels  15.6 us (23%)
  local copies, waits for them, and re-layouts  5.43 us (8%)
    ppermute x14, waiting for transfers between devices, spread(): lax.ppermute(tile, 'rows', [(row, row ^ step) for row in range(row_size)])  17.7 us
    ppermute x14, starting transfers between devices, spread(): lax.ppermute(tile, 'rows', [(row, row ^ step) for row in range(row_size)])  14.2 us
    unnamed x15, local copies, waits for them, and re-layouts  5.43 us
    pallas_call x1, Pallas kernels, front(): pl.pallas_call(functools.partial(front_kernel, groups, heads, head_size,...  5.28 us
    all_to_all x1, starting transfers between devices, swap(): lax.all_to_all(value, 'rows', split_axis=0, concat_axis=0, tiled=True, ax...  3.78 us
    pallas_call x2, Pallas kernels, last_tiles(): pl.pallas_call(functools.partial(last_kernel, slots, groups), out_shape=(...  3.72 us
    ppermute x1, waiting for transfers between devices, shards(): lax.ppermute(other, 'cols', turn(col_size, step + 1))  3.02 us
    ppermute x1, starting transfers between devices, shards(): cells.append(lax.ppermute(fact_cells, 'cols', turn(col_size, -step)))  2.97 us
  transfers between devices with their start and end apart: 18, of which 8 were waited for; matrix products, arithmetic and copies ran while one was open for 2% of the time, Pallas kernels for 17%

profile of v11, /device:TPU:0, one launch (start us, length us, event | category | flops | bytes accessed | tf_op | source)
XLA Modules:
  0.0 66.1 jit_solution(10919487789174270625)
XLA Ops:
  0.0 3.0 %collective-permute-start = (bf16[48,4,512]{2,1,0:T(4,128)(2,1)}, bf16[48,4,512]{2,1,0:T(4,128)(2,1)S(1)}, u32[]{:S(2)}, u32[]{:S(2)}) collective-permute-start(bf16[48,4,512]{2,1,0:T(4,128)(2,1)} %refs_0_.1), channel_id=1, source_target_pairs={{0,1},{1,0},{2,3},{3,2},{4,5},{5,4},{6,7},{7,6},{8,9},{9,8},{10,11... | collective-permute-start | bytes 589832 | tf_op jit(solution)/shard_map/ppermute | solution.py:354
  3.0 1.1 %copy.13 = bf16[4,128,4,128]{3,1,2,0:T(8,128)(2,1)S(1)} copy(bf16[4,128,4,128]{3,2,1,0:T(4,128)(2,1)} %param.17) | data formatting | bytes 1048576 | tf_op args[7]
  4.1 2.7 %collective-permute-start.8 = (bf16[4,4,128,128]{3,2,1,0:T(8,128)(2,1)S(1)}, bf16[4,4,128,128]{3,2,1,0:T(8,128)(2,1)S(1)}, u32[]{:S(2)}, u32[]{:S(2)}) collective-permute-start(bf16[4,4,128,128]{3,2,1,0:T(8,128)(2,1)S(1)} %bitcast.8), channel_id=1, source_target_pairs={{0,16},{2,18},{4,20},{6,22},{8,24},{10,26},{12,28},{14,30},{16,0},... | collective-permute-start | bytes 1572872 | tf_op jit(solution)/shard_map/ppermute | solution.py:349
  7.5 1.2 %request.1 = s32[8,2,128]{2,1,0:T(2,128)} custom-call(s32[1,12]{1,0:T(1,128)S(1)} %copy-done.1, s32[2]{0:T(128)S(1)} %pad_add_fusion.refs_3_.me_ref), custom_call_target="tpu_custom_call" | custom-call | bytes 262144 | tf_op jit(solution)/shard_map/request/pallas_call | solution.py:59
  8.7 3.8 %all-to-all-start = ((s32[8,2,128]{2,1,0:T(2,128)}), s32[8,2,128]{2,1,0:T(2,128)S(1)}, u32[]{:S(2)}, u32[]{:S(2)}) async-start(s32[8,2,128]{2,1,0:T(2,128)} %request.1), calls=%async_computation | async-start | bytes 16384 | tf_op jit(solution)/shard_map/all_to_all | solution.py:346
  16.2 5.3 %front.1 = (f32[192,512]{1,0:T(8,128)S(1)}, bf16[4,384,128]{2,1,0:T(8,128)(2,1)S(1)}) custom-call(bf16[48,4,512]{2,1,0:T(4,128)(2,1)S(1)} %copy-done.3, bf16[48,4,512]{2,1,0:T(4,128)(2,1)S(1)} %collective-permute-done.refs_1_, s32[1,12]{1,0:T(1,128)S(1)} %copy-done.2, s32[2]{0:T(128)S(1)} %pad_add_fusion.refs_3_.me_ref, s32[12,48]{1,0:T(8,128)S(1)} %bitcast.10, ...), custom_call_target="tpu_custom_call" | custom-call | flops 1006632960 | bytes 4194304 | tf_op jit(solution)/shard_map/front/pallas_call | solution.py:206
  22.2 2.1 %collective-permute-start.1 = (bf16[1,4,128,128]{3,2,1,0:T(8,128)(2,1)S(1)}, bf16[1,4,128,128]{3,2,1,0:T(8,128)(2,1)S(1)}, u32[]{:S(2)}, u32[]{:S(2)}) collective-permute-start(bf16[1,4,128,128]{3,2,1,0:T(8,128)(2,1)S(1)} %get-tuple-element.28), channel_id=1, source_target_pairs={{0,4},{2,6},{4,0},{6,2},{8,12},{10,14},{12,8},{14,10},{16,20},{18,... | collective-permute-start | bytes 393224 | tf_op jit(solution)/shard_map/ppermute | solution.py:364
  24.5 1.9 %collective-permute-start.4 = (bf16[1,4,128,128]{3,2,1,0:T(8,128)(2,1)S(1)}, bf16[1,4,128,128]{3,2,1,0:T(8,128)(2,1)S(1)}, u32[]{:S(2)}, u32[]{:S(2)}) collective-permute-start(bf16[1,4,128,128]{3,2,1,0:T(8,128)(2,1)S(1)} %get-tuple-element.31), channel_id=1, source_target_pairs={{0,8},{2,10},{4,12},{6,14},{8,0},{10,2},{12,4},{14,6},{16,24},{18,... | collective-permute-start | bytes 393224 | tf_op jit(solution)/shard_map/ppermute | solution.py:364
  26.4 2.1 %collective-permute-done.1.refs_1_ = bf16[1,4,128,128]{3,2,1,0:T(8,128)(2,1)S(1)} collective-permute-done((bf16[1,4,128,128]{3,2,1,0:T(8,128)(2,1)S(1)}, bf16[1,4,128,128]{3,2,1,0:T(8,128)(2,1)S(1)}, u32[]{:S(2)}, u32[]{:S(2)}) %collective-permute-start.1) | collective-permute-done | bytes 131104 | tf_op jit(solution)/shard_map/ppermute | solution.py:364
  28.6 3.0 %collective-permute-start.5 = (bf16[1,4,128,128]{3,2,1,0:T(8,128)(2,1)S(1)}, bf16[1,4,128,128]{3,2,1,0:T(8,128)(2,1)S(1)}, u32[]{:S(2)}, u32[]{:S(2)}) collective-permute-start(bf16[1,4,128,128]{3,2,1,0:T(8,128)(2,1)S(1)} %get-tuple-element.32), channel_id=1, source_target_pairs={{0,12},{2,14},{4,8},{6,10},{8,4},{10,6},{12,0},{14,2},{16,28},{18,... | collective-permute-start | bytes 393224 | tf_op jit(solution)/shard_map/ppermute | solution.py:364
  31.6 1.7 %collective-permute-start.7 = (bf16[1,4,128,128]{3,2,1,0:T(8,128)(2,1)S(1)}, bf16[1,4,128,128]{3,2,1,0:T(8,128)(2,1)S(1)}, u32[]{:S(2)}, u32[]{:S(2)}) collective-permute-start(bf16[1,4,128,128]{3,2,1,0:T(8,128)(2,1)S(1)} %get-tuple-element.34), channel_id=1, source_target_pairs={{0,14},{2,12},{4,10},{6,8},{8,6},{10,4},{12,2},{14,0},{16,30},{18,... | collective-permute-start | bytes 393224 | tf_op jit(solution)/shard_map/ppermute | solution.py:364
  33.3 3.0 %collective-permute-done.5.refs_5_ = bf16[1,4,128,128]{3,2,1,0:T(8,128)(2,1)S(1)} collective-permute-done((bf16[1,4,128,128]{3,2,1,0:T(8,128)(2,1)S(1)}, bf16[1,4,128,128]{3,2,1,0:T(8,128)(2,1)S(1)}, u32[]{:S(2)}, u32[]{:S(2)}) %collective-permute-start.5) | collective-permute-done | bytes 131104 | tf_op jit(solution)/shard_map/ppermute | solution.py:364
  36.3 1.9 %collective-permute-done.6.refs_6_ = bf16[1,4,128,128]{3,2,1,0:T(8,128)(2,1)S(1)} collective-permute-done((bf16[1,4,128,128]{3,2,1,0:T(8,128)(2,1)S(1)}, bf16[1,4,128,128]{3,2,1,0:T(8,128)(2,1)S(1)}, u32[]{:S(2)}, u32[]{:S(2)}) %collective-permute-start.6) | collective-permute-done | bytes 131104 | tf_op jit(solution)/shard_map/ppermute | solution.py:364
  38.2 3.5 %collective-permute-done.7.refs_7_ = bf16[1,4,128,128]{3,2,1,0:T(8,128)(2,1)S(1)} collective-permute-done((bf16[1,4,128,128]{3,2,1,0:T(8,128)(2,1)S(1)}, bf16[1,4,128,128]{3,2,1,0:T(8,128)(2,1)S(1)}, u32[]{:S(2)}, u32[]{:S(2)}) %collective-permute-start.7) | collective-permute-done | bytes 131104 | tf_op jit(solution)/shard_map/ppermute | solution.py:364
  43.0 1.2 %collective-permute-start.11 = (bf16[1,4,128,128]{3,2,1,0:T(8,128)(2,1)S(1)}, bf16[1,4,128,128]{3,2,1,0:T(8,128)(2,1)S(1)}, u32[]{:S(2)}, u32[]{:S(2)}) collective-permute-start(bf16[1,4,128,128]{3,2,1,0:T(8,128)(2,1)S(1)} %get-tuple-element.40), channel_id=1, source_target_pairs={{0,8},{2,10},{4,12},{6,14},{8,0},{10,2},{12,4},{14,6},{16,24},{18,... | collective-permute-start | bytes 393224 | tf_op jit(solution)/shard_map/ppermute | solution.py:364
  44.2 2.0 %collective-permute-start.12 = (bf16[1,4,128,128]{3,2,1,0:T(8,128)(2,1)S(1)}, bf16[1,4,128,128]{3,2,1,0:T(8,128)(2,1)S(1)}, u32[]{:S(2)}, u32[]{:S(2)}) collective-permute-start(bf16[1,4,128,128]{3,2,1,0:T(8,128)(2,1)S(1)} %get-tuple-element.41), channel_id=1, source_target_pairs={{0,12},{2,14},{4,8},{6,10},{8,4},{10,6},{12,0},{14,2},{16,28},{18,... | collective-permute-start | bytes 393224 | tf_op jit(solution)/shard_map/ppermute | solution.py:364
  46.2 1.5 %collective-permute-start.14 = (bf16[1,4,128,128]{3,2,1,0:T(8,128)(2,1)S(1)}, bf16[1,4,128,128]{3,2,1,0:T(8,128)(2,1)S(1)}, u32[]{:S(2)}, u32[]{:S(2)}) collective-permute-start(bf16[1,4,128,128]{3,2,1,0:T(8,128)(2,1)S(1)} %get-tuple-element.43), channel_id=1, source_target_pairs={{0,14},{2,12},{4,10},{6,8},{8,6},{10,4},{12,2},{14,0},{16,30},{18,... | collective-permute-start | bytes 393224 | tf_op jit(solution)/shard_map/ppermute | solution.py:364
  48.6 2.4 %first_tiles.1 = (f32[4,384,128]{2,1,0:T(8,128)S(1)}, f32[384,128]{1,0:T(8,128)S(1)}) custom-call(bf16[4,384,128]{2,1,0:T(8,128)(2,1)S(1)} %get-tuple-element.26.refs_0_.asked_ref, bf16[1,4,128,128]{3,2,1,0:T(8,128)(2,1)S(1)} %get-tuple-element.27.refs_0_, bf16[1,4,128,128]{3,2,1,0:T(8,128)(2,1)S(1)} %collective-permute-done.1.refs_1_, ...), custom_call_target="tpu_custom_call" | custom-call | flops 805306368 | bytes 4194304 | tf_op jit(solution)/shard_map/first_tiles/pallas_call | solution.py:256
  51.0 2.4 %collective-permute-done.12.refs_4_ = bf16[1,4,128,128]{3,2,1,0:T(8,128)(2,1)S(1)} collective-permute-done((bf16[1,4,128,128]{3,2,1,0:T(8,128)(2,1)S(1)}, bf16[1,4,128,128]{3,2,1,0:T(8,128)(2,1)S(1)}, u32[]{:S(2)}, u32[]{:S(2)}) %collective-permute-start.12) | collective-permute-done | bytes 131104 | tf_op jit(solution)/shard_map/ppermute | solution.py:364
  53.4 3.8 %collective-permute-done.14.refs_6_ = bf16[1,4,128,128]{3,2,1,0:T(8,128)(2,1)S(1)} collective-permute-done((bf16[1,4,128,128]{3,2,1,0:T(8,128)(2,1)S(1)}, bf16[1,4,128,128]{3,2,1,0:T(8,128)(2,1)S(1)}, u32[]{:S(2)}, u32[]{:S(2)}) %collective-permute-start.14) | collective-permute-done | bytes 131104 | tf_op jit(solution)/shard_map/ppermute | solution.py:364
  57.2 1.9 %last_tiles.2.refs_8_ = bf16[192,256]{1,0:T(8,128)(2,1)S(1)} custom-call(bf16[4,384,128]{2,1,0:T(8,128)(2,1)S(1)} %get-tuple-element.26.refs_0_.asked_ref, f32[4,384,128]{2,1,0:T(8,128)S(1)} %get-tuple-element.35.sums_ref, f32[384,128]{1,0:T(8,128)S(1)} %get-tuple-element.36.tops_ref, bf16[1,4,128,128]{3,2,1,0:T(8,128)(2,1)S(1)} %get-tuple-element.37.refs_0_, ...), custom_call_target="tpu_custom_call" | custom-call | flops 402653184 | bytes 4194304 | tf_op jit(solution)/shard_map/last_tiles/pallas_call | solution.py:293
  59.7 1.9 %last_tiles.3.refs_0_ = bf16[192,256]{1,0:T(8,128)(2,1)S(1)} custom-call(bf16[4,384,128]{2,1,0:T(8,128)(2,1)S(1)} %get-tuple-element.26.refs_0_.asked_ref, f32[4,384,128]{2,1,0:T(8,128)S(1)} %get-tuple-element.35.sums_ref, f32[384,128]{1,0:T(8,128)S(1)} %get-tuple-element.36.tops_ref, bf16[1,4,128,128]{3,2,1,0:T(8,128)(2,1)S(1)} %get-tuple-element.37.refs_0_, ...), custom_call_target="tpu_custom_call" | custom-call | flops 402653184 | bytes 4194304 | tf_op jit(solution)/shard_map/last_tiles/pallas_call | solution.py:293
  61.6 3.0 %collective-permute-done.16.refs_1_ = bf16[192,256]{1,0:T(8,128)(2,1)S(1)} collective-permute-done((bf16[192,256]{1,0:T(8,128)(2,1)S(1)}, bf16[192,256]{1,0:T(8,128)(2,1)S(1)}, u32[]{:S(2)}, u32[]{:S(2)}) %collective-permute-start.16) | collective-permute-done | bytes 98336 | tf_op jit(solution)/shard_map/ppermute | solution.py:377
  64.6 1.5 %finish.1 = bf16[48,4,512]{2,1,0:T(4,128)(2,1)} custom-call(s32[2]{0:T(128)S(1)} %pad_add_fusion.refs_3_.me_ref, bf16[512,512]{1,0:T(8,128)(2,1)S(1)} %copy-done, f32[192,512]{1,0:T(8,128)S(1)} %get-tuple-element.25.resid_ref, bf16[192,256]{1,0:T(8,128)(2,1)S(1)} %last_tiles.3.refs_0_, bf16[192,256]{1,0:T(8,128)(2,1)S(1)} %collective-permute-done.16.refs_1_), custom_call_target="tpu_custom_call" | custom-call | flops 100663296 | bytes 1048576 | tf_op jit(solution)/shard_map/finish/pallas_call | solution.py:316
  (36 shorter events, 8.1 us)
Async XLA Ops:
  0.0 12.5 %collective-permute-start = (bf16[48,4,512]{2,1,0:T(4,128)(2,1)}, bf16[48,4,512]{2,1,0:T(4,128)(2,1)S(1)}, u32[]{:S(2)}, u32[]{:S(2)}) collective-permute-start(bf16[48,4,512]{2,1,0:T(4,128)(2,1)} %refs_0_.1), channel_id=1, source_target_pairs={{0,1},{1,0},{2,3},{3,2},{4,5},{5,4},{6,7},{7,6},{8,9},{9,8},{10,11... | collective-permute-start | bytes 589832 | tf_op jit(solution)/shard_map/ppermute | solution.py:354
  4.1 37.7 %collective-permute-start.8 = (bf16[4,4,128,128]{3,2,1,0:T(8,128)(2,1)S(1)}, bf16[4,4,128,128]{3,2,1,0:T(8,128)(2,1)S(1)}, u32[]{:S(2)}, u32[]{:S(2)}) collective-permute-start(bf16[4,4,128,128]{3,2,1,0:T(8,128)(2,1)S(1)} %bitcast.8), channel_id=1, source_target_pairs={{0,16},{2,18},{4,20},{6,22},{8,24},{10,26},{12,28},{14,30},{16,0},... | collective-permute-start | bytes 1572872 | tf_op jit(solution)/shard_map/ppermute | solution.py:349
  8.7 12.7 %all-to-all-start = ((s32[8,2,128]{2,1,0:T(2,128)}), s32[8,2,128]{2,1,0:T(2,128)S(1)}, u32[]{:S(2)}, u32[]{:S(2)}) async-start(s32[8,2,128]{2,1,0:T(2,128)} %request.1), calls=%async_computation | async-start | bytes 16384 | tf_op jit(solution)/shard_map/all_to_all | solution.py:346
  12.5 0.7 copy-start.2
  13.2 0.9 %copy-start.3 = (bf16[48,4,512]{2,1,0:T(4,128)(2,1)S(1)}, bf16[48,4,512]{2,1,0:T(4,128)(2,1)}, u32[]{:S(2)}) copy-start(bf16[48,4,512]{2,1,0:T(4,128)(2,1)} %refs_0_.1) | copy-start | bytes 589828
  14.1 0.7 %copy-start.4 = (s32[48,12]{0,1:T(8,128)S(1)}, s32[48,12]{0,1:T(8,128)}, u32[]{:S(2)}) copy-start(s32[48,12]{0,1:T(8,128)} %param.19) | copy-start | bytes 6916
  14.8 0.7 %copy-start.5 = (f32[512]{0:T(512)S(1)}, f32[512]{0:T(512)}, u32[]{:S(2)}) copy-start(f32[512]{0:T(512)} %param.11) | copy-start | bytes 6148
  15.5 0.7 %copy-start.6 = (f32[512]{0:T(512)S(1)}, f32[512]{0:T(512)}, u32[]{:S(2)}) copy-start(f32[512]{0:T(512)} %param.14) | copy-start | bytes 6148
  22.2 6.4 %collective-permute-start.1 = (bf16[1,4,128,128]{3,2,1,0:T(8,128)(2,1)S(1)}, bf16[1,4,128,128]{3,2,1,0:T(8,128)(2,1)S(1)}, u32[]{:S(2)}, u32[]{:S(2)}) collective-permute-start(bf16[1,4,128,128]{3,2,1,0:T(8,128)(2,1)S(1)} %get-tuple-element.28), channel_id=1, source_target_pairs={{0,4},{2,6},{4,0},{6,2},{8,12},{10,14},{12,8},{14,10},{16,20},{18,... | collective-permute-start | bytes 393224 | tf_op jit(solution)/shard_map/ppermute | solution.py:364
  24.3 7.2 %collective-permute-start.2 = (bf16[1,4,128,128]{3,2,1,0:T(8,128)(2,1)S(1)}, bf16[1,4,128,128]{3,2,1,0:T(8,128)(2,1)S(1)}, u32[]{:S(2)}, u32[]{:S(2)}) collective-permute-start(bf16[1,4,128,128]{3,2,1,0:T(8,128)(2,1)S(1)} %get-tuple-element.29), channel_id=1, source_target_pairs={{0,2},{2,0},{4,6},{6,4},{8,10},{10,8},{12,14},{14,12},{16,18},{18,... | collective-permute-start | bytes 393224 | tf_op jit(solution)/shard_map/ppermute | solution.py:364
  24.3 7.2 %collective-permute-start.3 = (bf16[1,4,128,128]{3,2,1,0:T(8,128)(2,1)S(1)}, bf16[1,4,128,128]{3,2,1,0:T(8,128)(2,1)S(1)}, u32[]{:S(2)}, u32[]{:S(2)}) collective-permute-start(bf16[1,4,128,128]{3,2,1,0:T(8,128)(2,1)S(1)} %get-tuple-element.30), channel_id=1, source_target_pairs={{0,6},{2,4},{4,2},{6,0},{8,14},{10,12},{12,10},{14,8},{16,22},{18,... | collective-permute-start | bytes 393224 | tf_op jit(solution)/shard_map/ppermute | solution.py:364
  24.5 8.8 %collective-permute-start.4 = (bf16[1,4,128,128]{3,2,1,0:T(8,128)(2,1)S(1)}, bf16[1,4,128,128]{3,2,1,0:T(8,128)(2,1)S(1)}, u32[]{:S(2)}, u32[]{:S(2)}) collective-permute-start(bf16[1,4,128,128]{3,2,1,0:T(8,128)(2,1)S(1)} %get-tuple-element.31), channel_id=1, source_target_pairs={{0,8},{2,10},{4,12},{6,14},{8,0},{10,2},{12,4},{14,6},{16,24},{18,... | collective-permute-start | bytes 393224 | tf_op jit(solution)/shard_map/ppermute | solution.py:364
  28.6 7.8 %collective-permute-start.5 = (bf16[1,4,128,128]{3,2,1,0:T(8,128)(2,1)S(1)}, bf16[1,4,128,128]{3,2,1,0:T(8,128)(2,1)S(1)}, u32[]{:S(2)}, u32[]{:S(2)}) collective-permute-start(bf16[1,4,128,128]{3,2,1,0:T(8,128)(2,1)S(1)} %get-tuple-element.32), channel_id=1, source_target_pairs={{0,12},{2,14},{4,8},{6,10},{8,4},{10,6},{12,0},{14,2},{16,28},{18,... | collective-permute-start | bytes 393224 | tf_op jit(solution)/shard_map/ppermute | solution.py:364
  31.5 6.7 %collective-permute-start.6 = (bf16[1,4,128,128]{3,2,1,0:T(8,128)(2,1)S(1)}, bf16[1,4,128,128]{3,2,1,0:T(8,128)(2,1)S(1)}, u32[]{:S(2)}, u32[]{:S(2)}) collective-permute-start(bf16[1,4,128,128]{3,2,1,0:T(8,128)(2,1)S(1)} %get-tuple-element.33), channel_id=1, source_target_pairs={{0,10},{2,8},{4,14},{6,12},{8,2},{10,0},{12,6},{14,4},{16,26},{18,... | collective-permute-start | bytes 393224 | tf_op jit(solution)/shard_map/ppermute | solution.py:364
  31.6 10.2 %collective-permute-start.7 = (bf16[1,4,128,128]{3,2,1,0:T(8,128)(2,1)S(1)}, bf16[1,4,128,128]{3,2,1,0:T(8,128)(2,1)S(1)}, u32[]{:S(2)}, u32[]{:S(2)}) collective-permute-start(bf16[1,4,128,128]{3,2,1,0:T(8,128)(2,1)S(1)} %get-tuple-element.34), channel_id=1, source_target_pairs={{0,14},{2,12},{4,10},{6,8},{8,6},{10,4},{12,2},{14,0},{16,30},{18,... | collective-permute-start | bytes 393224 | tf_op jit(solution)/shard_map/ppermute | solution.py:364
  42.5 3.7 %collective-permute-start.9 = (bf16[1,4,128,128]{3,2,1,0:T(8,128)(2,1)S(1)}, bf16[1,4,128,128]{3,2,1,0:T(8,128)(2,1)S(1)}, u32[]{:S(2)}, u32[]{:S(2)}) collective-permute-start(bf16[1,4,128,128]{3,2,1,0:T(8,128)(2,1)S(1)} %get-tuple-element.38), channel_id=1, source_target_pairs={{0,2},{2,0},{4,6},{6,4},{8,10},{10,8},{12,14},{14,12},{16,18},{18,... | collective-permute-start | bytes 393224 | tf_op jit(solution)/shard_map/ppermute | solution.py:364
  42.7 5.8 %collective-permute-start.10 = (bf16[1,4,128,128]{3,2,1,0:T(8,128)(2,1)S(1)}, bf16[1,4,128,128]{3,2,1,0:T(8,128)(2,1)S(1)}, u32[]{:S(2)}, u32[]{:S(2)}) collective-permute-start(bf16[1,4,128,128]{3,2,1,0:T(8,128)(2,1)S(1)} %get-tuple-element.39), channel_id=1, source_target_pairs={{0,4},{2,6},{4,0},{6,2},{8,12},{10,14},{12,8},{14,10},{16,20},{18,... | collective-permute-start | bytes 393224 | tf_op jit(solution)/shard_map/ppermute | solution.py:364
  43.0 7.9 %collective-permute-start.11 = (bf16[1,4,128,128]{3,2,1,0:T(8,128)(2,1)S(1)}, bf16[1,4,128,128]{3,2,1,0:T(8,128)(2,1)S(1)}, u32[]{:S(2)}, u32[]{:S(2)}) collective-permute-start(bf16[1,4,128,128]{3,2,1,0:T(8,128)(2,1)S(1)} %get-tuple-element.40), channel_id=1, source_target_pairs={{0,8},{2,10},{4,12},{6,14},{8,0},{10,2},{12,4},{14,6},{16,24},{18,... | collective-permute-start | bytes 393224 | tf_op jit(solution)/shard_map/ppermute | solution.py:364
  44.2 9.1 %collective-permute-start.12 = (bf16[1,4,128,128]{3,2,1,0:T(8,128)(2,1)S(1)}, bf16[1,4,128,128]{3,2,1,0:T(8,128)(2,1)S(1)}, u32[]{:S(2)}, u32[]{:S(2)}) collective-permute-start(bf16[1,4,128,128]{3,2,1,0:T(8,128)(2,1)S(1)} %get-tuple-element.41), channel_id=1, source_target_pairs={{0,12},{2,14},{4,8},{6,10},{8,4},{10,6},{12,0},{14,2},{16,28},{18,... | collective-permute-start | bytes 393224 | tf_op jit(solution)/shard_map/ppermute | solution.py:364
  46.2 7.2 %collective-permute-start.13 = (bf16[1,4,128,128]{3,2,1,0:T(8,128)(2,1)S(1)}, bf16[1,4,128,128]{3,2,1,0:T(8,128)(2,1)S(1)}, u32[]{:S(2)}, u32[]{:S(2)}) collective-permute-start(bf16[1,4,128,128]{3,2,1,0:T(8,128)(2,1)S(1)} %get-tuple-element.42), channel_id=1, source_target_pairs={{0,10},{2,8},{4,14},{6,12},{8,2},{10,0},{12,6},{14,4},{16,26},{18,... | collective-permute-start | bytes 393224 | tf_op jit(solution)/shard_map/ppermute | solution.py:364
  46.2 11.0 %collective-permute-start.14 = (bf16[1,4,128,128]{3,2,1,0:T(8,128)(2,1)S(1)}, bf16[1,4,128,128]{3,2,1,0:T(8,128)(2,1)S(1)}, u32[]{:S(2)}, u32[]{:S(2)}) collective-permute-start(bf16[1,4,128,128]{3,2,1,0:T(8,128)(2,1)S(1)} %get-tuple-element.43), channel_id=1, source_target_pairs={{0,14},{2,12},{4,10},{6,8},{8,6},{10,4},{12,2},{14,0},{16,30},{18,... | collective-permute-start | bytes 393224 | tf_op jit(solution)/shard_map/ppermute | solution.py:364
  48.5 8.7 %collective-permute-start.15 = (bf16[1,4,128,128]{3,2,1,0:T(8,128)(2,1)S(1)}, bf16[1,4,128,128]{3,2,1,0:T(8,128)(2,1)S(1)}, u32[]{:S(2)}, u32[]{:S(2)}) collective-permute-start(bf16[1,4,128,128]{3,2,1,0:T(8,128)(2,1)S(1)} %get-tuple-element.44), channel_id=1, source_target_pairs={{0,6},{2,4},{4,2},{6,0},{8,14},{10,12},{12,10},{14,8},{16,22},{18,... | collective-permute-start | bytes 393224 | tf_op jit(solution)/shard_map/ppermute | solution.py:364
  59.1 5.5 %copy-start = (bf16[512,512]{1,0:T(8,128)(2,1)S(1)}, bf16[512,512]{1,0:T(8,128)(2,1)}, u32[]{:S(2)}) copy-start(bf16[512,512]{1,0:T(8,128)(2,1)} %weight_ref.1) | copy-start | bytes 1572868
  59.1 5.5 %collective-permute-start.16 = (bf16[192,256]{1,0:T(8,128)(2,1)S(1)}, bf16[192,256]{1,0:T(8,128)(2,1)S(1)}, u32[]{:S(2)}, u32[]{:S(2)}) collective-permute-start(bf16[192,256]{1,0:T(8,128)(2,1)S(1)} %last_tiles.2.refs_8_), channel_id=1, source_target_pairs={{0,1},{1,0},{2,3},{3,2},{4,5},{5,4},{6,7},{7,6},{8,9},{9,8},{10,11... | collective-permute-start | bytes 294920 | tf_op jit(solution)/shard_map/ppermute | solution.py:377
  (1 other events, 0.7 us)

commit v12 on v11

--- a/solution.py
+++ b/solution.py
@@ -40,6 +40,23 @@
 def slot_of(owner, row_me, row_size, paired):
     half = row_size // 2
     return owner ^ row_me if paired else lax.rem(owner + lax.div(row_me, half) * half, row_size)
+
+
+def tie_kernel(value_ref, after_ref, out_ref):
+    pass
+
+
+def tie(value, after):
+    return pl.pallas_call(
+        tie_kernel,
+        out_shape=jax.ShapeDtypeStruct(value.shape, value.dtype),
+        in_specs=[ANY, ANY],
+        out_specs=ANY,
+        input_output_aliases={0: 0},
+        compiler_params=params(0),
+        cost_estimate=pl.CostEstimate(flops=0, bytes_accessed=0, transcendentals=0),
+        name="tie",
+    )(value, after)
 
 
 def request_kernel(tiles_here, row_size, ids_ref, me_ref, out_ref):
@@ -105,9 +122,10 @@
 
 
 def front_kernel(groups, heads, head_size, chunk, cols, heads_here, tiles_here, row_size, paired, *refs):
-    cell_refs, refs = refs[:groups], refs[groups:]
-    (ids_ref, me_ref, mask_ref, gain_col_ref, gain_tile_ref, w_qkv_hbm, w_out_hbm, w_query_hbm,
-     resid_ref, asked_ref, normed_ref, packed_ref, w_qkv_ref, w_out_ref, w_query_ref, sems) = refs
+    cell_hbms, refs = refs[:groups], refs[groups:]
+    (me_ref, ids_hbm, mask_hbm, gain_col_hbm, gain_tile_hbm, w_qkv_hbm, w_out_hbm, w_query_hbm, after_ref,
+     resid_ref, asked_ref, normed_ref, packed_ref, w_qkv_ref, w_out_ref, w_query_ref, cell_refs,
+     ids_ref, mask_ref, gain_col_ref, gain_tile_ref, sems) = refs
     own_rows, width = resid_ref.shape
     steps = own_rows // chunk
     span = groups * chunk
@@ -115,15 +133,19 @@
     group_width = heads_here * head_size
     if w_query_hbm.shape[1] != group_width:
         w_query_hbm = w_query_hbm.at[:, pl.ds(pl.multiple_of(me_ref[1] * group_width, group_width), group_width)]
-    copies = [pltpu.make_async_copy(w_qkv_hbm.at[:, pl.ds(part * width, width)], w_qkv_ref.at[part], sems.at[part])
-              for part in range(3)]
-    copies.append(pltpu.make_async_copy(w_out_hbm, w_out_ref, sems.at[3]))
-    copies.append(pltpu.make_async_copy(w_query_hbm, w_query_ref, sems.at[4]))
+    pairs = [(hbm, cell_refs.at[group]) for group, hbm in enumerate(cell_hbms)]
+    pairs += [(gain_col_hbm, gain_col_ref)]
+    pairs += [(w_qkv_hbm.at[:, pl.ds(part * width, width)], w_qkv_ref.at[part]) for part in range(3)]
+    pairs += [(w_out_hbm, w_out_ref), (gain_tile_hbm, gain_tile_ref), (w_query_hbm, w_query_ref), (ids_hbm, ids_ref), (mask_hbm, mask_ref)]
+    copies = [pltpu.make_async_copy(*pair, sems.at[index]) for index, pair in enumerate(pairs)]
     for copy in copies:
         copy.start()
+    for copy in copies[:groups + 1]:
+        copy.wait()
+    copies = copies[groups + 1:]
 
     def cells_of(group, step):
-        cells = cell_refs[group][pl.ds(step * (chunk // cols), chunk // cols)].astype(jnp.float32)
+        cells = cell_refs[group, pl.ds(step * (chunk // cols), chunk // cols)].astype(jnp.float32)
         return cells.reshape(chunk, width)
 
     for step in range(steps):
@@ -153,7 +175,8 @@
             start = 2 * pair * span
             mixed = dot_rows(weights[start:start + 2 * span], packed_ref[2, rows, lanes])
             normed_ref[rows, lanes] = jnp.where(lane_low, mixed[:span], mixed[span:]).astype(jnp.bfloat16)
-    copies[3].wait()
+    for copy in copies[3:]:
+        copy.wait()
     delta = dot_rows(normed_ref[...], w_out_ref[...])
     for step in range(steps):
         for group in range(groups):
@@ -178,7 +201,6 @@
     row_of = cell // span * (chunk // cols) + cell % chunk // cols
     spread = (row_of == iota((total, shut.shape[0]), 1)).astype(jnp.bfloat16)
     bias = dot_rows(spread, shut) * BIG
-    copies[4].wait()
     asked = dot_rows(normed_ref[...], w_query_ref[...]).astype(jnp.bfloat16).astype(jnp.float32) * scale
     low = iota((total, lanes_two), 1) < head_size
     for head in range(heads_here):
@@ -197,25 +219,31 @@
 
 
 def front(cells, ids, me, key_mask, gain_col, w_qkv, w_out, gain_tile, w_query, heads, head_size, cols,
-          heads_here, tiles_here, row_size, paired):
+          heads_here, tiles_here, row_size, paired, after):
     groups = len(cells)
     width = cells[0].shape[2]
     own_rows = cells[0].shape[0] * cols
     total = groups * own_rows
-    weights = [(3, width, width), (width, width), (width, heads_here * head_size)]
+    key_mask, gain_col, gain_tile = key_mask.T, gain_col.reshape(1, width), gain_tile.reshape(1, width)
+    weights = [(3, width, width), (width, width), (width, heads_here * head_size), (groups,) + cells[0].shape]
+    scratch = [pltpu.VMEM(shape, jnp.bfloat16) for shape in [(total, width), (3, total, width)] + weights]
+    scratch += [pltpu.SMEM(ids.shape, jnp.int32), pltpu.VMEM(key_mask.shape, jnp.int32)]
+    scratch += [pltpu.VMEM((1, width), jnp.float32)] * 2 + [pltpu.SemaphoreType.DMA((groups + 9,))]
+    fetched = [pltpu.with_memory_space_constraint(value, pltpu.HBM)
+               for value in (ids, key_mask, gain_col, gain_tile, w_qkv, w_out, w_query)]
+    own = pltpu.with_memory_space_constraint(cells[0], pltpu.HBM)
     return pl.pallas_call(
         functools.partial(front_kernel, groups, heads, head_size, ROW_GROUP * cols, cols, heads_here, tiles_here, row_size, paired),
         out_shape=(jax.ShapeDtypeStruct((own_rows, width), jnp.float32),
                    jax.ShapeDtypeStruct((heads_here, total, 2 * head_size), jnp.bfloat16)),
-        in_specs=[VMEM] * groups + [SMEM, SMEM] + [VMEM] * 3 + [HBM] * 3,
+        in_specs=[HBM] + [ANY] * (groups - 1) + [SMEM] + [HBM] * 7 + [ANY],
         out_specs=(VMEM, VMEM),
-        scratch_shapes=[pltpu.VMEM((total, width), jnp.bfloat16), pltpu.VMEM((3, total, width), jnp.bfloat16)]
-        + [pltpu.VMEM(shape, jnp.bfloat16) for shape in weights] + [pltpu.SemaphoreType.DMA((5,))],
+        scratch_shapes=scratch,
         compiler_params=params(total),
         cost_estimate=pl.CostEstimate(flops=2 * total * width * 5 * width, bytes_accessed=4 * MIB,
                                       transcendentals=total * heads * 128),
         name="front",
-    )(*cells, ids, me, key_mask.T, gain_col.reshape(1, width), gain_tile.reshape(1, width), w_qkv, w_out, w_query)
+    )(own, *cells[1:], me, *fetched, after)
 
 
 def weigh(query, tile_refs, head, slots):
@@ -345,19 +373,19 @@
     def swap(value):
         return lax.all_to_all(value, "rows", split_axis=0, concat_axis=0, tiled=True, axis_index_groups=halves)
 
-    heads_first = jnp.transpose(tile_kv, (0, 2, 1, 3))
+    asked_of = request(tile_ids, me, tiles_here, row_size)
+    asked_by = swap(asked_of)
+    heads_first = tie(jnp.transpose(tile_kv, (0, 2, 1, 3)), asked_of)
     mirrored = lax.ppermute(heads_first, "rows", turn(row_size, half))
-    asked_by = swap(request(tile_ids, me, tiles_here, row_size))
 
     cells = [fact_cells]
     for step in range(1, col_size):
         cells.append(lax.ppermute(fact_cells, "cols", turn(col_size, -step)))
 
-    near_order = [0] + sorted(range(1, half), key=lambda step: (step & half // 2, step & 1, step))
-    far_order = [0, 1] + sorted(range(2, half), key=lambda step: (step != 2, not step & half // 2, step & 1, step))
-    near_slots, far_slots = (near_order, [half + step for step in far_order]) if paired else ([0], [half])
-
-    def spread(tiles, which, order, after):
+    order = [0, 1] + sorted(range(2, half), key=lambda step: (step != 2, not step & half // 2, step & 1, step))
+    near_slots, far_slots = (order, [half + step for step in order]) if paired else ([0], [half])
+
+    def spread(tiles, which, after):
         if not paired:
             return [swap(pick(tiles, asked_by, which, after))]
         picked = pick_each(tiles, asked_by, which, me, order, after)
@@ -366,11 +394,10 @@
 
     if group_width % 128:
         w_query = lax.dynamic_slice_in_dim(w_query, col_me * group_width, group_width, 1)
-    w_qkv, w_col_out, w_query = [pltpu.with_memory_space_constraint(weight, pltpu.HBM) for weight in (w_qkv, w_col_out, w_query)]
+    near = spread(heads_first, 0, [])
     residual, asked = front(cells, tile_ids, me, key_mask, gain_col, w_qkv, w_col_out, gain_tile, w_query,
-                            heads_all, head_size, cols, heads_here, tiles_here, row_size, paired)
-    near = spread(heads_first, 0, near_order, [asked])
-    far = spread(mirrored, 1, far_order, near)
+                            heads_all, head_size, cols, heads_here, tiles_here, row_size, paired, near[0])
+    far = spread(mirrored, 1, [asked] + near[1:3])
     sums, tops = first_tiles(asked, near, near_slots, rows * cols)
     others = last_tiles(asked, sums, tops, far, far_slots, list(range(1, col_size)), rows * cols, [])
     own = last_tiles(asked, sums, tops, far, far_slots, [0], rows * cols, others[:1])

time: 66.5 us -> 62.4 us (0.938)
  blocking collectives: 0 us -> 9.81 us
  starting transfers between devices: 24.2 us -> 19.1 us
  waiting for transfers between devices: 20.7 us -> 16 us
  local copies, waits for them, and re-layouts: 5.43 us -> 1.84 us
    all_to_all x0 -> x1, blocking collectives: none -> 9.81 us  [swap(): lax.all_to_all(value, 'rows', split_axis=0, concat_axis=0, tiled=True, ax...]
    all_to_all x1 -> x0, starting transfers between devices: 3.78 us -> none  [swap(): lax.all_to_all(value, 'rows', split_axis=0, concat_axis=0, tiled=True, ax...]
    ppermute x14, waiting for transfers between devices: 17.7 us -> 13.9 us  [spread(): lax.ppermute(tile, 'rows', [(row, row ^ step) for row in range(row_size)])]
    unnamed x15 -> x7, local copies, waits for them, and re-layouts: 5.43 us -> 1.84 us
    ppermute x14, starting transfers between devices: 14.2 us -> 11.9 us  [spread(): lax.ppermute(tile, 'rows', [(row, row ^ step) for row in range(row_size)])]
    ppermute x1, starting transfers between devices: 2.65 us -> 4.1 us  [shards(): mirrored = lax.ppermute(heads_first, 'rows', turn(row_size, half))]
    ppermute x1, starting transfers between devices: 2.97 us -> 1.52 us  [shards(): cells.append(lax.ppermute(fact_cells, 'cols', turn(col_size, -step)))]
    ppermute x1, starting transfers between devices: 0.57 us -> 1.58 us  [shards(): lax.ppermute(other, 'cols', turn(col_size, step + 1))]
  transfers between devices with their start and end apart: 18 -> 17, of which waited for: 8 -> 7; matrix products, arithmetic and copies ran while one was open for 2% -> 0% of each run, Pallas kernels for 17% -> 18%
where the time goes in v12:
time: 62.4 us; the launch traced here: 62.2 us
  starting transfers between devices  19.1 us (31%)
  waiting for transfers between devices  16 us (26%)
  Pallas kernels  15.3 us (25%)
  blocking collectives  9.81 us (16%)
  local copies, waits for them, and re-layouts  1.84 us (3%)
    ppermute x14, waiting for transfers between devices, spread(): lax.ppermute(tile, 'rows', [(row, row ^ step) for row in range(row_size)])  13.9 us
    ppermute x14, starting transfers between devices, spread(): lax.ppermute(tile, 'rows', [(row, row ^ step) for row in range(row_size)])  11.9 us
    all_to_all x1, blocking collectives, swap(): lax.all_to_all(value, 'rows', split_axis=0, concat_axis=0, tiled=True, ax...  9.81 us
    pallas_call x1, Pallas kernels, front(): pl.pallas_call(functools.partial(front_kernel, groups, heads, head_size,...  5.51 us
    ppermute x1, starting transfers between devices, shards(): mirrored = lax.ppermute(heads_first, 'rows', turn(row_size, half))  4.1 us
    pallas_call x2, Pallas kernels, last_tiles(): pl.pallas_call(functools.partial(last_kernel, slots, groups), out_shape=(...  3.72 us
    pallas_call x1, Pallas kernels, first_tiles(): pl.pallas_call(functools.partial(first_kernel, slots, rows if rows <= 512...  2.43 us
    ppermute x1, waiting for transfers between devices, shards(): lax.ppermute(other, 'cols', turn(col_size, step + 1))  2.04 us
  transfers between devices with their start and end apart: 17, of which 7 were waited for; matrix products, arithmetic and copies ran while one was open for 0% of the time, Pallas kernels for 18%

profile of v12, /device:TPU:0, one launch (start us, length us, event | category | flops | bytes accessed | tf_op | source)
XLA Modules:
  0.0 62.2 jit_solution(6530705151539609843)
XLA Ops:
  0.0 1.2 %copy.14 = bf16[4,128,4,128]{3,1,2,0:T(8,128)(2,1)S(1)} copy(bf16[4,128,4,128]{3,2,1,0:T(4,128)(2,1)} %param.17) | data formatting | bytes 1048576 | tf_op args[7]
  2.6 4.1 %collective-permute-start.8 = (bf16[4,4,128,128]{3,2,1,0:T(8,128)(2,1)S(1)}, bf16[4,4,128,128]{3,2,1,0:T(8,128)(2,1)S(1)}, u32[]{:S(2)}, u32[]{:S(2)}) collective-permute-start(bf16[4,4,128,128]{3,2,1,0:T(8,128)(2,1)S(1)} %tie.1.tiles_ref), channel_id=1, source_target_pairs={{0,16},{2,18},{4,20},{6,22},{8,24},{10,26},{12,28},{14,30},{16,0},... | collective-permute-start | bytes 1572872 | tf_op jit(solution)/shard_map/ppermute | solution.py:379
  6.7 1.5 %collective-permute-start = (bf16[48,4,512]{2,1,0:T(4,128)(2,1)S(1)}, bf16[48,4,512]{2,1,0:T(4,128)(2,1)S(1)}, u32[]{:S(2)}, u32[]{:S(2)}) collective-permute-start(bf16[48,4,512]{2,1,0:T(4,128)(2,1)S(1)} %copy-done.2), channel_id=1, source_target_pairs={{0,1},{1,0},{2,3},{3,2},{4,5},{5,4},{6,7},{7,6},{8,9},{9,8},{10,11... | collective-permute-start | bytes 589832 | tf_op jit(solution)/shard_map/ppermute | solution.py:383
  8.2 9.8 %all_to_all.5.wanted_ref = s32[8,2,128]{2,1,0:T(2,128)S(1)} all-to-all(s32[8,2,128]{2,1,0:T(2,128)S(1)} %request.1.after_ref), channel_id=1, replica_groups={{0,2,4,6,8,10,12,14},{16,18,20,22,24,26,28,30},{1,3,5,7,9,11,13,15},{17..., dimensions={0} | all-to-all | bytes 16384 | tf_op jit(solution)/shard_map/all_to_all | solution.py:374
  18.8 1.6 %collective-permute-start.2 = (bf16[1,4,128,128]{3,2,1,0:T(8,128)(2,1)S(1)}, bf16[1,4,128,128]{3,2,1,0:T(8,128)(2,1)S(1)}, u32[]{:S(2)}, u32[]{:S(2)}) collective-permute-start(bf16[1,4,128,128]{3,2,1,0:T(8,128)(2,1)S(1)} %get-tuple-element.29), channel_id=1, source_target_pairs={{0,4},{2,6},{4,0},{6,2},{8,12},{10,14},{12,8},{14,10},{16,20},{18,... | collective-permute-start | bytes 393224 | tf_op jit(solution)/shard_map/ppermute | solution.py:392
  20.4 2.5 %collective-permute-start.3 = (bf16[1,4,128,128]{3,2,1,0:T(8,128)(2,1)S(1)}, bf16[1,4,128,128]{3,2,1,0:T(8,128)(2,1)S(1)}, u32[]{:S(2)}, u32[]{:S(2)}) collective-permute-start(bf16[1,4,128,128]{3,2,1,0:T(8,128)(2,1)S(1)} %get-tuple-element.30), channel_id=1, source_target_pairs={{0,8},{2,10},{4,12},{6,14},{8,0},{10,2},{12,4},{14,6},{16,24},{18,... | collective-permute-start | bytes 393224 | tf_op jit(solution)/shard_map/ppermute | solution.py:392
  22.9 0.9 %collective-permute-start.4 = (bf16[1,4,128,128]{3,2,1,0:T(8,128)(2,1)S(1)}, bf16[1,4,128,128]{3,2,1,0:T(8,128)(2,1)S(1)}, u32[]{:S(2)}, u32[]{:S(2)}) collective-permute-start(bf16[1,4,128,128]{3,2,1,0:T(8,128)(2,1)S(1)} %get-tuple-element.31), channel_id=1, source_target_pairs={{0,12},{2,14},{4,8},{6,10},{8,4},{10,6},{12,0},{14,2},{16,28},{18,... | collective-permute-start | bytes 393224 | tf_op jit(solution)/shard_map/ppermute | solution.py:392
  23.7 5.5 %front.1 = (f32[192,512]{1,0:T(8,128)S(1)}, bf16[4,384,128]{2,1,0:T(8,128)(2,1)S(1)}) custom-call(bf16[48,4,512]{2,1,0:T(4,128)(2,1)} %refs_0_.1, bf16[48,4,512]{2,1,0:T(4,128)(2,1)S(1)} %collective-permute-done.refs_1_, s32[2]{0:T(128)S(1)} %pad_add_fusion.me_ref.refs_2_, s32[1,12]{1,0:T(1,128)} %refs_3_.1, s32[12,48]{1,0:T(8,128)} %bitcast.9, ...), custom_call_target="tpu_custom_call" | custom-call | flops 1006632960 | bytes 4194304 | tf_op jit(solution)/shard_map/front/pallas_call | solution.py:235
  29.3 1.3 %collective-permute-start.5 = (bf16[1,4,128,128]{3,2,1,0:T(8,128)(2,1)S(1)}, bf16[1,4,128,128]{3,2,1,0:T(8,128)(2,1)S(1)}, u32[]{:S(2)}, u32[]{:S(2)}) collective-permute-start(bf16[1,4,128,128]{3,2,1,0:T(8,128)(2,1)S(1)} %get-tuple-element.32), channel_id=1, source_target_pairs={{0,10},{2,8},{4,14},{6,12},{8,2},{10,0},{12,6},{14,4},{16,26},{18,... | collective-permute-start | bytes 393224 | tf_op jit(solution)/shard_map/ppermute | solution.py:392
  31.1 1.5 %collective-permute-start.7 = (bf16[1,4,128,128]{3,2,1,0:T(8,128)(2,1)S(1)}, bf16[1,4,128,128]{3,2,1,0:T(8,128)(2,1)S(1)}, u32[]{:S(2)}, u32[]{:S(2)}) collective-permute-start(bf16[1,4,128,128]{3,2,1,0:T(8,128)(2,1)S(1)} %get-tuple-element.34), channel_id=1, source_target_pairs={{0,6},{2,4},{4,2},{6,0},{8,14},{10,12},{12,10},{14,8},{16,22},{18,... | collective-permute-start | bytes 393224 | tf_op jit(solution)/shard_map/ppermute | solution.py:392
  32.6 0.7 %pick_each.3 = (bf16[1,4,128,128]{3,2,1,0:T(8,128)(2,1)S(1)}, bf16[1,4,128,128]{3,2,1,0:T(8,128)(2,1)S(1)}, bf16[1,4,128,128]{3,2,1,0:T(8,128)(2,1)S(1)}, bf16[1...) custom-call(s32[8,2,128]{2,1,0:T(2,128)S(1)} %all_to_all.5.wanted_re, ...), custom_call_target="tpu_custom_call" | custom-call | bytes 2097152 | tf_op jit(solution)/shard_map/pick_each/pallas_call | solution.py:113
  33.5 3.0 %collective-permute-done.4.refs_4_ = bf16[1,4,128,128]{3,2,1,0:T(8,128)(2,1)S(1)} collective-permute-done((bf16[1,4,128,128]{3,2,1,0:T(8,128)(2,1)S(1)}, bf16[1,4,128,128]{3,2,1,0:T(8,128)(2,1)S(1)}, u32[]{:S(2)}, u32[]{:S(2)}) %collective-permute-start.4) | collective-permute-done | bytes 131104 | tf_op jit(solution)/shard_map/ppermute | solution.py:392
  37.0 1.2 %collective-permute-done.5.refs_5_ = bf16[1,4,128,128]{3,2,1,0:T(8,128)(2,1)S(1)} collective-permute-done((bf16[1,4,128,128]{3,2,1,0:T(8,128)(2,1)S(1)}, bf16[1,4,128,128]{3,2,1,0:T(8,128)(2,1)S(1)}, u32[]{:S(2)}, u32[]{:S(2)}) %collective-permute-start.5) | collective-permute-done | bytes 131104 | tf_op jit(solution)/shard_map/ppermute | solution.py:392
  38.2 3.9 %collective-permute-done.6.refs_6_ = bf16[1,4,128,128]{3,2,1,0:T(8,128)(2,1)S(1)} collective-permute-done((bf16[1,4,128,128]{3,2,1,0:T(8,128)(2,1)S(1)}, bf16[1,4,128,128]{3,2,1,0:T(8,128)(2,1)S(1)}, u32[]{:S(2)}, u32[]{:S(2)}) %collective-permute-start.6) | collective-permute-done | bytes 131104 | tf_op jit(solution)/shard_map/ppermute | solution.py:392
  42.1 1.3 %collective-permute-start.13 = (bf16[1,4,128,128]{3,2,1,0:T(8,128)(2,1)S(1)}, bf16[1,4,128,128]{3,2,1,0:T(8,128)(2,1)S(1)}, u32[]{:S(2)}, u32[]{:S(2)}) collective-permute-start(bf16[1,4,128,128]{3,2,1,0:T(8,128)(2,1)S(1)} %get-tuple-element.42), channel_id=1, source_target_pairs={{0,10},{2,8},{4,14},{6,12},{8,2},{10,0},{12,6},{14,4},{16,26},{18,... | collective-permute-start | bytes 393224 | tf_op jit(solution)/shard_map/ppermute | solution.py:392
  43.4 1.1 %collective-permute-start.14 = (bf16[1,4,128,128]{3,2,1,0:T(8,128)(2,1)S(1)}, bf16[1,4,128,128]{3,2,1,0:T(8,128)(2,1)S(1)}, u32[]{:S(2)}, u32[]{:S(2)}) collective-permute-start(bf16[1,4,128,128]{3,2,1,0:T(8,128)(2,1)S(1)} %get-tuple-element.43), channel_id=1, source_target_pairs={{0,14},{2,12},{4,10},{6,8},{8,6},{10,4},{12,2},{14,0},{16,30},{18,... | collective-permute-start | bytes 393224 | tf_op jit(solution)/shard_map/ppermute | solution.py:392
  45.4 2.4 %first_tiles.1 = (f32[4,384,128]{2,1,0:T(8,128)S(1)}, f32[384,128]{1,0:T(8,128)S(1)}) custom-call(bf16[4,384,128]{2,1,0:T(8,128)(2,1)S(1)} %get-tuple-element.27.asked_ref.refs_0_, bf16[1,4,128,128]{3,2,1,0:T(8,128)(2,1)S(1)} %get-tuple-element.25.refs_10_.refs_0_, bf16[1,4,128,128]{3,2,1,0:T(8,128)(2,1)S(1)} %collective-permute-done.1.refs_1_, ...), custom_call_target="tpu_custom_call" | custom-call | flops 805306368 | bytes 4194304 | tf_op jit(solution)/shard_map/first_tiles/pallas_call | solution.py:284
  47.9 1.5 %collective-permute-done.12.refs_4_ = bf16[1,4,128,128]{3,2,1,0:T(8,128)(2,1)S(1)} collective-permute-done((bf16[1,4,128,128]{3,2,1,0:T(8,128)(2,1)S(1)}, bf16[1,4,128,128]{3,2,1,0:T(8,128)(2,1)S(1)}, u32[]{:S(2)}, u32[]{:S(2)}) %collective-permute-start.12) | collective-permute-done | bytes 131104 | tf_op jit(solution)/shard_map/ppermute | solution.py:392
  49.4 3.9 %collective-permute-done.14.refs_6_ = bf16[1,4,128,128]{3,2,1,0:T(8,128)(2,1)S(1)} collective-permute-done((bf16[1,4,128,128]{3,2,1,0:T(8,128)(2,1)S(1)}, bf16[1,4,128,128]{3,2,1,0:T(8,128)(2,1)S(1)}, u32[]{:S(2)}, u32[]{:S(2)}) %collective-permute-start.14) | collective-permute-done | bytes 131104 | tf_op jit(solution)/shard_map/ppermute | solution.py:392
  53.3 1.9 %last_tiles.2.refs_8_ = bf16[192,256]{1,0:T(8,128)(2,1)S(1)} custom-call(bf16[4,384,128]{2,1,0:T(8,128)(2,1)S(1)} %get-tuple-element.27.asked_ref.refs_0_, f32[4,384,128]{2,1,0:T(8,128)S(1)} %get-tuple-element.35.sums_ref, f32[384,128]{1,0:T(8,128)S(1)} %get-tuple-element.36.tops_ref, bf16[1,4,128,128]{3,2,1,0:T(8,128)(2,1)S(1)} %get-tuple-element.37.refs_0_, ...), custom_call_target="tpu_custom_call" | custom-call | flops 402653184 | bytes 4194304 | tf_op jit(solution)/shard_map/last_tiles/pallas_call | solution.py:321
  55.2 1.6 %collective-permute-start.16 = (bf16[192,256]{1,0:T(8,128)(2,1)S(1)}, bf16[192,256]{1,0:T(8,128)(2,1)S(1)}, u32[]{:S(2)}, u32[]{:S(2)}) collective-permute-start(bf16[192,256]{1,0:T(8,128)(2,1)S(1)} %last_tiles.2.refs_8_), channel_id=1, source_target_pairs={{0,1},{1,0},{2,3},{3,2},{4,5},{5,4},{6,7},{7,6},{8,9},{9,8},{10,11... | collective-permute-start | bytes 294920 | tf_op jit(solution)/shard_map/ppermute | solution.py:404
  56.8 1.9 %last_tiles.3.refs_0_ = bf16[192,256]{1,0:T(8,128)(2,1)S(1)} custom-call(bf16[4,384,128]{2,1,0:T(8,128)(2,1)S(1)} %get-tuple-element.27.asked_ref.refs_0_, f32[4,384,128]{2,1,0:T(8,128)S(1)} %get-tuple-element.35.sums_ref, f32[384,128]{1,0:T(8,128)S(1)} %get-tuple-element.36.tops_ref, bf16[1,4,128,128]{3,2,1,0:T(8,128)(2,1)S(1)} %get-tuple-element.37.refs_0_, ...), custom_call_target="tpu_custom_call" | custom-call | flops 402653184 | bytes 4194304 | tf_op jit(solution)/shard_map/last_tiles/pallas_call | solution.py:321
  58.7 2.0 %collective-permute-done.16.refs_1_ = bf16[192,256]{1,0:T(8,128)(2,1)S(1)} collective-permute-done((bf16[192,256]{1,0:T(8,128)(2,1)S(1)}, bf16[192,256]{1,0:T(8,128)(2,1)S(1)}, u32[]{:S(2)}, u32[]{:S(2)}) %collective-permute-start.16) | collective-permute-done | bytes 98336 | tf_op jit(solution)/shard_map/ppermute | solution.py:404
  60.7 1.5 %finish.1 = bf16[48,4,512]{2,1,0:T(4,128)(2,1)} custom-call(s32[2]{0:T(128)S(1)} %pad_add_fusion.me_ref.refs_2_, bf16[512,512]{1,0:T(8,128)(2,1)S(1)} %copy-done, f32[192,512]{1,0:T(8,128)S(1)} %get-tuple-element.26.resid_ref, bf16[192,256]{1,0:T(8,128)(2,1)S(1)} %last_tiles.3.refs_0_, bf16[192,256]{1,0:T(8,128)(2,1)S(1)} %collective-permute-done.16.refs_1_), custom_call_target="tpu_custom_call" | custom-call | flops 100663296 | bytes 1048576 | tf_op jit(solution)/shard_map/finish/pallas_call | solution.py:344
  (28 shorter events, 4.2 us)
Async XLA Ops:
  0.0 6.7 %copy-start.2 = (bf16[48,4,512]{2,1,0:T(4,128)(2,1)S(1)}, bf16[48,4,512]{2,1,0:T(4,128)(2,1)}, u32[]{:S(2)}) copy-start(bf16[48,4,512]{2,1,0:T(4,128)(2,1)} %refs_0_.1) | copy-start | bytes 589828
  1.3 0.7 %copy-start.1 = (s32[1,12]{1,0:T(1,128)S(1)}, s32[1,12]{1,0:T(1,128)}, u32[]{:S(2)}) copy-start(s32[1,12]{1,0:T(1,128)} %refs_3_.1) | copy-start | bytes 148
  2.6 28.5 %collective-permute-start.8 = (bf16[4,4,128,128]{3,2,1,0:T(8,128)(2,1)S(1)}, bf16[4,4,128,128]{3,2,1,0:T(8,128)(2,1)S(1)}, u32[]{:S(2)}, u32[]{:S(2)}) collective-permute-start(bf16[4,4,128,128]{3,2,1,0:T(8,128)(2,1)S(1)} %tie.1.tiles_ref), channel_id=1, source_target_pairs={{0,16},{2,18},{4,20},{6,22},{8,24},{10,26},{12,28},{14,30},{16,0},... | collective-permute-start | bytes 1572872 | tf_op jit(solution)/shard_map/ppermute | solution.py:379
  6.7 16.2 %collective-permute-start = (bf16[48,4,512]{2,1,0:T(4,128)(2,1)S(1)}, bf16[48,4,512]{2,1,0:T(4,128)(2,1)S(1)}, u32[]{:S(2)}, u32[]{:S(2)}) collective-permute-start(bf16[48,4,512]{2,1,0:T(4,128)(2,1)S(1)} %copy-done.2), channel_id=1, source_target_pairs={{0,1},{1,0},{2,3},{3,2},{4,5},{5,4},{6,7},{7,6},{8,9},{9,8},{10,11... | collective-permute-start | bytes 589832 | tf_op jit(solution)/shard_map/ppermute | solution.py:383
  18.8 10.5 %collective-permute-start.1 = (bf16[1,4,128,128]{3,2,1,0:T(8,128)(2,1)S(1)}, bf16[1,4,128,128]{3,2,1,0:T(8,128)(2,1)S(1)}, u32[]{:S(2)}, u32[]{:S(2)}) collective-permute-start(bf16[1,4,128,128]{3,2,1,0:T(8,128)(2,1)S(1)} %get-tuple-element.28), channel_id=1, source_target_pairs={{0,2},{2,0},{4,6},{6,4},{8,10},{10,8},{12,14},{14,12},{16,18},{18,... | collective-permute-start | bytes 393224 | tf_op jit(solution)/shard_map/ppermute | solution.py:392
  18.8 11.7 %collective-permute-start.2 = (bf16[1,4,128,128]{3,2,1,0:T(8,128)(2,1)S(1)}, bf16[1,4,128,128]{3,2,1,0:T(8,128)(2,1)S(1)}, u32[]{:S(2)}, u32[]{:S(2)}) collective-permute-start(bf16[1,4,128,128]{3,2,1,0:T(8,128)(2,1)S(1)} %get-tuple-element.29), channel_id=1, source_target_pairs={{0,4},{2,6},{4,0},{6,2},{8,12},{10,14},{12,8},{14,10},{16,20},{18,... | collective-permute-start | bytes 393224 | tf_op jit(solution)/shard_map/ppermute | solution.py:392
  20.4 13.0 %collective-permute-start.3 = (bf16[1,4,128,128]{3,2,1,0:T(8,128)(2,1)S(1)}, bf16[1,4,128,128]{3,2,1,0:T(8,128)(2,1)S(1)}, u32[]{:S(2)}, u32[]{:S(2)}) collective-permute-start(bf16[1,4,128,128]{3,2,1,0:T(8,128)(2,1)S(1)} %get-tuple-element.30), channel_id=1, source_target_pairs={{0,8},{2,10},{4,12},{6,14},{8,0},{10,2},{12,4},{14,6},{16,24},{18,... | collective-permute-start | bytes 393224 | tf_op jit(solution)/shard_map/ppermute | solution.py:392
  22.9 13.7 %collective-permute-start.4 = (bf16[1,4,128,128]{3,2,1,0:T(8,128)(2,1)S(1)}, bf16[1,4,128,128]{3,2,1,0:T(8,128)(2,1)S(1)}, u32[]{:S(2)}, u32[]{:S(2)}) collective-permute-start(bf16[1,4,128,128]{3,2,1,0:T(8,128)(2,1)S(1)} %get-tuple-element.31), channel_id=1, source_target_pairs={{0,12},{2,14},{4,8},{6,10},{8,4},{10,6},{12,0},{14,2},{16,28},{18,... | collective-permute-start | bytes 393224 | tf_op jit(solution)/shard_map/ppermute | solution.py:392
  29.3 8.9 %collective-permute-start.5 = (bf16[1,4,128,128]{3,2,1,0:T(8,128)(2,1)S(1)}, bf16[1,4,128,128]{3,2,1,0:T(8,128)(2,1)S(1)}, u32[]{:S(2)}, u32[]{:S(2)}) collective-permute-start(bf16[1,4,128,128]{3,2,1,0:T(8,128)(2,1)S(1)} %get-tuple-element.32), channel_id=1, source_target_pairs={{0,10},{2,8},{4,14},{6,12},{8,2},{10,0},{12,6},{14,4},{16,26},{18,... | collective-permute-start | bytes 393224 | tf_op jit(solution)/shard_map/ppermute | solution.py:392
  30.6 11.6 %collective-permute-start.6 = (bf16[1,4,128,128]{3,2,1,0:T(8,128)(2,1)S(1)}, bf16[1,4,128,128]{3,2,1,0:T(8,128)(2,1)S(1)}, u32[]{:S(2)}, u32[]{:S(2)}) collective-permute-start(bf16[1,4,128,128]{3,2,1,0:T(8,128)(2,1)S(1)} %get-tuple-element.33), channel_id=1, source_target_pairs={{0,14},{2,12},{4,10},{6,8},{8,6},{10,4},{12,2},{14,0},{16,30},{18,... | collective-permute-start | bytes 393224 | tf_op jit(solution)/shard_map/ppermute | solution.py:392
  31.1 11.0 %collective-permute-start.7 = (bf16[1,4,128,128]{3,2,1,0:T(8,128)(2,1)S(1)}, bf16[1,4,128,128]{3,2,1,0:T(8,128)(2,1)S(1)}, u32[]{:S(2)}, u32[]{:S(2)}) collective-permute-start(bf16[1,4,128,128]{3,2,1,0:T(8,128)(2,1)S(1)} %get-tuple-element.34), channel_id=1, source_target_pairs={{0,6},{2,4},{4,2},{6,0},{8,14},{10,12},{12,10},{14,8},{16,22},{18,... | collective-permute-start | bytes 393224 | tf_op jit(solution)/shard_map/ppermute | solution.py:392
  33.4 10.0 %collective-permute-start.9 = (bf16[1,4,128,128]{3,2,1,0:T(8,128)(2,1)S(1)}, bf16[1,4,128,128]{3,2,1,0:T(8,128)(2,1)S(1)}, u32[]{:S(2)}, u32[]{:S(2)}) collective-permute-start(bf16[1,4,128,128]{3,2,1,0:T(8,128)(2,1)S(1)} %get-tuple-element.38), channel_id=1, source_target_pairs={{0,2},{2,0},{4,6},{6,4},{8,10},{10,8},{12,14},{14,12},{16,18},{18,... | collective-permute-start | bytes 393224 | tf_op jit(solution)/shard_map/ppermute | solution.py:392
  36.5 8.3 %collective-permute-start.10 = (bf16[1,4,128,128]{3,2,1,0:T(8,128)(2,1)S(1)}, bf16[1,4,128,128]{3,2,1,0:T(8,128)(2,1)S(1)}, u32[]{:S(2)}, u32[]{:S(2)}) collective-permute-start(bf16[1,4,128,128]{3,2,1,0:T(8,128)(2,1)S(1)} %get-tuple-element.39), channel_id=1, source_target_pairs={{0,4},{2,6},{4,0},{6,2},{8,12},{10,14},{12,8},{14,10},{16,20},{18,... | collective-permute-start | bytes 393224 | tf_op jit(solution)/shard_map/ppermute | solution.py:392
  38.2 9.7 %collective-permute-start.11 = (bf16[1,4,128,128]{3,2,1,0:T(8,128)(2,1)S(1)}, bf16[1,4,128,128]{3,2,1,0:T(8,128)(2,1)S(1)}, u32[]{:S(2)}, u32[]{:S(2)}) collective-permute-start(bf16[1,4,128,128]{3,2,1,0:T(8,128)(2,1)S(1)} %get-tuple-element.40), channel_id=1, source_target_pairs={{0,8},{2,10},{4,12},{6,14},{8,0},{10,2},{12,4},{14,6},{16,24},{18,... | collective-permute-start | bytes 393224 | tf_op jit(solution)/shard_map/ppermute | solution.py:392
  42.1 7.3 %collective-permute-start.12 = (bf16[1,4,128,128]{3,2,1,0:T(8,128)(2,1)S(1)}, bf16[1,4,128,128]{3,2,1,0:T(8,128)(2,1)S(1)}, u32[]{:S(2)}, u32[]{:S(2)}) collective-permute-start(bf16[1,4,128,128]{3,2,1,0:T(8,128)(2,1)S(1)} %get-tuple-element.41), channel_id=1, source_target_pairs={{0,12},{2,14},{4,8},{6,10},{8,4},{10,6},{12,0},{14,2},{16,28},{18,... | collective-permute-start | bytes 393224 | tf_op jit(solution)/shard_map/ppermute | solution.py:392
  42.1 7.2 %collective-permute-start.13 = (bf16[1,4,128,128]{3,2,1,0:T(8,128)(2,1)S(1)}, bf16[1,4,128,128]{3,2,1,0:T(8,128)(2,1)S(1)}, u32[]{:S(2)}, u32[]{:S(2)}) collective-permute-start(bf16[1,4,128,128]{3,2,1,0:T(8,128)(2,1)S(1)} %get-tuple-element.42), channel_id=1, source_target_pairs={{0,10},{2,8},{4,14},{6,12},{8,2},{10,0},{12,6},{14,4},{16,26},{18,... | collective-permute-start | bytes 393224 | tf_op jit(solution)/shard_map/ppermute | solution.py:392
  43.4 9.9 %collective-permute-start.14 = (bf16[1,4,128,128]{3,2,1,0:T(8,128)(2,1)S(1)}, bf16[1,4,128,128]{3,2,1,0:T(8,128)(2,1)S(1)}, u32[]{:S(2)}, u32[]{:S(2)}) collective-permute-start(bf16[1,4,128,128]{3,2,1,0:T(8,128)(2,1)S(1)} %get-tuple-element.43), channel_id=1, source_target_pairs={{0,14},{2,12},{4,10},{6,8},{8,6},{10,4},{12,2},{14,0},{16,30},{18,... | collective-permute-start | bytes 393224 | tf_op jit(solution)/shard_map/ppermute | solution.py:392
  44.8 8.5 %collective-permute-start.15 = (bf16[1,4,128,128]{3,2,1,0:T(8,128)(2,1)S(1)}, bf16[1,4,128,128]{3,2,1,0:T(8,128)(2,1)S(1)}, u32[]{:S(2)}, u32[]{:S(2)}) collective-permute-start(bf16[1,4,128,128]{3,2,1,0:T(8,128)(2,1)S(1)} %get-tuple-element.44), channel_id=1, source_target_pairs={{0,6},{2,4},{4,2},{6,0},{8,14},{10,12},{12,10},{14,8},{16,22},{18,... | collective-permute-start | bytes 393224 | tf_op jit(solution)/shard_map/ppermute | solution.py:392
  55.2 5.5 %copy-start = (bf16[512,512]{1,0:T(8,128)(2,1)S(1)}, bf16[512,512]{1,0:T(8,128)(2,1)}, u32[]{:S(2)}) copy-start(bf16[512,512]{1,0:T(8,128)(2,1)} %weight_ref.1) | copy-start | bytes 1572868
  55.2 5.5 %collective-permute-start.16 = (bf16[192,256]{1,0:T(8,128)(2,1)S(1)}, bf16[192,256]{1,0:T(8,128)(2,1)S(1)}, u32[]{:S(2)}, u32[]{:S(2)}) collective-permute-start(bf16[192,256]{1,0:T(8,128)(2,1)S(1)} %last_tiles.2.refs_8_), channel_id=1, source_target_pairs={{0,1},{1,0},{2,3},{3,2},{4,5},{5,4},{6,7},{7,6},{8,9},{9,8},{10,11... | collective-permute-start | bytes 294920 | tf_op jit(solution)/shard_map/ppermute | solution.py:404

commit v13 on v12

--- a/solution.py
+++ b/solution.py
@@ -292,6 +292,39 @@
     )(asked, *tiles)
 
 
+def merge(asked_ref, sums_ref, tops_ref, tile_refs, slots, head, rows):
+    top, sums = weigh(asked_ref[head, rows, :], tile_refs, head, slots)
+    old_top = tops_ref[rows, head:head + 1]
+    new_top = jnp.maximum(top, old_top)
+    return new_top, sums_ref[head, rows, :] * jnp.exp(old_top - new_top) + sums * jnp.exp(top - new_top)
+
+
+def more_kernel(slots, block, asked_ref, old_sums_ref, old_tops_ref, *refs):
+    tile_refs, (sums_ref, tops_ref) = refs[:len(slots)], refs[len(slots):]
+    heads, rows_all, lanes = asked_ref.shape
+    lane = iota((block, lanes), 1)
+    for step in range(rows_all // block):
+        rows = pl.ds(step * block, block)
+        tops = jnp.zeros((block, lanes), jnp.float32)
+        for head in range(heads):
+            top, sums_ref[head, rows, :] = merge(asked_ref, old_sums_ref, old_tops_ref, tile_refs, slots, head, rows)
+            tops = jnp.where(lane == head, top, tops)
+        tops_ref[rows, :] = tops
+
+
+def more_tiles(asked, sums, tops, tiles, slots, own_rows):
+    rows = asked.shape[1]
+    return pl.pallas_call(
+        functools.partial(more_kernel, slots, rows if rows <= 512 else own_rows),
+        out_shape=(jax.ShapeDtypeStruct(sums.shape, jnp.float32), jax.ShapeDtypeStruct(tops.shape, jnp.float32)),
+        in_specs=[VMEM] * (3 + len(tiles)),
+        out_specs=(VMEM, VMEM),
+        compiler_params=params(rows),
+        cost_estimate=attention_cost(asked, tiles),
+        name="more_tiles",
+    )(asked, sums, tops, *tiles)
+
+
 def last_kernel(slots, groups, asked_ref, sums_ref, tops_ref, *refs):
     tile_refs, out_refs = refs[:len(slots)], refs[-len(groups):]
     heads, lanes = asked_ref.shape[0], asked_ref.shape[2]
@@ -302,10 +335,7 @@
         rows = pl.ds(group * block, block)
         low = None
         for head in range(heads):
-            top, sums = weigh(asked_ref[head, rows, :], tile_refs, head, slots)
-            old_top = tops_ref[rows, head:head + 1]
-            new_top = jnp.maximum(top, old_top)
-            sums = sums_ref[head, rows, :] * jnp.exp(old_top - new_top) + sums * jnp.exp(top - new_top)
+            _, sums = merge(asked_ref, sums_ref, tops_ref, tile_refs, slots, head, rows)
             turned = pltpu.roll(sums, half, 1)
             if head % 2:
                 out_ref[:, pl.ds(head // 2 * lanes, lanes)] = jnp.where(lane_low, low, sums / turned).astype(jnp.bfloat16)
@@ -382,7 +412,7 @@
     for step in range(1, col_size):
         cells.append(lax.ppermute(fact_cells, "cols", turn(col_size, -step)))
 
-    order = [0, 1] + sorted(range(2, half), key=lambda step: (step != 2, not step & half // 2, step & 1, step))
+    order = [0] + sorted(range(1, half), key=lambda step: (not step & half // 2, step & 1, -(step & 2) if step < half // 2 else step))
     near_slots, far_slots = (order, [half + step for step in order]) if paired else ([0], [half])
 
     def spread(tiles, which, after):
@@ -394,11 +424,15 @@
 
     if group_width % 128:
         w_query = lax.dynamic_slice_in_dim(w_query, col_me * group_width, group_width, 1)
-    near = spread(heads_first, 0, [])
+    near = spread(heads_first, 0, cells[1:])
     residual, asked = front(cells, tile_ids, me, key_mask, gain_col, w_qkv, w_col_out, gain_tile, w_query,
                             heads_all, head_size, cols, heads_here, tiles_here, row_size, paired, near[0])
     far = spread(mirrored, 1, [asked] + near[1:3])
     sums, tops = first_tiles(asked, near, near_slots, rows * cols)
+    batch = len(far) // 2
+    if batch:
+        sums, tops = more_tiles(asked, sums, tops, far[:batch], far_slots[:batch], rows * cols)
+    far, far_slots = far[batch:], far_slots[batch:]
     others = last_tiles(asked, sums, tops, far, far_slots, list(range(1, col_size)), rows * cols, [])
     own = last_tiles(asked, sums, tops, far, far_slots, [0], rows * cols, others[:1])
     answers = list(own) + [lax.ppermute(other, "cols", turn(col_size, step + 1)) for step, other in enumerate(others)]

time: 62.4 us -> 66.4 us (1.064)
  waiting for transfers between devices: 16 us -> 18 us
  Pallas kernels: 15.3 us -> 16.5 us
  starting transfers between devices: 19.1 us -> 19.9 us
    ppermute x14, waiting for transfers between devices: 13.9 us -> 16.1 us  [spread(): lax.ppermute(tile, 'rows', [(row, row ^ step) for row in range(row_size)])]
    pallas_call x0 -> x1, Pallas kernels: none -> 2.03 us  [more_tiles(): pl.pallas_call(functools.partial(more_kernel, slots, rows if rows <= 512...]
    pallas_call x2, Pallas kernels: 3.72 us -> 2.89 us  [last_tiles(): pl.pallas_call(functools.partial(last_kernel, slots, groups), out_shape=(...]
    ppermute x14, starting transfers between devices: 11.9 us -> 12.7 us  [spread(): lax.ppermute(tile, 'rows', [(row, row ^ step) for row in range(row_size)])]
  transfers between devices with their start and end apart: 17 -> 17, of which waited for: 7 -> 7; matrix products, arithmetic and copies ran while one was open for 0% -> 0% of each run, Pallas kernels for 18% -> 19%
where the time goes in v13:
time: 66.4 us; the launch traced here: 66.2 us
  starting transfers between devices  19.9 us (30%)
  waiting for transfers between devices  18 us (27%)
  Pallas kernels  16.5 us (25%)
  blocking collectives  9.81 us (15%)
  local copies, waits for them, and re-layouts  1.84 us (3%)
    ppermute x14, waiting for transfers between devices, spread(): lax.ppermute(tile, 'rows', [(row, row ^ step) for row in range(row_size)])  16.1 us
    ppermute x14, starting transfers between devices, spread(): lax.ppermute(tile, 'rows', [(row, row ^ step) for row in range(row_size)])  12.7 us
    all_to_all x1, blocking collectives, swap(): lax.all_to_all(value, 'rows', split_axis=0, concat_axis=0, tiled=True, ax...  9.81 us
    pallas_call x1, Pallas kernels, front(): pl.pallas_call(functools.partial(front_kernel, groups, heads, head_size,...  5.51 us
    ppermute x1, starting transfers between devices, shards(): mirrored = lax.ppermute(heads_first, 'rows', turn(row_size, half))  4.1 us
    pallas_call x2, Pallas kernels, last_tiles(): pl.pallas_call(functools.partial(last_kernel, slots, groups), out_shape=(...  2.89 us
    pallas_call x1, Pallas kernels, first_tiles(): pl.pallas_call(functools.partial(first_kernel, slots, rows if rows <= 512...  2.4 us
    pallas_call x1, Pallas kernels, more_tiles(): pl.pallas_call(functools.partial(more_kernel, slots, rows if rows <= 512...  2.03 us
  transfers between devices with their start and end apart: 17, of which 7 were waited for; matrix products, arithmetic and copies ran while one was open for 0% of the time, Pallas kernels for 19%

profile of v13, /device:TPU:0, one launch (start us, length us, event | category | flops | bytes accessed | tf_op | source)
XLA Modules:
  0.0 66.2 jit_solution(11009043734512435192)
XLA Ops:
  0.0 1.2 %copy.14 = bf16[4,128,4,128]{3,1,2,0:T(8,128)(2,1)S(1)} copy(bf16[4,128,4,128]{3,2,1,0:T(4,128)(2,1)} %param.17) | data formatting | bytes 1048576 | tf_op args[7]
  2.6 4.1 %collective-permute-start.8 = (bf16[4,4,128,128]{3,2,1,0:T(8,128)(2,1)S(1)}, bf16[4,4,128,128]{3,2,1,0:T(8,128)(2,1)S(1)}, u32[]{:S(2)}, u32[]{:S(2)}) collective-permute-start(bf16[4,4,128,128]{3,2,1,0:T(8,128)(2,1)S(1)} %tie.1.tiles_ref), channel_id=1, source_target_pairs={{0,16},{2,18},{4,20},{6,22},{8,24},{10,26},{12,28},{14,30},{16,0},... | collective-permute-start | bytes 1572872 | tf_op jit(solution)/shard_map/ppermute | solution.py:409
  6.7 1.5 %collective-permute-start = (bf16[48,4,512]{2,1,0:T(4,128)(2,1)S(1)}, bf16[48,4,512]{2,1,0:T(4,128)(2,1)S(1)}, u32[]{:S(2)}, u32[]{:S(2)}) collective-permute-start(bf16[48,4,512]{2,1,0:T(4,128)(2,1)S(1)} %copy-done.2), channel_id=1, source_target_pairs={{0,1},{1,0},{2,3},{3,2},{4,5},{5,4},{6,7},{7,6},{8,9},{9,8},{10,11... | collective-permute-start | bytes 589832 | tf_op jit(solution)/shard_map/ppermute | solution.py:413
  8.2 9.8 %all_to_all.5.wanted_ref = s32[8,2,128]{2,1,0:T(2,128)S(1)} all-to-all(s32[8,2,128]{2,1,0:T(2,128)S(1)} %request.1.after_ref), channel_id=1, replica_groups={{0,2,4,6,8,10,12,14},{16,18,20,22,24,26,28,30},{1,3,5,7,9,11,13,15},{17..., dimensions={0} | all-to-all | bytes 16384 | tf_op jit(solution)/shard_map/all_to_all | solution.py:404
  18.0 0.7 %pick_each.2 = (bf16[1,4,128,128]{3,2,1,0:T(8,128)(2,1)S(1)}, bf16[1,4,128,128]{3,2,1,0:T(8,128)(2,1)S(1)}, bf16[1,4,128,128]{3,2,1,0:T(8,128)(2,1)S(1)}, bf16[1...) custom-call(s32[8,2,128]{2,1,0:T(2,128)S(1)} %all_to_all.5.wanted_re, ...), custom_call_target="tpu_custom_call" | custom-call | bytes 2097152 | tf_op jit(solution)/shard_map/pick_each/pallas_call | solution.py:113
  18.8 3.4 %collective-permute-start.1 = (bf16[1,4,128,128]{3,2,1,0:T(8,128)(2,1)S(1)}, bf16[1,4,128,128]{3,2,1,0:T(8,128)(2,1)S(1)}, u32[]{:S(2)}, u32[]{:S(2)}) collective-permute-start(bf16[1,4,128,128]{3,2,1,0:T(8,128)(2,1)S(1)} %get-tuple-element.30), channel_id=1, source_target_pairs={{0,8},{2,10},{4,12},{6,14},{8,0},{10,2},{12,4},{14,6},{16,24},{18,... | collective-permute-start | bytes 393224 | tf_op jit(solution)/shard_map/ppermute | solution.py:422
  22.3 1.1 %collective-permute-start.3 = (bf16[1,4,128,128]{3,2,1,0:T(8,128)(2,1)S(1)}, bf16[1,4,128,128]{3,2,1,0:T(8,128)(2,1)S(1)}, u32[]{:S(2)}, u32[]{:S(2)}) collective-permute-start(bf16[1,4,128,128]{3,2,1,0:T(8,128)(2,1)S(1)} %get-tuple-element.32), channel_id=1, source_target_pairs={{0,10},{2,8},{4,14},{6,12},{8,2},{10,0},{12,6},{14,4},{16,26},{18,... | collective-permute-start | bytes 393224 | tf_op jit(solution)/shard_map/ppermute | solution.py:422
  23.3 1.6 %collective-permute-start.4 = (bf16[1,4,128,128]{3,2,1,0:T(8,128)(2,1)S(1)}, bf16[1,4,128,128]{3,2,1,0:T(8,128)(2,1)S(1)}, u32[]{:S(2)}, u32[]{:S(2)}) collective-permute-start(bf16[1,4,128,128]{3,2,1,0:T(8,128)(2,1)S(1)} %get-tuple-element.33), channel_id=1, source_target_pairs={{0,14},{2,12},{4,10},{6,8},{8,6},{10,4},{12,2},{14,0},{16,30},{18,... | collective-permute-start | bytes 393224 | tf_op jit(solution)/shard_map/ppermute | solution.py:422
  24.9 7.8 %collective-permute-done.1.refs_1_ = bf16[1,4,128,128]{3,2,1,0:T(8,128)(2,1)S(1)} collective-permute-done((bf16[1,4,128,128]{3,2,1,0:T(8,128)(2,1)S(1)}, bf16[1,4,128,128]{3,2,1,0:T(8,128)(2,1)S(1)}, u32[]{:S(2)}, u32[]{:S(2)}) %collective-permute-start.1) | collective-permute-done | bytes 131104 | tf_op jit(solution)/shard_map/ppermute | solution.py:422
  32.7 1.5 %collective-permute-start.5 = (bf16[1,4,128,128]{3,2,1,0:T(8,128)(2,1)S(1)}, bf16[1,4,128,128]{3,2,1,0:T(8,128)(2,1)S(1)}, u32[]{:S(2)}, u32[]{:S(2)}) collective-permute-start(bf16[1,4,128,128]{3,2,1,0:T(8,128)(2,1)S(1)} %get-tuple-element.34), channel_id=1, source_target_pairs={{0,4},{2,6},{4,0},{6,2},{8,12},{10,14},{12,8},{14,10},{16,20},{18,... | collective-permute-start | bytes 393224 | tf_op jit(solution)/shard_map/ppermute | solution.py:422
  34.2 5.5 %front.1 = (f32[192,512]{1,0:T(8,128)S(1)}, bf16[4,384,128]{2,1,0:T(8,128)(2,1)S(1)}) custom-call(bf16[48,4,512]{2,1,0:T(4,128)(2,1)} %refs_0_.1, bf16[48,4,512]{2,1,0:T(4,128)(2,1)S(1)} %collective-permute-done.refs_0_.refs_1_, s32[2]{0:T(128)S(1)} %pad_add_fusion.me_ref.refs_2_, s32[1,12]{1,0:T(1,128)} %refs_3_.1, s32[12,48]{1,0:T(8,128)} %bitcast.9, ...), custom_call_target="tpu_custom_call" | custom-call | flops 1006632960 | bytes 4194304 | tf_op jit(solution)/shard_map/front/pallas_call | solution.py:235
  40.4 0.7 %pick_each.3 = (bf16[1,4,128,128]{3,2,1,0:T(8,128)(2,1)S(1)}, bf16[1,4,128,128]{3,2,1,0:T(8,128)(2,1)S(1)}, bf16[1,4,128,128]{3,2,1,0:T(8,128)(2,1)S(1)}, bf16[1...) custom-call(s32[8,2,128]{2,1,0:T(2,128)S(1)} %all_to_all.5.wanted_re, ...), custom_call_target="tpu_custom_call" | custom-call | bytes 2097152 | tf_op jit(solution)/shard_map/pick_each/pallas_call | solution.py:113
  42.0 2.3 %collective-permute-start.10 = (bf16[1,4,128,128]{3,2,1,0:T(8,128)(2,1)S(1)}, bf16[1,4,128,128]{3,2,1,0:T(8,128)(2,1)S(1)}, u32[]{:S(2)}, u32[]{:S(2)}) collective-permute-start(bf16[1,4,128,128]{3,2,1,0:T(8,128)(2,1)S(1)} %get-tuple-element.41), channel_id=1, source_target_pairs={{0,12},{2,14},{4,8},{6,10},{8,4},{10,6},{12,0},{14,2},{16,28},{18,... | collective-permute-start | bytes 393224 | tf_op jit(solution)/shard_map/ppermute | solution.py:422
  44.3 1.2 %collective-permute-done.6.refs_6_ = bf16[1,4,128,128]{3,2,1,0:T(8,128)(2,1)S(1)} collective-permute-done((bf16[1,4,128,128]{3,2,1,0:T(8,128)(2,1)S(1)}, bf16[1,4,128,128]{3,2,1,0:T(8,128)(2,1)S(1)}, u32[]{:S(2)}, u32[]{:S(2)}) %collective-permute-start.6) | collective-permute-done | bytes 131104 | tf_op jit(solution)/shard_map/ppermute | solution.py:422
  46.0 1.5 %collective-permute-start.13 = (bf16[1,4,128,128]{3,2,1,0:T(8,128)(2,1)S(1)}, bf16[1,4,128,128]{3,2,1,0:T(8,128)(2,1)S(1)}, u32[]{:S(2)}, u32[]{:S(2)}) collective-permute-start(bf16[1,4,128,128]{3,2,1,0:T(8,128)(2,1)S(1)} %get-tuple-element.46), channel_id=1, source_target_pairs={{0,4},{2,6},{4,0},{6,2},{8,12},{10,14},{12,8},{14,10},{16,20},{18,... | collective-permute-start | bytes 393224 | tf_op jit(solution)/shard_map/ppermute | solution.py:422
  47.6 3.8 %collective-permute-done.10.refs_2_ = bf16[1,4,128,128]{3,2,1,0:T(8,128)(2,1)S(1)} collective-permute-done((bf16[1,4,128,128]{3,2,1,0:T(8,128)(2,1)S(1)}, bf16[1,4,128,128]{3,2,1,0:T(8,128)(2,1)S(1)}, u32[]{:S(2)}, u32[]{:S(2)}) %collective-permute-start.10) | collective-permute-done | bytes 131104 | tf_op jit(solution)/shard_map/ppermute | solution.py:422
  51.4 2.4 %first_tiles.1 = (f32[4,384,128]{2,1,0:T(8,128)S(1)}, f32[384,128]{1,0:T(8,128)S(1)}) custom-call(bf16[4,384,128]{2,1,0:T(8,128)(2,1)S(1)} %get-tuple-element.29.asked_ref.refs_0_, bf16[1,4,128,128]{3,2,1,0:T(8,128)(2,1)S(1)} %get-tuple-element.27.refs_10_.refs_0_, bf16[1,4,128,128]{3,2,1,0:T(8,128)(2,1)S(1)} %collective-permute-done.1.refs_1_, ...), custom_call_target="tpu_custom_call" | custom-call | flops 805306368 | bytes 4194304 | tf_op jit(solution)/shard_map/first_tiles/pallas_call | solution.py:284
  53.8 2.0 %more_tiles.1 = (f32[4,384,128]{2,1,0:T(8,128)S(1)}, f32[384,128]{1,0:T(8,128)S(1)}) custom-call(bf16[4,384,128]{2,1,0:T(8,128)(2,1)S(1)} %get-tuple-element.29.asked_ref.refs_0_, f32[4,384,128]{2,1,0:T(8,128)S(1)} %get-tuple-element.37.old_sums_ref, f32[384,128]{1,0:T(8,128)S(1)} %get-tuple-element.38.old_tops_ref, ...), custom_call_target="tpu_custom_call" | custom-call | flops 402653184 | bytes 4194304 | tf_op jit(solution)/shard_map/more_tiles/pallas_call | solution.py:317
  55.9 2.4 %collective-permute-done.14.refs_2_ = bf16[1,4,128,128]{3,2,1,0:T(8,128)(2,1)S(1)} collective-permute-done((bf16[1,4,128,128]{3,2,1,0:T(8,128)(2,1)S(1)}, bf16[1,4,128,128]{3,2,1,0:T(8,128)(2,1)S(1)}, u32[]{:S(2)}, u32[]{:S(2)}) %collective-permute-start.14) | collective-permute-done | bytes 131104 | tf_op jit(solution)/shard_map/ppermute | solution.py:422
  58.3 1.4 %last_tiles.2.refs_4_ = bf16[192,256]{1,0:T(8,128)(2,1)S(1)} custom-call(bf16[4,384,128]{2,1,0:T(8,128)(2,1)S(1)} %get-tuple-element.29.asked_ref.refs_0_, f32[4,384,128]{2,1,0:T(8,128)S(1)} %get-tuple-element.43.sums_ref, f32[384,128]{1,0:T(8,128)S(1)} %get-tuple-element.44.tops_ref, bf16[1,4,128,128]{3,2,1,0:T(8,128)(2,1)S(1)} %collective-permute-done.12.refs_0_, ...), custom_call_target="tpu_custom_call" | custom-call | flops 201326592 | bytes 4194304 | tf_op jit(solution)/shard_map/last_tiles/pallas_call | solution.py:351
  59.8 1.6 %collective-permute-start.16 = (bf16[192,256]{1,0:T(8,128)(2,1)S(1)}, bf16[192,256]{1,0:T(8,128)(2,1)S(1)}, u32[]{:S(2)}, u32[]{:S(2)}) collective-permute-start(bf16[192,256]{1,0:T(8,128)(2,1)S(1)} %last_tiles.2.refs_4_), channel_id=1, source_target_pairs={{0,1},{1,0},{2,3},{3,2},{4,5},{5,4},{6,7},{7,6},{8,9},{9,8},{10,11... | collective-permute-start | bytes 294920 | tf_op jit(solution)/shard_map/ppermute | solution.py:438
  61.3 1.4 %last_tiles.3.refs_0_ = bf16[192,256]{1,0:T(8,128)(2,1)S(1)} custom-call(bf16[4,384,128]{2,1,0:T(8,128)(2,1)S(1)} %get-tuple-element.29.asked_ref.refs_0_, f32[4,384,128]{2,1,0:T(8,128)S(1)} %get-tuple-element.43.sums_ref, f32[384,128]{1,0:T(8,128)S(1)} %get-tuple-element.44.tops_ref, bf16[1,4,128,128]{3,2,1,0:T(8,128)(2,1)S(1)} %collective-permute-done.12.refs_0_, ...), custom_call_target="tpu_custom_call" | custom-call | flops 201326592 | bytes 4194304 | tf_op jit(solution)/shard_map/last_tiles/pallas_call | solution.py:351
  62.8 1.9 %collective-permute-done.16.refs_1_ = bf16[192,256]{1,0:T(8,128)(2,1)S(1)} collective-permute-done((bf16[192,256]{1,0:T(8,128)(2,1)S(1)}, bf16[192,256]{1,0:T(8,128)(2,1)S(1)}, u32[]{:S(2)}, u32[]{:S(2)}) %collective-permute-start.16) | collective-permute-done | bytes 98336 | tf_op jit(solution)/shard_map/ppermute | solution.py:438
  64.7 1.5 %finish.1 = bf16[48,4,512]{2,1,0:T(4,128)(2,1)} custom-call(s32[2]{0:T(128)S(1)} %pad_add_fusion.me_ref.refs_2_, bf16[512,512]{1,0:T(8,128)(2,1)S(1)} %copy-done, f32[192,512]{1,0:T(8,128)S(1)} %get-tuple-element.28.resid_ref, bf16[192,256]{1,0:T(8,128)(2,1)S(1)} %last_tiles.3.refs_0_, bf16[192,256]{1,0:T(8,128)(2,1)S(1)} %collective-permute-done.16.refs_1_), custom_call_target="tpu_custom_call" | custom-call | flops 100663296 | bytes 1048576 | tf_op jit(solution)/shard_map/finish/pallas_call | solution.py:374
  (29 shorter events, 3.5 us)
Async XLA Ops:
  0.0 6.7 %copy-start.2 = (bf16[48,4,512]{2,1,0:T(4,128)(2,1)S(1)}, bf16[48,4,512]{2,1,0:T(4,128)(2,1)}, u32[]{:S(2)}) copy-start(bf16[48,4,512]{2,1,0:T(4,128)(2,1)} %refs_0_.1) | copy-start | bytes 589828
  1.3 0.7 copy-start.1
  2.6 37.3 %collective-permute-start.8 = (bf16[4,4,128,128]{3,2,1,0:T(8,128)(2,1)S(1)}, bf16[4,4,128,128]{3,2,1,0:T(8,128)(2,1)S(1)}, u32[]{:S(2)}, u32[]{:S(2)}) collective-permute-start(bf16[4,4,128,128]{3,2,1,0:T(8,128)(2,1)S(1)} %tie.1.tiles_ref), channel_id=1, source_target_pairs={{0,16},{2,18},{4,20},{6,22},{8,24},{10,26},{12,28},{14,30},{16,0},... | collective-permute-start | bytes 1572872 | tf_op jit(solution)/shard_map/ppermute | solution.py:409
  6.7 11.3 %collective-permute-start = (bf16[48,4,512]{2,1,0:T(4,128)(2,1)S(1)}, bf16[48,4,512]{2,1,0:T(4,128)(2,1)S(1)}, u32[]{:S(2)}, u32[]{:S(2)}) collective-permute-start(bf16[48,4,512]{2,1,0:T(4,128)(2,1)S(1)} %copy-done.2), channel_id=1, source_target_pairs={{0,1},{1,0},{2,3},{3,2},{4,5},{5,4},{6,7},{7,6},{8,9},{9,8},{10,11... | collective-permute-start | bytes 589832 | tf_op jit(solution)/shard_map/ppermute | solution.py:413
  18.8 14.0 %collective-permute-start.1 = (bf16[1,4,128,128]{3,2,1,0:T(8,128)(2,1)S(1)}, bf16[1,4,128,128]{3,2,1,0:T(8,128)(2,1)S(1)}, u32[]{:S(2)}, u32[]{:S(2)}) collective-permute-start(bf16[1,4,128,128]{3,2,1,0:T(8,128)(2,1)S(1)} %get-tuple-element.30), channel_id=1, source_target_pairs={{0,8},{2,10},{4,12},{6,14},{8,0},{10,2},{12,4},{14,6},{16,24},{18,... | collective-permute-start | bytes 393224 | tf_op jit(solution)/shard_map/ppermute | solution.py:422
  22.2 17.6 %collective-permute-start.2 = (bf16[1,4,128,128]{3,2,1,0:T(8,128)(2,1)S(1)}, bf16[1,4,128,128]{3,2,1,0:T(8,128)(2,1)S(1)}, u32[]{:S(2)}, u32[]{:S(2)}) collective-permute-start(bf16[1,4,128,128]{3,2,1,0:T(8,128)(2,1)S(1)} %get-tuple-element.31), channel_id=1, source_target_pairs={{0,12},{2,14},{4,8},{6,10},{8,4},{10,6},{12,0},{14,2},{16,28},{18,... | collective-permute-start | bytes 393224 | tf_op jit(solution)/shard_map/ppermute | solution.py:422
  22.3 18.9 %collective-permute-start.3 = (bf16[1,4,128,128]{3,2,1,0:T(8,128)(2,1)S(1)}, bf16[1,4,128,128]{3,2,1,0:T(8,128)(2,1)S(1)}, u32[]{:S(2)}, u32[]{:S(2)}) collective-permute-start(bf16[1,4,128,128]{3,2,1,0:T(8,128)(2,1)S(1)} %get-tuple-element.32), channel_id=1, source_target_pairs={{0,10},{2,8},{4,14},{6,12},{8,2},{10,0},{12,6},{14,4},{16,26},{18,... | collective-permute-start | bytes 393224 | tf_op jit(solution)/shard_map/ppermute | solution.py:422
  23.3 18.6 %collective-permute-start.4 = (bf16[1,4,128,128]{3,2,1,0:T(8,128)(2,1)S(1)}, bf16[1,4,128,128]{3,2,1,0:T(8,128)(2,1)S(1)}, u32[]{:S(2)}, u32[]{:S(2)}) collective-permute-start(bf16[1,4,128,128]{3,2,1,0:T(8,128)(2,1)S(1)} %get-tuple-element.33), channel_id=1, source_target_pairs={{0,14},{2,12},{4,10},{6,8},{8,6},{10,4},{12,2},{14,0},{16,30},{18,... | collective-permute-start | bytes 393224 | tf_op jit(solution)/shard_map/ppermute | solution.py:422
  32.7 11.6 %collective-permute-start.5 = (bf16[1,4,128,128]{3,2,1,0:T(8,128)(2,1)S(1)}, bf16[1,4,128,128]{3,2,1,0:T(8,128)(2,1)S(1)}, u32[]{:S(2)}, u32[]{:S(2)}) collective-permute-start(bf16[1,4,128,128]{3,2,1,0:T(8,128)(2,1)S(1)} %get-tuple-element.34), channel_id=1, source_target_pairs={{0,4},{2,6},{4,0},{6,2},{8,12},{10,14},{12,8},{14,10},{16,20},{18,... | collective-permute-start | bytes 393224 | tf_op jit(solution)/shard_map/ppermute | solution.py:422
  39.8 5.8 %collective-permute-start.6 = (bf16[1,4,128,128]{3,2,1,0:T(8,128)(2,1)S(1)}, bf16[1,4,128,128]{3,2,1,0:T(8,128)(2,1)S(1)}, u32[]{:S(2)}, u32[]{:S(2)}) collective-permute-start(bf16[1,4,128,128]{3,2,1,0:T(8,128)(2,1)S(1)} %get-tuple-element.35), channel_id=1, source_target_pairs={{0,6},{2,4},{4,2},{6,0},{8,14},{10,12},{12,10},{14,8},{16,22},{18,... | collective-permute-start | bytes 393224 | tf_op jit(solution)/shard_map/ppermute | solution.py:422
  39.8 6.1 %collective-permute-start.7 = (bf16[1,4,128,128]{3,2,1,0:T(8,128)(2,1)S(1)}, bf16[1,4,128,128]{3,2,1,0:T(8,128)(2,1)S(1)}, u32[]{:S(2)}, u32[]{:S(2)}) collective-permute-start(bf16[1,4,128,128]{3,2,1,0:T(8,128)(2,1)S(1)} %get-tuple-element.36), channel_id=1, source_target_pairs={{0,2},{2,0},{4,6},{6,4},{8,10},{10,8},{12,14},{14,12},{16,18},{18,... | collective-permute-start | bytes 393224 | tf_op jit(solution)/shard_map/ppermute | solution.py:422
  41.2 6.4 %collective-permute-start.9 = (bf16[1,4,128,128]{3,2,1,0:T(8,128)(2,1)S(1)}, bf16[1,4,128,128]{3,2,1,0:T(8,128)(2,1)S(1)}, u32[]{:S(2)}, u32[]{:S(2)}) collective-permute-start(bf16[1,4,128,128]{3,2,1,0:T(8,128)(2,1)S(1)} %get-tuple-element.40), channel_id=1, source_target_pairs={{0,8},{2,10},{4,12},{6,14},{8,0},{10,2},{12,4},{14,6},{16,24},{18,... | collective-permute-start | bytes 393224 | tf_op jit(solution)/shard_map/ppermute | solution.py:422
  42.0 9.4 %collective-permute-start.10 = (bf16[1,4,128,128]{3,2,1,0:T(8,128)(2,1)S(1)}, bf16[1,4,128,128]{3,2,1,0:T(8,128)(2,1)S(1)}, u32[]{:S(2)}, u32[]{:S(2)}) collective-permute-start(bf16[1,4,128,128]{3,2,1,0:T(8,128)(2,1)S(1)} %get-tuple-element.41), channel_id=1, source_target_pairs={{0,12},{2,14},{4,8},{6,10},{8,4},{10,6},{12,0},{14,2},{16,28},{18,... | collective-permute-start | bytes 393224 | tf_op jit(solution)/shard_map/ppermute | solution.py:422
  44.3 9.6 %collective-permute-start.11 = (bf16[1,4,128,128]{3,2,1,0:T(8,128)(2,1)S(1)}, bf16[1,4,128,128]{3,2,1,0:T(8,128)(2,1)S(1)}, u32[]{:S(2)}, u32[]{:S(2)}) collective-permute-start(bf16[1,4,128,128]{3,2,1,0:T(8,128)(2,1)S(1)} %get-tuple-element.42), channel_id=1, source_target_pairs={{0,10},{2,8},{4,14},{6,12},{8,2},{10,0},{12,6},{14,4},{16,26},{18,... | collective-permute-start | bytes 393224 | tf_op jit(solution)/shard_map/ppermute | solution.py:422
  45.5 10.4 %collective-permute-start.12 = (bf16[1,4,128,128]{3,2,1,0:T(8,128)(2,1)S(1)}, bf16[1,4,128,128]{3,2,1,0:T(8,128)(2,1)S(1)}, u32[]{:S(2)}, u32[]{:S(2)}) collective-permute-start(bf16[1,4,128,128]{3,2,1,0:T(8,128)(2,1)S(1)} %get-tuple-element.45), channel_id=1, source_target_pairs={{0,14},{2,12},{4,10},{6,8},{8,6},{10,4},{12,2},{14,0},{16,30},{18,... | collective-permute-start | bytes 393224 | tf_op jit(solution)/shard_map/ppermute | solution.py:422
  46.0 9.9 %collective-permute-start.13 = (bf16[1,4,128,128]{3,2,1,0:T(8,128)(2,1)S(1)}, bf16[1,4,128,128]{3,2,1,0:T(8,128)(2,1)S(1)}, u32[]{:S(2)}, u32[]{:S(2)}) collective-permute-start(bf16[1,4,128,128]{3,2,1,0:T(8,128)(2,1)S(1)} %get-tuple-element.46), channel_id=1, source_target_pairs={{0,4},{2,6},{4,0},{6,2},{8,12},{10,14},{12,8},{14,10},{16,20},{18,... | collective-permute-start | bytes 393224 | tf_op jit(solution)/shard_map/ppermute | solution.py:422
  47.6 10.7 %collective-permute-start.14 = (bf16[1,4,128,128]{3,2,1,0:T(8,128)(2,1)S(1)}, bf16[1,4,128,128]{3,2,1,0:T(8,128)(2,1)S(1)}, u32[]{:S(2)}, u32[]{:S(2)}) collective-permute-start(bf16[1,4,128,128]{3,2,1,0:T(8,128)(2,1)S(1)} %get-tuple-element.47), channel_id=1, source_target_pairs={{0,6},{2,4},{4,2},{6,0},{8,14},{10,12},{12,10},{14,8},{16,22},{18,... | collective-permute-start | bytes 393224 | tf_op jit(solution)/shard_map/ppermute | solution.py:422
  51.4 6.9 %collective-permute-start.15 = (bf16[1,4,128,128]{3,2,1,0:T(8,128)(2,1)S(1)}, bf16[1,4,128,128]{3,2,1,0:T(8,128)(2,1)S(1)}, u32[]{:S(2)}, u32[]{:S(2)}) collective-permute-start(bf16[1,4,128,128]{3,2,1,0:T(8,128)(2,1)S(1)} %get-tuple-element.48), channel_id=1, source_target_pairs={{0,2},{2,0},{4,6},{6,4},{8,10},{10,8},{12,14},{14,12},{16,18},{18,... | collective-permute-start | bytes 393224 | tf_op jit(solution)/shard_map/ppermute | solution.py:422
  58.3 6.4 %copy-start = (bf16[512,512]{1,0:T(8,128)(2,1)S(1)}, bf16[512,512]{1,0:T(8,128)(2,1)}, u32[]{:S(2)}) copy-start(bf16[512,512]{1,0:T(8,128)(2,1)} %weight_ref.1) | copy-start | bytes 1572868
  59.8 4.9 %collective-permute-start.16 = (bf16[192,256]{1,0:T(8,128)(2,1)S(1)}, bf16[192,256]{1,0:T(8,128)(2,1)S(1)}, u32[]{:S(2)}, u32[]{:S(2)}) collective-permute-start(bf16[192,256]{1,0:T(8,128)(2,1)S(1)} %last_tiles.2.refs_4_), channel_id=1, source_target_pairs={{0,1},{1,0},{2,3},{3,2},{4,5},{5,4},{6,7},{7,6},{8,9},{9,8},{10,11... | collective-permute-start | bytes 294920 | tf_op jit(solution)/shard_map/ppermute | solution.py:438

commit v14 on v13

--- a/solution.py
+++ b/solution.py
@@ -39,7 +39,9 @@
 
 def slot_of(owner, row_me, row_size, paired):
     half = row_size // 2
-    return owner ^ row_me if paired else lax.rem(owner + lax.div(row_me, half) * half, row_size)
+    near = lax.div(owner, half) == lax.div(row_me, half)
+    far_slot = half + (lax.rem(owner ^ row_me, half) if paired else lax.rem(owner, half))
+    return jnp.where(near, lax.rem(owner, half), far_slot)
 
 
 def tie_kernel(value_ref, after_ref, out_ref):
@@ -413,21 +415,19 @@
         cells.append(lax.ppermute(fact_cells, "cols", turn(col_size, -step)))
 
     order = [0] + sorted(range(1, half), key=lambda step: (not step & half // 2, step & 1, -(step & 2) if step < half // 2 else step))
-    near_slots, far_slots = (order, [half + step for step in order]) if paired else ([0], [half])
-
-    def spread(tiles, which, after):
-        if not paired:
-            return [swap(pick(tiles, asked_by, which, after))]
-        picked = pick_each(tiles, asked_by, which, me, order, after)
-        return [tile if step == 0 else lax.ppermute(tile, "rows", [(row, row ^ step) for row in range(row_size)])
-                for step, tile in zip(order, picked)]
-
+    near_slots, far_slots = [0], [half + step for step in order] if paired else [half]
     if group_width % 128:
         w_query = lax.dynamic_slice_in_dim(w_query, col_me * group_width, group_width, 1)
-    near = spread(heads_first, 0, cells[1:])
+    sent = pick(heads_first, asked_by, 0, cells[1:])
+    near = [swap(sent)]
     residual, asked = front(cells, tile_ids, me, key_mask, gain_col, w_qkv, w_col_out, gain_tile, w_query,
-                            heads_all, head_size, cols, heads_here, tiles_here, row_size, paired, near[0])
-    far = spread(mirrored, 1, [asked] + near[1:3])
+                            heads_all, head_size, cols, heads_here, tiles_here, row_size, paired, sent)
+    if paired:
+        picked = pick_each(mirrored, asked_by, 1, me, order, [asked])
+        far = [tile if step == 0 else lax.ppermute(tile, "rows", [(row, row ^ step) for row in range(row_size)])
+               for step, tile in zip(order, picked)]
+    else:
+        far = [swap(pick(mirrored, asked_by, 1, [asked]))]
     sums, tops = first_tiles(asked, near, near_slots, rows * cols)
     batch = len(far) // 2
     if batch:

time: 66.4 us -> 71.8 us (1.081)
  waiting for transfers between devices: 18 us -> 28.2 us
  blocking collectives: 9.81 us -> 0 us
  starting transfers between devices: 19.9 us -> 22.6 us
  Pallas kernels: 16.5 us -> 18.7 us
    ppermute x1, waiting for transfers between devices: 0.01 us -> 15.4 us  [shards(): mirrored = lax.ppermute(heads_first, 'rows', turn(row_size, half))]
    all_to_all x1 -> x0, blocking collectives: 9.81 us -> none  [swap(): lax.all_to_all(value, 'rows', split_axis=0, concat_axis=0, tiled=True, ax...]
    ppermute x14 -> x7, waiting for transfers between devices: 16.1 us -> 6.43 us  [shards(): lax.ppermute(tile, 'rows', [(row, row ^ step) for row in range(row_size)])]
    all_to_all x0 -> x2, starting transfers between devices: none -> 7.34 us  [swap(): lax.all_to_all(value, 'rows', split_axis=0, concat_axis=0, tiled=True, ax...]
    ppermute x14 -> x7, starting transfers between devices: 12.7 us -> 9.08 us  [shards(): lax.ppermute(tile, 'rows', [(row, row ^ step) for row in range(row_size)])]
    all_to_all x0 -> x2, waiting for transfers between devices: none -> 3.53 us  [swap(): lax.all_to_all(value, 'rows', split_axis=0, concat_axis=0, tiled=True, ax...]
    pallas_call x0 -> x1, Pallas kernels: none -> 1.72 us  [pick(): pl.pallas_call(functools.partial(pick_kernel, which), out_shape=jax.Shape...]
    ppermute x1, starting transfers between devices: 1.52 us -> 2.97 us  [shards(): cells.append(lax.ppermute(fact_cells, 'cols', turn(col_size, -step)))]
  transfers between devices with their start and end apart: 17 -> 12, of which waited for: 7 -> 6; matrix products, arithmetic and copies ran while one was open for 0% -> 2% of each run, Pallas kernels for 19% -> 20%
where the time goes in v14:
time: 71.8 us; the launch traced here: 71.5 us
  waiting for transfers between devices  28.2 us (39%)
  starting transfers between devices  22.6 us (31%)
  Pallas kernels  18.7 us (26%)
  local copies, waits for them, and re-layouts  1.8 us (3%)
    ppermute x1, waiting for transfers between devices, shards(): mirrored = lax.ppermute(heads_first, 'rows', turn(row_size, half))  15.4 us
    ppermute x7, starting transfers between devices, shards(): lax.ppermute(tile, 'rows', [(row, row ^ step) for row in range(row_size)])  9.08 us
    all_to_all x2, starting transfers between devices, swap(): lax.all_to_all(value, 'rows', split_axis=0, concat_axis=0, tiled=True, ax...  7.34 us
    ppermute x7, waiting for transfers between devices, shards(): lax.ppermute(tile, 'rows', [(row, row ^ step) for row in range(row_size)])  6.43 us
    pallas_call x1, Pallas kernels, front(): pl.pallas_call(functools.partial(front_kernel, groups, heads, head_size,...  5.5 us
    all_to_all x2, waiting for transfers between devices, swap(): lax.all_to_all(value, 'rows', split_axis=0, concat_axis=0, tiled=True, ax...  3.53 us
    ppermute x1, starting transfers between devices, shards(): cells.append(lax.ppermute(fact_cells, 'cols', turn(col_size, -step)))  2.97 us
    pallas_call x2, Pallas kernels, last_tiles(): pl.pallas_call(functools.partial(last_kernel, slots, groups), out_shape=(...  2.88 us
  transfers between devices with their start and end apart: 12, of which 6 were waited for; matrix products, arithmetic and copies ran while one was open for 2% of the time, Pallas kernels for 20%

profile of v14, /device:TPU:0, one launch (start us, length us, event | category | flops | bytes accessed | tf_op | source)
XLA Modules:
  0.0 71.5 jit_solution(13709244717580124637)
XLA Ops:
  0.0 3.0 %collective-permute-start = (bf16[48,4,512]{2,1,0:T(4,128)(2,1)}, bf16[48,4,512]{2,1,0:T(4,128)(2,1)S(1)}, u32[]{:S(2)}, u32[]{:S(2)}) collective-permute-start(bf16[48,4,512]{2,1,0:T(4,128)(2,1)} %refs_0_.1), channel_id=1, source_target_pairs={{0,1},{1,0},{2,3},{3,2},{4,5},{5,4},{6,7},{7,6},{8,9},{9,8},{10,11... | collective-permute-start | bytes 589832 | tf_op jit(solution)/shard_map/ppermute | solution.py:415
  3.7 1.2 %request.1.after_ref = s32[8,2,128]{2,1,0:T(2,128)} custom-call(s32[1,12]{1,0:T(1,128)S(1)} %copy-done.1, s32[2]{0:T(128)S(1)} %pad_add_fusion.me_ref.refs_2_), custom_call_target="tpu_custom_call" | custom-call | bytes 262144 | tf_op jit(solution)/shard_map/request/pallas_call | solution.py:78
  4.9 3.8 %all-to-all-start = ((s32[8,2,128]{2,1,0:T(2,128)}), s32[8,2,128]{2,1,0:T(2,128)S(1)}, u32[]{:S(2)}, u32[]{:S(2)}) async-start(s32[8,2,128]{2,1,0:T(2,128)} %request.1.after_ref), calls=%async_computation | async-start | bytes 16384 | tf_op jit(solution)/shard_map/all_to_all | solution.py:406
  8.7 1.1 %copy.14 = bf16[4,128,4,128]{3,1,2,0:T(8,128)(2,1)S(1)} copy(bf16[4,128,4,128]{3,2,1,0:T(4,128)(2,1)} %param.17) | data formatting | bytes 1048576 | tf_op args[7]
  9.9 3.5 %all-to-all-done.wanted_ref = s32[8,2,128]{2,1,0:T(2,128)S(1)} async-done(((s32[8,2,128]{2,1,0:T(2,128)}), s32[8,2,128]{2,1,0:T(2,128)S(1)}, u32[]{:S(2)}, u32[]{:S(2)}) %all-to-all-start) | async-done | bytes 8224 | tf_op jit(solution)/shard_map/all_to_all | solution.py:406
  13.4 1.7 %pick.1.refs_10_ = bf16[8,4,128,128]{3,2,1,0:T(8,128)(2,1)} custom-call(s32[8,2,128]{2,1,0:T(2,128)S(1)} %all-to-all-done.wanted_ref, bf16[4,4,128,128]{3,2,1,0:T(8,128)(2,1)S(1)} %tie.1.tiles_ref, bf16[48,4,512]{2,1,0:T(4,128)(2,1)S(1)} %collective-permute-done.refs_0_.refs_1_), custom_call_target="tpu_custom_call" | custom-call | bytes 2097152 | tf_op jit(solution)/shard_map/pick/pallas_call | solution.py:96
  15.1 3.6 %all-to-all-start.1 = ((bf16[8,4,128,128]{3,2,1,0:T(8,128)(2,1)}), bf16[8,4,128,128]{3,2,1,0:T(8,128)(2,1)S(1)}, u32[]{:S(2)}, u32[]{:S(2)}) async-start(bf16[8,4,128,128]{3,2,1,0:T(8,128)(2,1)} %pick.1.refs_10_), calls=%async_computation.1 | async-start | bytes 2097152 | tf_op jit(solution)/shard_map/all_to_all | solution.py:406
  18.7 2.7 %collective-permute-start.1 = (bf16[4,4,128,128]{3,2,1,0:T(8,128)(2,1)S(1)}, bf16[4,4,128,128]{3,2,1,0:T(8,128)(2,1)S(1)}, u32[]{:S(2)}, u32[]{:S(2)}) collective-permute-start(bf16[4,4,128,128]{3,2,1,0:T(8,128)(2,1)S(1)} %tie.1.tiles_ref), channel_id=1, source_target_pairs={{0,16},{2,18},{4,20},{6,22},{8,24},{10,26},{12,28},{14,30},{16,0},... | collective-permute-start | bytes 1572872 | tf_op jit(solution)/shard_map/ppermute | solution.py:411
  21.3 5.5 %front.1 = (f32[192,512]{1,0:T(8,128)S(1)}, bf16[4,384,128]{2,1,0:T(8,128)(2,1)S(1)}) custom-call(bf16[48,4,512]{2,1,0:T(4,128)(2,1)} %refs_0_.1, bf16[48,4,512]{2,1,0:T(4,128)(2,1)S(1)} %collective-permute-done.refs_0_.refs_1_, s32[2]{0:T(128)S(1)} %pad_add_fusion.me_ref.refs_2_, s32[1,12]{1,0:T(1,128)} %refs_3_.1, s32[12,48]{1,0:T(8,128)} %bitcast.9, ...), custom_call_target="tpu_custom_call" | custom-call | flops 1006632960 | bytes 4194304 | tf_op jit(solution)/shard_map/front/pallas_call | solution.py:237
  26.8 15.4 %collective-permute-done.1.tiles_ref = bf16[4,4,128,128]{3,2,1,0:T(8,128)(2,1)S(1)} collective-permute-done((bf16[4,4,128,128]{3,2,1,0:T(8,128)(2,1)S(1)}, bf16[4,4,128,128]{3,2,1,0:T(8,128)(2,1)S(1)}, u32[]{:S(2)}, u32[]{:S(2)}) %collective-permute-start.1) | collective-permute-done | bytes 524320 | tf_op jit(solution)/shard_map/ppermute | solution.py:411
  42.2 1.4 %pick_each.1 = (bf16[1,4,128,128]{3,2,1,0:T(8,128)(2,1)S(1)}, bf16[1,4,128,128]{3,2,1,0:T(8,128)(2,1)S(1)}, bf16[1,4,128,128]{3,2,1,0:T(8,128)(2,1)S(1)}, bf16[1...) custom-call(s32[8,2,128]{2,1,0:T(2,128)S(1)} %all-to-all-done.wanted, ...), custom_call_target="tpu_custom_call" | custom-call | bytes 2097152 | tf_op jit(solution)/shard_map/pick_each/pallas_call | solution.py:115
  43.7 4.6 %collective-permute-start.2 = (bf16[1,4,128,128]{3,2,1,0:T(8,128)(2,1)S(1)}, bf16[1,4,128,128]{3,2,1,0:T(8,128)(2,1)S(1)}, u32[]{:S(2)}, u32[]{:S(2)}) collective-permute-start(bf16[1,4,128,128]{3,2,1,0:T(8,128)(2,1)S(1)} %get-tuple-element.24), channel_id=1, source_target_pairs={{0,8},{2,10},{4,12},{6,14},{8,0},{10,2},{12,4},{14,6},{16,24},{18,... | collective-permute-start | bytes 393224 | tf_op jit(solution)/shard_map/ppermute | solution.py:427
  48.3 0.9 %collective-permute-start.3 = (bf16[1,4,128,128]{3,2,1,0:T(8,128)(2,1)S(1)}, bf16[1,4,128,128]{3,2,1,0:T(8,128)(2,1)S(1)}, u32[]{:S(2)}, u32[]{:S(2)}) collective-permute-start(bf16[1,4,128,128]{3,2,1,0:T(8,128)(2,1)S(1)} %get-tuple-element.25), channel_id=1, source_target_pairs={{0,12},{2,14},{4,8},{6,10},{8,4},{10,6},{12,0},{14,2},{16,28},{18,... | collective-permute-start | bytes 393224 | tf_op jit(solution)/shard_map/ppermute | solution.py:427
  49.2 0.7 collective-permute-start.4
  49.9 1.0 %collective-permute-start.5 = (bf16[1,4,128,128]{3,2,1,0:T(8,128)(2,1)}, bf16[1,4,128,128]{3,2,1,0:T(8,128)(2,1)S(1)}, u32[]{:S(2)}, u32[]{:S(2)}) collective-permute-start(bf16[1,4,128,128]{3,2,1,0:T(8,128)(2,1)} %get-tuple-element.29), channel_id=1, source_target_pairs={{0,14},{2,12},{4,10},{6,8},{8,6},{10,4},{12,2},{14,0},{16,30},{18,... | collective-permute-start | bytes 393224 | tf_op jit(solution)/shard_map/ppermute | solution.py:427
  51.0 1.5 %collective-permute-start.6 = (bf16[1,4,128,128]{3,2,1,0:T(8,128)(2,1)S(1)}, bf16[1,4,128,128]{3,2,1,0:T(8,128)(2,1)S(1)}, u32[]{:S(2)}, u32[]{:S(2)}) collective-permute-start(bf16[1,4,128,128]{3,2,1,0:T(8,128)(2,1)S(1)} %get-tuple-element.30), channel_id=1, source_target_pairs={{0,4},{2,6},{4,0},{6,2},{8,12},{10,14},{12,8},{14,10},{16,20},{18,... | collective-permute-start | bytes 393224 | tf_op jit(solution)/shard_map/ppermute | solution.py:427
  52.8 3.6 %collective-permute-done.3.refs_2_ = bf16[1,4,128,128]{3,2,1,0:T(8,128)(2,1)S(1)} collective-permute-done((bf16[1,4,128,128]{3,2,1,0:T(8,128)(2,1)S(1)}, bf16[1,4,128,128]{3,2,1,0:T(8,128)(2,1)S(1)}, u32[]{:S(2)}, u32[]{:S(2)}) %collective-permute-start.3) | collective-permute-done | bytes 131104 | tf_op jit(solution)/shard_map/ppermute | solution.py:427
  56.4 2.4 %first_tiles.1 = (f32[4,384,128]{2,1,0:T(8,128)S(1)}, f32[384,128]{1,0:T(8,128)S(1)}) custom-call(bf16[4,384,128]{2,1,0:T(8,128)(2,1)S(1)} %get-tuple-element.20.asked_ref.refs_0_, bf16[8,4,128,128]{3,2,1,0:T(8,128)(2,1)S(1)} %all-to-all-done.1.refs_0_), custom_call_target="tpu_custom_call" | custom-call | flops 805306368 | bytes 4194304 | tf_op jit(solution)/shard_map/first_tiles/pallas_call | solution.py:286
  58.8 2.0 %more_tiles.1 = (f32[4,384,128]{2,1,0:T(8,128)S(1)}, f32[384,128]{1,0:T(8,128)S(1)}) custom-call(bf16[4,384,128]{2,1,0:T(8,128)(2,1)S(1)} %get-tuple-element.20.asked_ref.refs_0_, f32[4,384,128]{2,1,0:T(8,128)S(1)} %get-tuple-element.21.old_sums_ref, f32[384,128]{1,0:T(8,128)S(1)} %get-tuple-element.22.old_tops_ref, ...), custom_call_target="tpu_custom_call" | custom-call | flops 402653184 | bytes 4194304 | tf_op jit(solution)/shard_map/more_tiles/pallas_call | solution.py:319
  61.1 2.6 %collective-permute-done.7.refs_2_ = bf16[1,4,128,128]{3,2,1,0:T(8,128)(2,1)S(1)} collective-permute-done((bf16[1,4,128,128]{3,2,1,0:T(8,128)(2,1)S(1)}, bf16[1,4,128,128]{3,2,1,0:T(8,128)(2,1)S(1)}, u32[]{:S(2)}, u32[]{:S(2)}) %collective-permute-start.7) | collective-permute-done | bytes 131104 | tf_op jit(solution)/shard_map/ppermute | solution.py:427
  63.6 1.4 %last_tiles.2.refs_4_ = bf16[192,256]{1,0:T(8,128)(2,1)S(1)} custom-call(bf16[4,384,128]{2,1,0:T(8,128)(2,1)S(1)} %get-tuple-element.20.asked_ref.refs_0_, f32[4,384,128]{2,1,0:T(8,128)S(1)} %get-tuple-element.27.sums_ref, f32[384,128]{1,0:T(8,128)S(1)} %get-tuple-element.28.tops_ref, bf16[1,4,128,128]{3,2,1,0:T(8,128)(2,1)S(1)} %collective-permute-done.5.refs_0_, ...), custom_call_target="tpu_custom_call" | custom-call | flops 201326592 | bytes 4194304 | tf_op jit(solution)/shard_map/last_tiles/pallas_call | solution.py:353
  65.7 1.4 %last_tiles.3.refs_0_ = bf16[192,256]{1,0:T(8,128)(2,1)S(1)} custom-call(bf16[4,384,128]{2,1,0:T(8,128)(2,1)S(1)} %get-tuple-element.20.asked_ref.refs_0_, f32[4,384,128]{2,1,0:T(8,128)S(1)} %get-tuple-element.27.sums_ref, f32[384,128]{1,0:T(8,128)S(1)} %get-tuple-element.28.tops_ref, bf16[1,4,128,128]{3,2,1,0:T(8,128)(2,1)S(1)} %collective-permute-done.5.refs_0_, ...), custom_call_target="tpu_custom_call" | custom-call | flops 201326592 | bytes 4194304 | tf_op jit(solution)/shard_map/last_tiles/pallas_call | solution.py:353
  67.1 2.9 %collective-permute-done.9.refs_1_ = bf16[192,256]{1,0:T(8,128)(2,1)S(1)} collective-permute-done((bf16[192,256]{1,0:T(8,128)(2,1)S(1)}, bf16[192,256]{1,0:T(8,128)(2,1)S(1)}, u32[]{:S(2)}, u32[]{:S(2)}) %collective-permute-start.9) | collective-permute-done | bytes 98336 | tf_op jit(solution)/shard_map/ppermute | solution.py:438
  70.0 1.5 %finish.1 = bf16[48,4,512]{2,1,0:T(4,128)(2,1)} custom-call(s32[2]{0:T(128)S(1)} %pad_add_fusion.me_ref.refs_2_, bf16[512,512]{1,0:T(8,128)(2,1)S(1)} %copy-done, f32[192,512]{1,0:T(8,128)S(1)} %get-tuple-element.19.resid_ref, bf16[192,256]{1,0:T(8,128)(2,1)S(1)} %last_tiles.3.refs_0_, bf16[192,256]{1,0:T(8,128)(2,1)S(1)} %collective-permute-done.9.refs_1_), custom_call_target="tpu_custom_call" | custom-call | flops 100663296 | bytes 1048576 | tf_op jit(solution)/shard_map/finish/pallas_call | solution.py:376
  (16 shorter events, 1.9 us)
Async XLA Ops:
  0.0 13.4 %collective-permute-start = (bf16[48,4,512]{2,1,0:T(4,128)(2,1)}, bf16[48,4,512]{2,1,0:T(4,128)(2,1)S(1)}, u32[]{:S(2)}, u32[]{:S(2)}) collective-permute-start(bf16[48,4,512]{2,1,0:T(4,128)(2,1)} %refs_0_.1), channel_id=1, source_target_pairs={{0,1},{1,0},{2,3},{3,2},{4,5},{5,4},{6,7},{7,6},{8,9},{9,8},{10,11... | collective-permute-start | bytes 589832 | tf_op jit(solution)/shard_map/ppermute | solution.py:415
  3.0 0.7 copy-start.1
  4.9 8.5 %all-to-all-start = ((s32[8,2,128]{2,1,0:T(2,128)}), s32[8,2,128]{2,1,0:T(2,128)S(1)}, u32[]{:S(2)}, u32[]{:S(2)}) async-start(s32[8,2,128]{2,1,0:T(2,128)} %request.1.after_ref), calls=%async_computation | async-start | bytes 16384 | tf_op jit(solution)/shard_map/all_to_all | solution.py:406
  15.1 41.3 %all-to-all-start.1 = ((bf16[8,4,128,128]{3,2,1,0:T(8,128)(2,1)}), bf16[8,4,128,128]{3,2,1,0:T(8,128)(2,1)S(1)}, u32[]{:S(2)}, u32[]{:S(2)}) async-start(bf16[8,4,128,128]{3,2,1,0:T(8,128)(2,1)} %pick.1.refs_10_), calls=%async_computation.1 | async-start | bytes 2097152 | tf_op jit(solution)/shard_map/all_to_all | solution.py:406
  18.7 23.6 %collective-permute-start.1 = (bf16[4,4,128,128]{3,2,1,0:T(8,128)(2,1)S(1)}, bf16[4,4,128,128]{3,2,1,0:T(8,128)(2,1)S(1)}, u32[]{:S(2)}, u32[]{:S(2)}) collective-permute-start(bf16[4,4,128,128]{3,2,1,0:T(8,128)(2,1)S(1)} %tie.1.tiles_ref), channel_id=1, source_target_pairs={{0,16},{2,18},{4,20},{6,22},{8,24},{10,26},{12,28},{14,30},{16,0},... | collective-permute-start | bytes 1572872 | tf_op jit(solution)/shard_map/ppermute | solution.py:411
  43.7 8.8 %collective-permute-start.2 = (bf16[1,4,128,128]{3,2,1,0:T(8,128)(2,1)S(1)}, bf16[1,4,128,128]{3,2,1,0:T(8,128)(2,1)S(1)}, u32[]{:S(2)}, u32[]{:S(2)}) collective-permute-start(bf16[1,4,128,128]{3,2,1,0:T(8,128)(2,1)S(1)} %get-tuple-element.24), channel_id=1, source_target_pairs={{0,8},{2,10},{4,12},{6,14},{8,0},{10,2},{12,4},{14,6},{16,24},{18,... | collective-permute-start | bytes 393224 | tf_op jit(solution)/shard_map/ppermute | solution.py:427
  48.3 8.1 %collective-permute-start.3 = (bf16[1,4,128,128]{3,2,1,0:T(8,128)(2,1)S(1)}, bf16[1,4,128,128]{3,2,1,0:T(8,128)(2,1)S(1)}, u32[]{:S(2)}, u32[]{:S(2)}) collective-permute-start(bf16[1,4,128,128]{3,2,1,0:T(8,128)(2,1)S(1)} %get-tuple-element.25), channel_id=1, source_target_pairs={{0,12},{2,14},{4,8},{6,10},{8,4},{10,6},{12,0},{14,2},{16,28},{18,... | collective-permute-start | bytes 393224 | tf_op jit(solution)/shard_map/ppermute | solution.py:427
  49.2 9.5 %collective-permute-start.4 = (bf16[1,4,128,128]{3,2,1,0:T(8,128)(2,1)}, bf16[1,4,128,128]{3,2,1,0:T(8,128)(2,1)S(1)}, u32[]{:S(2)}, u32[]{:S(2)}) collective-permute-start(bf16[1,4,128,128]{3,2,1,0:T(8,128)(2,1)} %get-tuple-element.26), channel_id=1, source_target_pairs={{0,10},{2,8},{4,14},{6,12},{8,2},{10,0},{12,6},{14,4},{16,26},{18,... | collective-permute-start | bytes 393224 | tf_op jit(solution)/shard_map/ppermute | solution.py:427
  49.9 10.9 %collective-permute-start.5 = (bf16[1,4,128,128]{3,2,1,0:T(8,128)(2,1)}, bf16[1,4,128,128]{3,2,1,0:T(8,128)(2,1)S(1)}, u32[]{:S(2)}, u32[]{:S(2)}) collective-permute-start(bf16[1,4,128,128]{3,2,1,0:T(8,128)(2,1)} %get-tuple-element.29), channel_id=1, source_target_pairs={{0,14},{2,12},{4,10},{6,8},{8,6},{10,4},{12,2},{14,0},{16,30},{18,... | collective-permute-start | bytes 393224 | tf_op jit(solution)/shard_map/ppermute | solution.py:427
  51.0 10.1 %collective-permute-start.6 = (bf16[1,4,128,128]{3,2,1,0:T(8,128)(2,1)S(1)}, bf16[1,4,128,128]{3,2,1,0:T(8,128)(2,1)S(1)}, u32[]{:S(2)}, u32[]{:S(2)}) collective-permute-start(bf16[1,4,128,128]{3,2,1,0:T(8,128)(2,1)S(1)} %get-tuple-element.30), channel_id=1, source_target_pairs={{0,4},{2,6},{4,0},{6,2},{8,12},{10,14},{12,8},{14,10},{16,20},{18,... | collective-permute-start | bytes 393224 | tf_op jit(solution)/shard_map/ppermute | solution.py:427
  52.5 11.2 %collective-permute-start.7 = (bf16[1,4,128,128]{3,2,1,0:T(8,128)(2,1)S(1)}, bf16[1,4,128,128]{3,2,1,0:T(8,128)(2,1)S(1)}, u32[]{:S(2)}, u32[]{:S(2)}) collective-permute-start(bf16[1,4,128,128]{3,2,1,0:T(8,128)(2,1)S(1)} %get-tuple-element.31), channel_id=1, source_target_pairs={{0,6},{2,4},{4,2},{6,0},{8,14},{10,12},{12,10},{14,8},{16,22},{18,... | collective-permute-start | bytes 393224 | tf_op jit(solution)/shard_map/ppermute | solution.py:427
  56.4 7.2 %collective-permute-start.8 = (bf16[1,4,128,128]{3,2,1,0:T(8,128)(2,1)S(1)}, bf16[1,4,128,128]{3,2,1,0:T(8,128)(2,1)S(1)}, u32[]{:S(2)}, u32[]{:S(2)}) collective-permute-start(bf16[1,4,128,128]{3,2,1,0:T(8,128)(2,1)S(1)} %get-tuple-element.32), channel_id=1, source_target_pairs={{0,2},{2,0},{4,6},{6,4},{8,10},{10,8},{12,14},{14,12},{16,18},{18,... | collective-permute-start | bytes 393224 | tf_op jit(solution)/shard_map/ppermute | solution.py:427
  63.6 6.3 %copy-start = (bf16[512,512]{1,0:T(8,128)(2,1)S(1)}, bf16[512,512]{1,0:T(8,128)(2,1)}, u32[]{:S(2)}) copy-start(bf16[512,512]{1,0:T(8,128)(2,1)} %weight_ref.1) | copy-start | bytes 1572868
  65.1 4.9 %collective-permute-start.9 = (bf16[192,256]{1,0:T(8,128)(2,1)S(1)}, bf16[192,256]{1,0:T(8,128)(2,1)S(1)}, u32[]{:S(2)}, u32[]{:S(2)}) collective-permute-start(bf16[192,256]{1,0:T(8,128)(2,1)S(1)} %last_tiles.2.refs_4_), channel_id=1, source_target_pairs={{0,1},{1,0},{2,3},{3,2},{4,5},{5,4},{6,7},{7,6},{8,9},{9,8},{10,11... | collective-permute-start | bytes 294920 | tf_op jit(solution)/shard_map/ppermute | solution.py:438

commit v15 on v13

--- a/solution.py
+++ b/solution.py
@@ -121,11 +121,11 @@
     )(wanted, me, tiles, *after)
 
 
-def front_kernel(groups, heads, head_size, chunk, cols, heads_here, tiles_here, row_size, paired, *refs):
+def front_kernel(groups, heads, head_size, chunk, cols, heads_here, tiles_here, row_size, paired, waited, *refs):
     cell_hbms, refs = refs[:groups], refs[groups:]
-    (me_ref, ids_hbm, mask_hbm, gain_col_hbm, gain_tile_hbm, w_qkv_hbm, w_out_hbm, w_query_hbm, after_ref,
-     resid_ref, asked_ref, normed_ref, packed_ref, w_qkv_ref, w_out_ref, w_query_ref, cell_refs,
-     ids_ref, mask_ref, gain_col_ref, gain_tile_ref, sems) = refs
+    (me_ref, ids_hbm, mask_hbm, gain_col_hbm, gain_tile_hbm, w_qkv_hbm, w_out_hbm, w_query_hbm) = refs[:8]
+    (resid_ref, asked_ref, normed_ref, packed_ref, w_qkv_ref, w_out_ref, w_query_ref, cell_refs,
+     ids_ref, mask_ref, gain_col_ref, gain_tile_ref, sems) = refs[8 + waited:]
     own_rows, width = resid_ref.shape
     steps = own_rows // chunk
     span = groups * chunk
@@ -233,17 +233,18 @@
                for value in (ids, key_mask, gain_col, gain_tile, w_qkv, w_out, w_query)]
     own = pltpu.with_memory_space_constraint(cells[0], pltpu.HBM)
     return pl.pallas_call(
-        functools.partial(front_kernel, groups, heads, head_size, ROW_GROUP * cols, cols, heads_here, tiles_here, row_size, paired),
+        functools.partial(front_kernel, groups, heads, head_size, ROW_GROUP * cols, cols, heads_here, tiles_here, row_size, paired,
+                          len(after)),
         out_shape=(jax.ShapeDtypeStruct((own_rows, width), jnp.float32),
                    jax.ShapeDtypeStruct((heads_here, total, 2 * head_size), jnp.bfloat16)),
-        in_specs=[HBM] + [ANY] * (groups - 1) + [SMEM] + [HBM] * 7 + [ANY],
+        in_specs=[HBM] + [ANY] * (groups - 1) + [SMEM] + [HBM] * 7 + [ANY] * len(after),
         out_specs=(VMEM, VMEM),
         scratch_shapes=scratch,
         compiler_params=params(total),
         cost_estimate=pl.CostEstimate(flops=2 * total * width * 5 * width, bytes_accessed=4 * MIB,
                                       transcendentals=total * heads * 128),
         name="front",
-    )(own, *cells[1:], me, *fetched, after)
+    )(own, *cells[1:], me, *fetched, *after)
 
 
 def weigh(query, tile_refs, head, slots):
@@ -412,10 +413,12 @@
     for step in range(1, col_size):
         cells.append(lax.ppermute(fact_cells, "cols", turn(col_size, -step)))
 
-    order = [0] + sorted(range(1, half), key=lambda step: (not step & half // 2, step & 1, -(step & 2) if step < half // 2 else step))
-    near_slots, far_slots = (order, [half + step for step in order]) if paired else ([0], [half])
-
-    def spread(tiles, which, after):
+    across = half // 2
+    near_order = [0, 1] + sorted(range(2, half), key=lambda step: (step != 2, not step & across, step & 1, step))
+    far_order = [0, across] + sorted(set(range(1, half)) - {across}, key=lambda step: (step != 2, not step & across, step & 1, -step))
+    near_slots, far_slots = (near_order, [half + step for step in far_order]) if paired else ([0], [half])
+
+    def spread(tiles, which, order, after):
         if not paired:
             return [swap(pick(tiles, asked_by, which, after))]
         picked = pick_each(tiles, asked_by, which, me, order, after)
@@ -424,10 +427,10 @@
 
     if group_width % 128:
         w_query = lax.dynamic_slice_in_dim(w_query, col_me * group_width, group_width, 1)
-    near = spread(heads_first, 0, cells[1:])
+    near = spread(heads_first, 0, near_order, cells[1:])
     residual, asked = front(cells, tile_ids, me, key_mask, gain_col, w_qkv, w_col_out, gain_tile, w_query,
-                            heads_all, head_size, cols, heads_here, tiles_here, row_size, paired, near[0])
-    far = spread(mirrored, 1, [asked] + near[1:3])
+                            heads_all, head_size, cols, heads_here, tiles_here, row_size, paired, near[:3])
+    far = spread(mirrored, 1, far_order, [asked])
     sums, tops = first_tiles(asked, near, near_slots, rows * cols)
     batch = len(far) // 2
     if batch:

time: 66.4 us -> 62.1 us (0.935)
  waiting for transfers between devices: 18 us -> 11.4 us
  starting transfers between devices: 19.9 us -> 22.1 us
    ppermute x14, waiting for transfers between devices: 16.1 us -> 9.09 us  [spread(): lax.ppermute(tile, 'rows', [(row, row ^ step) for row in range(row_size)])]
    ppermute x14, starting transfers between devices: 12.7 us -> 15 us  [spread(): lax.ppermute(tile, 'rows', [(row, row ^ step) for row in range(row_size)])]
  transfers between devices with their start and end apart: 17 -> 17, of which waited for: 7 -> 6; matrix products, arithmetic and copies ran while one was open for 0% -> 0% of each run, Pallas kernels for 19% -> 21%
where the time goes in v15:
time: 62.1 us; the launch traced here: 61.9 us
  starting transfers between devices  22.1 us (36%)
  Pallas kernels  16.5 us (27%)
  waiting for transfers between devices  11.4 us (18%)
  blocking collectives  9.81 us (16%)
  local copies, waits for them, and re-layouts  1.84 us (3%)
    ppermute x14, starting transfers between devices, spread(): lax.ppermute(tile, 'rows', [(row, row ^ step) for row in range(row_size)])  15 us
    all_to_all x1, blocking collectives, swap(): lax.all_to_all(value, 'rows', split_axis=0, concat_axis=0, tiled=True, ax...  9.81 us
    ppermute x14, waiting for transfers between devices, spread(): lax.ppermute(tile, 'rows', [(row, row ^ step) for row in range(row_size)])  9.09 us
    pallas_call x1, Pallas kernels, front(): pl.pallas_call(functools.partial(front_kernel, groups, heads, head_size,...  5.51 us
    ppermute x1, starting transfers between devices, shards(): mirrored = lax.ppermute(heads_first, 'rows', turn(row_size, half))  4.1 us
    pallas_call x2, Pallas kernels, last_tiles(): pl.pallas_call(functools.partial(last_kernel, slots, groups), out_shape=(...  2.88 us
    pallas_call x1, Pallas kernels, first_tiles(): pl.pallas_call(functools.partial(first_kernel, slots, rows if rows <= 512...  2.4 us
    ppermute x1, waiting for transfers between devices, shards(): lax.ppermute(other, 'cols', turn(col_size, step + 1))  2.3 us
  transfers between devices with their start and end apart: 17, of which 6 were waited for; matrix products, arithmetic and copies ran while one was open for 0% of the time, Pallas kernels for 21%

profile of v15, /device:TPU:0, one launch (start us, length us, event | category | flops | bytes accessed | tf_op | source)
XLA Modules:
  0.0 61.9 jit_solution(16325310871539665990)
XLA Ops:
  0.0 1.2 %copy.14 = bf16[4,128,4,128]{3,1,2,0:T(8,128)(2,1)S(1)} copy(bf16[4,128,4,128]{3,2,1,0:T(4,128)(2,1)} %param.17) | data formatting | bytes 1048576 | tf_op args[7]
  2.6 4.1 %collective-permute-start.8 = (bf16[4,4,128,128]{3,2,1,0:T(8,128)(2,1)S(1)}, bf16[4,4,128,128]{3,2,1,0:T(8,128)(2,1)S(1)}, u32[]{:S(2)}, u32[]{:S(2)}) collective-permute-start(bf16[4,4,128,128]{3,2,1,0:T(8,128)(2,1)S(1)} %tie.1.tiles_ref), channel_id=1, source_target_pairs={{0,16},{2,18},{4,20},{6,22},{8,24},{10,26},{12,28},{14,30},{16,0},... | collective-permute-start | bytes 1572872 | tf_op jit(solution)/shard_map/ppermute | solution.py:410
  6.7 1.5 %collective-permute-start = (bf16[48,4,512]{2,1,0:T(4,128)(2,1)S(1)}, bf16[48,4,512]{2,1,0:T(4,128)(2,1)S(1)}, u32[]{:S(2)}, u32[]{:S(2)}) collective-permute-start(bf16[48,4,512]{2,1,0:T(4,128)(2,1)S(1)} %copy-done.2), channel_id=1, source_target_pairs={{0,1},{1,0},{2,3},{3,2},{4,5},{5,4},{6,7},{7,6},{8,9},{9,8},{10,11... | collective-permute-start | bytes 589832 | tf_op jit(solution)/shard_map/ppermute | solution.py:414
  8.2 9.8 %all_to_all.5.wanted_ref = s32[8,2,128]{2,1,0:T(2,128)S(1)} all-to-all(s32[8,2,128]{2,1,0:T(2,128)S(1)} %request.1.after_ref), channel_id=1, replica_groups={{0,2,4,6,8,10,12,14},{16,18,20,22,24,26,28,30},{1,3,5,7,9,11,13,15},{17..., dimensions={0} | all-to-all | bytes 16384 | tf_op jit(solution)/shard_map/all_to_all | solution.py:405
  18.8 1.6 %collective-permute-start.2 = (bf16[1,4,128,128]{3,2,1,0:T(8,128)(2,1)S(1)}, bf16[1,4,128,128]{3,2,1,0:T(8,128)(2,1)S(1)}, u32[]{:S(2)}, u32[]{:S(2)}) collective-permute-start(bf16[1,4,128,128]{3,2,1,0:T(8,128)(2,1)S(1)} %get-tuple-element.29), channel_id=1, source_target_pairs={{0,4},{2,6},{4,0},{6,2},{8,12},{10,14},{12,8},{14,10},{16,20},{18,... | collective-permute-start | bytes 393224 | tf_op jit(solution)/shard_map/ppermute | solution.py:425
  20.4 2.5 %collective-permute-start.3 = (bf16[1,4,128,128]{3,2,1,0:T(8,128)(2,1)S(1)}, bf16[1,4,128,128]{3,2,1,0:T(8,128)(2,1)S(1)}, u32[]{:S(2)}, u32[]{:S(2)}) collective-permute-start(bf16[1,4,128,128]{3,2,1,0:T(8,128)(2,1)S(1)} %get-tuple-element.32), channel_id=1, source_target_pairs={{0,8},{2,10},{4,12},{6,14},{8,0},{10,2},{12,4},{14,6},{16,24},{18,... | collective-permute-start | bytes 393224 | tf_op jit(solution)/shard_map/ppermute | solution.py:425
  22.9 0.9 %collective-permute-start.4 = (bf16[1,4,128,128]{3,2,1,0:T(8,128)(2,1)S(1)}, bf16[1,4,128,128]{3,2,1,0:T(8,128)(2,1)S(1)}, u32[]{:S(2)}, u32[]{:S(2)}) collective-permute-start(bf16[1,4,128,128]{3,2,1,0:T(8,128)(2,1)S(1)} %get-tuple-element.33), channel_id=1, source_target_pairs={{0,12},{2,14},{4,8},{6,10},{8,4},{10,6},{12,0},{14,2},{16,28},{18,... | collective-permute-start | bytes 393224 | tf_op jit(solution)/shard_map/ppermute | solution.py:425
  23.7 1.2 %collective-permute-start.5 = (bf16[1,4,128,128]{3,2,1,0:T(8,128)(2,1)S(1)}, bf16[1,4,128,128]{3,2,1,0:T(8,128)(2,1)S(1)}, u32[]{:S(2)}, u32[]{:S(2)}) collective-permute-start(bf16[1,4,128,128]{3,2,1,0:T(8,128)(2,1)S(1)} %get-tuple-element.34), channel_id=1, source_target_pairs={{0,10},{2,8},{4,14},{6,12},{8,2},{10,0},{12,6},{14,4},{16,26},{18,... | collective-permute-start | bytes 393224 | tf_op jit(solution)/shard_map/ppermute | solution.py:425
  25.0 2.4 %collective-permute-start.6 = (bf16[1,4,128,128]{3,2,1,0:T(8,128)(2,1)S(1)}, bf16[1,4,128,128]{3,2,1,0:T(8,128)(2,1)S(1)}, u32[]{:S(2)}, u32[]{:S(2)}) collective-permute-start(bf16[1,4,128,128]{3,2,1,0:T(8,128)(2,1)S(1)} %get-tuple-element.35), channel_id=1, source_target_pairs={{0,14},{2,12},{4,10},{6,8},{8,6},{10,4},{12,2},{14,0},{16,30},{18,... | collective-permute-start | bytes 393224 | tf_op jit(solution)/shard_map/ppermute | solution.py:425
  27.4 5.5 %front.1 = (f32[192,512]{1,0:T(8,128)S(1)}, bf16[4,384,128]{2,1,0:T(8,128)(2,1)S(1)}) custom-call(bf16[48,4,512]{2,1,0:T(4,128)(2,1)} %refs_0_.1, bf16[48,4,512]{2,1,0:T(4,128)(2,1)S(1)} %collective-permute-done.refs_0_.refs_1_, s32[2]{0:T(128)S(1)} %pad_add_fusion.me_ref.refs_2_, s32[1,12]{1,0:T(1,128)} %refs_3_.1, s32[12,48]{1,0:T(8,128)} %bitcast.9, ...), custom_call_target="tpu_custom_call" | custom-call | flops 1006632960 | bytes 4194304 | tf_op jit(solution)/shard_map/front/pallas_call | solution.py:235
  32.9 2.0 %collective-permute-start.7 = (bf16[1,4,128,128]{3,2,1,0:T(8,128)(2,1)S(1)}, bf16[1,4,128,128]{3,2,1,0:T(8,128)(2,1)S(1)}, u32[]{:S(2)}, u32[]{:S(2)}) collective-permute-start(bf16[1,4,128,128]{3,2,1,0:T(8,128)(2,1)S(1)} %get-tuple-element.36), channel_id=1, source_target_pairs={{0,6},{2,4},{4,2},{6,0},{8,14},{10,12},{12,10},{14,8},{16,22},{18,... | collective-permute-start | bytes 393224 | tf_op jit(solution)/shard_map/ppermute | solution.py:425
  37.0 1.3 %collective-permute-done.5.refs_5_ = bf16[1,4,128,128]{3,2,1,0:T(8,128)(2,1)S(1)} collective-permute-done((bf16[1,4,128,128]{3,2,1,0:T(8,128)(2,1)S(1)}, bf16[1,4,128,128]{3,2,1,0:T(8,128)(2,1)S(1)}, u32[]{:S(2)}, u32[]{:S(2)}) %collective-permute-start.5) | collective-permute-done | bytes 131104 | tf_op jit(solution)/shard_map/ppermute | solution.py:425
  38.2 1.0 %collective-permute-start.11 = (bf16[1,4,128,128]{3,2,1,0:T(8,128)(2,1)S(1)}, bf16[1,4,128,128]{3,2,1,0:T(8,128)(2,1)S(1)}, u32[]{:S(2)}, u32[]{:S(2)}) collective-permute-start(bf16[1,4,128,128]{3,2,1,0:T(8,128)(2,1)S(1)} %get-tuple-element.42), channel_id=1, source_target_pairs={{0,12},{2,14},{4,8},{6,10},{8,4},{10,6},{12,0},{14,2},{16,28},{18,... | collective-permute-start | bytes 393224 | tf_op jit(solution)/shard_map/ppermute | solution.py:425
  39.2 2.9 %collective-permute-done.6.refs_6_ = bf16[1,4,128,128]{3,2,1,0:T(8,128)(2,1)S(1)} collective-permute-done((bf16[1,4,128,128]{3,2,1,0:T(8,128)(2,1)S(1)}, bf16[1,4,128,128]{3,2,1,0:T(8,128)(2,1)S(1)}, u32[]{:S(2)}, u32[]{:S(2)}) %collective-permute-start.6) | collective-permute-done | bytes 131104 | tf_op jit(solution)/shard_map/ppermute | solution.py:425
  42.1 1.7 %collective-permute-start.13 = (bf16[1,4,128,128]{3,2,1,0:T(8,128)(2,1)S(1)}, bf16[1,4,128,128]{3,2,1,0:T(8,128)(2,1)S(1)}, u32[]{:S(2)}, u32[]{:S(2)}) collective-permute-start(bf16[1,4,128,128]{3,2,1,0:T(8,128)(2,1)S(1)} %get-tuple-element.46), channel_id=1, source_target_pairs={{0,10},{2,8},{4,14},{6,12},{8,2},{10,0},{12,6},{14,4},{16,26},{18,... | collective-permute-start | bytes 393224 | tf_op jit(solution)/shard_map/ppermute | solution.py:425
  44.0 1.2 %collective-permute-start.14 = (bf16[1,4,128,128]{3,2,1,0:T(8,128)(2,1)S(1)}, bf16[1,4,128,128]{3,2,1,0:T(8,128)(2,1)S(1)}, u32[]{:S(2)}, u32[]{:S(2)}) collective-permute-start(bf16[1,4,128,128]{3,2,1,0:T(8,128)(2,1)S(1)} %get-tuple-element.47), channel_id=1, source_target_pairs={{0,6},{2,4},{4,2},{6,0},{8,14},{10,12},{12,10},{14,8},{16,22},{18,... | collective-permute-start | bytes 393224 | tf_op jit(solution)/shard_map/ppermute | solution.py:425
  45.1 4.0 %collective-permute-done.10.refs_2_ = bf16[1,4,128,128]{3,2,1,0:T(8,128)(2,1)S(1)} collective-permute-done((bf16[1,4,128,128]{3,2,1,0:T(8,128)(2,1)S(1)}, bf16[1,4,128,128]{3,2,1,0:T(8,128)(2,1)S(1)}, u32[]{:S(2)}, u32[]{:S(2)}) %collective-permute-start.10) | collective-permute-done | bytes 131104 | tf_op jit(solution)/shard_map/ppermute | solution.py:425
  49.1 2.4 %first_tiles.1 = (f32[4,384,128]{2,1,0:T(8,128)S(1)}, f32[384,128]{1,0:T(8,128)S(1)}) custom-call(bf16[4,384,128]{2,1,0:T(8,128)(2,1)S(1)} %get-tuple-element.31.asked_ref.refs_0_, bf16[1,4,128,128]{3,2,1,0:T(8,128)(2,1)S(1)} %get-tuple-element.27.refs_10_.refs_0_, bf16[1,4,128,128]{3,2,1,0:T(8,128)(2,1)S(1)} %collective-permute-done.1.refs_11_.refs_1_, ...), custom_call_target="tpu_custom_call" | custom-call | flops 805306368 | bytes 4194304 | tf_op jit(solution)/shard_map/first_tiles/pallas_call | solution.py:285
  51.6 2.0 %more_tiles.1 = (f32[4,384,128]{2,1,0:T(8,128)S(1)}, f32[384,128]{1,0:T(8,128)S(1)}) custom-call(bf16[4,384,128]{2,1,0:T(8,128)(2,1)S(1)} %get-tuple-element.31.asked_ref.refs_0_, f32[4,384,128]{2,1,0:T(8,128)S(1)} %get-tuple-element.37.old_sums_ref, f32[384,128]{1,0:T(8,128)S(1)} %get-tuple-element.38.old_tops_ref, ...), custom_call_target="tpu_custom_call" | custom-call | flops 402653184 | bytes 4194304 | tf_op jit(solution)/shard_map/more_tiles/pallas_call | solution.py:318
  53.7 1.4 %last_tiles.2.refs_4_ = bf16[192,256]{1,0:T(8,128)(2,1)S(1)} custom-call(bf16[4,384,128]{2,1,0:T(8,128)(2,1)S(1)} %get-tuple-element.31.asked_ref.refs_0_, f32[4,384,128]{2,1,0:T(8,128)S(1)} %get-tuple-element.43.sums_ref, f32[384,128]{1,0:T(8,128)S(1)} %get-tuple-element.44.tops_ref, bf16[1,4,128,128]{3,2,1,0:T(8,128)(2,1)S(1)} %collective-permute-done.12.refs_0_, ...), custom_call_target="tpu_custom_call" | custom-call | flops 201326592 | bytes 4194304 | tf_op jit(solution)/shard_map/last_tiles/pallas_call | solution.py:352
  55.1 1.5 %collective-permute-start.16 = (bf16[192,256]{1,0:T(8,128)(2,1)S(1)}, bf16[192,256]{1,0:T(8,128)(2,1)S(1)}, u32[]{:S(2)}, u32[]{:S(2)}) collective-permute-start(bf16[192,256]{1,0:T(8,128)(2,1)S(1)} %last_tiles.2.refs_4_), channel_id=1, source_target_pairs={{0,1},{1,0},{2,3},{3,2},{4,5},{5,4},{6,7},{7,6},{8,9},{9,8},{10,11... | collective-permute-start | bytes 294920 | tf_op jit(solution)/shard_map/ppermute | solution.py:441
  56.6 1.4 %last_tiles.3.refs_0_ = bf16[192,256]{1,0:T(8,128)(2,1)S(1)} custom-call(bf16[4,384,128]{2,1,0:T(8,128)(2,1)S(1)} %get-tuple-element.31.asked_ref.refs_0_, f32[4,384,128]{2,1,0:T(8,128)S(1)} %get-tuple-element.43.sums_ref, f32[384,128]{1,0:T(8,128)S(1)} %get-tuple-element.44.tops_ref, bf16[1,4,128,128]{3,2,1,0:T(8,128)(2,1)S(1)} %collective-permute-done.12.refs_0_, ...), custom_call_target="tpu_custom_call" | custom-call | flops 201326592 | bytes 4194304 | tf_op jit(solution)/shard_map/last_tiles/pallas_call | solution.py:352
  58.1 2.3 %collective-permute-done.16.refs_1_ = bf16[192,256]{1,0:T(8,128)(2,1)S(1)} collective-permute-done((bf16[192,256]{1,0:T(8,128)(2,1)S(1)}, bf16[192,256]{1,0:T(8,128)(2,1)S(1)}, u32[]{:S(2)}, u32[]{:S(2)}) %collective-permute-start.16) | collective-permute-done | bytes 98336 | tf_op jit(solution)/shard_map/ppermute | solution.py:441
  60.4 1.5 %finish.1 = bf16[48,4,512]{2,1,0:T(4,128)(2,1)} custom-call(s32[2]{0:T(128)S(1)} %pad_add_fusion.me_ref.refs_2_, bf16[512,512]{1,0:T(8,128)(2,1)S(1)} %copy-done, f32[192,512]{1,0:T(8,128)S(1)} %get-tuple-element.30.resid_ref, bf16[192,256]{1,0:T(8,128)(2,1)S(1)} %last_tiles.3.refs_0_, bf16[192,256]{1,0:T(8,128)(2,1)S(1)} %collective-permute-done.16.refs_1_), custom_call_target="tpu_custom_call" | custom-call | flops 100663296 | bytes 1048576 | tf_op jit(solution)/shard_map/finish/pallas_call | solution.py:375
  (29 shorter events, 4.5 us)
Async XLA Ops:
  0.0 6.7 %copy-start.2 = (bf16[48,4,512]{2,1,0:T(4,128)(2,1)S(1)}, bf16[48,4,512]{2,1,0:T(4,128)(2,1)}, u32[]{:S(2)}) copy-start(bf16[48,4,512]{2,1,0:T(4,128)(2,1)} %refs_0_.1) | copy-start | bytes 589828
  1.3 0.7 %copy-start.1 = (s32[1,12]{1,0:T(1,128)S(1)}, s32[1,12]{1,0:T(1,128)}, u32[]{:S(2)}) copy-start(s32[1,12]{1,0:T(1,128)} %refs_3_.1) | copy-start | bytes 148
  2.6 30.4 %collective-permute-start.8 = (bf16[4,4,128,128]{3,2,1,0:T(8,128)(2,1)S(1)}, bf16[4,4,128,128]{3,2,1,0:T(8,128)(2,1)S(1)}, u32[]{:S(2)}, u32[]{:S(2)}) collective-permute-start(bf16[4,4,128,128]{3,2,1,0:T(8,128)(2,1)S(1)} %tie.1.tiles_ref), channel_id=1, source_target_pairs={{0,16},{2,18},{4,20},{6,22},{8,24},{10,26},{12,28},{14,30},{16,0},... | collective-permute-start | bytes 1572872 | tf_op jit(solution)/shard_map/ppermute | solution.py:410
  6.7 11.3 %collective-permute-start = (bf16[48,4,512]{2,1,0:T(4,128)(2,1)S(1)}, bf16[48,4,512]{2,1,0:T(4,128)(2,1)S(1)}, u32[]{:S(2)}, u32[]{:S(2)}) collective-permute-start(bf16[48,4,512]{2,1,0:T(4,128)(2,1)S(1)} %copy-done.2), channel_id=1, source_target_pairs={{0,1},{1,0},{2,3},{3,2},{4,5},{5,4},{6,7},{7,6},{8,9},{9,8},{10,11... | collective-permute-start | bytes 589832 | tf_op jit(solution)/shard_map/ppermute | solution.py:414
  18.8 5.0 %collective-permute-start.1 = (bf16[1,4,128,128]{3,2,1,0:T(8,128)(2,1)S(1)}, bf16[1,4,128,128]{3,2,1,0:T(8,128)(2,1)S(1)}, u32[]{:S(2)}, u32[]{:S(2)}) collective-permute-start(bf16[1,4,128,128]{3,2,1,0:T(8,128)(2,1)S(1)} %get-tuple-element.28), channel_id=1, source_target_pairs={{0,2},{2,0},{4,6},{6,4},{8,10},{10,8},{12,14},{14,12},{16,18},{18,... | collective-permute-start | bytes 393224 | tf_op jit(solution)/shard_map/ppermute | solution.py:425
  18.8 6.1 %collective-permute-start.2 = (bf16[1,4,128,128]{3,2,1,0:T(8,128)(2,1)S(1)}, bf16[1,4,128,128]{3,2,1,0:T(8,128)(2,1)S(1)}, u32[]{:S(2)}, u32[]{:S(2)}) collective-permute-start(bf16[1,4,128,128]{3,2,1,0:T(8,128)(2,1)S(1)} %get-tuple-element.29), channel_id=1, source_target_pairs={{0,4},{2,6},{4,0},{6,2},{8,12},{10,14},{12,8},{14,10},{16,20},{18,... | collective-permute-start | bytes 393224 | tf_op jit(solution)/shard_map/ppermute | solution.py:425
  20.4 15.3 %collective-permute-start.3 = (bf16[1,4,128,128]{3,2,1,0:T(8,128)(2,1)S(1)}, bf16[1,4,128,128]{3,2,1,0:T(8,128)(2,1)S(1)}, u32[]{:S(2)}, u32[]{:S(2)}) collective-permute-start(bf16[1,4,128,128]{3,2,1,0:T(8,128)(2,1)S(1)} %get-tuple-element.32), channel_id=1, source_target_pairs={{0,8},{2,10},{4,12},{6,14},{8,0},{10,2},{12,4},{14,6},{16,24},{18,... | collective-permute-start | bytes 393224 | tf_op jit(solution)/shard_map/ppermute | solution.py:425
  22.9 13.6 %collective-permute-start.4 = (bf16[1,4,128,128]{3,2,1,0:T(8,128)(2,1)S(1)}, bf16[1,4,128,128]{3,2,1,0:T(8,128)(2,1)S(1)}, u32[]{:S(2)}, u32[]{:S(2)}) collective-permute-start(bf16[1,4,128,128]{3,2,1,0:T(8,128)(2,1)S(1)} %get-tuple-element.33), channel_id=1, source_target_pairs={{0,12},{2,14},{4,8},{6,10},{8,4},{10,6},{12,0},{14,2},{16,28},{18,... | collective-permute-start | bytes 393224 | tf_op jit(solution)/shard_map/ppermute | solution.py:425
  23.7 14.5 %collective-permute-start.5 = (bf16[1,4,128,128]{3,2,1,0:T(8,128)(2,1)S(1)}, bf16[1,4,128,128]{3,2,1,0:T(8,128)(2,1)S(1)}, u32[]{:S(2)}, u32[]{:S(2)}) collective-permute-start(bf16[1,4,128,128]{3,2,1,0:T(8,128)(2,1)S(1)} %get-tuple-element.34), channel_id=1, source_target_pairs={{0,10},{2,8},{4,14},{6,12},{8,2},{10,0},{12,6},{14,4},{16,26},{18,... | collective-permute-start | bytes 393224 | tf_op jit(solution)/shard_map/ppermute | solution.py:425
  25.0 17.1 %collective-permute-start.6 = (bf16[1,4,128,128]{3,2,1,0:T(8,128)(2,1)S(1)}, bf16[1,4,128,128]{3,2,1,0:T(8,128)(2,1)S(1)}, u32[]{:S(2)}, u32[]{:S(2)}) collective-permute-start(bf16[1,4,128,128]{3,2,1,0:T(8,128)(2,1)S(1)} %get-tuple-element.35), channel_id=1, source_target_pairs={{0,14},{2,12},{4,10},{6,8},{8,6},{10,4},{12,2},{14,0},{16,30},{18,... | collective-permute-start | bytes 393224 | tf_op jit(solution)/shard_map/ppermute | solution.py:425
  32.9 9.2 %collective-permute-start.7 = (bf16[1,4,128,128]{3,2,1,0:T(8,128)(2,1)S(1)}, bf16[1,4,128,128]{3,2,1,0:T(8,128)(2,1)S(1)}, u32[]{:S(2)}, u32[]{:S(2)}) collective-permute-start(bf16[1,4,128,128]{3,2,1,0:T(8,128)(2,1)S(1)} %get-tuple-element.36), channel_id=1, source_target_pairs={{0,6},{2,4},{4,2},{6,0},{8,14},{10,12},{12,10},{14,8},{16,22},{18,... | collective-permute-start | bytes 393224 | tf_op jit(solution)/shard_map/ppermute | solution.py:425
  35.7 8.3 %collective-permute-start.9 = (bf16[1,4,128,128]{3,2,1,0:T(8,128)(2,1)S(1)}, bf16[1,4,128,128]{3,2,1,0:T(8,128)(2,1)S(1)}, u32[]{:S(2)}, u32[]{:S(2)}) collective-permute-start(bf16[1,4,128,128]{3,2,1,0:T(8,128)(2,1)S(1)} %get-tuple-element.40), channel_id=1, source_target_pairs={{0,8},{2,10},{4,12},{6,14},{8,0},{10,2},{12,4},{14,6},{16,24},{18,... | collective-permute-start | bytes 393224 | tf_op jit(solution)/shard_map/ppermute | solution.py:425
  36.5 12.7 %collective-permute-start.10 = (bf16[1,4,128,128]{3,2,1,0:T(8,128)(2,1)S(1)}, bf16[1,4,128,128]{3,2,1,0:T(8,128)(2,1)S(1)}, u32[]{:S(2)}, u32[]{:S(2)}) collective-permute-start(bf16[1,4,128,128]{3,2,1,0:T(8,128)(2,1)S(1)} %get-tuple-element.41), channel_id=1, source_target_pairs={{0,4},{2,6},{4,0},{6,2},{8,12},{10,14},{12,8},{14,10},{16,20},{18,... | collective-permute-start | bytes 393224 | tf_op jit(solution)/shard_map/ppermute | solution.py:425
  38.2 13.4 %collective-permute-start.11 = (bf16[1,4,128,128]{3,2,1,0:T(8,128)(2,1)S(1)}, bf16[1,4,128,128]{3,2,1,0:T(8,128)(2,1)S(1)}, u32[]{:S(2)}, u32[]{:S(2)}) collective-permute-start(bf16[1,4,128,128]{3,2,1,0:T(8,128)(2,1)S(1)} %get-tuple-element.42), channel_id=1, source_target_pairs={{0,12},{2,14},{4,8},{6,10},{8,4},{10,6},{12,0},{14,2},{16,28},{18,... | collective-permute-start | bytes 393224 | tf_op jit(solution)/shard_map/ppermute | solution.py:425
  42.1 11.5 %collective-permute-start.12 = (bf16[1,4,128,128]{3,2,1,0:T(8,128)(2,1)S(1)}, bf16[1,4,128,128]{3,2,1,0:T(8,128)(2,1)S(1)}, u32[]{:S(2)}, u32[]{:S(2)}) collective-permute-start(bf16[1,4,128,128]{3,2,1,0:T(8,128)(2,1)S(1)} %get-tuple-element.45), channel_id=1, source_target_pairs={{0,14},{2,12},{4,10},{6,8},{8,6},{10,4},{12,2},{14,0},{16,30},{18,... | collective-permute-start | bytes 393224 | tf_op jit(solution)/shard_map/ppermute | solution.py:425
  42.1 11.5 %collective-permute-start.13 = (bf16[1,4,128,128]{3,2,1,0:T(8,128)(2,1)S(1)}, bf16[1,4,128,128]{3,2,1,0:T(8,128)(2,1)S(1)}, u32[]{:S(2)}, u32[]{:S(2)}) collective-permute-start(bf16[1,4,128,128]{3,2,1,0:T(8,128)(2,1)S(1)} %get-tuple-element.46), channel_id=1, source_target_pairs={{0,10},{2,8},{4,14},{6,12},{8,2},{10,0},{12,6},{14,4},{16,26},{18,... | collective-permute-start | bytes 393224 | tf_op jit(solution)/shard_map/ppermute | solution.py:425
  44.0 9.7 %collective-permute-start.14 = (bf16[1,4,128,128]{3,2,1,0:T(8,128)(2,1)S(1)}, bf16[1,4,128,128]{3,2,1,0:T(8,128)(2,1)S(1)}, u32[]{:S(2)}, u32[]{:S(2)}) collective-permute-start(bf16[1,4,128,128]{3,2,1,0:T(8,128)(2,1)S(1)} %get-tuple-element.47), channel_id=1, source_target_pairs={{0,6},{2,4},{4,2},{6,0},{8,14},{10,12},{12,10},{14,8},{16,22},{18,... | collective-permute-start | bytes 393224 | tf_op jit(solution)/shard_map/ppermute | solution.py:425
  49.1 4.5 %collective-permute-start.15 = (bf16[1,4,128,128]{3,2,1,0:T(8,128)(2,1)S(1)}, bf16[1,4,128,128]{3,2,1,0:T(8,128)(2,1)S(1)}, u32[]{:S(2)}, u32[]{:S(2)}) collective-permute-start(bf16[1,4,128,128]{3,2,1,0:T(8,128)(2,1)S(1)} %get-tuple-element.48), channel_id=1, source_target_pairs={{0,2},{2,0},{4,6},{6,4},{8,10},{10,8},{12,14},{14,12},{16,18},{18,... | collective-permute-start | bytes 393224 | tf_op jit(solution)/shard_map/ppermute | solution.py:425
  53.6 6.7 %copy-start = (bf16[512,512]{1,0:T(8,128)(2,1)S(1)}, bf16[512,512]{1,0:T(8,128)(2,1)}, u32[]{:S(2)}) copy-start(bf16[512,512]{1,0:T(8,128)(2,1)} %weight_ref.1) | copy-start | bytes 1572868
  55.1 5.3 %collective-permute-start.16 = (bf16[192,256]{1,0:T(8,128)(2,1)S(1)}, bf16[192,256]{1,0:T(8,128)(2,1)S(1)}, u32[]{:S(2)}, u32[]{:S(2)}) collective-permute-start(bf16[192,256]{1,0:T(8,128)(2,1)S(1)} %last_tiles.2.refs_4_), channel_id=1, source_target_pairs={{0,1},{1,0},{2,3},{3,2},{4,5},{5,4},{6,7},{7,6},{8,9},{9,8},{10,11... | collective-permute-start | bytes 294920 | tf_op jit(solution)/shard_map/ppermute | solution.py:441

commit v16 on v15

--- a/solution.py
+++ b/solution.py
@@ -415,7 +415,8 @@
 
     across = half // 2
     near_order = [0, 1] + sorted(range(2, half), key=lambda step: (step != 2, not step & across, step & 1, step))
-    far_order = [0, across] + sorted(set(range(1, half)) - {across}, key=lambda step: (step != 2, not step & across, step & 1, -step))
+    rest = sorted(set(range(2, half)) - {across}, key=lambda step: (not step & across, step & 1, -step))
+    far_order = list(dict.fromkeys([0, across, 1] + rest[:1] + rest[-2:-1] + rest[1:-2] + rest[-1:]))
     near_slots, far_slots = (near_order, [half + step for step in far_order]) if paired else ([0], [half])
 
     def spread(tiles, which, order, after):
@@ -427,10 +428,10 @@
 
     if group_width % 128:
         w_query = lax.dynamic_slice_in_dim(w_query, col_me * group_width, group_width, 1)
-    near = spread(heads_first, 0, near_order, cells[1:])
     residual, asked = front(cells, tile_ids, me, key_mask, gain_col, w_qkv, w_col_out, gain_tile, w_query,
-                            heads_all, head_size, cols, heads_here, tiles_here, row_size, paired, near[:3])
-    far = spread(mirrored, 1, far_order, [asked])
+                            heads_all, head_size, cols, heads_here, tiles_here, row_size, paired, [])
+    near = spread(heads_first, 0, near_order, [asked])
+    far = spread(mirrored, 1, far_order, near[1:3])
     sums, tops = first_tiles(asked, near, near_slots, rows * cols)
     batch = len(far) // 2
     if batch:

time: 62.1 us -> 64.3 us (1.035)
  waiting for transfers between devices: 11.4 us -> 23.9 us
  blocking collectives: 9.81 us -> 0 us
  starting transfers between devices: 22.1 us -> 21.1 us
    all_to_all x1 -> x0, blocking collectives: 9.81 us -> none  [swap(): lax.all_to_all(value, 'rows', split_axis=0, concat_axis=0, tiled=True, ax...]
    ppermute x14, waiting for transfers between devices: 9.09 us -> 18.5 us  [spread(): lax.ppermute(tile, 'rows', [(row, row ^ step) for row in range(row_size)])]
    ppermute x14, starting transfers between devices: 15 us -> 10.2 us  [spread(): lax.ppermute(tile, 'rows', [(row, row ^ step) for row in range(row_size)])]
    all_to_all x0 -> x1, starting transfers between devices: none -> 3.78 us  [swap(): lax.all_to_all(value, 'rows', split_axis=0, concat_axis=0, tiled=True, ax...]
    ppermute x1, waiting for transfers between devices: 0.01 us -> 2.53 us  [shards(): mirrored = lax.ppermute(heads_first, 'rows', turn(row_size, half))]
    ppermute x1, waiting for transfers between devices: 0.01 us -> 1.06 us  [shards(): cells.append(lax.ppermute(fact_cells, 'cols', turn(col_size, -step)))]
  transfers between devices with their start and end apart: 17 -> 18, of which waited for: 6 -> 12; matrix products, arithmetic and copies ran while one was open for 0% -> 0% of each run, Pallas kernels for 21% -> 20%
where the time goes in v16:
time: 64.3 us; the launch traced here: 64.1 us
  waiting for transfers between devices  23.9 us (37%)
  starting transfers between devices  21.1 us (33%)
  Pallas kernels  17 us (26%)
  local copies, waits for them, and re-layouts  1.84 us (3%)
    ppermute x14, waiting for transfers between devices, spread(): lax.ppermute(tile, 'rows', [(row, row ^ step) for row in range(row_size)])  18.5 us
    ppermute x14, starting transfers between devices, spread(): lax.ppermute(tile, 'rows', [(row, row ^ step) for row in range(row_size)])  10.2 us
    pallas_call x1, Pallas kernels, front(): pl.pallas_call(functools.partial(front_kernel, groups, heads, head_size,...  5.51 us
    ppermute x1, starting transfers between devices, shards(): mirrored = lax.ppermute(heads_first, 'rows', turn(row_size, half))  4.04 us
    all_to_all x1, starting transfers between devices, swap(): lax.all_to_all(value, 'rows', split_axis=0, concat_axis=0, tiled=True, ax...  3.78 us
    pallas_call x2, Pallas kernels, last_tiles(): pl.pallas_call(functools.partial(last_kernel, slots, groups), out_shape=(...  2.87 us
    ppermute x1, waiting for transfers between devices, shards(): mirrored = lax.ppermute(heads_first, 'rows', turn(row_size, half))  2.53 us
    pallas_call x1, Pallas kernels, first_tiles(): pl.pallas_call(functools.partial(first_kernel, slots, rows if rows <= 512...  2.38 us
  transfers between devices with their start and end apart: 18, of which 12 were waited for; matrix products, arithmetic and copies ran while one was open for 0% of the time, Pallas kernels for 20%

profile of v16, /device:TPU:0, one launch (start us, length us, event | category | flops | bytes accessed | tf_op | source)
XLA Modules:
  0.0 64.1 jit_solution(1338193345393690613)
XLA Ops:
  3.1 4.0 %collective-permute-start.8 = (bf16[4,4,128,128]{3,2,1,0:T(8,128)(2,1)S(1)}, bf16[4,4,128,128]{3,2,1,0:T(8,128)(2,1)S(1)}, u32[]{:S(2)}, u32[]{:S(2)}) collective-permute-start(bf16[4,4,128,128]{3,2,1,0:T(8,128)(2,1)S(1)} %tie.1.tiles_ref), channel_id=1, source_target_pairs={{0,16},{2,18},{4,20},{6,22},{8,24},{10,26},{12,28},{14,30},{16,0},... | collective-permute-start | bytes 1572872 | tf_op jit(solution)/shard_map/ppermute | solution.py:410
  7.2 1.5 %collective-permute-start = (bf16[48,4,512]{2,1,0:T(4,128)(2,1)S(1)}, bf16[48,4,512]{2,1,0:T(4,128)(2,1)S(1)}, u32[]{:S(2)}, u32[]{:S(2)}) collective-permute-start(bf16[48,4,512]{2,1,0:T(4,128)(2,1)S(1)} %copy-done.2), channel_id=1, source_target_pairs={{0,1},{1,0},{2,3},{3,2},{4,5},{5,4},{6,7},{7,6},{8,9},{9,8},{10,11... | collective-permute-start | bytes 589832 | tf_op jit(solution)/shard_map/ppermute | solution.py:414
  8.7 3.8 %all-to-all-start = ((s32[8,2,128]{2,1,0:T(2,128)}), s32[8,2,128]{2,1,0:T(2,128)S(1)}, u32[]{:S(2)}, u32[]{:S(2)}) async-start(s32[8,2,128]{2,1,0:T(2,128)} %request.1.after_ref), calls=%async_computation | async-start | bytes 16384 | tf_op jit(solution)/shard_map/all_to_all | solution.py:405
  13.5 5.5 %front.1 = (f32[192,512]{1,0:T(8,128)S(1)}, bf16[4,384,128]{2,1,0:T(8,128)(2,1)S(1)}) custom-call(bf16[48,4,512]{2,1,0:T(4,128)(2,1)} %refs_0_.1, bf16[48,4,512]{2,1,0:T(4,128)(2,1)S(1)} %collective-permute-done.refs_1_, s32[2]{0:T(128)S(1)} %pad_add_fusion.refs_2_.me_ref, s32[1,12]{1,0:T(1,128)} %ids_ref.1, s32[12,48]{1,0:T(8,128)} %bitcast.9, ...), custom_call_target="tpu_custom_call" | custom-call | flops 1006632960 | bytes 4194304 | tf_op jit(solution)/shard_map/front/pallas_call | solution.py:235
  19.9 1.6 %collective-permute-start.2 = (bf16[1,4,128,128]{3,2,1,0:T(8,128)(2,1)S(1)}, bf16[1,4,128,128]{3,2,1,0:T(8,128)(2,1)S(1)}, u32[]{:S(2)}, u32[]{:S(2)}) collective-permute-start(bf16[1,4,128,128]{3,2,1,0:T(8,128)(2,1)S(1)} %get-tuple-element.31), channel_id=1, source_target_pairs={{0,4},{2,6},{4,0},{6,2},{8,12},{10,14},{12,8},{14,10},{16,20},{18,... | collective-permute-start | bytes 393224 | tf_op jit(solution)/shard_map/ppermute | solution.py:426
  21.5 1.9 %collective-permute-start.3 = (bf16[1,4,128,128]{3,2,1,0:T(8,128)(2,1)S(1)}, bf16[1,4,128,128]{3,2,1,0:T(8,128)(2,1)S(1)}, u32[]{:S(2)}, u32[]{:S(2)}) collective-permute-start(bf16[1,4,128,128]{3,2,1,0:T(8,128)(2,1)S(1)} %get-tuple-element.32), channel_id=1, source_target_pairs={{0,8},{2,10},{4,12},{6,14},{8,0},{10,2},{12,4},{14,6},{16,24},{18,... | collective-permute-start | bytes 393224 | tf_op jit(solution)/shard_map/ppermute | solution.py:426
  24.2 1.2 %collective-permute-start.5 = (bf16[1,4,128,128]{3,2,1,0:T(8,128)(2,1)S(1)}, bf16[1,4,128,128]{3,2,1,0:T(8,128)(2,1)S(1)}, u32[]{:S(2)}, u32[]{:S(2)}) collective-permute-start(bf16[1,4,128,128]{3,2,1,0:T(8,128)(2,1)S(1)} %get-tuple-element.34), channel_id=1, source_target_pairs={{0,10},{2,8},{4,14},{6,12},{8,2},{10,0},{12,6},{14,4},{16,26},{18,... | collective-permute-start | bytes 393224 | tf_op jit(solution)/shard_map/ppermute | solution.py:426
  25.8 2.1 %collective-permute-start.6 = (bf16[1,4,128,128]{3,2,1,0:T(8,128)(2,1)S(1)}, bf16[1,4,128,128]{3,2,1,0:T(8,128)(2,1)S(1)}, u32[]{:S(2)}, u32[]{:S(2)}) collective-permute-start(bf16[1,4,128,128]{3,2,1,0:T(8,128)(2,1)S(1)} %get-tuple-element.35), channel_id=1, source_target_pairs={{0,14},{2,12},{4,10},{6,8},{8,6},{10,4},{12,2},{14,0},{16,30},{18,... | collective-permute-start | bytes 393224 | tf_op jit(solution)/shard_map/ppermute | solution.py:426
  27.9 2.5 %collective-permute-done.8.tiles_ref = bf16[4,4,128,128]{3,2,1,0:T(8,128)(2,1)S(1)} collective-permute-done((bf16[4,4,128,128]{3,2,1,0:T(8,128)(2,1)S(1)}, bf16[4,4,128,128]{3,2,1,0:T(8,128)(2,1)S(1)}, u32[]{:S(2)}, u32[]{:S(2)}) %collective-permute-start.8) | collective-permute-done | bytes 524320 | tf_op jit(solution)/shard_map/ppermute | solution.py:410
  31.3 1.9 %collective-permute-done.3.refs_3_ = bf16[1,4,128,128]{3,2,1,0:T(8,128)(2,1)S(1)} collective-permute-done((bf16[1,4,128,128]{3,2,1,0:T(8,128)(2,1)S(1)}, bf16[1,4,128,128]{3,2,1,0:T(8,128)(2,1)S(1)}, u32[]{:S(2)}, u32[]{:S(2)}) %collective-permute-start.3) | collective-permute-done | bytes 131104 | tf_op jit(solution)/shard_map/ppermute | solution.py:426
  33.2 3.8 %collective-permute-done.4.refs_4_ = bf16[1,4,128,128]{3,2,1,0:T(8,128)(2,1)S(1)} collective-permute-done((bf16[1,4,128,128]{3,2,1,0:T(8,128)(2,1)S(1)}, bf16[1,4,128,128]{3,2,1,0:T(8,128)(2,1)S(1)}, u32[]{:S(2)}, u32[]{:S(2)}) %collective-permute-start.4) | collective-permute-done | bytes 131104 | tf_op jit(solution)/shard_map/ppermute | solution.py:426
  37.0 1.7 %collective-permute-done.5.refs_5_ = bf16[1,4,128,128]{3,2,1,0:T(8,128)(2,1)S(1)} collective-permute-done((bf16[1,4,128,128]{3,2,1,0:T(8,128)(2,1)S(1)}, bf16[1,4,128,128]{3,2,1,0:T(8,128)(2,1)S(1)}, u32[]{:S(2)}, u32[]{:S(2)}) %collective-permute-start.5) | collective-permute-done | bytes 131104 | tf_op jit(solution)/shard_map/ppermute | solution.py:426
  39.4 3.2 %collective-permute-done.6.refs_6_ = bf16[1,4,128,128]{3,2,1,0:T(8,128)(2,1)S(1)} collective-permute-done((bf16[1,4,128,128]{3,2,1,0:T(8,128)(2,1)S(1)}, bf16[1,4,128,128]{3,2,1,0:T(8,128)(2,1)S(1)}, u32[]{:S(2)}, u32[]{:S(2)}) %collective-permute-start.6) | collective-permute-done | bytes 131104 | tf_op jit(solution)/shard_map/ppermute | solution.py:426
  43.0 1.5 %collective-permute-done.9.refs_1_ = bf16[1,4,128,128]{3,2,1,0:T(8,128)(2,1)S(1)} collective-permute-done((bf16[1,4,128,128]{3,2,1,0:T(8,128)(2,1)S(1)}, bf16[1,4,128,128]{3,2,1,0:T(8,128)(2,1)S(1)}, u32[]{:S(2)}, u32[]{:S(2)}) %collective-permute-start.9) | collective-permute-done | bytes 131104 | tf_op jit(solution)/shard_map/ppermute | solution.py:426
  44.5 1.3 %collective-permute-start.14 = (bf16[1,4,128,128]{3,2,1,0:T(8,128)(2,1)S(1)}, bf16[1,4,128,128]{3,2,1,0:T(8,128)(2,1)S(1)}, u32[]{:S(2)}, u32[]{:S(2)}) collective-permute-start(bf16[1,4,128,128]{3,2,1,0:T(8,128)(2,1)S(1)} %get-tuple-element.47), channel_id=1, source_target_pairs={{0,10},{2,8},{4,14},{6,12},{8,2},{10,0},{12,6},{14,4},{16,26},{18,... | collective-permute-start | bytes 393224 | tf_op jit(solution)/shard_map/ppermute | solution.py:426
  45.8 2.4 %first_tiles.1 = (f32[4,384,128]{2,1,0:T(8,128)S(1)}, f32[384,128]{1,0:T(8,128)S(1)}) custom-call(bf16[4,384,128]{2,1,0:T(8,128)(2,1)S(1)} %get-tuple-element.28.refs_0_.asked_ref, bf16[1,4,128,128]{3,2,1,0:T(8,128)(2,1)S(1)} %get-tuple-element.29.refs_0_, bf16[1,4,128,128]{3,2,1,0:T(8,128)(2,1)S(1)} %collective-permute-done.1.refs_1_.refs_0_, ...), custom_call_target="tpu_custom_call" | custom-call | flops 805306368 | bytes 4194304 | tf_op jit(solution)/shard_map/first_tiles/pallas_call | solution.py:285
  48.4 2.0 %more_tiles.1 = (f32[4,384,128]{2,1,0:T(8,128)S(1)}, f32[384,128]{1,0:T(8,128)S(1)}) custom-call(bf16[4,384,128]{2,1,0:T(8,128)(2,1)S(1)} %get-tuple-element.28.refs_0_.asked_ref, f32[4,384,128]{2,1,0:T(8,128)S(1)} %get-tuple-element.37.old_sums_ref, f32[384,128]{1,0:T(8,128)S(1)} %get-tuple-element.38.old_tops_ref, ...), custom_call_target="tpu_custom_call" | custom-call | flops 402653184 | bytes 4194304 | tf_op jit(solution)/shard_map/more_tiles/pallas_call | solution.py:318
  50.4 3.5 %collective-permute-done.12.refs_0_ = bf16[1,4,128,128]{3,2,1,0:T(8,128)(2,1)S(1)} collective-permute-done((bf16[1,4,128,128]{3,2,1,0:T(8,128)(2,1)S(1)}, bf16[1,4,128,128]{3,2,1,0:T(8,128)(2,1)S(1)}, u32[]{:S(2)}, u32[]{:S(2)}) %collective-permute-start.12) | collective-permute-done | bytes 131104 | tf_op jit(solution)/shard_map/ppermute | solution.py:426
  53.9 2.3 %collective-permute-done.15.refs_3_ = bf16[1,4,128,128]{3,2,1,0:T(8,128)(2,1)S(1)} collective-permute-done((bf16[1,4,128,128]{3,2,1,0:T(8,128)(2,1)S(1)}, bf16[1,4,128,128]{3,2,1,0:T(8,128)(2,1)S(1)}, u32[]{:S(2)}, u32[]{:S(2)}) %collective-permute-start.15) | collective-permute-done | bytes 131104 | tf_op jit(solution)/shard_map/ppermute | solution.py:426
  56.2 1.4 %last_tiles.2.refs_4_ = bf16[192,256]{1,0:T(8,128)(2,1)S(1)} custom-call(bf16[4,384,128]{2,1,0:T(8,128)(2,1)S(1)} %get-tuple-element.28.refs_0_.asked_ref, f32[4,384,128]{2,1,0:T(8,128)S(1)} %get-tuple-element.43.sums_ref, f32[384,128]{1,0:T(8,128)S(1)} %get-tuple-element.44.tops_ref, bf16[1,4,128,128]{3,2,1,0:T(8,128)(2,1)S(1)} %collective-permute-done.12.refs_0_, ...), custom_call_target="tpu_custom_call" | custom-call | flops 201326592 | bytes 4194304 | tf_op jit(solution)/shard_map/last_tiles/pallas_call | solution.py:352
  57.7 1.6 %collective-permute-start.16 = (bf16[192,256]{1,0:T(8,128)(2,1)S(1)}, bf16[192,256]{1,0:T(8,128)(2,1)S(1)}, u32[]{:S(2)}, u32[]{:S(2)}) collective-permute-start(bf16[192,256]{1,0:T(8,128)(2,1)S(1)} %last_tiles.2.refs_4_), channel_id=1, source_target_pairs={{0,1},{1,0},{2,3},{3,2},{4,5},{5,4},{6,7},{7,6},{8,9},{9,8},{10,11... | collective-permute-start | bytes 294920 | tf_op jit(solution)/shard_map/ppermute | solution.py:442
  59.3 1.4 %last_tiles.3.refs_0_ = bf16[192,256]{1,0:T(8,128)(2,1)S(1)} custom-call(bf16[4,384,128]{2,1,0:T(8,128)(2,1)S(1)} %get-tuple-element.28.refs_0_.asked_ref, f32[4,384,128]{2,1,0:T(8,128)S(1)} %get-tuple-element.43.sums_ref, f32[384,128]{1,0:T(8,128)S(1)} %get-tuple-element.44.tops_ref, bf16[1,4,128,128]{3,2,1,0:T(8,128)(2,1)S(1)} %collective-permute-done.12.refs_0_, ...), custom_call_target="tpu_custom_call" | custom-call | flops 201326592 | bytes 4194304 | tf_op jit(solution)/shard_map/last_tiles/pallas_call | solution.py:352
  60.7 1.8 %collective-permute-done.16.refs_1_ = bf16[192,256]{1,0:T(8,128)(2,1)S(1)} collective-permute-done((bf16[192,256]{1,0:T(8,128)(2,1)S(1)}, bf16[192,256]{1,0:T(8,128)(2,1)S(1)}, u32[]{:S(2)}, u32[]{:S(2)}) %collective-permute-start.16) | collective-permute-done | bytes 98336 | tf_op jit(solution)/shard_map/ppermute | solution.py:442
  62.6 1.5 %finish.1 = bf16[48,4,512]{2,1,0:T(4,128)(2,1)} custom-call(s32[2]{0:T(128)S(1)} %pad_add_fusion.refs_2_.me_ref, bf16[512,512]{1,0:T(8,128)(2,1)S(1)} %copy-done, f32[192,512]{1,0:T(8,128)S(1)} %get-tuple-element.27.resid_ref, bf16[192,256]{1,0:T(8,128)(2,1)S(1)} %last_tiles.3.refs_0_, bf16[192,256]{1,0:T(8,128)(2,1)S(1)} %collective-permute-done.16.refs_1_), custom_call_target="tpu_custom_call" | custom-call | flops 100663296 | bytes 1048576 | tf_op jit(solution)/shard_map/finish/pallas_call | solution.py:375
  (30 shorter events, 8.4 us)
Async XLA Ops:
  0.0 7.2 %copy-start.2 = (bf16[48,4,512]{2,1,0:T(4,128)(2,1)S(1)}, bf16[48,4,512]{2,1,0:T(4,128)(2,1)}, u32[]{:S(2)}) copy-start(bf16[48,4,512]{2,1,0:T(4,128)(2,1)} %refs_0_.1) | copy-start | bytes 589828
  1.3 0.7 %copy-start.1 = (s32[1,12]{1,0:T(1,128)S(1)}, s32[1,12]{1,0:T(1,128)}, u32[]{:S(2)}) copy-start(s32[1,12]{1,0:T(1,128)} %ids_ref.1) | copy-start | bytes 148
  3.1 27.3 %collective-permute-start.8 = (bf16[4,4,128,128]{3,2,1,0:T(8,128)(2,1)S(1)}, bf16[4,4,128,128]{3,2,1,0:T(8,128)(2,1)S(1)}, u32[]{:S(2)}, u32[]{:S(2)}) collective-permute-start(bf16[4,4,128,128]{3,2,1,0:T(8,128)(2,1)S(1)} %tie.1.tiles_ref), channel_id=1, source_target_pairs={{0,16},{2,18},{4,20},{6,22},{8,24},{10,26},{12,28},{14,30},{16,0},... | collective-permute-start | bytes 1572872 | tf_op jit(solution)/shard_map/ppermute | solution.py:410
  7.2 6.4 %collective-permute-start = (bf16[48,4,512]{2,1,0:T(4,128)(2,1)S(1)}, bf16[48,4,512]{2,1,0:T(4,128)(2,1)S(1)}, u32[]{:S(2)}, u32[]{:S(2)}) collective-permute-start(bf16[48,4,512]{2,1,0:T(4,128)(2,1)S(1)} %copy-done.2), channel_id=1, source_target_pairs={{0,1},{1,0},{2,3},{3,2},{4,5},{5,4},{6,7},{7,6},{8,9},{9,8},{10,11... | collective-permute-start | bytes 589832 | tf_op jit(solution)/shard_map/ppermute | solution.py:414
  8.7 10.4 %all-to-all-start = ((s32[8,2,128]{2,1,0:T(2,128)}), s32[8,2,128]{2,1,0:T(2,128)S(1)}, u32[]{:S(2)}, u32[]{:S(2)}) async-start(s32[8,2,128]{2,1,0:T(2,128)} %request.1.after_ref), calls=%async_computation | async-start | bytes 16384 | tf_op jit(solution)/shard_map/all_to_all | solution.py:405
  19.8 4.4 %collective-permute-start.1 = (bf16[1,4,128,128]{3,2,1,0:T(8,128)(2,1)S(1)}, bf16[1,4,128,128]{3,2,1,0:T(8,128)(2,1)S(1)}, u32[]{:S(2)}, u32[]{:S(2)}) collective-permute-start(bf16[1,4,128,128]{3,2,1,0:T(8,128)(2,1)S(1)} %get-tuple-element.30), channel_id=1, source_target_pairs={{0,2},{2,0},{4,6},{6,4},{8,10},{10,8},{12,14},{14,12},{16,18},{18,... | collective-permute-start | bytes 393224 | tf_op jit(solution)/shard_map/ppermute | solution.py:426
  19.9 5.9 %collective-permute-start.2 = (bf16[1,4,128,128]{3,2,1,0:T(8,128)(2,1)S(1)}, bf16[1,4,128,128]{3,2,1,0:T(8,128)(2,1)S(1)}, u32[]{:S(2)}, u32[]{:S(2)}) collective-permute-start(bf16[1,4,128,128]{3,2,1,0:T(8,128)(2,1)S(1)} %get-tuple-element.31), channel_id=1, source_target_pairs={{0,4},{2,6},{4,0},{6,2},{8,12},{10,14},{12,8},{14,10},{16,20},{18,... | collective-permute-start | bytes 393224 | tf_op jit(solution)/shard_map/ppermute | solution.py:426
  21.5 11.7 %collective-permute-start.3 = (bf16[1,4,128,128]{3,2,1,0:T(8,128)(2,1)S(1)}, bf16[1,4,128,128]{3,2,1,0:T(8,128)(2,1)S(1)}, u32[]{:S(2)}, u32[]{:S(2)}) collective-permute-start(bf16[1,4,128,128]{3,2,1,0:T(8,128)(2,1)S(1)} %get-tuple-element.32), channel_id=1, source_target_pairs={{0,8},{2,10},{4,12},{6,14},{8,0},{10,2},{12,4},{14,6},{16,24},{18,... | collective-permute-start | bytes 393224 | tf_op jit(solution)/shard_map/ppermute | solution.py:426
  23.4 13.7 %collective-permute-start.4 = (bf16[1,4,128,128]{3,2,1,0:T(8,128)(2,1)S(1)}, bf16[1,4,128,128]{3,2,1,0:T(8,128)(2,1)S(1)}, u32[]{:S(2)}, u32[]{:S(2)}) collective-permute-start(bf16[1,4,128,128]{3,2,1,0:T(8,128)(2,1)S(1)} %get-tuple-element.33), channel_id=1, source_target_pairs={{0,12},{2,14},{4,8},{6,10},{8,4},{10,6},{12,0},{14,2},{16,28},{18,... | collective-permute-start | bytes 393224 | tf_op jit(solution)/shard_map/ppermute | solution.py:426
  24.2 14.5 %collective-permute-start.5 = (bf16[1,4,128,128]{3,2,1,0:T(8,128)(2,1)S(1)}, bf16[1,4,128,128]{3,2,1,0:T(8,128)(2,1)S(1)}, u32[]{:S(2)}, u32[]{:S(2)}) collective-permute-start(bf16[1,4,128,128]{3,2,1,0:T(8,128)(2,1)S(1)} %get-tuple-element.34), channel_id=1, source_target_pairs={{0,10},{2,8},{4,14},{6,12},{8,2},{10,0},{12,6},{14,4},{16,26},{18,... | collective-permute-start | bytes 393224 | tf_op jit(solution)/shard_map/ppermute | solution.py:426
  25.8 16.7 %collective-permute-start.6 = (bf16[1,4,128,128]{3,2,1,0:T(8,128)(2,1)S(1)}, bf16[1,4,128,128]{3,2,1,0:T(8,128)(2,1)S(1)}, u32[]{:S(2)}, u32[]{:S(2)}) collective-permute-start(bf16[1,4,128,128]{3,2,1,0:T(8,128)(2,1)S(1)} %get-tuple-element.35), channel_id=1, source_target_pairs={{0,14},{2,12},{4,10},{6,8},{8,6},{10,4},{12,2},{14,0},{16,30},{18,... | collective-permute-start | bytes 393224 | tf_op jit(solution)/shard_map/ppermute | solution.py:426
  30.4 12.6 %collective-permute-start.7 = (bf16[1,4,128,128]{3,2,1,0:T(8,128)(2,1)S(1)}, bf16[1,4,128,128]{3,2,1,0:T(8,128)(2,1)S(1)}, u32[]{:S(2)}, u32[]{:S(2)}) collective-permute-start(bf16[1,4,128,128]{3,2,1,0:T(8,128)(2,1)S(1)} %get-tuple-element.36), channel_id=1, source_target_pairs={{0,6},{2,4},{4,2},{6,0},{8,14},{10,12},{12,10},{14,8},{16,22},{18,... | collective-permute-start | bytes 393224 | tf_op jit(solution)/shard_map/ppermute | solution.py:426
  33.2 11.3 %collective-permute-start.9 = (bf16[1,4,128,128]{3,2,1,0:T(8,128)(2,1)S(1)}, bf16[1,4,128,128]{3,2,1,0:T(8,128)(2,1)S(1)}, u32[]{:S(2)}, u32[]{:S(2)}) collective-permute-start(bf16[1,4,128,128]{3,2,1,0:T(8,128)(2,1)S(1)} %get-tuple-element.40), channel_id=1, source_target_pairs={{0,8},{2,10},{4,12},{6,14},{8,0},{10,2},{12,4},{14,6},{16,24},{18,... | collective-permute-start | bytes 393224 | tf_op jit(solution)/shard_map/ppermute | solution.py:426
  37.0 8.7 %collective-permute-start.10 = (bf16[1,4,128,128]{3,2,1,0:T(8,128)(2,1)S(1)}, bf16[1,4,128,128]{3,2,1,0:T(8,128)(2,1)S(1)}, u32[]{:S(2)}, u32[]{:S(2)}) collective-permute-start(bf16[1,4,128,128]{3,2,1,0:T(8,128)(2,1)S(1)} %get-tuple-element.41), channel_id=1, source_target_pairs={{0,2},{2,0},{4,6},{6,4},{8,10},{10,8},{12,14},{14,12},{16,18},{18,... | collective-permute-start | bytes 393224 | tf_op jit(solution)/shard_map/ppermute | solution.py:426
  38.8 9.6 %collective-permute-start.11 = (bf16[1,4,128,128]{3,2,1,0:T(8,128)(2,1)S(1)}, bf16[1,4,128,128]{3,2,1,0:T(8,128)(2,1)S(1)}, u32[]{:S(2)}, u32[]{:S(2)}) collective-permute-start(bf16[1,4,128,128]{3,2,1,0:T(8,128)(2,1)S(1)} %get-tuple-element.42), channel_id=1, source_target_pairs={{0,12},{2,14},{4,8},{6,10},{8,4},{10,6},{12,0},{14,2},{16,28},{18,... | collective-permute-start | bytes 393224 | tf_op jit(solution)/shard_map/ppermute | solution.py:426
  42.5 11.4 %collective-permute-start.12 = (bf16[1,4,128,128]{3,2,1,0:T(8,128)(2,1)S(1)}, bf16[1,4,128,128]{3,2,1,0:T(8,128)(2,1)S(1)}, u32[]{:S(2)}, u32[]{:S(2)}) collective-permute-start(bf16[1,4,128,128]{3,2,1,0:T(8,128)(2,1)S(1)} %get-tuple-element.45), channel_id=1, source_target_pairs={{0,4},{2,6},{4,0},{6,2},{8,12},{10,14},{12,8},{14,10},{16,20},{18,... | collective-permute-start | bytes 393224 | tf_op jit(solution)/shard_map/ppermute | solution.py:426
  43.0 10.9 %collective-permute-start.13 = (bf16[1,4,128,128]{3,2,1,0:T(8,128)(2,1)S(1)}, bf16[1,4,128,128]{3,2,1,0:T(8,128)(2,1)S(1)}, u32[]{:S(2)}, u32[]{:S(2)}) collective-permute-start(bf16[1,4,128,128]{3,2,1,0:T(8,128)(2,1)S(1)} %get-tuple-element.46), channel_id=1, source_target_pairs={{0,14},{2,12},{4,10},{6,8},{8,6},{10,4},{12,2},{14,0},{16,30},{18,... | collective-permute-start | bytes 393224 | tf_op jit(solution)/shard_map/ppermute | solution.py:426
  44.5 9.5 %collective-permute-start.14 = (bf16[1,4,128,128]{3,2,1,0:T(8,128)(2,1)S(1)}, bf16[1,4,128,128]{3,2,1,0:T(8,128)(2,1)S(1)}, u32[]{:S(2)}, u32[]{:S(2)}) collective-permute-start(bf16[1,4,128,128]{3,2,1,0:T(8,128)(2,1)S(1)} %get-tuple-element.47), channel_id=1, source_target_pairs={{0,10},{2,8},{4,14},{6,12},{8,2},{10,0},{12,6},{14,4},{16,26},{18,... | collective-permute-start | bytes 393224 | tf_op jit(solution)/shard_map/ppermute | solution.py:426
  45.8 10.5 %collective-permute-start.15 = (bf16[1,4,128,128]{3,2,1,0:T(8,128)(2,1)S(1)}, bf16[1,4,128,128]{3,2,1,0:T(8,128)(2,1)S(1)}, u32[]{:S(2)}, u32[]{:S(2)}) collective-permute-start(bf16[1,4,128,128]{3,2,1,0:T(8,128)(2,1)S(1)} %get-tuple-element.48), channel_id=1, source_target_pairs={{0,6},{2,4},{4,2},{6,0},{8,14},{10,12},{12,10},{14,8},{16,22},{18,... | collective-permute-start | bytes 393224 | tf_op jit(solution)/shard_map/ppermute | solution.py:426
  56.2 6.3 %copy-start = (bf16[512,512]{1,0:T(8,128)(2,1)S(1)}, bf16[512,512]{1,0:T(8,128)(2,1)}, u32[]{:S(2)}) copy-start(bf16[512,512]{1,0:T(8,128)(2,1)} %weight_ref.1) | copy-start | bytes 1572868
  57.7 4.9 %collective-permute-start.16 = (bf16[192,256]{1,0:T(8,128)(2,1)S(1)}, bf16[192,256]{1,0:T(8,128)(2,1)S(1)}, u32[]{:S(2)}, u32[]{:S(2)}) collective-permute-start(bf16[192,256]{1,0:T(8,128)(2,1)S(1)} %last_tiles.2.refs_4_), channel_id=1, source_target_pairs={{0,1},{1,0},{2,3},{3,2},{4,5},{5,4},{6,7},{7,6},{8,9},{9,8},{10,11... | collective-permute-start | bytes 294920 | tf_op jit(solution)/shard_map/ppermute | solution.py:442

commit v17 on v16

--- a/solution.py
+++ b/solution.py
@@ -60,22 +60,20 @@
 
 
 def request_kernel(tiles_here, row_size, ids_ref, me_ref, out_ref):
-    half = row_size // 2
     peer, which = iota(out_ref.shape, 0), iota(out_ref.shape, 1)
     wanted = jnp.zeros(out_ref.shape, jnp.int32)
     for slot in range(ids_ref.shape[1]):
         tile = ids_ref[0, slot]
         owner = lax.div(tile, tiles_here)
-        far = jnp.where(lax.div(owner, half) == lax.div(me_ref[0], half), 0, 1)
-        here = (peer == jnp.where(tile < 0, -1, lax.rem(owner, half))) & (which == far)
-        wanted = jnp.where(here, lax.rem(tile, tiles_here), wanted)
+        target = jnp.where(which == 0, owner, lax.rem(owner + row_size // 2, row_size))
+        wanted = jnp.where((peer == target) & (tile >= 0), lax.rem(tile, tiles_here), wanted)
     out_ref[...] = wanted
 
 
 def request(ids, me, tiles_here, row_size):
     return pl.pallas_call(
         functools.partial(request_kernel, tiles_here, row_size),
-        out_shape=jax.ShapeDtypeStruct((row_size // 2, 2, 128), jnp.int32),
+        out_shape=jax.ShapeDtypeStruct((row_size, 2, 128), jnp.int32),
         in_specs=[SMEM, SMEM],
         out_specs=VMEM,
         compiler_params=params(0),
@@ -84,28 +82,28 @@
     )(ids, me)
 
 
-def pick_kernel(which, wanted_ref, tiles_ref, *refs):
+def pick_kernel(which, wanted_ref, me_ref, tiles_ref, *refs):
     out_ref = refs[-1]
-    for peer in range(out_ref.shape[0]):
-        out_ref[peer] = tiles_ref[wanted_ref[peer, which, 0]]
-
-
-def pick(tiles, wanted, which, after):
+    half = out_ref.shape[0]
+    for peer in range(half):
+        out_ref[peer] = tiles_ref[wanted_ref[lax.div(me_ref[0], half) * half + peer, which, 0]]
+
+
+def pick(tiles, wanted, which, me, after):
     return pl.pallas_call(
         functools.partial(pick_kernel, which),
-        out_shape=jax.ShapeDtypeStruct(wanted.shape[:1] + tiles.shape[1:], tiles.dtype),
-        in_specs=[SMEM, VMEM] + [ANY] * len(after),
+        out_shape=jax.ShapeDtypeStruct((wanted.shape[0] // 2,) + tiles.shape[1:], tiles.dtype),
+        in_specs=[SMEM, SMEM, VMEM] + [ANY] * len(after),
         out_specs=VMEM,
         compiler_params=params(0),
         cost_estimate=pl.CostEstimate(flops=0, bytes_accessed=2 * MIB, transcendentals=0),
         name="pick",
-    )(wanted, tiles, *after)
+    )(wanted, me, tiles, *after)
 
 
 def pick_each_kernel(which, order, wanted_ref, me_ref, tiles_ref, *refs):
-    place = lax.rem(me_ref[0], wanted_ref.shape[0])
     for step, out_ref in zip(order, refs[-len(order):]):
-        out_ref[0] = tiles_ref[wanted_ref[place ^ step, which, 0]]
+        out_ref[0] = tiles_ref[wanted_ref[me_ref[0] ^ step, which, 0]]
 
 
 def pick_each(tiles, wanted, which, me, order, after):
@@ -249,8 +247,8 @@
 
 def weigh(query, tile_refs, head, slots):
     key_parts, val_parts = [], []
-    for ref, slot in zip(tile_refs, slots):
-        tiles = ref[:, head]
+    for refs, slot in zip(tile_refs, slots):
+        tiles = functools.reduce(jnp.add, [ref[:, head] for ref in refs])
         count, keys, lanes = tiles.shape
         lane = iota(tiles.shape, 2)
         marks = (lane == iota(tiles.shape, 0) + (lanes // 2 + slot)).astype(tiles.dtype)
@@ -268,7 +266,7 @@
 
 
 def first_kernel(slots, block, asked_ref, *refs):
-    tile_refs, (sums_ref, tops_ref) = refs[:len(slots)], refs[len(slots):]
+    tile_refs, (sums_ref, tops_ref) = [[ref] for ref in refs[:len(slots)]], refs[len(slots):]
     heads, rows_all, lanes = asked_ref.shape
     lane = iota((block, lanes), 1)
     for step in range(rows_all // block):
@@ -301,7 +299,7 @@
 
 
 def more_kernel(slots, block, asked_ref, old_sums_ref, old_tops_ref, *refs):
-    tile_refs, (sums_ref, tops_ref) = refs[:len(slots)], refs[len(slots):]
+    tile_refs, (sums_ref, tops_ref) = [[ref] for ref in refs[:len(slots)]], refs[len(slots):]
     heads, rows_all, lanes = asked_ref.shape
     lane = iota((block, lanes), 1)
     for step in range(rows_all // block):
@@ -326,8 +324,9 @@
     )(asked, sums, tops, *tiles)
 
 
-def last_kernel(slots, groups, asked_ref, sums_ref, tops_ref, *refs):
-    tile_refs, out_refs = refs[:len(slots)], refs[-len(groups):]
+def last_kernel(slots, ways, groups, asked_ref, sums_ref, tops_ref, *refs):
+    out_refs = refs[-len(groups):]
+    tile_refs = [refs[ways * index:ways * (index + 1)] for index in range(len(slots))]
     heads, lanes = asked_ref.shape[0], asked_ref.shape[2]
     block = out_refs[0].shape[0]
     half = lanes // 2
@@ -350,7 +349,7 @@
     heads, rows, lanes = asked.shape
     out = jax.ShapeDtypeStruct((own_rows, heads * lanes // 2), jnp.bfloat16)
     return pl.pallas_call(
-        functools.partial(last_kernel, slots, groups),
+        functools.partial(last_kernel, slots, len(tiles) // len(slots), groups),
         out_shape=(out,) * len(groups),
         in_specs=[VMEM] * (3 + len(tiles)) + [ANY] * len(after),
         out_specs=(VMEM,) * len(groups),
@@ -405,7 +404,7 @@
         return lax.all_to_all(value, "rows", split_axis=0, concat_axis=0, tiled=True, axis_index_groups=halves)
 
     asked_of = request(tile_ids, me, tiles_here, row_size)
-    asked_by = swap(asked_of)
+    asked_by = lax.all_to_all(asked_of, "rows", split_axis=0, concat_axis=0, tiled=True)
     heads_first = tie(jnp.transpose(tile_kv, (0, 2, 1, 3)), asked_of)
     mirrored = lax.ppermute(heads_first, "rows", turn(row_size, half))
 
@@ -414,29 +413,33 @@
         cells.append(lax.ppermute(fact_cells, "cols", turn(col_size, -step)))
 
     across = half // 2
-    near_order = [0, 1] + sorted(range(2, half), key=lambda step: (step != 2, not step & across, step & 1, step))
-    rest = sorted(set(range(2, half)) - {across}, key=lambda step: (not step & across, step & 1, -step))
-    far_order = list(dict.fromkeys([0, across, 1] + rest[:1] + rest[-2:-1] + rest[1:-2] + rest[-1:]))
-    near_slots, far_slots = (near_order, [half + step for step in far_order]) if paired else ([0], [half])
-
-    def spread(tiles, which, order, after):
-        if not paired:
-            return [swap(pick(tiles, asked_by, which, after))]
-        picked = pick_each(tiles, asked_by, which, me, order, after)
-        return [tile if step == 0 else lax.ppermute(tile, "rows", [(row, row ^ step) for row in range(row_size)])
-                for step, tile in zip(order, picked)]
+
+    def send(tile, step, some=False):
+        inner = [row for row in range(row_size) if not some or bool(row & half) != bool(row & across)]
+        return lax.ppermute(tile, "rows", [(row, row ^ step) for row in inner])
 
     if group_width % 128:
         w_query = lax.dynamic_slice_in_dim(w_query, col_me * group_width, group_width, 1)
     residual, asked = front(cells, tile_ids, me, key_mask, gain_col, w_qkv, w_col_out, gain_tile, w_query,
                             heads_all, head_size, cols, heads_here, tiles_here, row_size, paired, [])
-    near = spread(heads_first, 0, near_order, [asked])
-    far = spread(mirrored, 1, far_order, near[1:3])
-    sums, tops = first_tiles(asked, near, near_slots, rows * cols)
-    batch = len(far) // 2
-    if batch:
-        sums, tops = more_tiles(asked, sums, tops, far[:batch], far_slots[:batch], rows * cols)
-    far, far_slots = far[batch:], far_slots[batch:]
+    if paired:
+        aside = list(range(1, across))
+        over = sorted(range(across, half), key=lambda step: (step & 1, step))
+        near_order = sorted(aside, key=lambda step: step != 1)[:2] + over + aside[2:]
+        picked = pick_each(heads_first, asked_by, 0, me, [0] + near_order + [half + step for step in over], [asked])
+        near = list(picked[:1]) + [send(tile, step) for step, tile in zip(near_order, picked[1:])]
+        straight = [send(tile, half + step, True) for step, tile in zip(over, picked[half:])]
+        mirror_picked = pick_each(mirrored, asked_by, 1, me, [0] + aside + over, near[1:3])
+        far = list(mirror_picked[:1]) + [send(tile, step) for step, tile in zip(aside, mirror_picked[1:])]
+        outward = [send(tile, step, True) for step, tile in zip(over, mirror_picked[across:])]
+        sums, tops = first_tiles(asked, near, [0] + near_order, rows * cols)
+        sums, tops = more_tiles(asked, sums, tops, far, [half + step for step in [0] + aside], rows * cols)
+        far = [way for ways in zip(straight, outward) for way in ways]
+        far_slots = [half + step for step in over]
+    else:
+        near = [swap(pick(heads_first, asked_by, 0, me, [asked]))]
+        far, far_slots = [swap(pick(mirrored, asked_by, 1, me, near))], [half]
+        sums, tops = first_tiles(asked, near, [0], rows * cols)
     others = last_tiles(asked, sums, tops, far, far_slots, list(range(1, col_size)), rows * cols, [])
     own = last_tiles(asked, sums, tops, far, far_slots, [0], rows * cols, others[:1])
     answers = list(own) + [lax.ppermute(other, "cols", turn(col_size, step + 1)) for step, other in enumerate(others)]

time: 64.3 us -> 79.7 us (1.24)
  waiting for transfers between devices: 23.9 us -> 34.3 us
  starting transfers between devices: 21.1 us -> 25.6 us
    all_to_all x1, waiting for transfers between devices: 0.01 us -> 12.5 us  [shards(): lax.all_to_all(asked_of, 'rows', split_axis=0, concat_axis=0, tiled=True)]
    ppermute x14 -> x18, starting transfers between devices: 10.2 us -> 14.5 us  [send(): return lax.ppermute(tile, 'rows', [(row, row ^ step) for row in inner])]
    ppermute x1, waiting for transfers between devices: 2.53 us -> 0.01 us  [shards(): mirrored = lax.ppermute(heads_first, 'rows', turn(row_size, half))]
    ppermute x14 -> x18, waiting for transfers between devices: 18.5 us -> 19 us  [send(): return lax.ppermute(tile, 'rows', [(row, row ^ step) for row in inner])]
  transfers between devices with their start and end apart: 18 -> 22, of which waited for: 12 -> 13; matrix products, arithmetic and copies ran while one was open for 0% -> 0% of each run, Pallas kernels for 20% -> 17%
where the time goes in v17:
time: 79.7 us; the launch traced here: 79.3 us
  waiting for transfers between devices  34.3 us (43%)
  starting transfers between devices  25.6 us (32%)
  Pallas kernels  17.3 us (22%)
  local copies, waits for them, and re-layouts  1.84 us (2%)
    ppermute x18, waiting for transfers between devices, send(): return lax.ppermute(tile, 'rows', [(row, row ^ step) for row in inner])  19 us
    ppermute x18, starting transfers between devices, send(): return lax.ppermute(tile, 'rows', [(row, row ^ step) for row in inner])  14.5 us
    all_to_all x1, waiting for transfers between devices, shards(): lax.all_to_all(asked_of, 'rows', split_axis=0, concat_axis=0, tiled=True)  12.5 us
    pallas_call x1, Pallas kernels, front(): pl.pallas_call(functools.partial(front_kernel, groups, heads, head_size,...  5.51 us
    ppermute x1, starting transfers between devices, shards(): mirrored = lax.ppermute(heads_first, 'rows', turn(row_size, half))  4.04 us
    all_to_all x1, starting transfers between devices, shards(): lax.all_to_all(asked_of, 'rows', split_axis=0, concat_axis=0, tiled=True)  3.88 us
    pallas_call x2, Pallas kernels, last_tiles(): pl.pallas_call(functools.partial(last_kernel, slots, len(tiles) // len(sl...  2.86 us
    pallas_call x1, Pallas kernels, first_tiles(): pl.pallas_call(functools.partial(first_kernel, slots, rows if rows <= 512...  2.38 us
  transfers between devices with their start and end apart: 22, of which 13 were waited for; matrix products, arithmetic and copies ran while one was open for 0% of the time, Pallas kernels for 17%

profile of v17, /device:TPU:0, one launch (start us, length us, event | category | flops | bytes accessed | tf_op | source)
XLA Modules:
  0.0 79.3 jit_solution(14031405755500154614)
XLA Ops:
  3.2 4.0 %collective-permute-start.8 = (bf16[4,4,128,128]{3,2,1,0:T(8,128)(2,1)S(1)}, bf16[4,4,128,128]{3,2,1,0:T(8,128)(2,1)S(1)}, u32[]{:S(2)}, u32[]{:S(2)}) collective-permute-start(bf16[4,4,128,128]{3,2,1,0:T(8,128)(2,1)S(1)} %tie.1.tiles_ref), channel_id=1, source_target_pairs={{0,16},{2,18},{4,20},{6,22},{8,24},{10,26},{12,28},{14,30},{16,0},... | collective-permute-start | bytes 1572872 | tf_op jit(solution)/shard_map/ppermute | solution.py:409
  7.2 1.5 %collective-permute-start = (bf16[48,4,512]{2,1,0:T(4,128)(2,1)S(1)}, bf16[48,4,512]{2,1,0:T(4,128)(2,1)S(1)}, u32[]{:S(2)}, u32[]{:S(2)}) collective-permute-start(bf16[48,4,512]{2,1,0:T(4,128)(2,1)S(1)} %copy-done.2), channel_id=1, source_target_pairs={{0,1},{1,0},{2,3},{3,2},{4,5},{5,4},{6,7},{7,6},{8,9},{9,8},{10,11... | collective-permute-start | bytes 589832 | tf_op jit(solution)/shard_map/ppermute | solution.py:413
  8.7 3.9 %all-to-all-start = ((s32[16,2,128]{2,1,0:T(2,128)}), s32[16,2,128]{2,1,0:T(2,128)S(1)}, u32[]{:S(2)}, u32[]{:S(2)}) async-start(s32[16,2,128]{2,1,0:T(2,128)} %request.1.after_ref), calls=%async_computation | async-start | bytes 32768 | tf_op jit(solution)/shard_map/all_to_all | solution.py:407
  13.6 5.5 %front.1 = (f32[192,512]{1,0:T(8,128)S(1)}, bf16[4,384,128]{2,1,0:T(8,128)(2,1)S(1)}) custom-call(bf16[48,4,512]{2,1,0:T(4,128)(2,1)} %refs_0_.1, bf16[48,4,512]{2,1,0:T(4,128)(2,1)S(1)} %collective-permute-done.refs_1_, s32[2]{0:T(128)S(1)} %pad_add_fusion.refs_2_.me_ref, s32[1,12]{1,0:T(1,128)} %ids_ref.1, s32[12,48]{1,0:T(8,128)} %bitcast.9, ...), custom_call_target="tpu_custom_call" | custom-call | flops 1006632960 | bytes 4194304 | tf_op jit(solution)/shard_map/front/pallas_call | solution.py:233
  19.1 12.5 %all-to-all-done.wanted_ref = s32[16,2,128]{2,1,0:T(2,128)S(1)} async-done(((s32[16,2,128]{2,1,0:T(2,128)}), s32[16,2,128]{2,1,0:T(2,128)S(1)}, u32[]{:S(2)}, u32[]{:S(2)}) %all-to-all-start) | async-done | bytes 16416 | tf_op jit(solution)/shard_map/all_to_all | solution.py:407
  34.0 2.2 %collective-permute-start.4 = (bf16[1,4,128,128]{3,2,1,0:T(8,128)(2,1)S(1)}, bf16[1,4,128,128]{3,2,1,0:T(8,128)(2,1)S(1)}, u32[]{:S(2)}, u32[]{:S(2)}) collective-permute-start(bf16[1,4,128,128]{3,2,1,0:T(8,128)(2,1)S(1)} %get-tuple-element.37), channel_id=1, source_target_pairs={{0,12},{2,14},{4,8},{6,10},{8,4},{10,6},{12,0},{14,2},{16,28},{18,... | collective-permute-start | bytes 393224 | tf_op jit(solution)/shard_map/ppermute | solution.py:419
  36.2 2.3 %collective-permute-done.2.refs_2_.refs_1_ = bf16[1,4,128,128]{3,2,1,0:T(8,128)(2,1)S(1)} collective-permute-done((bf16[1,4,128,128]{3,2,1,0:T(8,128)(2,1)S(1)}, bf16[1,4,128,128]{3,2,1,0:T(8,128)(2,1)S(1)}, u32[]{:S(2)}, u32[]{:S(2)}) %collective-permute-start.2) | collective-permute-done | bytes 131104 | tf_op jit(solution)/shard_map/ppermute | solution.py:419
  41.8 1.5 %collective-permute-done.4.refs_4_ = bf16[1,4,128,128]{3,2,1,0:T(8,128)(2,1)S(1)} collective-permute-done((bf16[1,4,128,128]{3,2,1,0:T(8,128)(2,1)S(1)}, bf16[1,4,128,128]{3,2,1,0:T(8,128)(2,1)S(1)}, u32[]{:S(2)}, u32[]{:S(2)}) %collective-permute-start.4) | collective-permute-done | bytes 131104 | tf_op jit(solution)/shard_map/ppermute | solution.py:419
  44.7 2.6 %collective-permute-done.6.refs_6_ = bf16[1,4,128,128]{3,2,1,0:T(8,128)(2,1)S(1)} collective-permute-done((bf16[1,4,128,128]{3,2,1,0:T(8,128)(2,1)S(1)}, bf16[1,4,128,128]{3,2,1,0:T(8,128)(2,1)S(1)}, u32[]{:S(2)}, u32[]{:S(2)}) %collective-permute-start.6) | collective-permute-done | bytes 131104 | tf_op jit(solution)/shard_map/ppermute | solution.py:419
  50.7 1.3 %collective-permute-start.13 = (bf16[1,4,128,128]{3,2,1,0:T(8,128)(2,1)S(1)}, bf16[1,4,128,128]{3,2,1,0:T(8,128)(2,1)S(1)}, u32[]{:S(2)}, u32[]{:S(2)}) collective-permute-start(bf16[1,4,128,128]{3,2,1,0:T(8,128)(2,1)S(1)} %get-tuple-element.50), channel_id=1, source_target_pairs={{8,0},{10,2},{12,4},{14,6},{16,24},{18,26},{20,28},{22,30},{9,1},{... | collective-permute-start | bytes 393224 | tf_op jit(solution)/shard_map/ppermute | solution.py:419
  52.1 1.3 %collective-permute-start.15 = (bf16[1,4,128,128]{3,2,1,0:T(8,128)(2,1)S(1)}, bf16[1,4,128,128]{3,2,1,0:T(8,128)(2,1)S(1)}, u32[]{:S(2)}, u32[]{:S(2)}) collective-permute-start(bf16[1,4,128,128]{3,2,1,0:T(8,128)(2,1)S(1)} %get-tuple-element.52), channel_id=1, source_target_pairs={{8,4},{10,6},{12,0},{14,2},{16,28},{18,30},{20,24},{22,26},{9,5},{... | collective-permute-start | bytes 393224 | tf_op jit(solution)/shard_map/ppermute | solution.py:419
  53.4 1.6 %collective-permute-done.10.refs_2_ = bf16[1,4,128,128]{3,2,1,0:T(8,128)(2,1)S(1)} collective-permute-done((bf16[1,4,128,128]{3,2,1,0:T(8,128)(2,1)S(1)}, bf16[1,4,128,128]{3,2,1,0:T(8,128)(2,1)S(1)}, u32[]{:S(2)}, u32[]{:S(2)}) %collective-permute-start.10) | collective-permute-done | bytes 131104 | tf_op jit(solution)/shard_map/ppermute | solution.py:419
  54.9 1.3 %collective-permute-start.17 = (bf16[1,4,128,128]{3,2,1,0:T(8,128)(2,1)S(1)}, bf16[1,4,128,128]{3,2,1,0:T(8,128)(2,1)S(1)}, u32[]{:S(2)}, u32[]{:S(2)}) collective-permute-start(bf16[1,4,128,128]{3,2,1,0:T(8,128)(2,1)S(1)} %get-tuple-element.54), channel_id=1, source_target_pairs={{8,2},{10,0},{12,6},{14,4},{16,26},{18,24},{20,30},{22,28},{9,3},{... | collective-permute-start | bytes 393224 | tf_op jit(solution)/shard_map/ppermute | solution.py:419
  56.2 1.5 %collective-permute-start.19 = (bf16[1,4,128,128]{3,2,1,0:T(8,128)(2,1)S(1)}, bf16[1,4,128,128]{3,2,1,0:T(8,128)(2,1)S(1)}, u32[]{:S(2)}, u32[]{:S(2)}) collective-permute-start(bf16[1,4,128,128]{3,2,1,0:T(8,128)(2,1)S(1)} %get-tuple-element.56), channel_id=1, source_target_pairs={{8,6},{10,4},{12,2},{14,0},{16,30},{18,28},{20,26},{22,24},{9,7},{... | collective-permute-start | bytes 393224 | tf_op jit(solution)/shard_map/ppermute | solution.py:419
  57.7 2.4 %first_tiles.1 = (f32[4,384,128]{2,1,0:T(8,128)S(1)}, f32[384,128]{1,0:T(8,128)S(1)}) custom-call(bf16[4,384,128]{2,1,0:T(8,128)(2,1)S(1)} %get-tuple-element.32.refs_0_.asked_ref, bf16[1,4,128,128]{3,2,1,0:T(8,128)(2,1)S(1)} %get-tuple-element.33.refs_0_, bf16[1,4,128,128]{3,2,1,0:T(8,128)(2,1)S(1)} %collective-permute-done.1.refs_1_.refs_0_, ...), custom_call_target="tpu_custom_call" | custom-call | flops 805306368 | bytes 4194304 | tf_op jit(solution)/shard_map/first_tiles/pallas_call | solution.py:283
  60.1 2.0 %more_tiles.1 = (f32[4,384,128]{2,1,0:T(8,128)S(1)}, f32[384,128]{1,0:T(8,128)S(1)}) custom-call(bf16[4,384,128]{2,1,0:T(8,128)(2,1)S(1)} %get-tuple-element.32.refs_0_.asked_ref, f32[4,384,128]{2,1,0:T(8,128)S(1)} %get-tuple-element.41.old_sums_ref, f32[384,128]{1,0:T(8,128)S(1)} %get-tuple-element.42.old_tops_ref, ...), custom_call_target="tpu_custom_call" | custom-call | flops 402653184 | bytes 4194304 | tf_op jit(solution)/shard_map/more_tiles/pallas_call | solution.py:316
  63.4 2.9 %collective-permute-done.15.refs_3_ = bf16[1,4,128,128]{3,2,1,0:T(8,128)(2,1)S(1)} collective-permute-done((bf16[1,4,128,128]{3,2,1,0:T(8,128)(2,1)S(1)}, bf16[1,4,128,128]{3,2,1,0:T(8,128)(2,1)S(1)}, u32[]{:S(2)}, u32[]{:S(2)}) %collective-permute-start.15) | collective-permute-done | bytes 131104 | tf_op jit(solution)/shard_map/ppermute | solution.py:419
  66.3 1.6 %collective-permute-done.17.refs_5_ = bf16[1,4,128,128]{3,2,1,0:T(8,128)(2,1)S(1)} collective-permute-done((bf16[1,4,128,128]{3,2,1,0:T(8,128)(2,1)S(1)}, bf16[1,4,128,128]{3,2,1,0:T(8,128)(2,1)S(1)}, u32[]{:S(2)}, u32[]{:S(2)}) %collective-permute-start.17) | collective-permute-done | bytes 131104 | tf_op jit(solution)/shard_map/ppermute | solution.py:419
  67.9 3.6 %collective-permute-done.19.refs_7_ = bf16[1,4,128,128]{3,2,1,0:T(8,128)(2,1)S(1)} collective-permute-done((bf16[1,4,128,128]{3,2,1,0:T(8,128)(2,1)S(1)}, bf16[1,4,128,128]{3,2,1,0:T(8,128)(2,1)S(1)}, u32[]{:S(2)}, u32[]{:S(2)}) %collective-permute-start.19) | collective-permute-done | bytes 131104 | tf_op jit(solution)/shard_map/ppermute | solution.py:419
  71.5 1.4 %last_tiles.2.refs_8_ = bf16[192,256]{1,0:T(8,128)(2,1)S(1)} custom-call(bf16[4,384,128]{2,1,0:T(8,128)(2,1)S(1)} %get-tuple-element.32.refs_0_.asked_ref, f32[4,384,128]{2,1,0:T(8,128)S(1)} %get-tuple-element.47.sums_ref, f32[384,128]{1,0:T(8,128)S(1)} %get-tuple-element.48.tops_ref, bf16[1,4,128,128]{3,2,1,0:T(8,128)(2,1)S(1)} %collective-permute-done.12.refs_0_, ...), custom_call_target="tpu_custom_call" | custom-call | flops 402653184 | bytes 4194304 | tf_op jit(solution)/shard_map/last_tiles/pallas_call | solution.py:351
  72.9 1.6 %collective-permute-start.20 = (bf16[192,256]{1,0:T(8,128)(2,1)S(1)}, bf16[192,256]{1,0:T(8,128)(2,1)S(1)}, u32[]{:S(2)}, u32[]{:S(2)}) collective-permute-start(bf16[192,256]{1,0:T(8,128)(2,1)S(1)} %last_tiles.2.refs_8_), channel_id=1, source_target_pairs={{0,1},{1,0},{2,3},{3,2},{4,5},{5,4},{6,7},{7,6},{8,9},{9,8},{10,11... | collective-permute-start | bytes 294920 | tf_op jit(solution)/shard_map/ppermute | solution.py:445
  74.5 1.4 %last_tiles.3.refs_0_ = bf16[192,256]{1,0:T(8,128)(2,1)S(1)} custom-call(bf16[4,384,128]{2,1,0:T(8,128)(2,1)S(1)} %get-tuple-element.32.refs_0_.asked_ref, f32[4,384,128]{2,1,0:T(8,128)S(1)} %get-tuple-element.47.sums_ref, f32[384,128]{1,0:T(8,128)S(1)} %get-tuple-element.48.tops_ref, bf16[1,4,128,128]{3,2,1,0:T(8,128)(2,1)S(1)} %collective-permute-done.12.refs_0_, ...), custom_call_target="tpu_custom_call" | custom-call | flops 402653184 | bytes 4194304 | tf_op jit(solution)/shard_map/last_tiles/pallas_call | solution.py:351
  75.9 1.9 %collective-permute-done.20.refs_1_ = bf16[192,256]{1,0:T(8,128)(2,1)S(1)} collective-permute-done((bf16[192,256]{1,0:T(8,128)(2,1)S(1)}, bf16[192,256]{1,0:T(8,128)(2,1)S(1)}, u32[]{:S(2)}, u32[]{:S(2)}) %collective-permute-start.20) | collective-permute-done | bytes 98336 | tf_op jit(solution)/shard_map/ppermute | solution.py:445
  77.8 1.5 %finish.1 = bf16[48,4,512]{2,1,0:T(4,128)(2,1)} custom-call(s32[2]{0:T(128)S(1)} %pad_add_fusion.refs_2_.me_ref, bf16[512,512]{1,0:T(8,128)(2,1)S(1)} %copy-done, f32[192,512]{1,0:T(8,128)S(1)} %get-tuple-element.31.resid_ref, bf16[192,256]{1,0:T(8,128)(2,1)S(1)} %last_tiles.3.refs_0_, bf16[192,256]{1,0:T(8,128)(2,1)S(1)} %collective-permute-done.20.refs_1_), custom_call_target="tpu_custom_call" | custom-call | flops 100663296 | bytes 1048576 | tf_op jit(solution)/shard_map/finish/pallas_call | solution.py:374
  (38 shorter events, 15.8 us)
Async XLA Ops:
  0.0 7.2 %copy-start.2 = (bf16[48,4,512]{2,1,0:T(4,128)(2,1)S(1)}, bf16[48,4,512]{2,1,0:T(4,128)(2,1)}, u32[]{:S(2)}) copy-start(bf16[48,4,512]{2,1,0:T(4,128)(2,1)} %refs_0_.1) | copy-start | bytes 589828
  3.2 37.1 %collective-permute-start.8 = (bf16[4,4,128,128]{3,2,1,0:T(8,128)(2,1)S(1)}, bf16[4,4,128,128]{3,2,1,0:T(8,128)(2,1)S(1)}, u32[]{:S(2)}, u32[]{:S(2)}) collective-permute-start(bf16[4,4,128,128]{3,2,1,0:T(8,128)(2,1)S(1)} %tie.1.tiles_ref), channel_id=1, source_target_pairs={{0,16},{2,18},{4,20},{6,22},{8,24},{10,26},{12,28},{14,30},{16,0},... | collective-permute-start | bytes 1572872 | tf_op jit(solution)/shard_map/ppermute | solution.py:409
  7.2 6.4 %collective-permute-start = (bf16[48,4,512]{2,1,0:T(4,128)(2,1)S(1)}, bf16[48,4,512]{2,1,0:T(4,128)(2,1)S(1)}, u32[]{:S(2)}, u32[]{:S(2)}) collective-permute-start(bf16[48,4,512]{2,1,0:T(4,128)(2,1)S(1)} %copy-done.2), channel_id=1, source_target_pairs={{0,1},{1,0},{2,3},{3,2},{4,5},{5,4},{6,7},{7,6},{8,9},{9,8},{10,11... | collective-permute-start | bytes 589832 | tf_op jit(solution)/shard_map/ppermute | solution.py:413
  8.7 22.9 %all-to-all-start = ((s32[16,2,128]{2,1,0:T(2,128)}), s32[16,2,128]{2,1,0:T(2,128)S(1)}, u32[]{:S(2)}, u32[]{:S(2)}) async-start(s32[16,2,128]{2,1,0:T(2,128)} %request.1.after_ref), calls=%async_computation | async-start | bytes 32768 | tf_op jit(solution)/shard_map/all_to_all | solution.py:407
  32.5 3.7 %collective-permute-start.1 = (bf16[1,4,128,128]{3,2,1,0:T(8,128)(2,1)S(1)}, bf16[1,4,128,128]{3,2,1,0:T(8,128)(2,1)S(1)}, u32[]{:S(2)}, u32[]{:S(2)}) collective-permute-start(bf16[1,4,128,128]{3,2,1,0:T(8,128)(2,1)S(1)} %get-tuple-element.34), channel_id=1, source_target_pairs={{0,2},{2,0},{4,6},{6,4},{8,10},{10,8},{12,14},{14,12},{16,18},{18,... | collective-permute-start | bytes 393224 | tf_op jit(solution)/shard_map/ppermute | solution.py:419
  32.7 5.8 %collective-permute-start.2 = (bf16[1,4,128,128]{3,2,1,0:T(8,128)(2,1)S(1)}, bf16[1,4,128,128]{3,2,1,0:T(8,128)(2,1)S(1)}, u32[]{:S(2)}, u32[]{:S(2)}) collective-permute-start(bf16[1,4,128,128]{3,2,1,0:T(8,128)(2,1)S(1)} %get-tuple-element.35), channel_id=1, source_target_pairs={{0,4},{2,6},{4,0},{6,2},{8,12},{10,14},{12,8},{14,10},{16,20},{18,... | collective-permute-start | bytes 393224 | tf_op jit(solution)/shard_map/ppermute | solution.py:419
  33.3 6.3 %collective-permute-start.3 = (bf16[1,4,128,128]{3,2,1,0:T(8,128)(2,1)S(1)}, bf16[1,4,128,128]{3,2,1,0:T(8,128)(2,1)S(1)}, u32[]{:S(2)}, u32[]{:S(2)}) collective-permute-start(bf16[1,4,128,128]{3,2,1,0:T(8,128)(2,1)S(1)} %get-tuple-element.36), channel_id=1, source_target_pairs={{0,8},{2,10},{4,12},{6,14},{8,0},{10,2},{12,4},{14,6},{16,24},{18,... | collective-permute-start | bytes 393224 | tf_op jit(solution)/shard_map/ppermute | solution.py:419
  34.0 9.4 %collective-permute-start.4 = (bf16[1,4,128,128]{3,2,1,0:T(8,128)(2,1)S(1)}, bf16[1,4,128,128]{3,2,1,0:T(8,128)(2,1)S(1)}, u32[]{:S(2)}, u32[]{:S(2)}) collective-permute-start(bf16[1,4,128,128]{3,2,1,0:T(8,128)(2,1)S(1)} %get-tuple-element.37), channel_id=1, source_target_pairs={{0,12},{2,14},{4,8},{6,10},{8,4},{10,6},{12,0},{14,2},{16,28},{18,... | collective-permute-start | bytes 393224 | tf_op jit(solution)/shard_map/ppermute | solution.py:419
  36.2 7.8 %collective-permute-start.5 = (bf16[1,4,128,128]{3,2,1,0:T(8,128)(2,1)S(1)}, bf16[1,4,128,128]{3,2,1,0:T(8,128)(2,1)S(1)}, u32[]{:S(2)}, u32[]{:S(2)}) collective-permute-start(bf16[1,4,128,128]{3,2,1,0:T(8,128)(2,1)S(1)} %get-tuple-element.38), channel_id=1, source_target_pairs={{0,10},{2,8},{4,14},{6,12},{8,2},{10,0},{12,6},{14,4},{16,26},{18,... | collective-permute-start | bytes 393224 | tf_op jit(solution)/shard_map/ppermute | solution.py:419
  38.5 8.8 %collective-permute-start.6 = (bf16[1,4,128,128]{3,2,1,0:T(8,128)(2,1)S(1)}, bf16[1,4,128,128]{3,2,1,0:T(8,128)(2,1)S(1)}, u32[]{:S(2)}, u32[]{:S(2)}) collective-permute-start(bf16[1,4,128,128]{3,2,1,0:T(8,128)(2,1)S(1)} %get-tuple-element.39), channel_id=1, source_target_pairs={{0,14},{2,12},{4,10},{6,8},{8,6},{10,4},{12,2},{14,0},{16,30},{18,... | collective-permute-start | bytes 393224 | tf_op jit(solution)/shard_map/ppermute | solution.py:419
  39.6 9.0 %collective-permute-start.7 = (bf16[1,4,128,128]{3,2,1,0:T(8,128)(2,1)S(1)}, bf16[1,4,128,128]{3,2,1,0:T(8,128)(2,1)S(1)}, u32[]{:S(2)}, u32[]{:S(2)}) collective-permute-start(bf16[1,4,128,128]{3,2,1,0:T(8,128)(2,1)S(1)} %get-tuple-element.40), channel_id=1, source_target_pairs={{0,6},{2,4},{4,2},{6,0},{8,14},{10,12},{12,10},{14,8},{16,22},{18,... | collective-permute-start | bytes 393224 | tf_op jit(solution)/shard_map/ppermute | solution.py:419
  40.3 9.2 %collective-permute-start.12 = (bf16[1,4,128,128]{3,2,1,0:T(8,128)(2,1)S(1)}, bf16[1,4,128,128]{3,2,1,0:T(8,128)(2,1)S(1)}, u32[]{:S(2)}, u32[]{:S(2)}) collective-permute-start(bf16[1,4,128,128]{3,2,1,0:T(8,128)(2,1)S(1)} %get-tuple-element.49), channel_id=1, source_target_pairs={{8,16},{10,18},{12,20},{14,22},{16,8},{18,10},{20,12},{22,14},{9,1... | collective-permute-start | bytes 393224 | tf_op jit(solution)/shard_map/ppermute | solution.py:419
  43.4 6.7 %collective-permute-start.14 = (bf16[1,4,128,128]{3,2,1,0:T(8,128)(2,1)S(1)}, bf16[1,4,128,128]{3,2,1,0:T(8,128)(2,1)S(1)}, u32[]{:S(2)}, u32[]{:S(2)}) collective-permute-start(bf16[1,4,128,128]{3,2,1,0:T(8,128)(2,1)S(1)} %get-tuple-element.51), channel_id=1, source_target_pairs={{8,20},{10,22},{12,16},{14,18},{16,12},{18,14},{20,8},{22,10},{9,2... | collective-permute-start | bytes 393224 | tf_op jit(solution)/shard_map/ppermute | solution.py:419
  44.0 6.7 %collective-permute-start.16 = (bf16[1,4,128,128]{3,2,1,0:T(8,128)(2,1)S(1)}, bf16[1,4,128,128]{3,2,1,0:T(8,128)(2,1)S(1)}, u32[]{:S(2)}, u32[]{:S(2)}) collective-permute-start(bf16[1,4,128,128]{3,2,1,0:T(8,128)(2,1)S(1)} %get-tuple-element.53), channel_id=1, source_target_pairs={{8,18},{10,16},{12,22},{14,20},{16,10},{18,8},{20,14},{22,12},{9,1... | collective-permute-start | bytes 393224 | tf_op jit(solution)/shard_map/ppermute | solution.py:419
  47.3 4.7 %collective-permute-start.9 = (bf16[1,4,128,128]{3,2,1,0:T(8,128)(2,1)S(1)}, bf16[1,4,128,128]{3,2,1,0:T(8,128)(2,1)S(1)}, u32[]{:S(2)}, u32[]{:S(2)}) collective-permute-start(bf16[1,4,128,128]{3,2,1,0:T(8,128)(2,1)S(1)} %get-tuple-element.44), channel_id=1, source_target_pairs={{0,2},{2,0},{4,6},{6,4},{8,10},{10,8},{12,14},{14,12},{16,18},{18,... | collective-permute-start | bytes 393224 | tf_op jit(solution)/shard_map/ppermute | solution.py:419
  48.6 6.3 %collective-permute-start.10 = (bf16[1,4,128,128]{3,2,1,0:T(8,128)(2,1)S(1)}, bf16[1,4,128,128]{3,2,1,0:T(8,128)(2,1)S(1)}, u32[]{:S(2)}, u32[]{:S(2)}) collective-permute-start(bf16[1,4,128,128]{3,2,1,0:T(8,128)(2,1)S(1)} %get-tuple-element.45), channel_id=1, source_target_pairs={{0,4},{2,6},{4,0},{6,2},{8,12},{10,14},{12,8},{14,10},{16,20},{18,... | collective-permute-start | bytes 393224 | tf_op jit(solution)/shard_map/ppermute | solution.py:419
  49.5 6.7 %collective-permute-start.11 = (bf16[1,4,128,128]{3,2,1,0:T(8,128)(2,1)S(1)}, bf16[1,4,128,128]{3,2,1,0:T(8,128)(2,1)S(1)}, u32[]{:S(2)}, u32[]{:S(2)}) collective-permute-start(bf16[1,4,128,128]{3,2,1,0:T(8,128)(2,1)S(1)} %get-tuple-element.46), channel_id=1, source_target_pairs={{0,6},{2,4},{4,2},{6,0},{8,14},{10,12},{12,10},{14,8},{16,22},{18,... | collective-permute-start | bytes 393224 | tf_op jit(solution)/shard_map/ppermute | solution.py:419
  50.1 12.1 %collective-permute-start.18 = (bf16[1,4,128,128]{3,2,1,0:T(8,128)(2,1)S(1)}, bf16[1,4,128,128]{3,2,1,0:T(8,128)(2,1)S(1)}, u32[]{:S(2)}, u32[]{:S(2)}) collective-permute-start(bf16[1,4,128,128]{3,2,1,0:T(8,128)(2,1)S(1)} %get-tuple-element.55), channel_id=1, source_target_pairs={{8,22},{10,20},{12,18},{14,16},{16,14},{18,12},{20,10},{22,8},{9,2... | collective-permute-start | bytes 393224 | tf_op jit(solution)/shard_map/ppermute | solution.py:419
  50.7 12.7 %collective-permute-start.13 = (bf16[1,4,128,128]{3,2,1,0:T(8,128)(2,1)S(1)}, bf16[1,4,128,128]{3,2,1,0:T(8,128)(2,1)S(1)}, u32[]{:S(2)}, u32[]{:S(2)}) collective-permute-start(bf16[1,4,128,128]{3,2,1,0:T(8,128)(2,1)S(1)} %get-tuple-element.50), channel_id=1, source_target_pairs={{8,0},{10,2},{12,4},{14,6},{16,24},{18,26},{20,28},{22,30},{9,1},{... | collective-permute-start | bytes 393224 | tf_op jit(solution)/shard_map/ppermute | solution.py:419
  52.1 14.3 %collective-permute-start.15 = (bf16[1,4,128,128]{3,2,1,0:T(8,128)(2,1)S(1)}, bf16[1,4,128,128]{3,2,1,0:T(8,128)(2,1)S(1)}, u32[]{:S(2)}, u32[]{:S(2)}) collective-permute-start(bf16[1,4,128,128]{3,2,1,0:T(8,128)(2,1)S(1)} %get-tuple-element.52), channel_id=1, source_target_pairs={{8,4},{10,6},{12,0},{14,2},{16,28},{18,30},{20,24},{22,26},{9,5},{... | collective-permute-start | bytes 393224 | tf_op jit(solution)/shard_map/ppermute | solution.py:419
  54.9 12.9 %collective-permute-start.17 = (bf16[1,4,128,128]{3,2,1,0:T(8,128)(2,1)S(1)}, bf16[1,4,128,128]{3,2,1,0:T(8,128)(2,1)S(1)}, u32[]{:S(2)}, u32[]{:S(2)}) collective-permute-start(bf16[1,4,128,128]{3,2,1,0:T(8,128)(2,1)S(1)} %get-tuple-element.54), channel_id=1, source_target_pairs={{8,2},{10,0},{12,6},{14,4},{16,26},{18,24},{20,30},{22,28},{9,3},{... | collective-permute-start | bytes 393224 | tf_op jit(solution)/shard_map/ppermute | solution.py:419
  56.2 15.2 %collective-permute-start.19 = (bf16[1,4,128,128]{3,2,1,0:T(8,128)(2,1)S(1)}, bf16[1,4,128,128]{3,2,1,0:T(8,128)(2,1)S(1)}, u32[]{:S(2)}, u32[]{:S(2)}) collective-permute-start(bf16[1,4,128,128]{3,2,1,0:T(8,128)(2,1)S(1)} %get-tuple-element.56), channel_id=1, source_target_pairs={{8,6},{10,4},{12,2},{14,0},{16,30},{18,28},{20,26},{22,24},{9,7},{... | collective-permute-start | bytes 393224 | tf_op jit(solution)/shard_map/ppermute | solution.py:419
  72.9 4.9 %copy-start = (bf16[512,512]{1,0:T(8,128)(2,1)S(1)}, bf16[512,512]{1,0:T(8,128)(2,1)}, u32[]{:S(2)}) copy-start(bf16[512,512]{1,0:T(8,128)(2,1)} %weight_ref.1) | copy-start | bytes 1572868
  72.9 4.9 %collective-permute-start.20 = (bf16[192,256]{1,0:T(8,128)(2,1)S(1)}, bf16[192,256]{1,0:T(8,128)(2,1)S(1)}, u32[]{:S(2)}, u32[]{:S(2)}) collective-permute-start(bf16[192,256]{1,0:T(8,128)(2,1)S(1)} %last_tiles.2.refs_8_), channel_id=1, source_target_pairs={{0,1},{1,0},{2,3},{3,2},{4,5},{5,4},{6,7},{7,6},{8,9},{9,8},{10,11... | collective-permute-start | bytes 294920 | tf_op jit(solution)/shard_map/ppermute | solution.py:445
  (1 other events, 0.7 us)

commit v18 on v16

--- a/solution.py
+++ b/solution.py
@@ -360,27 +360,29 @@
     )(asked, sums, tops, *tiles, *after)
 
 
-def finish_kernel(me_ref, weight_ref, resid_ref, *refs):
-    answer_refs, out_ref = refs[:-1], refs[-1]
-    group_width = answer_refs[0].shape[1]
-    final = resid_ref[...]
-    for step, answer_ref in enumerate(answer_refs):
-        group = lax.rem(me_ref[1] - step + len(answer_refs), len(answer_refs))
-        rows = pl.ds(pl.multiple_of(group * group_width, group_width), group_width)
-        final = final + dot_rows(answer_ref[...], weight_ref[rows, :])
-    out_ref[...] = final.reshape(out_ref.shape).astype(out_ref.dtype)
-
-
-def finish(me, weight, residual, answers, shape):
-    return pl.pallas_call(
-        finish_kernel,
-        out_shape=jax.ShapeDtypeStruct(shape, jnp.bfloat16),
-        in_specs=[SMEM, VMEM, VMEM] + [VMEM] * len(answers),
-        out_specs=VMEM,
+def own_kernel(me_ref, weight_ref, resid_ref, answer_ref, partial_ref, *part_refs):
+    groups, group_width = len(part_refs) + 1, answer_ref.shape[1]
+
+    def rows(step):
+        group = lax.rem(me_ref[1] - step + groups, groups)
+        return weight_ref[pl.ds(pl.multiple_of(group * group_width, group_width), group_width), :]
+
+    partial_ref[...] = resid_ref[...] + dot_rows(answer_ref[...], rows(0))
+    for step, part_ref in enumerate(part_refs):
+        part_ref[...] = rows(step + 1)
+
+
+def own_part(me, weight, residual, answer, groups):
+    part = jax.ShapeDtypeStruct((answer.shape[1], weight.shape[1]), weight.dtype)
+    return pl.pallas_call(
+        own_kernel,
+        out_shape=(jax.ShapeDtypeStruct(residual.shape, jnp.float32),) + (part,) * (groups - 1),
+        in_specs=[SMEM, VMEM, VMEM, VMEM],
+        out_specs=(VMEM,) * groups,
         compiler_params=params(0),
-        cost_estimate=pl.CostEstimate(flops=2 * residual.size * weight.shape[0], bytes_accessed=MIB, transcendentals=0),
-        name="finish",
-    )(me, weight, residual, *answers)
+        cost_estimate=pl.CostEstimate(flops=2 * residual.size * answer.shape[1], bytes_accessed=MIB, transcendentals=0),
+        name="own_part",
+    )(me, weight, residual, answer)
 
 
 def turn(size, step):
@@ -415,11 +417,13 @@
 
     across = half // 2
     near_order = [0, 1] + sorted(range(2, half), key=lambda step: (step != 2, not step & across, step & 1, step))
-    rest = sorted(set(range(2, half)) - {across}, key=lambda step: (not step & across, step & 1, -step))
-    far_order = list(dict.fromkeys([0, across, 1] + rest[:1] + rest[-2:-1] + rest[1:-2] + rest[-1:]))
+    rest = sorted(set(range(2, half)) - {across}, key=lambda step: (step != 2, not step & across, step & 1, -step))
+    far_order = list(dict.fromkeys([0, across] + rest + [1]))
     near_slots, far_slots = (near_order, [half + step for step in far_order]) if paired else ([0], [half])
 
     def spread(tiles, which, order, after):
+        if not order:
+            return []
         if not paired:
             return [swap(pick(tiles, asked_by, which, after))]
         picked = pick_each(tiles, asked_by, which, me, order, after)
@@ -431,16 +435,19 @@
     residual, asked = front(cells, tile_ids, me, key_mask, gain_col, w_qkv, w_col_out, gain_tile, w_query,
                             heads_all, head_size, cols, heads_here, tiles_here, row_size, paired, [])
     near = spread(heads_first, 0, near_order, [asked])
-    far = spread(mirrored, 1, far_order, near[1:3])
+    far = spread(mirrored, 1, far_order[:-1] if paired else far_order, near[1:3])
     sums, tops = first_tiles(asked, near, near_slots, rows * cols)
+    far += spread(mirrored, 1, far_order[-1:] if paired else [], [tops])
     batch = len(far) // 2
     if batch:
         sums, tops = more_tiles(asked, sums, tops, far[:batch], far_slots[:batch], rows * cols)
     far, far_slots = far[batch:], far_slots[batch:]
     others = last_tiles(asked, sums, tops, far, far_slots, list(range(1, col_size)), rows * cols, [])
     own = last_tiles(asked, sums, tops, far, far_slots, [0], rows * cols, others[:1])
-    answers = list(own) + [lax.ppermute(other, "cols", turn(col_size, step + 1)) for step, other in enumerate(others)]
-    return finish(me, w_tile_out, residual, answers, fact_cells.shape)
+    final, *weights = own_part(me, w_tile_out, residual, own[0], col_size)
+    for step, (other, weight) in enumerate(zip(others, weights)):
+        final = final + dot_rows(lax.ppermute(other, "cols", turn(col_size, step + 1)), weight)
+    return final.astype(jnp.bfloat16).reshape(rows, cols, width)
 
 
 def solution(mesh):

time: 64.3 us -> 62.2 us (0.967)
  waiting for transfers between devices: 23.9 us -> 18.6 us
  starting transfers between devices: 21.1 us -> 23.3 us
  local copies, waits for them, and re-layouts: 1.84 us -> 2.57 us
    ppermute x14, waiting for transfers between devices: 18.5 us -> 14 us  [spread(): lax.ppermute(tile, 'rows', [(row, row ^ step) for row in range(row_size)])]
    ppermute x14, starting transfers between devices: 10.2 us -> 12.4 us  [spread(): lax.ppermute(tile, 'rows', [(row, row ^ step) for row in range(row_size)])]
    ppermute x1, waiting for transfers between devices: 1.84 us -> 1.08 us  [shards(): lax.ppermute(other, 'cols', turn(col_size, step + 1))]
    pallas_call x1, Pallas kernels: 1.52 us -> 0.76 us  [own_part(): pl.pallas_call(own_kernel, out_shape=(jax.ShapeDtypeStruct(residual.shape...]
    reshape x0 -> x1, local copies, waits for them, and re-layouts: none -> 0.73 us  [shards(): return final.astype(jnp.bfloat16).reshape(rows, cols, width)]
    pallas_call x2 -> x3, Pallas kernels: 1.5 us -> 2.18 us  [pick_each(): pl.pallas_call(functools.partial(pick_each_kernel, which, order), out_sha...]
  transfers between devices with their start and end apart: 18 -> 18, of which waited for: 12 -> 11; matrix products, arithmetic and copies ran while one was open for 0% -> 0% of each run, Pallas kernels for 20% -> 23%
where the time goes in v18:
time: 62.2 us; the launch traced here: 61.9 us
  starting transfers between devices  23.3 us (37%)
  waiting for transfers between devices  18.6 us (30%)
  Pallas kernels  17 us (27%)
  local copies, waits for them, and re-layouts  2.57 us (4%)
    ppermute x14, waiting for transfers between devices, spread(): lax.ppermute(tile, 'rows', [(row, row ^ step) for row in range(row_size)])  14 us
    ppermute x14, starting transfers between devices, spread(): lax.ppermute(tile, 'rows', [(row, row ^ step) for row in range(row_size)])  12.4 us
    pallas_call x1, Pallas kernels, front(): pl.pallas_call(functools.partial(front_kernel, groups, heads, head_size,...  5.51 us
    ppermute x1, starting transfers between devices, shards(): mirrored = lax.ppermute(heads_first, 'rows', turn(row_size, half))  4.04 us
    all_to_all x1, starting transfers between devices, swap(): lax.all_to_all(value, 'rows', split_axis=0, concat_axis=0, tiled=True, ax...  3.78 us
    pallas_call x2, Pallas kernels, last_tiles(): pl.pallas_call(functools.partial(last_kernel, slots, groups), out_shape=(...  2.87 us
    ppermute x1, waiting for transfers between devices, shards(): mirrored = lax.ppermute(heads_first, 'rows', turn(row_size, half))  2.53 us
    pallas_call x1, Pallas kernels, first_tiles(): pl.pallas_call(functools.partial(first_kernel, slots, rows if rows <= 512...  2.4 us
  transfers between devices with their start and end apart: 18, of which 11 were waited for; matrix products, arithmetic and copies ran while one was open for 0% of the time, Pallas kernels for 23%

profile of v18, /device:TPU:0, one launch (start us, length us, event | category | flops | bytes accessed | tf_op | source)
XLA Modules:
  0.0 61.9 jit_solution(16956298501225122698)
XLA Ops:
  0.0 1.2 %copy.14 = bf16[4,128,4,128]{3,1,2,0:T(8,128)(2,1)S(1)} copy(bf16[4,128,4,128]{3,2,1,0:T(4,128)(2,1)} %param.17) | data formatting | bytes 1048576 | tf_op args[7]
  1.9 1.2 %request.1.after_ref = s32[8,2,128]{2,1,0:T(2,128)} custom-call(s32[1,12]{1,0:T(1,128)S(1)} %copy-done.1, s32[2]{0:T(128)S(1)} %pad_add_fusion.refs_2_.me_ref), custom_call_target="tpu_custom_call" | custom-call | bytes 262144 | tf_op jit(solution)/shard_map/request/pallas_call | solution.py:76
  3.1 4.0 %collective-permute-start.8 = (bf16[4,4,128,128]{3,2,1,0:T(8,128)(2,1)S(1)}, bf16[4,4,128,128]{3,2,1,0:T(8,128)(2,1)S(1)}, u32[]{:S(2)}, u32[]{:S(2)}) collective-permute-start(bf16[4,4,128,128]{3,2,1,0:T(8,128)(2,1)S(1)} %tie.1.tiles_ref), channel_id=1, source_target_pairs={{0,16},{2,18},{4,20},{6,22},{8,24},{10,26},{12,28},{14,30},{16,0},... | collective-permute-start | bytes 1572872 | tf_op jit(solution)/shard_map/ppermute | solution.py:412
  7.2 1.5 %collective-permute-start = (bf16[48,4,512]{2,1,0:T(4,128)(2,1)S(1)}, bf16[48,4,512]{2,1,0:T(4,128)(2,1)S(1)}, u32[]{:S(2)}, u32[]{:S(2)}) collective-permute-start(bf16[48,4,512]{2,1,0:T(4,128)(2,1)S(1)} %copy-done.2), channel_id=1, source_target_pairs={{0,1},{1,0},{2,3},{3,2},{4,5},{5,4},{6,7},{7,6},{8,9},{9,8},{10,11... | collective-permute-start | bytes 589832 | tf_op jit(solution)/shard_map/ppermute | solution.py:416
  8.7 3.8 %all-to-all-start = ((s32[8,2,128]{2,1,0:T(2,128)}), s32[8,2,128]{2,1,0:T(2,128)S(1)}, u32[]{:S(2)}, u32[]{:S(2)}) async-start(s32[8,2,128]{2,1,0:T(2,128)} %request.1.after_ref), calls=%async_computation | async-start | bytes 16384 | tf_op jit(solution)/shard_map/all_to_all | solution.py:407
  13.5 5.5 %front.1 = (f32[192,512]{1,0:T(8,128)S(1)}, bf16[4,384,128]{2,1,0:T(8,128)(2,1)S(1)}) custom-call(bf16[48,4,512]{2,1,0:T(4,128)(2,1)} %refs_0_.1, bf16[48,4,512]{2,1,0:T(4,128)(2,1)S(1)} %collective-permute-done.refs_1_, s32[2]{0:T(128)S(1)} %pad_add_fusion.refs_2_.me_ref, s32[1,12]{1,0:T(1,128)} %ids_ref.1, s32[12,48]{1,0:T(8,128)} %bitcast.11, ...), custom_call_target="tpu_custom_call" | custom-call | flops 1006632960 | bytes 4194304 | tf_op jit(solution)/shard_map/front/pallas_call | solution.py:235
  19.9 1.6 %collective-permute-start.2 = (bf16[1,4,128,128]{3,2,1,0:T(8,128)(2,1)S(1)}, bf16[1,4,128,128]{3,2,1,0:T(8,128)(2,1)S(1)}, u32[]{:S(2)}, u32[]{:S(2)}) collective-permute-start(bf16[1,4,128,128]{3,2,1,0:T(8,128)(2,1)S(1)} %get-tuple-element.32), channel_id=1, source_target_pairs={{0,4},{2,6},{4,0},{6,2},{8,12},{10,14},{12,8},{14,10},{16,20},{18,... | collective-permute-start | bytes 393224 | tf_op jit(solution)/shard_map/ppermute | solution.py:430
  21.5 1.9 %collective-permute-start.3 = (bf16[1,4,128,128]{3,2,1,0:T(8,128)(2,1)S(1)}, bf16[1,4,128,128]{3,2,1,0:T(8,128)(2,1)S(1)}, u32[]{:S(2)}, u32[]{:S(2)}) collective-permute-start(bf16[1,4,128,128]{3,2,1,0:T(8,128)(2,1)S(1)} %get-tuple-element.33), channel_id=1, source_target_pairs={{0,8},{2,10},{4,12},{6,14},{8,0},{10,2},{12,4},{14,6},{16,24},{18,... | collective-permute-start | bytes 393224 | tf_op jit(solution)/shard_map/ppermute | solution.py:430
  24.2 1.2 %collective-permute-start.5 = (bf16[1,4,128,128]{3,2,1,0:T(8,128)(2,1)S(1)}, bf16[1,4,128,128]{3,2,1,0:T(8,128)(2,1)S(1)}, u32[]{:S(2)}, u32[]{:S(2)}) collective-permute-start(bf16[1,4,128,128]{3,2,1,0:T(8,128)(2,1)S(1)} %get-tuple-element.35), channel_id=1, source_target_pairs={{0,10},{2,8},{4,14},{6,12},{8,2},{10,0},{12,6},{14,4},{16,26},{18,... | collective-permute-start | bytes 393224 | tf_op jit(solution)/shard_map/ppermute | solution.py:430
  25.8 2.1 %collective-permute-start.6 = (bf16[1,4,128,128]{3,2,1,0:T(8,128)(2,1)S(1)}, bf16[1,4,128,128]{3,2,1,0:T(8,128)(2,1)S(1)}, u32[]{:S(2)}, u32[]{:S(2)}) collective-permute-start(bf16[1,4,128,128]{3,2,1,0:T(8,128)(2,1)S(1)} %get-tuple-element.36), channel_id=1, source_target_pairs={{0,14},{2,12},{4,10},{6,8},{8,6},{10,4},{12,2},{14,0},{16,30},{18,... | collective-permute-start | bytes 393224 | tf_op jit(solution)/shard_map/ppermute | solution.py:430
  27.9 2.5 %collective-permute-done.8.tiles_ref = bf16[4,4,128,128]{3,2,1,0:T(8,128)(2,1)S(1)} collective-permute-done((bf16[4,4,128,128]{3,2,1,0:T(8,128)(2,1)S(1)}, bf16[4,4,128,128]{3,2,1,0:T(8,128)(2,1)S(1)}, u32[]{:S(2)}, u32[]{:S(2)}) %collective-permute-start.8) | collective-permute-done | bytes 524320 | tf_op jit(solution)/shard_map/ppermute | solution.py:412
  31.3 1.9 %collective-permute-done.3.refs_3_ = bf16[1,4,128,128]{3,2,1,0:T(8,128)(2,1)S(1)} collective-permute-done((bf16[1,4,128,128]{3,2,1,0:T(8,128)(2,1)S(1)}, bf16[1,4,128,128]{3,2,1,0:T(8,128)(2,1)S(1)}, u32[]{:S(2)}, u32[]{:S(2)}) %collective-permute-start.3) | collective-permute-done | bytes 131104 | tf_op jit(solution)/shard_map/ppermute | solution.py:430
  33.2 3.8 %collective-permute-done.4.refs_4_ = bf16[1,4,128,128]{3,2,1,0:T(8,128)(2,1)S(1)} collective-permute-done((bf16[1,4,128,128]{3,2,1,0:T(8,128)(2,1)S(1)}, bf16[1,4,128,128]{3,2,1,0:T(8,128)(2,1)S(1)}, u32[]{:S(2)}, u32[]{:S(2)}) %collective-permute-start.4) | collective-permute-done | bytes 131104 | tf_op jit(solution)/shard_map/ppermute | solution.py:430
  37.5 1.2 %collective-permute-done.5.refs_5_ = bf16[1,4,128,128]{3,2,1,0:T(8,128)(2,1)S(1)} collective-permute-done((bf16[1,4,128,128]{3,2,1,0:T(8,128)(2,1)S(1)}, bf16[1,4,128,128]{3,2,1,0:T(8,128)(2,1)S(1)}, u32[]{:S(2)}, u32[]{:S(2)}) %collective-permute-start.5) | collective-permute-done | bytes 131104 | tf_op jit(solution)/shard_map/ppermute | solution.py:430
  39.4 3.3 %collective-permute-done.6.refs_6_ = bf16[1,4,128,128]{3,2,1,0:T(8,128)(2,1)S(1)} collective-permute-done((bf16[1,4,128,128]{3,2,1,0:T(8,128)(2,1)S(1)}, bf16[1,4,128,128]{3,2,1,0:T(8,128)(2,1)S(1)}, u32[]{:S(2)}, u32[]{:S(2)}) %collective-permute-start.6) | collective-permute-done | bytes 131104 | tf_op jit(solution)/shard_map/ppermute | solution.py:430
  42.7 2.4 %first_tiles.1 = (f32[4,384,128]{2,1,0:T(8,128)S(1)}, f32[384,128]{1,0:T(8,128)S(1)}) custom-call(bf16[4,384,128]{2,1,0:T(8,128)(2,1)S(1)} %get-tuple-element.29.refs_0_.asked_ref, bf16[1,4,128,128]{3,2,1,0:T(8,128)(2,1)S(1)} %get-tuple-element.30.refs_0_, bf16[1,4,128,128]{3,2,1,0:T(8,128)(2,1)S(1)} %collective-permute-done.1.refs_1_.refs_0_, ...), custom_call_target="tpu_custom_call" | custom-call | flops 805306368 | bytes 4194304 | tf_op jit(solution)/shard_map/first_tiles/pallas_call | solution.py:285
  45.1 1.6 %collective-permute-start.13 = (bf16[1,4,128,128]{3,2,1,0:T(8,128)(2,1)S(1)}, bf16[1,4,128,128]{3,2,1,0:T(8,128)(2,1)S(1)}, u32[]{:S(2)}, u32[]{:S(2)}) collective-permute-start(bf16[1,4,128,128]{3,2,1,0:T(8,128)(2,1)S(1)} %get-tuple-element.47), channel_id=1, source_target_pairs={{0,10},{2,8},{4,14},{6,12},{8,2},{10,0},{12,6},{14,4},{16,26},{18,... | collective-permute-start | bytes 393224 | tf_op jit(solution)/shard_map/ppermute | solution.py:430
  47.5 1.3 %collective-permute-start.14 = (bf16[1,4,128,128]{3,2,1,0:T(8,128)(2,1)S(1)}, bf16[1,4,128,128]{3,2,1,0:T(8,128)(2,1)S(1)}, u32[]{:S(2)}, u32[]{:S(2)}) collective-permute-start(bf16[1,4,128,128]{3,2,1,0:T(8,128)(2,1)S(1)} %get-tuple-element.48), channel_id=1, source_target_pairs={{0,6},{2,4},{4,2},{6,0},{8,14},{10,12},{12,10},{14,8},{16,22},{18,... | collective-permute-start | bytes 393224 | tf_op jit(solution)/shard_map/ppermute | solution.py:430
  49.2 2.0 %more_tiles.1 = (f32[4,384,128]{2,1,0:T(8,128)S(1)}, f32[384,128]{1,0:T(8,128)S(1)}) custom-call(bf16[4,384,128]{2,1,0:T(8,128)(2,1)S(1)} %get-tuple-element.29.refs_0_.asked_ref, f32[4,384,128]{2,1,0:T(8,128)S(1)} %get-tuple-element.38.old_sums_ref, f32[384,128]{1,0:T(8,128)S(1)} %get-tuple-element.39.old_tops_ref.refs_0_, ...), custom_call_target="tpu_custom_call" | custom-call | flops 402653184 | bytes 4194304 | tf_op jit(solution)/shard_map/more_tiles/pallas_call | solution.py:318
  51.7 1.7 %collective-permute-done.13.refs_1_ = bf16[1,4,128,128]{3,2,1,0:T(8,128)(2,1)S(1)} collective-permute-done((bf16[1,4,128,128]{3,2,1,0:T(8,128)(2,1)S(1)}, bf16[1,4,128,128]{3,2,1,0:T(8,128)(2,1)S(1)}, u32[]{:S(2)}, u32[]{:S(2)}) %collective-permute-start.13) | collective-permute-done | bytes 131104 | tf_op jit(solution)/shard_map/ppermute | solution.py:430
  53.4 1.2 %collective-permute-done.14.refs_2_ = bf16[1,4,128,128]{3,2,1,0:T(8,128)(2,1)S(1)} collective-permute-done((bf16[1,4,128,128]{3,2,1,0:T(8,128)(2,1)S(1)}, bf16[1,4,128,128]{3,2,1,0:T(8,128)(2,1)S(1)}, u32[]{:S(2)}, u32[]{:S(2)}) %collective-permute-start.14) | collective-permute-done | bytes 131104 | tf_op jit(solution)/shard_map/ppermute | solution.py:430
  54.6 1.4 %last_tiles.2.refs_4_ = bf16[192,256]{1,0:T(8,128)(2,1)S(1)} custom-call(bf16[4,384,128]{2,1,0:T(8,128)(2,1)S(1)} %get-tuple-element.29.refs_0_.asked_ref, f32[4,384,128]{2,1,0:T(8,128)S(1)} %get-tuple-element.44.sums_ref, f32[384,128]{1,0:T(8,128)S(1)} %get-tuple-element.45.tops_ref, bf16[1,4,128,128]{3,2,1,0:T(8,128)(2,1)S(1)} %collective-permute-done.12.refs_0_, ...), custom_call_target="tpu_custom_call" | custom-call | flops 201326592 | bytes 4194304 | tf_op jit(solution)/shard_map/last_tiles/pallas_call | solution.py:352
  56.1 1.6 %collective-permute-start.16 = (bf16[192,256]{1,0:T(8,128)(2,1)S(1)}, bf16[192,256]{1,0:T(8,128)(2,1)S(1)}, u32[]{:S(2)}, u32[]{:S(2)}) collective-permute-start(bf16[192,256]{1,0:T(8,128)(2,1)S(1)} %last_tiles.2.refs_4_), channel_id=1, source_target_pairs={{0,1},{1,0},{2,3},{3,2},{4,5},{5,4},{6,7},{7,6},{8,9},{9,8},{10,11... | collective-permute-start | bytes 294920 | tf_op jit(solution)/shard_map/ppermute | solution.py:449
  57.6 1.4 %last_tiles.3.answer_ref = bf16[192,256]{1,0:T(8,128)(2,1)S(1)} custom-call(bf16[4,384,128]{2,1,0:T(8,128)(2,1)S(1)} %get-tuple-element.29.refs_0_.asked_ref, f32[4,384,128]{2,1,0:T(8,128)S(1)} %get-tuple-element.44.sums_ref, f32[384,128]{1,0:T(8,128)S(1)} %get-tuple-element.45.tops_ref, bf16[1,4,128,128]{3,2,1,0:T(8,128)(2,1)S(1)} %collective-permute-done.12.refs_0_, ...), custom_call_target="tpu_custom_call" | custom-call | flops 201326592 | bytes 4194304 | tf_op jit(solution)/shard_map/last_tiles/pallas_call | solution.py:352
  (34 shorter events, 10.2 us)
Async XLA Ops:
  0.0 7.2 %copy-start.2 = (bf16[48,4,512]{2,1,0:T(4,128)(2,1)S(1)}, bf16[48,4,512]{2,1,0:T(4,128)(2,1)}, u32[]{:S(2)}) copy-start(bf16[48,4,512]{2,1,0:T(4,128)(2,1)} %refs_0_.1) | copy-start | bytes 589828
  1.3 0.7 %copy-start.1 = (s32[1,12]{1,0:T(1,128)S(1)}, s32[1,12]{1,0:T(1,128)}, u32[]{:S(2)}) copy-start(s32[1,12]{1,0:T(1,128)} %ids_ref.1) | copy-start | bytes 148
  3.1 27.3 %collective-permute-start.8 = (bf16[4,4,128,128]{3,2,1,0:T(8,128)(2,1)S(1)}, bf16[4,4,128,128]{3,2,1,0:T(8,128)(2,1)S(1)}, u32[]{:S(2)}, u32[]{:S(2)}) collective-permute-start(bf16[4,4,128,128]{3,2,1,0:T(8,128)(2,1)S(1)} %tie.1.tiles_ref), channel_id=1, source_target_pairs={{0,16},{2,18},{4,20},{6,22},{8,24},{10,26},{12,28},{14,30},{16,0},... | collective-permute-start | bytes 1572872 | tf_op jit(solution)/shard_map/ppermute | solution.py:412
  7.2 6.4 %collective-permute-start = (bf16[48,4,512]{2,1,0:T(4,128)(2,1)S(1)}, bf16[48,4,512]{2,1,0:T(4,128)(2,1)S(1)}, u32[]{:S(2)}, u32[]{:S(2)}) collective-permute-start(bf16[48,4,512]{2,1,0:T(4,128)(2,1)S(1)} %copy-done.2), channel_id=1, source_target_pairs={{0,1},{1,0},{2,3},{3,2},{4,5},{5,4},{6,7},{7,6},{8,9},{9,8},{10,11... | collective-permute-start | bytes 589832 | tf_op jit(solution)/shard_map/ppermute | solution.py:416
  8.7 10.4 %all-to-all-start = ((s32[8,2,128]{2,1,0:T(2,128)}), s32[8,2,128]{2,1,0:T(2,128)S(1)}, u32[]{:S(2)}, u32[]{:S(2)}) async-start(s32[8,2,128]{2,1,0:T(2,128)} %request.1.after_ref), calls=%async_computation | async-start | bytes 16384 | tf_op jit(solution)/shard_map/all_to_all | solution.py:407
  19.8 4.4 %collective-permute-start.1 = (bf16[1,4,128,128]{3,2,1,0:T(8,128)(2,1)S(1)}, bf16[1,4,128,128]{3,2,1,0:T(8,128)(2,1)S(1)}, u32[]{:S(2)}, u32[]{:S(2)}) collective-permute-start(bf16[1,4,128,128]{3,2,1,0:T(8,128)(2,1)S(1)} %get-tuple-element.31), channel_id=1, source_target_pairs={{0,2},{2,0},{4,6},{6,4},{8,10},{10,8},{12,14},{14,12},{16,18},{18,... | collective-permute-start | bytes 393224 | tf_op jit(solution)/shard_map/ppermute | solution.py:430
  19.9 5.9 %collective-permute-start.2 = (bf16[1,4,128,128]{3,2,1,0:T(8,128)(2,1)S(1)}, bf16[1,4,128,128]{3,2,1,0:T(8,128)(2,1)S(1)}, u32[]{:S(2)}, u32[]{:S(2)}) collective-permute-start(bf16[1,4,128,128]{3,2,1,0:T(8,128)(2,1)S(1)} %get-tuple-element.32), channel_id=1, source_target_pairs={{0,4},{2,6},{4,0},{6,2},{8,12},{10,14},{12,8},{14,10},{16,20},{18,... | collective-permute-start | bytes 393224 | tf_op jit(solution)/shard_map/ppermute | solution.py:430
  21.5 11.7 %collective-permute-start.3 = (bf16[1,4,128,128]{3,2,1,0:T(8,128)(2,1)S(1)}, bf16[1,4,128,128]{3,2,1,0:T(8,128)(2,1)S(1)}, u32[]{:S(2)}, u32[]{:S(2)}) collective-permute-start(bf16[1,4,128,128]{3,2,1,0:T(8,128)(2,1)S(1)} %get-tuple-element.33), channel_id=1, source_target_pairs={{0,8},{2,10},{4,12},{6,14},{8,0},{10,2},{12,4},{14,6},{16,24},{18,... | collective-permute-start | bytes 393224 | tf_op jit(solution)/shard_map/ppermute | solution.py:430
  23.4 13.7 %collective-permute-start.4 = (bf16[1,4,128,128]{3,2,1,0:T(8,128)(2,1)S(1)}, bf16[1,4,128,128]{3,2,1,0:T(8,128)(2,1)S(1)}, u32[]{:S(2)}, u32[]{:S(2)}) collective-permute-start(bf16[1,4,128,128]{3,2,1,0:T(8,128)(2,1)S(1)} %get-tuple-element.34), channel_id=1, source_target_pairs={{0,12},{2,14},{4,8},{6,10},{8,4},{10,6},{12,0},{14,2},{16,28},{18,... | collective-permute-start | bytes 393224 | tf_op jit(solution)/shard_map/ppermute | solution.py:430
  24.2 14.5 %collective-permute-start.5 = (bf16[1,4,128,128]{3,2,1,0:T(8,128)(2,1)S(1)}, bf16[1,4,128,128]{3,2,1,0:T(8,128)(2,1)S(1)}, u32[]{:S(2)}, u32[]{:S(2)}) collective-permute-start(bf16[1,4,128,128]{3,2,1,0:T(8,128)(2,1)S(1)} %get-tuple-element.35), channel_id=1, source_target_pairs={{0,10},{2,8},{4,14},{6,12},{8,2},{10,0},{12,6},{14,4},{16,26},{18,... | collective-permute-start | bytes 393224 | tf_op jit(solution)/shard_map/ppermute | solution.py:430
  25.8 16.8 %collective-permute-start.6 = (bf16[1,4,128,128]{3,2,1,0:T(8,128)(2,1)S(1)}, bf16[1,4,128,128]{3,2,1,0:T(8,128)(2,1)S(1)}, u32[]{:S(2)}, u32[]{:S(2)}) collective-permute-start(bf16[1,4,128,128]{3,2,1,0:T(8,128)(2,1)S(1)} %get-tuple-element.36), channel_id=1, source_target_pairs={{0,14},{2,12},{4,10},{6,8},{8,6},{10,4},{12,2},{14,0},{16,30},{18,... | collective-permute-start | bytes 393224 | tf_op jit(solution)/shard_map/ppermute | solution.py:430
  30.4 12.2 %collective-permute-start.7 = (bf16[1,4,128,128]{3,2,1,0:T(8,128)(2,1)S(1)}, bf16[1,4,128,128]{3,2,1,0:T(8,128)(2,1)S(1)}, u32[]{:S(2)}, u32[]{:S(2)}) collective-permute-start(bf16[1,4,128,128]{3,2,1,0:T(8,128)(2,1)S(1)} %get-tuple-element.37), channel_id=1, source_target_pairs={{0,6},{2,4},{4,2},{6,0},{8,14},{10,12},{12,10},{14,8},{16,22},{18,... | collective-permute-start | bytes 393224 | tf_op jit(solution)/shard_map/ppermute | solution.py:430
  33.2 14.3 %collective-permute-start.9 = (bf16[1,4,128,128]{3,2,1,0:T(8,128)(2,1)S(1)}, bf16[1,4,128,128]{3,2,1,0:T(8,128)(2,1)S(1)}, u32[]{:S(2)}, u32[]{:S(2)}) collective-permute-start(bf16[1,4,128,128]{3,2,1,0:T(8,128)(2,1)S(1)} %get-tuple-element.41), channel_id=1, source_target_pairs={{0,8},{2,10},{4,12},{6,14},{8,0},{10,2},{12,4},{14,6},{16,24},{18,... | collective-permute-start | bytes 393224 | tf_op jit(solution)/shard_map/ppermute | solution.py:430
  37.0 11.7 %collective-permute-start.10 = (bf16[1,4,128,128]{3,2,1,0:T(8,128)(2,1)S(1)}, bf16[1,4,128,128]{3,2,1,0:T(8,128)(2,1)S(1)}, u32[]{:S(2)}, u32[]{:S(2)}) collective-permute-start(bf16[1,4,128,128]{3,2,1,0:T(8,128)(2,1)S(1)} %get-tuple-element.42), channel_id=1, source_target_pairs={{0,4},{2,6},{4,0},{6,2},{8,12},{10,14},{12,8},{14,10},{16,20},{18,... | collective-permute-start | bytes 393224 | tf_op jit(solution)/shard_map/ppermute | solution.py:430
  38.8 10.5 %collective-permute-start.11 = (bf16[1,4,128,128]{3,2,1,0:T(8,128)(2,1)S(1)}, bf16[1,4,128,128]{3,2,1,0:T(8,128)(2,1)S(1)}, u32[]{:S(2)}, u32[]{:S(2)}) collective-permute-start(bf16[1,4,128,128]{3,2,1,0:T(8,128)(2,1)S(1)} %get-tuple-element.43), channel_id=1, source_target_pairs={{0,12},{2,14},{4,8},{6,10},{8,4},{10,6},{12,0},{14,2},{16,28},{18,... | collective-permute-start | bytes 393224 | tf_op jit(solution)/shard_map/ppermute | solution.py:430
  45.1 6.6 %collective-permute-start.12 = (bf16[1,4,128,128]{3,2,1,0:T(8,128)(2,1)S(1)}, bf16[1,4,128,128]{3,2,1,0:T(8,128)(2,1)S(1)}, u32[]{:S(2)}, u32[]{:S(2)}) collective-permute-start(bf16[1,4,128,128]{3,2,1,0:T(8,128)(2,1)S(1)} %get-tuple-element.46), channel_id=1, source_target_pairs={{0,14},{2,12},{4,10},{6,8},{8,6},{10,4},{12,2},{14,0},{16,30},{18,... | collective-permute-start | bytes 393224 | tf_op jit(solution)/shard_map/ppermute | solution.py:430
  45.1 8.3 %collective-permute-start.13 = (bf16[1,4,128,128]{3,2,1,0:T(8,128)(2,1)S(1)}, bf16[1,4,128,128]{3,2,1,0:T(8,128)(2,1)S(1)}, u32[]{:S(2)}, u32[]{:S(2)}) collective-permute-start(bf16[1,4,128,128]{3,2,1,0:T(8,128)(2,1)S(1)} %get-tuple-element.47), channel_id=1, source_target_pairs={{0,10},{2,8},{4,14},{6,12},{8,2},{10,0},{12,6},{14,4},{16,26},{18,... | collective-permute-start | bytes 393224 | tf_op jit(solution)/shard_map/ppermute | solution.py:430
  47.5 7.1 %collective-permute-start.14 = (bf16[1,4,128,128]{3,2,1,0:T(8,128)(2,1)S(1)}, bf16[1,4,128,128]{3,2,1,0:T(8,128)(2,1)S(1)}, u32[]{:S(2)}, u32[]{:S(2)}) collective-permute-start(bf16[1,4,128,128]{3,2,1,0:T(8,128)(2,1)S(1)} %get-tuple-element.48), channel_id=1, source_target_pairs={{0,6},{2,4},{4,2},{6,0},{8,14},{10,12},{12,10},{14,8},{16,22},{18,... | collective-permute-start | bytes 393224 | tf_op jit(solution)/shard_map/ppermute | solution.py:430
  48.8 5.8 %collective-permute-start.15 = (bf16[1,4,128,128]{3,2,1,0:T(8,128)(2,1)S(1)}, bf16[1,4,128,128]{3,2,1,0:T(8,128)(2,1)S(1)}, u32[]{:S(2)}, u32[]{:S(2)}) collective-permute-start(bf16[1,4,128,128]{3,2,1,0:T(8,128)(2,1)S(1)} %pick_each.5), channel_id=1, source_target_pairs={{0,2},{2,0},{4,6},{6,4},{8,10},{10,8},{12,14},{14,12},{16,18},{18,... | collective-permute-start | bytes 393224 | tf_op jit(solution)/shard_map/ppermute | solution.py:430
  54.6 4.5 %copy-start = (bf16[512,512]{1,0:T(8,128)(2,1)S(1)}, bf16[512,512]{1,0:T(8,128)(2,1)}, u32[]{:S(2)}) copy-start(bf16[512,512]{1,0:T(8,128)(2,1)} %weight_ref.1) | copy-start | bytes 1572868
  56.1 4.9 %collective-permute-start.16 = (bf16[192,256]{1,0:T(8,128)(2,1)S(1)}, bf16[192,256]{1,0:T(8,128)(2,1)S(1)}, u32[]{:S(2)}, u32[]{:S(2)}) collective-permute-start(bf16[192,256]{1,0:T(8,128)(2,1)S(1)} %last_tiles.2.refs_4_), channel_id=1, source_target_pairs={{0,1},{1,0},{2,3},{3,2},{4,5},{5,4},{6,7},{7,6},{8,9},{9,8},{10,11... | collective-permute-start | bytes 294920 | tf_op jit(solution)/shard_map/ppermute | solution.py:449

commit v19 on v18

--- a/solution.py
+++ b/solution.py
@@ -268,7 +268,7 @@
 
 
 def first_kernel(slots, block, asked_ref, *refs):
-    tile_refs, (sums_ref, tops_ref) = refs[:len(slots)], refs[len(slots):]
+    tile_refs, (sums_ref, tops_ref) = refs[:len(slots)], refs[-2:]
     heads, rows_all, lanes = asked_ref.shape
     lane = iota((block, lanes), 1)
     for step in range(rows_all // block):
@@ -280,17 +280,17 @@
         tops_ref[rows, :] = tops
 
 
-def first_tiles(asked, tiles, slots, own_rows):
+def first_tiles(asked, tiles, slots, own_rows, after):
     heads, rows, lanes = asked.shape
     return pl.pallas_call(
         functools.partial(first_kernel, slots, rows if rows <= 512 else own_rows),
         out_shape=(jax.ShapeDtypeStruct((heads, rows, lanes), jnp.float32), jax.ShapeDtypeStruct((rows, lanes), jnp.float32)),
-        in_specs=[VMEM] * (1 + len(tiles)),
+        in_specs=[VMEM] * (1 + len(tiles)) + [ANY] * len(after),
         out_specs=(VMEM, VMEM),
         compiler_params=params(rows),
         cost_estimate=attention_cost(asked, tiles),
         name="first_tiles",
-    )(asked, *tiles)
+    )(asked, *tiles, *after)
 
 
 def merge(asked_ref, sums_ref, tops_ref, tile_refs, slots, head, rows):
@@ -436,7 +436,7 @@
                             heads_all, head_size, cols, heads_here, tiles_here, row_size, paired, [])
     near = spread(heads_first, 0, near_order, [asked])
     far = spread(mirrored, 1, far_order[:-1] if paired else far_order, near[1:3])
-    sums, tops = first_tiles(asked, near, near_slots, rows * cols)
+    sums, tops = first_tiles(asked, near, near_slots, rows * cols, far[1:2])
     far += spread(mirrored, 1, far_order[-1:] if paired else [], [tops])
     batch = len(far) // 2
     if batch:

time: 62.2 us -> 61.4 us (0.987)
    ppermute x14, waiting for transfers between devices: 14 us -> 13.3 us  [spread(): lax.ppermute(tile, 'rows', [(row, row ^ step) for row in range(row_size)])]
where the time goes in v19:
time: 61.4 us; the launch traced here: 61.2 us
  starting transfers between devices  23.2 us (38%)
  waiting for transfers between devices  18 us (29%)
  Pallas kernels  17 us (28%)
  local copies, waits for them, and re-layouts  2.57 us (4%)
    ppermute x14, waiting for transfers between devices, spread(): lax.ppermute(tile, 'rows', [(row, row ^ step) for row in range(row_size)])  13.3 us
    ppermute x14, starting transfers between devices, spread(): lax.ppermute(tile, 'rows', [(row, row ^ step) for row in range(row_size)])  12.3 us
    pallas_call x1, Pallas kernels, front(): pl.pallas_call(functools.partial(front_kernel, groups, heads, head_size,...  5.51 us
    ppermute x1, starting transfers between devices, shards(): mirrored = lax.ppermute(heads_first, 'rows', turn(row_size, half))  4.04 us
    all_to_all x1, starting transfers between devices, swap(): lax.all_to_all(value, 'rows', split_axis=0, concat_axis=0, tiled=True, ax...  3.78 us
    pallas_call x2, Pallas kernels, last_tiles(): pl.pallas_call(functools.partial(last_kernel, slots, groups), out_shape=(...  2.87 us
    ppermute x1, waiting for transfers between devices, shards(): mirrored = lax.ppermute(heads_first, 'rows', turn(row_size, half))  2.53 us
    pallas_call x1, Pallas kernels, first_tiles(): pl.pallas_call(functools.partial(first_kernel, slots, rows if rows <= 512...  2.4 us
  transfers between devices with their start and end apart: 18, of which 11 were waited for; matrix products, arithmetic and copies ran while one was open for 0% of the time, Pallas kernels for 23%

profile of v19, /device:TPU:0, one launch (start us, length us, event | category | flops | bytes accessed | tf_op | source)
XLA Modules:
  0.0 61.2 jit_solution(12018492081251849857)
XLA Ops:
  0.0 1.2 %copy.14 = bf16[4,128,4,128]{3,1,2,0:T(8,128)(2,1)S(1)} copy(bf16[4,128,4,128]{3,2,1,0:T(4,128)(2,1)} %param.17) | data formatting | bytes 1048576 | tf_op args[7]
  1.9 1.2 %request.1.after_ref = s32[8,2,128]{2,1,0:T(2,128)} custom-call(s32[1,12]{1,0:T(1,128)S(1)} %copy-done.1, s32[2]{0:T(128)S(1)} %pad_add_fusion.refs_2_.me_ref), custom_call_target="tpu_custom_call" | custom-call | bytes 262144 | tf_op jit(solution)/shard_map/request/pallas_call | solution.py:76
  3.1 4.0 %collective-permute-start.8 = (bf16[4,4,128,128]{3,2,1,0:T(8,128)(2,1)S(1)}, bf16[4,4,128,128]{3,2,1,0:T(8,128)(2,1)S(1)}, u32[]{:S(2)}, u32[]{:S(2)}) collective-permute-start(bf16[4,4,128,128]{3,2,1,0:T(8,128)(2,1)S(1)} %tie.1.tiles_ref), channel_id=1, source_target_pairs={{0,16},{2,18},{4,20},{6,22},{8,24},{10,26},{12,28},{14,30},{16,0},... | collective-permute-start | bytes 1572872 | tf_op jit(solution)/shard_map/ppermute | solution.py:412
  7.2 1.5 %collective-permute-start = (bf16[48,4,512]{2,1,0:T(4,128)(2,1)S(1)}, bf16[48,4,512]{2,1,0:T(4,128)(2,1)S(1)}, u32[]{:S(2)}, u32[]{:S(2)}) collective-permute-start(bf16[48,4,512]{2,1,0:T(4,128)(2,1)S(1)} %copy-done.2), channel_id=1, source_target_pairs={{0,1},{1,0},{2,3},{3,2},{4,5},{5,4},{6,7},{7,6},{8,9},{9,8},{10,11... | collective-permute-start | bytes 589832 | tf_op jit(solution)/shard_map/ppermute | solution.py:416
  8.7 3.8 %all-to-all-start = ((s32[8,2,128]{2,1,0:T(2,128)}), s32[8,2,128]{2,1,0:T(2,128)S(1)}, u32[]{:S(2)}, u32[]{:S(2)}) async-start(s32[8,2,128]{2,1,0:T(2,128)} %request.1.after_ref), calls=%async_computation | async-start | bytes 16384 | tf_op jit(solution)/shard_map/all_to_all | solution.py:407
  13.5 5.5 %front.1 = (f32[192,512]{1,0:T(8,128)S(1)}, bf16[4,384,128]{2,1,0:T(8,128)(2,1)S(1)}) custom-call(bf16[48,4,512]{2,1,0:T(4,128)(2,1)} %refs_0_.1, bf16[48,4,512]{2,1,0:T(4,128)(2,1)S(1)} %collective-permute-done.refs_1_, s32[2]{0:T(128)S(1)} %pad_add_fusion.refs_2_.me_ref, s32[1,12]{1,0:T(1,128)} %ids_ref.1, s32[12,48]{1,0:T(8,128)} %bitcast.11, ...), custom_call_target="tpu_custom_call" | custom-call | flops 1006632960 | bytes 4194304 | tf_op jit(solution)/shard_map/front/pallas_call | solution.py:235
  19.9 1.6 %collective-permute-start.2 = (bf16[1,4,128,128]{3,2,1,0:T(8,128)(2,1)S(1)}, bf16[1,4,128,128]{3,2,1,0:T(8,128)(2,1)S(1)}, u32[]{:S(2)}, u32[]{:S(2)}) collective-permute-start(bf16[1,4,128,128]{3,2,1,0:T(8,128)(2,1)S(1)} %get-tuple-element.32), channel_id=1, source_target_pairs={{0,4},{2,6},{4,0},{6,2},{8,12},{10,14},{12,8},{14,10},{16,20},{18,... | collective-permute-start | bytes 393224 | tf_op jit(solution)/shard_map/ppermute | solution.py:430
  21.5 1.9 %collective-permute-start.3 = (bf16[1,4,128,128]{3,2,1,0:T(8,128)(2,1)S(1)}, bf16[1,4,128,128]{3,2,1,0:T(8,128)(2,1)S(1)}, u32[]{:S(2)}, u32[]{:S(2)}) collective-permute-start(bf16[1,4,128,128]{3,2,1,0:T(8,128)(2,1)S(1)} %get-tuple-element.33), channel_id=1, source_target_pairs={{0,8},{2,10},{4,12},{6,14},{8,0},{10,2},{12,4},{14,6},{16,24},{18,... | collective-permute-start | bytes 393224 | tf_op jit(solution)/shard_map/ppermute | solution.py:430
  24.2 1.2 %collective-permute-start.5 = (bf16[1,4,128,128]{3,2,1,0:T(8,128)(2,1)S(1)}, bf16[1,4,128,128]{3,2,1,0:T(8,128)(2,1)S(1)}, u32[]{:S(2)}, u32[]{:S(2)}) collective-permute-start(bf16[1,4,128,128]{3,2,1,0:T(8,128)(2,1)S(1)} %get-tuple-element.35), channel_id=1, source_target_pairs={{0,10},{2,8},{4,14},{6,12},{8,2},{10,0},{12,6},{14,4},{16,26},{18,... | collective-permute-start | bytes 393224 | tf_op jit(solution)/shard_map/ppermute | solution.py:430
  25.8 2.1 %collective-permute-start.6 = (bf16[1,4,128,128]{3,2,1,0:T(8,128)(2,1)S(1)}, bf16[1,4,128,128]{3,2,1,0:T(8,128)(2,1)S(1)}, u32[]{:S(2)}, u32[]{:S(2)}) collective-permute-start(bf16[1,4,128,128]{3,2,1,0:T(8,128)(2,1)S(1)} %get-tuple-element.36), channel_id=1, source_target_pairs={{0,14},{2,12},{4,10},{6,8},{8,6},{10,4},{12,2},{14,0},{16,30},{18,... | collective-permute-start | bytes 393224 | tf_op jit(solution)/shard_map/ppermute | solution.py:430
  27.9 2.5 %collective-permute-done.8.tiles_ref = bf16[4,4,128,128]{3,2,1,0:T(8,128)(2,1)S(1)} collective-permute-done((bf16[4,4,128,128]{3,2,1,0:T(8,128)(2,1)S(1)}, bf16[4,4,128,128]{3,2,1,0:T(8,128)(2,1)S(1)}, u32[]{:S(2)}, u32[]{:S(2)}) %collective-permute-start.8) | collective-permute-done | bytes 524320 | tf_op jit(solution)/shard_map/ppermute | solution.py:412
  31.3 1.9 %collective-permute-done.3.refs_3_ = bf16[1,4,128,128]{3,2,1,0:T(8,128)(2,1)S(1)} collective-permute-done((bf16[1,4,128,128]{3,2,1,0:T(8,128)(2,1)S(1)}, bf16[1,4,128,128]{3,2,1,0:T(8,128)(2,1)S(1)}, u32[]{:S(2)}, u32[]{:S(2)}) %collective-permute-start.3) | collective-permute-done | bytes 131104 | tf_op jit(solution)/shard_map/ppermute | solution.py:430
  33.2 3.8 %collective-permute-done.4.refs_4_ = bf16[1,4,128,128]{3,2,1,0:T(8,128)(2,1)S(1)} collective-permute-done((bf16[1,4,128,128]{3,2,1,0:T(8,128)(2,1)S(1)}, bf16[1,4,128,128]{3,2,1,0:T(8,128)(2,1)S(1)}, u32[]{:S(2)}, u32[]{:S(2)}) %collective-permute-start.4) | collective-permute-done | bytes 131104 | tf_op jit(solution)/shard_map/ppermute | solution.py:430
  37.5 1.2 %collective-permute-done.5.refs_5_ = bf16[1,4,128,128]{3,2,1,0:T(8,128)(2,1)S(1)} collective-permute-done((bf16[1,4,128,128]{3,2,1,0:T(8,128)(2,1)S(1)}, bf16[1,4,128,128]{3,2,1,0:T(8,128)(2,1)S(1)}, u32[]{:S(2)}, u32[]{:S(2)}) %collective-permute-start.5) | collective-permute-done | bytes 131104 | tf_op jit(solution)/shard_map/ppermute | solution.py:430
  39.4 3.3 %collective-permute-done.6.refs_6_ = bf16[1,4,128,128]{3,2,1,0:T(8,128)(2,1)S(1)} collective-permute-done((bf16[1,4,128,128]{3,2,1,0:T(8,128)(2,1)S(1)}, bf16[1,4,128,128]{3,2,1,0:T(8,128)(2,1)S(1)}, u32[]{:S(2)}, u32[]{:S(2)}) %collective-permute-start.6) | collective-permute-done | bytes 131104 | tf_op jit(solution)/shard_map/ppermute | solution.py:430
  42.7 1.7 %collective-permute-start.13 = (bf16[1,4,128,128]{3,2,1,0:T(8,128)(2,1)S(1)}, bf16[1,4,128,128]{3,2,1,0:T(8,128)(2,1)S(1)}, u32[]{:S(2)}, u32[]{:S(2)}) collective-permute-start(bf16[1,4,128,128]{3,2,1,0:T(8,128)(2,1)S(1)} %get-tuple-element.47), channel_id=1, source_target_pairs={{0,10},{2,8},{4,14},{6,12},{8,2},{10,0},{12,6},{14,4},{16,26},{18,... | collective-permute-start | bytes 393224 | tf_op jit(solution)/shard_map/ppermute | solution.py:430
  44.5 1.2 %collective-permute-start.14 = (bf16[1,4,128,128]{3,2,1,0:T(8,128)(2,1)S(1)}, bf16[1,4,128,128]{3,2,1,0:T(8,128)(2,1)S(1)}, u32[]{:S(2)}, u32[]{:S(2)}) collective-permute-start(bf16[1,4,128,128]{3,2,1,0:T(8,128)(2,1)S(1)} %get-tuple-element.48), channel_id=1, source_target_pairs={{0,6},{2,4},{4,2},{6,0},{8,14},{10,12},{12,10},{14,8},{16,22},{18,... | collective-permute-start | bytes 393224 | tf_op jit(solution)/shard_map/ppermute | solution.py:430
  45.7 2.4 %first_tiles.1 = (f32[4,384,128]{2,1,0:T(8,128)S(1)}, f32[384,128]{1,0:T(8,128)S(1)}) custom-call(bf16[4,384,128]{2,1,0:T(8,128)(2,1)S(1)} %get-tuple-element.29.refs_0_.asked_ref, bf16[1,4,128,128]{3,2,1,0:T(8,128)(2,1)S(1)} %get-tuple-element.30.refs_0_, bf16[1,4,128,128]{3,2,1,0:T(8,128)(2,1)S(1)} %collective-permute-done.1.refs_0_.refs_1_, ...), custom_call_target="tpu_custom_call" | custom-call | flops 805306368 | bytes 4194304 | tf_op jit(solution)/shard_map/first_tiles/pallas_call | solution.py:285
  49.4 2.0 %more_tiles.1 = (f32[4,384,128]{2,1,0:T(8,128)S(1)}, f32[384,128]{1,0:T(8,128)S(1)}) custom-call(bf16[4,384,128]{2,1,0:T(8,128)(2,1)S(1)} %get-tuple-element.29.refs_0_.asked_ref, f32[4,384,128]{2,1,0:T(8,128)S(1)} %get-tuple-element.39.old_sums_ref, f32[384,128]{1,0:T(8,128)S(1)} %get-tuple-element.40.old_tops_ref.refs_0_, ...), custom_call_target="tpu_custom_call" | custom-call | flops 402653184 | bytes 4194304 | tf_op jit(solution)/shard_map/more_tiles/pallas_call | solution.py:318
  51.4 1.5 %collective-permute-done.13.refs_1_ = bf16[1,4,128,128]{3,2,1,0:T(8,128)(2,1)S(1)} collective-permute-done((bf16[1,4,128,128]{3,2,1,0:T(8,128)(2,1)S(1)}, bf16[1,4,128,128]{3,2,1,0:T(8,128)(2,1)S(1)}, u32[]{:S(2)}, u32[]{:S(2)}) %collective-permute-start.13) | collective-permute-done | bytes 131104 | tf_op jit(solution)/shard_map/ppermute | solution.py:430
  53.9 1.4 %last_tiles.2.refs_4_ = bf16[192,256]{1,0:T(8,128)(2,1)S(1)} custom-call(bf16[4,384,128]{2,1,0:T(8,128)(2,1)S(1)} %get-tuple-element.29.refs_0_.asked_ref, f32[4,384,128]{2,1,0:T(8,128)S(1)} %get-tuple-element.44.sums_ref, f32[384,128]{1,0:T(8,128)S(1)} %get-tuple-element.45.tops_ref, bf16[1,4,128,128]{3,2,1,0:T(8,128)(2,1)S(1)} %collective-permute-done.12.refs_0_, ...), custom_call_target="tpu_custom_call" | custom-call | flops 201326592 | bytes 4194304 | tf_op jit(solution)/shard_map/last_tiles/pallas_call | solution.py:352
  55.3 1.6 %collective-permute-start.16 = (bf16[192,256]{1,0:T(8,128)(2,1)S(1)}, bf16[192,256]{1,0:T(8,128)(2,1)S(1)}, u32[]{:S(2)}, u32[]{:S(2)}) collective-permute-start(bf16[192,256]{1,0:T(8,128)(2,1)S(1)} %last_tiles.2.refs_4_), channel_id=1, source_target_pairs={{0,1},{1,0},{2,3},{3,2},{4,5},{5,4},{6,7},{7,6},{8,9},{9,8},{10,11... | collective-permute-start | bytes 294920 | tf_op jit(solution)/shard_map/ppermute | solution.py:449
  56.9 1.4 %last_tiles.3.answer_ref = bf16[192,256]{1,0:T(8,128)(2,1)S(1)} custom-call(bf16[4,384,128]{2,1,0:T(8,128)(2,1)S(1)} %get-tuple-element.29.refs_0_.asked_ref, f32[4,384,128]{2,1,0:T(8,128)S(1)} %get-tuple-element.44.sums_ref, f32[384,128]{1,0:T(8,128)S(1)} %get-tuple-element.45.tops_ref, bf16[1,4,128,128]{3,2,1,0:T(8,128)(2,1)S(1)} %collective-permute-done.12.refs_0_, ...), custom_call_target="tpu_custom_call" | custom-call | flops 201326592 | bytes 4194304 | tf_op jit(solution)/shard_map/last_tiles/pallas_call | solution.py:352
  59.1 1.1 %collective-permute-done.16 = bf16[192,256]{1,0:T(8,128)(2,1)S(1)} collective-permute-done((bf16[192,256]{1,0:T(8,128)(2,1)S(1)}, bf16[192,256]{1,0:T(8,128)(2,1)S(1)}, u32[]{:S(2)}, u32[]{:S(2)}) %collective-permute-start.16) | collective-permute-done | bytes 98336 | tf_op jit(solution)/shard_map/ppermute | solution.py:449
  (34 shorter events, 10.0 us)
Async XLA Ops:
  0.0 7.2 %copy-start.2 = (bf16[48,4,512]{2,1,0:T(4,128)(2,1)S(1)}, bf16[48,4,512]{2,1,0:T(4,128)(2,1)}, u32[]{:S(2)}) copy-start(bf16[48,4,512]{2,1,0:T(4,128)(2,1)} %refs_0_.1) | copy-start | bytes 589828
  1.3 0.7 %copy-start.1 = (s32[1,12]{1,0:T(1,128)S(1)}, s32[1,12]{1,0:T(1,128)}, u32[]{:S(2)}) copy-start(s32[1,12]{1,0:T(1,128)} %ids_ref.1) | copy-start | bytes 148
  3.1 27.3 %collective-permute-start.8 = (bf16[4,4,128,128]{3,2,1,0:T(8,128)(2,1)S(1)}, bf16[4,4,128,128]{3,2,1,0:T(8,128)(2,1)S(1)}, u32[]{:S(2)}, u32[]{:S(2)}) collective-permute-start(bf16[4,4,128,128]{3,2,1,0:T(8,128)(2,1)S(1)} %tie.1.tiles_ref), channel_id=1, source_target_pairs={{0,16},{2,18},{4,20},{6,22},{8,24},{10,26},{12,28},{14,30},{16,0},... | collective-permute-start | bytes 1572872 | tf_op jit(solution)/shard_map/ppermute | solution.py:412
  7.2 6.4 %collective-permute-start = (bf16[48,4,512]{2,1,0:T(4,128)(2,1)S(1)}, bf16[48,4,512]{2,1,0:T(4,128)(2,1)S(1)}, u32[]{:S(2)}, u32[]{:S(2)}) collective-permute-start(bf16[48,4,512]{2,1,0:T(4,128)(2,1)S(1)} %copy-done.2), channel_id=1, source_target_pairs={{0,1},{1,0},{2,3},{3,2},{4,5},{5,4},{6,7},{7,6},{8,9},{9,8},{10,11... | collective-permute-start | bytes 589832 | tf_op jit(solution)/shard_map/ppermute | solution.py:416
  8.7 10.4 %all-to-all-start = ((s32[8,2,128]{2,1,0:T(2,128)}), s32[8,2,128]{2,1,0:T(2,128)S(1)}, u32[]{:S(2)}, u32[]{:S(2)}) async-start(s32[8,2,128]{2,1,0:T(2,128)} %request.1.after_ref), calls=%async_computation | async-start | bytes 16384 | tf_op jit(solution)/shard_map/all_to_all | solution.py:407
  19.8 4.4 %collective-permute-start.1 = (bf16[1,4,128,128]{3,2,1,0:T(8,128)(2,1)S(1)}, bf16[1,4,128,128]{3,2,1,0:T(8,128)(2,1)S(1)}, u32[]{:S(2)}, u32[]{:S(2)}) collective-permute-start(bf16[1,4,128,128]{3,2,1,0:T(8,128)(2,1)S(1)} %get-tuple-element.31), channel_id=1, source_target_pairs={{0,2},{2,0},{4,6},{6,4},{8,10},{10,8},{12,14},{14,12},{16,18},{18,... | collective-permute-start | bytes 393224 | tf_op jit(solution)/shard_map/ppermute | solution.py:430
  19.9 5.9 %collective-permute-start.2 = (bf16[1,4,128,128]{3,2,1,0:T(8,128)(2,1)S(1)}, bf16[1,4,128,128]{3,2,1,0:T(8,128)(2,1)S(1)}, u32[]{:S(2)}, u32[]{:S(2)}) collective-permute-start(bf16[1,4,128,128]{3,2,1,0:T(8,128)(2,1)S(1)} %get-tuple-element.32), channel_id=1, source_target_pairs={{0,4},{2,6},{4,0},{6,2},{8,12},{10,14},{12,8},{14,10},{16,20},{18,... | collective-permute-start | bytes 393224 | tf_op jit(solution)/shard_map/ppermute | solution.py:430
  21.5 11.7 %collective-permute-start.3 = (bf16[1,4,128,128]{3,2,1,0:T(8,128)(2,1)S(1)}, bf16[1,4,128,128]{3,2,1,0:T(8,128)(2,1)S(1)}, u32[]{:S(2)}, u32[]{:S(2)}) collective-permute-start(bf16[1,4,128,128]{3,2,1,0:T(8,128)(2,1)S(1)} %get-tuple-element.33), channel_id=1, source_target_pairs={{0,8},{2,10},{4,12},{6,14},{8,0},{10,2},{12,4},{14,6},{16,24},{18,... | collective-permute-start | bytes 393224 | tf_op jit(solution)/shard_map/ppermute | solution.py:430
  23.4 13.7 %collective-permute-start.4 = (bf16[1,4,128,128]{3,2,1,0:T(8,128)(2,1)S(1)}, bf16[1,4,128,128]{3,2,1,0:T(8,128)(2,1)S(1)}, u32[]{:S(2)}, u32[]{:S(2)}) collective-permute-start(bf16[1,4,128,128]{3,2,1,0:T(8,128)(2,1)S(1)} %get-tuple-element.34), channel_id=1, source_target_pairs={{0,12},{2,14},{4,8},{6,10},{8,4},{10,6},{12,0},{14,2},{16,28},{18,... | collective-permute-start | bytes 393224 | tf_op jit(solution)/shard_map/ppermute | solution.py:430
  24.2 14.5 %collective-permute-start.5 = (bf16[1,4,128,128]{3,2,1,0:T(8,128)(2,1)S(1)}, bf16[1,4,128,128]{3,2,1,0:T(8,128)(2,1)S(1)}, u32[]{:S(2)}, u32[]{:S(2)}) collective-permute-start(bf16[1,4,128,128]{3,2,1,0:T(8,128)(2,1)S(1)} %get-tuple-element.35), channel_id=1, source_target_pairs={{0,10},{2,8},{4,14},{6,12},{8,2},{10,0},{12,6},{14,4},{16,26},{18,... | collective-permute-start | bytes 393224 | tf_op jit(solution)/shard_map/ppermute | solution.py:430
  25.8 16.8 %collective-permute-start.6 = (bf16[1,4,128,128]{3,2,1,0:T(8,128)(2,1)S(1)}, bf16[1,4,128,128]{3,2,1,0:T(8,128)(2,1)S(1)}, u32[]{:S(2)}, u32[]{:S(2)}) collective-permute-start(bf16[1,4,128,128]{3,2,1,0:T(8,128)(2,1)S(1)} %get-tuple-element.36), channel_id=1, source_target_pairs={{0,14},{2,12},{4,10},{6,8},{8,6},{10,4},{12,2},{14,0},{16,30},{18,... | collective-permute-start | bytes 393224 | tf_op jit(solution)/shard_map/ppermute | solution.py:430
  30.4 12.2 %collective-permute-start.7 = (bf16[1,4,128,128]{3,2,1,0:T(8,128)(2,1)S(1)}, bf16[1,4,128,128]{3,2,1,0:T(8,128)(2,1)S(1)}, u32[]{:S(2)}, u32[]{:S(2)}) collective-permute-start(bf16[1,4,128,128]{3,2,1,0:T(8,128)(2,1)S(1)} %get-tuple-element.37), channel_id=1, source_target_pairs={{0,6},{2,4},{4,2},{6,0},{8,14},{10,12},{12,10},{14,8},{16,22},{18,... | collective-permute-start | bytes 393224 | tf_op jit(solution)/shard_map/ppermute | solution.py:430
  33.2 11.3 %collective-permute-start.9 = (bf16[1,4,128,128]{3,2,1,0:T(8,128)(2,1)S(1)}, bf16[1,4,128,128]{3,2,1,0:T(8,128)(2,1)S(1)}, u32[]{:S(2)}, u32[]{:S(2)}) collective-permute-start(bf16[1,4,128,128]{3,2,1,0:T(8,128)(2,1)S(1)} %get-tuple-element.38), channel_id=1, source_target_pairs={{0,8},{2,10},{4,12},{6,14},{8,0},{10,2},{12,4},{14,6},{16,24},{18,... | collective-permute-start | bytes 393224 | tf_op jit(solution)/shard_map/ppermute | solution.py:430
  37.0 11.8 %collective-permute-start.10 = (bf16[1,4,128,128]{3,2,1,0:T(8,128)(2,1)S(1)}, bf16[1,4,128,128]{3,2,1,0:T(8,128)(2,1)S(1)}, u32[]{:S(2)}, u32[]{:S(2)}) collective-permute-start(bf16[1,4,128,128]{3,2,1,0:T(8,128)(2,1)S(1)} %get-tuple-element.42), channel_id=1, source_target_pairs={{0,4},{2,6},{4,0},{6,2},{8,12},{10,14},{12,8},{14,10},{16,20},{18,... | collective-permute-start | bytes 393224 | tf_op jit(solution)/shard_map/ppermute | solution.py:430
  38.8 10.6 %collective-permute-start.11 = (bf16[1,4,128,128]{3,2,1,0:T(8,128)(2,1)S(1)}, bf16[1,4,128,128]{3,2,1,0:T(8,128)(2,1)S(1)}, u32[]{:S(2)}, u32[]{:S(2)}) collective-permute-start(bf16[1,4,128,128]{3,2,1,0:T(8,128)(2,1)S(1)} %get-tuple-element.43), channel_id=1, source_target_pairs={{0,12},{2,14},{4,8},{6,10},{8,4},{10,6},{12,0},{14,2},{16,28},{18,... | collective-permute-start | bytes 393224 | tf_op jit(solution)/shard_map/ppermute | solution.py:430
  42.7 8.7 %collective-permute-start.12 = (bf16[1,4,128,128]{3,2,1,0:T(8,128)(2,1)S(1)}, bf16[1,4,128,128]{3,2,1,0:T(8,128)(2,1)S(1)}, u32[]{:S(2)}, u32[]{:S(2)}) collective-permute-start(bf16[1,4,128,128]{3,2,1,0:T(8,128)(2,1)S(1)} %get-tuple-element.46), channel_id=1, source_target_pairs={{0,14},{2,12},{4,10},{6,8},{8,6},{10,4},{12,2},{14,0},{16,30},{18,... | collective-permute-start | bytes 393224 | tf_op jit(solution)/shard_map/ppermute | solution.py:430
  42.7 10.2 %collective-permute-start.13 = (bf16[1,4,128,128]{3,2,1,0:T(8,128)(2,1)S(1)}, bf16[1,4,128,128]{3,2,1,0:T(8,128)(2,1)S(1)}, u32[]{:S(2)}, u32[]{:S(2)}) collective-permute-start(bf16[1,4,128,128]{3,2,1,0:T(8,128)(2,1)S(1)} %get-tuple-element.47), channel_id=1, source_target_pairs={{0,10},{2,8},{4,14},{6,12},{8,2},{10,0},{12,6},{14,4},{16,26},{18,... | collective-permute-start | bytes 393224 | tf_op jit(solution)/shard_map/ppermute | solution.py:430
  44.5 9.3 %collective-permute-start.14 = (bf16[1,4,128,128]{3,2,1,0:T(8,128)(2,1)S(1)}, bf16[1,4,128,128]{3,2,1,0:T(8,128)(2,1)S(1)}, u32[]{:S(2)}, u32[]{:S(2)}) collective-permute-start(bf16[1,4,128,128]{3,2,1,0:T(8,128)(2,1)S(1)} %get-tuple-element.48), channel_id=1, source_target_pairs={{0,6},{2,4},{4,2},{6,0},{8,14},{10,12},{12,10},{14,8},{16,22},{18,... | collective-permute-start | bytes 393224 | tf_op jit(solution)/shard_map/ppermute | solution.py:430
  48.8 5.1 %collective-permute-start.15 = (bf16[1,4,128,128]{3,2,1,0:T(8,128)(2,1)S(1)}, bf16[1,4,128,128]{3,2,1,0:T(8,128)(2,1)S(1)}, u32[]{:S(2)}, u32[]{:S(2)}) collective-permute-start(bf16[1,4,128,128]{3,2,1,0:T(8,128)(2,1)S(1)} %pick_each.5), channel_id=1, source_target_pairs={{0,2},{2,0},{4,6},{6,4},{8,10},{10,8},{12,14},{14,12},{16,18},{18,... | collective-permute-start | bytes 393224 | tf_op jit(solution)/shard_map/ppermute | solution.py:430
  53.9 4.5 %copy-start = (bf16[512,512]{1,0:T(8,128)(2,1)S(1)}, bf16[512,512]{1,0:T(8,128)(2,1)}, u32[]{:S(2)}) copy-start(bf16[512,512]{1,0:T(8,128)(2,1)} %weight_ref.1) | copy-start | bytes 1572868
  55.3 4.9 %collective-permute-start.16 = (bf16[192,256]{1,0:T(8,128)(2,1)S(1)}, bf16[192,256]{1,0:T(8,128)(2,1)S(1)}, u32[]{:S(2)}, u32[]{:S(2)}) collective-permute-start(bf16[192,256]{1,0:T(8,128)(2,1)S(1)} %last_tiles.2.refs_4_), channel_id=1, source_target_pairs={{0,1},{1,0},{2,3},{3,2},{4,5},{5,4},{6,7},{7,6},{8,9},{9,8},{10,11... | collective-permute-start | bytes 294920 | tf_op jit(solution)/shard_map/ppermute | solution.py:449

commit v20 on v19

--- a/solution.py
+++ b/solution.py
@@ -40,23 +40,6 @@
 def slot_of(owner, row_me, row_size, paired):
     half = row_size // 2
     return owner ^ row_me if paired else lax.rem(owner + lax.div(row_me, half) * half, row_size)
-
-
-def tie_kernel(value_ref, after_ref, out_ref):
-    pass
-
-
-def tie(value, after):
-    return pl.pallas_call(
-        tie_kernel,
-        out_shape=jax.ShapeDtypeStruct(value.shape, value.dtype),
-        in_specs=[ANY, ANY],
-        out_specs=ANY,
-        input_output_aliases={0: 0},
-        compiler_params=params(0),
-        cost_estimate=pl.CostEstimate(flops=0, bytes_accessed=0, transcendentals=0),
-        name="tie",
-    )(value, after)
 
 
 def request_kernel(tiles_here, row_size, ids_ref, me_ref, out_ref):
@@ -408,7 +391,7 @@
 
     asked_of = request(tile_ids, me, tiles_here, row_size)
     asked_by = swap(asked_of)
-    heads_first = tie(jnp.transpose(tile_kv, (0, 2, 1, 3)), asked_of)
+    heads_first = jnp.transpose(tile_kv, (0, 2, 1, 3))
     mirrored = lax.ppermute(heads_first, "rows", turn(row_size, half))
 
     cells = [fact_cells]
@@ -438,7 +421,7 @@
     far = spread(mirrored, 1, far_order[:-1] if paired else far_order, near[1:3])
     sums, tops = first_tiles(asked, near, near_slots, rows * cols, far[1:2])
     far += spread(mirrored, 1, far_order[-1:] if paired else [], [tops])
-    batch = len(far) // 2
+    batch = (len(far) + 2) // 2 if paired else 0
     if batch:
         sums, tops = more_tiles(asked, sums, tops, far[:batch], far_slots[:batch], rows * cols)
     far, far_slots = far[batch:], far_slots[batch:]

time: 61.4 us -> 59.5 us (0.969)
  waiting for transfers between devices: 18 us -> 16.8 us
  starting transfers between devices: 23.2 us -> 22.3 us
    ppermute x1, waiting for transfers between devices: 1.06 us -> 0.01 us  [shards(): cells.append(lax.ppermute(fact_cells, 'cols', turn(col_size, -step)))]
    ppermute x14, starting transfers between devices: 12.3 us -> 11.3 us  [spread(): lax.ppermute(tile, 'rows', [(row, row ^ step) for row in range(row_size)])]
    ppermute x1, waiting for transfers between devices: 2.53 us -> 1.67 us  [shards(): mirrored = lax.ppermute(heads_first, 'rows', turn(row_size, half))]
    ppermute x14, waiting for transfers between devices: 13.3 us -> 14 us  [spread(): lax.ppermute(tile, 'rows', [(row, row ^ step) for row in range(row_size)])]
    unnamed x7 -> x5, local copies, waits for them, and re-layouts: 1.84 us -> 1.8 us
  transfers between devices with their start and end apart: 18 -> 18, of which waited for: 11 -> 10; matrix products, arithmetic and copies ran while one was open for 0% -> 0% of each run, Pallas kernels for 23% -> 27%
where the time goes in v20:
time: 59.5 us; the launch traced here: 59.2 us
  starting transfers between devices  22.3 us (37%)
  Pallas kernels  17.1 us (29%)
  waiting for transfers between devices  16.8 us (28%)
  local copies, waits for them, and re-layouts  2.52 us (4%)
    ppermute x14, waiting for transfers between devices, spread(): lax.ppermute(tile, 'rows', [(row, row ^ step) for row in range(row_size)])  14 us
    ppermute x14, starting transfers between devices, spread(): lax.ppermute(tile, 'rows', [(row, row ^ step) for row in range(row_size)])  11.3 us
    pallas_call x1, Pallas kernels, front(): pl.pallas_call(functools.partial(front_kernel, groups, heads, head_size,...  5.51 us
    ppermute x1, starting transfers between devices, shards(): mirrored = lax.ppermute(heads_first, 'rows', turn(row_size, half))  4.1 us
    all_to_all x1, starting transfers between devices, swap(): lax.all_to_all(value, 'rows', split_axis=0, concat_axis=0, tiled=True, ax...  3.78 us
    pallas_call x2, Pallas kernels, last_tiles(): pl.pallas_call(functools.partial(last_kernel, slots, groups), out_shape=(...  2.78 us
    pallas_call x1, Pallas kernels, first_tiles(): pl.pallas_call(functools.partial(first_kernel, slots, rows if rows <= 512...  2.37 us
    pallas_call x1, Pallas kernels, more_tiles(): pl.pallas_call(functools.partial(more_kernel, slots, rows if rows <= 512...  2.29 us
  transfers between devices with their start and end apart: 18, of which 10 were waited for; matrix products, arithmetic and copies ran while one was open for 0% of the time, Pallas kernels for 27%

profile of v20, /device:TPU:0, one launch (start us, length us, event | category | flops | bytes accessed | tf_op | source)
XLA Modules:
  0.0 59.2 jit_solution(4234655592738396921)
XLA Ops:
  0.0 1.1 %copy.13 = bf16[4,128,4,128]{3,1,2,0:T(8,128)(2,1)S(1)} copy(bf16[4,128,4,128]{3,2,1,0:T(4,128)(2,1)} %param.17) | data formatting | bytes 1048576 | tf_op args[7]
  1.1 4.1 %collective-permute-start.8 = (bf16[4,4,128,128]{3,2,1,0:T(8,128)(2,1)S(1)}, bf16[4,4,128,128]{3,2,1,0:T(8,128)(2,1)S(1)}, u32[]{:S(2)}, u32[]{:S(2)}) collective-permute-start(bf16[4,4,128,128]{3,2,1,0:T(8,128)(2,1)S(1)} %bitcast.10), channel_id=1, source_target_pairs={{0,16},{2,18},{4,20},{6,22},{8,24},{10,26},{12,28},{14,30},{16,0},... | collective-permute-start | bytes 1572872 | tf_op jit(solution)/shard_map/ppermute | solution.py:395
  5.2 1.5 %collective-permute-start = (bf16[48,4,512]{2,1,0:T(4,128)(2,1)}, bf16[48,4,512]{2,1,0:T(4,128)(2,1)S(1)}, u32[]{:S(2)}, u32[]{:S(2)}) collective-permute-start(bf16[48,4,512]{2,1,0:T(4,128)(2,1)} %refs_0_.1), channel_id=1, source_target_pairs={{0,1},{1,0},{2,3},{3,2},{4,5},{5,4},{6,7},{7,6},{8,9},{9,8},{10,11... | collective-permute-start | bytes 589832 | tf_op jit(solution)/shard_map/ppermute | solution.py:399
  7.5 1.2 %request.1 = s32[8,2,128]{2,1,0:T(2,128)} custom-call(s32[1,12]{1,0:T(1,128)S(1)} %copy-done.1, s32[2]{0:T(128)S(1)} %pad_add_fusion.refs_2_.me_ref), custom_call_target="tpu_custom_call" | custom-call | bytes 262144 | tf_op jit(solution)/shard_map/request/pallas_call | solution.py:59
  8.7 3.8 %all-to-all-start = ((s32[8,2,128]{2,1,0:T(2,128)}), s32[8,2,128]{2,1,0:T(2,128)S(1)}, u32[]{:S(2)}, u32[]{:S(2)}) async-start(s32[8,2,128]{2,1,0:T(2,128)} %request.1), calls=%async_computation | async-start | bytes 16384 | tf_op jit(solution)/shard_map/all_to_all | solution.py:390
  12.5 5.5 %front.1 = (f32[192,512]{1,0:T(8,128)S(1)}, bf16[4,384,128]{2,1,0:T(8,128)(2,1)S(1)}) custom-call(bf16[48,4,512]{2,1,0:T(4,128)(2,1)} %refs_0_.1, bf16[48,4,512]{2,1,0:T(4,128)(2,1)S(1)} %collective-permute-done.refs_1_, s32[2]{0:T(128)S(1)} %pad_add_fusion.refs_2_.me_ref, s32[1,12]{1,0:T(1,128)} %ids_ref.1, s32[12,48]{1,0:T(8,128)} %bitcast.12, ...), custom_call_target="tpu_custom_call" | custom-call | flops 1006632960 | bytes 4194304 | tf_op jit(solution)/shard_map/front/pallas_call | solution.py:218
  19.4 1.7 %collective-permute-start.2 = (bf16[1,4,128,128]{3,2,1,0:T(8,128)(2,1)S(1)}, bf16[1,4,128,128]{3,2,1,0:T(8,128)(2,1)S(1)}, u32[]{:S(2)}, u32[]{:S(2)}) collective-permute-start(bf16[1,4,128,128]{3,2,1,0:T(8,128)(2,1)S(1)} %get-tuple-element.32), channel_id=1, source_target_pairs={{0,4},{2,6},{4,0},{6,2},{8,12},{10,14},{12,8},{14,10},{16,20},{18,... | collective-permute-start | bytes 393224 | tf_op jit(solution)/shard_map/ppermute | solution.py:413
  21.0 1.5 %collective-permute-start.3 = (bf16[1,4,128,128]{3,2,1,0:T(8,128)(2,1)S(1)}, bf16[1,4,128,128]{3,2,1,0:T(8,128)(2,1)S(1)}, u32[]{:S(2)}, u32[]{:S(2)}) collective-permute-start(bf16[1,4,128,128]{3,2,1,0:T(8,128)(2,1)S(1)} %get-tuple-element.33), channel_id=1, source_target_pairs={{0,8},{2,10},{4,12},{6,14},{8,0},{10,2},{12,4},{14,6},{16,24},{18,... | collective-permute-start | bytes 393224 | tf_op jit(solution)/shard_map/ppermute | solution.py:413
  23.6 1.4 %collective-permute-done.2.refs_1_.refs_2_ = bf16[1,4,128,128]{3,2,1,0:T(8,128)(2,1)S(1)} collective-permute-done((bf16[1,4,128,128]{3,2,1,0:T(8,128)(2,1)S(1)}, bf16[1,4,128,128]{3,2,1,0:T(8,128)(2,1)S(1)}, u32[]{:S(2)}, u32[]{:S(2)}) %collective-permute-start.2) | collective-permute-done | bytes 131104 | tf_op jit(solution)/shard_map/ppermute | solution.py:413
  25.0 1.8 %collective-permute-start.6 = (bf16[1,4,128,128]{3,2,1,0:T(8,128)(2,1)S(1)}, bf16[1,4,128,128]{3,2,1,0:T(8,128)(2,1)S(1)}, u32[]{:S(2)}, u32[]{:S(2)}) collective-permute-start(bf16[1,4,128,128]{3,2,1,0:T(8,128)(2,1)S(1)} %get-tuple-element.36), channel_id=1, source_target_pairs={{0,14},{2,12},{4,10},{6,8},{8,6},{10,4},{12,2},{14,0},{16,30},{18,... | collective-permute-start | bytes 393224 | tf_op jit(solution)/shard_map/ppermute | solution.py:413
  26.8 1.7 %collective-permute-done.8.tiles_ref = bf16[4,4,128,128]{3,2,1,0:T(8,128)(2,1)S(1)} collective-permute-done((bf16[4,4,128,128]{3,2,1,0:T(8,128)(2,1)S(1)}, bf16[4,4,128,128]{3,2,1,0:T(8,128)(2,1)S(1)}, u32[]{:S(2)}, u32[]{:S(2)}) %collective-permute-start.8) | collective-permute-done | bytes 524320 | tf_op jit(solution)/shard_map/ppermute | solution.py:395
  29.3 2.0 %collective-permute-done.3.refs_3_ = bf16[1,4,128,128]{3,2,1,0:T(8,128)(2,1)S(1)} collective-permute-done((bf16[1,4,128,128]{3,2,1,0:T(8,128)(2,1)S(1)}, bf16[1,4,128,128]{3,2,1,0:T(8,128)(2,1)S(1)}, u32[]{:S(2)}, u32[]{:S(2)}) %collective-permute-start.3) | collective-permute-done | bytes 131104 | tf_op jit(solution)/shard_map/ppermute | solution.py:413
  31.3 3.8 %collective-permute-done.4.refs_4_ = bf16[1,4,128,128]{3,2,1,0:T(8,128)(2,1)S(1)} collective-permute-done((bf16[1,4,128,128]{3,2,1,0:T(8,128)(2,1)S(1)}, bf16[1,4,128,128]{3,2,1,0:T(8,128)(2,1)S(1)}, u32[]{:S(2)}, u32[]{:S(2)}) %collective-permute-start.4) | collective-permute-done | bytes 131104 | tf_op jit(solution)/shard_map/ppermute | solution.py:413
  35.6 1.2 %collective-permute-done.5.refs_5_ = bf16[1,4,128,128]{3,2,1,0:T(8,128)(2,1)S(1)} collective-permute-done((bf16[1,4,128,128]{3,2,1,0:T(8,128)(2,1)S(1)}, bf16[1,4,128,128]{3,2,1,0:T(8,128)(2,1)S(1)}, u32[]{:S(2)}, u32[]{:S(2)}) %collective-permute-start.5) | collective-permute-done | bytes 131104 | tf_op jit(solution)/shard_map/ppermute | solution.py:413
  37.5 3.2 %collective-permute-done.6.refs_6_ = bf16[1,4,128,128]{3,2,1,0:T(8,128)(2,1)S(1)} collective-permute-done((bf16[1,4,128,128]{3,2,1,0:T(8,128)(2,1)S(1)}, bf16[1,4,128,128]{3,2,1,0:T(8,128)(2,1)S(1)}, u32[]{:S(2)}, u32[]{:S(2)}) %collective-permute-start.6) | collective-permute-done | bytes 131104 | tf_op jit(solution)/shard_map/ppermute | solution.py:413
  40.7 1.7 %collective-permute-start.13 = (bf16[1,4,128,128]{3,2,1,0:T(8,128)(2,1)S(1)}, bf16[1,4,128,128]{3,2,1,0:T(8,128)(2,1)S(1)}, u32[]{:S(2)}, u32[]{:S(2)}) collective-permute-start(bf16[1,4,128,128]{3,2,1,0:T(8,128)(2,1)S(1)} %get-tuple-element.47), channel_id=1, source_target_pairs={{0,10},{2,8},{4,14},{6,12},{8,2},{10,0},{12,6},{14,4},{16,26},{18,... | collective-permute-start | bytes 393224 | tf_op jit(solution)/shard_map/ppermute | solution.py:413
  42.6 1.1 %collective-permute-start.14 = (bf16[1,4,128,128]{3,2,1,0:T(8,128)(2,1)S(1)}, bf16[1,4,128,128]{3,2,1,0:T(8,128)(2,1)S(1)}, u32[]{:S(2)}, u32[]{:S(2)}) collective-permute-start(bf16[1,4,128,128]{3,2,1,0:T(8,128)(2,1)S(1)} %get-tuple-element.48), channel_id=1, source_target_pairs={{0,6},{2,4},{4,2},{6,0},{8,14},{10,12},{12,10},{14,8},{16,22},{18,... | collective-permute-start | bytes 393224 | tf_op jit(solution)/shard_map/ppermute | solution.py:413
  43.7 2.4 %first_tiles.1 = (f32[4,384,128]{2,1,0:T(8,128)S(1)}, f32[384,128]{1,0:T(8,128)S(1)}) custom-call(bf16[4,384,128]{2,1,0:T(8,128)(2,1)S(1)} %get-tuple-element.29.refs_0_.asked_ref, bf16[1,4,128,128]{3,2,1,0:T(8,128)(2,1)S(1)} %get-tuple-element.30.refs_0_, bf16[1,4,128,128]{3,2,1,0:T(8,128)(2,1)S(1)} %collective-permute-done.1.refs_0_.refs_1_, ...), custom_call_target="tpu_custom_call" | custom-call | flops 805306368 | bytes 4194304 | tf_op jit(solution)/shard_map/first_tiles/pallas_call | solution.py:268
  47.5 1.7 %collective-permute-done.12.refs_4_ = bf16[1,4,128,128]{3,2,1,0:T(8,128)(2,1)S(1)} collective-permute-done((bf16[1,4,128,128]{3,2,1,0:T(8,128)(2,1)S(1)}, bf16[1,4,128,128]{3,2,1,0:T(8,128)(2,1)S(1)}, u32[]{:S(2)}, u32[]{:S(2)}) %collective-permute-start.12) | collective-permute-done | bytes 131104 | tf_op jit(solution)/shard_map/ppermute | solution.py:413
  49.1 2.3 %more_tiles.1 = (f32[4,384,128]{2,1,0:T(8,128)S(1)}, f32[384,128]{1,0:T(8,128)S(1)}) custom-call(bf16[4,384,128]{2,1,0:T(8,128)(2,1)S(1)} %get-tuple-element.29.refs_0_.asked_ref, f32[4,384,128]{2,1,0:T(8,128)S(1)} %get-tuple-element.39.old_sums_ref, f32[384,128]{1,0:T(8,128)S(1)} %get-tuple-element.40.old_tops_ref.refs_0_, ...), custom_call_target="tpu_custom_call" | custom-call | flops 503316480 | bytes 4194304 | tf_op jit(solution)/shard_map/more_tiles/pallas_call | solution.py:301
  51.9 1.4 %last_tiles.2.refs_3_ = bf16[192,256]{1,0:T(8,128)(2,1)S(1)} custom-call(bf16[4,384,128]{2,1,0:T(8,128)(2,1)S(1)} %get-tuple-element.29.refs_0_.asked_ref, f32[4,384,128]{2,1,0:T(8,128)S(1)} %get-tuple-element.45.sums_ref, f32[384,128]{1,0:T(8,128)S(1)} %get-tuple-element.46.tops_ref, bf16[1,4,128,128]{3,2,1,0:T(8,128)(2,1)S(1)} %collective-permute-done.13.refs_0_, ...), custom_call_target="tpu_custom_call" | custom-call | flops 150994944 | bytes 4194304 | tf_op jit(solution)/shard_map/last_tiles/pallas_call | solution.py:335
  53.3 1.6 %collective-permute-start.16 = (bf16[192,256]{1,0:T(8,128)(2,1)S(1)}, bf16[192,256]{1,0:T(8,128)(2,1)S(1)}, u32[]{:S(2)}, u32[]{:S(2)}) collective-permute-start(bf16[192,256]{1,0:T(8,128)(2,1)S(1)} %last_tiles.2.refs_3_), channel_id=1, source_target_pairs={{0,1},{1,0},{2,3},{3,2},{4,5},{5,4},{6,7},{7,6},{8,9},{9,8},{10,11... | collective-permute-start | bytes 294920 | tf_op jit(solution)/shard_map/ppermute | solution.py:432
  54.9 1.4 %last_tiles.3.answer_ref = bf16[192,256]{1,0:T(8,128)(2,1)S(1)} custom-call(bf16[4,384,128]{2,1,0:T(8,128)(2,1)S(1)} %get-tuple-element.29.refs_0_.asked_ref, f32[4,384,128]{2,1,0:T(8,128)S(1)} %get-tuple-element.45.sums_ref, f32[384,128]{1,0:T(8,128)S(1)} %get-tuple-element.46.tops_ref, bf16[1,4,128,128]{3,2,1,0:T(8,128)(2,1)S(1)} %collective-permute-done.13.refs_0_, ...), custom_call_target="tpu_custom_call" | custom-call | flops 150994944 | bytes 4194304 | tf_op jit(solution)/shard_map/last_tiles/pallas_call | solution.py:335
  57.1 1.1 %collective-permute-done.16 = bf16[192,256]{1,0:T(8,128)(2,1)S(1)} collective-permute-done((bf16[192,256]{1,0:T(8,128)(2,1)S(1)}, bf16[192,256]{1,0:T(8,128)(2,1)S(1)}, u32[]{:S(2)}, u32[]{:S(2)}) %collective-permute-start.16) | collective-permute-done | bytes 98336 | tf_op jit(solution)/shard_map/ppermute | solution.py:432
  (31 shorter events, 9.0 us)
Async XLA Ops:
  1.1 27.4 %collective-permute-start.8 = (bf16[4,4,128,128]{3,2,1,0:T(8,128)(2,1)S(1)}, bf16[4,4,128,128]{3,2,1,0:T(8,128)(2,1)S(1)}, u32[]{:S(2)}, u32[]{:S(2)}) collective-permute-start(bf16[4,4,128,128]{3,2,1,0:T(8,128)(2,1)S(1)} %bitcast.10), channel_id=1, source_target_pairs={{0,16},{2,18},{4,20},{6,22},{8,24},{10,26},{12,28},{14,30},{16,0},... | collective-permute-start | bytes 1572872 | tf_op jit(solution)/shard_map/ppermute | solution.py:395
  5.2 7.3 %collective-permute-start = (bf16[48,4,512]{2,1,0:T(4,128)(2,1)}, bf16[48,4,512]{2,1,0:T(4,128)(2,1)S(1)}, u32[]{:S(2)}, u32[]{:S(2)}) collective-permute-start(bf16[48,4,512]{2,1,0:T(4,128)(2,1)} %refs_0_.1), channel_id=1, source_target_pairs={{0,1},{1,0},{2,3},{3,2},{4,5},{5,4},{6,7},{7,6},{8,9},{9,8},{10,11... | collective-permute-start | bytes 589832 | tf_op jit(solution)/shard_map/ppermute | solution.py:399
  6.8 0.7 %copy-start.1 = (s32[1,12]{1,0:T(1,128)S(1)}, s32[1,12]{1,0:T(1,128)}, u32[]{:S(2)}) copy-start(s32[1,12]{1,0:T(1,128)} %ids_ref.1) | copy-start | bytes 148
  8.7 9.3 %all-to-all-start = ((s32[8,2,128]{2,1,0:T(2,128)}), s32[8,2,128]{2,1,0:T(2,128)S(1)}, u32[]{:S(2)}, u32[]{:S(2)}) async-start(s32[8,2,128]{2,1,0:T(2,128)} %request.1), calls=%async_computation | async-start | bytes 16384 | tf_op jit(solution)/shard_map/all_to_all | solution.py:390
  18.8 4.1 %collective-permute-start.1 = (bf16[1,4,128,128]{3,2,1,0:T(8,128)(2,1)S(1)}, bf16[1,4,128,128]{3,2,1,0:T(8,128)(2,1)S(1)}, u32[]{:S(2)}, u32[]{:S(2)}) collective-permute-start(bf16[1,4,128,128]{3,2,1,0:T(8,128)(2,1)S(1)} %get-tuple-element.31), channel_id=1, source_target_pairs={{0,2},{2,0},{4,6},{6,4},{8,10},{10,8},{12,14},{14,12},{16,18},{18,... | collective-permute-start | bytes 393224 | tf_op jit(solution)/shard_map/ppermute | solution.py:413
  19.4 5.7 %collective-permute-start.2 = (bf16[1,4,128,128]{3,2,1,0:T(8,128)(2,1)S(1)}, bf16[1,4,128,128]{3,2,1,0:T(8,128)(2,1)S(1)}, u32[]{:S(2)}, u32[]{:S(2)}) collective-permute-start(bf16[1,4,128,128]{3,2,1,0:T(8,128)(2,1)S(1)} %get-tuple-element.32), channel_id=1, source_target_pairs={{0,4},{2,6},{4,0},{6,2},{8,12},{10,14},{12,8},{14,10},{16,20},{18,... | collective-permute-start | bytes 393224 | tf_op jit(solution)/shard_map/ppermute | solution.py:413
  21.0 10.3 %collective-permute-start.3 = (bf16[1,4,128,128]{3,2,1,0:T(8,128)(2,1)S(1)}, bf16[1,4,128,128]{3,2,1,0:T(8,128)(2,1)S(1)}, u32[]{:S(2)}, u32[]{:S(2)}) collective-permute-start(bf16[1,4,128,128]{3,2,1,0:T(8,128)(2,1)S(1)} %get-tuple-element.33), channel_id=1, source_target_pairs={{0,8},{2,10},{4,12},{6,14},{8,0},{10,2},{12,4},{14,6},{16,24},{18,... | collective-permute-start | bytes 393224 | tf_op jit(solution)/shard_map/ppermute | solution.py:413
  22.5 12.6 %collective-permute-start.4 = (bf16[1,4,128,128]{3,2,1,0:T(8,128)(2,1)S(1)}, bf16[1,4,128,128]{3,2,1,0:T(8,128)(2,1)S(1)}, u32[]{:S(2)}, u32[]{:S(2)}) collective-permute-start(bf16[1,4,128,128]{3,2,1,0:T(8,128)(2,1)S(1)} %get-tuple-element.34), channel_id=1, source_target_pairs={{0,12},{2,14},{4,8},{6,10},{8,4},{10,6},{12,0},{14,2},{16,28},{18,... | collective-permute-start | bytes 393224 | tf_op jit(solution)/shard_map/ppermute | solution.py:413
  22.9 13.9 %collective-permute-start.5 = (bf16[1,4,128,128]{3,2,1,0:T(8,128)(2,1)S(1)}, bf16[1,4,128,128]{3,2,1,0:T(8,128)(2,1)S(1)}, u32[]{:S(2)}, u32[]{:S(2)}) collective-permute-start(bf16[1,4,128,128]{3,2,1,0:T(8,128)(2,1)S(1)} %get-tuple-element.35), channel_id=1, source_target_pairs={{0,10},{2,8},{4,14},{6,12},{8,2},{10,0},{12,6},{14,4},{16,26},{18,... | collective-permute-start | bytes 393224 | tf_op jit(solution)/shard_map/ppermute | solution.py:413
  25.0 15.6 %collective-permute-start.6 = (bf16[1,4,128,128]{3,2,1,0:T(8,128)(2,1)S(1)}, bf16[1,4,128,128]{3,2,1,0:T(8,128)(2,1)S(1)}, u32[]{:S(2)}, u32[]{:S(2)}) collective-permute-start(bf16[1,4,128,128]{3,2,1,0:T(8,128)(2,1)S(1)} %get-tuple-element.36), channel_id=1, source_target_pairs={{0,14},{2,12},{4,10},{6,8},{8,6},{10,4},{12,2},{14,0},{16,30},{18,... | collective-permute-start | bytes 393224 | tf_op jit(solution)/shard_map/ppermute | solution.py:413
  28.5 12.2 %collective-permute-start.7 = (bf16[1,4,128,128]{3,2,1,0:T(8,128)(2,1)S(1)}, bf16[1,4,128,128]{3,2,1,0:T(8,128)(2,1)S(1)}, u32[]{:S(2)}, u32[]{:S(2)}) collective-permute-start(bf16[1,4,128,128]{3,2,1,0:T(8,128)(2,1)S(1)} %get-tuple-element.37), channel_id=1, source_target_pairs={{0,6},{2,4},{4,2},{6,0},{8,14},{10,12},{12,10},{14,8},{16,22},{18,... | collective-permute-start | bytes 393224 | tf_op jit(solution)/shard_map/ppermute | solution.py:413
  31.3 11.3 %collective-permute-start.9 = (bf16[1,4,128,128]{3,2,1,0:T(8,128)(2,1)S(1)}, bf16[1,4,128,128]{3,2,1,0:T(8,128)(2,1)S(1)}, u32[]{:S(2)}, u32[]{:S(2)}) collective-permute-start(bf16[1,4,128,128]{3,2,1,0:T(8,128)(2,1)S(1)} %get-tuple-element.38), channel_id=1, source_target_pairs={{0,8},{2,10},{4,12},{6,14},{8,0},{10,2},{12,4},{14,6},{16,24},{18,... | collective-permute-start | bytes 393224 | tf_op jit(solution)/shard_map/ppermute | solution.py:413
  35.1 11.7 %collective-permute-start.10 = (bf16[1,4,128,128]{3,2,1,0:T(8,128)(2,1)S(1)}, bf16[1,4,128,128]{3,2,1,0:T(8,128)(2,1)S(1)}, u32[]{:S(2)}, u32[]{:S(2)}) collective-permute-start(bf16[1,4,128,128]{3,2,1,0:T(8,128)(2,1)S(1)} %get-tuple-element.42), channel_id=1, source_target_pairs={{0,4},{2,6},{4,0},{6,2},{8,12},{10,14},{12,8},{14,10},{16,20},{18,... | collective-permute-start | bytes 393224 | tf_op jit(solution)/shard_map/ppermute | solution.py:413
  36.8 10.7 %collective-permute-start.11 = (bf16[1,4,128,128]{3,2,1,0:T(8,128)(2,1)S(1)}, bf16[1,4,128,128]{3,2,1,0:T(8,128)(2,1)S(1)}, u32[]{:S(2)}, u32[]{:S(2)}) collective-permute-start(bf16[1,4,128,128]{3,2,1,0:T(8,128)(2,1)S(1)} %get-tuple-element.43), channel_id=1, source_target_pairs={{0,12},{2,14},{4,8},{6,10},{8,4},{10,6},{12,0},{14,2},{16,28},{18,... | collective-permute-start | bytes 393224 | tf_op jit(solution)/shard_map/ppermute | solution.py:413
  40.7 8.5 %collective-permute-start.12 = (bf16[1,4,128,128]{3,2,1,0:T(8,128)(2,1)S(1)}, bf16[1,4,128,128]{3,2,1,0:T(8,128)(2,1)S(1)}, u32[]{:S(2)}, u32[]{:S(2)}) collective-permute-start(bf16[1,4,128,128]{3,2,1,0:T(8,128)(2,1)S(1)} %get-tuple-element.44), channel_id=1, source_target_pairs={{0,14},{2,12},{4,10},{6,8},{8,6},{10,4},{12,2},{14,0},{16,30},{18,... | collective-permute-start | bytes 393224 | tf_op jit(solution)/shard_map/ppermute | solution.py:413
  40.7 10.8 %collective-permute-start.13 = (bf16[1,4,128,128]{3,2,1,0:T(8,128)(2,1)S(1)}, bf16[1,4,128,128]{3,2,1,0:T(8,128)(2,1)S(1)}, u32[]{:S(2)}, u32[]{:S(2)}) collective-permute-start(bf16[1,4,128,128]{3,2,1,0:T(8,128)(2,1)S(1)} %get-tuple-element.47), channel_id=1, source_target_pairs={{0,10},{2,8},{4,14},{6,12},{8,2},{10,0},{12,6},{14,4},{16,26},{18,... | collective-permute-start | bytes 393224 | tf_op jit(solution)/shard_map/ppermute | solution.py:413
  42.6 9.3 %collective-permute-start.14 = (bf16[1,4,128,128]{3,2,1,0:T(8,128)(2,1)S(1)}, bf16[1,4,128,128]{3,2,1,0:T(8,128)(2,1)S(1)}, u32[]{:S(2)}, u32[]{:S(2)}) collective-permute-start(bf16[1,4,128,128]{3,2,1,0:T(8,128)(2,1)S(1)} %get-tuple-element.48), channel_id=1, source_target_pairs={{0,6},{2,4},{4,2},{6,0},{8,14},{10,12},{12,10},{14,8},{16,22},{18,... | collective-permute-start | bytes 393224 | tf_op jit(solution)/shard_map/ppermute | solution.py:413
  46.8 5.1 %collective-permute-start.15 = (bf16[1,4,128,128]{3,2,1,0:T(8,128)(2,1)S(1)}, bf16[1,4,128,128]{3,2,1,0:T(8,128)(2,1)S(1)}, u32[]{:S(2)}, u32[]{:S(2)}) collective-permute-start(bf16[1,4,128,128]{3,2,1,0:T(8,128)(2,1)S(1)} %pick_each.5), channel_id=1, source_target_pairs={{0,2},{2,0},{4,6},{6,4},{8,10},{10,8},{12,14},{14,12},{16,18},{18,... | collective-permute-start | bytes 393224 | tf_op jit(solution)/shard_map/ppermute | solution.py:413
  51.9 4.4 %copy-start = (bf16[512,512]{1,0:T(8,128)(2,1)S(1)}, bf16[512,512]{1,0:T(8,128)(2,1)}, u32[]{:S(2)}) copy-start(bf16[512,512]{1,0:T(8,128)(2,1)} %weight_ref.1) | copy-start | bytes 1572868
  53.3 4.9 %collective-permute-start.16 = (bf16[192,256]{1,0:T(8,128)(2,1)S(1)}, bf16[192,256]{1,0:T(8,128)(2,1)S(1)}, u32[]{:S(2)}, u32[]{:S(2)}) collective-permute-start(bf16[192,256]{1,0:T(8,128)(2,1)S(1)} %last_tiles.2.refs_3_), channel_id=1, source_target_pairs={{0,1},{1,0},{2,3},{3,2},{4,5},{5,4},{6,7},{7,6},{8,9},{9,8},{10,11... | collective-permute-start | bytes 294920 | tf_op jit(solution)/shard_map/ppermute | solution.py:432

commit v21 on v20

--- a/solution.py
+++ b/solution.py
@@ -399,9 +399,12 @@
         cells.append(lax.ppermute(fact_cells, "cols", turn(col_size, -step)))
 
     across = half // 2
-    near_order = [0, 1] + sorted(range(2, half), key=lambda step: (step != 2, not step & across, step & 1, step))
-    rest = sorted(set(range(2, half)) - {across}, key=lambda step: (step != 2, not step & across, step & 1, -step))
-    far_order = list(dict.fromkeys([0, across] + rest + [1]))
+
+    def turns(step):
+        return bool(step & across) and bool(step & (across - 1) & ~1)
+
+    near_order = [0, 1] + sorted(range(2, half), key=lambda step: (turns(step), step != 2, not step & across, step))
+    far_order = [0] + sorted(range(2, half), key=lambda step: (turns(step), step & 1, not step & across, step)) + [1]
     near_slots, far_slots = (near_order, [half + step for step in far_order]) if paired else ([0], [half])
 
     def spread(tiles, which, order, after):
@@ -421,7 +424,7 @@
     far = spread(mirrored, 1, far_order[:-1] if paired else far_order, near[1:3])
     sums, tops = first_tiles(asked, near, near_slots, rows * cols, far[1:2])
     far += spread(mirrored, 1, far_order[-1:] if paired else [], [tops])
-    batch = (len(far) + 2) // 2 if paired else 0
+    batch = len(far) // 2
     if batch:
         sums, tops = more_tiles(asked, sums, tops, far[:batch], far_slots[:batch], rows * cols)
     far, far_slots = far[batch:], far_slots[batch:]

time: 59.5 us -> 59.4 us (level)
    ppermute x1, waiting for transfers between devices: 1.67 us -> 0.25 us  [shards(): mirrored = lax.ppermute(heads_first, 'rows', turn(row_size, half))]
    ppermute x14, waiting for transfers between devices: 14 us -> 15.4 us  [spread(): lax.ppermute(tile, 'rows', [(row, row ^ step) for row in range(row_size)])]
  transfers between devices with their start and end apart: 18 -> 18, of which waited for: 10 -> 10; matrix products, arithmetic and copies ran while one was open for 0% -> 0% of each run, Pallas kernels for 27% -> 26%
where the time goes in v21:
time: 59.4 us; the launch traced here: 59.1 us
  starting transfers between devices  22.5 us (38%)
  Pallas kernels  17 us (29%)
  waiting for transfers between devices  16.7 us (28%)
  local copies, waits for them, and re-layouts  2.52 us (4%)
    ppermute x14, waiting for transfers between devices, spread(): lax.ppermute(tile, 'rows', [(row, row ^ step) for row in range(row_size)])  15.4 us
    ppermute x14, starting transfers between devices, spread(): lax.ppermute(tile, 'rows', [(row, row ^ step) for row in range(row_size)])  11.5 us
    pallas_call x1, Pallas kernels, front(): pl.pallas_call(functools.partial(front_kernel, groups, heads, head_size,...  5.51 us
    ppermute x1, starting transfers between devices, shards(): mirrored = lax.ppermute(heads_first, 'rows', turn(row_size, half))  4.1 us
    all_to_all x1, starting transfers between devices, swap(): lax.all_to_all(value, 'rows', split_axis=0, concat_axis=0, tiled=True, ax...  3.78 us
    pallas_call x2, Pallas kernels, last_tiles(): pl.pallas_call(functools.partial(last_kernel, slots, groups), out_shape=(...  2.87 us
    pallas_call x1, Pallas kernels, first_tiles(): pl.pallas_call(functools.partial(first_kernel, slots, rows if rows <= 512...  2.4 us
    pallas_call x3, Pallas kernels, pick_each(): pl.pallas_call(functools.partial(pick_each_kernel, which, order), out_sha...  2.19 us
  transfers between devices with their start and end apart: 18, of which 10 were waited for; matrix products, arithmetic and copies ran while one was open for 0% of the time, Pallas kernels for 26%

profile of v21, /device:TPU:0, one launch (start us, length us, event | category | flops | bytes accessed | tf_op | source)
XLA Modules:
  0.0 59.1 jit_solution(11169592745282891547)
XLA Ops:
  0.0 1.1 %copy.13 = bf16[4,128,4,128]{3,1,2,0:T(8,128)(2,1)S(1)} copy(bf16[4,128,4,128]{3,2,1,0:T(4,128)(2,1)} %param.17) | data formatting | bytes 1048576 | tf_op args[7]
  1.1 4.1 %collective-permute-start.8 = (bf16[4,4,128,128]{3,2,1,0:T(8,128)(2,1)S(1)}, bf16[4,4,128,128]{3,2,1,0:T(8,128)(2,1)S(1)}, u32[]{:S(2)}, u32[]{:S(2)}) collective-permute-start(bf16[4,4,128,128]{3,2,1,0:T(8,128)(2,1)S(1)} %bitcast.10), channel_id=1, source_target_pairs={{0,16},{2,18},{4,20},{6,22},{8,24},{10,26},{12,28},{14,30},{16,0},... | collective-permute-start | bytes 1572872 | tf_op jit(solution)/shard_map/ppermute | solution.py:395
  5.2 1.5 %collective-permute-start = (bf16[48,4,512]{2,1,0:T(4,128)(2,1)}, bf16[48,4,512]{2,1,0:T(4,128)(2,1)S(1)}, u32[]{:S(2)}, u32[]{:S(2)}) collective-permute-start(bf16[48,4,512]{2,1,0:T(4,128)(2,1)} %refs_0_.1), channel_id=1, source_target_pairs={{0,1},{1,0},{2,3},{3,2},{4,5},{5,4},{6,7},{7,6},{8,9},{9,8},{10,11... | collective-permute-start | bytes 589832 | tf_op jit(solution)/shard_map/ppermute | solution.py:399
  7.5 1.2 %request.1 = s32[8,2,128]{2,1,0:T(2,128)} custom-call(s32[1,12]{1,0:T(1,128)S(1)} %copy-done.1, s32[2]{0:T(128)S(1)} %pad_add_fusion.refs_2_.me_ref), custom_call_target="tpu_custom_call" | custom-call | bytes 262144 | tf_op jit(solution)/shard_map/request/pallas_call | solution.py:59
  8.7 3.8 %all-to-all-start = ((s32[8,2,128]{2,1,0:T(2,128)}), s32[8,2,128]{2,1,0:T(2,128)S(1)}, u32[]{:S(2)}, u32[]{:S(2)}) async-start(s32[8,2,128]{2,1,0:T(2,128)} %request.1), calls=%async_computation | async-start | bytes 16384 | tf_op jit(solution)/shard_map/all_to_all | solution.py:390
  12.5 5.5 %front.1 = (f32[192,512]{1,0:T(8,128)S(1)}, bf16[4,384,128]{2,1,0:T(8,128)(2,1)S(1)}) custom-call(bf16[48,4,512]{2,1,0:T(4,128)(2,1)} %refs_0_.1, bf16[48,4,512]{2,1,0:T(4,128)(2,1)S(1)} %collective-permute-done.refs_1_, s32[2]{0:T(128)S(1)} %pad_add_fusion.refs_2_.me_ref, s32[1,12]{1,0:T(1,128)} %ids_ref.1, s32[12,48]{1,0:T(8,128)} %bitcast.12, ...), custom_call_target="tpu_custom_call" | custom-call | flops 1006632960 | bytes 4194304 | tf_op jit(solution)/shard_map/front/pallas_call | solution.py:218
  19.4 1.7 %collective-permute-start.2 = (bf16[1,4,128,128]{3,2,1,0:T(8,128)(2,1)S(1)}, bf16[1,4,128,128]{3,2,1,0:T(8,128)(2,1)S(1)}, u32[]{:S(2)}, u32[]{:S(2)}) collective-permute-start(bf16[1,4,128,128]{3,2,1,0:T(8,128)(2,1)S(1)} %get-tuple-element.32), channel_id=1, source_target_pairs={{0,4},{2,6},{4,0},{6,2},{8,12},{10,14},{12,8},{14,10},{16,20},{18,... | collective-permute-start | bytes 393224 | tf_op jit(solution)/shard_map/ppermute | solution.py:416
  21.0 1.5 %collective-permute-start.3 = (bf16[1,4,128,128]{3,2,1,0:T(8,128)(2,1)S(1)}, bf16[1,4,128,128]{3,2,1,0:T(8,128)(2,1)S(1)}, u32[]{:S(2)}, u32[]{:S(2)}) collective-permute-start(bf16[1,4,128,128]{3,2,1,0:T(8,128)(2,1)S(1)} %get-tuple-element.33), channel_id=1, source_target_pairs={{0,8},{2,10},{4,12},{6,14},{8,0},{10,2},{12,4},{14,6},{16,24},{18,... | collective-permute-start | bytes 393224 | tf_op jit(solution)/shard_map/ppermute | solution.py:416
  23.1 1.9 %collective-permute-done.2.refs_1_.refs_2_ = bf16[1,4,128,128]{3,2,1,0:T(8,128)(2,1)S(1)} collective-permute-done((bf16[1,4,128,128]{3,2,1,0:T(8,128)(2,1)S(1)}, bf16[1,4,128,128]{3,2,1,0:T(8,128)(2,1)S(1)}, u32[]{:S(2)}, u32[]{:S(2)}) %collective-permute-start.2) | collective-permute-done | bytes 131104 | tf_op jit(solution)/shard_map/ppermute | solution.py:416
  25.0 3.2 %collective-permute-start.6 = (bf16[1,4,128,128]{3,2,1,0:T(8,128)(2,1)S(1)}, bf16[1,4,128,128]{3,2,1,0:T(8,128)(2,1)S(1)}, u32[]{:S(2)}, u32[]{:S(2)}) collective-permute-start(bf16[1,4,128,128]{3,2,1,0:T(8,128)(2,1)S(1)} %get-tuple-element.36), channel_id=1, source_target_pairs={{0,12},{2,14},{4,8},{6,10},{8,4},{10,6},{12,0},{14,2},{16,28},{18,... | collective-permute-start | bytes 393224 | tf_op jit(solution)/shard_map/ppermute | solution.py:416
  28.5 1.2 %collective-permute-start.7 = (bf16[1,4,128,128]{3,2,1,0:T(8,128)(2,1)S(1)}, bf16[1,4,128,128]{3,2,1,0:T(8,128)(2,1)S(1)}, u32[]{:S(2)}, u32[]{:S(2)}) collective-permute-start(bf16[1,4,128,128]{3,2,1,0:T(8,128)(2,1)S(1)} %get-tuple-element.37), channel_id=1, source_target_pairs={{0,14},{2,12},{4,10},{6,8},{8,6},{10,4},{12,2},{14,0},{16,30},{18,... | collective-permute-start | bytes 393224 | tf_op jit(solution)/shard_map/ppermute | solution.py:416
  30.5 0.8 %collective-permute-done.3.refs_3_ = bf16[1,4,128,128]{3,2,1,0:T(8,128)(2,1)S(1)} collective-permute-done((bf16[1,4,128,128]{3,2,1,0:T(8,128)(2,1)S(1)}, bf16[1,4,128,128]{3,2,1,0:T(8,128)(2,1)S(1)}, u32[]{:S(2)}, u32[]{:S(2)}) %collective-permute-start.3) | collective-permute-done | bytes 131104 | tf_op jit(solution)/shard_map/ppermute | solution.py:416
  31.3 2.6 %collective-permute-done.4.refs_4_ = bf16[1,4,128,128]{3,2,1,0:T(8,128)(2,1)S(1)} collective-permute-done((bf16[1,4,128,128]{3,2,1,0:T(8,128)(2,1)S(1)}, bf16[1,4,128,128]{3,2,1,0:T(8,128)(2,1)S(1)}, u32[]{:S(2)}, u32[]{:S(2)}) %collective-permute-start.4) | collective-permute-done | bytes 131104 | tf_op jit(solution)/shard_map/ppermute | solution.py:416
  33.9 1.5 %collective-permute-start.10 = (bf16[1,4,128,128]{3,2,1,0:T(8,128)(2,1)S(1)}, bf16[1,4,128,128]{3,2,1,0:T(8,128)(2,1)S(1)}, u32[]{:S(2)}, u32[]{:S(2)}) collective-permute-start(bf16[1,4,128,128]{3,2,1,0:T(8,128)(2,1)S(1)} %get-tuple-element.42), channel_id=1, source_target_pairs={{0,4},{2,6},{4,0},{6,2},{8,12},{10,14},{12,8},{14,10},{16,20},{18,... | collective-permute-start | bytes 393224 | tf_op jit(solution)/shard_map/ppermute | solution.py:416
  35.5 2.5 %collective-permute-done.6.refs_6_ = bf16[1,4,128,128]{3,2,1,0:T(8,128)(2,1)S(1)} collective-permute-done((bf16[1,4,128,128]{3,2,1,0:T(8,128)(2,1)S(1)}, bf16[1,4,128,128]{3,2,1,0:T(8,128)(2,1)S(1)}, u32[]{:S(2)}, u32[]{:S(2)}) %collective-permute-start.6) | collective-permute-done | bytes 131104 | tf_op jit(solution)/shard_map/ppermute | solution.py:416
  38.0 2.6 %collective-permute-done.7.refs_7_ = bf16[1,4,128,128]{3,2,1,0:T(8,128)(2,1)S(1)} collective-permute-done((bf16[1,4,128,128]{3,2,1,0:T(8,128)(2,1)S(1)}, bf16[1,4,128,128]{3,2,1,0:T(8,128)(2,1)S(1)}, u32[]{:S(2)}, u32[]{:S(2)}) %collective-permute-start.7) | collective-permute-done | bytes 131104 | tf_op jit(solution)/shard_map/ppermute | solution.py:416
  40.6 1.9 %collective-permute-done.9.refs_8_.refs_1_ = bf16[1,4,128,128]{3,2,1,0:T(8,128)(2,1)S(1)} collective-permute-done((bf16[1,4,128,128]{3,2,1,0:T(8,128)(2,1)S(1)}, bf16[1,4,128,128]{3,2,1,0:T(8,128)(2,1)S(1)}, u32[]{:S(2)}, u32[]{:S(2)}) %collective-permute-start.9) | collective-permute-done | bytes 131104 | tf_op jit(solution)/shard_map/ppermute | solution.py:416
  42.9 2.4 %first_tiles.1 = (f32[4,384,128]{2,1,0:T(8,128)S(1)}, f32[384,128]{1,0:T(8,128)S(1)}) custom-call(bf16[4,384,128]{2,1,0:T(8,128)(2,1)S(1)} %get-tuple-element.29.refs_0_.asked_ref, bf16[1,4,128,128]{3,2,1,0:T(8,128)(2,1)S(1)} %get-tuple-element.30.refs_0_, bf16[1,4,128,128]{3,2,1,0:T(8,128)(2,1)S(1)} %collective-permute-done.1.refs_0_.refs_1_, ...), custom_call_target="tpu_custom_call" | custom-call | flops 805306368 | bytes 4194304 | tf_op jit(solution)/shard_map/first_tiles/pallas_call | solution.py:268
  46.9 2.0 %more_tiles.1 = (f32[4,384,128]{2,1,0:T(8,128)S(1)}, f32[384,128]{1,0:T(8,128)S(1)}) custom-call(bf16[4,384,128]{2,1,0:T(8,128)(2,1)S(1)} %get-tuple-element.29.refs_0_.asked_ref, f32[4,384,128]{2,1,0:T(8,128)S(1)} %get-tuple-element.39.old_sums_ref, f32[384,128]{1,0:T(8,128)S(1)} %get-tuple-element.40.old_tops_ref.refs_0_, ...), custom_call_target="tpu_custom_call" | custom-call | flops 402653184 | bytes 4194304 | tf_op jit(solution)/shard_map/more_tiles/pallas_call | solution.py:301
  49.2 2.6 %collective-permute-done.14.refs_2_ = bf16[1,4,128,128]{3,2,1,0:T(8,128)(2,1)S(1)} collective-permute-done((bf16[1,4,128,128]{3,2,1,0:T(8,128)(2,1)S(1)}, bf16[1,4,128,128]{3,2,1,0:T(8,128)(2,1)S(1)}, u32[]{:S(2)}, u32[]{:S(2)}) %collective-permute-start.14) | collective-permute-done | bytes 131104 | tf_op jit(solution)/shard_map/ppermute | solution.py:416
  51.8 1.4 %last_tiles.2.refs_4_ = bf16[192,256]{1,0:T(8,128)(2,1)S(1)} custom-call(bf16[4,384,128]{2,1,0:T(8,128)(2,1)S(1)} %get-tuple-element.29.refs_0_.asked_ref, f32[4,384,128]{2,1,0:T(8,128)S(1)} %get-tuple-element.44.sums_ref, f32[384,128]{1,0:T(8,128)S(1)} %get-tuple-element.45.tops_ref, bf16[1,4,128,128]{3,2,1,0:T(8,128)(2,1)S(1)} %collective-permute-done.12.refs_0_, ...), custom_call_target="tpu_custom_call" | custom-call | flops 201326592 | bytes 4194304 | tf_op jit(solution)/shard_map/last_tiles/pallas_call | solution.py:335
  53.3 1.6 %collective-permute-start.16 = (bf16[192,256]{1,0:T(8,128)(2,1)S(1)}, bf16[192,256]{1,0:T(8,128)(2,1)S(1)}, u32[]{:S(2)}, u32[]{:S(2)}) collective-permute-start(bf16[192,256]{1,0:T(8,128)(2,1)S(1)} %last_tiles.2.refs_4_), channel_id=1, source_target_pairs={{0,1},{1,0},{2,3},{3,2},{4,5},{5,4},{6,7},{7,6},{8,9},{9,8},{10,11... | collective-permute-start | bytes 294920 | tf_op jit(solution)/shard_map/ppermute | solution.py:435
  54.9 1.4 %last_tiles.3.answer_ref = bf16[192,256]{1,0:T(8,128)(2,1)S(1)} custom-call(bf16[4,384,128]{2,1,0:T(8,128)(2,1)S(1)} %get-tuple-element.29.refs_0_.asked_ref, f32[4,384,128]{2,1,0:T(8,128)S(1)} %get-tuple-element.44.sums_ref, f32[384,128]{1,0:T(8,128)S(1)} %get-tuple-element.45.tops_ref, bf16[1,4,128,128]{3,2,1,0:T(8,128)(2,1)S(1)} %collective-permute-done.12.refs_0_, ...), custom_call_target="tpu_custom_call" | custom-call | flops 201326592 | bytes 4194304 | tf_op jit(solution)/shard_map/last_tiles/pallas_call | solution.py:335
  57.1 1.0 %collective-permute-done.16 = bf16[192,256]{1,0:T(8,128)(2,1)S(1)} collective-permute-done((bf16[192,256]{1,0:T(8,128)(2,1)S(1)}, bf16[192,256]{1,0:T(8,128)(2,1)S(1)}, u32[]{:S(2)}, u32[]{:S(2)}) %collective-permute-start.16) | collective-permute-done | bytes 98336 | tf_op jit(solution)/shard_map/ppermute | solution.py:435
  (31 shorter events, 7.6 us)
Async XLA Ops:
  1.1 27.4 %collective-permute-start.8 = (bf16[4,4,128,128]{3,2,1,0:T(8,128)(2,1)S(1)}, bf16[4,4,128,128]{3,2,1,0:T(8,128)(2,1)S(1)}, u32[]{:S(2)}, u32[]{:S(2)}) collective-permute-start(bf16[4,4,128,128]{3,2,1,0:T(8,128)(2,1)S(1)} %bitcast.10), channel_id=1, source_target_pairs={{0,16},{2,18},{4,20},{6,22},{8,24},{10,26},{12,28},{14,30},{16,0},... | collective-permute-start | bytes 1572872 | tf_op jit(solution)/shard_map/ppermute | solution.py:395
  5.2 7.3 %collective-permute-start = (bf16[48,4,512]{2,1,0:T(4,128)(2,1)}, bf16[48,4,512]{2,1,0:T(4,128)(2,1)S(1)}, u32[]{:S(2)}, u32[]{:S(2)}) collective-permute-start(bf16[48,4,512]{2,1,0:T(4,128)(2,1)} %refs_0_.1), channel_id=1, source_target_pairs={{0,1},{1,0},{2,3},{3,2},{4,5},{5,4},{6,7},{7,6},{8,9},{9,8},{10,11... | collective-permute-start | bytes 589832 | tf_op jit(solution)/shard_map/ppermute | solution.py:399
  6.8 0.7 %copy-start.1 = (s32[1,12]{1,0:T(1,128)S(1)}, s32[1,12]{1,0:T(1,128)}, u32[]{:S(2)}) copy-start(s32[1,12]{1,0:T(1,128)} %ids_ref.1) | copy-start | bytes 148
  8.7 9.3 %all-to-all-start = ((s32[8,2,128]{2,1,0:T(2,128)}), s32[8,2,128]{2,1,0:T(2,128)S(1)}, u32[]{:S(2)}, u32[]{:S(2)}) async-start(s32[8,2,128]{2,1,0:T(2,128)} %request.1), calls=%async_computation | async-start | bytes 16384 | tf_op jit(solution)/shard_map/all_to_all | solution.py:390
  18.8 3.7 %collective-permute-start.1 = (bf16[1,4,128,128]{3,2,1,0:T(8,128)(2,1)S(1)}, bf16[1,4,128,128]{3,2,1,0:T(8,128)(2,1)S(1)}, u32[]{:S(2)}, u32[]{:S(2)}) collective-permute-start(bf16[1,4,128,128]{3,2,1,0:T(8,128)(2,1)S(1)} %get-tuple-element.31), channel_id=1, source_target_pairs={{0,2},{2,0},{4,6},{6,4},{8,10},{10,8},{12,14},{14,12},{16,18},{18,... | collective-permute-start | bytes 393224 | tf_op jit(solution)/shard_map/ppermute | solution.py:416
  19.4 5.7 %collective-permute-start.2 = (bf16[1,4,128,128]{3,2,1,0:T(8,128)(2,1)S(1)}, bf16[1,4,128,128]{3,2,1,0:T(8,128)(2,1)S(1)}, u32[]{:S(2)}, u32[]{:S(2)}) collective-permute-start(bf16[1,4,128,128]{3,2,1,0:T(8,128)(2,1)S(1)} %get-tuple-element.32), channel_id=1, source_target_pairs={{0,4},{2,6},{4,0},{6,2},{8,12},{10,14},{12,8},{14,10},{16,20},{18,... | collective-permute-start | bytes 393224 | tf_op jit(solution)/shard_map/ppermute | solution.py:416
  21.0 10.3 %collective-permute-start.3 = (bf16[1,4,128,128]{3,2,1,0:T(8,128)(2,1)S(1)}, bf16[1,4,128,128]{3,2,1,0:T(8,128)(2,1)S(1)}, u32[]{:S(2)}, u32[]{:S(2)}) collective-permute-start(bf16[1,4,128,128]{3,2,1,0:T(8,128)(2,1)S(1)} %get-tuple-element.33), channel_id=1, source_target_pairs={{0,8},{2,10},{4,12},{6,14},{8,0},{10,2},{12,4},{14,6},{16,24},{18,... | collective-permute-start | bytes 393224 | tf_op jit(solution)/shard_map/ppermute | solution.py:416
  22.5 11.4 %collective-permute-start.4 = (bf16[1,4,128,128]{3,2,1,0:T(8,128)(2,1)S(1)}, bf16[1,4,128,128]{3,2,1,0:T(8,128)(2,1)S(1)}, u32[]{:S(2)}, u32[]{:S(2)}) collective-permute-start(bf16[1,4,128,128]{3,2,1,0:T(8,128)(2,1)S(1)} %get-tuple-element.34), channel_id=1, source_target_pairs={{0,10},{2,8},{4,14},{6,12},{8,2},{10,0},{12,6},{14,4},{16,26},{18,... | collective-permute-start | bytes 393224 | tf_op jit(solution)/shard_map/ppermute | solution.py:416
  22.5 13.0 %collective-permute-start.5 = (bf16[1,4,128,128]{3,2,1,0:T(8,128)(2,1)S(1)}, bf16[1,4,128,128]{3,2,1,0:T(8,128)(2,1)S(1)}, u32[]{:S(2)}, u32[]{:S(2)}) collective-permute-start(bf16[1,4,128,128]{3,2,1,0:T(8,128)(2,1)S(1)} %get-tuple-element.35), channel_id=1, source_target_pairs={{0,6},{2,4},{4,2},{6,0},{8,14},{10,12},{12,10},{14,8},{16,22},{18,... | collective-permute-start | bytes 393224 | tf_op jit(solution)/shard_map/ppermute | solution.py:416
  25.0 12.9 %collective-permute-start.6 = (bf16[1,4,128,128]{3,2,1,0:T(8,128)(2,1)S(1)}, bf16[1,4,128,128]{3,2,1,0:T(8,128)(2,1)S(1)}, u32[]{:S(2)}, u32[]{:S(2)}) collective-permute-start(bf16[1,4,128,128]{3,2,1,0:T(8,128)(2,1)S(1)} %get-tuple-element.36), channel_id=1, source_target_pairs={{0,12},{2,14},{4,8},{6,10},{8,4},{10,6},{12,0},{14,2},{16,28},{18,... | collective-permute-start | bytes 393224 | tf_op jit(solution)/shard_map/ppermute | solution.py:416
  28.5 12.1 %collective-permute-start.7 = (bf16[1,4,128,128]{3,2,1,0:T(8,128)(2,1)S(1)}, bf16[1,4,128,128]{3,2,1,0:T(8,128)(2,1)S(1)}, u32[]{:S(2)}, u32[]{:S(2)}) collective-permute-start(bf16[1,4,128,128]{3,2,1,0:T(8,128)(2,1)S(1)} %get-tuple-element.37), channel_id=1, source_target_pairs={{0,14},{2,12},{4,10},{6,8},{8,6},{10,4},{12,2},{14,0},{16,30},{18,... | collective-permute-start | bytes 393224 | tf_op jit(solution)/shard_map/ppermute | solution.py:416
  31.3 11.3 %collective-permute-start.9 = (bf16[1,4,128,128]{3,2,1,0:T(8,128)(2,1)S(1)}, bf16[1,4,128,128]{3,2,1,0:T(8,128)(2,1)S(1)}, u32[]{:S(2)}, u32[]{:S(2)}) collective-permute-start(bf16[1,4,128,128]{3,2,1,0:T(8,128)(2,1)S(1)} %get-tuple-element.38), channel_id=1, source_target_pairs={{0,8},{2,10},{4,12},{6,14},{8,0},{10,2},{12,4},{14,6},{16,24},{18,... | collective-permute-start | bytes 393224 | tf_op jit(solution)/shard_map/ppermute | solution.py:416
  33.9 12.1 %collective-permute-start.10 = (bf16[1,4,128,128]{3,2,1,0:T(8,128)(2,1)S(1)}, bf16[1,4,128,128]{3,2,1,0:T(8,128)(2,1)S(1)}, u32[]{:S(2)}, u32[]{:S(2)}) collective-permute-start(bf16[1,4,128,128]{3,2,1,0:T(8,128)(2,1)S(1)} %get-tuple-element.42), channel_id=1, source_target_pairs={{0,4},{2,6},{4,0},{6,2},{8,12},{10,14},{12,8},{14,10},{16,20},{18,... | collective-permute-start | bytes 393224 | tf_op jit(solution)/shard_map/ppermute | solution.py:416
  35.5 11.4 %collective-permute-start.11 = (bf16[1,4,128,128]{3,2,1,0:T(8,128)(2,1)S(1)}, bf16[1,4,128,128]{3,2,1,0:T(8,128)(2,1)S(1)}, u32[]{:S(2)}, u32[]{:S(2)}) collective-permute-start(bf16[1,4,128,128]{3,2,1,0:T(8,128)(2,1)S(1)} %get-tuple-element.43), channel_id=1, source_target_pairs={{0,10},{2,8},{4,14},{6,12},{8,2},{10,0},{12,6},{14,4},{16,26},{18,... | collective-permute-start | bytes 393224 | tf_op jit(solution)/shard_map/ppermute | solution.py:416
  38.0 10.9 %collective-permute-start.12 = (bf16[1,4,128,128]{3,2,1,0:T(8,128)(2,1)S(1)}, bf16[1,4,128,128]{3,2,1,0:T(8,128)(2,1)S(1)}, u32[]{:S(2)}, u32[]{:S(2)}) collective-permute-start(bf16[1,4,128,128]{3,2,1,0:T(8,128)(2,1)S(1)} %get-tuple-element.46), channel_id=1, source_target_pairs={{0,6},{2,4},{4,2},{6,0},{8,14},{10,12},{12,10},{14,8},{16,22},{18,... | collective-permute-start | bytes 393224 | tf_op jit(solution)/shard_map/ppermute | solution.py:416
  40.6 8.6 %collective-permute-start.13 = (bf16[1,4,128,128]{3,2,1,0:T(8,128)(2,1)S(1)}, bf16[1,4,128,128]{3,2,1,0:T(8,128)(2,1)S(1)}, u32[]{:S(2)}, u32[]{:S(2)}) collective-permute-start(bf16[1,4,128,128]{3,2,1,0:T(8,128)(2,1)S(1)} %get-tuple-element.47), channel_id=1, source_target_pairs={{0,12},{2,14},{4,8},{6,10},{8,4},{10,6},{12,0},{14,2},{16,28},{18,... | collective-permute-start | bytes 393224 | tf_op jit(solution)/shard_map/ppermute | solution.py:416
  42.6 9.2 %collective-permute-start.14 = (bf16[1,4,128,128]{3,2,1,0:T(8,128)(2,1)S(1)}, bf16[1,4,128,128]{3,2,1,0:T(8,128)(2,1)S(1)}, u32[]{:S(2)}, u32[]{:S(2)}) collective-permute-start(bf16[1,4,128,128]{3,2,1,0:T(8,128)(2,1)S(1)} %get-tuple-element.48), channel_id=1, source_target_pairs={{0,14},{2,12},{4,10},{6,8},{8,6},{10,4},{12,2},{14,0},{16,30},{18,... | collective-permute-start | bytes 393224 | tf_op jit(solution)/shard_map/ppermute | solution.py:416
  46.1 5.8 %collective-permute-start.15 = (bf16[1,4,128,128]{3,2,1,0:T(8,128)(2,1)S(1)}, bf16[1,4,128,128]{3,2,1,0:T(8,128)(2,1)S(1)}, u32[]{:S(2)}, u32[]{:S(2)}) collective-permute-start(bf16[1,4,128,128]{3,2,1,0:T(8,128)(2,1)S(1)} %pick_each.5), channel_id=1, source_target_pairs={{0,2},{2,0},{4,6},{6,4},{8,10},{10,8},{12,14},{14,12},{16,18},{18,... | collective-permute-start | bytes 393224 | tf_op jit(solution)/shard_map/ppermute | solution.py:416
  51.8 4.5 %copy-start = (bf16[512,512]{1,0:T(8,128)(2,1)S(1)}, bf16[512,512]{1,0:T(8,128)(2,1)}, u32[]{:S(2)}) copy-start(bf16[512,512]{1,0:T(8,128)(2,1)} %weight_ref.1) | copy-start | bytes 1572868
  53.3 4.9 %collective-permute-start.16 = (bf16[192,256]{1,0:T(8,128)(2,1)S(1)}, bf16[192,256]{1,0:T(8,128)(2,1)S(1)}, u32[]{:S(2)}, u32[]{:S(2)}) collective-permute-start(bf16[192,256]{1,0:T(8,128)(2,1)S(1)} %last_tiles.2.refs_4_), channel_id=1, source_target_pairs={{0,1},{1,0},{2,3},{3,2},{4,5},{5,4},{6,7},{7,6},{8,9},{9,8},{10,11... | collective-permute-start | bytes 294920 | tf_op jit(solution)/shard_map/ppermute | solution.py:435

commit v22 on v21

--- a/solution.py
+++ b/solution.py
@@ -404,7 +404,7 @@
         return bool(step & across) and bool(step & (across - 1) & ~1)
 
     near_order = [0, 1] + sorted(range(2, half), key=lambda step: (turns(step), step != 2, not step & across, step))
-    far_order = [0] + sorted(range(2, half), key=lambda step: (turns(step), step & 1, not step & across, step)) + [1]
+    far_order = [0] + sorted(range(2, half), key=lambda step: (turns(step), step & 1, step)) + [1]
     near_slots, far_slots = (near_order, [half + step for step in far_order]) if paired else ([0], [half])
 
     def spread(tiles, which, order, after):

time: 59.4 us -> 59.4 us (level)
  waiting for transfers between devices: 16.7 us -> 15.9 us
  starting transfers between devices: 22.5 us -> 23.2 us
    ppermute x14, starting transfers between devices: 11.5 us -> 12.2 us  [spread(): lax.ppermute(tile, 'rows', [(row, row ^ step) for row in range(row_size)])]
    ppermute x14, waiting for transfers between devices: 15.4 us -> 14.6 us  [spread(): lax.ppermute(tile, 'rows', [(row, row ^ step) for row in range(row_size)])]
where the time goes in v22:
time: 59.4 us; the launch traced here: 59.1 us
  starting transfers between devices  23.2 us (39%)
  Pallas kernels  17 us (29%)
  waiting for transfers between devices  15.9 us (27%)
  local copies, waits for them, and re-layouts  2.53 us (4%)
    ppermute x14, waiting for transfers between devices, spread(): lax.ppermute(tile, 'rows', [(row, row ^ step) for row in range(row_size)])  14.6 us
    ppermute x14, starting transfers between devices, spread(): lax.ppermute(tile, 'rows', [(row, row ^ step) for row in range(row_size)])  12.2 us
    pallas_call x1, Pallas kernels, front(): pl.pallas_call(functools.partial(front_kernel, groups, heads, head_size,...  5.51 us
    ppermute x1, starting transfers between devices, shards(): mirrored = lax.ppermute(heads_first, 'rows', turn(row_size, half))  4.1 us
    all_to_all x1, starting transfers between devices, swap(): lax.all_to_all(value, 'rows', split_axis=0, concat_axis=0, tiled=True, ax...  3.78 us
    pallas_call x2, Pallas kernels, last_tiles(): pl.pallas_call(functools.partial(last_kernel, slots, groups), out_shape=(...  2.88 us
    pallas_call x1, Pallas kernels, first_tiles(): pl.pallas_call(functools.partial(first_kernel, slots, rows if rows <= 512...  2.4 us
    pallas_call x3, Pallas kernels, pick_each(): pl.pallas_call(functools.partial(pick_each_kernel, which, order), out_sha...  2.19 us
  transfers between devices with their start and end apart: 18, of which 10 were waited for; matrix products, arithmetic and copies ran while one was open for 0% of the time, Pallas kernels for 26%

profile of v22, /device:TPU:0, one launch (start us, length us, event | category | flops | bytes accessed | tf_op | source)
XLA Modules:
  0.0 59.1 jit_solution(17478354182231768791)
XLA Ops:
  0.0 1.1 %copy.13 = bf16[4,128,4,128]{3,1,2,0:T(8,128)(2,1)S(1)} copy(bf16[4,128,4,128]{3,2,1,0:T(4,128)(2,1)} %param.17) | data formatting | bytes 1048576 | tf_op args[7]
  1.1 4.1 %collective-permute-start.8 = (bf16[4,4,128,128]{3,2,1,0:T(8,128)(2,1)S(1)}, bf16[4,4,128,128]{3,2,1,0:T(8,128)(2,1)S(1)}, u32[]{:S(2)}, u32[]{:S(2)}) collective-permute-start(bf16[4,4,128,128]{3,2,1,0:T(8,128)(2,1)S(1)} %bitcast.10), channel_id=1, source_target_pairs={{0,16},{2,18},{4,20},{6,22},{8,24},{10,26},{12,28},{14,30},{16,0},... | collective-permute-start | bytes 1572872 | tf_op jit(solution)/shard_map/ppermute | solution.py:395
  5.2 1.5 %collective-permute-start = (bf16[48,4,512]{2,1,0:T(4,128)(2,1)}, bf16[48,4,512]{2,1,0:T(4,128)(2,1)S(1)}, u32[]{:S(2)}, u32[]{:S(2)}) collective-permute-start(bf16[48,4,512]{2,1,0:T(4,128)(2,1)} %refs_0_.1), channel_id=1, source_target_pairs={{0,1},{1,0},{2,3},{3,2},{4,5},{5,4},{6,7},{7,6},{8,9},{9,8},{10,11... | collective-permute-start | bytes 589832 | tf_op jit(solution)/shard_map/ppermute | solution.py:399
  7.5 1.2 %request.1 = s32[8,2,128]{2,1,0:T(2,128)} custom-call(s32[1,12]{1,0:T(1,128)S(1)} %copy-done.1, s32[2]{0:T(128)S(1)} %pad_add_fusion.refs_2_.me_ref), custom_call_target="tpu_custom_call" | custom-call | bytes 262144 | tf_op jit(solution)/shard_map/request/pallas_call | solution.py:59
  8.7 3.8 %all-to-all-start = ((s32[8,2,128]{2,1,0:T(2,128)}), s32[8,2,128]{2,1,0:T(2,128)S(1)}, u32[]{:S(2)}, u32[]{:S(2)}) async-start(s32[8,2,128]{2,1,0:T(2,128)} %request.1), calls=%async_computation | async-start | bytes 16384 | tf_op jit(solution)/shard_map/all_to_all | solution.py:390
  12.5 5.5 %front.1 = (f32[192,512]{1,0:T(8,128)S(1)}, bf16[4,384,128]{2,1,0:T(8,128)(2,1)S(1)}) custom-call(bf16[48,4,512]{2,1,0:T(4,128)(2,1)} %refs_0_.1, bf16[48,4,512]{2,1,0:T(4,128)(2,1)S(1)} %collective-permute-done.refs_1_, s32[2]{0:T(128)S(1)} %pad_add_fusion.refs_2_.me_ref, s32[1,12]{1,0:T(1,128)} %ids_ref.1, s32[12,48]{1,0:T(8,128)} %bitcast.12, ...), custom_call_target="tpu_custom_call" | custom-call | flops 1006632960 | bytes 4194304 | tf_op jit(solution)/shard_map/front/pallas_call | solution.py:218
  19.4 1.7 %collective-permute-start.2 = (bf16[1,4,128,128]{3,2,1,0:T(8,128)(2,1)S(1)}, bf16[1,4,128,128]{3,2,1,0:T(8,128)(2,1)S(1)}, u32[]{:S(2)}, u32[]{:S(2)}) collective-permute-start(bf16[1,4,128,128]{3,2,1,0:T(8,128)(2,1)S(1)} %get-tuple-element.32), channel_id=1, source_target_pairs={{0,4},{2,6},{4,0},{6,2},{8,12},{10,14},{12,8},{14,10},{16,20},{18,... | collective-permute-start | bytes 393224 | tf_op jit(solution)/shard_map/ppermute | solution.py:416
  21.0 1.5 %collective-permute-start.3 = (bf16[1,4,128,128]{3,2,1,0:T(8,128)(2,1)S(1)}, bf16[1,4,128,128]{3,2,1,0:T(8,128)(2,1)S(1)}, u32[]{:S(2)}, u32[]{:S(2)}) collective-permute-start(bf16[1,4,128,128]{3,2,1,0:T(8,128)(2,1)S(1)} %get-tuple-element.33), channel_id=1, source_target_pairs={{0,8},{2,10},{4,12},{6,14},{8,0},{10,2},{12,4},{14,6},{16,24},{18,... | collective-permute-start | bytes 393224 | tf_op jit(solution)/shard_map/ppermute | solution.py:416
  23.1 1.9 %collective-permute-done.2.refs_1_.refs_2_ = bf16[1,4,128,128]{3,2,1,0:T(8,128)(2,1)S(1)} collective-permute-done((bf16[1,4,128,128]{3,2,1,0:T(8,128)(2,1)S(1)}, bf16[1,4,128,128]{3,2,1,0:T(8,128)(2,1)S(1)}, u32[]{:S(2)}, u32[]{:S(2)}) %collective-permute-start.2) | collective-permute-done | bytes 131104 | tf_op jit(solution)/shard_map/ppermute | solution.py:416
  25.0 3.2 %collective-permute-start.6 = (bf16[1,4,128,128]{3,2,1,0:T(8,128)(2,1)S(1)}, bf16[1,4,128,128]{3,2,1,0:T(8,128)(2,1)S(1)}, u32[]{:S(2)}, u32[]{:S(2)}) collective-permute-start(bf16[1,4,128,128]{3,2,1,0:T(8,128)(2,1)S(1)} %get-tuple-element.36), channel_id=1, source_target_pairs={{0,12},{2,14},{4,8},{6,10},{8,4},{10,6},{12,0},{14,2},{16,28},{18,... | collective-permute-start | bytes 393224 | tf_op jit(solution)/shard_map/ppermute | solution.py:416
  28.5 1.2 %collective-permute-start.7 = (bf16[1,4,128,128]{3,2,1,0:T(8,128)(2,1)S(1)}, bf16[1,4,128,128]{3,2,1,0:T(8,128)(2,1)S(1)}, u32[]{:S(2)}, u32[]{:S(2)}) collective-permute-start(bf16[1,4,128,128]{3,2,1,0:T(8,128)(2,1)S(1)} %get-tuple-element.37), channel_id=1, source_target_pairs={{0,14},{2,12},{4,10},{6,8},{8,6},{10,4},{12,2},{14,0},{16,30},{18,... | collective-permute-start | bytes 393224 | tf_op jit(solution)/shard_map/ppermute | solution.py:416
  31.3 1.5 %collective-permute-start.9 = (bf16[1,4,128,128]{3,2,1,0:T(8,128)(2,1)S(1)}, bf16[1,4,128,128]{3,2,1,0:T(8,128)(2,1)S(1)}, u32[]{:S(2)}, u32[]{:S(2)}) collective-permute-start(bf16[1,4,128,128]{3,2,1,0:T(8,128)(2,1)S(1)} %get-tuple-element.38), channel_id=1, source_target_pairs={{0,4},{2,6},{4,0},{6,2},{8,12},{10,14},{12,8},{14,10},{16,20},{18,... | collective-permute-start | bytes 393224 | tf_op jit(solution)/shard_map/ppermute | solution.py:416
  32.8 1.1 %collective-permute-done.4.refs_4_ = bf16[1,4,128,128]{3,2,1,0:T(8,128)(2,1)S(1)} collective-permute-done((bf16[1,4,128,128]{3,2,1,0:T(8,128)(2,1)S(1)}, bf16[1,4,128,128]{3,2,1,0:T(8,128)(2,1)S(1)}, u32[]{:S(2)}, u32[]{:S(2)}) %collective-permute-start.4) | collective-permute-done | bytes 131104 | tf_op jit(solution)/shard_map/ppermute | solution.py:416
  33.9 1.4 %collective-permute-start.11 = (bf16[1,4,128,128]{3,2,1,0:T(8,128)(2,1)S(1)}, bf16[1,4,128,128]{3,2,1,0:T(8,128)(2,1)S(1)}, u32[]{:S(2)}, u32[]{:S(2)}) collective-permute-start(bf16[1,4,128,128]{3,2,1,0:T(8,128)(2,1)S(1)} %get-tuple-element.43), channel_id=1, source_target_pairs={{0,6},{2,4},{4,2},{6,0},{8,14},{10,12},{12,10},{14,8},{16,22},{18,... | collective-permute-start | bytes 393224 | tf_op jit(solution)/shard_map/ppermute | solution.py:416
  35.4 2.6 %collective-permute-done.6.refs_6_ = bf16[1,4,128,128]{3,2,1,0:T(8,128)(2,1)S(1)} collective-permute-done((bf16[1,4,128,128]{3,2,1,0:T(8,128)(2,1)S(1)}, bf16[1,4,128,128]{3,2,1,0:T(8,128)(2,1)S(1)}, u32[]{:S(2)}, u32[]{:S(2)}) %collective-permute-start.6) | collective-permute-done | bytes 131104 | tf_op jit(solution)/shard_map/ppermute | solution.py:416
  38.0 2.6 %collective-permute-done.7.refs_7_ = bf16[1,4,128,128]{3,2,1,0:T(8,128)(2,1)S(1)} collective-permute-done((bf16[1,4,128,128]{3,2,1,0:T(8,128)(2,1)S(1)}, bf16[1,4,128,128]{3,2,1,0:T(8,128)(2,1)S(1)}, u32[]{:S(2)}, u32[]{:S(2)}) %collective-permute-start.7) | collective-permute-done | bytes 131104 | tf_op jit(solution)/shard_map/ppermute | solution.py:416
  40.6 2.7 %collective-permute-done.9.refs_8_.refs_1_ = bf16[1,4,128,128]{3,2,1,0:T(8,128)(2,1)S(1)} collective-permute-done((bf16[1,4,128,128]{3,2,1,0:T(8,128)(2,1)S(1)}, bf16[1,4,128,128]{3,2,1,0:T(8,128)(2,1)S(1)}, u32[]{:S(2)}, u32[]{:S(2)}) %collective-permute-start.9) | collective-permute-done | bytes 131104 | tf_op jit(solution)/shard_map/ppermute | solution.py:416
  43.3 2.4 %first_tiles.1 = (f32[4,384,128]{2,1,0:T(8,128)S(1)}, f32[384,128]{1,0:T(8,128)S(1)}) custom-call(bf16[4,384,128]{2,1,0:T(8,128)(2,1)S(1)} %get-tuple-element.29.refs_0_.asked_ref, bf16[1,4,128,128]{3,2,1,0:T(8,128)(2,1)S(1)} %get-tuple-element.30.refs_0_, bf16[1,4,128,128]{3,2,1,0:T(8,128)(2,1)S(1)} %collective-permute-done.1.refs_0_.refs_1_, ...), custom_call_target="tpu_custom_call" | custom-call | flops 805306368 | bytes 4194304 | tf_op jit(solution)/shard_map/first_tiles/pallas_call | solution.py:268
  46.9 2.0 %more_tiles.1 = (f32[4,384,128]{2,1,0:T(8,128)S(1)}, f32[384,128]{1,0:T(8,128)S(1)}) custom-call(bf16[4,384,128]{2,1,0:T(8,128)(2,1)S(1)} %get-tuple-element.29.refs_0_.asked_ref, f32[4,384,128]{2,1,0:T(8,128)S(1)} %get-tuple-element.39.old_sums_ref, f32[384,128]{1,0:T(8,128)S(1)} %get-tuple-element.40.old_tops_ref.refs_0_, ...), custom_call_target="tpu_custom_call" | custom-call | flops 402653184 | bytes 4194304 | tf_op jit(solution)/shard_map/more_tiles/pallas_call | solution.py:301
  49.2 2.6 %collective-permute-done.14.refs_2_ = bf16[1,4,128,128]{3,2,1,0:T(8,128)(2,1)S(1)} collective-permute-done((bf16[1,4,128,128]{3,2,1,0:T(8,128)(2,1)S(1)}, bf16[1,4,128,128]{3,2,1,0:T(8,128)(2,1)S(1)}, u32[]{:S(2)}, u32[]{:S(2)}) %collective-permute-start.14) | collective-permute-done | bytes 131104 | tf_op jit(solution)/shard_map/ppermute | solution.py:416
  51.8 1.5 %last_tiles.2.refs_4_ = bf16[192,256]{1,0:T(8,128)(2,1)S(1)} custom-call(bf16[4,384,128]{2,1,0:T(8,128)(2,1)S(1)} %get-tuple-element.29.refs_0_.asked_ref, f32[4,384,128]{2,1,0:T(8,128)S(1)} %get-tuple-element.44.sums_ref, f32[384,128]{1,0:T(8,128)S(1)} %get-tuple-element.45.tops_ref, bf16[1,4,128,128]{3,2,1,0:T(8,128)(2,1)S(1)} %collective-permute-done.12.refs_0_, ...), custom_call_target="tpu_custom_call" | custom-call | flops 201326592 | bytes 4194304 | tf_op jit(solution)/shard_map/last_tiles/pallas_call | solution.py:335
  53.3 1.6 %collective-permute-start.16 = (bf16[192,256]{1,0:T(8,128)(2,1)S(1)}, bf16[192,256]{1,0:T(8,128)(2,1)S(1)}, u32[]{:S(2)}, u32[]{:S(2)}) collective-permute-start(bf16[192,256]{1,0:T(8,128)(2,1)S(1)} %last_tiles.2.refs_4_), channel_id=1, source_target_pairs={{0,1},{1,0},{2,3},{3,2},{4,5},{5,4},{6,7},{7,6},{8,9},{9,8},{10,11... | collective-permute-start | bytes 294920 | tf_op jit(solution)/shard_map/ppermute | solution.py:435
  54.9 1.4 %last_tiles.3.answer_ref = bf16[192,256]{1,0:T(8,128)(2,1)S(1)} custom-call(bf16[4,384,128]{2,1,0:T(8,128)(2,1)S(1)} %get-tuple-element.29.refs_0_.asked_ref, f32[4,384,128]{2,1,0:T(8,128)S(1)} %get-tuple-element.44.sums_ref, f32[384,128]{1,0:T(8,128)S(1)} %get-tuple-element.45.tops_ref, bf16[1,4,128,128]{3,2,1,0:T(8,128)(2,1)S(1)} %collective-permute-done.12.refs_0_, ...), custom_call_target="tpu_custom_call" | custom-call | flops 201326592 | bytes 4194304 | tf_op jit(solution)/shard_map/last_tiles/pallas_call | solution.py:335
  57.1 1.0 %collective-permute-done.16 = bf16[192,256]{1,0:T(8,128)(2,1)S(1)} collective-permute-done((bf16[192,256]{1,0:T(8,128)(2,1)S(1)}, bf16[192,256]{1,0:T(8,128)(2,1)S(1)}, u32[]{:S(2)}, u32[]{:S(2)}) %collective-permute-start.16) | collective-permute-done | bytes 98336 | tf_op jit(solution)/shard_map/ppermute | solution.py:435
  (31 shorter events, 7.7 us)
Async XLA Ops:
  1.1 27.4 %collective-permute-start.8 = (bf16[4,4,128,128]{3,2,1,0:T(8,128)(2,1)S(1)}, bf16[4,4,128,128]{3,2,1,0:T(8,128)(2,1)S(1)}, u32[]{:S(2)}, u32[]{:S(2)}) collective-permute-start(bf16[4,4,128,128]{3,2,1,0:T(8,128)(2,1)S(1)} %bitcast.10), channel_id=1, source_target_pairs={{0,16},{2,18},{4,20},{6,22},{8,24},{10,26},{12,28},{14,30},{16,0},... | collective-permute-start | bytes 1572872 | tf_op jit(solution)/shard_map/ppermute | solution.py:395
  5.2 7.3 %collective-permute-start = (bf16[48,4,512]{2,1,0:T(4,128)(2,1)}, bf16[48,4,512]{2,1,0:T(4,128)(2,1)S(1)}, u32[]{:S(2)}, u32[]{:S(2)}) collective-permute-start(bf16[48,4,512]{2,1,0:T(4,128)(2,1)} %refs_0_.1), channel_id=1, source_target_pairs={{0,1},{1,0},{2,3},{3,2},{4,5},{5,4},{6,7},{7,6},{8,9},{9,8},{10,11... | collective-permute-start | bytes 589832 | tf_op jit(solution)/shard_map/ppermute | solution.py:399
  6.8 0.7 %copy-start.1 = (s32[1,12]{1,0:T(1,128)S(1)}, s32[1,12]{1,0:T(1,128)}, u32[]{:S(2)}) copy-start(s32[1,12]{1,0:T(1,128)} %ids_ref.1) | copy-start | bytes 148
  8.7 9.3 %all-to-all-start = ((s32[8,2,128]{2,1,0:T(2,128)}), s32[8,2,128]{2,1,0:T(2,128)S(1)}, u32[]{:S(2)}, u32[]{:S(2)}) async-start(s32[8,2,128]{2,1,0:T(2,128)} %request.1), calls=%async_computation | async-start | bytes 16384 | tf_op jit(solution)/shard_map/all_to_all | solution.py:390
  18.8 3.7 %collective-permute-start.1 = (bf16[1,4,128,128]{3,2,1,0:T(8,128)(2,1)S(1)}, bf16[1,4,128,128]{3,2,1,0:T(8,128)(2,1)S(1)}, u32[]{:S(2)}, u32[]{:S(2)}) collective-permute-start(bf16[1,4,128,128]{3,2,1,0:T(8,128)(2,1)S(1)} %get-tuple-element.31), channel_id=1, source_target_pairs={{0,2},{2,0},{4,6},{6,4},{8,10},{10,8},{12,14},{14,12},{16,18},{18,... | collective-permute-start | bytes 393224 | tf_op jit(solution)/shard_map/ppermute | solution.py:416
  19.4 5.7 %collective-permute-start.2 = (bf16[1,4,128,128]{3,2,1,0:T(8,128)(2,1)S(1)}, bf16[1,4,128,128]{3,2,1,0:T(8,128)(2,1)S(1)}, u32[]{:S(2)}, u32[]{:S(2)}) collective-permute-start(bf16[1,4,128,128]{3,2,1,0:T(8,128)(2,1)S(1)} %get-tuple-element.32), channel_id=1, source_target_pairs={{0,4},{2,6},{4,0},{6,2},{8,12},{10,14},{12,8},{14,10},{16,20},{18,... | collective-permute-start | bytes 393224 | tf_op jit(solution)/shard_map/ppermute | solution.py:416
  21.0 10.3 %collective-permute-start.3 = (bf16[1,4,128,128]{3,2,1,0:T(8,128)(2,1)S(1)}, bf16[1,4,128,128]{3,2,1,0:T(8,128)(2,1)S(1)}, u32[]{:S(2)}, u32[]{:S(2)}) collective-permute-start(bf16[1,4,128,128]{3,2,1,0:T(8,128)(2,1)S(1)} %get-tuple-element.33), channel_id=1, source_target_pairs={{0,8},{2,10},{4,12},{6,14},{8,0},{10,2},{12,4},{14,6},{16,24},{18,... | collective-permute-start | bytes 393224 | tf_op jit(solution)/shard_map/ppermute | solution.py:416
  22.5 11.4 %collective-permute-start.4 = (bf16[1,4,128,128]{3,2,1,0:T(8,128)(2,1)S(1)}, bf16[1,4,128,128]{3,2,1,0:T(8,128)(2,1)S(1)}, u32[]{:S(2)}, u32[]{:S(2)}) collective-permute-start(bf16[1,4,128,128]{3,2,1,0:T(8,128)(2,1)S(1)} %get-tuple-element.34), channel_id=1, source_target_pairs={{0,10},{2,8},{4,14},{6,12},{8,2},{10,0},{12,6},{14,4},{16,26},{18,... | collective-permute-start | bytes 393224 | tf_op jit(solution)/shard_map/ppermute | solution.py:416
  22.5 11.4 %collective-permute-start.5 = (bf16[1,4,128,128]{3,2,1,0:T(8,128)(2,1)S(1)}, bf16[1,4,128,128]{3,2,1,0:T(8,128)(2,1)S(1)}, u32[]{:S(2)}, u32[]{:S(2)}) collective-permute-start(bf16[1,4,128,128]{3,2,1,0:T(8,128)(2,1)S(1)} %get-tuple-element.35), channel_id=1, source_target_pairs={{0,6},{2,4},{4,2},{6,0},{8,14},{10,12},{12,10},{14,8},{16,22},{18,... | collective-permute-start | bytes 393224 | tf_op jit(solution)/shard_map/ppermute | solution.py:416
  25.0 13.0 %collective-permute-start.6 = (bf16[1,4,128,128]{3,2,1,0:T(8,128)(2,1)S(1)}, bf16[1,4,128,128]{3,2,1,0:T(8,128)(2,1)S(1)}, u32[]{:S(2)}, u32[]{:S(2)}) collective-permute-start(bf16[1,4,128,128]{3,2,1,0:T(8,128)(2,1)S(1)} %get-tuple-element.36), channel_id=1, source_target_pairs={{0,12},{2,14},{4,8},{6,10},{8,4},{10,6},{12,0},{14,2},{16,28},{18,... | collective-permute-start | bytes 393224 | tf_op jit(solution)/shard_map/ppermute | solution.py:416
  28.5 12.1 %collective-permute-start.7 = (bf16[1,4,128,128]{3,2,1,0:T(8,128)(2,1)S(1)}, bf16[1,4,128,128]{3,2,1,0:T(8,128)(2,1)S(1)}, u32[]{:S(2)}, u32[]{:S(2)}) collective-permute-start(bf16[1,4,128,128]{3,2,1,0:T(8,128)(2,1)S(1)} %get-tuple-element.37), channel_id=1, source_target_pairs={{0,14},{2,12},{4,10},{6,8},{8,6},{10,4},{12,2},{14,0},{16,30},{18,... | collective-permute-start | bytes 393224 | tf_op jit(solution)/shard_map/ppermute | solution.py:416
  31.3 12.0 %collective-permute-start.9 = (bf16[1,4,128,128]{3,2,1,0:T(8,128)(2,1)S(1)}, bf16[1,4,128,128]{3,2,1,0:T(8,128)(2,1)S(1)}, u32[]{:S(2)}, u32[]{:S(2)}) collective-permute-start(bf16[1,4,128,128]{3,2,1,0:T(8,128)(2,1)S(1)} %get-tuple-element.38), channel_id=1, source_target_pairs={{0,4},{2,6},{4,0},{6,2},{8,12},{10,14},{12,8},{14,10},{16,20},{18,... | collective-permute-start | bytes 393224 | tf_op jit(solution)/shard_map/ppermute | solution.py:416
  33.9 12.5 %collective-permute-start.10 = (bf16[1,4,128,128]{3,2,1,0:T(8,128)(2,1)S(1)}, bf16[1,4,128,128]{3,2,1,0:T(8,128)(2,1)S(1)}, u32[]{:S(2)}, u32[]{:S(2)}) collective-permute-start(bf16[1,4,128,128]{3,2,1,0:T(8,128)(2,1)S(1)} %get-tuple-element.42), channel_id=1, source_target_pairs={{0,8},{2,10},{4,12},{6,14},{8,0},{10,2},{12,4},{14,6},{16,24},{18,... | collective-permute-start | bytes 393224 | tf_op jit(solution)/shard_map/ppermute | solution.py:416
  33.9 12.9 %collective-permute-start.11 = (bf16[1,4,128,128]{3,2,1,0:T(8,128)(2,1)S(1)}, bf16[1,4,128,128]{3,2,1,0:T(8,128)(2,1)S(1)}, u32[]{:S(2)}, u32[]{:S(2)}) collective-permute-start(bf16[1,4,128,128]{3,2,1,0:T(8,128)(2,1)S(1)} %get-tuple-element.43), channel_id=1, source_target_pairs={{0,6},{2,4},{4,2},{6,0},{8,14},{10,12},{12,10},{14,8},{16,22},{18,... | collective-permute-start | bytes 393224 | tf_op jit(solution)/shard_map/ppermute | solution.py:416
  38.0 10.9 %collective-permute-start.12 = (bf16[1,4,128,128]{3,2,1,0:T(8,128)(2,1)S(1)}, bf16[1,4,128,128]{3,2,1,0:T(8,128)(2,1)S(1)}, u32[]{:S(2)}, u32[]{:S(2)}) collective-permute-start(bf16[1,4,128,128]{3,2,1,0:T(8,128)(2,1)S(1)} %get-tuple-element.46), channel_id=1, source_target_pairs={{0,10},{2,8},{4,14},{6,12},{8,2},{10,0},{12,6},{14,4},{16,26},{18,... | collective-permute-start | bytes 393224 | tf_op jit(solution)/shard_map/ppermute | solution.py:416
  40.6 8.6 %collective-permute-start.13 = (bf16[1,4,128,128]{3,2,1,0:T(8,128)(2,1)S(1)}, bf16[1,4,128,128]{3,2,1,0:T(8,128)(2,1)S(1)}, u32[]{:S(2)}, u32[]{:S(2)}) collective-permute-start(bf16[1,4,128,128]{3,2,1,0:T(8,128)(2,1)S(1)} %get-tuple-element.47), channel_id=1, source_target_pairs={{0,12},{2,14},{4,8},{6,10},{8,4},{10,6},{12,0},{14,2},{16,28},{18,... | collective-permute-start | bytes 393224 | tf_op jit(solution)/shard_map/ppermute | solution.py:416
  43.3 8.5 %collective-permute-start.14 = (bf16[1,4,128,128]{3,2,1,0:T(8,128)(2,1)S(1)}, bf16[1,4,128,128]{3,2,1,0:T(8,128)(2,1)S(1)}, u32[]{:S(2)}, u32[]{:S(2)}) collective-permute-start(bf16[1,4,128,128]{3,2,1,0:T(8,128)(2,1)S(1)} %get-tuple-element.48), channel_id=1, source_target_pairs={{0,14},{2,12},{4,10},{6,8},{8,6},{10,4},{12,2},{14,0},{16,30},{18,... | collective-permute-start | bytes 393224 | tf_op jit(solution)/shard_map/ppermute | solution.py:416
  46.4 5.4 %collective-permute-start.15 = (bf16[1,4,128,128]{3,2,1,0:T(8,128)(2,1)S(1)}, bf16[1,4,128,128]{3,2,1,0:T(8,128)(2,1)S(1)}, u32[]{:S(2)}, u32[]{:S(2)}) collective-permute-start(bf16[1,4,128,128]{3,2,1,0:T(8,128)(2,1)S(1)} %pick_each.5), channel_id=1, source_target_pairs={{0,2},{2,0},{4,6},{6,4},{8,10},{10,8},{12,14},{14,12},{16,18},{18,... | collective-permute-start | bytes 393224 | tf_op jit(solution)/shard_map/ppermute | solution.py:416
  51.8 4.5 %copy-start = (bf16[512,512]{1,0:T(8,128)(2,1)S(1)}, bf16[512,512]{1,0:T(8,128)(2,1)}, u32[]{:S(2)}) copy-start(bf16[512,512]{1,0:T(8,128)(2,1)} %weight_ref.1) | copy-start | bytes 1572868
  53.3 4.9 %collective-permute-start.16 = (bf16[192,256]{1,0:T(8,128)(2,1)S(1)}, bf16[192,256]{1,0:T(8,128)(2,1)S(1)}, u32[]{:S(2)}, u32[]{:S(2)}) collective-permute-start(bf16[192,256]{1,0:T(8,128)(2,1)S(1)} %last_tiles.2.refs_4_), channel_id=1, source_target_pairs={{0,1},{1,0},{2,3},{3,2},{4,5},{5,4},{6,7},{7,6},{8,9},{9,8},{10,11... | collective-permute-start | bytes 294920 | tf_op jit(solution)/shard_map/ppermute | solution.py:435

commit v23 on v21

--- a/solution.py
+++ b/solution.py
@@ -424,10 +424,10 @@
     far = spread(mirrored, 1, far_order[:-1] if paired else far_order, near[1:3])
     sums, tops = first_tiles(asked, near, near_slots, rows * cols, far[1:2])
     far += spread(mirrored, 1, far_order[-1:] if paired else [], [tops])
-    batch = len(far) // 2
-    if batch:
-        sums, tops = more_tiles(asked, sums, tops, far[:batch], far_slots[:batch], rows * cols)
-    far, far_slots = far[batch:], far_slots[batch:]
+    for batch in (len(far) // 2, len(far) // 4):
+        if batch:
+            sums, tops = more_tiles(asked, sums, tops, far[:batch], far_slots[:batch], rows * cols)
+        far, far_slots = far[batch:], far_slots[batch:]
     others = last_tiles(asked, sums, tops, far, far_slots, list(range(1, col_size)), rows * cols, [])
     own = last_tiles(asked, sums, tops, far, far_slots, [0], rows * cols, others[:1])
     final, *weights = own_part(me, w_tile_out, residual, own[0], col_size)

time: 59.4 us -> 59.2 us (level)
  waiting for transfers between devices: 16.7 us -> 14.8 us
  Pallas kernels: 17 us -> 18.7 us
    pallas_call x1 -> x2, Pallas kernels: 2.03 us -> 4.06 us  [more_tiles(): pl.pallas_call(functools.partial(more_kernel, slots, rows if rows <= 512...]
    ppermute x14, waiting for transfers between devices: 15.4 us -> 13.4 us  [spread(): lax.ppermute(tile, 'rows', [(row, row ^ step) for row in range(row_size)])]
  transfers between devices with their start and end apart: 18 -> 18, of which waited for: 10 -> 10; matrix products, arithmetic and copies ran while one was open for 0% -> 0% of each run, Pallas kernels for 26% -> 30%
where the time goes in v23:
time: 59.2 us; the launch traced here: 59 us
  starting transfers between devices  22.5 us (38%)
  Pallas kernels  18.7 us (32%)
  waiting for transfers between devices  14.8 us (25%)
  local copies, waits for them, and re-layouts  2.53 us (4%)
    ppermute x14, waiting for transfers between devices, spread(): lax.ppermute(tile, 'rows', [(row, row ^ step) for row in range(row_size)])  13.4 us
    ppermute x14, starting transfers between devices, spread(): lax.ppermute(tile, 'rows', [(row, row ^ step) for row in range(row_size)])  11.5 us
    pallas_call x1, Pallas kernels, front(): pl.pallas_call(functools.partial(front_kernel, groups, heads, head_size,...  5.51 us
    ppermute x1, starting transfers between devices, shards(): mirrored = lax.ppermute(heads_first, 'rows', turn(row_size, half))  4.1 us
    pallas_call x2, Pallas kernels, more_tiles(): pl.pallas_call(functools.partial(more_kernel, slots, rows if rows <= 512...  4.06 us
    all_to_all x1, starting transfers between devices, swap(): lax.all_to_all(value, 'rows', split_axis=0, concat_axis=0, tiled=True, ax...  3.78 us
    pallas_call x2, Pallas kernels, last_tiles(): pl.pallas_call(functools.partial(last_kernel, slots, groups), out_shape=(...  2.6 us
    pallas_call x1, Pallas kernels, first_tiles(): pl.pallas_call(functools.partial(first_kernel, slots, rows if rows <= 512...  2.38 us
  transfers between devices with their start and end apart: 18, of which 10 were waited for; matrix products, arithmetic and copies ran while one was open for 0% of the time, Pallas kernels for 30%

profile of v23, /device:TPU:0, one launch (start us, length us, event | category | flops | bytes accessed | tf_op | source)
XLA Modules:
  0.0 59.0 jit_solution(18225860533160937276)
XLA Ops:
  0.0 1.1 %copy.13 = bf16[4,128,4,128]{3,1,2,0:T(8,128)(2,1)S(1)} copy(bf16[4,128,4,128]{3,2,1,0:T(4,128)(2,1)} %param.17) | data formatting | bytes 1048576 | tf_op args[7]
  1.1 4.1 %collective-permute-start.8 = (bf16[4,4,128,128]{3,2,1,0:T(8,128)(2,1)S(1)}, bf16[4,4,128,128]{3,2,1,0:T(8,128)(2,1)S(1)}, u32[]{:S(2)}, u32[]{:S(2)}) collective-permute-start(bf16[4,4,128,128]{3,2,1,0:T(8,128)(2,1)S(1)} %bitcast.10), channel_id=1, source_target_pairs={{0,16},{2,18},{4,20},{6,22},{8,24},{10,26},{12,28},{14,30},{16,0},... | collective-permute-start | bytes 1572872 | tf_op jit(solution)/shard_map/ppermute | solution.py:395
  5.2 1.5 %collective-permute-start = (bf16[48,4,512]{2,1,0:T(4,128)(2,1)}, bf16[48,4,512]{2,1,0:T(4,128)(2,1)S(1)}, u32[]{:S(2)}, u32[]{:S(2)}) collective-permute-start(bf16[48,4,512]{2,1,0:T(4,128)(2,1)} %refs_0_.1), channel_id=1, source_target_pairs={{0,1},{1,0},{2,3},{3,2},{4,5},{5,4},{6,7},{7,6},{8,9},{9,8},{10,11... | collective-permute-start | bytes 589832 | tf_op jit(solution)/shard_map/ppermute | solution.py:399
  7.5 1.2 %request.1 = s32[8,2,128]{2,1,0:T(2,128)} custom-call(s32[1,12]{1,0:T(1,128)S(1)} %copy-done.1, s32[2]{0:T(128)S(1)} %pad_add_fusion.refs_2_.me_ref), custom_call_target="tpu_custom_call" | custom-call | bytes 262144 | tf_op jit(solution)/shard_map/request/pallas_call | solution.py:59
  8.7 3.8 %all-to-all-start = ((s32[8,2,128]{2,1,0:T(2,128)}), s32[8,2,128]{2,1,0:T(2,128)S(1)}, u32[]{:S(2)}, u32[]{:S(2)}) async-start(s32[8,2,128]{2,1,0:T(2,128)} %request.1), calls=%async_computation | async-start | bytes 16384 | tf_op jit(solution)/shard_map/all_to_all | solution.py:390
  12.5 5.5 %front.1 = (f32[192,512]{1,0:T(8,128)S(1)}, bf16[4,384,128]{2,1,0:T(8,128)(2,1)S(1)}) custom-call(bf16[48,4,512]{2,1,0:T(4,128)(2,1)} %refs_0_.1, bf16[48,4,512]{2,1,0:T(4,128)(2,1)S(1)} %collective-permute-done.refs_1_, s32[2]{0:T(128)S(1)} %pad_add_fusion.refs_2_.me_ref, s32[1,12]{1,0:T(1,128)} %ids_ref.1, s32[12,48]{1,0:T(8,128)} %bitcast.12, ...), custom_call_target="tpu_custom_call" | custom-call | flops 1006632960 | bytes 4194304 | tf_op jit(solution)/shard_map/front/pallas_call | solution.py:218
  19.4 1.7 %collective-permute-start.2 = (bf16[1,4,128,128]{3,2,1,0:T(8,128)(2,1)S(1)}, bf16[1,4,128,128]{3,2,1,0:T(8,128)(2,1)S(1)}, u32[]{:S(2)}, u32[]{:S(2)}) collective-permute-start(bf16[1,4,128,128]{3,2,1,0:T(8,128)(2,1)S(1)} %get-tuple-element.34), channel_id=1, source_target_pairs={{0,4},{2,6},{4,0},{6,2},{8,12},{10,14},{12,8},{14,10},{16,20},{18,... | collective-permute-start | bytes 393224 | tf_op jit(solution)/shard_map/ppermute | solution.py:416
  21.0 1.5 %collective-permute-start.3 = (bf16[1,4,128,128]{3,2,1,0:T(8,128)(2,1)S(1)}, bf16[1,4,128,128]{3,2,1,0:T(8,128)(2,1)S(1)}, u32[]{:S(2)}, u32[]{:S(2)}) collective-permute-start(bf16[1,4,128,128]{3,2,1,0:T(8,128)(2,1)S(1)} %get-tuple-element.35), channel_id=1, source_target_pairs={{0,8},{2,10},{4,12},{6,14},{8,0},{10,2},{12,4},{14,6},{16,24},{18,... | collective-permute-start | bytes 393224 | tf_op jit(solution)/shard_map/ppermute | solution.py:416
  23.1 1.9 %collective-permute-done.2.refs_1_.refs_2_ = bf16[1,4,128,128]{3,2,1,0:T(8,128)(2,1)S(1)} collective-permute-done((bf16[1,4,128,128]{3,2,1,0:T(8,128)(2,1)S(1)}, bf16[1,4,128,128]{3,2,1,0:T(8,128)(2,1)S(1)}, u32[]{:S(2)}, u32[]{:S(2)}) %collective-permute-start.2) | collective-permute-done | bytes 131104 | tf_op jit(solution)/shard_map/ppermute | solution.py:416
  25.0 3.2 %collective-permute-start.6 = (bf16[1,4,128,128]{3,2,1,0:T(8,128)(2,1)S(1)}, bf16[1,4,128,128]{3,2,1,0:T(8,128)(2,1)S(1)}, u32[]{:S(2)}, u32[]{:S(2)}) collective-permute-start(bf16[1,4,128,128]{3,2,1,0:T(8,128)(2,1)S(1)} %get-tuple-element.38), channel_id=1, source_target_pairs={{0,12},{2,14},{4,8},{6,10},{8,4},{10,6},{12,0},{14,2},{16,28},{18,... | collective-permute-start | bytes 393224 | tf_op jit(solution)/shard_map/ppermute | solution.py:416
  28.5 1.2 %collective-permute-start.7 = (bf16[1,4,128,128]{3,2,1,0:T(8,128)(2,1)S(1)}, bf16[1,4,128,128]{3,2,1,0:T(8,128)(2,1)S(1)}, u32[]{:S(2)}, u32[]{:S(2)}) collective-permute-start(bf16[1,4,128,128]{3,2,1,0:T(8,128)(2,1)S(1)} %get-tuple-element.39), channel_id=1, source_target_pairs={{0,14},{2,12},{4,10},{6,8},{8,6},{10,4},{12,2},{14,0},{16,30},{18,... | collective-permute-start | bytes 393224 | tf_op jit(solution)/shard_map/ppermute | solution.py:416
  30.5 0.8 %collective-permute-done.3.refs_3_ = bf16[1,4,128,128]{3,2,1,0:T(8,128)(2,1)S(1)} collective-permute-done((bf16[1,4,128,128]{3,2,1,0:T(8,128)(2,1)S(1)}, bf16[1,4,128,128]{3,2,1,0:T(8,128)(2,1)S(1)}, u32[]{:S(2)}, u32[]{:S(2)}) %collective-permute-start.3) | collective-permute-done | bytes 131104 | tf_op jit(solution)/shard_map/ppermute | solution.py:416
  31.3 2.6 %collective-permute-done.4.refs_4_ = bf16[1,4,128,128]{3,2,1,0:T(8,128)(2,1)S(1)} collective-permute-done((bf16[1,4,128,128]{3,2,1,0:T(8,128)(2,1)S(1)}, bf16[1,4,128,128]{3,2,1,0:T(8,128)(2,1)S(1)}, u32[]{:S(2)}, u32[]{:S(2)}) %collective-permute-start.4) | collective-permute-done | bytes 131104 | tf_op jit(solution)/shard_map/ppermute | solution.py:416
  33.9 1.5 %collective-permute-start.10 = (bf16[1,4,128,128]{3,2,1,0:T(8,128)(2,1)S(1)}, bf16[1,4,128,128]{3,2,1,0:T(8,128)(2,1)S(1)}, u32[]{:S(2)}, u32[]{:S(2)}) collective-permute-start(bf16[1,4,128,128]{3,2,1,0:T(8,128)(2,1)S(1)} %get-tuple-element.44), channel_id=1, source_target_pairs={{0,4},{2,6},{4,0},{6,2},{8,12},{10,14},{12,8},{14,10},{16,20},{18,... | collective-permute-start | bytes 393224 | tf_op jit(solution)/shard_map/ppermute | solution.py:416
  35.5 2.5 %collective-permute-done.6.refs_6_ = bf16[1,4,128,128]{3,2,1,0:T(8,128)(2,1)S(1)} collective-permute-done((bf16[1,4,128,128]{3,2,1,0:T(8,128)(2,1)S(1)}, bf16[1,4,128,128]{3,2,1,0:T(8,128)(2,1)S(1)}, u32[]{:S(2)}, u32[]{:S(2)}) %collective-permute-start.6) | collective-permute-done | bytes 131104 | tf_op jit(solution)/shard_map/ppermute | solution.py:416
  38.0 2.6 %collective-permute-done.7.refs_7_ = bf16[1,4,128,128]{3,2,1,0:T(8,128)(2,1)S(1)} collective-permute-done((bf16[1,4,128,128]{3,2,1,0:T(8,128)(2,1)S(1)}, bf16[1,4,128,128]{3,2,1,0:T(8,128)(2,1)S(1)}, u32[]{:S(2)}, u32[]{:S(2)}) %collective-permute-start.7) | collective-permute-done | bytes 131104 | tf_op jit(solution)/shard_map/ppermute | solution.py:416
  40.6 1.9 %collective-permute-done.9.refs_8_.refs_1_ = bf16[1,4,128,128]{3,2,1,0:T(8,128)(2,1)S(1)} collective-permute-done((bf16[1,4,128,128]{3,2,1,0:T(8,128)(2,1)S(1)}, bf16[1,4,128,128]{3,2,1,0:T(8,128)(2,1)S(1)}, u32[]{:S(2)}, u32[]{:S(2)}) %collective-permute-start.9) | collective-permute-done | bytes 131104 | tf_op jit(solution)/shard_map/ppermute | solution.py:416
  42.9 2.4 %first_tiles.1 = (f32[4,384,128]{2,1,0:T(8,128)S(1)}, f32[384,128]{1,0:T(8,128)S(1)}) custom-call(bf16[4,384,128]{2,1,0:T(8,128)(2,1)S(1)} %get-tuple-element.31.refs_0_.asked_ref, bf16[1,4,128,128]{3,2,1,0:T(8,128)(2,1)S(1)} %get-tuple-element.32.refs_0_, bf16[1,4,128,128]{3,2,1,0:T(8,128)(2,1)S(1)} %collective-permute-done.1.refs_0_.refs_1_, ...), custom_call_target="tpu_custom_call" | custom-call | flops 805306368 | bytes 4194304 | tf_op jit(solution)/shard_map/first_tiles/pallas_call | solution.py:268
  46.8 2.0 %more_tiles.2 = (f32[4,384,128]{2,1,0:T(8,128)S(1)}, f32[384,128]{1,0:T(8,128)S(1)}) custom-call(bf16[4,384,128]{2,1,0:T(8,128)(2,1)S(1)} %get-tuple-element.31.refs_0_.asked_ref, f32[4,384,128]{2,1,0:T(8,128)S(1)} %get-tuple-element.41.old_sums_ref, f32[384,128]{1,0:T(8,128)S(1)} %get-tuple-element.42.old_tops_ref.refs_0_, ...), custom_call_target="tpu_custom_call" | custom-call | flops 402653184 | bytes 4194304 | tf_op jit(solution)/shard_map/more_tiles/pallas_call | solution.py:301
  49.2 2.0 %more_tiles.3 = (f32[4,384,128]{2,1,0:T(8,128)S(1)}, f32[384,128]{1,0:T(8,128)S(1)}) custom-call(bf16[4,384,128]{2,1,0:T(8,128)(2,1)S(1)} %get-tuple-element.31.refs_0_.asked_ref, f32[4,384,128]{2,1,0:T(8,128)S(1)} %get-tuple-element.46.old_sums_ref, f32[384,128]{1,0:T(8,128)S(1)} %get-tuple-element.47.old_tops_ref, ...), custom_call_target="tpu_custom_call" | custom-call | flops 201326592 | bytes 4194304 | tf_op jit(solution)/shard_map/more_tiles/pallas_call | solution.py:301
  51.8 1.3 %last_tiles.2.refs_2_ = bf16[192,256]{1,0:T(8,128)(2,1)S(1)} custom-call(bf16[4,384,128]{2,1,0:T(8,128)(2,1)S(1)} %get-tuple-element.31.refs_0_.asked_ref, f32[4,384,128]{2,1,0:T(8,128)S(1)} %get-tuple-element.50.sums_ref, f32[384,128]{1,0:T(8,128)S(1)} %get-tuple-element.51.tops_ref, bf16[1,4,128,128]{3,2,1,0:T(8,128)(2,1)S(1)} %collective-permute-done.14.refs_0_, ...), custom_call_target="tpu_custom_call" | custom-call | flops 100663296 | bytes 4194304 | tf_op jit(solution)/shard_map/last_tiles/pallas_call | solution.py:335
  53.1 1.6 %collective-permute-start.16 = (bf16[192,256]{1,0:T(8,128)(2,1)S(1)}, bf16[192,256]{1,0:T(8,128)(2,1)S(1)}, u32[]{:S(2)}, u32[]{:S(2)}) collective-permute-start(bf16[192,256]{1,0:T(8,128)(2,1)S(1)} %last_tiles.2.refs_2_), channel_id=1, source_target_pairs={{0,1},{1,0},{2,3},{3,2},{4,5},{5,4},{6,7},{7,6},{8,9},{9,8},{10,11... | collective-permute-start | bytes 294920 | tf_op jit(solution)/shard_map/ppermute | solution.py:435
  54.7 1.3 %last_tiles.3.answer_ref = bf16[192,256]{1,0:T(8,128)(2,1)S(1)} custom-call(bf16[4,384,128]{2,1,0:T(8,128)(2,1)S(1)} %get-tuple-element.31.refs_0_.asked_ref, f32[4,384,128]{2,1,0:T(8,128)S(1)} %get-tuple-element.50.sums_ref, f32[384,128]{1,0:T(8,128)S(1)} %get-tuple-element.51.tops_ref, bf16[1,4,128,128]{3,2,1,0:T(8,128)(2,1)S(1)} %collective-permute-done.14.refs_0_, ...), custom_call_target="tpu_custom_call" | custom-call | flops 100663296 | bytes 4194304 | tf_op jit(solution)/shard_map/last_tiles/pallas_call | solution.py:335
  56.8 1.2 %collective-permute-done.16 = bf16[192,256]{1,0:T(8,128)(2,1)S(1)} collective-permute-done((bf16[192,256]{1,0:T(8,128)(2,1)S(1)}, bf16[192,256]{1,0:T(8,128)(2,1)S(1)}, u32[]{:S(2)}, u32[]{:S(2)}) %collective-permute-start.16) | collective-permute-done | bytes 98336 | tf_op jit(solution)/shard_map/ppermute | solution.py:435
  (32 shorter events, 8.2 us)
Async XLA Ops:
  1.1 27.4 %collective-permute-start.8 = (bf16[4,4,128,128]{3,2,1,0:T(8,128)(2,1)S(1)}, bf16[4,4,128,128]{3,2,1,0:T(8,128)(2,1)S(1)}, u32[]{:S(2)}, u32[]{:S(2)}) collective-permute-start(bf16[4,4,128,128]{3,2,1,0:T(8,128)(2,1)S(1)} %bitcast.10), channel_id=1, source_target_pairs={{0,16},{2,18},{4,20},{6,22},{8,24},{10,26},{12,28},{14,30},{16,0},... | collective-permute-start | bytes 1572872 | tf_op jit(solution)/shard_map/ppermute | solution.py:395
  5.2 7.3 %collective-permute-start = (bf16[48,4,512]{2,1,0:T(4,128)(2,1)}, bf16[48,4,512]{2,1,0:T(4,128)(2,1)S(1)}, u32[]{:S(2)}, u32[]{:S(2)}) collective-permute-start(bf16[48,4,512]{2,1,0:T(4,128)(2,1)} %refs_0_.1), channel_id=1, source_target_pairs={{0,1},{1,0},{2,3},{3,2},{4,5},{5,4},{6,7},{7,6},{8,9},{9,8},{10,11... | collective-permute-start | bytes 589832 | tf_op jit(solution)/shard_map/ppermute | solution.py:399
  6.8 0.7 %copy-start.1 = (s32[1,12]{1,0:T(1,128)S(1)}, s32[1,12]{1,0:T(1,128)}, u32[]{:S(2)}) copy-start(s32[1,12]{1,0:T(1,128)} %ids_ref.1) | copy-start | bytes 148
  8.7 9.3 %all-to-all-start = ((s32[8,2,128]{2,1,0:T(2,128)}), s32[8,2,128]{2,1,0:T(2,128)S(1)}, u32[]{:S(2)}, u32[]{:S(2)}) async-start(s32[8,2,128]{2,1,0:T(2,128)} %request.1), calls=%async_computation | async-start | bytes 16384 | tf_op jit(solution)/shard_map/all_to_all | solution.py:390
  18.8 3.7 %collective-permute-start.1 = (bf16[1,4,128,128]{3,2,1,0:T(8,128)(2,1)S(1)}, bf16[1,4,128,128]{3,2,1,0:T(8,128)(2,1)S(1)}, u32[]{:S(2)}, u32[]{:S(2)}) collective-permute-start(bf16[1,4,128,128]{3,2,1,0:T(8,128)(2,1)S(1)} %get-tuple-element.33), channel_id=1, source_target_pairs={{0,2},{2,0},{4,6},{6,4},{8,10},{10,8},{12,14},{14,12},{16,18},{18,... | collective-permute-start | bytes 393224 | tf_op jit(solution)/shard_map/ppermute | solution.py:416
  19.4 5.7 %collective-permute-start.2 = (bf16[1,4,128,128]{3,2,1,0:T(8,128)(2,1)S(1)}, bf16[1,4,128,128]{3,2,1,0:T(8,128)(2,1)S(1)}, u32[]{:S(2)}, u32[]{:S(2)}) collective-permute-start(bf16[1,4,128,128]{3,2,1,0:T(8,128)(2,1)S(1)} %get-tuple-element.34), channel_id=1, source_target_pairs={{0,4},{2,6},{4,0},{6,2},{8,12},{10,14},{12,8},{14,10},{16,20},{18,... | collective-permute-start | bytes 393224 | tf_op jit(solution)/shard_map/ppermute | solution.py:416
  21.0 10.3 %collective-permute-start.3 = (bf16[1,4,128,128]{3,2,1,0:T(8,128)(2,1)S(1)}, bf16[1,4,128,128]{3,2,1,0:T(8,128)(2,1)S(1)}, u32[]{:S(2)}, u32[]{:S(2)}) collective-permute-start(bf16[1,4,128,128]{3,2,1,0:T(8,128)(2,1)S(1)} %get-tuple-element.35), channel_id=1, source_target_pairs={{0,8},{2,10},{4,12},{6,14},{8,0},{10,2},{12,4},{14,6},{16,24},{18,... | collective-permute-start | bytes 393224 | tf_op jit(solution)/shard_map/ppermute | solution.py:416
  22.5 11.4 %collective-permute-start.4 = (bf16[1,4,128,128]{3,2,1,0:T(8,128)(2,1)S(1)}, bf16[1,4,128,128]{3,2,1,0:T(8,128)(2,1)S(1)}, u32[]{:S(2)}, u32[]{:S(2)}) collective-permute-start(bf16[1,4,128,128]{3,2,1,0:T(8,128)(2,1)S(1)} %get-tuple-element.36), channel_id=1, source_target_pairs={{0,10},{2,8},{4,14},{6,12},{8,2},{10,0},{12,6},{14,4},{16,26},{18,... | collective-permute-start | bytes 393224 | tf_op jit(solution)/shard_map/ppermute | solution.py:416
  22.5 13.0 %collective-permute-start.5 = (bf16[1,4,128,128]{3,2,1,0:T(8,128)(2,1)S(1)}, bf16[1,4,128,128]{3,2,1,0:T(8,128)(2,1)S(1)}, u32[]{:S(2)}, u32[]{:S(2)}) collective-permute-start(bf16[1,4,128,128]{3,2,1,0:T(8,128)(2,1)S(1)} %get-tuple-element.37), channel_id=1, source_target_pairs={{0,6},{2,4},{4,2},{6,0},{8,14},{10,12},{12,10},{14,8},{16,22},{18,... | collective-permute-start | bytes 393224 | tf_op jit(solution)/shard_map/ppermute | solution.py:416
  25.0 12.9 %collective-permute-start.6 = (bf16[1,4,128,128]{3,2,1,0:T(8,128)(2,1)S(1)}, bf16[1,4,128,128]{3,2,1,0:T(8,128)(2,1)S(1)}, u32[]{:S(2)}, u32[]{:S(2)}) collective-permute-start(bf16[1,4,128,128]{3,2,1,0:T(8,128)(2,1)S(1)} %get-tuple-element.38), channel_id=1, source_target_pairs={{0,12},{2,14},{4,8},{6,10},{8,4},{10,6},{12,0},{14,2},{16,28},{18,... | collective-permute-start | bytes 393224 | tf_op jit(solution)/shard_map/ppermute | solution.py:416
  28.5 12.1 %collective-permute-start.7 = (bf16[1,4,128,128]{3,2,1,0:T(8,128)(2,1)S(1)}, bf16[1,4,128,128]{3,2,1,0:T(8,128)(2,1)S(1)}, u32[]{:S(2)}, u32[]{:S(2)}) collective-permute-start(bf16[1,4,128,128]{3,2,1,0:T(8,128)(2,1)S(1)} %get-tuple-element.39), channel_id=1, source_target_pairs={{0,14},{2,12},{4,10},{6,8},{8,6},{10,4},{12,2},{14,0},{16,30},{18,... | collective-permute-start | bytes 393224 | tf_op jit(solution)/shard_map/ppermute | solution.py:416
  31.3 11.3 %collective-permute-start.9 = (bf16[1,4,128,128]{3,2,1,0:T(8,128)(2,1)S(1)}, bf16[1,4,128,128]{3,2,1,0:T(8,128)(2,1)S(1)}, u32[]{:S(2)}, u32[]{:S(2)}) collective-permute-start(bf16[1,4,128,128]{3,2,1,0:T(8,128)(2,1)S(1)} %get-tuple-element.40), channel_id=1, source_target_pairs={{0,8},{2,10},{4,12},{6,14},{8,0},{10,2},{12,4},{14,6},{16,24},{18,... | collective-permute-start | bytes 393224 | tf_op jit(solution)/shard_map/ppermute | solution.py:416
  33.9 12.1 %collective-permute-start.10 = (bf16[1,4,128,128]{3,2,1,0:T(8,128)(2,1)S(1)}, bf16[1,4,128,128]{3,2,1,0:T(8,128)(2,1)S(1)}, u32[]{:S(2)}, u32[]{:S(2)}) collective-permute-start(bf16[1,4,128,128]{3,2,1,0:T(8,128)(2,1)S(1)} %get-tuple-element.44), channel_id=1, source_target_pairs={{0,4},{2,6},{4,0},{6,2},{8,12},{10,14},{12,8},{14,10},{16,20},{18,... | collective-permute-start | bytes 393224 | tf_op jit(solution)/shard_map/ppermute | solution.py:416
  35.5 11.4 %collective-permute-start.11 = (bf16[1,4,128,128]{3,2,1,0:T(8,128)(2,1)S(1)}, bf16[1,4,128,128]{3,2,1,0:T(8,128)(2,1)S(1)}, u32[]{:S(2)}, u32[]{:S(2)}) collective-permute-start(bf16[1,4,128,128]{3,2,1,0:T(8,128)(2,1)S(1)} %get-tuple-element.45), channel_id=1, source_target_pairs={{0,10},{2,8},{4,14},{6,12},{8,2},{10,0},{12,6},{14,4},{16,26},{18,... | collective-permute-start | bytes 393224 | tf_op jit(solution)/shard_map/ppermute | solution.py:416
  38.0 10.9 %collective-permute-start.12 = (bf16[1,4,128,128]{3,2,1,0:T(8,128)(2,1)S(1)}, bf16[1,4,128,128]{3,2,1,0:T(8,128)(2,1)S(1)}, u32[]{:S(2)}, u32[]{:S(2)}) collective-permute-start(bf16[1,4,128,128]{3,2,1,0:T(8,128)(2,1)S(1)} %get-tuple-element.48), channel_id=1, source_target_pairs={{0,6},{2,4},{4,2},{6,0},{8,14},{10,12},{12,10},{14,8},{16,22},{18,... | collective-permute-start | bytes 393224 | tf_op jit(solution)/shard_map/ppermute | solution.py:416
  40.6 8.6 %collective-permute-start.13 = (bf16[1,4,128,128]{3,2,1,0:T(8,128)(2,1)S(1)}, bf16[1,4,128,128]{3,2,1,0:T(8,128)(2,1)S(1)}, u32[]{:S(2)}, u32[]{:S(2)}) collective-permute-start(bf16[1,4,128,128]{3,2,1,0:T(8,128)(2,1)S(1)} %get-tuple-element.49), channel_id=1, source_target_pairs={{0,12},{2,14},{4,8},{6,10},{8,4},{10,6},{12,0},{14,2},{16,28},{18,... | collective-permute-start | bytes 393224 | tf_op jit(solution)/shard_map/ppermute | solution.py:416
  42.6 9.2 %collective-permute-start.14 = (bf16[1,4,128,128]{3,2,1,0:T(8,128)(2,1)S(1)}, bf16[1,4,128,128]{3,2,1,0:T(8,128)(2,1)S(1)}, u32[]{:S(2)}, u32[]{:S(2)}) collective-permute-start(bf16[1,4,128,128]{3,2,1,0:T(8,128)(2,1)S(1)} %get-tuple-element.52), channel_id=1, source_target_pairs={{0,14},{2,12},{4,10},{6,8},{8,6},{10,4},{12,2},{14,0},{16,30},{18,... | collective-permute-start | bytes 393224 | tf_op jit(solution)/shard_map/ppermute | solution.py:416
  46.0 5.8 %collective-permute-start.15 = (bf16[1,4,128,128]{3,2,1,0:T(8,128)(2,1)S(1)}, bf16[1,4,128,128]{3,2,1,0:T(8,128)(2,1)S(1)}, u32[]{:S(2)}, u32[]{:S(2)}) collective-permute-start(bf16[1,4,128,128]{3,2,1,0:T(8,128)(2,1)S(1)} %pick_each.5), channel_id=1, source_target_pairs={{0,2},{2,0},{4,6},{6,4},{8,10},{10,8},{12,14},{14,12},{16,18},{18,... | collective-permute-start | bytes 393224 | tf_op jit(solution)/shard_map/ppermute | solution.py:416
  51.8 4.2 %copy-start = (bf16[512,512]{1,0:T(8,128)(2,1)S(1)}, bf16[512,512]{1,0:T(8,128)(2,1)}, u32[]{:S(2)}) copy-start(bf16[512,512]{1,0:T(8,128)(2,1)} %weight_ref.1) | copy-start | bytes 1572868
  53.1 4.9 %collective-permute-start.16 = (bf16[192,256]{1,0:T(8,128)(2,1)S(1)}, bf16[192,256]{1,0:T(8,128)(2,1)S(1)}, u32[]{:S(2)}, u32[]{:S(2)}) collective-permute-start(bf16[192,256]{1,0:T(8,128)(2,1)S(1)} %last_tiles.2.refs_2_), channel_id=1, source_target_pairs={{0,1},{1,0},{2,3},{3,2},{4,5},{5,4},{6,7},{7,6},{8,9},{9,8},{10,11... | collective-permute-start | bytes 294920 | tf_op jit(solution)/shard_map/ppermute | solution.py:435

commit v24 on v22

--- a/solution.py
+++ b/solution.py
@@ -404,7 +404,7 @@
         return bool(step & across) and bool(step & (across - 1) & ~1)
 
     near_order = [0, 1] + sorted(range(2, half), key=lambda step: (turns(step), step != 2, not step & across, step))
-    far_order = [0] + sorted(range(2, half), key=lambda step: (turns(step), step & 1, step)) + [1]
+    far_order = [0] + sorted(range(2, half), key=lambda step: (turns(step), not step & across, step)) + [1]
     near_slots, far_slots = (near_order, [half + step for step in far_order]) if paired else ([0], [half])
 
     def spread(tiles, which, order, after):

time: 59.4 us -> 59.4 us (level)
  waiting for transfers between devices: 15.9 us -> 16.7 us
  starting transfers between devices: 23.2 us -> 22.5 us
    ppermute x14, starting transfers between devices: 12.2 us -> 11.5 us  [spread(): lax.ppermute(tile, 'rows', [(row, row ^ step) for row in range(row_size)])]
    ppermute x14, waiting for transfers between devices: 14.6 us -> 15.4 us  [spread(): lax.ppermute(tile, 'rows', [(row, row ^ step) for row in range(row_size)])]
where the time goes in v24:
time: 59.4 us; the launch traced here: 59.1 us
  starting transfers between devices  22.5 us (38%)
  Pallas kernels  17 us (29%)
  waiting for transfers between devices  16.7 us (28%)
  local copies, waits for them, and re-layouts  2.52 us (4%)
    ppermute x14, waiting for transfers between devices, spread(): lax.ppermute(tile, 'rows', [(row, row ^ step) for row in range(row_size)])  15.4 us
    ppermute x14, starting transfers between devices, spread(): lax.ppermute(tile, 'rows', [(row, row ^ step) for row in range(row_size)])  11.5 us
    pallas_call x1, Pallas kernels, front(): pl.pallas_call(functools.partial(front_kernel, groups, heads, head_size,...  5.51 us
    ppermute x1, starting transfers between devices, shards(): mirrored = lax.ppermute(heads_first, 'rows', turn(row_size, half))  4.1 us
    all_to_all x1, starting transfers between devices, swap(): lax.all_to_all(value, 'rows', split_axis=0, concat_axis=0, tiled=True, ax...  3.78 us
    pallas_call x2, Pallas kernels, last_tiles(): pl.pallas_call(functools.partial(last_kernel, slots, groups), out_shape=(...  2.87 us
    pallas_call x1, Pallas kernels, first_tiles(): pl.pallas_call(functools.partial(first_kernel, slots, rows if rows <= 512...  2.4 us
    pallas_call x3, Pallas kernels, pick_each(): pl.pallas_call(functools.partial(pick_each_kernel, which, order), out_sha...  2.19 us
  transfers between devices with their start and end apart: 18, of which 10 were waited for; matrix products, arithmetic and copies ran while one was open for 0% of the time, Pallas kernels for 26%

profile of v24, /device:TPU:0, one launch (start us, length us, event | category | flops | bytes accessed | tf_op | source)
XLA Modules:
  0.0 59.1 jit_solution(10009320511182745390)
XLA Ops:
  0.0 1.1 %copy.13 = bf16[4,128,4,128]{3,1,2,0:T(8,128)(2,1)S(1)} copy(bf16[4,128,4,128]{3,2,1,0:T(4,128)(2,1)} %param.17) | data formatting | bytes 1048576 | tf_op args[7]
  1.1 4.1 %collective-permute-start.8 = (bf16[4,4,128,128]{3,2,1,0:T(8,128)(2,1)S(1)}, bf16[4,4,128,128]{3,2,1,0:T(8,128)(2,1)S(1)}, u32[]{:S(2)}, u32[]{:S(2)}) collective-permute-start(bf16[4,4,128,128]{3,2,1,0:T(8,128)(2,1)S(1)} %bitcast.10), channel_id=1, source_target_pairs={{0,16},{2,18},{4,20},{6,22},{8,24},{10,26},{12,28},{14,30},{16,0},... | collective-permute-start | bytes 1572872 | tf_op jit(solution)/shard_map/ppermute | solution.py:395
  5.2 1.5 %collective-permute-start = (bf16[48,4,512]{2,1,0:T(4,128)(2,1)}, bf16[48,4,512]{2,1,0:T(4,128)(2,1)S(1)}, u32[]{:S(2)}, u32[]{:S(2)}) collective-permute-start(bf16[48,4,512]{2,1,0:T(4,128)(2,1)} %refs_0_.1), channel_id=1, source_target_pairs={{0,1},{1,0},{2,3},{3,2},{4,5},{5,4},{6,7},{7,6},{8,9},{9,8},{10,11... | collective-permute-start | bytes 589832 | tf_op jit(solution)/shard_map/ppermute | solution.py:399
  7.5 1.2 %request.1 = s32[8,2,128]{2,1,0:T(2,128)} custom-call(s32[1,12]{1,0:T(1,128)S(1)} %copy-done.1, s32[2]{0:T(128)S(1)} %pad_add_fusion.refs_2_.me_ref), custom_call_target="tpu_custom_call" | custom-call | bytes 262144 | tf_op jit(solution)/shard_map/request/pallas_call | solution.py:59
  8.7 3.8 %all-to-all-start = ((s32[8,2,128]{2,1,0:T(2,128)}), s32[8,2,128]{2,1,0:T(2,128)S(1)}, u32[]{:S(2)}, u32[]{:S(2)}) async-start(s32[8,2,128]{2,1,0:T(2,128)} %request.1), calls=%async_computation | async-start | bytes 16384 | tf_op jit(solution)/shard_map/all_to_all | solution.py:390
  12.5 5.5 %front.1 = (f32[192,512]{1,0:T(8,128)S(1)}, bf16[4,384,128]{2,1,0:T(8,128)(2,1)S(1)}) custom-call(bf16[48,4,512]{2,1,0:T(4,128)(2,1)} %refs_0_.1, bf16[48,4,512]{2,1,0:T(4,128)(2,1)S(1)} %collective-permute-done.refs_1_, s32[2]{0:T(128)S(1)} %pad_add_fusion.refs_2_.me_ref, s32[1,12]{1,0:T(1,128)} %ids_ref.1, s32[12,48]{1,0:T(8,128)} %bitcast.12, ...), custom_call_target="tpu_custom_call" | custom-call | flops 1006632960 | bytes 4194304 | tf_op jit(solution)/shard_map/front/pallas_call | solution.py:218
  19.4 1.7 %collective-permute-start.2 = (bf16[1,4,128,128]{3,2,1,0:T(8,128)(2,1)S(1)}, bf16[1,4,128,128]{3,2,1,0:T(8,128)(2,1)S(1)}, u32[]{:S(2)}, u32[]{:S(2)}) collective-permute-start(bf16[1,4,128,128]{3,2,1,0:T(8,128)(2,1)S(1)} %get-tuple-element.32), channel_id=1, source_target_pairs={{0,4},{2,6},{4,0},{6,2},{8,12},{10,14},{12,8},{14,10},{16,20},{18,... | collective-permute-start | bytes 393224 | tf_op jit(solution)/shard_map/ppermute | solution.py:416
  21.0 1.5 %collective-permute-start.3 = (bf16[1,4,128,128]{3,2,1,0:T(8,128)(2,1)S(1)}, bf16[1,4,128,128]{3,2,1,0:T(8,128)(2,1)S(1)}, u32[]{:S(2)}, u32[]{:S(2)}) collective-permute-start(bf16[1,4,128,128]{3,2,1,0:T(8,128)(2,1)S(1)} %get-tuple-element.33), channel_id=1, source_target_pairs={{0,8},{2,10},{4,12},{6,14},{8,0},{10,2},{12,4},{14,6},{16,24},{18,... | collective-permute-start | bytes 393224 | tf_op jit(solution)/shard_map/ppermute | solution.py:416
  23.1 1.9 %collective-permute-done.2.refs_1_.refs_2_ = bf16[1,4,128,128]{3,2,1,0:T(8,128)(2,1)S(1)} collective-permute-done((bf16[1,4,128,128]{3,2,1,0:T(8,128)(2,1)S(1)}, bf16[1,4,128,128]{3,2,1,0:T(8,128)(2,1)S(1)}, u32[]{:S(2)}, u32[]{:S(2)}) %collective-permute-start.2) | collective-permute-done | bytes 131104 | tf_op jit(solution)/shard_map/ppermute | solution.py:416
  25.0 3.2 %collective-permute-start.6 = (bf16[1,4,128,128]{3,2,1,0:T(8,128)(2,1)S(1)}, bf16[1,4,128,128]{3,2,1,0:T(8,128)(2,1)S(1)}, u32[]{:S(2)}, u32[]{:S(2)}) collective-permute-start(bf16[1,4,128,128]{3,2,1,0:T(8,128)(2,1)S(1)} %get-tuple-element.36), channel_id=1, source_target_pairs={{0,12},{2,14},{4,8},{6,10},{8,4},{10,6},{12,0},{14,2},{16,28},{18,... | collective-permute-start | bytes 393224 | tf_op jit(solution)/shard_map/ppermute | solution.py:416
  28.5 1.2 %collective-permute-start.7 = (bf16[1,4,128,128]{3,2,1,0:T(8,128)(2,1)S(1)}, bf16[1,4,128,128]{3,2,1,0:T(8,128)(2,1)S(1)}, u32[]{:S(2)}, u32[]{:S(2)}) collective-permute-start(bf16[1,4,128,128]{3,2,1,0:T(8,128)(2,1)S(1)} %get-tuple-element.37), channel_id=1, source_target_pairs={{0,14},{2,12},{4,10},{6,8},{8,6},{10,4},{12,2},{14,0},{16,30},{18,... | collective-permute-start | bytes 393224 | tf_op jit(solution)/shard_map/ppermute | solution.py:416
  30.5 0.8 %collective-permute-done.3.refs_3_ = bf16[1,4,128,128]{3,2,1,0:T(8,128)(2,1)S(1)} collective-permute-done((bf16[1,4,128,128]{3,2,1,0:T(8,128)(2,1)S(1)}, bf16[1,4,128,128]{3,2,1,0:T(8,128)(2,1)S(1)}, u32[]{:S(2)}, u32[]{:S(2)}) %collective-permute-start.3) | collective-permute-done | bytes 131104 | tf_op jit(solution)/shard_map/ppermute | solution.py:416
  31.3 2.6 %collective-permute-done.4.refs_4_ = bf16[1,4,128,128]{3,2,1,0:T(8,128)(2,1)S(1)} collective-permute-done((bf16[1,4,128,128]{3,2,1,0:T(8,128)(2,1)S(1)}, bf16[1,4,128,128]{3,2,1,0:T(8,128)(2,1)S(1)}, u32[]{:S(2)}, u32[]{:S(2)}) %collective-permute-start.4) | collective-permute-done | bytes 131104 | tf_op jit(solution)/shard_map/ppermute | solution.py:416
  33.9 1.5 %collective-permute-start.11 = (bf16[1,4,128,128]{3,2,1,0:T(8,128)(2,1)S(1)}, bf16[1,4,128,128]{3,2,1,0:T(8,128)(2,1)S(1)}, u32[]{:S(2)}, u32[]{:S(2)}) collective-permute-start(bf16[1,4,128,128]{3,2,1,0:T(8,128)(2,1)S(1)} %get-tuple-element.43), channel_id=1, source_target_pairs={{0,4},{2,6},{4,0},{6,2},{8,12},{10,14},{12,8},{14,10},{16,20},{18,... | collective-permute-start | bytes 393224 | tf_op jit(solution)/shard_map/ppermute | solution.py:416
  35.5 2.5 %collective-permute-done.6.refs_6_ = bf16[1,4,128,128]{3,2,1,0:T(8,128)(2,1)S(1)} collective-permute-done((bf16[1,4,128,128]{3,2,1,0:T(8,128)(2,1)S(1)}, bf16[1,4,128,128]{3,2,1,0:T(8,128)(2,1)S(1)}, u32[]{:S(2)}, u32[]{:S(2)}) %collective-permute-start.6) | collective-permute-done | bytes 131104 | tf_op jit(solution)/shard_map/ppermute | solution.py:416
  38.0 2.6 %collective-permute-done.7.refs_7_ = bf16[1,4,128,128]{3,2,1,0:T(8,128)(2,1)S(1)} collective-permute-done((bf16[1,4,128,128]{3,2,1,0:T(8,128)(2,1)S(1)}, bf16[1,4,128,128]{3,2,1,0:T(8,128)(2,1)S(1)}, u32[]{:S(2)}, u32[]{:S(2)}) %collective-permute-start.7) | collective-permute-done | bytes 131104 | tf_op jit(solution)/shard_map/ppermute | solution.py:416
  40.6 1.9 %collective-permute-done.9.refs_8_.refs_1_ = bf16[1,4,128,128]{3,2,1,0:T(8,128)(2,1)S(1)} collective-permute-done((bf16[1,4,128,128]{3,2,1,0:T(8,128)(2,1)S(1)}, bf16[1,4,128,128]{3,2,1,0:T(8,128)(2,1)S(1)}, u32[]{:S(2)}, u32[]{:S(2)}) %collective-permute-start.9) | collective-permute-done | bytes 131104 | tf_op jit(solution)/shard_map/ppermute | solution.py:416
  42.9 2.4 %first_tiles.1 = (f32[4,384,128]{2,1,0:T(8,128)S(1)}, f32[384,128]{1,0:T(8,128)S(1)}) custom-call(bf16[4,384,128]{2,1,0:T(8,128)(2,1)S(1)} %get-tuple-element.29.refs_0_.asked_ref, bf16[1,4,128,128]{3,2,1,0:T(8,128)(2,1)S(1)} %get-tuple-element.30.refs_0_, bf16[1,4,128,128]{3,2,1,0:T(8,128)(2,1)S(1)} %collective-permute-done.1.refs_0_.refs_1_, ...), custom_call_target="tpu_custom_call" | custom-call | flops 805306368 | bytes 4194304 | tf_op jit(solution)/shard_map/first_tiles/pallas_call | solution.py:268
  46.9 2.0 %more_tiles.1 = (f32[4,384,128]{2,1,0:T(8,128)S(1)}, f32[384,128]{1,0:T(8,128)S(1)}) custom-call(bf16[4,384,128]{2,1,0:T(8,128)(2,1)S(1)} %get-tuple-element.29.refs_0_.asked_ref, f32[4,384,128]{2,1,0:T(8,128)S(1)} %get-tuple-element.39.old_sums_ref, f32[384,128]{1,0:T(8,128)S(1)} %get-tuple-element.40.old_tops_ref.refs_0_, ...), custom_call_target="tpu_custom_call" | custom-call | flops 402653184 | bytes 4194304 | tf_op jit(solution)/shard_map/more_tiles/pallas_call | solution.py:301
  49.2 2.6 %collective-permute-done.14.refs_2_ = bf16[1,4,128,128]{3,2,1,0:T(8,128)(2,1)S(1)} collective-permute-done((bf16[1,4,128,128]{3,2,1,0:T(8,128)(2,1)S(1)}, bf16[1,4,128,128]{3,2,1,0:T(8,128)(2,1)S(1)}, u32[]{:S(2)}, u32[]{:S(2)}) %collective-permute-start.14) | collective-permute-done | bytes 131104 | tf_op jit(solution)/shard_map/ppermute | solution.py:416
  51.8 1.4 %last_tiles.2.refs_4_ = bf16[192,256]{1,0:T(8,128)(2,1)S(1)} custom-call(bf16[4,384,128]{2,1,0:T(8,128)(2,1)S(1)} %get-tuple-element.29.refs_0_.asked_ref, f32[4,384,128]{2,1,0:T(8,128)S(1)} %get-tuple-element.44.sums_ref, f32[384,128]{1,0:T(8,128)S(1)} %get-tuple-element.45.tops_ref, bf16[1,4,128,128]{3,2,1,0:T(8,128)(2,1)S(1)} %collective-permute-done.12.refs_0_, ...), custom_call_target="tpu_custom_call" | custom-call | flops 201326592 | bytes 4194304 | tf_op jit(solution)/shard_map/last_tiles/pallas_call | solution.py:335
  53.3 1.6 %collective-permute-start.16 = (bf16[192,256]{1,0:T(8,128)(2,1)S(1)}, bf16[192,256]{1,0:T(8,128)(2,1)S(1)}, u32[]{:S(2)}, u32[]{:S(2)}) collective-permute-start(bf16[192,256]{1,0:T(8,128)(2,1)S(1)} %last_tiles.2.refs_4_), channel_id=1, source_target_pairs={{0,1},{1,0},{2,3},{3,2},{4,5},{5,4},{6,7},{7,6},{8,9},{9,8},{10,11... | collective-permute-start | bytes 294920 | tf_op jit(solution)/shard_map/ppermute | solution.py:435
  54.9 1.4 %last_tiles.3.answer_ref = bf16[192,256]{1,0:T(8,128)(2,1)S(1)} custom-call(bf16[4,384,128]{2,1,0:T(8,128)(2,1)S(1)} %get-tuple-element.29.refs_0_.asked_ref, f32[4,384,128]{2,1,0:T(8,128)S(1)} %get-tuple-element.44.sums_ref, f32[384,128]{1,0:T(8,128)S(1)} %get-tuple-element.45.tops_ref, bf16[1,4,128,128]{3,2,1,0:T(8,128)(2,1)S(1)} %collective-permute-done.12.refs_0_, ...), custom_call_target="tpu_custom_call" | custom-call | flops 201326592 | bytes 4194304 | tf_op jit(solution)/shard_map/last_tiles/pallas_call | solution.py:335
  57.1 1.0 %collective-permute-done.16 = bf16[192,256]{1,0:T(8,128)(2,1)S(1)} collective-permute-done((bf16[192,256]{1,0:T(8,128)(2,1)S(1)}, bf16[192,256]{1,0:T(8,128)(2,1)S(1)}, u32[]{:S(2)}, u32[]{:S(2)}) %collective-permute-start.16) | collective-permute-done | bytes 98336 | tf_op jit(solution)/shard_map/ppermute | solution.py:435
  (31 shorter events, 7.6 us)
Async XLA Ops:
  1.1 27.4 %collective-permute-start.8 = (bf16[4,4,128,128]{3,2,1,0:T(8,128)(2,1)S(1)}, bf16[4,4,128,128]{3,2,1,0:T(8,128)(2,1)S(1)}, u32[]{:S(2)}, u32[]{:S(2)}) collective-permute-start(bf16[4,4,128,128]{3,2,1,0:T(8,128)(2,1)S(1)} %bitcast.10), channel_id=1, source_target_pairs={{0,16},{2,18},{4,20},{6,22},{8,24},{10,26},{12,28},{14,30},{16,0},... | collective-permute-start | bytes 1572872 | tf_op jit(solution)/shard_map/ppermute | solution.py:395
  5.2 7.3 %collective-permute-start = (bf16[48,4,512]{2,1,0:T(4,128)(2,1)}, bf16[48,4,512]{2,1,0:T(4,128)(2,1)S(1)}, u32[]{:S(2)}, u32[]{:S(2)}) collective-permute-start(bf16[48,4,512]{2,1,0:T(4,128)(2,1)} %refs_0_.1), channel_id=1, source_target_pairs={{0,1},{1,0},{2,3},{3,2},{4,5},{5,4},{6,7},{7,6},{8,9},{9,8},{10,11... | collective-permute-start | bytes 589832 | tf_op jit(solution)/shard_map/ppermute | solution.py:399
  6.8 0.7 %copy-start.1 = (s32[1,12]{1,0:T(1,128)S(1)}, s32[1,12]{1,0:T(1,128)}, u32[]{:S(2)}) copy-start(s32[1,12]{1,0:T(1,128)} %ids_ref.1) | copy-start | bytes 148
  8.7 9.3 %all-to-all-start = ((s32[8,2,128]{2,1,0:T(2,128)}), s32[8,2,128]{2,1,0:T(2,128)S(1)}, u32[]{:S(2)}, u32[]{:S(2)}) async-start(s32[8,2,128]{2,1,0:T(2,128)} %request.1), calls=%async_computation | async-start | bytes 16384 | tf_op jit(solution)/shard_map/all_to_all | solution.py:390
  18.8 3.7 %collective-permute-start.1 = (bf16[1,4,128,128]{3,2,1,0:T(8,128)(2,1)S(1)}, bf16[1,4,128,128]{3,2,1,0:T(8,128)(2,1)S(1)}, u32[]{:S(2)}, u32[]{:S(2)}) collective-permute-start(bf16[1,4,128,128]{3,2,1,0:T(8,128)(2,1)S(1)} %get-tuple-element.31), channel_id=1, source_target_pairs={{0,2},{2,0},{4,6},{6,4},{8,10},{10,8},{12,14},{14,12},{16,18},{18,... | collective-permute-start | bytes 393224 | tf_op jit(solution)/shard_map/ppermute | solution.py:416
  19.4 5.7 %collective-permute-start.2 = (bf16[1,4,128,128]{3,2,1,0:T(8,128)(2,1)S(1)}, bf16[1,4,128,128]{3,2,1,0:T(8,128)(2,1)S(1)}, u32[]{:S(2)}, u32[]{:S(2)}) collective-permute-start(bf16[1,4,128,128]{3,2,1,0:T(8,128)(2,1)S(1)} %get-tuple-element.32), channel_id=1, source_target_pairs={{0,4},{2,6},{4,0},{6,2},{8,12},{10,14},{12,8},{14,10},{16,20},{18,... | collective-permute-start | bytes 393224 | tf_op jit(solution)/shard_map/ppermute | solution.py:416
  21.0 10.3 %collective-permute-start.3 = (bf16[1,4,128,128]{3,2,1,0:T(8,128)(2,1)S(1)}, bf16[1,4,128,128]{3,2,1,0:T(8,128)(2,1)S(1)}, u32[]{:S(2)}, u32[]{:S(2)}) collective-permute-start(bf16[1,4,128,128]{3,2,1,0:T(8,128)(2,1)S(1)} %get-tuple-element.33), channel_id=1, source_target_pairs={{0,8},{2,10},{4,12},{6,14},{8,0},{10,2},{12,4},{14,6},{16,24},{18,... | collective-permute-start | bytes 393224 | tf_op jit(solution)/shard_map/ppermute | solution.py:416
  22.5 11.4 %collective-permute-start.4 = (bf16[1,4,128,128]{3,2,1,0:T(8,128)(2,1)S(1)}, bf16[1,4,128,128]{3,2,1,0:T(8,128)(2,1)S(1)}, u32[]{:S(2)}, u32[]{:S(2)}) collective-permute-start(bf16[1,4,128,128]{3,2,1,0:T(8,128)(2,1)S(1)} %get-tuple-element.34), channel_id=1, source_target_pairs={{0,10},{2,8},{4,14},{6,12},{8,2},{10,0},{12,6},{14,4},{16,26},{18,... | collective-permute-start | bytes 393224 | tf_op jit(solution)/shard_map/ppermute | solution.py:416
  22.5 11.4 %collective-permute-start.5 = (bf16[1,4,128,128]{3,2,1,0:T(8,128)(2,1)S(1)}, bf16[1,4,128,128]{3,2,1,0:T(8,128)(2,1)S(1)}, u32[]{:S(2)}, u32[]{:S(2)}) collective-permute-start(bf16[1,4,128,128]{3,2,1,0:T(8,128)(2,1)S(1)} %get-tuple-element.35), channel_id=1, source_target_pairs={{0,6},{2,4},{4,2},{6,0},{8,14},{10,12},{12,10},{14,8},{16,22},{18,... | collective-permute-start | bytes 393224 | tf_op jit(solution)/shard_map/ppermute | solution.py:416
  25.0 12.9 %collective-permute-start.6 = (bf16[1,4,128,128]{3,2,1,0:T(8,128)(2,1)S(1)}, bf16[1,4,128,128]{3,2,1,0:T(8,128)(2,1)S(1)}, u32[]{:S(2)}, u32[]{:S(2)}) collective-permute-start(bf16[1,4,128,128]{3,2,1,0:T(8,128)(2,1)S(1)} %get-tuple-element.36), channel_id=1, source_target_pairs={{0,12},{2,14},{4,8},{6,10},{8,4},{10,6},{12,0},{14,2},{16,28},{18,... | collective-permute-start | bytes 393224 | tf_op jit(solution)/shard_map/ppermute | solution.py:416
  28.5 12.1 %collective-permute-start.7 = (bf16[1,4,128,128]{3,2,1,0:T(8,128)(2,1)S(1)}, bf16[1,4,128,128]{3,2,1,0:T(8,128)(2,1)S(1)}, u32[]{:S(2)}, u32[]{:S(2)}) collective-permute-start(bf16[1,4,128,128]{3,2,1,0:T(8,128)(2,1)S(1)} %get-tuple-element.37), channel_id=1, source_target_pairs={{0,14},{2,12},{4,10},{6,8},{8,6},{10,4},{12,2},{14,0},{16,30},{18,... | collective-permute-start | bytes 393224 | tf_op jit(solution)/shard_map/ppermute | solution.py:416
  31.3 11.3 %collective-permute-start.9 = (bf16[1,4,128,128]{3,2,1,0:T(8,128)(2,1)S(1)}, bf16[1,4,128,128]{3,2,1,0:T(8,128)(2,1)S(1)}, u32[]{:S(2)}, u32[]{:S(2)}) collective-permute-start(bf16[1,4,128,128]{3,2,1,0:T(8,128)(2,1)S(1)} %get-tuple-element.38), channel_id=1, source_target_pairs={{0,8},{2,10},{4,12},{6,14},{8,0},{10,2},{12,4},{14,6},{16,24},{18,... | collective-permute-start | bytes 393224 | tf_op jit(solution)/shard_map/ppermute | solution.py:416
  33.9 12.1 %collective-permute-start.10 = (bf16[1,4,128,128]{3,2,1,0:T(8,128)(2,1)S(1)}, bf16[1,4,128,128]{3,2,1,0:T(8,128)(2,1)S(1)}, u32[]{:S(2)}, u32[]{:S(2)}) collective-permute-start(bf16[1,4,128,128]{3,2,1,0:T(8,128)(2,1)S(1)} %get-tuple-element.42), channel_id=1, source_target_pairs={{0,10},{2,8},{4,14},{6,12},{8,2},{10,0},{12,6},{14,4},{16,26},{18,... | collective-permute-start | bytes 393224 | tf_op jit(solution)/shard_map/ppermute | solution.py:416
  33.9 12.9 %collective-permute-start.11 = (bf16[1,4,128,128]{3,2,1,0:T(8,128)(2,1)S(1)}, bf16[1,4,128,128]{3,2,1,0:T(8,128)(2,1)S(1)}, u32[]{:S(2)}, u32[]{:S(2)}) collective-permute-start(bf16[1,4,128,128]{3,2,1,0:T(8,128)(2,1)S(1)} %get-tuple-element.43), channel_id=1, source_target_pairs={{0,4},{2,6},{4,0},{6,2},{8,12},{10,14},{12,8},{14,10},{16,20},{18,... | collective-permute-start | bytes 393224 | tf_op jit(solution)/shard_map/ppermute | solution.py:416
  38.0 10.9 %collective-permute-start.12 = (bf16[1,4,128,128]{3,2,1,0:T(8,128)(2,1)S(1)}, bf16[1,4,128,128]{3,2,1,0:T(8,128)(2,1)S(1)}, u32[]{:S(2)}, u32[]{:S(2)}) collective-permute-start(bf16[1,4,128,128]{3,2,1,0:T(8,128)(2,1)S(1)} %get-tuple-element.46), channel_id=1, source_target_pairs={{0,6},{2,4},{4,2},{6,0},{8,14},{10,12},{12,10},{14,8},{16,22},{18,... | collective-permute-start | bytes 393224 | tf_op jit(solution)/shard_map/ppermute | solution.py:416
  40.6 8.6 %collective-permute-start.13 = (bf16[1,4,128,128]{3,2,1,0:T(8,128)(2,1)S(1)}, bf16[1,4,128,128]{3,2,1,0:T(8,128)(2,1)S(1)}, u32[]{:S(2)}, u32[]{:S(2)}) collective-permute-start(bf16[1,4,128,128]{3,2,1,0:T(8,128)(2,1)S(1)} %get-tuple-element.47), channel_id=1, source_target_pairs={{0,12},{2,14},{4,8},{6,10},{8,4},{10,6},{12,0},{14,2},{16,28},{18,... | collective-permute-start | bytes 393224 | tf_op jit(solution)/shard_map/ppermute | solution.py:416
  42.6 9.2 %collective-permute-start.14 = (bf16[1,4,128,128]{3,2,1,0:T(8,128)(2,1)S(1)}, bf16[1,4,128,128]{3,2,1,0:T(8,128)(2,1)S(1)}, u32[]{:S(2)}, u32[]{:S(2)}) collective-permute-start(bf16[1,4,128,128]{3,2,1,0:T(8,128)(2,1)S(1)} %get-tuple-element.48), channel_id=1, source_target_pairs={{0,14},{2,12},{4,10},{6,8},{8,6},{10,4},{12,2},{14,0},{16,30},{18,... | collective-permute-start | bytes 393224 | tf_op jit(solution)/shard_map/ppermute | solution.py:416
  46.1 5.8 %collective-permute-start.15 = (bf16[1,4,128,128]{3,2,1,0:T(8,128)(2,1)S(1)}, bf16[1,4,128,128]{3,2,1,0:T(8,128)(2,1)S(1)}, u32[]{:S(2)}, u32[]{:S(2)}) collective-permute-start(bf16[1,4,128,128]{3,2,1,0:T(8,128)(2,1)S(1)} %pick_each.5), channel_id=1, source_target_pairs={{0,2},{2,0},{4,6},{6,4},{8,10},{10,8},{12,14},{14,12},{16,18},{18,... | collective-permute-start | bytes 393224 | tf_op jit(solution)/shard_map/ppermute | solution.py:416
  51.8 4.5 %copy-start = (bf16[512,512]{1,0:T(8,128)(2,1)S(1)}, bf16[512,512]{1,0:T(8,128)(2,1)}, u32[]{:S(2)}) copy-start(bf16[512,512]{1,0:T(8,128)(2,1)} %weight_ref.1) | copy-start | bytes 1572868
  53.3 4.9 %collective-permute-start.16 = (bf16[192,256]{1,0:T(8,128)(2,1)S(1)}, bf16[192,256]{1,0:T(8,128)(2,1)S(1)}, u32[]{:S(2)}, u32[]{:S(2)}) collective-permute-start(bf16[192,256]{1,0:T(8,128)(2,1)S(1)} %last_tiles.2.refs_4_), channel_id=1, source_target_pairs={{0,1},{1,0},{2,3},{3,2},{4,5},{5,4},{6,7},{7,6},{8,9},{9,8},{10,11... | collective-permute-start | bytes 294920 | tf_op jit(solution)/shard_map/ppermute | solution.py:435
